TPU v7x, 32 devices: a whole 2x2x4 slice. The times are simulated.
32 devices in a mesh: groups: 2 (over y), blk: 4 (over z), dp: 2 (over x), sub: 2 (over core).
Axes of the slice: x: 2, y: 2, z: 4, core: 2. Of those that a mesh axis runs over, the one named last changes fastest.
Arguments:
- activations: bfloat16 [4096, 5120], P(('groups', 'blk', 'dp'), 'sub'), parts along dimension 0, may hold values from -6 to 6
- norm_gain: bfloat16 [5120], replicated, may hold values from 0.099609375 to 1.8984375
- queries: bfloat16 [4096, 2560], P(('groups', 'blk', 'dp'), 'sub'), parts along dimension 0, may hold values from -44 to 44
- cotangent: bfloat16 [4096, 2560], P(('groups', 'blk', 'dp'), 'sub'), parts along dimension 0, may hold values from -5 to 5
- kv_weight: bfloat16 [2, 5120, 512], P(None, 'blk', 'sub'), may hold values from -0.078125 to 0.078125
- kv_bias: bfloat16 [2, 512], P(None, 'sub'), may hold values from -5 to 5
Outputs:
- grad_queries: bfloat16 [4096, 2560], P(('groups', 'blk', 'dp'), 'sub'), parts along dimension 0
- grad_weight: float32 [2, 10240, 512], P(None, ('groups', 'blk', 'dp'), 'sub'), parts along dimension 1
- grad_bias: float32 [4, 512], P('groups', 'sub'), parts along dimension 0
There are 2 independent parts, one for each index of `groups`. A program takes and returns all parts, laid end to end along the dimension named above; an argument that names none is the same for every part. Nothing has to cross between parts.
All inputs are finite; a program needn't handle non-finite values.
Results may differ from a plain program's by a relative error of at most 0.0065.
The roundings to bfloat16 on the way count: a program that leaves them out, or rounds other values in their place, can miss the bound.
Values may be sent and summed in bfloat16 or wider, within the bound.
No kernel may reach another device: no remote copies, remote signals or barrier semaphores. Data moves between devices by JAX's collectives and lax.ppermute only.
A program may use at most 64 MiB of HBM per device.

v0:
```python
import jax
import jax.numpy as jnp
from jax import lax
from jax.sharding import PartitionSpec as P

HEAD = 128


EPSILON = 1e-06
ROPE_BASE = 1000000.0


def passed_along(block, axis, distance):
    devices = range(lax.axis_size(axis))
    route = [((i - distance) % len(devices), i) for i in devices]
    return lax.ppermute(block, axis, route)


def normalize(activations, norm_gain):
    wide_values = activations.astype(jnp.float32)
    mean_square = jnp.mean(wide_values * wide_values, -1, keepdims=True)
    return (wide_values * lax.rsqrt(mean_square + EPSILON) * norm_gain.astype(jnp.float32)).astype(
        jnp.bfloat16
    )


def rope_tables(length, head_size):
    half_size = head_size // 2
    exponent = jnp.arange(half_size, dtype=jnp.float32) * (2.0 / head_size)
    frequency = jnp.exp(-exponent * jnp.log(jnp.float32(ROPE_BASE)))
    angles = jnp.arange(length, dtype=jnp.float32)[:, None] * frequency[None, :]
    cosine_table = jnp.cos(angles)
    sine_table = jnp.sin(angles)
    return (
        jnp.concatenate([cosine_table, cosine_table], -1),
        jnp.concatenate([sine_table, sine_table], -1),
    )


def rotate_half(vector):
    half_size = vector.shape[-1] // 2
    return jnp.concatenate([-vector[..., half_size:], vector[..., :half_size]], -1)


def rotate_back(vector):
    half_size = vector.shape[-1] // 2
    return jnp.concatenate([vector[..., half_size:], -vector[..., :half_size]], -1)


def attention_backward(raw_keys, raw_values, queries, cotangent):
    length = raw_keys.shape[0]
    key_heads = raw_keys.shape[1] // HEAD
    group_size = queries.shape[1] // raw_keys.shape[1]
    cosine_table, sine_table = rope_tables(length, HEAD)
    raw_heads = raw_keys.reshape(length, key_heads, HEAD)
    rotated_keys = (
        raw_heads * cosine_table[:, None, :] + rotate_half(raw_heads) * sine_table[:, None, :]
    ).astype(jnp.bfloat16)
    value_heads = raw_values.astype(jnp.bfloat16).reshape(length, key_heads, HEAD)
    query_heads = queries.reshape(length, key_heads, group_size, HEAD)
    grad_heads = cotangent.reshape(length, key_heads, group_size, HEAD)
    score_scale = HEAD ** (-0.5)
    scores = (
        jnp.einsum("tkgd,skd->kgts", query_heads, rotated_keys, preferred_element_type=jnp.float32)
        * score_scale
    )
    causal = jnp.arange(length)[:, None] >= jnp.arange(length)[None, :]
    scores = jnp.where(causal, scores, -jnp.inf)
    row_peak = jnp.max(scores, -1, keepdims=True)
    exponentials = jnp.exp(scores - row_peak)
    probability = exponentials / jnp.sum(exponentials, -1, keepdims=True)
    rounded_weights = probability.astype(jnp.bfloat16)
    grad_probability = jnp.einsum(
        "tkgd,skd->kgts", grad_heads, value_heads, preferred_element_type=jnp.float32
    )
    row_total = jnp.sum(probability * grad_probability, -1, keepdims=True)
    grad_scores = (probability * (grad_probability - row_total) * score_scale).astype(jnp.bfloat16)
    grad_query = jnp.einsum(
        "kgts,skd->tkgd", grad_scores, rotated_keys, preferred_element_type=jnp.float32
    )
    grad_query = grad_query.astype(jnp.bfloat16).reshape(length, -1)
    grad_rotated = jnp.einsum(
        "kgts,tkgd->skd", grad_scores, query_heads, preferred_element_type=jnp.float32
    )
    grad_value = jnp.einsum(
        "kgts,tkgd->skd", rounded_weights, grad_heads, preferred_element_type=jnp.float32
    )
    grad_key = grad_rotated * cosine_table[:, None, :] + rotate_back(
        grad_rotated * sine_table[:, None, :]
    )
    grad_pair = jnp.stack([grad_key.reshape(length, -1), grad_value.reshape(length, -1)]).astype(
        jnp.bfloat16
    )
    return (grad_query, grad_pair)


def local(activations, norm_gain, queries, cotangent, kv_weight, kv_bias):
    full_features = lax.all_gather(activations, "sub", axis=1, tiled=True)
    normed = normalize(full_features, norm_gain)
    cycle_size = lax.axis_size("blk")
    position = lax.axis_index("blk")
    block_rows = kv_weight.shape[1]
    columns = kv_weight.shape[2]
    length = activations.shape[0]

    def project(weight_block, source):
        normed_slab = lax.dynamic_slice_in_dim(normed, source * block_rows, block_rows, 1)
        return jnp.einsum(
            "tr,krc->ktc", normed_slab, weight_block, preferred_element_type=jnp.float32
        )

    def contribute(grad_block, source):
        normed_slab = lax.dynamic_slice_in_dim(normed, source * block_rows, block_rows, 1)
        return jnp.einsum(
            "tr,ktc->krc", normed_slab, grad_block, preferred_element_type=jnp.float32
        )

    def forward_turn(rotation, loop_state):
        held_block, projected = loop_state
        projected = projected + project(held_block, (position - rotation) % cycle_size)
        held_block = passed_along(held_block, "blk", 1)
        return (held_block, projected)

    empty_sums = jnp.zeros((2, length, columns), jnp.float32)
    held_block, projected = lax.fori_loop(0, cycle_size - 1, forward_turn, (kv_weight, empty_sums))
    projected = projected + project(held_block, (position + 1) % cycle_size)
    raw_pair = projected + kv_bias.astype(jnp.float32)[:, None, :]
    grad_query, grad_pair = attention_backward(raw_pair[0], raw_pair[1], queries, cotangent)
    bias_grad = lax.psum(jnp.sum(grad_pair.astype(jnp.float32), axis=1), ("blk", "dp"))

    def backward_turn(rotation, accumulator):
        accumulator = accumulator + contribute(grad_pair, (position + 1 + rotation) % cycle_size)
        return passed_along(accumulator, "blk", -1)

    accumulator = lax.fori_loop(
        0, cycle_size - 1, backward_turn, jnp.zeros((2, block_rows, columns), jnp.float32)
    )
    accumulator = accumulator + contribute(grad_pair, position)
    grad_weight = lax.psum_scatter(accumulator, "dp", scatter_dimension=1, tiled=True)
    return (grad_query, grad_weight, bias_grad)


def solution(mesh):
    placed = (
        P(("groups", "blk", "dp"), "sub"),
        P(),
        P(("groups", "blk", "dp"), "sub"),
        P(("groups", "blk", "dp"), "sub"),
        P(None, "blk", "sub"),
        P(None, "sub"),
    )
    return jax.shard_map(
        local,
        mesh=mesh,
        in_specs=placed,
        out_specs=(
            P(("groups", "blk", "dp"), "sub"),
            P(None, ("groups", "blk", "dp"), "sub"),
            P("groups", "sub"),
        ),
        check_vma=False,
    )
```

profile of v0, /device:TPU:0, one launch (start us, length us, event | category | flops | bytes accessed | tf_op | source)
XLA Modules:
  0.0 373.7 jit_solution(10895773389723506124)
XLA Ops:
  8.7 1.1 copy.27
  11.8 11.9 %all-gather.2.cloned.1.call-done = bf16[256,5120]{1,0:T(8,128)(2,1)} async-done(((bf16[256,2560]{1,0:T(8,128)(2,1)}), bf16[256,5120]{1,0:T(8,128)(2,1)}) %all-gather.2.cloned.1.call-update) | async-done | bytes 2621456 | tf_op jit(solution)/shard_map/all_gather | solution.py:98
  23.7 2.5 fusion.10
  26.2 2.3 fusion.12
  28.5 96.4 %while.34 = (s32[]{:T(128)}, bf16[2,1280,256]{2,1,0:T(8,128)(2,1)S(1)}, f32[2,256,256]{2,1,0:T(8,128)S(1)}, s32[]{:T(128)}, bf16[256,5120]{1,0:T(8,128)(2,1)}, /...) while((s32[]{:T(128)}, ...), condition=%wide.region_2.3_spmd.clone, body=%wide.region_1.2_spmd.clone.sunk | while | flops 335806496 | bytes 10879306 | solution.py:125
  28.6 1.8 collective-permute-start.1
  30.4 1.7 fusion.78
  32.0 29.4 %collective-permute-done.1 = bf16[2,1280,256]{2,1,0:T(8,128)(2,1)S(1)} collective-permute-done((bf16[2,1280,256]{2,1,0:T(8,128)(2,1)S(1)}, bf16[2,1280,256]{2,1,0:T(8,128)(2,1)S(1)}, u32[]{:S(2)}, u32[]{:S(2)}) %collective-permute-start.1) | collective-permute-done | bytes 1310752 | tf_op jit(solution)/shard_map/while/body/eval_jaxpr/ppermute | solution.py:16
  61.6 1.7 fusion.78
  63.3 30.3 %collective-permute-done.1 = bf16[2,1280,256]{2,1,0:T(8,128)(2,1)S(1)} collective-permute-done((bf16[2,1280,256]{2,1,0:T(8,128)(2,1)S(1)}, bf16[2,1280,256]{2,1,0:T(8,128)(2,1)S(1)}, u32[]{:S(2)}, u32[]{:S(2)}) %collective-permute-start.1) | collective-permute-done | bytes 1310752 | tf_op jit(solution)/shard_map/while/body/eval_jaxpr/ppermute | solution.py:16
  93.8 1.7 fusion.78
  95.5 29.4 %collective-permute-done.1 = bf16[2,1280,256]{2,1,0:T(8,128)(2,1)S(1)} collective-permute-done((bf16[2,1280,256]{2,1,0:T(8,128)(2,1)S(1)}, bf16[2,1280,256]{2,1,0:T(8,128)(2,1)S(1)}, u32[]{:S(2)}, u32[]{:S(2)}) %collective-permute-start.1) | collective-permute-done | bytes 1310752 | tf_op jit(solution)/shard_map/while/body/eval_jaxpr/ppermute | solution.py:16
  125.1 1.7 fusion.26
  128.3 3.7 fusion.55
  131.9 3.0 fusion.31
  134.9 3.6 fusion.27
  139.0 178.9 %while.33 = (s32[]{:T(128)}, f32[2,1280,256]{2,1,0:T(8,128)S(1)}, s32[]{:T(128)}, bf16[256,5120]{1,0:T(8,128)(2,1)}, bf16[2,256,256]{2,1,0:T(8,128)(2,1)S(1)}, /...) while((s32[]{:T(128)}, f32[2,1280,256]{2,1,0:T(8,128)S(1)}, ...), condition=%wide.region_7.8_spmd, body=%wide.region_6.7_spmd.sunk | while | flops 336199712 | bytes 16646464 | solution.py:135
  139.0 3.2 fusion.75
  142.2 56.7 %collective-permute-done = f32[2,1280,256]{2,1,0:T(8,128)S(1)} collective-permute-done((f32[2,1280,256]{2,1,0:T(8,128)}, f32[2,1280,256]{2,1,0:T(8,128)S(1)}, u32[]{:S(2)}, u32[]{:S(2)}) %collective-permute-start) | collective-permute-done | bytes 2621472 | tf_op jit(solution)/shard_map/while/body/eval_jaxpr/ppermute | solution.py:16
  198.9 3.2 fusion.75
  202.1 2.1 collective-permute-start
  204.2 53.7 %collective-permute-done = f32[2,1280,256]{2,1,0:T(8,128)S(1)} collective-permute-done((f32[2,1280,256]{2,1,0:T(8,128)}, f32[2,1280,256]{2,1,0:T(8,128)S(1)}, u32[]{:S(2)}, u32[]{:S(2)}) %collective-permute-start) | collective-permute-done | bytes 2621472 | tf_op jit(solution)/shard_map/while/body/eval_jaxpr/ppermute | solution.py:16
  257.8 3.2 fusion.75
  261.0 4.2 %collective-permute-start = (f32[2,1280,256]{2,1,0:T(8,128)}, f32[2,1280,256]{2,1,0:T(8,128)S(1)}, u32[]{:S(2)}, u32[]{:S(2)}) collective-permute-start(f32[2,1280,256]{2,1,0:T(8,128)} %fusion.75), channel_id=1, source_target_pairs={{4,0},{8,4},{12,8},{0,12},{5,1},{9,5},{13,9},{1,13},{6,2},{10,6},{... | collective-permute-start | bytes 7864328 | tf_op jit(solution)/shard_map/while/body/eval_jaxpr/ppermute | solution.py:16
  265.2 52.7 %collective-permute-done = f32[2,1280,256]{2,1,0:T(8,128)S(1)} collective-permute-done((f32[2,1280,256]{2,1,0:T(8,128)}, f32[2,1280,256]{2,1,0:T(8,128)S(1)}, u32[]{:S(2)}, u32[]{:S(2)}) %collective-permute-start) | collective-permute-done | bytes 2621472 | tf_op jit(solution)/shard_map/while/body/eval_jaxpr/ppermute | solution.py:16
  317.9 2.1 copy.38
  320.1 4.0 %fusion.13 = f32[2,1280,256]{1,2,0:T(8,128)} fusion(f32[2,1280,256]{1,2,0:T(8,128)} %copy.38, bf16[256,5120]{1,0:T(8,128)(2,1)} %get-tuple-element.473, s32[]{:T(128)S(6)} %select_n.74, bf16[1,256,256]{1,2,0:T(8,128)(2,1)S(1)} %bitcast.125, bf16[1,256,256]{1,2,0:T(8,128)(2,1)S(1)} %bitcast.122), kind=kOutput, calls=%fused_computation.18 | convolution fusion | flops 336330752 | bytes 6160388 | tf_op jit(solution)/shard_map/tr,ktc->krc/dot_general | solution.py:114
  325.0 5.0 %convolution_convert_fusion = bf16[2,128,5,256]{3,1,2,0:T(8,128)(2,1)S(1)} fusion(bf16[256,2,128,1]{0,2,3,1:T(8,128)(2,1)S(1)} %copy-done.7, f32[2,256,256,5]{2,1,3,0:T(8,128)} %copy-done.2, f32[2,5,256,256]{2,3,1,0:T(8,128)} %get-tuple-element.336, f32[2,5,256]{2,1,0:T(8,128)S(1)} %get-tuple-element.335), kind=kOutput, calls=%fused_computation.27 | convolution fusion | flops 172690176 | bytes 6039552 | tf_op jit(solution)/shard_map/kgts,skd->tkgd/dot_general | solution.py:78
  330.0 1.1 copy.39
  331.2 23.0 %psum.7 = f32[2,256]{1,0:T(2,128)} all-reduce(f32[2,256]{1,0:T(2,128)S(1)} %convert_reduce_fusion), channel_id=1, replica_groups=mesh['groups'=2,'blk'=4,'dp'=2,'sub'=2] {'blk','dp'}, use_global_device_ids=true, to_apply=%region_10.11 | all-reduce | flops 512 | bytes 4096 | tf_op jit(solution)/shard_map/psum | solution.py:129
  354.2 9.8 %reduce-scatter.2.cloned.1.call-done = f32[2,640,256]{1,2,0:T(8,128)} async-done(((f32[2,1280,256]{1,2,0:T(8,128)}), f32[2,640,256]{1,2,0:T(8,128)}) %reduce-scatter.2.cloned.1.call-update) | async-done | bytes 1310736 | tf_op jit(solution)/shard_map/reduce_scatter | solution.py:139
  364.0 2.8 copy.40
  (54 shorter events, 7.0 us)
Async XLA Ops:
  7.2 0.8 copy-start.10
  7.2 0.9 copy-start.9
  7.2 1.5 copy-start.5
  7.2 2.5 copy-start.6
  7.2 16.5 %all-gather.2.cloned.1.call-start = ((), (), s32[]{:S(2)}) async-start(), calls=%async_computation.1 | async-start | bytes 3932160 | tf_op jit(solution)/shard_map/all_gather | solution.py:98
  7.9 356.1 %reduce-scatter.2.cloned.1.call-start = ((), (), s32[]{:S(2)}) async-start(), calls=%async_computation.2 | async-start | bytes 3932160 | tf_op jit(solution)/shard_map/reduce_scatter | solution.py:139
  9.7 16.4 %copy-start.8 = (f32[5120]{0:T(1024)S(1)}, f32[5120]{0:T(1024)}, u32[]{:S(2)}) copy-start(f32[5120]{0:T(1024)} %convert_element_type.37) | copy-start | bytes 61444
  23.7 2.5 copy-start.1
  26.2 2.3 copy-start
  28.6 32.9 %collective-permute-start.1 = (bf16[2,1280,256]{2,1,0:T(8,128)(2,1)S(1)}, bf16[2,1280,256]{2,1,0:T(8,128)(2,1)S(1)}, u32[]{:S(2)}, u32[]{:S(2)}) collective-permute-start(bf16[2,1280,256]{2,1,0:T(8,128)(2,1)S(1)} %copy.61), channel_id=1, source_target_pairs={{12,0},{0,4},{4,8},{8,12},{13,1},{1,5},{5,9},{9,13},{14,2},{2,6},{... | collective-permute-start | bytes 3932168 | tf_op jit(solution)/shard_map/while/body/eval_jaxpr/ppermute | solution.py:16
  61.5 32.1 %collective-permute-start.1 = (bf16[2,1280,256]{2,1,0:T(8,128)(2,1)S(1)}, bf16[2,1280,256]{2,1,0:T(8,128)(2,1)S(1)}, u32[]{:S(2)}, u32[]{:S(2)}) collective-permute-start(bf16[2,1280,256]{2,1,0:T(8,128)(2,1)S(1)} %copy.61), channel_id=1, source_target_pairs={{12,0},{0,4},{4,8},{8,12},{13,1},{1,5},{5,9},{9,13},{14,2},{2,6},{... | collective-permute-start | bytes 3932168 | tf_op jit(solution)/shard_map/while/body/eval_jaxpr/ppermute | solution.py:16
  93.7 31.2 %collective-permute-start.1 = (bf16[2,1280,256]{2,1,0:T(8,128)(2,1)S(1)}, bf16[2,1280,256]{2,1,0:T(8,128)(2,1)S(1)}, u32[]{:S(2)}, u32[]{:S(2)}) collective-permute-start(bf16[2,1280,256]{2,1,0:T(8,128)(2,1)S(1)} %copy.61), channel_id=1, source_target_pairs={{12,0},{0,4},{4,8},{8,12},{13,1},{1,5},{5,9},{9,13},{14,2},{2,6},{... | collective-permute-start | bytes 3932168 | tf_op jit(solution)/shard_map/while/body/eval_jaxpr/ppermute | solution.py:16
  125.1 1.8 copy-start.3
  127.4 7.5 %copy-start.2 = (f32[2,256,256,5]{2,1,3,0:T(8,128)}, f32[2,256,256,5]{2,1,3,0:T(8,128)S(1)}, u32[]{:S(2)}) copy-start(f32[2,256,256,5]{2,1,3,0:T(8,128)S(1)} %fusion.56) | copy-start | bytes 7864324
  134.9 3.7 copy-start.4
  142.2 56.7 %collective-permute-start = (f32[2,1280,256]{2,1,0:T(8,128)}, f32[2,1280,256]{2,1,0:T(8,128)S(1)}, u32[]{:S(2)}, u32[]{:S(2)}) collective-permute-start(f32[2,1280,256]{2,1,0:T(8,128)} %fusion.75), channel_id=1, source_target_pairs={{4,0},{8,4},{12,8},{0,12},{5,1},{9,5},{13,9},{1,13},{6,2},{10,6},{... | collective-permute-start | bytes 7864328 | tf_op jit(solution)/shard_map/while/body/eval_jaxpr/ppermute | solution.py:16
  202.1 55.8 %collective-permute-start = (f32[2,1280,256]{2,1,0:T(8,128)}, f32[2,1280,256]{2,1,0:T(8,128)S(1)}, u32[]{:S(2)}, u32[]{:S(2)}) collective-permute-start(f32[2,1280,256]{2,1,0:T(8,128)} %fusion.75), channel_id=1, source_target_pairs={{4,0},{8,4},{12,8},{0,12},{5,1},{9,5},{13,9},{1,13},{6,2},{10,6},{... | collective-permute-start | bytes 7864328 | tf_op jit(solution)/shard_map/while/body/eval_jaxpr/ppermute | solution.py:16
  261.0 56.9 %collective-permute-start = (f32[2,1280,256]{2,1,0:T(8,128)}, f32[2,1280,256]{2,1,0:T(8,128)S(1)}, u32[]{:S(2)}, u32[]{:S(2)}) collective-permute-start(f32[2,1280,256]{2,1,0:T(8,128)} %fusion.75), channel_id=1, source_target_pairs={{4,0},{8,4},{12,8},{0,12},{5,1},{9,5},{13,9},{1,13},{6,2},{10,6},{... | collective-permute-start | bytes 7864328 | tf_op jit(solution)/shard_map/while/body/eval_jaxpr/ppermute | solution.py:16
  324.1 0.9 copy-start.7
Sparse Core Ops, SparseCore 0:
  9.6 14.0 all-gather.1
  324.2 39.7 reduce-scatter.1
where the time goes:
time: 374 us
  waiting for transfers between devices  275 us (74%)
  matrix products  36 us (10%)
  blocking collectives  23 us (6%)
  between operations  14.3 us (4%)
  local copies, waits for them, and re-layouts  9.88 us (3%)
  starting transfers between devices  8.24 us (2%)
  other arithmetic  7.48 us (2%)
    ppermute x6, waiting for transfers between devices, passed_along(): return lax.ppermute(block, axis, route)  252 us
    psum x1, blocking collectives, local(): lax.psum(jnp.sum(grad_pair.astype(jnp.float32), axis=1), ('blk', 'dp'))  23 us
    dot_general x4, matrix products, contribute(): jnp.einsum('tr,ktc->krc', normed_slab, grad_block, preferred_element_type...  13.5 us
    all_gather x1, waiting for transfers between devices, local(): full_features = lax.all_gather(activations, 'sub', axis=1, tiled=True)  11.9 us
    reduce_scatter x1, waiting for transfers between devices, local(): lax.psum_scatter(accumulator, 'dp', scatter_dimension=1, tiled=True)  9.84 us
    ppermute x6, starting transfers between devices, passed_along(): return lax.ppermute(block, axis, route)  8.16 us
  transfers between devices with their start and end apart: 8, of which 8 were waited for; matrix products, arithmetic and copies ran while one was open for 4% of the time, Pallas kernels for 0%

commit v1 on v0

--- a/solution.py
+++ b/solution.py
@@ -8,20 +8,6 @@
 
 EPSILON = 1e-06
 ROPE_BASE = 1000000.0
-
-
-def passed_along(block, axis, distance):
-    devices = range(lax.axis_size(axis))
-    route = [((i - distance) % len(devices), i) for i in devices]
-    return lax.ppermute(block, axis, route)
-
-
-def normalize(activations, norm_gain):
-    wide_values = activations.astype(jnp.float32)
-    mean_square = jnp.mean(wide_values * wide_values, -1, keepdims=True)
-    return (wide_values * lax.rsqrt(mean_square + EPSILON) * norm_gain.astype(jnp.float32)).astype(
-        jnp.bfloat16
-    )
 
 
 def rope_tables(length, head_size):
@@ -88,55 +74,74 @@
     grad_key = grad_rotated * cosine_table[:, None, :] + rotate_back(
         grad_rotated * sine_table[:, None, :]
     )
-    grad_pair = jnp.stack([grad_key.reshape(length, -1), grad_value.reshape(length, -1)]).astype(
-        jnp.bfloat16
-    )
-    return (grad_query, grad_pair)
+    grad_pair = jnp.concatenate([grad_key.reshape(length, -1), grad_value.reshape(length, -1)], -1)
+    return (grad_query, grad_pair.astype(jnp.bfloat16))
+
+
+def other_core(block):
+    return lax.ppermute(block, "sub", [(0, 1), (1, 0)])
 
 
 def local(activations, norm_gain, queries, cotangent, kv_weight, kv_bias):
-    full_features = lax.all_gather(activations, "sub", axis=1, tiled=True)
-    normed = normalize(full_features, norm_gain)
-    cycle_size = lax.axis_size("blk")
-    position = lax.axis_index("blk")
+    blocks, replicas = lax.axis_size("blk"), lax.axis_size("dp")
+    sequences = blocks * replicas
+    group, block, replica = lax.axis_index("groups"), lax.axis_index("blk"), lax.axis_index("dp")
+    core = lax.axis_index("sub")
+    features = activations.shape[1]
     block_rows = kv_weight.shape[1]
     columns = kv_weight.shape[2]
-    length = activations.shape[0]
+    share = block_rows // replicas
 
-    def project(weight_block, source):
-        normed_slab = lax.dynamic_slice_in_dim(normed, source * block_rows, block_rows, 1)
-        return jnp.einsum(
-            "tr,krc->ktc", normed_slab, weight_block, preferred_element_type=jnp.float32
-        )
+    piece = lax.dynamic_slice(kv_weight, (group, replica * share, 0), (1, share, columns))[0]
+    weight = lax.all_gather(piece, ("groups", "blk", "dp"), axis=0, tiled=True)
+    weight = weight.reshape(2, -1, columns)
 
-    def contribute(grad_block, source):
-        normed_slab = lax.dynamic_slice_in_dim(normed, source * block_rows, block_rows, 1)
-        return jnp.einsum(
-            "tr,ktc->krc", normed_slab, grad_block, preferred_element_type=jnp.float32
-        )
+    wide_values = activations.astype(jnp.float32)
+    square_sum = jnp.sum(wide_values * wide_values, -1, keepdims=True)
+    square_sum = square_sum + other_core(square_sum)
+    gain = lax.dynamic_slice_in_dim(norm_gain, core * features, features, 0).astype(jnp.float32)
+    normed = (wide_values * lax.rsqrt(square_sum / (2 * features) + EPSILON) * gain).astype(
+        jnp.bfloat16
+    )
+    normed_other = other_core(normed)
 
-    def forward_turn(rotation, loop_state):
-        held_block, projected = loop_state
-        projected = projected + project(held_block, (position - rotation) % cycle_size)
-        held_block = passed_along(held_block, "blk", 1)
-        return (held_block, projected)
+    half = sequences // 2
+    number = block * replicas + replica
 
-    empty_sums = jnp.zeros((2, length, columns), jnp.float32)
-    held_block, projected = lax.fori_loop(0, cycle_size - 1, forward_turn, (kv_weight, empty_sums))
-    projected = projected + project(held_block, (position + 1) % cycle_size)
-    raw_pair = projected + kv_bias.astype(jnp.float32)[:, None, :]
+    def place(index, on_core):
+        return ((index // replicas) * replicas + index % replicas) * 2 + on_core
+
+    slabs = []
+    for turn in range(half):
+        route = []
+        for source in range(sequences):
+            for on_core in range(2):
+                goal = half * on_core + (turn + source // 2) % half
+                route.append((place(source, on_core), place(goal, source % 2)))
+        slab = (turn + number // 2) % half
+        sent = lax.dynamic_slice_in_dim(normed, slab * share, share, 1)
+        slabs.append(lax.ppermute(sent, ("blk", "dp", "sub"), route))
+    slabs_own = jnp.stack(slabs)
+    slabs_other = other_core(slabs_own)
+
+    def project(values, rows):
+        part = lax.dynamic_slice_in_dim(weight, rows * features, features, 1)
+        return jnp.einsum("tr,krc->ktc", values, part, preferred_element_type=jnp.float32)
+
+    raw_pair = project(normed, core) + project(normed_other, 1 - core)
+    raw_pair = raw_pair + kv_bias.astype(jnp.float32)[:, None, :]
     grad_query, grad_pair = attention_backward(raw_pair[0], raw_pair[1], queries, cotangent)
-    bias_grad = lax.psum(jnp.sum(grad_pair.astype(jnp.float32), axis=1), ("blk", "dp"))
 
-    def backward_turn(rotation, accumulator):
-        accumulator = accumulator + contribute(grad_pair, (position + 1 + rotation) % cycle_size)
-        return passed_along(accumulator, "blk", -1)
-
-    accumulator = lax.fori_loop(
-        0, cycle_size - 1, backward_turn, jnp.zeros((2, block_rows, columns), jnp.float32)
-    )
-    accumulator = accumulator + contribute(grad_pair, position)
-    grad_weight = lax.psum_scatter(accumulator, "dp", scatter_dimension=1, tiled=True)
+    everyone = lax.all_gather(grad_pair, ("blk", "dp"), axis=0)
+    bias_grad = jnp.sum(everyone.astype(jnp.float32), axis=(0, 1)).reshape(2, columns)
+    paired = everyone.reshape(half, 2, -1, 2 * columns)
+    order = (number % half - jnp.arange(half)) % half
+    grads_own = jnp.take(lax.dynamic_index_in_dim(paired, core, 1, False), order, axis=0)
+    grads_other = jnp.take(lax.dynamic_index_in_dim(paired, 1 - core, 1, False), order, axis=0)
+    grad_weight = jnp.einsum(
+        "ntr,ntc->rc", slabs_own, grads_own, preferred_element_type=jnp.float32
+    ) + jnp.einsum("ntr,ntc->rc", slabs_other, grads_other, preferred_element_type=jnp.float32)
+    grad_weight = jnp.moveaxis(grad_weight.reshape(share, 2, columns), 1, 0)
     return (grad_query, grad_weight, bias_grad)
 
 

time: 374 us -> 206 us (0.55)
  the two profiles are of different devices: /device:TPU:0 before, /device:TPU:9 now
where the time goes in v1:
time: 206 us
  waiting for transfers between devices  123 us (60%)
  matrix products  27.8 us (13%)
  starting transfers between devices  19.9 us (10%)
  between operations  14.5 us (7%)
  local copies, waits for them, and re-layouts  13.8 us (7%)
  other arithmetic  6.76 us (3%)
    all_gather x1, waiting for transfers between devices, local(): weight = lax.all_gather(piece, ('groups', 'blk', 'dp'), axis=0, tiled=True)  80.1 us
    ppermute x4, waiting for transfers between devices, local(): slabs.append(lax.ppermute(sent, ('blk', 'dp', 'sub'), route))  42.9 us
    ppermute x4, starting transfers between devices, local(): slabs.append(lax.ppermute(sent, ('blk', 'dp', 'sub'), route))  12.7 us
    ppermute x3, starting transfers between devices, other_core(): return lax.ppermute(block, 'sub', [(0, 1), (1, 0)])  7.13 us
    dot_general x2, matrix products, project(): jnp.einsum('tr,krc->ktc', values, part, preferred_element_type=jnp.float32)  5.99 us
    dot_general x1, matrix products, attention_backward(): jnp.einsum('kgts,skd->tkgd', grad_scores, rotated_keys, preferred_element...  5.03 us
    dot_general x1, matrix products, attention_backward(): jnp.einsum('kgts,tkgd->skd', grad_scores, query_heads, preferred_element_...  4.98 us
  transfers between devices with their start and end apart: 9, of which 6 were waited for; matrix products, arithmetic and copies ran while one was open for 10% of the time, Pallas kernels for 0%

profile of v1, /device:TPU:9, one launch (start us, length us, event | category | flops | bytes accessed | tf_op | source)
XLA Modules:
  0.0 205.8 jit_solution(11997404785414373978)
XLA Ops:
  7.3 1.2 copy-done
  8.5 0.7 constant_dynamic-slice_fusion.4
  9.3 1.7 fusion.2
  11.0 0.7 collective-permute-start
  11.7 0.8 dynamic-slice_convert_fusion
  12.5 1.4 fusion.4
  14.5 1.3 copy.50
  16.2 80.1 %all-gather.6.cloned.1.call-done = bf16[1,10240,256]{2,1,0:T(8,128)(2,1)} async-done(((bf16[1,640,256]{2,1,0:T(8,128)(2,1)}), bf16[1,10240,256]{2,1,0:T(8,128)(2,1)}) %all-gather.6.cloned.1.call-update) | async-done | bytes 5242896 | tf_op jit(solution)/shard_map/all_gather | solution.py:96
  96.3 3.0 %fusion.10 = f32[2,256,256]{2,1,0:T(8,128)S(1)} fusion(bf16[2,5120,256]{2,1,0:T(8,128)(2,1)} %bitcast.134, s32[]{:T(128)S(6)} %select_n.81, bf16[256,2560]{1,0:T(8,128)(2,1)} %fusion.4), kind=kOutput, calls=%fused_computation.19 | convolution fusion | flops 671088640 | bytes 4456452 | tf_op jit(solution)/shard_map/tr,krc->ktc/dot_general | solution.py:129
  99.3 3.0 %fusion.33 = f32[2,256,256]{1,2,0:T(8,128)S(1)} fusion(f32[2,256,256]{2,1,0:T(8,128)S(1)} %fusion.10, bf16[256,2560]{1,0:T(8,128)(2,1)} %collective-permute-done.1, bf16[2,5120,256]{2,1,0:T(8,128)(2,1)} %bitcast.135, s32[]{:T(128)S(6)} %select_n.82, f32[2,256]{1,0:T(2,128)S(1)} %convert_element_type.46), kind=kOutput, calls=%fused_computation.39 | convolution fusion | flops 671350784 | bytes 4982788 | tf_op jit(solution)/shard_map/tr,krc->ktc/dot_general | solution.py:129
  102.4 2.0 fusion.72
  104.5 2.5 %fusion.71 = (f32[2,5,256]{2,1,0:T(8,128)S(1)}, f32[2,5,256,256]{2,3,1,0:T(8,128)}) fusion(pred[256,256]{0,1:T(8,128)(4,1)S(1)} %iota_compare_fusion, bf16[256,2,128,1]{0,2,3,1:T(8,128)(2,1)S(1)} %fusion.56, bf16[256,2,5,128]{0,3,2,1:T(8,128)(2,1)S(1)} %bitcast.117), kind=kOutput, calls=%fused_computation.95 | convolution fusion | flops 170393856 | bytes 3483648 | tf_op jit(solution)/shard_map/sub | solution.py:56
  107.0 2.3 %fusion.42 = bf16[2,256,128]{1,2,0:T(8,128)(2,1)S(1)} fusion(bf16[256,2,5,128]{0,3,2,1:T(8,128)(2,1)S(1)} %bitcast.112, f32[2,5,256,256]{2,3,1,0:T(8,128)} %get-tuple-element.29, f32[2,5,256]{2,1,0:T(8,128)S(1)} %get-tuple-element.28), kind=kOutput, calls=%fused_computation.42 | convolution fusion | flops 169148416 | bytes 3418112 | tf_op jit(solution)/shard_map/kgts,tkgd->skd/dot_general | solution.py:71
  109.4 5.0 %fusion.38 = f32[2,256,128]{1,2,0:T(8,128)S(1)} fusion(bf16[256,2,5,128]{0,3,2,1:T(8,128)(2,1)S(1)} %bitcast.118, f32[2,256,256,5]{2,1,3,0:T(8,128)} %fusion.72, f32[2,5,256,256]{2,3,1,0:T(8,128)} %get-tuple-element.29, f32[2,5,256]{2,1,0:T(8,128)S(1)} %get-tuple-element.28), kind=kOutput, calls=%fused_computation.40 | convolution fusion | flops 172362496 | bytes 6170624 | tf_op jit(solution)/shard_map/kgts,tkgd->skd/dot_general | solution.py:68
  115.5 1.4 constant_dynamic-slice_fusion.3
  116.9 4.6 %collective-permute-start.5 = (bf16[256,640]{1,0:T(8,128)(2,1)S(1)}, bf16[256,640]{1,0:T(8,128)(2,1)S(1)}, u32[]{:S(2)}, u32[]{:S(2)}) collective-permute-start(bf16[256,640]{1,0:T(8,128)(2,1)S(1)} %get-tuple-element.19), channel_id=1, source_target_pairs={{0,6},{1,14},{2,7},{3,15},{4,0},{5,8},{6,1},{7,9},{8,2},{9,10},{10... | collective-permute-start | bytes 983048 | tf_op jit(solution)/shard_map/ppermute | solution.py:123
  121.5 0.9 collective-permute-start.4
  122.4 3.7 %collective-permute-start.3 = (bf16[256,640]{1,0:T(8,128)(2,1)S(1)}, bf16[256,640]{1,0:T(8,128)(2,1)S(1)}, u32[]{:S(2)}, u32[]{:S(2)}) collective-permute-start(bf16[256,640]{1,0:T(8,128)(2,1)S(1)} %get-tuple-element.21), channel_id=1, source_target_pairs={{0,2},{1,10},{2,3},{3,11},{4,4},{5,12},{6,5},{7,13},{8,6},{9,14},{... | collective-permute-start | bytes 983048 | tf_op jit(solution)/shard_map/ppermute | solution.py:123
  126.1 3.5 %collective-permute-start.2 = (bf16[256,640]{1,0:T(8,128)(2,1)S(1)}, bf16[256,640]{1,0:T(8,128)(2,1)S(1)}, u32[]{:S(2)}, u32[]{:S(2)}) collective-permute-start(bf16[256,640]{1,0:T(8,128)(2,1)S(1)} %get-tuple-element.18), channel_id=1, source_target_pairs={{0,0},{1,8},{2,1},{3,9},{4,2},{5,10},{6,3},{7,11},{8,4},{9,12},{10... | collective-permute-start | bytes 983048 | tf_op jit(solution)/shard_map/ppermute | solution.py:123
  129.6 3.3 %collective-permute-done.5 = bf16[256,640]{1,0:T(8,128)(2,1)S(1)} collective-permute-done((bf16[256,640]{1,0:T(8,128)(2,1)S(1)}, bf16[256,640]{1,0:T(8,128)(2,1)S(1)}, u32[]{:S(2)}, u32[]{:S(2)}) %collective-permute-start.5) | collective-permute-done | bytes 327712 | tf_op jit(solution)/shard_map/ppermute | solution.py:123
  132.9 11.8 %collective-permute-done.4 = bf16[256,640]{1,0:T(8,128)(2,1)S(1)} collective-permute-done((bf16[256,640]{1,0:T(8,128)(2,1)S(1)}, bf16[256,640]{1,0:T(8,128)(2,1)S(1)}, u32[]{:S(2)}, u32[]{:S(2)}) %collective-permute-start.4) | collective-permute-done | bytes 327712 | tf_op jit(solution)/shard_map/ppermute | solution.py:123
  144.7 13.7 %collective-permute-done.3 = bf16[256,640]{1,0:T(8,128)(2,1)S(1)} collective-permute-done((bf16[256,640]{1,0:T(8,128)(2,1)S(1)}, bf16[256,640]{1,0:T(8,128)(2,1)S(1)}, u32[]{:S(2)}, u32[]{:S(2)}) %collective-permute-start.3) | collective-permute-done | bytes 327712 | tf_op jit(solution)/shard_map/ppermute | solution.py:123
  158.4 14.1 %collective-permute-done.2 = bf16[256,640]{1,0:T(8,128)(2,1)S(1)} collective-permute-done((bf16[256,640]{1,0:T(8,128)(2,1)S(1)}, bf16[256,640]{1,0:T(8,128)(2,1)S(1)}, u32[]{:S(2)}, u32[]{:S(2)}) %collective-permute-start.2) | collective-permute-done | bytes 327712 | tf_op jit(solution)/shard_map/ppermute | solution.py:123
  172.5 1.3 pad_maximum_fusion
  173.8 6.1 %collective-permute-start.6 = (bf16[4,256,640]{2,1,0:T(8,128)(2,1)}, bf16[4,256,640]{2,1,0:T(8,128)(2,1)}, u32[]{:S(2)}, u32[]{:S(2)}) collective-permute-start(bf16[4,256,640]{2,1,0:T(8,128)(2,1)} %pad_maximum_fusion), channel_id=1, source_target_pairs={{0,1},{1,0},{2,3},{3,2},{4,5},{5,4},{6,7},{7,6},{8,9},{9,8},{10,11... | collective-permute-start | bytes 3932168 | tf_op jit(solution)/shard_map/ppermute | solution.py:82
  179.9 5.0 %convolution_convert_fusion = bf16[2,128,5,256]{3,1,2,0:T(8,128)(2,1)S(1)} fusion(bf16[256,2,128,1]{0,2,3,1:T(8,128)(2,1)S(1)} %fusion.56, f32[2,256,256,5]{2,1,3,0:T(8,128)} %fusion.72, f32[2,5,256,256]{2,3,1,0:T(8,128)} %get-tuple-element.29, f32[2,5,256]{2,1,0:T(8,128)S(1)} %get-tuple-element.28), kind=kOutput, calls=%fused_computation.25 | convolution fusion | flops 172690176 | bytes 6039552 | tf_op jit(solution)/shard_map/kgts,skd->tkgd/dot_general | solution.py:64
  184.9 1.1 copy.66
  186.0 1.8 dynamic-slice_bitcast_fusion.1
  187.8 1.6 gather_fusion.1
  190.0 2.8 %convolution_bitcast_fusion = f32[640,512]{0,1:T(8,128)S(1)} fusion(bf16[4,256,640]{2,1,0:T(8,128)(2,1)} %collective-permute-done.6, bf16[4,256,512]{2,1,0:T(8,128)(2,1)} %gather_fusion.1, pred[4]{0:T(512)(128)(4,1)S(1)} %compare_and_fusion), kind=kOutput, calls=%fused_computation.22 | convolution fusion | flops 671612928 | bytes 3670020 | tf_op jit(solution)/shard_map/ntr,ntc->rc/dot_general | solution.py:143
  192.9 2.2 %fusion.13 = f32[640,512]{0,1:T(8,128)} fusion(f32[640,512]{0,1:T(8,128)S(1)} %convolution_bitcast_fusion, bf16[4,256,512]{2,1,0:T(8,128)(2,1)S(1)} %gather_fusion, pred[4]{0:T(512)(128)(4,1)S(1)} %compare_and_fusion, bf16[1,256,640]{2,1,0:T(8,128)(2,1)S(1)} %bitcast.123, bf16[1,256,640]{2,1,0:T(8,128)(2,1)S(1)} %bitcast.125, ...), kind=kOutput, calls=%fused_computation.24 | convolution fusion | flops 673906688 | bytes 4980740 | tf_op jit(solution)/shard_map/ntr,ntc->rc/dot_general | solution.py:141
  195.1 2.9 %copy.65 = f32[640,2,256]{2,0,1:T(8,128)} copy(f32[640,2,256]{0,2,1:T(8,128)} %bitcast.116) | data formatting | bytes 2621440 | tf_op jit(solution)/shard_map/reshape | solution.py:144
  (57 shorter events, 3.9 us)
Async XLA Ops:
  7.2 1.3 copy-start
  7.2 5.3 %copy-start.2 = (bf16[256,2560]{1,0:T(8,128)(2,1)S(1)}, bf16[256,2560]{1,0:T(8,128)(2,1)}, u32[]{:S(2)}) copy-start(bf16[256,2560]{1,0:T(8,128)(2,1)} %param.8) | copy-start | bytes 3932164
  7.2 7.1 %copy-start.12 = (bf16[2,256]{1,0:T(2,128)(2,1)S(1)}, bf16[2,256]{1,0:T(2,128)(2,1)}, u32[]{:S(2)}) copy-start(bf16[2,256]{1,0:T(2,128)(2,1)} %param.13) | copy-start | bytes 3076
  7.2 7.1 %copy-start.3 = (bf16[256,1280]{1,0:T(8,128)(2,1)S(1)}, bf16[256,1280]{1,0:T(8,128)(2,1)}, u32[]{:S(2)}) copy-start(bf16[256,1280]{1,0:T(8,128)(2,1)} %param.11) | copy-start | bytes 1966084
  7.2 89.1 %all-gather.6.cloned.1.call-start = ((), (), s32[]{:S(2)}) async-start(), calls=%async_computation.1 | async-start | bytes 5570560 | tf_op jit(solution)/shard_map/all_gather | solution.py:96
  9.3 176.7 %all-gather.4.cloned.1.call-start = ((), (), s32[]{:S(2)}) async-start(), calls=%async_computation | async-start | bytes 2359296 | tf_op jit(solution)/shard_map/all_gather | solution.py:135
  11.0 1.6 collective-permute-start
  14.0 85.3 %collective-permute-start.1 = (bf16[256,2560]{1,0:T(8,128)(2,1)}, bf16[256,2560]{1,0:T(8,128)(2,1)}, u32[]{:S(2)}, u32[]{:S(2)}) collective-permute-start(bf16[256,2560]{1,0:T(8,128)(2,1)} %fusion.4), channel_id=1, source_target_pairs={{0,1},{1,0},{2,3},{3,2},{4,5},{5,4},{6,7},{7,6},{8,9},{9,8},{10,11... | collective-permute-start | bytes 3932168 | tf_op jit(solution)/shard_map/ppermute | solution.py:82
  116.9 16.0 %collective-permute-start.5 = (bf16[256,640]{1,0:T(8,128)(2,1)S(1)}, bf16[256,640]{1,0:T(8,128)(2,1)S(1)}, u32[]{:S(2)}, u32[]{:S(2)}) collective-permute-start(bf16[256,640]{1,0:T(8,128)(2,1)S(1)} %get-tuple-element.19), channel_id=1, source_target_pairs={{0,6},{1,14},{2,7},{3,15},{4,0},{5,8},{6,1},{7,9},{8,2},{9,10},{10... | collective-permute-start | bytes 983048 | tf_op jit(solution)/shard_map/ppermute | solution.py:123
  121.5 23.2 %collective-permute-start.4 = (bf16[256,640]{1,0:T(8,128)(2,1)S(1)}, bf16[256,640]{1,0:T(8,128)(2,1)S(1)}, u32[]{:S(2)}, u32[]{:S(2)}) collective-permute-start(bf16[256,640]{1,0:T(8,128)(2,1)S(1)} %get-tuple-element.20), channel_id=1, source_target_pairs={{0,4},{1,12},{2,5},{3,13},{4,6},{5,14},{6,7},{7,15},{8,0},{9,8},{1... | collective-permute-start | bytes 983048 | tf_op jit(solution)/shard_map/ppermute | solution.py:123
  122.4 36.0 %collective-permute-start.3 = (bf16[256,640]{1,0:T(8,128)(2,1)S(1)}, bf16[256,640]{1,0:T(8,128)(2,1)S(1)}, u32[]{:S(2)}, u32[]{:S(2)}) collective-permute-start(bf16[256,640]{1,0:T(8,128)(2,1)S(1)} %get-tuple-element.21), channel_id=1, source_target_pairs={{0,2},{1,10},{2,3},{3,11},{4,4},{5,12},{6,5},{7,13},{8,6},{9,14},{... | collective-permute-start | bytes 983048 | tf_op jit(solution)/shard_map/ppermute | solution.py:123
  126.1 46.4 %collective-permute-start.2 = (bf16[256,640]{1,0:T(8,128)(2,1)S(1)}, bf16[256,640]{1,0:T(8,128)(2,1)S(1)}, u32[]{:S(2)}, u32[]{:S(2)}) collective-permute-start(bf16[256,640]{1,0:T(8,128)(2,1)S(1)} %get-tuple-element.18), channel_id=1, source_target_pairs={{0,0},{1,8},{2,1},{3,9},{4,2},{5,10},{6,3},{7,11},{8,4},{9,12},{10... | collective-permute-start | bytes 983048 | tf_op jit(solution)/shard_map/ppermute | solution.py:123
  132.9 39.6 %copy-start.4 = (bf16[256,640]{1,0:T(8,128)(2,1)}, bf16[256,640]{1,0:T(8,128)(2,1)S(1)}, u32[]{:S(2)}) copy-start(bf16[256,640]{1,0:T(8,128)(2,1)S(1)} %collective-permute-done.5) | copy-start | bytes 983044
  144.7 29.1 %copy-start.6 = (bf16[256,640]{1,0:T(8,128)(2,1)}, bf16[256,640]{1,0:T(8,128)(2,1)S(1)}, u32[]{:S(2)}) copy-start(bf16[256,640]{1,0:T(8,128)(2,1)S(1)} %collective-permute-done.4) | copy-start | bytes 983044
  158.4 15.4 %copy-start.8 = (bf16[256,640]{1,0:T(8,128)(2,1)}, bf16[256,640]{1,0:T(8,128)(2,1)S(1)}, u32[]{:S(2)}) copy-start(bf16[256,640]{1,0:T(8,128)(2,1)S(1)} %collective-permute-done.3) | copy-start | bytes 983044
  172.5 1.3 copy-start.10
  173.8 16.3 %collective-permute-start.6 = (bf16[4,256,640]{2,1,0:T(8,128)(2,1)}, bf16[4,256,640]{2,1,0:T(8,128)(2,1)}, u32[]{:S(2)}, u32[]{:S(2)}) collective-permute-start(bf16[4,256,640]{2,1,0:T(8,128)(2,1)} %pad_maximum_fusion), channel_id=1, source_target_pairs={{0,1},{1,0},{2,3},{3,2},{4,5},{5,4},{6,7},{7,6},{8,9},{9,8},{10,11... | collective-permute-start | bytes 3932168 | tf_op jit(solution)/shard_map/ppermute | solution.py:82
  190.0 2.9 %copy-start.5 = (bf16[256,640]{1,0:T(8,128)(2,1)S(1)}, bf16[256,640]{1,0:T(8,128)(2,1)}, u32[]{:S(2)}) copy-start(bf16[256,640]{1,0:T(8,128)(2,1)} %copy-done.4) | copy-start | bytes 983044
  190.0 2.9 %copy-start.7 = (bf16[256,640]{1,0:T(8,128)(2,1)S(1)}, bf16[256,640]{1,0:T(8,128)(2,1)}, u32[]{:S(2)}) copy-start(bf16[256,640]{1,0:T(8,128)(2,1)} %copy-done.6) | copy-start | bytes 983044
  190.0 2.9 %copy-start.9 = (bf16[256,640]{1,0:T(8,128)(2,1)S(1)}, bf16[256,640]{1,0:T(8,128)(2,1)}, u32[]{:S(2)}) copy-start(bf16[256,640]{1,0:T(8,128)(2,1)} %copy-done.8) | copy-start | bytes 983044
  190.0 2.9 %copy-start.11 = (bf16[256,640]{1,0:T(8,128)(2,1)S(1)}, bf16[256,640]{1,0:T(8,128)(2,1)}, u32[]{:S(2)}) copy-start(bf16[256,640]{1,0:T(8,128)(2,1)} %copy-done.10) | copy-start | bytes 983044
  195.1 2.9 %copy-start.1 = (bf16[8,256,512]{2,1,0:T(8,128)(2,1)S(1)}, bf16[8,256,512]{2,1,0:T(8,128)(2,1)}, u32[]{:S(2)}) copy-start(bf16[8,256,512]{2,1,0:T(8,128)(2,1)} %all-gather.4.cloned.1.call-done) | copy-start | bytes 6291460
Sparse Core Ops, SparseCore 0:
  11.4 84.8 all-gather.5
  115.5 60.1 all-gather.3

commit v2 on v1

v2 whole, which is shorter than its diff:
```python
import functools

import jax
import jax.numpy as jnp
from jax import lax
from jax.experimental import pallas as pl
from jax.experimental.pallas import tpu as pltpu
from jax.sharding import PartitionSpec as P

HEAD = 128


EPSILON = 1e-06
ROPE_BASE = 1000000.0
SCALE = HEAD ** (-0.5)
VMEM_BYTES = 48 * 1024 * 1024
IN_VMEM = pl.BlockSpec(memory_space=pltpu.VMEM)
IN_SMEM = pl.BlockSpec(memory_space=pltpu.SMEM)


def rope_tables(length):
    half_size = HEAD // 2
    exponent = jnp.arange(half_size, dtype=jnp.float32) * (2.0 / HEAD)
    frequency = jnp.exp(-exponent * jnp.log(jnp.float32(ROPE_BASE)))
    angles = jnp.arange(length, dtype=jnp.float32)[:, None] * frequency[None, :]
    cosine_table = jnp.cos(angles)
    sine_table = jnp.sin(angles)
    return (
        jnp.concatenate([cosine_table, cosine_table], -1),
        jnp.concatenate([-sine_table, sine_table], -1),
    )


def product(left, right):
    return jnp.dot(left, right, preferred_element_type=jnp.float32)


def product_rows(left, right):
    return lax.dot_general(
        left, right, (((1,), (1,)), ((), ())), preferred_element_type=jnp.float32
    )


def own_block_kernel(values_at, values_ref, weight_ref, sums_ref):
    for j in range(2):
        sums_ref[j] = product(values_ref[...], weight_ref[j])


def add_block(at_ref, values_ref, pieces, sums_ref, sums_out):
    group, replica = at_ref[1], at_ref[2]
    rows = pieces[0].shape[0]
    near = values_ref[:, pl.ds(pl.multiple_of(replica * rows, 128), rows)]
    far = values_ref[:, pl.ds(pl.multiple_of((1 - replica) * rows, 128), rows)]
    along_x, along_y = pieces[1], pieces[2]
    sums_out[group] = (
        sums_ref[group] + product(near, pieces[0][...]) + product(far, along_x[...])
    )
    sums_out[1 - group] = (
        sums_ref[1 - group] + product(near, along_y[...]) + product(far, pieces[3][...])
    )


def block_kernel(at_ref, values_ref, p0, p1, p2, p3, sums_ref, sums_out):
    add_block(at_ref, values_ref, (p0, p1, p2, p3), sums_ref, sums_out)


def whole_spec(shape):
    return pl.BlockSpec(shape, lambda i, at: (0,) * len(shape))


def values_spec(length, rows):
    return pl.BlockSpec((length, rows), lambda i, at: (0, at[0]))


def own_block(at, normed, kv_weight):
    length = normed.shape[0]
    _, rows, columns = kv_weight.shape
    shape = (2, length, columns)
    return pl.pallas_call(
        own_block_kernel,
        grid_spec=pltpu.PrefetchScalarGridSpec(
            num_scalar_prefetch=1,
            grid=(1,),
            in_specs=[values_spec(length, rows), whole_spec(kv_weight.shape)],
            out_specs=whole_spec(shape),
        ),
        out_shape=jax.ShapeDtypeStruct(shape, jnp.float32),
        compiler_params=pltpu.CompilerParams(vmem_limit_bytes=VMEM_BYTES),
        cost_estimate=pl.CostEstimate(
            flops=4 * length * rows * columns, bytes_accessed=2500000, transcendentals=0
        ),
        name="own_block",
    )(at, normed, kv_weight)


def other_block(at, normed, pieces, sums):
    length = normed.shape[0]
    rows, columns = pieces[0].shape
    return pl.pallas_call(
        block_kernel,
        grid_spec=pltpu.PrefetchScalarGridSpec(
            num_scalar_prefetch=1,
            grid=(1,),
            in_specs=[values_spec(length, 2 * rows)]
            + [whole_spec((rows, columns))] * 4
            + [whole_spec(sums.shape)],
            out_specs=whole_spec(sums.shape),
        ),
        out_shape=jax.ShapeDtypeStruct(sums.shape, jnp.float32),
        compiler_params=pltpu.CompilerParams(vmem_limit_bytes=VMEM_BYTES),
        cost_estimate=pl.CostEstimate(
            flops=8 * length * rows * columns, bytes_accessed=3000000, transcendentals=0
        ),
        name="other_block",
    )(at, normed, *pieces, sums)


def attention_body(raw_of, cosine, sine, queries_ref, cotangent_ref, grad_query_ref, pair_ref):
    length, columns = cosine.shape[0], pair_ref.shape[1] // 2
    key_heads = columns // HEAD
    group_size = queries_ref.shape[1] // columns
    key_at = lax.broadcasted_iota(jnp.int32, (length, length), 0)
    query_at = lax.broadcasted_iota(jnp.int32, (length, length), 1)
    causal = key_at <= query_at
    for head in range(key_heads):
        lanes = slice(head * HEAD, (head + 1) * HEAD)
        raw = raw_of(0, lanes)
        wide_keys = raw * cosine + pltpu.roll(raw, HEAD // 2, 1) * sine
        keys = wide_keys.astype(jnp.bfloat16)
        keys_across = wide_keys.T.astype(jnp.bfloat16)
        values = raw_of(1, lanes).astype(jnp.bfloat16)
        grad_rotated = jnp.zeros((length, HEAD), jnp.float32)
        grad_value = jnp.zeros((length, HEAD), jnp.float32)
        for member in range(group_size):
            start = (head * group_size + member) * HEAD
            query = queries_ref[:, start : start + HEAD]
            upstream = cotangent_ref[:, start : start + HEAD]
            scores = jnp.where(causal, product_rows(keys, query), -jnp.inf)
            peak = jnp.max(scores, 0, keepdims=True)
            exponentials = jnp.exp((scores - peak) * SCALE)
            probability = exponentials * (1.0 / jnp.sum(exponentials, 0, keepdims=True))
            grad_probability = product_rows(values, upstream)
            total = jnp.sum(probability * grad_probability, 0, keepdims=True)
            grad_scores = (probability * (grad_probability - total) * SCALE).astype(jnp.bfloat16)
            grad_rotated += product(grad_scores, query)
            grad_value += product(probability.astype(jnp.bfloat16), upstream)
            grad_query = product(keys_across, grad_scores)
            grad_query_ref[:, start : start + HEAD] = grad_query.T.astype(jnp.bfloat16)
        grad_key = grad_rotated * cosine - pltpu.roll(grad_rotated, HEAD // 2, 1) * sine
        pair_ref[:, lanes] = grad_key.astype(jnp.bfloat16)
        pair_ref[:, columns + head * HEAD : columns + (head + 1) * HEAD] = grad_value.astype(
            jnp.bfloat16
        )


def attention_kernel(
    at_ref, values_ref, p0, p1, p2, p3, sums_ref, bias_ref, cosine_ref, sine_ref, queries_ref,
    cotangent_ref, grad_query_ref, pair_ref, raw_ref,
):
    add_block(at_ref, values_ref, (p0, p1, p2, p3), sums_ref, raw_ref)

    def raw_of(j, lanes):
        return raw_ref[j, :, lanes] + bias_ref[j : j + 1, lanes]

    attention_body(
        raw_of, cosine_ref[...], sine_ref[...], queries_ref, cotangent_ref, grad_query_ref, pair_ref
    )


def attention(at, normed, pieces, sums, bias, cosine, sine, queries, cotangent):
    length = normed.shape[0]
    rows, columns = pieces[0].shape
    pair = (length, 2 * columns)
    rest = (sums, bias, cosine, sine, queries, cotangent)
    return pl.pallas_call(
        attention_kernel,
        grid_spec=pltpu.PrefetchScalarGridSpec(
            num_scalar_prefetch=1,
            grid=(1,),
            in_specs=[values_spec(length, 2 * rows)]
            + [whole_spec((rows, columns))] * 4
            + [whole_spec(array.shape) for array in rest],
            out_specs=[whole_spec(queries.shape), whole_spec(pair)],
            scratch_shapes=[pltpu.VMEM(sums.shape, jnp.float32)],
        ),
        out_shape=[
            jax.ShapeDtypeStruct(queries.shape, jnp.bfloat16),
            jax.ShapeDtypeStruct(pair, jnp.bfloat16),
        ],
        compiler_params=pltpu.CompilerParams(vmem_limit_bytes=VMEM_BYTES),
        cost_estimate=pl.CostEstimate(
            flops=10 * length * length * queries.shape[1],
            bytes_accessed=5000000,
            transcendentals=length * length * queries.shape[1] // HEAD,
        ),
        name="attention",
    )(at, normed, *pieces, *rest)


def gradient_kernel(turns, first, last, *refs):
    at_ref, own_ref, other_ref = refs[:3]
    count = len(turns)
    pairs = refs[3 : 3 + count]
    refs = refs[3 + count :]
    if not first:
        sums_ref, bias_sums_ref = refs[:2]
        refs = refs[2:]
    weight_ref, bias_ref = refs
    columns = weight_ref.shape[2]

    def run(same_ref, mate_ref):
        total = None
        for (slot, same), pair in zip(turns, pairs):
            slab = (same_ref if same else mate_ref)[at_ref[slot]]
            term = product(slab, pair[...])
            total = term if total is None else total + term
        for j in range(2):
            part = total[:, j * columns : (j + 1) * columns]
            weight_ref[j] = part if first else sums_ref[j] + part

    pl.when(at_ref[0] == 1)(lambda: run(own_ref, other_ref))
    pl.when(at_ref[0] == 0)(lambda: run(other_ref, own_ref))
    total = None
    for pair in pairs:
        term = jnp.sum(pair[...].astype(jnp.float32), axis=0, keepdims=True)
        total = term if total is None else total + term
    for j in range(2):
        part = total[:, j * columns : (j + 1) * columns]
        bias_ref[j : j + 1, :] = part if first else bias_sums_ref[j : j + 1, :] + part


def gradient(at, own, other, turns, pairs, sums):
    _, share, length = own.shape
    columns = pairs[0].shape[1] // 2
    operands = (at, own, other, *pairs) + (sums or ())
    return pl.pallas_call(
        functools.partial(gradient_kernel, turns, sums is None, True),
        in_specs=[IN_SMEM] + [IN_VMEM] * (len(operands) - 1),
        out_specs=[IN_VMEM, IN_VMEM],
        out_shape=[
            jax.ShapeDtypeStruct((2, share, columns), jnp.float32),
            jax.ShapeDtypeStruct((2, columns), jnp.float32),
        ],
        compiler_params=pltpu.CompilerParams(vmem_limit_bytes=VMEM_BYTES),
        cost_estimate=pl.CostEstimate(
            flops=4 * len(pairs) * length * share * columns,
            bytes_accessed=5000000,
            transcendentals=0,
        ),
        name="gradient",
    )(*operands)


def swapped(block, axis):
    return lax.ppermute(block, axis, [(0, 1), (1, 0)])


def turned(block, axis, distance):
    size = lax.axis_size(axis)
    return lax.ppermute(block, axis, [(i, (i + distance) % size) for i in range(size)])


def round_ring(block, axis):
    size = lax.axis_size(axis)
    found = {0: block}
    for step in range(1, size // 2 + 1):
        found[step] = turned(found[step - 1], axis, 1)
        if step <= (size - 1) // 2:
            found[-step] = turned(found[1 - step], axis, -1)
    return found


def slabs_of_tokens(normed, share):
    blocks, replicas = lax.axis_size("blk"), lax.axis_size("dp")
    sequences = blocks * replicas
    half = sequences // 2
    number = lax.axis_index("blk") * replicas + lax.axis_index("dp")
    slabs = []
    for turn in range(half):
        route = []
        for source in range(sequences):
            for core in range(2):
                goal = half * core + (turn + source // 2) % half
                route.append((source * 2 + core, goal * 2 + source % 2))
        slab = (turn + number // 2) % half
        sent = lax.dynamic_slice_in_dim(normed, slab * share, share, 1)
        slabs.append(lax.ppermute(sent, ("blk", "dp", "sub"), route))
    return slabs


def normalize_half(activations, norm_gain):
    core = lax.axis_index("sub")
    features = activations.shape[1]
    wide_values = activations.astype(jnp.float32)
    square_sum = jnp.sum(wide_values * wide_values, -1, keepdims=True)
    square_sum = square_sum + swapped(square_sum, "sub")
    gain = lax.dynamic_slice_in_dim(norm_gain, core * features, features, 0).astype(jnp.float32)
    mean_square = square_sum / (2 * features)
    return (wide_values * lax.rsqrt(mean_square + EPSILON) * gain).astype(jnp.bfloat16)


def local(activations, norm_gain, queries, cotangent, kv_weight, kv_bias):
    blocks, replicas = lax.axis_size("blk"), lax.axis_size("dp")
    group, block, replica = lax.axis_index("groups"), lax.axis_index("blk"), lax.axis_index("dp")
    core = lax.axis_index("sub")
    _, block_rows, columns = kv_weight.shape
    length = activations.shape[0]
    share = block_rows // replicas
    half = blocks * replicas // 2
    number = block * replicas + replica
    slab_here = number % half

    normed = normalize_half(activations, norm_gain)
    normed_other = swapped(normed, "sub")
    normed_whole = jnp.where(
        core == 0,
        jnp.concatenate([normed, normed_other], 1),
        jnp.concatenate([normed_other, normed], 1),
    )
    cosine, sine = rope_tables(length)
    bias = kv_bias.astype(jnp.float32)

    piece = lax.dynamic_slice(kv_weight, (group, replica * share, 0), (1, share, columns))[0]

    if blocks == 4 and replicas == 2:
        ring = round_ring(piece, "blk")
        gathered = []
        for distance in (1, -1, 2):
            near = ring[distance]
            along_x, along_y = swapped(near, "dp"), swapped(near, "groups")
            if distance == -1:
                both = swapped(along_y, "dp")
            else:
                both = swapped(along_x, "groups")
            gathered.append((distance, (near, along_x, along_y, both)))

        def where(distance):
            return jnp.stack([(block - distance) % blocks, group, replica]).astype(jnp.int32)

        normed_late, _ = lax.optimization_barrier((normed, ring[2]))
        slabs = slabs_of_tokens(normed_late, share)

        sums = own_block(where(0), normed_whole, kv_weight)
        for distance, pieces in gathered[:-1]:
            sums = other_block(where(distance), normed_whole, pieces, sums)
        distance, pieces = gathered[-1]
        grad_query, grad_pair = attention(
            where(distance), normed_whole, pieces, sums, bias, cosine, sine, queries, cotangent
        )

        slabs_own = jnp.stack([slab.T for slab in slabs])
        slabs_other = swapped(slabs_own, "sub")
        pairs = round_ring(grad_pair, "blk")
        at = jnp.stack(
            [(replica == core).astype(jnp.int32)]
            + [(slab_here - (block - distance)) % half for distance in (0, 1, -1, 2)]
        ).astype(jnp.int32)
        sums = None
        for some in ((0, 1, -1), (2,)):
            turns, held = [], []
            for distance in some:
                slot = 1 + (0, 1, -1, 2).index(distance)
                turns += [(slot, True), (slot, False)]
                held += [pairs[distance], swapped(pairs[distance], "dp")]
            sums = gradient(at, slabs_own, slabs_other, tuple(turns), held, sums)
        grad_weight, grad_bias = sums
        return (grad_query, grad_weight, grad_bias)

    return general(
        piece, normed, normed_other, bias, cosine, sine, queries, cotangent, columns, share
    )


def plain_attention_kernel(
    raw_ref, bias_ref, cosine_ref, sine_ref, queries_ref, cotangent_ref, grad_query_ref, pair_ref
):
    def raw_of(j, lanes):
        return raw_ref[j, :, lanes] + bias_ref[j : j + 1, lanes]

    attention_body(
        raw_of, cosine_ref[...], sine_ref[...], queries_ref, cotangent_ref, grad_query_ref, pair_ref
    )


def general(piece, normed, normed_other, bias, cosine, sine, queries, cotangent, columns, share):
    core = lax.axis_index("sub")
    blocks, replicas = lax.axis_size("blk"), lax.axis_size("dp")
    length, features = normed.shape
    half = blocks * replicas // 2
    number = lax.axis_index("blk") * replicas + lax.axis_index("dp")
    weight = lax.all_gather(piece, ("groups", "blk", "dp"), axis=0, tiled=True)
    weight = weight.reshape(2, -1, columns)
    slabs_own = jnp.stack(slabs_of_tokens(normed, share))
    slabs_other = swapped(slabs_own, "sub")

    def project(values, rows):
        part = lax.dynamic_slice_in_dim(weight, rows * features, features, 1)
        return jnp.einsum("tr,krc->ktc", values, part, preferred_element_type=jnp.float32)

    raw_pair = project(normed, core) + project(normed_other, 1 - core)
    grad_query, grad_pair = pl.pallas_call(
        plain_attention_kernel,
        in_specs=[IN_VMEM] * 6,
        out_specs=[IN_VMEM] * 2,
        out_shape=[
            jax.ShapeDtypeStruct(queries.shape, jnp.bfloat16),
            jax.ShapeDtypeStruct((length, 2 * columns), jnp.bfloat16),
        ],
        compiler_params=pltpu.CompilerParams(vmem_limit_bytes=VMEM_BYTES),
        name="plain_attention",
    )(raw_pair, bias, cosine, sine, queries, cotangent)

    everyone = lax.all_gather(grad_pair, ("blk", "dp"), axis=0)
    grad_bias = jnp.sum(everyone.astype(jnp.float32), axis=(0, 1)).reshape(2, columns)
    paired = everyone.reshape(half, 2, -1, 2 * columns)
    order = (number % half - jnp.arange(half)) % half
    grads_own = jnp.take(lax.dynamic_index_in_dim(paired, core, 1, False), order, axis=0)
    grads_other = jnp.take(lax.dynamic_index_in_dim(paired, 1 - core, 1, False), order, axis=0)
    grad_weight = jnp.einsum(
        "ntr,ntc->rc", slabs_own, grads_own, preferred_element_type=jnp.float32
    ) + jnp.einsum("ntr,ntc->rc", slabs_other, grads_other, preferred_element_type=jnp.float32)
    grad_weight = jnp.moveaxis(grad_weight.reshape(share, 2, columns), 1, 0)
    return (grad_query, grad_weight, grad_bias)


def solution(mesh):
    placed = (
        P(("groups", "blk", "dp"), "sub"),
        P(),
        P(("groups", "blk", "dp"), "sub"),
        P(("groups", "blk", "dp"), "sub"),
        P(None, "blk", "sub"),
        P(None, "sub"),
    )
    return jax.shard_map(
        local,
        mesh=mesh,
        in_specs=placed,
        out_specs=(
            P(("groups", "blk", "dp"), "sub"),
            P(None, ("groups", "blk", "dp"), "sub"),
            P("groups", "sub"),
        ),
        check_vma=False,
    )
```

time: 206 us -> 131 us (0.64)
  the two profiles are of different devices: /device:TPU:9 before, /device:TPU:0 now
where the time goes in v2:
time: 131 us; the launch traced here: 130 us
  waiting for transfers between devices  56.7 us (43%)
  starting transfers between devices  39.4 us (30%)
  Pallas kernels  18 us (14%)
  local copies, waits for them, and re-layouts  9.65 us (7%)
  other arithmetic  5.32 us (4%)
    ppermute x6, waiting for transfers between devices, turned(): lax.ppermute(block, axis, [(i, (i + distance) % size) for i in range(size)])  28.5 us
    ppermute x16, starting transfers between devices, swapped(): return lax.ppermute(block, axis, [(0, 1), (1, 0)])  20.5 us
    ppermute x4, waiting for transfers between devices, slabs_of_tokens(): slabs.append(lax.ppermute(sent, ('blk', 'dp', 'sub'), route))  17 us
    ppermute x16, waiting for transfers between devices, swapped(): return lax.ppermute(block, axis, [(0, 1), (1, 0)])  11.3 us
    ppermute x6, starting transfers between devices, turned(): lax.ppermute(block, axis, [(i, (i + distance) % size) for i in range(size)])  10.7 us
    ppermute x4, starting transfers between devices, slabs_of_tokens(): slabs.append(lax.ppermute(sent, ('blk', 'dp', 'sub'), route))  8.1 us
    pallas_call x1, Pallas kernels, attention(): pl.pallas_call(attention_kernel, grid_spec=pltpu.PrefetchScalarGridSpec(n...  6.96 us
    pallas_call x2, Pallas kernels, gradient(): pl.pallas_call(functools.partial(gradient_kernel, turns, sums is None, Tr...  6.43 us
  transfers between devices with their start and end apart: 26, of which 11 were waited for; matrix products, arithmetic and copies ran while one was open for 8% of the time, Pallas kernels for 11%

profile of v2, /device:TPU:0, one launch (start us, length us, event | category | flops | bytes accessed | tf_op | source)
XLA Modules:
  0.0 130.0 jit_solution(5097911376012900903)
XLA Ops:
  1.7 3.1 %collective-permute-start.2 = (bf16[640,256]{1,0:T(8,128)(2,1)S(1)}, bf16[640,256]{1,0:T(8,128)(2,1)S(1)}, u32[]{:S(2)}, u32[]{:S(2)}) collective-permute-start(bf16[640,256]{1,0:T(8,128)(2,1)S(1)} %dynamic-slice_bitcast_fusion), channel_id=1, source_target_pairs={{0,4},{4,8},{8,12},{12,0},{1,5},{5,9},{9,13},{13,1},{2,6},{6,10},{... | collective-permute-start | bytes 983048 | tf_op jit(solution)/shard_map/ppermute | solution.py:260
  4.7 1.6 %copy.14 = bf16[256,2560]{0,1:T(8,128)(2,1)S(1)} copy(bf16[256,2560]{1,0:T(8,128)(2,1)} %param.6) | data formatting | bytes 2621440 | tf_op args[0]
  8.6 5.9 %collective-permute-done.2.p0 = bf16[640,256]{1,0:T(8,128)(2,1)S(1)} collective-permute-done((bf16[640,256]{1,0:T(8,128)(2,1)S(1)}, bf16[640,256]{1,0:T(8,128)(2,1)S(1)}, u32[]{:S(2)}, u32[]{:S(2)}) %collective-permute-start.2) | collective-permute-done | bytes 327712 | tf_op jit(solution)/shard_map/ppermute | solution.py:260
  14.5 3.8 %collective-permute-start.7 = (bf16[640,256]{1,0:T(8,128)(2,1)}, bf16[640,256]{1,0:T(8,128)(2,1)}, u32[]{:S(2)}, u32[]{:S(2)}) collective-permute-start(bf16[640,256]{1,0:T(8,128)(2,1)} %copy-done.11), channel_id=1, source_target_pairs={{0,12},{4,0},{8,4},{12,8},{1,13},{5,1},{9,5},{13,9},{2,14},{6,2},{... | collective-permute-start | bytes 983048 | tf_op jit(solution)/shard_map/ppermute | solution.py:260
  18.3 1.5 %collective-permute-start.11 = (bf16[640,256]{1,0:T(8,128)(2,1)S(1)}, bf16[640,256]{1,0:T(8,128)(2,1)S(1)}, u32[]{:S(2)}, u32[]{:S(2)}) collective-permute-start(bf16[640,256]{1,0:T(8,128)(2,1)S(1)} %collective-permute-done.2.p0), channel_id=1, source_target_pairs={{0,2},{2,0},{1,3},{3,1},{4,6},{6,4},{5,7},{7,5},{8,10},{10,8},{9,1... | collective-permute-start | bytes 983048 | tf_op jit(solution)/shard_map/ppermute | solution.py:255
  19.9 7.0 %collective-permute-done.3.p0 = bf16[640,256]{1,0:T(8,128)(2,1)S(1)} collective-permute-done((bf16[640,256]{1,0:T(8,128)(2,1)S(1)}, bf16[640,256]{1,0:T(8,128)(2,1)S(1)}, u32[]{:S(2)}, u32[]{:S(2)}) %collective-permute-start.3) | collective-permute-done | bytes 327712 | tf_op jit(solution)/shard_map/ppermute | solution.py:260
  27.7 4.6 %collective-permute-start.15 = (bf16[256,640]{0,1:T(8,128)(2,1)S(1)}, bf16[256,640]{0,1:T(8,128)(2,1)S(1)}, u32[]{:S(2)}, u32[]{:S(2)}) collective-permute-start(bf16[256,640]{0,1:T(8,128)(2,1)S(1)} %get-tuple-element.20), channel_id=1, source_target_pairs={{0,2},{1,10},{2,3},{3,11},{4,4},{5,12},{6,5},{7,13},{8,6},{9,14},{... | collective-permute-start | bytes 983048 | tf_op jit(solution)/shard_map/ppermute | solution.py:287
  32.6 2.5 %collective-permute-start.17 = (bf16[256,640]{0,1:T(8,128)(2,1)S(1)}, bf16[256,640]{0,1:T(8,128)(2,1)S(1)}, u32[]{:S(2)}, u32[]{:S(2)}) collective-permute-start(bf16[256,640]{0,1:T(8,128)(2,1)S(1)} %get-tuple-element.18), channel_id=1, source_target_pairs={{0,6},{1,14},{2,7},{3,15},{4,0},{5,8},{6,1},{7,9},{8,2},{9,10},{10... | collective-permute-start | bytes 983048 | tf_op jit(solution)/shard_map/ppermute | solution.py:287
  35.7 1.6 %collective-permute-start.12 = (bf16[640,256]{1,0:T(8,128)(2,1)S(1)}, bf16[640,256]{1,0:T(8,128)(2,1)S(1)}, u32[]{:S(2)}, u32[]{:S(2)}) collective-permute-start(bf16[640,256]{1,0:T(8,128)(2,1)S(1)} %collective-permute-done.2.p0), channel_id=1, source_target_pairs={{0,16},{16,0},{1,17},{17,1},{2,18},{18,2},{3,19},{19,3},{4,20},{20... | collective-permute-start | bytes 983048 | tf_op jit(solution)/shard_map/ppermute | solution.py:255
  37.3 8.3 %collective-permute-done.15 = bf16[256,640]{0,1:T(8,128)(2,1)S(1)} collective-permute-done((bf16[256,640]{0,1:T(8,128)(2,1)S(1)}, bf16[256,640]{0,1:T(8,128)(2,1)S(1)}, u32[]{:S(2)}, u32[]{:S(2)}) %collective-permute-start.15) | collective-permute-done | bytes 327712 | tf_op jit(solution)/shard_map/ppermute | solution.py:287
  45.6 1.1 collective-permute-start.9
  46.7 8.7 %collective-permute-done.16 = bf16[256,640]{0,1:T(8,128)(2,1)S(1)} collective-permute-done((bf16[256,640]{0,1:T(8,128)(2,1)S(1)}, bf16[256,640]{0,1:T(8,128)(2,1)S(1)}, u32[]{:S(2)}, u32[]{:S(2)}) %collective-permute-start.16) | collective-permute-done | bytes 327712 | tf_op jit(solution)/shard_map/ppermute | solution.py:287
  55.4 1.5 %collective-permute-start.13 = (bf16[640,256]{1,0:T(8,128)(2,1)S(1)}, bf16[640,256]{1,0:T(8,128)(2,1)S(1)}, u32[]{:S(2)}, u32[]{:S(2)}) collective-permute-start(bf16[640,256]{1,0:T(8,128)(2,1)S(1)} %collective-permute-done.11.p1), channel_id=1, source_target_pairs={{0,16},{16,0},{1,17},{17,1},{2,18},{18,2},{3,19},{19,3},{4,20},{20... | collective-permute-start | bytes 983048 | tf_op jit(solution)/shard_map/ppermute | solution.py:255
  57.6 1.2 pad_maximum_fusion.refs_1_
  59.6 5.1 %collective-permute-start.8 = (bf16[640,256]{1,0:T(8,128)(2,1)}, bf16[640,256]{1,0:T(8,128)(2,1)}, u32[]{:S(2)}, u32[]{:S(2)}) collective-permute-start(bf16[640,256]{1,0:T(8,128)(2,1)} %collective-permute-done.7.p0), channel_id=1, source_target_pairs={{0,2},{2,0},{1,3},{3,1},{4,6},{6,4},{5,7},{7,5},{8,10},{10,8},{9,1... | collective-permute-start | bytes 983048 | tf_op jit(solution)/shard_map/ppermute | solution.py:255
  66.5 5.3 %collective-permute-start.10 = (bf16[640,256]{1,0:T(8,128)(2,1)}, bf16[640,256]{1,0:T(8,128)(2,1)}, u32[]{:S(2)}, u32[]{:S(2)}) collective-permute-start(bf16[640,256]{1,0:T(8,128)(2,1)} %collective-permute-done.9.p2), channel_id=1, source_target_pairs={{0,2},{2,0},{1,3},{3,1},{4,6},{6,4},{5,7},{7,5},{8,10},{10,8},{9,1... | collective-permute-start | bytes 983048 | tf_op jit(solution)/shard_map/ppermute | solution.py:255
  71.8 1.5 %collective-permute-start.6 = (bf16[640,256]{1,0:T(8,128)(2,1)}, bf16[640,256]{1,0:T(8,128)(2,1)}, u32[]{:S(2)}, u32[]{:S(2)}) collective-permute-start(bf16[640,256]{1,0:T(8,128)(2,1)} %collective-permute-done.4.p1), channel_id=1, source_target_pairs={{0,16},{16,0},{1,17},{17,1},{2,18},{18,2},{3,19},{19,3},{4,20},{20... | collective-permute-start | bytes 983048 | tf_op jit(solution)/shard_map/ppermute | solution.py:255
  73.4 1.8 %maximum_select_fusion = bf16[256,5120]{0,1:T(8,128)(2,1)} fusion(bf16[256,2560]{0,1:T(8,128)(2,1)S(1)} %collective-permute-done.1, bf16[256,2560]{0,1:T(8,128)(2,1)S(1)} %fusion.2, pred[]{:T(512)S(6)} %eq.20), kind=kLoop, calls=%fused_computation.5 | loop fusion | flops 11796480 | bytes 5242881 | tf_op jit(solution)/shard_map/jit(_where)/select_n | solution.py:315
  75.2 3.0 %copy.18.values_ref = bf16[256,5120]{1,0:T(8,128)(2,1)S(1)} copy(bf16[256,5120]{0,1:T(8,128)(2,1)} %maximum_select_fusion) | data formatting | bytes 5242880 | tf_op jit(solution)/shard_map/jit(_where)/select_n | solution.py:315
  78.2 1.3 %copy-done.1 = bf16[2,1280,256]{2,1,0:T(8,128)(2,1)S(1)} copy-done((bf16[2,1280,256]{2,1,0:T(8,128)(2,1)S(1)}, bf16[2,1280,256]{2,1,0:T(8,128)(2,1)}, u32[]{:S(2)}) %copy-start.1) | copy-done | bytes 1310744
  79.5 1.0 own_block.1.sums_ref
  81.4 1.2 other_block.2.sums_ref
  82.6 2.4 %other_block.3.sums_ref = f32[2,256,256]{2,1,0:T(8,128)S(1)} custom-call(s32[3]{0:T(128)S(1)} %get-tuple-element.25.at_ref, bf16[256,5120]{1,0:T(8,128)(2,1)S(1)} %copy.18.values_ref, bf16[640,256]{1,0:T(8,128)(2,1)} %collective-permute-done.7.p0, bf16[640,256]{1,0:T(8,128)(2,1)} %collective-permute-done.8.p1, bf16[640,256]{1,0:T(8,128)(2,1)} %collective-permute-done.9.p2, ...), custom_call_target="tpu_custom_call" | custom-call | flops 335544320 | bytes 3000000 | tf_op jit(solution)/shard_map/other_block/pallas_call | solution.py:99
  85.1 7.0 %attention.1 = (bf16[256,1280]{1,0:T(8,128)(2,1)}, bf16[256,512]{1,0:T(8,128)(2,1)S(1)}) custom-call(s32[3]{0:T(128)S(1)} %get-tuple-element.24.at_ref, bf16[256,5120]{1,0:T(8,128)(2,1)} %copy-done, bf16[640,256]{1,0:T(8,128)(2,1)S(1)} %collective-permute-done.3.p0, bf16[640,256]{1,0:T(8,128)(2,1)} %collective-permute-done.4.p1, ...), custom_call_target="tpu_custom_call" | custom-call | flops 838860800 | bytes 5000000 | tf_op jit(solution)/shard_map/attention/pallas_call | solution.py:175
  92.0 3.8 %collective-permute-start.24 = (bf16[256,512]{1,0:T(8,128)(2,1)S(1)}, bf16[256,512]{1,0:T(8,128)(2,1)S(1)}, u32[]{:S(2)}, u32[]{:S(2)}) collective-permute-start(bf16[256,512]{1,0:T(8,128)(2,1)S(1)} %get-tuple-element.12.refs_3_), channel_id=1, source_target_pairs={{0,12},{4,0},{8,4},{12,8},{1,13},{5,1},{9,5},{13,9},{2,14},{6,2},{... | collective-permute-start | bytes 786440 | tf_op jit(solution)/shard_map/ppermute | solution.py:260
  95.9 7.2 %collective-permute-done.19.refs_5_ = bf16[256,512]{1,0:T(8,128)(2,1)S(1)} collective-permute-done((bf16[256,512]{1,0:T(8,128)(2,1)S(1)}, bf16[256,512]{1,0:T(8,128)(2,1)S(1)}, u32[]{:S(2)}, u32[]{:S(2)}) %collective-permute-start.19) | collective-permute-done | bytes 262176 | tf_op jit(solution)/shard_map/ppermute | solution.py:260
  103.1 2.0 %collective-permute-start.23 = (bf16[256,512]{1,0:T(8,128)(2,1)S(1)}, bf16[256,512]{1,0:T(8,128)(2,1)S(1)}, u32[]{:S(2)}, u32[]{:S(2)}) collective-permute-start(bf16[256,512]{1,0:T(8,128)(2,1)S(1)} %collective-permute-done.19.refs_5_), channel_id=1, source_target_pairs={{0,2},{2,0},{1,3},{3,1},{4,6},{6,4},{5,7},{7,5},{8,10},{10,8},{9,1... | collective-permute-start | bytes 786440 | tf_op jit(solution)/shard_map/ppermute | solution.py:255
  106.1 7.4 %collective-permute-done.20.refs_3_ = bf16[256,512]{1,0:T(8,128)(2,1)S(1)} collective-permute-done((bf16[256,512]{1,0:T(8,128)(2,1)S(1)}, bf16[256,512]{1,0:T(8,128)(2,1)S(1)}, u32[]{:S(2)}, u32[]{:S(2)}) %collective-permute-start.20) | collective-permute-done | bytes 262176 | tf_op jit(solution)/shard_map/ppermute | solution.py:260
  113.6 4.3 %collective-permute-done.23.refs_6_ = bf16[256,512]{1,0:T(8,128)(2,1)S(1)} collective-permute-done((bf16[256,512]{1,0:T(8,128)(2,1)S(1)}, bf16[256,512]{1,0:T(8,128)(2,1)S(1)}, u32[]{:S(2)}, u32[]{:S(2)}) %collective-permute-start.23) | collective-permute-done | bytes 262176 | tf_op jit(solution)/shard_map/ppermute | solution.py:255
  117.9 5.6 %collective-permute-done.25.refs_8_ = bf16[256,512]{1,0:T(8,128)(2,1)S(1)} collective-permute-done((bf16[256,512]{1,0:T(8,128)(2,1)S(1)}, bf16[256,512]{1,0:T(8,128)(2,1)S(1)}, u32[]{:S(2)}, u32[]{:S(2)}) %collective-permute-start.25) | collective-permute-done | bytes 262176 | tf_op jit(solution)/shard_map/ppermute | solution.py:255
  123.5 3.1 %gradient.2 = (f32[2,640,256]{2,1,0:T(8,128)S(1)}, f32[2,256]{1,0:T(2,128)S(1)}) custom-call(s32[5]{0:T(128)S(1)} %stack.88.refs_0_, bf16[4,640,256]{2,1,0:T(8,128)(2,1)} %pad_maximum_fusion.refs_1_, bf16[4,640,256]{2,1,0:T(8,128)(2,1)} %collective-permute-done.18.refs_2_, bf16[256,512]{1,0:T(8,128)(2,1)S(1)} %get-tuple-element.12.refs_3_, ...), custom_call_target="tpu_custom_call" | custom-call | flops 1006632960 | bytes 5000000 | tf_op jit(solution)/shard_map/gradient/pallas_call | solution.py:236
  126.7 3.3 %gradient.3 = (f32[2,640,256]{2,1,0:T(8,128)}, f32[2,256]{1,0:T(2,128)}) custom-call(s32[5]{0:T(128)S(1)} %stack.88.refs_0_, bf16[4,640,256]{2,1,0:T(8,128)(2,1)} %pad_maximum_fusion.refs_1_, bf16[4,640,256]{2,1,0:T(8,128)(2,1)} %collective-permute-done.18.refs_2_, bf16[256,512]{1,0:T(8,128)(2,1)S(1)} %collective-permute-done.20.refs_3_, ...), custom_call_target="tpu_custom_call" | custom-call | flops 335544320 | bytes 5000000 | tf_op jit(solution)/shard_map/gradient/pallas_call | solution.py:236
  (72 shorter events, 10.2 us)
Async XLA Ops:
  1.6 7.0 %copy-start.11 = (bf16[640,256]{1,0:T(8,128)(2,1)}, bf16[640,256]{1,0:T(8,128)(2,1)S(1)}, u32[]{:S(2)}) copy-start(bf16[640,256]{1,0:T(8,128)(2,1)S(1)} %dynamic-slice_bitcast_fusion) | copy-start | bytes 983044
  1.7 12.8 %collective-permute-start.2 = (bf16[640,256]{1,0:T(8,128)(2,1)S(1)}, bf16[640,256]{1,0:T(8,128)(2,1)S(1)}, u32[]{:S(2)}, u32[]{:S(2)}) collective-permute-start(bf16[640,256]{1,0:T(8,128)(2,1)S(1)} %dynamic-slice_bitcast_fusion), channel_id=1, source_target_pairs={{0,4},{4,8},{8,12},{12,0},{1,5},{5,9},{9,13},{13,1},{2,6},{6,10},{... | collective-permute-start | bytes 983048 | tf_op jit(solution)/shard_map/ppermute | solution.py:260
  6.7 1.2 collective-permute-start
  7.9 10.4 %copy-start.13 = (bf16[2,256]{1,0:T(2,128)(2,1)S(1)}, bf16[2,256]{1,0:T(2,128)(2,1)}, u32[]{:S(2)}) copy-start(bf16[2,256]{1,0:T(2,128)(2,1)} %param.11) | copy-start | bytes 3076
  8.3 63.5 %collective-permute-start.1 = (bf16[256,2560]{0,1:T(8,128)(2,1)S(1)}, bf16[256,2560]{0,1:T(8,128)(2,1)S(1)}, u32[]{:S(2)}, u32[]{:S(2)}) collective-permute-start(bf16[256,2560]{0,1:T(8,128)(2,1)S(1)} %fusion.2), channel_id=1, source_target_pairs={{0,1},{1,0},{2,3},{3,2},{4,5},{5,4},{6,7},{7,6},{8,9},{9,8},{10,11... | collective-permute-start | bytes 3932168 | tf_op jit(solution)/shard_map/ppermute | solution.py:255
  14.5 12.5 %collective-permute-start.3 = (bf16[640,256]{1,0:T(8,128)(2,1)S(1)}, bf16[640,256]{1,0:T(8,128)(2,1)S(1)}, u32[]{:S(2)}, u32[]{:S(2)}) collective-permute-start(bf16[640,256]{1,0:T(8,128)(2,1)S(1)} %collective-permute-done.2.p0), channel_id=1, source_target_pairs={{0,4},{4,8},{8,12},{12,0},{1,5},{5,9},{9,13},{13,1},{2,6},{6,10},{... | collective-permute-start | bytes 983048 | tf_op jit(solution)/shard_map/ppermute | solution.py:260
  14.5 17.9 %collective-permute-start.7 = (bf16[640,256]{1,0:T(8,128)(2,1)}, bf16[640,256]{1,0:T(8,128)(2,1)}, u32[]{:S(2)}, u32[]{:S(2)}) collective-permute-start(bf16[640,256]{1,0:T(8,128)(2,1)} %copy-done.11), channel_id=1, source_target_pairs={{0,12},{4,0},{8,4},{12,8},{1,13},{5,1},{9,5},{13,9},{2,14},{6,2},{... | collective-permute-start | bytes 983048 | tf_op jit(solution)/shard_map/ppermute | solution.py:260
  18.3 14.3 %collective-permute-start.11 = (bf16[640,256]{1,0:T(8,128)(2,1)S(1)}, bf16[640,256]{1,0:T(8,128)(2,1)S(1)}, u32[]{:S(2)}, u32[]{:S(2)}) collective-permute-start(bf16[640,256]{1,0:T(8,128)(2,1)S(1)} %collective-permute-done.2.p0), channel_id=1, source_target_pairs={{0,2},{2,0},{1,3},{3,1},{4,6},{6,4},{5,7},{7,5},{8,10},{10,8},{9,1... | collective-permute-start | bytes 983048 | tf_op jit(solution)/shard_map/ppermute | solution.py:255
  27.0 8.7 %collective-permute-start.14 = (bf16[256,640]{0,1:T(8,128)(2,1)S(1)}, bf16[256,640]{0,1:T(8,128)(2,1)S(1)}, u32[]{:S(2)}, u32[]{:S(2)}) collective-permute-start(bf16[256,640]{0,1:T(8,128)(2,1)S(1)} %get-tuple-element.17), channel_id=1, source_target_pairs={{0,0},{1,8},{2,1},{3,9},{4,2},{5,10},{6,3},{7,11},{8,4},{9,12},{10... | collective-permute-start | bytes 983048 | tf_op jit(solution)/shard_map/ppermute | solution.py:287
  27.7 17.9 %collective-permute-start.15 = (bf16[256,640]{0,1:T(8,128)(2,1)S(1)}, bf16[256,640]{0,1:T(8,128)(2,1)S(1)}, u32[]{:S(2)}, u32[]{:S(2)}) collective-permute-start(bf16[256,640]{0,1:T(8,128)(2,1)S(1)} %get-tuple-element.20), channel_id=1, source_target_pairs={{0,2},{1,10},{2,3},{3,11},{4,4},{5,12},{6,5},{7,13},{8,6},{9,14},{... | collective-permute-start | bytes 983048 | tf_op jit(solution)/shard_map/ppermute | solution.py:287
  32.4 23.0 %collective-permute-start.16 = (bf16[256,640]{0,1:T(8,128)(2,1)S(1)}, bf16[256,640]{0,1:T(8,128)(2,1)S(1)}, u32[]{:S(2)}, u32[]{:S(2)}) collective-permute-start(bf16[256,640]{0,1:T(8,128)(2,1)S(1)} %get-tuple-element.19), channel_id=1, source_target_pairs={{0,4},{1,12},{2,5},{3,13},{4,6},{5,14},{6,7},{7,15},{8,0},{9,8},{1... | collective-permute-start | bytes 983048 | tf_op jit(solution)/shard_map/ppermute | solution.py:287
  32.6 26.2 %copy-start.4 = (bf16[640,256]{1,0:T(8,128)(2,1)}, bf16[640,256]{1,0:T(8,128)(2,1)S(1)}, u32[]{:S(2)}) copy-start(bf16[640,256]{1,0:T(8,128)(2,1)S(1)} %collective-permute-done.11.p1) | copy-start | bytes 983044
  32.6 22.8 %collective-permute-start.17 = (bf16[256,640]{0,1:T(8,128)(2,1)S(1)}, bf16[256,640]{0,1:T(8,128)(2,1)S(1)}, u32[]{:S(2)}, u32[]{:S(2)}) collective-permute-start(bf16[256,640]{0,1:T(8,128)(2,1)S(1)} %get-tuple-element.18), channel_id=1, source_target_pairs={{0,6},{1,14},{2,7},{3,15},{4,0},{5,8},{6,1},{7,9},{8,2},{9,10},{10... | collective-permute-start | bytes 983048 | tf_op jit(solution)/shard_map/ppermute | solution.py:287
  35.7 23.1 %collective-permute-start.12 = (bf16[640,256]{1,0:T(8,128)(2,1)S(1)}, bf16[640,256]{1,0:T(8,128)(2,1)S(1)}, u32[]{:S(2)}, u32[]{:S(2)}) collective-permute-start(bf16[640,256]{1,0:T(8,128)(2,1)S(1)} %collective-permute-done.2.p0), channel_id=1, source_target_pairs={{0,16},{16,0},{1,17},{17,1},{2,18},{18,2},{3,19},{19,3},{4,20},{20... | collective-permute-start | bytes 983048 | tf_op jit(solution)/shard_map/ppermute | solution.py:255
  45.6 19.1 %collective-permute-start.9 = (bf16[640,256]{1,0:T(8,128)(2,1)}, bf16[640,256]{1,0:T(8,128)(2,1)}, u32[]{:S(2)}, u32[]{:S(2)}) collective-permute-start(bf16[640,256]{1,0:T(8,128)(2,1)} %collective-permute-done.7.p0), channel_id=1, source_target_pairs={{0,16},{16,0},{1,17},{17,1},{2,18},{18,2},{3,19},{19,3},{4,20},{20... | collective-permute-start | bytes 983048 | tf_op jit(solution)/shard_map/ppermute | solution.py:255
  55.4 16.4 %collective-permute-start.4 = (bf16[640,256]{1,0:T(8,128)(2,1)S(1)}, bf16[640,256]{1,0:T(8,128)(2,1)}, u32[]{:S(2)}, u32[]{:S(2)}) collective-permute-start(bf16[640,256]{1,0:T(8,128)(2,1)S(1)} %collective-permute-done.3.p0), channel_id=1, source_target_pairs={{0,2},{2,0},{1,3},{3,1},{4,6},{6,4},{5,7},{7,5},{8,10},{10,8},{9,1... | collective-permute-start | bytes 983048 | tf_op jit(solution)/shard_map/ppermute | solution.py:255
  55.4 10.3 %collective-permute-start.13 = (bf16[640,256]{1,0:T(8,128)(2,1)S(1)}, bf16[640,256]{1,0:T(8,128)(2,1)S(1)}, u32[]{:S(2)}, u32[]{:S(2)}) collective-permute-start(bf16[640,256]{1,0:T(8,128)(2,1)S(1)} %collective-permute-done.11.p1), channel_id=1, source_target_pairs={{0,16},{16,0},{1,17},{17,1},{2,18},{18,2},{3,19},{19,3},{4,20},{20... | collective-permute-start | bytes 983048 | tf_op jit(solution)/shard_map/ppermute | solution.py:255
  59.6 23.0 %collective-permute-start.8 = (bf16[640,256]{1,0:T(8,128)(2,1)}, bf16[640,256]{1,0:T(8,128)(2,1)}, u32[]{:S(2)}, u32[]{:S(2)}) collective-permute-start(bf16[640,256]{1,0:T(8,128)(2,1)} %collective-permute-done.7.p0), channel_id=1, source_target_pairs={{0,2},{2,0},{1,3},{3,1},{4,6},{6,4},{5,7},{7,5},{8,10},{10,8},{9,1... | collective-permute-start | bytes 983048 | tf_op jit(solution)/shard_map/ppermute | solution.py:255
  64.6 20.4 %collective-permute-start.5 = (bf16[640,256]{1,0:T(8,128)(2,1)S(1)}, bf16[640,256]{1,0:T(8,128)(2,1)}, u32[]{:S(2)}, u32[]{:S(2)}) collective-permute-start(bf16[640,256]{1,0:T(8,128)(2,1)S(1)} %collective-permute-done.3.p0), channel_id=1, source_target_pairs={{0,16},{16,0},{1,17},{17,1},{2,18},{18,2},{3,19},{19,3},{4,20},{20... | collective-permute-start | bytes 983048 | tf_op jit(solution)/shard_map/ppermute | solution.py:255
  66.5 16.1 %collective-permute-start.10 = (bf16[640,256]{1,0:T(8,128)(2,1)}, bf16[640,256]{1,0:T(8,128)(2,1)}, u32[]{:S(2)}, u32[]{:S(2)}) collective-permute-start(bf16[640,256]{1,0:T(8,128)(2,1)} %collective-permute-done.9.p2), channel_id=1, source_target_pairs={{0,2},{2,0},{1,3},{3,1},{4,6},{6,4},{5,7},{7,5},{8,10},{10,8},{9,1... | collective-permute-start | bytes 983048 | tf_op jit(solution)/shard_map/ppermute | solution.py:255
  71.8 51.7 %collective-permute-start.18 = (bf16[4,640,256]{2,1,0:T(8,128)(2,1)}, bf16[4,640,256]{2,1,0:T(8,128)(2,1)}, u32[]{:S(2)}, u32[]{:S(2)}) collective-permute-start(bf16[4,640,256]{2,1,0:T(8,128)(2,1)} %pad_maximum_fusion.refs_1_), channel_id=1, source_target_pairs={{0,1},{1,0},{2,3},{3,2},{4,5},{5,4},{6,7},{7,6},{8,9},{9,8},{10,11... | collective-permute-start | bytes 3932168 | tf_op jit(solution)/shard_map/ppermute | solution.py:255
  71.8 13.2 %collective-permute-start.6 = (bf16[640,256]{1,0:T(8,128)(2,1)}, bf16[640,256]{1,0:T(8,128)(2,1)}, u32[]{:S(2)}, u32[]{:S(2)}) collective-permute-start(bf16[640,256]{1,0:T(8,128)(2,1)} %collective-permute-done.4.p1), channel_id=1, source_target_pairs={{0,16},{16,0},{1,17},{17,1},{2,18},{18,2},{3,19},{19,3},{4,20},{20... | collective-permute-start | bytes 983048 | tf_op jit(solution)/shard_map/ppermute | solution.py:255
  79.5 3.1 %copy-start = (bf16[256,5120]{1,0:T(8,128)(2,1)}, bf16[256,5120]{1,0:T(8,128)(2,1)S(1)}, u32[]{:S(2)}) copy-start(bf16[256,5120]{1,0:T(8,128)(2,1)S(1)} %copy.18.values_ref) | copy-start | bytes 7864324
  82.6 2.5 %copy-start.2 = (bf16[256,1280]{1,0:T(8,128)(2,1)S(1)}, bf16[256,1280]{1,0:T(8,128)(2,1)}, u32[]{:S(2)}) copy-start(bf16[256,1280]{1,0:T(8,128)(2,1)} %queries_ref.1) | copy-start | bytes 1966084
  82.6 2.5 %copy-start.3 = (bf16[256,1280]{1,0:T(8,128)(2,1)S(1)}, bf16[256,1280]{1,0:T(8,128)(2,1)}, u32[]{:S(2)}) copy-start(bf16[256,1280]{1,0:T(8,128)(2,1)} %cotangent_ref.1) | copy-start | bytes 1966084
  92.0 11.0 %collective-permute-start.19 = (bf16[256,512]{1,0:T(8,128)(2,1)S(1)}, bf16[256,512]{1,0:T(8,128)(2,1)S(1)}, u32[]{:S(2)}, u32[]{:S(2)}) collective-permute-start(bf16[256,512]{1,0:T(8,128)(2,1)S(1)} %get-tuple-element.12.refs_3_), channel_id=1, source_target_pairs={{0,4},{4,8},{8,12},{12,0},{1,5},{5,9},{9,13},{13,1},{2,6},{6,10},{... | collective-permute-start | bytes 786440 | tf_op jit(solution)/shard_map/ppermute | solution.py:260
  92.0 14.0 %collective-permute-start.24 = (bf16[256,512]{1,0:T(8,128)(2,1)S(1)}, bf16[256,512]{1,0:T(8,128)(2,1)S(1)}, u32[]{:S(2)}, u32[]{:S(2)}) collective-permute-start(bf16[256,512]{1,0:T(8,128)(2,1)S(1)} %get-tuple-element.12.refs_3_), channel_id=1, source_target_pairs={{0,12},{4,0},{8,4},{12,8},{1,13},{5,1},{9,5},{13,9},{2,14},{6,2},{... | collective-permute-start | bytes 786440 | tf_op jit(solution)/shard_map/ppermute | solution.py:260
  103.0 10.5 %collective-permute-start.20 = (bf16[256,512]{1,0:T(8,128)(2,1)S(1)}, bf16[256,512]{1,0:T(8,128)(2,1)S(1)}, u32[]{:S(2)}, u32[]{:S(2)}) collective-permute-start(bf16[256,512]{1,0:T(8,128)(2,1)S(1)} %collective-permute-done.19.refs_5_), channel_id=1, source_target_pairs={{0,4},{4,8},{8,12},{12,0},{1,5},{5,9},{9,13},{13,1},{2,6},{6,10},{... | collective-permute-start | bytes 786440 | tf_op jit(solution)/shard_map/ppermute | solution.py:260
  103.0 10.6 %collective-permute-start.22 = (bf16[256,512]{1,0:T(8,128)(2,1)S(1)}, bf16[256,512]{1,0:T(8,128)(2,1)S(1)}, u32[]{:S(2)}, u32[]{:S(2)}) collective-permute-start(bf16[256,512]{1,0:T(8,128)(2,1)S(1)} %get-tuple-element.12.refs_3_), channel_id=1, source_target_pairs={{0,2},{2,0},{1,3},{3,1},{4,6},{6,4},{5,7},{7,5},{8,10},{10,8},{9,1... | collective-permute-start | bytes 786440 | tf_op jit(solution)/shard_map/ppermute | solution.py:255
  103.1 14.8 %collective-permute-start.23 = (bf16[256,512]{1,0:T(8,128)(2,1)S(1)}, bf16[256,512]{1,0:T(8,128)(2,1)S(1)}, u32[]{:S(2)}, u32[]{:S(2)}) collective-permute-start(bf16[256,512]{1,0:T(8,128)(2,1)S(1)} %collective-permute-done.19.refs_5_), channel_id=1, source_target_pairs={{0,2},{2,0},{1,3},{3,1},{4,6},{6,4},{5,7},{7,5},{8,10},{10,8},{9,1... | collective-permute-start | bytes 786440 | tf_op jit(solution)/shard_map/ppermute | solution.py:255
  106.0 17.5 %collective-permute-start.25 = (bf16[256,512]{1,0:T(8,128)(2,1)S(1)}, bf16[256,512]{1,0:T(8,128)(2,1)S(1)}, u32[]{:S(2)}, u32[]{:S(2)}) collective-permute-start(bf16[256,512]{1,0:T(8,128)(2,1)S(1)} %collective-permute-done.24.refs_7_), channel_id=1, source_target_pairs={{0,2},{2,0},{1,3},{3,1},{4,6},{6,4},{5,7},{7,5},{8,10},{10,8},{9,1... | collective-permute-start | bytes 786440 | tf_op jit(solution)/shard_map/ppermute | solution.py:255
  113.5 13.2 %collective-permute-start.21 = (bf16[256,512]{1,0:T(8,128)(2,1)S(1)}, bf16[256,512]{1,0:T(8,128)(2,1)S(1)}, u32[]{:S(2)}, u32[]{:S(2)}) collective-permute-start(bf16[256,512]{1,0:T(8,128)(2,1)S(1)} %collective-permute-done.20.refs_3_), channel_id=1, source_target_pairs={{0,2},{2,0},{1,3},{3,1},{4,6},{6,4},{5,7},{7,5},{8,10},{10,8},{9,1... | collective-permute-start | bytes 786440 | tf_op jit(solution)/shard_map/ppermute | solution.py:255
  (8 other events, 10.0 us)

commit v3 on v2

v3 whole, which is shorter than its diff:
```python
import functools

import jax
import jax.numpy as jnp
from jax import lax
from jax.experimental import pallas as pl
from jax.experimental.pallas import tpu as pltpu
from jax.sharding import PartitionSpec as P

HEAD = 128


EPSILON = 1e-06
ROPE_BASE = 1000000.0
SCALE = HEAD ** (-0.5)
VMEM_BYTES = 48 * 1024 * 1024
IN_VMEM = pl.BlockSpec(memory_space=pltpu.VMEM)


def rope_tables(length):
    half_size = HEAD // 2
    exponent = jnp.arange(half_size, dtype=jnp.float32) * (2.0 / HEAD)
    frequency = jnp.exp(-exponent * jnp.log(jnp.float32(ROPE_BASE)))
    angles = jnp.arange(length, dtype=jnp.float32)[:, None] * frequency[None, :]
    cosine_table = jnp.cos(angles)
    sine_table = jnp.sin(angles)
    return (
        jnp.concatenate([cosine_table, cosine_table], -1),
        jnp.concatenate([-sine_table, sine_table], -1),
    )


def product(left, right):
    return jnp.dot(left, right, preferred_element_type=jnp.float32)


def product_rows(left, right):
    return lax.dot_general(
        left, right, (((1,), (1,)), ((), ())), preferred_element_type=jnp.float32
    )


def features_of(own_ref, other_ref, block, offset, rows):
    blocks_held = own_ref.shape[1] // (2 * rows)
    here = block // blocks_held == lax.axis_index("sub")
    start = pl.multiple_of((block % blocks_held) * (2 * rows) + offset, 128)
    place = pl.ds(start, rows)
    return jnp.where(here, own_ref[:, place], other_ref[:, place])


def block_terms(own_ref, other_ref, block, pieces):
    replica = lax.axis_index("dp")
    rows = pieces[0].shape[0]
    near = features_of(own_ref, other_ref, block, replica * rows, rows)
    far = features_of(own_ref, other_ref, block, (1 - replica) * rows, rows)
    return (
        product(near, pieces[0][...]) + product(far, pieces[1][...]),
        product(near, pieces[2][...]) + product(far, pieces[3][...]),
    )


def block_from(distance):
    blocks = lax.axis_size("blk")
    return lax.rem(lax.axis_index("blk") + (blocks - distance), blocks)


def project_kernel(distances, own_ref, other_ref, weight_ref, *refs):
    sums_ref = refs[-1]
    group, replica = lax.axis_index("groups"), lax.axis_index("dp")
    half_rows = weight_ref.shape[1] // 2
    here = lax.axis_index("blk")
    first = features_of(own_ref, other_ref, here, 0, half_rows)
    second = features_of(own_ref, other_ref, here, half_rows, half_rows)
    totals = [
        product(first, weight_ref[j, :half_rows]) + product(second, weight_ref[j, half_rows:])
        for j in (group, 1 - group)
    ]
    for at, distance in enumerate(distances):
        pieces = refs[4 * at : 4 * at + 4]
        terms = block_terms(own_ref, other_ref, block_from(distance), pieces)
        totals = [total + term for total, term in zip(totals, terms)]
    sums_ref[group] = totals[0]
    sums_ref[1 - group] = totals[1]


def project(normed, normed_other, kv_weight, gathered):
    length = normed.shape[0]
    _, rows, columns = kv_weight.shape
    distances = tuple(distance for distance, _ in gathered)
    pieces = [piece for _, four in gathered for piece in four]
    return pl.pallas_call(
        functools.partial(project_kernel, distances),
        in_specs=[IN_VMEM] * (3 + len(pieces)),
        out_specs=IN_VMEM,
        out_shape=jax.ShapeDtypeStruct((2, length, columns), jnp.float32),
        compiler_params=pltpu.CompilerParams(vmem_limit_bytes=VMEM_BYTES),
        cost_estimate=pl.CostEstimate(
            flops=4 * length * rows * columns * (1 + len(distances)),
            bytes_accessed=7000000,
            transcendentals=0,
        ),
        name="project",
    )(normed, normed_other, kv_weight, *pieces)


def attention_body(raw_of, cosine, sine, queries_ref, cotangent_ref, grad_query_ref, pair_ref):
    length, columns = cosine.shape[0], pair_ref.shape[1] // 2
    key_heads = columns // HEAD
    group_size = queries_ref.shape[1] // columns
    key_at = lax.broadcasted_iota(jnp.int32, (length, length), 0)
    query_at = lax.broadcasted_iota(jnp.int32, (length, length), 1)
    causal = key_at <= query_at
    for head in range(key_heads):
        lanes = slice(head * HEAD, (head + 1) * HEAD)
        raw = raw_of(0, lanes)
        wide_keys = raw * cosine + pltpu.roll(raw, HEAD // 2, 1) * sine
        keys = wide_keys.astype(jnp.bfloat16)
        keys_across = wide_keys.T.astype(jnp.bfloat16)
        values = raw_of(1, lanes).astype(jnp.bfloat16)
        grad_rotated = jnp.zeros((length, HEAD), jnp.float32)
        grad_value = jnp.zeros((length, HEAD), jnp.float32)
        for member in range(group_size):
            start = (head * group_size + member) * HEAD
            query = queries_ref[:, start : start + HEAD]
            upstream = cotangent_ref[:, start : start + HEAD]
            scores = jnp.where(causal, product_rows(keys, query), -jnp.inf)
            peak = jnp.max(scores, 0, keepdims=True)
            exponentials = jnp.exp((scores - peak) * SCALE)
            probability = exponentials * (1.0 / jnp.sum(exponentials, 0, keepdims=True))
            grad_probability = product_rows(values, upstream)
            total = jnp.sum(probability * grad_probability, 0, keepdims=True)
            grad_scores = (probability * (grad_probability - total) * SCALE).astype(jnp.bfloat16)
            grad_rotated += product(grad_scores, query)
            grad_value += product(probability.astype(jnp.bfloat16), upstream)
            grad_query = product(keys_across, grad_scores)
            grad_query_ref[:, start : start + HEAD] = grad_query.T.astype(jnp.bfloat16)
        grad_key = grad_rotated * cosine - pltpu.roll(grad_rotated, HEAD // 2, 1) * sine
        pair_ref[:, lanes] = grad_key.astype(jnp.bfloat16)
        pair_ref[:, columns + head * HEAD : columns + (head + 1) * HEAD] = grad_value.astype(
            jnp.bfloat16
        )


def attention_kernel(
    distance, own_ref, other_ref, p0, p1, p2, p3, sums_ref, bias_ref, cosine_ref, sine_ref,
    queries_ref, cotangent_ref, grad_query_ref, pair_ref, raw_ref,
):
    group = lax.axis_index("groups")
    terms = block_terms(own_ref, other_ref, block_from(distance), (p0, p1, p2, p3))
    raw_ref[group] = sums_ref[group] + terms[0]
    raw_ref[1 - group] = sums_ref[1 - group] + terms[1]

    def raw_of(j, lanes):
        return raw_ref[j, :, lanes] + bias_ref[j : j + 1, lanes]

    attention_body(
        raw_of, cosine_ref[...], sine_ref[...], queries_ref, cotangent_ref, grad_query_ref, pair_ref
    )


def attention(distance, normed, normed_other, pieces, sums, bias, cosine, sine, queries, cotangent):
    length = normed.shape[0]
    columns = pieces[0].shape[1]
    operands = (normed, normed_other, *pieces, sums, bias, cosine, sine, queries, cotangent)
    return pl.pallas_call(
        functools.partial(attention_kernel, distance),
        in_specs=[IN_VMEM] * len(operands),
        out_specs=[IN_VMEM] * 2,
        scratch_shapes=[pltpu.VMEM(sums.shape, jnp.float32)],
        out_shape=[
            jax.ShapeDtypeStruct(queries.shape, jnp.bfloat16),
            jax.ShapeDtypeStruct((length, 2 * columns), jnp.bfloat16),
        ],
        compiler_params=pltpu.CompilerParams(vmem_limit_bytes=VMEM_BYTES),
        cost_estimate=pl.CostEstimate(
            flops=10 * length * length * queries.shape[1],
            bytes_accessed=5000000,
            transcendentals=length * length * queries.shape[1] // HEAD,
        ),
        name="attention",
    )(*operands)


def gradient_kernel(count, first, *refs):
    slabs, pairs = refs[1 : 1 + count], refs[1 + count : 1 + 2 * count]
    refs = refs[1 + 2 * count :]
    weight_ref, bias_ref = refs[-2:]
    columns = weight_ref.shape[2]
    total = None
    for slab, pair in zip(slabs, pairs):
        term = product(slab[0], pair[...])
        total = term if total is None else total + term
    for j in range(2):
        part = total[:, j * columns : (j + 1) * columns]
        weight_ref[j] = part if first else refs[0][j] + part

    @pl.when(pl.program_id(0) == 0)
    def _():
        total = None
        for pair in pairs:
            term = jnp.sum(pair[...].astype(jnp.float32), axis=0, keepdims=True)
            total = term if total is None else total + term
        for j in range(2):
            part = total[:, j * columns : (j + 1) * columns]
            bias_ref[j : j + 1, :] = part if first else refs[1][j : j + 1, :] + part


def gradient(at, slabs, pairs, sums):
    _, share, length = slabs.shape
    columns = pairs[0].shape[1] // 2
    count = len(pairs)
    tile = share // 2 if share % 32 == 0 else share

    def slab_spec(turn):
        return pl.BlockSpec((1, tile, length), lambda i, at: (at[turn], i, 0))

    weight_spec = pl.BlockSpec((2, tile, columns), lambda i, at: (0, i, 0))
    bias_spec = pl.BlockSpec((2, columns), lambda i, at: (0, 0))
    in_specs = [slab_spec(turn) for turn in range(count)]
    in_specs += [pl.BlockSpec((length, 2 * columns), lambda i, at: (0, 0))] * count
    if sums:
        in_specs += [weight_spec, bias_spec]
    return pl.pallas_call(
        functools.partial(gradient_kernel, count, sums is None),
        grid_spec=pltpu.PrefetchScalarGridSpec(
            num_scalar_prefetch=1,
            grid=(share // tile,),
            in_specs=in_specs,
            out_specs=[weight_spec, bias_spec],
        ),
        out_shape=[
            jax.ShapeDtypeStruct((2, share, columns), jnp.float32),
            jax.ShapeDtypeStruct((2, columns), jnp.float32),
        ],
        compiler_params=pltpu.CompilerParams(vmem_limit_bytes=VMEM_BYTES),
        cost_estimate=pl.CostEstimate(
            flops=4 * count * length * share * columns, bytes_accessed=5000000, transcendentals=0
        ),
        name="gradient",
    )(at, *([slabs] * count), *pairs, *(sums or ()))


def norm_kernel(values_ref, scale_ref, gain_ref, normed_ref, *slab_refs):
    blocks, replicas = lax.axis_size("blk"), lax.axis_size("dp")
    number = lax.axis_index("blk") * replicas + lax.axis_index("dp")
    half = blocks * replicas // 2
    share = values_ref.shape[1] // half

    def scaled(place):
        wide_values = values_ref[:, place].astype(jnp.float32)
        return wide_values * scale_ref[...] * gain_ref[:, place]

    for slab in range(half):
        place = pl.ds(slab * share, share)
        normed_ref[:, place] = scaled(place).astype(jnp.bfloat16)
    for turn, slab_ref in enumerate(slab_refs):
        slab = lax.rem(turn + number // 2, half)
        place = pl.ds(pl.multiple_of(slab * share, 128), share)
        slab_ref[...] = scaled(place).T.astype(jnp.bfloat16)


def norm(activations, scale, gain, slabs):
    length, features = activations.shape
    return pl.pallas_call(
        norm_kernel,
        in_specs=[IN_VMEM] * 3,
        out_specs=[IN_VMEM] * (1 + slabs),
        out_shape=[jax.ShapeDtypeStruct(activations.shape, jnp.bfloat16)]
        + [jax.ShapeDtypeStruct((features // slabs, length), jnp.bfloat16)] * slabs,
        compiler_params=pltpu.CompilerParams(vmem_limit_bytes=VMEM_BYTES),
        cost_estimate=pl.CostEstimate(
            flops=4 * length * features, bytes_accessed=6 * length * features, transcendentals=0
        ),
        name="norm",
    )(activations, scale, gain)


def swapped(block, axis):
    return lax.ppermute(block, axis, [(0, 1), (1, 0)])


def turned(block, axis, distance):
    size = lax.axis_size(axis)
    return lax.ppermute(block, axis, [(i, (i + distance) % size) for i in range(size)])


def after(block, *others):
    return lax.optimization_barrier((block, *others))[0]


def slab_route(turn):
    sequences = lax.axis_size("blk") * lax.axis_size("dp")
    half = sequences // 2
    route = []
    for source in range(sequences):
        for core in range(2):
            goal = half * core + (turn + source // 2) % half
            route.append((source * 2 + core, goal * 2 + source % 2))
    return route


def sent_slab(slab, turn):
    return lax.ppermute(slab, ("blk", "dp", "sub"), slab_route(turn))


def scale_and_gain(activations, norm_gain):
    core = lax.axis_index("sub")
    features = activations.shape[1]
    wide_values = activations.astype(jnp.float32)
    square_sum = jnp.sum(wide_values * wide_values, -1, keepdims=True)
    square_sum = square_sum + swapped(square_sum, "sub")
    gain = lax.dynamic_slice_in_dim(norm_gain, core * features, features, 0).astype(jnp.float32)
    return lax.rsqrt(square_sum / (2 * features) + EPSILON), gain


def local(activations, norm_gain, queries, cotangent, kv_weight, kv_bias):
    blocks, replicas = lax.axis_size("blk"), lax.axis_size("dp")
    group, block, replica = lax.axis_index("groups"), lax.axis_index("blk"), lax.axis_index("dp")
    core = lax.axis_index("sub")
    _, block_rows, columns = kv_weight.shape
    length = activations.shape[0]
    share = block_rows // replicas
    half = blocks * replicas // 2
    number = block * replicas + replica
    slab_here = number % half

    piece = lax.dynamic_slice(kv_weight, (group, replica * share, 0), (1, share, columns))[0]
    scale, gain = scale_and_gain(activations, norm_gain)
    cosine, sine = rope_tables(length)
    bias = kv_bias.astype(jnp.float32)

    if not (blocks == 4 and replicas == 2):
        return general(
            piece, activations, scale, gain, bias, cosine, sine, queries, cotangent
        )

    normed, *slabs = norm(activations, scale, gain[None, :], half)
    normed_other = swapped(normed, "sub")

    up, down = turned(piece, "blk", 1), turned(piece, "blk", -1)
    up, down, normed_other = lax.optimization_barrier((up, down, normed_other))
    twice = turned(up, "blk", 1)
    up_x, up_y = swapped(up, "dp"), swapped(up, "groups")
    down_x, down_y = swapped(down, "dp"), swapped(down, "groups")
    twice, up_x, up_y, down_x, down_y = lax.optimization_barrier(
        (twice, up_x, up_y, down_x, down_y)
    )
    twice_x, twice_y = swapped(twice, "dp"), swapped(twice, "groups")
    up_both, down_both = swapped(up_x, "groups"), swapped(down_y, "dp")
    slabs = [sent_slab(after(slab, twice), turn) for turn, slab in enumerate(slabs)]
    twice_x, twice_y, up_both, down_both, slabs[0] = lax.optimization_barrier(
        (twice_x, twice_y, up_both, down_both, slabs[0])
    )
    twice_both = swapped(twice_x, "groups")

    gathered = [(1, (up, up_x, up_y, up_both)), (-1, (down, down_x, down_y, down_both))]
    sums = project(normed, normed_other, kv_weight, gathered)
    sums = after(sums, slabs[1])
    grad_query, grad_pair = attention(
        2, normed, normed_other, (twice, twice_x, twice_y, twice_both), sums, bias, cosine, sine,
        queries, cotangent,
    )

    grad_pair, *slabs = lax.optimization_barrier((grad_pair, *slabs))
    slabs_own = jnp.stack(slabs)
    slabs_held = jnp.concatenate([slabs_own, swapped(slabs_own, "sub")])

    def slab_of(distance, same):
        source = replica if same else 1 - replica
        turn = (slab_here - (block - distance)) % half
        return (source != core) * half + turn

    pair_up, pair_down = turned(grad_pair, "blk", 1), turned(grad_pair, "blk", -1)
    pair_x = swapped(grad_pair, "dp")
    pair_up, pair_down, pair_x = lax.optimization_barrier((pair_up, pair_down, pair_x))
    pair_twice = turned(pair_up, "blk", 1)
    pair_up_x, pair_down_x = swapped(pair_up, "dp"), swapped(pair_down, "dp")
    pair_twice, pair_up_x = lax.optimization_barrier((pair_twice, pair_up_x))
    pair_twice_x = swapped(pair_twice, "dp")
    first = {
        (0, True): grad_pair,
        (0, False): pair_x,
        (1, True): pair_up,
        (-1, True): pair_down,
        (1, False): pair_up_x,
        (-1, False): pair_down_x,
    }
    last = {(2, True): pair_twice, (2, False): pair_twice_x}
    sums = None
    for some in (first, last):
        at = jnp.stack([slab_of(*which) for which in some]).astype(jnp.int32)
        sums = gradient(at, slabs_held, list(some.values()), sums)
    grad_weight, grad_bias = sums
    return (grad_query, grad_weight, grad_bias)


def plain_attention_kernel(
    raw_ref, bias_ref, cosine_ref, sine_ref, queries_ref, cotangent_ref, grad_query_ref, pair_ref
):
    def raw_of(j, lanes):
        return raw_ref[j, :, lanes] + bias_ref[j : j + 1, lanes]

    attention_body(
        raw_of, cosine_ref[...], sine_ref[...], queries_ref, cotangent_ref, grad_query_ref, pair_ref
    )


def general(piece, activations, scale, gain, bias, cosine, sine, queries, cotangent):
    core = lax.axis_index("sub")
    blocks, replicas = lax.axis_size("blk"), lax.axis_size("dp")
    length, features = activations.shape
    share, columns = piece.shape
    half = blocks * replicas // 2
    number = lax.axis_index("blk") * replicas + lax.axis_index("dp")
    normed = (activations.astype(jnp.float32) * scale * gain).astype(jnp.bfloat16)
    normed_other = swapped(normed, "sub")
    weight = lax.all_gather(piece, ("groups", "blk", "dp"), axis=0, tiled=True)
    weight = weight.reshape(2, -1, columns)
    slabs = []
    for turn in range(half):
        slab = (turn + number // 2) % half
        slabs.append(sent_slab(lax.dynamic_slice_in_dim(normed, slab * share, share, 1), turn))
    slabs_own = jnp.stack(slabs)
    slabs_other = swapped(slabs_own, "sub")

    def part(values, rows):
        taken = lax.dynamic_slice_in_dim(weight, rows * features, features, 1)
        return jnp.einsum("tr,krc->ktc", values, taken, preferred_element_type=jnp.float32)

    raw_pair = part(normed, core) + part(normed_other, 1 - core)
    grad_query, grad_pair = pl.pallas_call(
        plain_attention_kernel,
        in_specs=[IN_VMEM] * 6,
        out_specs=[IN_VMEM] * 2,
        out_shape=[
            jax.ShapeDtypeStruct(queries.shape, jnp.bfloat16),
            jax.ShapeDtypeStruct((length, 2 * columns), jnp.bfloat16),
        ],
        compiler_params=pltpu.CompilerParams(vmem_limit_bytes=VMEM_BYTES),
        name="plain_attention",
    )(raw_pair, bias, cosine, sine, queries, cotangent)

    everyone = lax.all_gather(grad_pair, ("blk", "dp"), axis=0)
    grad_bias = jnp.sum(everyone.astype(jnp.float32), axis=(0, 1)).reshape(2, columns)
    paired = everyone.reshape(half, 2, -1, 2 * columns)
    order = (number % half - jnp.arange(half)) % half
    grads_own = jnp.take(lax.dynamic_index_in_dim(paired, core, 1, False), order, axis=0)
    grads_other = jnp.take(lax.dynamic_index_in_dim(paired, 1 - core, 1, False), order, axis=0)
    grad_weight = jnp.einsum(
        "ntr,ntc->rc", slabs_own, grads_own, preferred_element_type=jnp.float32
    ) + jnp.einsum("ntr,ntc->rc", slabs_other, grads_other, preferred_element_type=jnp.float32)
    grad_weight = jnp.moveaxis(grad_weight.reshape(share, 2, columns), 1, 0)
    return (grad_query, grad_weight, grad_bias)


def solution(mesh):
    placed = (
        P(("groups", "blk", "dp"), "sub"),
        P(),
        P(("groups", "blk", "dp"), "sub"),
        P(("groups", "blk", "dp"), "sub"),
        P(None, "blk", "sub"),
        P(None, "sub"),
    )
    return jax.shard_map(
        local,
        mesh=mesh,
        in_specs=placed,
        out_specs=(
            P(("groups", "blk", "dp"), "sub"),
            P(None, ("groups", "blk", "dp"), "sub"),
            P("groups", "sub"),
        ),
        check_vma=False,
    )
```

time: 131 us -> 124 us (0.947)
  local copies, waits for them, and re-layouts: 9.65 us -> 4.87 us
  waiting for transfers between devices: 56.7 us -> 60.5 us
  Pallas kernels: 18 us -> 14.7 us
  other arithmetic: 5.32 us -> 3.82 us
    ppermute x16, waiting for transfers between devices: 11.3 us -> 23.9 us  [swapped(): return lax.ppermute(block, axis, [(0, 1), (1, 0)])]
    ppermute x4, waiting for transfers between devices: 17 us -> 4.84 us  [sent_slab(): return lax.ppermute(slab, ('blk', 'dp', 'sub'), slab_route(turn))]
    pallas_call x6 -> x5, Pallas kernels: 18 us -> 14.7 us  [the longest x1 6.39 us: attention(): pl.pallas_call(functools.partial(attention_kernel, distance), in_specs=[I...]
    ppermute x6, waiting for transfers between devices: 28.5 us -> 31.8 us  [turned(): lax.ppermute(block, axis, [(i, (i + distance) % size) for i in range(size)])]
    select_n x1 -> x0, local copies, waits for them, and re-layouts: 2.98 us -> none  [local(): jnp.where(core == 0, jnp.concatenate([normed, normed_other], 1), jnp.conc...]
    unnamed x29 -> x32, local copies, waits for them, and re-layouts: 5.5 us -> 3.54 us
    select_n x1 -> x0, other arithmetic: 1.83 us -> none  [local(): jnp.where(core == 0, jnp.concatenate([normed, normed_other], 1), jnp.conc...]
    reduce_sum x1, other arithmetic: 0.37 us -> 1.76 us  [scale_and_gain(): square_sum = jnp.sum(wide_values * wide_values, -1, keepdims=True)]
  transfers between devices with their start and end apart: 26 -> 26, of which waited for: 11 -> 19; matrix products, arithmetic and copies ran while one was open for 8% -> 3% of each run, Pallas kernels for 11% -> 9%
where the time goes in v3:
time: 124 us; the launch traced here: 123 us
  waiting for transfers between devices  60.5 us (49%)
  starting transfers between devices  38.7 us (31%)
  Pallas kernels  14.7 us (12%)
  local copies, waits for them, and re-layouts  4.87 us (4%)
  other arithmetic  3.82 us (3%)
    ppermute x6, waiting for transfers between devices, turned(): lax.ppermute(block, axis, [(i, (i + distance) % size) for i in range(size)])  31.8 us
    ppermute x16, waiting for transfers between devices, swapped(): return lax.ppermute(block, axis, [(0, 1), (1, 0)])  23.9 us
    ppermute x16, starting transfers between devices, swapped(): return lax.ppermute(block, axis, [(0, 1), (1, 0)])  20 us
    ppermute x6, starting transfers between devices, turned(): lax.ppermute(block, axis, [(i, (i + distance) % size) for i in range(size)])  11.3 us
    ppermute x4, starting transfers between devices, sent_slab(): return lax.ppermute(slab, ('blk', 'dp', 'sub'), slab_route(turn))  7.38 us
    pallas_call x1, Pallas kernels, attention(): pl.pallas_call(functools.partial(attention_kernel, distance), in_specs=[I...  6.39 us
    ppermute x4, waiting for transfers between devices, sent_slab(): return lax.ppermute(slab, ('blk', 'dp', 'sub'), slab_route(turn))  4.84 us
    pallas_call x2, Pallas kernels, gradient(): pl.pallas_call(functools.partial(gradient_kernel, count, sums is None), g...  4.49 us
  transfers between devices with their start and end apart: 26, of which 19 were waited for; matrix products, arithmetic and copies ran while one was open for 3% of the time, Pallas kernels for 9%

profile of v3, /device:TPU:0, one launch (start us, length us, event | category | flops | bytes accessed | tf_op | source)
XLA Modules:
  0.0 123.4 jit_solution(18431143979241400856)
XLA Ops:
  0.6 1.8 %multiply_reduce_fusion = f32[256]{0:T(256)S(1)} fusion(bf16[256,2560]{1,0:T(8,128)(2,1)} %values_ref.1), kind=kLoop, calls=%fused_computation | loop fusion | flops 1965824 | bytes 1311744 | tf_op jit(solution)/shard_map/reduce_sum | solution.py:310
  7.7 2.8 %collective-permute-start.1 = (bf16[640,256]{1,0:T(8,128)(2,1)S(1)}, bf16[640,256]{1,0:T(8,128)(2,1)S(1)}, u32[]{:S(2)}, u32[]{:S(2)}) collective-permute-start(bf16[640,256]{1,0:T(8,128)(2,1)S(1)} %dynamic-slice_bitcast_fusion), channel_id=1, source_target_pairs={{0,4},{4,8},{8,12},{12,0},{1,5},{5,9},{9,13},{13,1},{2,6},{6,10},{... | collective-permute-start | bytes 983048 | tf_op jit(solution)/shard_map/ppermute | solution.py:284
  10.5 2.1 %collective-permute-start.2 = (bf16[640,256]{1,0:T(8,128)(2,1)S(1)}, bf16[640,256]{1,0:T(8,128)(2,1)S(1)}, u32[]{:S(2)}, u32[]{:S(2)}) collective-permute-start(bf16[640,256]{1,0:T(8,128)(2,1)S(1)} %dynamic-slice_bitcast_fusion), channel_id=1, source_target_pairs={{0,12},{4,0},{8,4},{12,8},{1,13},{5,1},{9,5},{13,9},{2,14},{6,2},{... | collective-permute-start | bytes 983048 | tf_op jit(solution)/shard_map/ppermute | solution.py:284
  12.6 8.5 %collective-permute-done.1.refs_0_ = bf16[640,256]{1,0:T(8,128)(2,1)S(1)} collective-permute-done((bf16[640,256]{1,0:T(8,128)(2,1)S(1)}, bf16[640,256]{1,0:T(8,128)(2,1)S(1)}, u32[]{:S(2)}, u32[]{:S(2)}) %collective-permute-start.1) | collective-permute-done | bytes 327712 | tf_op jit(solution)/shard_map/ppermute | solution.py:284
  21.0 6.1 %collective-permute-done.2.refs_4_ = bf16[640,256]{1,0:T(8,128)(2,1)S(1)} collective-permute-done((bf16[640,256]{1,0:T(8,128)(2,1)S(1)}, bf16[640,256]{1,0:T(8,128)(2,1)S(1)}, u32[]{:S(2)}, u32[]{:S(2)}) %collective-permute-start.2) | collective-permute-done | bytes 327712 | tf_op jit(solution)/shard_map/ppermute | solution.py:284
  28.3 1.5 %collective-permute-start.5 = (bf16[640,256]{1,0:T(8,128)(2,1)S(1)}, bf16[640,256]{1,0:T(8,128)(2,1)S(1)}, u32[]{:S(2)}, u32[]{:S(2)}) collective-permute-start(bf16[640,256]{1,0:T(8,128)(2,1)S(1)} %collective-permute-done.1.refs_0_), channel_id=1, source_target_pairs={{0,2},{2,0},{1,3},{3,1},{4,6},{6,4},{5,7},{7,5},{8,10},{10,8},{9,1... | collective-permute-start | bytes 983048 | tf_op jit(solution)/shard_map/ppermute | solution.py:279
  29.8 1.5 %collective-permute-start.6 = (bf16[640,256]{1,0:T(8,128)(2,1)S(1)}, bf16[640,256]{1,0:T(8,128)(2,1)S(1)}, u32[]{:S(2)}, u32[]{:S(2)}) collective-permute-start(bf16[640,256]{1,0:T(8,128)(2,1)S(1)} %collective-permute-done.1.refs_0_), channel_id=1, source_target_pairs={{0,16},{16,0},{1,17},{17,1},{2,18},{18,2},{3,19},{19,3},{4,20},{20... | collective-permute-start | bytes 983048 | tf_op jit(solution)/shard_map/ppermute | solution.py:279
  32.3 5.7 %collective-permute-done.4.p0 = bf16[640,256]{1,0:T(8,128)(2,1)S(1)} collective-permute-done((bf16[640,256]{1,0:T(8,128)(2,1)S(1)}, bf16[640,256]{1,0:T(8,128)(2,1)S(1)}, u32[]{:S(2)}, u32[]{:S(2)}) %collective-permute-start.4) | collective-permute-done | bytes 327712 | tf_op jit(solution)/shard_map/ppermute | solution.py:284
  38.9 1.5 %collective-permute-done.6.refs_2_ = bf16[640,256]{1,0:T(8,128)(2,1)S(1)} collective-permute-done((bf16[640,256]{1,0:T(8,128)(2,1)S(1)}, bf16[640,256]{1,0:T(8,128)(2,1)S(1)}, u32[]{:S(2)}, u32[]{:S(2)}) %collective-permute-start.6) | collective-permute-done | bytes 327712 | tf_op jit(solution)/shard_map/ppermute | solution.py:279
  40.4 4.2 %collective-permute-done.7.refs_5_ = bf16[640,256]{1,0:T(8,128)(2,1)S(1)} collective-permute-done((bf16[640,256]{1,0:T(8,128)(2,1)S(1)}, bf16[640,256]{1,0:T(8,128)(2,1)S(1)}, u32[]{:S(2)}, u32[]{:S(2)}) %collective-permute-start.7) | collective-permute-done | bytes 327712 | tf_op jit(solution)/shard_map/ppermute | solution.py:279
  46.4 1.5 %collective-permute-start.10 = (bf16[640,256]{1,0:T(8,128)(2,1)S(1)}, bf16[640,256]{1,0:T(8,128)(2,1)S(1)}, u32[]{:S(2)}, u32[]{:S(2)}) collective-permute-start(bf16[640,256]{1,0:T(8,128)(2,1)S(1)} %collective-permute-done.4.p0), channel_id=1, source_target_pairs={{0,16},{16,0},{1,17},{17,1},{2,18},{18,2},{3,19},{19,3},{4,20},{20... | collective-permute-start | bytes 983048 | tf_op jit(solution)/shard_map/ppermute | solution.py:279
  48.5 1.5 %collective-permute-start.12 = (bf16[640,256]{1,0:T(8,128)(2,1)S(1)}, bf16[640,256]{1,0:T(8,128)(2,1)S(1)}, u32[]{:S(2)}, u32[]{:S(2)}) collective-permute-start(bf16[640,256]{1,0:T(8,128)(2,1)S(1)} %collective-permute-done.8.refs_6_), channel_id=1, source_target_pairs={{0,2},{2,0},{1,3},{3,1},{4,6},{6,4},{5,7},{7,5},{8,10},{10,8},{9,1... | collective-permute-start | bytes 983048 | tf_op jit(solution)/shard_map/ppermute | solution.py:279
  49.9 1.6 %collective-permute-start.13 = (bf16[640,256]{1,0:T(8,128)(2,1)}, bf16[640,256]{1,0:T(8,128)(2,1)S(1)}, u32[]{:S(2)}, u32[]{:S(2)}) collective-permute-start(bf16[640,256]{1,0:T(8,128)(2,1)} %copy-done.5), channel_id=1, source_target_pairs={{0,0},{1,8},{2,1},{3,9},{4,2},{5,10},{6,3},{7,11},{8,4},{9,12},{10... | collective-permute-start | bytes 983048 | tf_op jit(solution)/shard_map/ppermute | solution.py:303
  51.6 5.0 %collective-permute-done.9.p1 = bf16[640,256]{1,0:T(8,128)(2,1)S(1)} collective-permute-done((bf16[640,256]{1,0:T(8,128)(2,1)S(1)}, bf16[640,256]{1,0:T(8,128)(2,1)S(1)}, u32[]{:S(2)}, u32[]{:S(2)}) %collective-permute-start.9) | collective-permute-done | bytes 327712 | tf_op jit(solution)/shard_map/ppermute | solution.py:279
  56.5 2.4 %collective-permute-start.15 = (bf16[640,256]{1,0:T(8,128)(2,1)}, bf16[640,256]{1,0:T(8,128)(2,1)S(1)}, u32[]{:S(2)}, u32[]{:S(2)}) collective-permute-start(bf16[640,256]{1,0:T(8,128)(2,1)} %copy-done.4), channel_id=1, source_target_pairs={{0,2},{1,10},{2,3},{3,11},{4,4},{5,12},{6,5},{7,13},{8,6},{9,14},{... | collective-permute-start | bytes 983048 | tf_op jit(solution)/shard_map/ppermute | solution.py:303
  59.6 1.7 %collective-permute-done.11.refs_3_ = bf16[640,256]{1,0:T(8,128)(2,1)S(1)} collective-permute-done((bf16[640,256]{1,0:T(8,128)(2,1)S(1)}, bf16[640,256]{1,0:T(8,128)(2,1)S(1)}, u32[]{:S(2)}, u32[]{:S(2)}) %collective-permute-start.11) | collective-permute-done | bytes 327712 | tf_op jit(solution)/shard_map/ppermute | solution.py:279
  61.4 2.7 %collective-permute-start.17 = (bf16[640,256]{1,0:T(8,128)(2,1)S(1)}, bf16[640,256]{1,0:T(8,128)(2,1)S(1)}, u32[]{:S(2)}, u32[]{:S(2)}) collective-permute-start(bf16[640,256]{1,0:T(8,128)(2,1)S(1)} %get-tuple-element.66), channel_id=1, source_target_pairs={{0,6},{1,14},{2,7},{3,15},{4,0},{5,8},{6,1},{7,9},{8,2},{9,10},{10... | collective-permute-start | bytes 983048 | tf_op jit(solution)/shard_map/ppermute | solution.py:303
  64.1 1.6 %collective-permute-start.14 = (bf16[640,256]{1,0:T(8,128)(2,1)S(1)}, bf16[640,256]{1,0:T(8,128)(2,1)S(1)}, u32[]{:S(2)}, u32[]{:S(2)}) collective-permute-start(bf16[640,256]{1,0:T(8,128)(2,1)S(1)} %collective-permute-done.9.p1), channel_id=1, source_target_pairs={{0,16},{16,0},{1,17},{17,1},{2,18},{18,2},{3,19},{19,3},{4,20},{20... | collective-permute-start | bytes 983048 | tf_op jit(solution)/shard_map/ppermute | solution.py:279
  66.4 2.8 %project.1.sums_ref = f32[2,256,256]{2,1,0:T(8,128)S(1)} custom-call(bf16[256,2560]{1,0:T(8,128)(2,1)S(1)} %get-tuple-element.42.own_ref, bf16[256,2560]{1,0:T(8,128)(2,1)S(1)} %collective-permute-done.3.other_ref, bf16[2,1280,256]{2,1,0:T(8,128)(2,1)} %weight_ref.1, bf16[640,256]{1,0:T(8,128)(2,1)S(1)} %collective-permute-done.1.refs_0_, ...), custom_call_target="tpu_custom_call" | custom-call | flops 1006632960 | bytes 7000000 | tf_op jit(solution)/shard_map/project/pallas_call | solution.py:91
  69.5 2.7 %collective-permute-done.14.p3 = bf16[640,256]{1,0:T(8,128)(2,1)S(1)} collective-permute-done((bf16[640,256]{1,0:T(8,128)(2,1)S(1)}, bf16[640,256]{1,0:T(8,128)(2,1)S(1)}, u32[]{:S(2)}, u32[]{:S(2)}) %collective-permute-start.14) | collective-permute-done | bytes 327712 | tf_op jit(solution)/shard_map/ppermute | solution.py:279
  72.2 6.4 %attention.1 = (bf16[256,1280]{1,0:T(8,128)(2,1)}, bf16[256,512]{1,0:T(8,128)(2,1)S(1)}) custom-call(bf16[256,2560]{1,0:T(8,128)(2,1)S(1)} %get-tuple-element.42.own_ref, bf16[256,2560]{1,0:T(8,128)(2,1)} %copy-done.1, bf16[640,256]{1,0:T(8,128)(2,1)S(1)} %collective-permute-done.4.p0, bf16[640,256]{1,0:T(8,128)(2,1)S(1)} %collective-permute-done.9.p1, ...), custom_call_target="tpu_custom_call" | custom-call | flops 838860800 | bytes 5000000 | tf_op jit(solution)/shard_map/attention/pallas_call | solution.py:165
  78.6 4.6 %collective-permute-done.16 = bf16[640,256]{1,0:T(8,128)(2,1)S(1)} collective-permute-done((bf16[640,256]{1,0:T(8,128)(2,1)S(1)}, bf16[640,256]{1,0:T(8,128)(2,1)S(1)}, u32[]{:S(2)}, u32[]{:S(2)}) %collective-permute-start.16) | collective-permute-done | bytes 327712 | tf_op jit(solution)/shard_map/ppermute | solution.py:303
  84.6 3.2 %collective-permute-start.19 = (bf16[256,512]{1,0:T(8,128)(2,1)S(1)}, bf16[256,512]{1,0:T(8,128)(2,1)S(1)}, u32[]{:S(2)}, u32[]{:S(2)}) collective-permute-start(bf16[256,512]{1,0:T(8,128)(2,1)S(1)} %get-tuple-element.71.refs_7_), channel_id=1, source_target_pairs={{0,4},{4,8},{8,12},{12,0},{1,5},{5,9},{9,13},{13,1},{2,6},{6,10},{... | collective-permute-start | bytes 786440 | tf_op jit(solution)/shard_map/ppermute | solution.py:284
  88.5 5.1 %collective-permute-start.21 = (bf16[256,512]{1,0:T(8,128)(2,1)S(1)}, bf16[256,512]{1,0:T(8,128)(2,1)S(1)}, u32[]{:S(2)}, u32[]{:S(2)}) collective-permute-start(bf16[256,512]{1,0:T(8,128)(2,1)S(1)} %get-tuple-element.71.refs_7_), channel_id=1, source_target_pairs={{0,2},{2,0},{1,3},{3,1},{4,6},{6,4},{5,7},{7,5},{8,10},{10,8},{9,1... | collective-permute-start | bytes 786440 | tf_op jit(solution)/shard_map/ppermute | solution.py:279
  95.6 5.0 %collective-permute-done.20.refs_10_ = bf16[256,512]{1,0:T(8,128)(2,1)S(1)} collective-permute-done((bf16[256,512]{1,0:T(8,128)(2,1)S(1)}, bf16[256,512]{1,0:T(8,128)(2,1)S(1)}, u32[]{:S(2)}, u32[]{:S(2)}) %collective-permute-start.20) | collective-permute-done | bytes 262176 | tf_op jit(solution)/shard_map/ppermute | solution.py:284
  102.0 1.9 %collective-permute-start.23 = (bf16[256,512]{1,0:T(8,128)(2,1)S(1)}, bf16[256,512]{1,0:T(8,128)(2,1)S(1)}, u32[]{:S(2)}, u32[]{:S(2)}) collective-permute-start(bf16[256,512]{1,0:T(8,128)(2,1)S(1)} %collective-permute-done.19.refs_9_), channel_id=1, source_target_pairs={{0,2},{2,0},{1,3},{3,1},{4,6},{6,4},{5,7},{7,5},{8,10},{10,8},{9,1... | collective-permute-start | bytes 786440 | tf_op jit(solution)/shard_map/ppermute | solution.py:279
  105.2 5.5 %collective-permute-done.22.refs_3_ = bf16[256,512]{1,0:T(8,128)(2,1)S(1)} collective-permute-done((bf16[256,512]{1,0:T(8,128)(2,1)S(1)}, bf16[256,512]{1,0:T(8,128)(2,1)S(1)}, u32[]{:S(2)}, u32[]{:S(2)}) %collective-permute-start.22) | collective-permute-done | bytes 262176 | tf_op jit(solution)/shard_map/ppermute | solution.py:284
  111.3 2.2 %collective-permute-start.24 = (bf16[256,512]{1,0:T(8,128)(2,1)S(1)}, bf16[256,512]{1,0:T(8,128)(2,1)S(1)}, u32[]{:S(2)}, u32[]{:S(2)}) collective-permute-start(bf16[256,512]{1,0:T(8,128)(2,1)S(1)} %collective-permute-done.22.refs_3_), channel_id=1, source_target_pairs={{0,2},{2,0},{1,3},{3,1},{4,6},{6,4},{5,7},{7,5},{8,10},{10,8},{9,1... | collective-permute-start | bytes 786440 | tf_op jit(solution)/shard_map/ppermute | solution.py:279
  113.6 3.3 %collective-permute-done.25.refs_12_ = bf16[256,512]{1,0:T(8,128)(2,1)S(1)} collective-permute-done((bf16[256,512]{1,0:T(8,128)(2,1)S(1)}, bf16[256,512]{1,0:T(8,128)(2,1)S(1)}, u32[]{:S(2)}, u32[]{:S(2)}) %collective-permute-start.25) | collective-permute-done | bytes 262176 | tf_op jit(solution)/shard_map/ppermute | solution.py:279
  116.9 2.2 %gradient.2 = (f32[2,640,256]{2,1,0:T(8,128)S(1)}, f32[2,256]{1,0:T(2,128)S(1)}) custom-call(s32[6]{0:T(128)S(1)} %stack.59.refs_0_, bf16[8,640,256]{2,1,0:T(8,128)(2,1)S(1)} %constant_dynamic-update-slice_fusion.refs_1_.refs_2_.refs_3_.refs_4_.refs_5_.refs_6_, ...), custom_call_target="tpu_custom_call" | custom-call | flops 1006632960 | bytes 5000000 | tf_op jit(solution)/shard_map/gradient/pallas_call | solution.py:223
  119.1 2.0 %collective-permute-done.24.refs_4_ = bf16[256,512]{1,0:T(8,128)(2,1)S(1)} collective-permute-done((bf16[256,512]{1,0:T(8,128)(2,1)S(1)}, bf16[256,512]{1,0:T(8,128)(2,1)S(1)}, u32[]{:S(2)}, u32[]{:S(2)}) %collective-permute-start.24) | collective-permute-done | bytes 262176 | tf_op jit(solution)/shard_map/ppermute | solution.py:279
  121.2 2.3 %gradient.3 = (f32[2,640,256]{2,1,0:T(8,128)}, f32[2,256]{1,0:T(2,128)}) custom-call(s32[2]{0:T(128)S(1)} %pad_add_fusion.refs_0_, bf16[8,640,256]{2,1,0:T(8,128)(2,1)S(1)} %constant_dynamic-update-slice_fusion.refs_1_.refs_2_.refs_3_.refs_4_.refs_5_.refs_6_, ...), custom_call_target="tpu_custom_call" | custom-call | flops 335544320 | bytes 5000000 | tf_op jit(solution)/shard_map/gradient/pallas_call | solution.py:223
  (72 shorter events, 19.5 us)
Async XLA Ops:
  2.4 1.3 %collective-permute-start = (f32[256,1]{0,1:T(1,128)S(1)}, f32[256,1]{0,1:T(1,128)S(1)}, u32[]{:S(2)}, u32[]{:S(2)}) collective-permute-start(f32[256,1]{0,1:T(1,128)S(1)} %bitcast.23), channel_id=1, source_target_pairs={{0,1},{1,0},{2,3},{3,2},{4,5},{5,4},{6,7},{7,6},{8,9},{9,8},{10,11... | collective-permute-start | bytes 3080 | tf_op jit(solution)/shard_map/ppermute | solution.py:279
  3.9 62.3 %copy-start.13 = (bf16[2,256]{1,0:T(2,128)(2,1)S(1)}, bf16[2,256]{1,0:T(2,128)(2,1)}, u32[]{:S(2)}) copy-start(bf16[2,256]{1,0:T(2,128)(2,1)} %param.11) | copy-start | bytes 3076
  6.4 20.8 %collective-permute-start.3 = (bf16[256,2560]{1,0:T(8,128)(2,1)S(1)}, bf16[256,2560]{1,0:T(8,128)(2,1)S(1)}, u32[]{:S(2)}, u32[]{:S(2)}) collective-permute-start(bf16[256,2560]{1,0:T(8,128)(2,1)S(1)} %get-tuple-element.42.own_ref), channel_id=1, source_target_pairs={{0,1},{1,0},{2,3},{3,2},{4,5},{5,4},{6,7},{7,6},{8,9},{9,8},{10,11... | collective-permute-start | bytes 3932168 | tf_op jit(solution)/shard_map/ppermute | solution.py:279
  7.7 13.4 %collective-permute-start.1 = (bf16[640,256]{1,0:T(8,128)(2,1)S(1)}, bf16[640,256]{1,0:T(8,128)(2,1)S(1)}, u32[]{:S(2)}, u32[]{:S(2)}) collective-permute-start(bf16[640,256]{1,0:T(8,128)(2,1)S(1)} %dynamic-slice_bitcast_fusion), channel_id=1, source_target_pairs={{0,4},{4,8},{8,12},{12,0},{1,5},{5,9},{9,13},{13,1},{2,6},{6,10},{... | collective-permute-start | bytes 983048 | tf_op jit(solution)/shard_map/ppermute | solution.py:284
  10.5 16.7 %collective-permute-start.2 = (bf16[640,256]{1,0:T(8,128)(2,1)S(1)}, bf16[640,256]{1,0:T(8,128)(2,1)S(1)}, u32[]{:S(2)}, u32[]{:S(2)}) collective-permute-start(bf16[640,256]{1,0:T(8,128)(2,1)S(1)} %dynamic-slice_bitcast_fusion), channel_id=1, source_target_pairs={{0,12},{4,0},{8,4},{12,8},{1,13},{5,1},{9,5},{13,9},{2,14},{6,2},{... | collective-permute-start | bytes 983048 | tf_op jit(solution)/shard_map/ppermute | solution.py:284
  27.2 42.1 %copy-start.1 = (bf16[256,2560]{1,0:T(8,128)(2,1)}, bf16[256,2560]{1,0:T(8,128)(2,1)S(1)}, u32[]{:S(2)}) copy-start(bf16[256,2560]{1,0:T(8,128)(2,1)S(1)} %collective-permute-done.3.other_ref) | copy-start | bytes 3932164
  27.2 10.9 %collective-permute-start.4 = (bf16[640,256]{1,0:T(8,128)(2,1)S(1)}, bf16[640,256]{1,0:T(8,128)(2,1)S(1)}, u32[]{:S(2)}, u32[]{:S(2)}) collective-permute-start(bf16[640,256]{1,0:T(8,128)(2,1)S(1)} %collective-permute-done.1.refs_0_), channel_id=1, source_target_pairs={{0,4},{4,8},{8,12},{12,0},{1,5},{5,9},{9,13},{13,1},{2,6},{6,10},{... | collective-permute-start | bytes 983048 | tf_op jit(solution)/shard_map/ppermute | solution.py:284
  28.3 10.6 %collective-permute-start.5 = (bf16[640,256]{1,0:T(8,128)(2,1)S(1)}, bf16[640,256]{1,0:T(8,128)(2,1)S(1)}, u32[]{:S(2)}, u32[]{:S(2)}) collective-permute-start(bf16[640,256]{1,0:T(8,128)(2,1)S(1)} %collective-permute-done.1.refs_0_), channel_id=1, source_target_pairs={{0,2},{2,0},{1,3},{3,1},{4,6},{6,4},{5,7},{7,5},{8,10},{10,8},{9,1... | collective-permute-start | bytes 983048 | tf_op jit(solution)/shard_map/ppermute | solution.py:279
  29.8 10.6 %collective-permute-start.6 = (bf16[640,256]{1,0:T(8,128)(2,1)S(1)}, bf16[640,256]{1,0:T(8,128)(2,1)S(1)}, u32[]{:S(2)}, u32[]{:S(2)}) collective-permute-start(bf16[640,256]{1,0:T(8,128)(2,1)S(1)} %collective-permute-done.1.refs_0_), channel_id=1, source_target_pairs={{0,16},{16,0},{1,17},{17,1},{2,18},{18,2},{3,19},{19,3},{4,20},{20... | collective-permute-start | bytes 983048 | tf_op jit(solution)/shard_map/ppermute | solution.py:279
  31.3 13.4 %collective-permute-start.7 = (bf16[640,256]{1,0:T(8,128)(2,1)S(1)}, bf16[640,256]{1,0:T(8,128)(2,1)S(1)}, u32[]{:S(2)}, u32[]{:S(2)}) collective-permute-start(bf16[640,256]{1,0:T(8,128)(2,1)S(1)} %collective-permute-done.2.refs_4_), channel_id=1, source_target_pairs={{0,2},{2,0},{1,3},{3,1},{4,6},{6,4},{5,7},{7,5},{8,10},{10,8},{9,1... | collective-permute-start | bytes 983048 | tf_op jit(solution)/shard_map/ppermute | solution.py:279
  31.8 14.1 %collective-permute-start.8 = (bf16[640,256]{1,0:T(8,128)(2,1)S(1)}, bf16[640,256]{1,0:T(8,128)(2,1)S(1)}, u32[]{:S(2)}, u32[]{:S(2)}) collective-permute-start(bf16[640,256]{1,0:T(8,128)(2,1)S(1)} %collective-permute-done.2.refs_4_), channel_id=1, source_target_pairs={{0,16},{16,0},{1,17},{17,1},{2,18},{18,2},{3,19},{19,3},{4,20},{20... | collective-permute-start | bytes 983048 | tf_op jit(solution)/shard_map/ppermute | solution.py:279
  45.9 10.6 %collective-permute-start.9 = (bf16[640,256]{1,0:T(8,128)(2,1)S(1)}, bf16[640,256]{1,0:T(8,128)(2,1)S(1)}, u32[]{:S(2)}, u32[]{:S(2)}) collective-permute-start(bf16[640,256]{1,0:T(8,128)(2,1)S(1)} %collective-permute-done.4.p0), channel_id=1, source_target_pairs={{0,2},{2,0},{1,3},{3,1},{4,6},{6,4},{5,7},{7,5},{8,10},{10,8},{9,1... | collective-permute-start | bytes 983048 | tf_op jit(solution)/shard_map/ppermute | solution.py:279
  46.4 12.6 %collective-permute-start.10 = (bf16[640,256]{1,0:T(8,128)(2,1)S(1)}, bf16[640,256]{1,0:T(8,128)(2,1)S(1)}, u32[]{:S(2)}, u32[]{:S(2)}) collective-permute-start(bf16[640,256]{1,0:T(8,128)(2,1)S(1)} %collective-permute-done.4.p0), channel_id=1, source_target_pairs={{0,16},{16,0},{1,17},{17,1},{2,18},{18,2},{3,19},{19,3},{4,20},{20... | collective-permute-start | bytes 983048 | tf_op jit(solution)/shard_map/ppermute | solution.py:279
  47.9 13.5 %collective-permute-start.11 = (bf16[640,256]{1,0:T(8,128)(2,1)S(1)}, bf16[640,256]{1,0:T(8,128)(2,1)S(1)}, u32[]{:S(2)}, u32[]{:S(2)}) collective-permute-start(bf16[640,256]{1,0:T(8,128)(2,1)S(1)} %collective-permute-done.5.refs_1_), channel_id=1, source_target_pairs={{0,16},{16,0},{1,17},{17,1},{2,18},{18,2},{3,19},{19,3},{4,20},{20... | collective-permute-start | bytes 983048 | tf_op jit(solution)/shard_map/ppermute | solution.py:279
  48.5 15.6 %collective-permute-start.12 = (bf16[640,256]{1,0:T(8,128)(2,1)S(1)}, bf16[640,256]{1,0:T(8,128)(2,1)S(1)}, u32[]{:S(2)}, u32[]{:S(2)}) collective-permute-start(bf16[640,256]{1,0:T(8,128)(2,1)S(1)} %collective-permute-done.8.refs_6_), channel_id=1, source_target_pairs={{0,2},{2,0},{1,3},{3,1},{4,6},{6,4},{5,7},{7,5},{8,10},{10,8},{9,1... | collective-permute-start | bytes 983048 | tf_op jit(solution)/shard_map/ppermute | solution.py:279
  49.9 14.1 %collective-permute-start.13 = (bf16[640,256]{1,0:T(8,128)(2,1)}, bf16[640,256]{1,0:T(8,128)(2,1)S(1)}, u32[]{:S(2)}, u32[]{:S(2)}) collective-permute-start(bf16[640,256]{1,0:T(8,128)(2,1)} %copy-done.5), channel_id=1, source_target_pairs={{0,0},{1,8},{2,1},{3,9},{4,2},{5,10},{6,3},{7,11},{8,4},{9,12},{10... | collective-permute-start | bytes 983048 | tf_op jit(solution)/shard_map/ppermute | solution.py:303
  56.5 13.0 %collective-permute-start.15 = (bf16[640,256]{1,0:T(8,128)(2,1)}, bf16[640,256]{1,0:T(8,128)(2,1)S(1)}, u32[]{:S(2)}, u32[]{:S(2)}) collective-permute-start(bf16[640,256]{1,0:T(8,128)(2,1)} %copy-done.4), channel_id=1, source_target_pairs={{0,2},{1,10},{2,3},{3,11},{4,4},{5,12},{6,5},{7,13},{8,6},{9,14},{... | collective-permute-start | bytes 983048 | tf_op jit(solution)/shard_map/ppermute | solution.py:303
  59.0 24.2 %collective-permute-start.16 = (bf16[640,256]{1,0:T(8,128)(2,1)S(1)}, bf16[640,256]{1,0:T(8,128)(2,1)S(1)}, u32[]{:S(2)}, u32[]{:S(2)}) collective-permute-start(bf16[640,256]{1,0:T(8,128)(2,1)S(1)} %get-tuple-element.64), channel_id=1, source_target_pairs={{0,4},{1,12},{2,5},{3,13},{4,6},{5,14},{6,7},{7,15},{8,0},{9,8},{1... | collective-permute-start | bytes 983048 | tf_op jit(solution)/shard_map/ppermute | solution.py:303
  61.4 21.8 %collective-permute-start.17 = (bf16[640,256]{1,0:T(8,128)(2,1)S(1)}, bf16[640,256]{1,0:T(8,128)(2,1)S(1)}, u32[]{:S(2)}, u32[]{:S(2)}) collective-permute-start(bf16[640,256]{1,0:T(8,128)(2,1)S(1)} %get-tuple-element.66), channel_id=1, source_target_pairs={{0,6},{1,14},{2,7},{3,15},{4,0},{5,8},{6,1},{7,9},{8,2},{9,10},{10... | collective-permute-start | bytes 983048 | tf_op jit(solution)/shard_map/ppermute | solution.py:303
  64.1 19.1 %copy-start.11 = (bf16[640,256]{1,0:T(8,128)(2,1)}, bf16[640,256]{1,0:T(8,128)(2,1)S(1)}, u32[]{:S(2)}) copy-start(bf16[640,256]{1,0:T(8,128)(2,1)S(1)} %collective-permute-done.13) | copy-start | bytes 983044
  64.1 8.1 %collective-permute-start.14 = (bf16[640,256]{1,0:T(8,128)(2,1)S(1)}, bf16[640,256]{1,0:T(8,128)(2,1)S(1)}, u32[]{:S(2)}, u32[]{:S(2)}) collective-permute-start(bf16[640,256]{1,0:T(8,128)(2,1)S(1)} %collective-permute-done.9.p1), channel_id=1, source_target_pairs={{0,16},{16,0},{1,17},{17,1},{2,18},{18,2},{3,19},{19,3},{4,20},{20... | collective-permute-start | bytes 983048 | tf_op jit(solution)/shard_map/ppermute | solution.py:279
  69.5 13.8 %copy-start.8 = (bf16[640,256]{1,0:T(8,128)(2,1)}, bf16[640,256]{1,0:T(8,128)(2,1)S(1)}, u32[]{:S(2)}) copy-start(bf16[640,256]{1,0:T(8,128)(2,1)S(1)} %collective-permute-done.15) | copy-start | bytes 983044
  84.5 29.0 %collective-permute-start.18 = (bf16[4,640,256]{2,1,0:T(8,128)(2,1)}, bf16[4,640,256]{2,1,0:T(8,128)(2,1)S(1)}, u32[]{:S(2)}, u32[]{:S(2)}) collective-permute-start(bf16[4,640,256]{2,1,0:T(8,128)(2,1)} %pad_maximum_fusion), channel_id=1, source_target_pairs={{0,1},{1,0},{2,3},{3,2},{4,5},{5,4},{6,7},{7,6},{8,9},{9,8},{10,11... | collective-permute-start | bytes 3932168 | tf_op jit(solution)/shard_map/ppermute | solution.py:279
  84.6 20.3 %copy-start.10 = (bf16[640,256]{1,0:T(8,128)(2,1)S(1)}, bf16[640,256]{1,0:T(8,128)(2,1)}, u32[]{:S(2)}) copy-start(bf16[640,256]{1,0:T(8,128)(2,1)} %copy-done.9) | copy-start | bytes 983044
  84.6 28.8 %copy-start.7 = (bf16[640,256]{1,0:T(8,128)(2,1)S(1)}, bf16[640,256]{1,0:T(8,128)(2,1)}, u32[]{:S(2)}) copy-start(bf16[640,256]{1,0:T(8,128)(2,1)} %copy-done.6) | copy-start | bytes 983044
  84.6 11.0 %collective-permute-start.19 = (bf16[256,512]{1,0:T(8,128)(2,1)S(1)}, bf16[256,512]{1,0:T(8,128)(2,1)S(1)}, u32[]{:S(2)}, u32[]{:S(2)}) collective-permute-start(bf16[256,512]{1,0:T(8,128)(2,1)S(1)} %get-tuple-element.71.refs_7_), channel_id=1, source_target_pairs={{0,4},{4,8},{8,12},{12,0},{1,5},{5,9},{9,13},{13,1},{2,6},{6,10},{... | collective-permute-start | bytes 786440 | tf_op jit(solution)/shard_map/ppermute | solution.py:284
  87.8 12.8 %collective-permute-start.20 = (bf16[256,512]{1,0:T(8,128)(2,1)S(1)}, bf16[256,512]{1,0:T(8,128)(2,1)S(1)}, u32[]{:S(2)}, u32[]{:S(2)}) collective-permute-start(bf16[256,512]{1,0:T(8,128)(2,1)S(1)} %get-tuple-element.71.refs_7_), channel_id=1, source_target_pairs={{0,12},{4,0},{8,4},{12,8},{1,13},{5,1},{9,5},{13,9},{2,14},{6,2},{... | collective-permute-start | bytes 786440 | tf_op jit(solution)/shard_map/ppermute | solution.py:284
  88.5 12.2 %collective-permute-start.21 = (bf16[256,512]{1,0:T(8,128)(2,1)S(1)}, bf16[256,512]{1,0:T(8,128)(2,1)S(1)}, u32[]{:S(2)}, u32[]{:S(2)}) collective-permute-start(bf16[256,512]{1,0:T(8,128)(2,1)S(1)} %get-tuple-element.71.refs_7_), channel_id=1, source_target_pairs={{0,2},{2,0},{1,3},{3,1},{4,6},{6,4},{5,7},{7,5},{8,10},{10,8},{9,1... | collective-permute-start | bytes 786440 | tf_op jit(solution)/shard_map/ppermute | solution.py:279
  100.7 10.1 %collective-permute-start.22 = (bf16[256,512]{1,0:T(8,128)(2,1)S(1)}, bf16[256,512]{1,0:T(8,128)(2,1)S(1)}, u32[]{:S(2)}, u32[]{:S(2)}) collective-permute-start(bf16[256,512]{1,0:T(8,128)(2,1)S(1)} %collective-permute-done.19.refs_9_), channel_id=1, source_target_pairs={{0,4},{4,8},{8,12},{12,0},{1,5},{5,9},{9,13},{13,1},{2,6},{6,10},{... | collective-permute-start | bytes 786440 | tf_op jit(solution)/shard_map/ppermute | solution.py:284
  102.0 9.2 %collective-permute-start.23 = (bf16[256,512]{1,0:T(8,128)(2,1)S(1)}, bf16[256,512]{1,0:T(8,128)(2,1)S(1)}, u32[]{:S(2)}, u32[]{:S(2)}) collective-permute-start(bf16[256,512]{1,0:T(8,128)(2,1)S(1)} %collective-permute-done.19.refs_9_), channel_id=1, source_target_pairs={{0,2},{2,0},{1,3},{3,1},{4,6},{6,4},{5,7},{7,5},{8,10},{10,8},{9,1... | collective-permute-start | bytes 786440 | tf_op jit(solution)/shard_map/ppermute | solution.py:279
  105.0 11.9 %collective-permute-start.25 = (bf16[256,512]{1,0:T(8,128)(2,1)S(1)}, bf16[256,512]{1,0:T(8,128)(2,1)S(1)}, u32[]{:S(2)}, u32[]{:S(2)}) collective-permute-start(bf16[256,512]{1,0:T(8,128)(2,1)S(1)} %collective-permute-done.20.refs_10_), channel_id=1, source_target_pairs={{0,2},{2,0},{1,3},{3,1},{4,6},{6,4},{5,7},{7,5},{8,10},{10,8},{9,1... | collective-permute-start | bytes 786440 | tf_op jit(solution)/shard_map/ppermute | solution.py:279
  111.3 9.9 %collective-permute-start.24 = (bf16[256,512]{1,0:T(8,128)(2,1)S(1)}, bf16[256,512]{1,0:T(8,128)(2,1)S(1)}, u32[]{:S(2)}, u32[]{:S(2)}) collective-permute-start(bf16[256,512]{1,0:T(8,128)(2,1)S(1)} %collective-permute-done.22.refs_3_), channel_id=1, source_target_pairs={{0,2},{2,0},{1,3},{3,1},{4,6},{6,4},{5,7},{7,5},{8,10},{10,8},{9,1... | collective-permute-start | bytes 786440 | tf_op jit(solution)/shard_map/ppermute | solution.py:279
  (8 other events, 21.4 us)

commit v4 on v3

--- a/solution.py
+++ b/solution.py
@@ -53,18 +53,27 @@
     rows = pieces[0].shape[0]
     near = features_of(own_ref, other_ref, block, replica * rows, rows)
     far = features_of(own_ref, other_ref, block, (1 - replica) * rows, rows)
+    cut = pieces[3].shape[0]
     return (
         product(near, pieces[0][...]) + product(far, pieces[1][...]),
-        product(near, pieces[2][...]) + product(far, pieces[3][...]),
-    )
-
-
-def block_from(distance):
-    blocks = lax.axis_size("blk")
-    return lax.rem(lax.axis_index("blk") + (blocks - distance), blocks)
-
-
-def project_kernel(distances, own_ref, other_ref, weight_ref, *refs):
+        product(near, pieces[2][...])
+        + product(far[:, :cut], pieces[3][...])
+        + product(far[:, cut:], pieces[4][...]),
+    )
+
+
+def block_from(step):
+    here = lax.axis_index("blk")
+    swap = here + 1 - 2 * lax.rem(here, 2)
+    if step == 0:
+        return swap
+    inner = jnp.logical_or(here == 1, here == 2)
+    if step == 1:
+        return jnp.where(inner, 3 - here, jnp.where(here == 0, 2, 1))
+    return jnp.where(inner, 3 - swap, 3 - here)
+
+
+def project_kernel(steps, own_ref, other_ref, weight_ref, *refs):
     sums_ref = refs[-1]
     group, replica = lax.axis_index("groups"), lax.axis_index("dp")
     half_rows = weight_ref.shape[1] // 2
@@ -75,9 +84,9 @@
         product(first, weight_ref[j, :half_rows]) + product(second, weight_ref[j, half_rows:])
         for j in (group, 1 - group)
     ]
-    for at, distance in enumerate(distances):
-        pieces = refs[4 * at : 4 * at + 4]
-        terms = block_terms(own_ref, other_ref, block_from(distance), pieces)
+    for at, step in enumerate(steps):
+        pieces = refs[5 * at : 5 * at + 5]
+        terms = block_terms(own_ref, other_ref, block_from(step), pieces)
         totals = [total + term for total, term in zip(totals, terms)]
     sums_ref[group] = totals[0]
     sums_ref[1 - group] = totals[1]
@@ -86,16 +95,16 @@
 def project(normed, normed_other, kv_weight, gathered):
     length = normed.shape[0]
     _, rows, columns = kv_weight.shape
-    distances = tuple(distance for distance, _ in gathered)
-    pieces = [piece for _, four in gathered for piece in four]
+    steps = tuple(step for step, _ in gathered)
+    pieces = [piece for _, parts in gathered for piece in parts]
     return pl.pallas_call(
-        functools.partial(project_kernel, distances),
+        functools.partial(project_kernel, steps),
         in_specs=[IN_VMEM] * (3 + len(pieces)),
         out_specs=IN_VMEM,
         out_shape=jax.ShapeDtypeStruct((2, length, columns), jnp.float32),
         compiler_params=pltpu.CompilerParams(vmem_limit_bytes=VMEM_BYTES),
         cost_estimate=pl.CostEstimate(
-            flops=4 * length * rows * columns * (1 + len(distances)),
+            flops=4 * length * rows * columns * (1 + len(steps)),
             bytes_accessed=7000000,
             transcendentals=0,
         ),
@@ -142,11 +151,11 @@
 
 
 def attention_kernel(
-    distance, own_ref, other_ref, p0, p1, p2, p3, sums_ref, bias_ref, cosine_ref, sine_ref,
+    step, own_ref, other_ref, p0, p1, p2, p3, p4, sums_ref, bias_ref, cosine_ref, sine_ref,
     queries_ref, cotangent_ref, grad_query_ref, pair_ref, raw_ref,
 ):
     group = lax.axis_index("groups")
-    terms = block_terms(own_ref, other_ref, block_from(distance), (p0, p1, p2, p3))
+    terms = block_terms(own_ref, other_ref, block_from(step), (p0, p1, p2, p3, p4))
     raw_ref[group] = sums_ref[group] + terms[0]
     raw_ref[1 - group] = sums_ref[1 - group] + terms[1]
 
@@ -158,12 +167,12 @@
     )
 
 
-def attention(distance, normed, normed_other, pieces, sums, bias, cosine, sine, queries, cotangent):
+def attention(step, normed, normed_other, pieces, sums, bias, cosine, sine, queries, cotangent):
     length = normed.shape[0]
     columns = pieces[0].shape[1]
     operands = (normed, normed_other, *pieces, sums, bias, cosine, sine, queries, cotangent)
     return pl.pallas_call(
-        functools.partial(attention_kernel, distance),
+        functools.partial(attention_kernel, step),
         in_specs=[IN_VMEM] * len(operands),
         out_specs=[IN_VMEM] * 2,
         scratch_shapes=[pltpu.VMEM(sums.shape, jnp.float32)],
@@ -279,9 +288,21 @@
     return lax.ppermute(block, axis, [(0, 1), (1, 0)])
 
 
-def turned(block, axis, distance):
-    size = lax.axis_size(axis)
-    return lax.ppermute(block, axis, [(i, (i + distance) % size) for i in range(size)])
+def neighbours(block):
+    return lax.ppermute(block, "blk", [(0, 1), (1, 0), (2, 3), (3, 2)])
+
+
+def inner(block):
+    return lax.ppermute(block, "blk", [(1, 2), (2, 1)])
+
+
+def outward(block):
+    return lax.ppermute(block, "blk", [(1, 0), (2, 3)])
+
+
+def at_inner(held, arrived):
+    here = lax.axis_index("blk")
+    return jnp.where(jnp.logical_or(here == 1, here == 2), held, arrived)
 
 
 def after(block, *others):
@@ -334,62 +355,72 @@
             piece, activations, scale, gain, bias, cosine, sine, queries, cotangent
         )
 
+    cut = (share * 3 // 5) // 128 * 128
+    first, middle = neighbours(piece), inner(piece)
+    first, middle, scale = lax.optimization_barrier((first, middle, scale))
     normed, *slabs = norm(activations, scale, gain[None, :], half)
     normed_other = swapped(normed, "sub")
-
-    up, down = turned(piece, "blk", 1), turned(piece, "blk", -1)
-    up, down, normed_other = lax.optimization_barrier((up, down, normed_other))
-    twice = turned(up, "blk", 1)
-    up_x, up_y = swapped(up, "dp"), swapped(up, "groups")
-    down_x, down_y = swapped(down, "dp"), swapped(down, "groups")
-    twice, up_x, up_y, down_x, down_y = lax.optimization_barrier(
-        (twice, up_x, up_y, down_x, down_y)
-    )
-    twice_x, twice_y = swapped(twice, "dp"), swapped(twice, "groups")
-    up_both, down_both = swapped(up_x, "groups"), swapped(down_y, "dp")
-    slabs = [sent_slab(after(slab, twice), turn) for turn, slab in enumerate(slabs)]
-    twice_x, twice_y, up_both, down_both, slabs[0] = lax.optimization_barrier(
-        (twice_x, twice_y, up_both, down_both, slabs[0])
-    )
-    twice_both = swapped(twice_x, "groups")
-
-    gathered = [(1, (up, up_x, up_y, up_both)), (-1, (down, down_x, down_y, down_both))]
+    outer, far = outward(middle), inner(first)
+    first_x, first_y = swapped(first, "dp"), swapped(first, "groups")
+    outer, far, first_x, first_y, normed_other = lax.optimization_barrier(
+        (outer, far, first_x, first_y, normed_other)
+    )
+    second = at_inner(middle, outer)
+    end = outward(far)
+    second_x, second_y = swapped(second, "dp"), swapped(second, "groups")
+    first_both = (swapped(first_x[:cut], "groups"), swapped(first_y[cut:], "dp"))
+    end, second_x, second_y, first_both = lax.optimization_barrier(
+        (end, second_x, second_y, first_both)
+    )
+    third = at_inner(far, end)
+    third_x, third_y = swapped(third, "dp"), swapped(third, "groups")
+    second_both = (swapped(second_x[:cut], "groups"), swapped(second_y[cut:], "dp"))
+    slabs = [sent_slab(after(slab, end), turn) for turn, slab in enumerate(slabs)]
+    third_x, third_y, second_both, slabs[0] = lax.optimization_barrier(
+        (third_x, third_y, second_both, slabs[0])
+    )
+    third_both = (swapped(third_x[:cut], "groups"), swapped(third_y[cut:], "dp"))
+
+    gathered = [(0, (first, first_x, first_y, *first_both))]
+    gathered += [(1, (second, second_x, second_y, *second_both))]
     sums = project(normed, normed_other, kv_weight, gathered)
     sums = after(sums, slabs[1])
     grad_query, grad_pair = attention(
-        2, normed, normed_other, (twice, twice_x, twice_y, twice_both), sums, bias, cosine, sine,
+        2, normed, normed_other, (third, third_x, third_y, *third_both), sums, bias, cosine, sine,
         queries, cotangent,
     )
 
-    grad_pair, *slabs = lax.optimization_barrier((grad_pair, *slabs))
+    grad_pair, slabs[2] = lax.optimization_barrier((grad_pair, slabs[2]))
+
+    def slab_of(source, same):
+        from_replica = replica if same else 1 - replica
+        return (from_replica != core) * half + (slab_here - source) % half
+
+    pair = grad_pair
+    pair_first, pair_middle, pair_x = neighbours(pair), inner(pair), swapped(pair, "dp")
+    pair_first, pair_middle, pair_x, slabs[3] = lax.optimization_barrier(
+        (pair_first, pair_middle, pair_x, slabs[3])
+    )
     slabs_own = jnp.stack(slabs)
     slabs_held = jnp.concatenate([slabs_own, swapped(slabs_own, "sub")])
-
-    def slab_of(distance, same):
-        source = replica if same else 1 - replica
-        turn = (slab_here - (block - distance)) % half
-        return (source != core) * half + turn
-
-    pair_up, pair_down = turned(grad_pair, "blk", 1), turned(grad_pair, "blk", -1)
-    pair_x = swapped(grad_pair, "dp")
-    pair_up, pair_down, pair_x = lax.optimization_barrier((pair_up, pair_down, pair_x))
-    pair_twice = turned(pair_up, "blk", 1)
-    pair_up_x, pair_down_x = swapped(pair_up, "dp"), swapped(pair_down, "dp")
-    pair_twice, pair_up_x = lax.optimization_barrier((pair_twice, pair_up_x))
-    pair_twice_x = swapped(pair_twice, "dp")
-    first = {
-        (0, True): grad_pair,
-        (0, False): pair_x,
-        (1, True): pair_up,
-        (-1, True): pair_down,
-        (1, False): pair_up_x,
-        (-1, False): pair_down_x,
-    }
-    last = {(2, True): pair_twice, (2, False): pair_twice_x}
+    pair_outer, pair_far = outward(pair_middle), inner(pair_first)
+    pair_first_x = swapped(pair_first, "dp")
+    pair_outer, pair_far, pair_first_x = lax.optimization_barrier(
+        (pair_outer, pair_far, pair_first_x)
+    )
+    pair_second = at_inner(pair_middle, pair_outer)
+    pair_end = outward(pair_far)
+    pair_second_x = swapped(pair_second, "dp")
+    pair_third = at_inner(pair_far, pair_end)
+    pair_third_x = swapped(pair_third, "dp")
+    sources = [block] + [block_from(step) for step in range(3)]
+    held = [(pair, pair_x), (pair_first, pair_first_x)]
+    held += [(pair_second, pair_second_x), (pair_third, pair_third_x)]
     sums = None
-    for some in (first, last):
-        at = jnp.stack([slab_of(*which) for which in some]).astype(jnp.int32)
-        sums = gradient(at, slabs_held, list(some.values()), sums)
+    for some in (slice(0, 3), slice(3, 4)):
+        at = [slab_of(source, same) for source in sources[some] for same in (True, False)]
+        pairs = [one for both in held[some] for one in both]
+        sums = gradient(jnp.stack(at).astype(jnp.int32), slabs_held, pairs, sums)
     grad_weight, grad_bias = sums
     return (grad_query, grad_weight, grad_bias)
 

time: 124 us -> 134 us (1.081)
  starting transfers between devices: 38.7 us -> 49.9 us
  waiting for transfers between devices: 60.5 us -> 56.4 us
    ppermute x16 -> x19, waiting for transfers between devices: 23.9 us -> 17.3 us  [swapped(): return lax.ppermute(block, axis, [(0, 1), (1, 0)])]
    ppermute x4, starting transfers between devices: 7.38 us -> 13.4 us  [sent_slab(): return lax.ppermute(slab, ('blk', 'dp', 'sub'), slab_route(turn))]
    ppermute x6 -> x10, waiting for transfers between devices: 31.8 us -> 37.1 us  [the longest x4 26.5 us: outward(): return lax.ppermute(block, 'blk', [(1, 0), (2, 3)])]
    ppermute x16 -> x19, starting transfers between devices: 20 us -> 24.1 us  [swapped(): return lax.ppermute(block, axis, [(0, 1), (1, 0)])]
    ppermute x4, waiting for transfers between devices: 4.84 us -> 2.06 us  [sent_slab(): return lax.ppermute(slab, ('blk', 'dp', 'sub'), slab_route(turn))]
    ppermute x6 -> x10, starting transfers between devices: 11.3 us -> 12.3 us  [the longest x4 5.15 us: outward(): return lax.ppermute(block, 'blk', [(1, 0), (2, 3)])]
    unnamed x32 -> x40, local copies, waits for them, and re-layouts: 3.54 us -> 4.05 us
  transfers between devices with their start and end apart: 26 -> 33, of which waited for: 19 -> 11; matrix products, arithmetic and copies ran while one was open for 3% -> 5% of each run, Pallas kernels for 9% -> 9%
where the time goes in v4:
time: 134 us
  waiting for transfers between devices  56.4 us (42%)
  starting transfers between devices  49.9 us (37%)
  Pallas kernels  15.5 us (12%)
  local copies, waits for them, and re-layouts  5.54 us (4%)
  other arithmetic  5 us (4%)
    ppermute x4, waiting for transfers between devices, outward(): return lax.ppermute(block, 'blk', [(1, 0), (2, 3)])  26.5 us
    ppermute x19, starting transfers between devices, swapped(): return lax.ppermute(block, axis, [(0, 1), (1, 0)])  24.1 us
    ppermute x19, waiting for transfers between devices, swapped(): return lax.ppermute(block, axis, [(0, 1), (1, 0)])  17.3 us
    ppermute x4, starting transfers between devices, sent_slab(): return lax.ppermute(slab, ('blk', 'dp', 'sub'), slab_route(turn))  13.4 us
    ppermute x2, waiting for transfers between devices, neighbours(): return lax.ppermute(block, 'blk', [(0, 1), (1, 0), (2, 3), (3, 2)])  10.6 us
    pallas_call x1, Pallas kernels, attention(): pl.pallas_call(functools.partial(attention_kernel, step), in_specs=[IN_VM...  6.49 us
    ppermute x4, starting transfers between devices, outward(): return lax.ppermute(block, 'blk', [(1, 0), (2, 3)])  5.15 us
    pallas_call x2, Pallas kernels, gradient(): pl.pallas_call(functools.partial(gradient_kernel, count, sums is None), g...  4.5 us
  transfers between devices with their start and end apart: 33, of which 11 were waited for; matrix products, arithmetic and copies ran while one was open for 5% of the time, Pallas kernels for 9%

profile of v4, /device:TPU:0, one launch (start us, length us, event | category | flops | bytes accessed | tf_op | source)
XLA Modules:
  0.0 133.5 jit_solution(1934144043259749539)
XLA Ops:
  1.8 3.1 %collective-permute-start = (bf16[640,256]{1,0:T(8,128)(2,1)S(1)}, bf16[640,256]{1,0:T(8,128)(2,1)}, u32[]{:S(2)}, u32[]{:S(2)}) collective-permute-start(bf16[640,256]{1,0:T(8,128)(2,1)S(1)} %dynamic-slice_bitcast_fusion), channel_id=1, source_target_pairs={{0,4},{4,0},{8,12},{12,8},{1,5},{5,1},{9,13},{13,9},{2,6},{6,2},{1... | collective-permute-start | bytes 983048 | tf_op jit(solution)/shard_map/ppermute | solution.py:292
  6.2 1.7 %multiply_reduce_fusion = f32[256]{0:T(256)S(1)} fusion(bf16[256,2560]{1,0:T(8,128)(2,1)} %values_ref.1), kind=kLoop, calls=%fused_computation | loop fusion | flops 1965824 | bytes 1311744 | tf_op jit(solution)/shard_map/reduce_sum | solution.py:331
  9.5 3.2 %collective-permute-done.refs_0_ = bf16[640,256]{1,0:T(8,128)(2,1)} collective-permute-done((bf16[640,256]{1,0:T(8,128)(2,1)S(1)}, bf16[640,256]{1,0:T(8,128)(2,1)}, u32[]{:S(2)}, u32[]{:S(2)}) %collective-permute-start) | collective-permute-done | bytes 327712 | tf_op jit(solution)/shard_map/ppermute | solution.py:292
  12.7 1.6 %norm.1 = (bf16[256,2560]{1,0:T(8,128)(2,1)S(1)}, bf16[640,256]{1,0:T(8,128)(2,1)S(1)}, bf16[640,256]{1,0:T(8,128)(2,1)S(1)}, bf16[640,256]{1,0:T(8,128)(2,1)S(1)}, bf16[640,256]{1,0:T(8,128)(2,1)}) custom-call(bf16[256,2560]{1,0:T(8,128)(2,1)S(1)} %copy-done, f32[256,1]{1,0:T(8,128)S(1)} %add_rsqrt_fusion.scale_ref, f32[1,2560]{1,0:T(1,128)S(1)} %reshape.13.gain_ref), custom_call_target="tpu_custom_call" | custom-call | flops 2621440 | bytes 3932160 | tf_op jit(solution)/shard_map/norm/pallas_call | solution.py:273
  17.8 1.4 %collective-permute-start.4 = (bf16[640,256]{1,0:T(8,128)(2,1)}, bf16[640,256]{1,0:T(8,128)(2,1)}, u32[]{:S(2)}, u32[]{:S(2)}) collective-permute-start(bf16[640,256]{1,0:T(8,128)(2,1)} %collective-permute-done.refs_0_), channel_id=1, source_target_pairs={{4,8},{8,4},{5,9},{9,5},{6,10},{10,6},{7,11},{11,7},{20,24},{24,20... | collective-permute-start | bytes 983048 | tf_op jit(solution)/shard_map/ppermute | solution.py:296
  19.2 1.7 %collective-permute-start.5 = (bf16[640,256]{1,0:T(8,128)(2,1)}, bf16[640,256]{1,0:T(8,128)(2,1)S(1)}, u32[]{:S(2)}, u32[]{:S(2)}) collective-permute-start(bf16[640,256]{1,0:T(8,128)(2,1)} %collective-permute-done.refs_0_), channel_id=1, source_target_pairs={{0,2},{2,0},{1,3},{3,1},{4,6},{6,4},{5,7},{7,5},{8,10},{10,8},{9,1... | collective-permute-start | bytes 983048 | tf_op jit(solution)/shard_map/ppermute | solution.py:288
  20.9 1.5 %collective-permute-start.6 = (bf16[640,256]{1,0:T(8,128)(2,1)}, bf16[640,256]{1,0:T(8,128)(2,1)S(1)}, u32[]{:S(2)}, u32[]{:S(2)}) collective-permute-start(bf16[640,256]{1,0:T(8,128)(2,1)} %collective-permute-done.refs_0_), channel_id=1, source_target_pairs={{0,16},{16,0},{1,17},{17,1},{2,18},{18,2},{3,19},{19,3},{4,20},{20... | collective-permute-start | bytes 983048 | tf_op jit(solution)/shard_map/ppermute | solution.py:288
  22.4 8.9 %collective-permute-done.3 = bf16[640,256]{1,0:T(8,128)(2,1)} collective-permute-done((bf16[640,256]{1,0:T(8,128)(2,1)}, bf16[640,256]{1,0:T(8,128)(2,1)}, u32[]{:S(2)}, u32[]{:S(2)}) %collective-permute-start.3) | collective-permute-done | bytes 327712 | tf_op jit(solution)/shard_map/ppermute | solution.py:300
  33.6 1.6 %collective-permute-start.9 = (bf16[640,256]{1,0:T(8,128)(2,1)S(1)}, bf16[640,256]{1,0:T(8,128)(2,1)S(1)}, u32[]{:S(2)}, u32[]{:S(2)}) collective-permute-start(bf16[640,256]{1,0:T(8,128)(2,1)S(1)} %broadcast_select_fusion.1.refs_5_), channel_id=1, source_target_pairs={{0,2},{2,0},{1,3},{3,1},{4,6},{6,4},{5,7},{7,5},{8,10},{10,8},{9,1... | collective-permute-start | bytes 983048 | tf_op jit(solution)/shard_map/ppermute | solution.py:288
  35.2 1.5 %collective-permute-start.10 = (bf16[640,256]{1,0:T(8,128)(2,1)S(1)}, bf16[640,256]{1,0:T(8,128)(2,1)S(1)}, u32[]{:S(2)}, u32[]{:S(2)}) collective-permute-start(bf16[640,256]{1,0:T(8,128)(2,1)S(1)} %broadcast_select_fusion.1.refs_5_), channel_id=1, source_target_pairs={{0,16},{16,0},{1,17},{17,1},{2,18},{18,2},{3,19},{19,3},{4,20},{20... | collective-permute-start | bytes 983048 | tf_op jit(solution)/shard_map/ppermute | solution.py:288
  37.9 8.1 %collective-permute-done.12.refs_4_ = bf16[256,256]{1,0:T(8,128)(2,1)S(1)} collective-permute-done((bf16[256,256]{1,0:T(8,128)(2,1)S(1)}, bf16[256,256]{1,0:T(8,128)(2,1)S(1)}, u32[]{:S(2)}, u32[]{:S(2)}) %collective-permute-start.12) | collective-permute-done | bytes 131104 | tf_op jit(solution)/shard_map/ppermute | solution.py:288
  46.1 2.6 %collective-permute-done.11.refs_3_ = bf16[384,256]{1,0:T(8,128)(2,1)S(1)} collective-permute-done((bf16[384,256]{1,0:T(8,128)(2,1)S(1)}, bf16[384,256]{1,0:T(8,128)(2,1)S(1)}, u32[]{:S(2)}, u32[]{:S(2)}) %collective-permute-start.11) | collective-permute-done | bytes 196640 | tf_op jit(solution)/shard_map/ppermute | solution.py:288
  48.7 1.6 %collective-permute-start.15 = (bf16[384,256]{1,0:T(8,128)(2,1)S(1)}, bf16[384,256]{1,0:T(8,128)(2,1)S(1)}, u32[]{:S(2)}, u32[]{:S(2)}) collective-permute-start(bf16[384,256]{1,0:T(8,128)(2,1)S(1)} %slice.20), channel_id=1, source_target_pairs={{0,16},{16,0},{1,17},{17,1},{2,18},{18,2},{3,19},{19,3},{4,20},{20... | collective-permute-start | bytes 589832 | tf_op jit(solution)/shard_map/ppermute | solution.py:288
  51.0 1.6 %collective-permute-start.13 = (bf16[640,256]{1,0:T(8,128)(2,1)S(1)}, bf16[640,256]{1,0:T(8,128)(2,1)S(1)}, u32[]{:S(2)}, u32[]{:S(2)}) collective-permute-start(bf16[640,256]{1,0:T(8,128)(2,1)S(1)} %broadcast_select_fusion.p0), channel_id=1, source_target_pairs={{0,2},{2,0},{1,3},{3,1},{4,6},{6,4},{5,7},{7,5},{8,10},{10,8},{9,1... | collective-permute-start | bytes 983048 | tf_op jit(solution)/shard_map/ppermute | solution.py:288
  53.7 3.1 %collective-permute-done.16.refs_9_ = bf16[256,256]{1,0:T(8,128)(2,1)S(1)} collective-permute-done((bf16[256,256]{1,0:T(8,128)(2,1)S(1)}, bf16[256,256]{1,0:T(8,128)(2,1)S(1)}, u32[]{:S(2)}, u32[]{:S(2)}) %collective-permute-start.16) | collective-permute-done | bytes 131104 | tf_op jit(solution)/shard_map/ppermute | solution.py:288
  56.8 2.4 %collective-permute-start.20 = (bf16[640,256]{1,0:T(8,128)(2,1)S(1)}, bf16[640,256]{1,0:T(8,128)(2,1)S(1)}, u32[]{:S(2)}, u32[]{:S(2)}) collective-permute-start(bf16[640,256]{1,0:T(8,128)(2,1)S(1)} %copy-done.7), channel_id=1, source_target_pairs={{0,2},{1,10},{2,3},{3,11},{4,4},{5,12},{6,5},{7,13},{8,6},{9,14},{... | collective-permute-start | bytes 983048 | tf_op jit(solution)/shard_map/ppermute | solution.py:324
  59.3 3.5 %collective-permute-start.21 = (bf16[640,256]{1,0:T(8,128)(2,1)S(1)}, bf16[640,256]{1,0:T(8,128)(2,1)S(1)}, u32[]{:S(2)}, u32[]{:S(2)}) collective-permute-start(bf16[640,256]{1,0:T(8,128)(2,1)S(1)} %copy-done.5), channel_id=1, source_target_pairs={{0,4},{1,12},{2,5},{3,13},{4,6},{5,14},{6,7},{7,15},{8,0},{9,8},{1... | collective-permute-start | bytes 983048 | tf_op jit(solution)/shard_map/ppermute | solution.py:324
  64.2 6.2 %collective-permute-start.19 = (bf16[256,256]{1,0:T(8,128)(2,1)S(1)}, bf16[256,256]{1,0:T(8,128)(2,1)S(1)}, u32[]{:S(2)}, u32[]{:S(2)}) collective-permute-start(bf16[256,256]{1,0:T(8,128)(2,1)S(1)} %slice.23), channel_id=1, source_target_pairs={{0,2},{2,0},{1,3},{3,1},{4,6},{6,4},{5,7},{7,5},{8,10},{10,8},{9,1... | collective-permute-start | bytes 393224 | tf_op jit(solution)/shard_map/ppermute | solution.py:288
  70.6 6.8 %collective-permute-start.25 = (bf16[640,256]{1,0:T(8,128)(2,1)}, bf16[640,256]{1,0:T(8,128)(2,1)}, u32[]{:S(2)}, u32[]{:S(2)}) collective-permute-start(bf16[640,256]{1,0:T(8,128)(2,1)} %get-tuple-element.77), channel_id=1, source_target_pairs={{0,6},{1,14},{2,7},{3,15},{4,0},{5,8},{6,1},{7,9},{8,2},{9,10},{10... | collective-permute-start | bytes 983048 | tf_op jit(solution)/shard_map/ppermute | solution.py:324
  77.4 2.8 %project.1.sums_ref = f32[2,256,256]{2,1,0:T(8,128)S(1)} custom-call(bf16[256,2560]{1,0:T(8,128)(2,1)S(1)} %get-tuple-element.47.own_ref, bf16[256,2560]{1,0:T(8,128)(2,1)S(1)} %collective-permute-done.7.other_ref, bf16[2,1280,256]{2,1,0:T(8,128)(2,1)} %weight_ref.1, bf16[640,256]{1,0:T(8,128)(2,1)} %collective-permute-done.refs_0_, ...), custom_call_target="tpu_custom_call" | custom-call | flops 1006632960 | bytes 7000000 | tf_op jit(solution)/shard_map/project/pallas_call | solution.py:100
  80.3 6.5 %attention.1 = (bf16[256,1280]{1,0:T(8,128)(2,1)}, bf16[256,512]{1,0:T(8,128)(2,1)S(1)}) custom-call(bf16[256,2560]{1,0:T(8,128)(2,1)S(1)} %get-tuple-element.47.own_ref, bf16[256,2560]{1,0:T(8,128)(2,1)} %copy-done.1, bf16[640,256]{1,0:T(8,128)(2,1)S(1)} %broadcast_select_fusion.p0, bf16[640,256]{1,0:T(8,128)(2,1)S(1)} %collective-permute-done.13.p1, ...), custom_call_target="tpu_custom_call" | custom-call | flops 838860800 | bytes 5000000 | tf_op jit(solution)/shard_map/attention/pallas_call | solution.py:174
  86.8 2.1 %collective-permute-done.21 = bf16[640,256]{1,0:T(8,128)(2,1)S(1)} collective-permute-done((bf16[640,256]{1,0:T(8,128)(2,1)S(1)}, bf16[640,256]{1,0:T(8,128)(2,1)S(1)}, u32[]{:S(2)}, u32[]{:S(2)}) %collective-permute-start.21) | collective-permute-done | bytes 327712 | tf_op jit(solution)/shard_map/ppermute | solution.py:324
  90.6 7.4 %collective-permute-done.22.refs_9_ = bf16[256,512]{1,0:T(8,128)(2,1)S(1)} collective-permute-done((bf16[256,512]{1,0:T(8,128)(2,1)S(1)}, bf16[256,512]{1,0:T(8,128)(2,1)S(1)}, u32[]{:S(2)}, u32[]{:S(2)}) %collective-permute-start.22) | collective-permute-done | bytes 262176 | tf_op jit(solution)/shard_map/ppermute | solution.py:292
  98.7 1.6 %collective-permute-start.29 = (bf16[256,512]{1,0:T(8,128)(2,1)S(1)}, bf16[256,512]{1,0:T(8,128)(2,1)S(1)}, u32[]{:S(2)}, u32[]{:S(2)}) collective-permute-start(bf16[256,512]{1,0:T(8,128)(2,1)S(1)} %collective-permute-done.22.refs_9_), channel_id=1, source_target_pairs={{0,2},{2,0},{1,3},{3,1},{4,6},{6,4},{5,7},{7,5},{8,10},{10,8},{9,1... | collective-permute-start | bytes 786440 | tf_op jit(solution)/shard_map/ppermute | solution.py:288
  100.3 1.4 %pad_maximum_fusion = bf16[4,640,256]{2,1,0:T(8,128)(2,1)S(1)} fusion(bf16[1,640,256]{2,1,0:T(8,128)(2,1)} %bitcast.7, bf16[1,640,256]{2,1,0:T(8,128)(2,1)} %bitcast.19, bf16[1,640,256]{2,1,0:T(8,128)(2,1)} %bitcast.21, bf16[1,640,256]{2,1,0:T(8,128)(2,1)S(1)} %bitcast.20), kind=kLoop, calls=%fused_computation.1 | loop fusion | flops 1966080 | bytes 2621440 | tf_op jit(solution)/shard_map/stack | solution.py:404
  103.1 10.8 %collective-permute-done.27 = bf16[256,512]{1,0:T(8,128)(2,1)S(1)} collective-permute-done((bf16[256,512]{1,0:T(8,128)(2,1)S(1)}, bf16[256,512]{1,0:T(8,128)(2,1)S(1)}, u32[]{:S(2)}, u32[]{:S(2)}) %collective-permute-start.27) | collective-permute-done | bytes 262176 | tf_op jit(solution)/shard_map/ppermute | solution.py:300
  115.3 1.8 %collective-permute-start.32 = (bf16[256,512]{1,0:T(8,128)(2,1)S(1)}, bf16[256,512]{1,0:T(8,128)(2,1)S(1)}, u32[]{:S(2)}, u32[]{:S(2)}) collective-permute-start(bf16[256,512]{1,0:T(8,128)(2,1)S(1)} %broadcast_select_fusion.2.refs_11_), channel_id=1, source_target_pairs={{0,2},{2,0},{1,3},{3,1},{4,6},{6,4},{5,7},{7,5},{8,10},{10,8},{9,1... | collective-permute-start | bytes 786440 | tf_op jit(solution)/shard_map/ppermute | solution.py:288
  117.1 6.8 %collective-permute-done.30 = bf16[256,512]{1,0:T(8,128)(2,1)S(1)} collective-permute-done((bf16[256,512]{1,0:T(8,128)(2,1)S(1)}, bf16[256,512]{1,0:T(8,128)(2,1)S(1)}, u32[]{:S(2)}, u32[]{:S(2)}) %collective-permute-start.30) | collective-permute-done | bytes 262176 | tf_op jit(solution)/shard_map/ppermute | solution.py:300
  124.0 1.8 %collective-permute-start.31 = (bf16[256,512]{1,0:T(8,128)(2,1)S(1)}, bf16[256,512]{1,0:T(8,128)(2,1)S(1)}, u32[]{:S(2)}, u32[]{:S(2)}) collective-permute-start(bf16[256,512]{1,0:T(8,128)(2,1)S(1)} %broadcast_select_fusion.3.refs_3_), channel_id=1, source_target_pairs={{0,2},{2,0},{1,3},{3,1},{4,6},{6,4},{5,7},{7,5},{8,10},{10,8},{9,1... | collective-permute-start | bytes 786440 | tf_op jit(solution)/shard_map/ppermute | solution.py:288
  126.9 2.2 %gradient.2 = (f32[2,640,256]{2,1,0:T(8,128)S(1)}, f32[2,256]{1,0:T(2,128)S(1)}) custom-call(s32[6]{0:T(128)S(1)} %stack.59.refs_0_, bf16[8,640,256]{2,1,0:T(8,128)(2,1)S(1)} %constant_dynamic-update-slice_fusion.refs_1_.refs_2_.refs_3_.refs_4_.refs_5_.refs_6_, ...), custom_call_target="tpu_custom_call" | custom-call | flops 1006632960 | bytes 5000000 | tf_op jit(solution)/shard_map/gradient/pallas_call | solution.py:232
  129.1 2.2 %collective-permute-done.31.refs_4_ = bf16[256,512]{1,0:T(8,128)(2,1)S(1)} collective-permute-done((bf16[256,512]{1,0:T(8,128)(2,1)S(1)}, bf16[256,512]{1,0:T(8,128)(2,1)S(1)}, u32[]{:S(2)}, u32[]{:S(2)}) %collective-permute-start.31) | collective-permute-done | bytes 262176 | tf_op jit(solution)/shard_map/ppermute | solution.py:288
  131.3 2.3 %gradient.3 = (f32[2,640,256]{2,1,0:T(8,128)}, f32[2,256]{1,0:T(2,128)}) custom-call(s32[2]{0:T(128)S(1)} %pad_add_fusion.refs_0_, bf16[8,640,256]{2,1,0:T(8,128)(2,1)S(1)} %constant_dynamic-update-slice_fusion.refs_1_.refs_2_.refs_3_.refs_4_.refs_5_.refs_6_, ...), custom_call_target="tpu_custom_call" | custom-call | flops 335544320 | bytes 5000000 | tf_op jit(solution)/shard_map/gradient/pallas_call | solution.py:232
  (103 shorter events, 20.6 us)
Async XLA Ops:
  1.8 10.9 %collective-permute-start = (bf16[640,256]{1,0:T(8,128)(2,1)S(1)}, bf16[640,256]{1,0:T(8,128)(2,1)}, u32[]{:S(2)}, u32[]{:S(2)}) collective-permute-start(bf16[640,256]{1,0:T(8,128)(2,1)S(1)} %dynamic-slice_bitcast_fusion), channel_id=1, source_target_pairs={{0,4},{4,0},{8,12},{12,8},{1,5},{5,1},{9,13},{13,9},{2,6},{6,2},{1... | collective-permute-start | bytes 983048 | tf_op jit(solution)/shard_map/ppermute | solution.py:292
  4.9 7.8 %collective-permute-start.1 = (bf16[640,256]{1,0:T(8,128)(2,1)S(1)}, bf16[640,256]{1,0:T(8,128)(2,1)}, u32[]{:S(2)}, u32[]{:S(2)}) collective-permute-start(bf16[640,256]{1,0:T(8,128)(2,1)S(1)} %dynamic-slice_bitcast_fusion), channel_id=1, source_target_pairs={{4,8},{8,4},{5,9},{9,5},{6,10},{10,6},{7,11},{11,7},{20,24},{24,20... | collective-permute-start | bytes 983048 | tf_op jit(solution)/shard_map/ppermute | solution.py:296
  16.5 14.7 %collective-permute-start.7 = (bf16[256,2560]{1,0:T(8,128)(2,1)S(1)}, bf16[256,2560]{1,0:T(8,128)(2,1)S(1)}, u32[]{:S(2)}, u32[]{:S(2)}) collective-permute-start(bf16[256,2560]{1,0:T(8,128)(2,1)S(1)} %get-tuple-element.47.own_ref), channel_id=1, source_target_pairs={{0,1},{1,0},{2,3},{3,2},{4,5},{5,4},{6,7},{7,6},{8,9},{9,8},{10,11... | collective-permute-start | bytes 3932168 | tf_op jit(solution)/shard_map/ppermute | solution.py:288
  16.5 14.7 %collective-permute-start.3 = (bf16[640,256]{1,0:T(8,128)(2,1)}, bf16[640,256]{1,0:T(8,128)(2,1)}, u32[]{:S(2)}, u32[]{:S(2)}) collective-permute-start(bf16[640,256]{1,0:T(8,128)(2,1)} %collective-permute-done.1), channel_id=1, source_target_pairs={{4,0},{8,12},{5,1},{9,13},{6,2},{10,14},{7,3},{11,15},{20,16},{24,... | collective-permute-start | bytes 983048 | tf_op jit(solution)/shard_map/ppermute | solution.py:300
  17.8 13.4 %collective-permute-start.4 = (bf16[640,256]{1,0:T(8,128)(2,1)}, bf16[640,256]{1,0:T(8,128)(2,1)}, u32[]{:S(2)}, u32[]{:S(2)}) collective-permute-start(bf16[640,256]{1,0:T(8,128)(2,1)} %collective-permute-done.refs_0_), channel_id=1, source_target_pairs={{4,8},{8,4},{5,9},{9,5},{6,10},{10,6},{7,11},{11,7},{20,24},{24,20... | collective-permute-start | bytes 983048 | tf_op jit(solution)/shard_map/ppermute | solution.py:296
  19.2 12.0 %collective-permute-start.5 = (bf16[640,256]{1,0:T(8,128)(2,1)}, bf16[640,256]{1,0:T(8,128)(2,1)S(1)}, u32[]{:S(2)}, u32[]{:S(2)}) collective-permute-start(bf16[640,256]{1,0:T(8,128)(2,1)} %collective-permute-done.refs_0_), channel_id=1, source_target_pairs={{0,2},{2,0},{1,3},{3,1},{4,6},{6,4},{5,7},{7,5},{8,10},{10,8},{9,1... | collective-permute-start | bytes 983048 | tf_op jit(solution)/shard_map/ppermute | solution.py:288
  20.9 10.4 %collective-permute-start.6 = (bf16[640,256]{1,0:T(8,128)(2,1)}, bf16[640,256]{1,0:T(8,128)(2,1)S(1)}, u32[]{:S(2)}, u32[]{:S(2)}) collective-permute-start(bf16[640,256]{1,0:T(8,128)(2,1)} %collective-permute-done.refs_0_), channel_id=1, source_target_pairs={{0,16},{16,0},{1,17},{17,1},{2,18},{18,2},{3,19},{19,3},{4,20},{20... | collective-permute-start | bytes 983048 | tf_op jit(solution)/shard_map/ppermute | solution.py:288
  31.3 17.4 %collective-permute-start.8 = (bf16[640,256]{1,0:T(8,128)(2,1)}, bf16[640,256]{1,0:T(8,128)(2,1)S(1)}, u32[]{:S(2)}, u32[]{:S(2)}) collective-permute-start(bf16[640,256]{1,0:T(8,128)(2,1)} %collective-permute-done.4), channel_id=1, source_target_pairs={{4,0},{8,12},{5,1},{9,13},{6,2},{10,14},{7,3},{11,15},{20,16},{24,... | collective-permute-start | bytes 983048 | tf_op jit(solution)/shard_map/ppermute | solution.py:300
  33.6 15.0 %collective-permute-start.9 = (bf16[640,256]{1,0:T(8,128)(2,1)S(1)}, bf16[640,256]{1,0:T(8,128)(2,1)S(1)}, u32[]{:S(2)}, u32[]{:S(2)}) collective-permute-start(bf16[640,256]{1,0:T(8,128)(2,1)S(1)} %broadcast_select_fusion.1.refs_5_), channel_id=1, source_target_pairs={{0,2},{2,0},{1,3},{3,1},{4,6},{6,4},{5,7},{7,5},{8,10},{10,8},{9,1... | collective-permute-start | bytes 983048 | tf_op jit(solution)/shard_map/ppermute | solution.py:288
  35.2 13.5 %collective-permute-start.10 = (bf16[640,256]{1,0:T(8,128)(2,1)S(1)}, bf16[640,256]{1,0:T(8,128)(2,1)S(1)}, u32[]{:S(2)}, u32[]{:S(2)}) collective-permute-start(bf16[640,256]{1,0:T(8,128)(2,1)S(1)} %broadcast_select_fusion.1.refs_5_), channel_id=1, source_target_pairs={{0,16},{16,0},{1,17},{17,1},{2,18},{18,2},{3,19},{19,3},{4,20},{20... | collective-permute-start | bytes 983048 | tf_op jit(solution)/shard_map/ppermute | solution.py:288
  36.7 11.9 %collective-permute-start.11 = (bf16[384,256]{1,0:T(8,128)(2,1)S(1)}, bf16[384,256]{1,0:T(8,128)(2,1)S(1)}, u32[]{:S(2)}, u32[]{:S(2)}) collective-permute-start(bf16[384,256]{1,0:T(8,128)(2,1)S(1)} %slice.18), channel_id=1, source_target_pairs={{0,16},{16,0},{1,17},{17,1},{2,18},{18,2},{3,19},{19,3},{4,20},{20... | collective-permute-start | bytes 589832 | tf_op jit(solution)/shard_map/ppermute | solution.py:288
  37.3 8.7 %collective-permute-start.12 = (bf16[256,256]{1,0:T(8,128)(2,1)S(1)}, bf16[256,256]{1,0:T(8,128)(2,1)S(1)}, u32[]{:S(2)}, u32[]{:S(2)}) collective-permute-start(bf16[256,256]{1,0:T(8,128)(2,1)S(1)} %slice.19), channel_id=1, source_target_pairs={{0,2},{2,0},{1,3},{3,1},{4,6},{6,4},{5,7},{7,5},{8,10},{10,8},{9,1... | collective-permute-start | bytes 393224 | tf_op jit(solution)/shard_map/ppermute | solution.py:288
  48.7 10.6 %collective-permute-start.15 = (bf16[384,256]{1,0:T(8,128)(2,1)S(1)}, bf16[384,256]{1,0:T(8,128)(2,1)S(1)}, u32[]{:S(2)}, u32[]{:S(2)}) collective-permute-start(bf16[384,256]{1,0:T(8,128)(2,1)S(1)} %slice.20), channel_id=1, source_target_pairs={{0,16},{16,0},{1,17},{17,1},{2,18},{18,2},{3,19},{19,3},{4,20},{20... | collective-permute-start | bytes 589832 | tf_op jit(solution)/shard_map/ppermute | solution.py:288
  50.3 6.5 %collective-permute-start.16 = (bf16[256,256]{1,0:T(8,128)(2,1)S(1)}, bf16[256,256]{1,0:T(8,128)(2,1)S(1)}, u32[]{:S(2)}, u32[]{:S(2)}) collective-permute-start(bf16[256,256]{1,0:T(8,128)(2,1)S(1)} %slice.21), channel_id=1, source_target_pairs={{0,2},{2,0},{1,3},{3,1},{4,6},{6,4},{5,7},{7,5},{8,10},{10,8},{9,1... | collective-permute-start | bytes 393224 | tf_op jit(solution)/shard_map/ppermute | solution.py:288
  51.0 12.4 %collective-permute-start.13 = (bf16[640,256]{1,0:T(8,128)(2,1)S(1)}, bf16[640,256]{1,0:T(8,128)(2,1)S(1)}, u32[]{:S(2)}, u32[]{:S(2)}) collective-permute-start(bf16[640,256]{1,0:T(8,128)(2,1)S(1)} %broadcast_select_fusion.p0), channel_id=1, source_target_pairs={{0,2},{2,0},{1,3},{3,1},{4,6},{6,4},{5,7},{7,5},{8,10},{10,8},{9,1... | collective-permute-start | bytes 983048 | tf_op jit(solution)/shard_map/ppermute | solution.py:288
  52.5 10.8 %collective-permute-start.14 = (bf16[640,256]{1,0:T(8,128)(2,1)S(1)}, bf16[640,256]{1,0:T(8,128)(2,1)S(1)}, u32[]{:S(2)}, u32[]{:S(2)}) collective-permute-start(bf16[640,256]{1,0:T(8,128)(2,1)S(1)} %broadcast_select_fusion.p0), channel_id=1, source_target_pairs={{0,16},{16,0},{1,17},{17,1},{2,18},{18,2},{3,19},{19,3},{4,20},{20... | collective-permute-start | bytes 983048 | tf_op jit(solution)/shard_map/ppermute | solution.py:288
  53.0 10.3 %collective-permute-start.17 = (bf16[640,256]{1,0:T(8,128)(2,1)S(1)}, bf16[640,256]{1,0:T(8,128)(2,1)S(1)}, u32[]{:S(2)}, u32[]{:S(2)}) collective-permute-start(bf16[640,256]{1,0:T(8,128)(2,1)S(1)} %copy-done.9), channel_id=1, source_target_pairs={{0,0},{1,8},{2,1},{3,9},{4,2},{5,10},{6,3},{7,11},{8,4},{9,12},{10... | collective-permute-start | bytes 983048 | tf_op jit(solution)/shard_map/ppermute | solution.py:324
  56.8 23.4 %collective-permute-start.20 = (bf16[640,256]{1,0:T(8,128)(2,1)S(1)}, bf16[640,256]{1,0:T(8,128)(2,1)S(1)}, u32[]{:S(2)}, u32[]{:S(2)}) collective-permute-start(bf16[640,256]{1,0:T(8,128)(2,1)S(1)} %copy-done.7), channel_id=1, source_target_pairs={{0,2},{1,10},{2,3},{3,11},{4,4},{5,12},{6,5},{7,13},{8,6},{9,14},{... | collective-permute-start | bytes 983048 | tf_op jit(solution)/shard_map/ppermute | solution.py:324
  59.3 29.6 %collective-permute-start.21 = (bf16[640,256]{1,0:T(8,128)(2,1)S(1)}, bf16[640,256]{1,0:T(8,128)(2,1)S(1)}, u32[]{:S(2)}, u32[]{:S(2)}) collective-permute-start(bf16[640,256]{1,0:T(8,128)(2,1)S(1)} %copy-done.5), channel_id=1, source_target_pairs={{0,4},{1,12},{2,5},{3,13},{4,6},{5,14},{6,7},{7,15},{8,0},{9,8},{1... | collective-permute-start | bytes 983048 | tf_op jit(solution)/shard_map/ppermute | solution.py:324
  63.4 16.9 %collective-permute-start.18 = (bf16[384,256]{1,0:T(8,128)(2,1)S(1)}, bf16[384,256]{1,0:T(8,128)(2,1)S(1)}, u32[]{:S(2)}, u32[]{:S(2)}) collective-permute-start(bf16[384,256]{1,0:T(8,128)(2,1)S(1)} %slice.22), channel_id=1, source_target_pairs={{0,16},{16,0},{1,17},{17,1},{2,18},{18,2},{3,19},{19,3},{4,20},{20... | collective-permute-start | bytes 589832 | tf_op jit(solution)/shard_map/ppermute | solution.py:288
  64.2 16.1 %collective-permute-start.19 = (bf16[256,256]{1,0:T(8,128)(2,1)S(1)}, bf16[256,256]{1,0:T(8,128)(2,1)S(1)}, u32[]{:S(2)}, u32[]{:S(2)}) collective-permute-start(bf16[256,256]{1,0:T(8,128)(2,1)S(1)} %slice.23), channel_id=1, source_target_pairs={{0,2},{2,0},{1,3},{3,1},{4,6},{6,4},{5,7},{7,5},{8,10},{10,8},{9,1... | collective-permute-start | bytes 393224 | tf_op jit(solution)/shard_map/ppermute | solution.py:288
  70.6 20.0 %collective-permute-start.25 = (bf16[640,256]{1,0:T(8,128)(2,1)}, bf16[640,256]{1,0:T(8,128)(2,1)}, u32[]{:S(2)}, u32[]{:S(2)}) collective-permute-start(bf16[640,256]{1,0:T(8,128)(2,1)} %get-tuple-element.77), channel_id=1, source_target_pairs={{0,6},{1,14},{2,7},{3,15},{4,0},{5,8},{6,1},{7,9},{8,2},{9,10},{10... | collective-permute-start | bytes 983048 | tf_op jit(solution)/shard_map/ppermute | solution.py:324
  88.8 9.1 %collective-permute-start.22 = (bf16[256,512]{1,0:T(8,128)(2,1)S(1)}, bf16[256,512]{1,0:T(8,128)(2,1)S(1)}, u32[]{:S(2)}, u32[]{:S(2)}) collective-permute-start(bf16[256,512]{1,0:T(8,128)(2,1)S(1)} %get-tuple-element.75.refs_7_), channel_id=1, source_target_pairs={{0,4},{4,0},{8,12},{12,8},{1,5},{5,1},{9,13},{13,9},{2,6},{6,2},{1... | collective-permute-start | bytes 786440 | tf_op jit(solution)/shard_map/ppermute | solution.py:292
  89.6 8.4 %collective-permute-start.23 = (bf16[256,512]{1,0:T(8,128)(2,1)S(1)}, bf16[256,512]{1,0:T(8,128)(2,1)S(1)}, u32[]{:S(2)}, u32[]{:S(2)}) collective-permute-start(bf16[256,512]{1,0:T(8,128)(2,1)S(1)} %get-tuple-element.75.refs_7_), channel_id=1, source_target_pairs={{4,8},{8,4},{5,9},{9,5},{6,10},{10,6},{7,11},{11,7},{20,24},{24,20... | collective-permute-start | bytes 786440 | tf_op jit(solution)/shard_map/ppermute | solution.py:296
  90.2 7.7 %collective-permute-start.24 = (bf16[256,512]{1,0:T(8,128)(2,1)S(1)}, bf16[256,512]{1,0:T(8,128)(2,1)S(1)}, u32[]{:S(2)}, u32[]{:S(2)}) collective-permute-start(bf16[256,512]{1,0:T(8,128)(2,1)S(1)} %get-tuple-element.75.refs_7_), channel_id=1, source_target_pairs={{0,2},{2,0},{1,3},{3,1},{4,6},{6,4},{5,7},{7,5},{8,10},{10,8},{9,1... | collective-permute-start | bytes 786440 | tf_op jit(solution)/shard_map/ppermute | solution.py:288
  98.0 15.9 %collective-permute-start.28 = (bf16[256,512]{1,0:T(8,128)(2,1)S(1)}, bf16[256,512]{1,0:T(8,128)(2,1)S(1)}, u32[]{:S(2)}, u32[]{:S(2)}) collective-permute-start(bf16[256,512]{1,0:T(8,128)(2,1)S(1)} %collective-permute-done.22.refs_9_), channel_id=1, source_target_pairs={{4,8},{8,4},{5,9},{9,5},{6,10},{10,6},{7,11},{11,7},{20,24},{24,20... | collective-permute-start | bytes 786440 | tf_op jit(solution)/shard_map/ppermute | solution.py:296
  98.7 15.3 %collective-permute-start.29 = (bf16[256,512]{1,0:T(8,128)(2,1)S(1)}, bf16[256,512]{1,0:T(8,128)(2,1)S(1)}, u32[]{:S(2)}, u32[]{:S(2)}) collective-permute-start(bf16[256,512]{1,0:T(8,128)(2,1)S(1)} %collective-permute-done.22.refs_9_), channel_id=1, source_target_pairs={{0,2},{2,0},{1,3},{3,1},{4,6},{6,4},{5,7},{7,5},{8,10},{10,8},{9,1... | collective-permute-start | bytes 786440 | tf_op jit(solution)/shard_map/ppermute | solution.py:288
  101.7 25.1 %collective-permute-start.26 = (bf16[4,640,256]{2,1,0:T(8,128)(2,1)S(1)}, bf16[4,640,256]{2,1,0:T(8,128)(2,1)S(1)}, u32[]{:S(2)}, u32[]{:S(2)}) collective-permute-start(bf16[4,640,256]{2,1,0:T(8,128)(2,1)S(1)} %pad_maximum_fusion), channel_id=1, source_target_pairs={{0,1},{1,0},{2,3},{3,2},{4,5},{5,4},{6,7},{7,6},{8,9},{9,8},{10,11... | collective-permute-start | bytes 3932168 | tf_op jit(solution)/shard_map/ppermute | solution.py:288
  101.7 12.2 %collective-permute-start.27 = (bf16[256,512]{1,0:T(8,128)(2,1)S(1)}, bf16[256,512]{1,0:T(8,128)(2,1)S(1)}, u32[]{:S(2)}, u32[]{:S(2)}) collective-permute-start(bf16[256,512]{1,0:T(8,128)(2,1)S(1)} %collective-permute-done.23), channel_id=1, source_target_pairs={{4,0},{8,12},{5,1},{9,13},{6,2},{10,14},{7,3},{11,15},{20,16},{24,... | collective-permute-start | bytes 786440 | tf_op jit(solution)/shard_map/ppermute | solution.py:300
  113.9 10.0 %collective-permute-start.30 = (bf16[256,512]{1,0:T(8,128)(2,1)S(1)}, bf16[256,512]{1,0:T(8,128)(2,1)S(1)}, u32[]{:S(2)}, u32[]{:S(2)}) collective-permute-start(bf16[256,512]{1,0:T(8,128)(2,1)S(1)} %collective-permute-done.28), channel_id=1, source_target_pairs={{4,0},{8,12},{5,1},{9,13},{6,2},{10,14},{7,3},{11,15},{20,16},{24,... | collective-permute-start | bytes 786440 | tf_op jit(solution)/shard_map/ppermute | solution.py:300
  115.3 11.6 %collective-permute-start.32 = (bf16[256,512]{1,0:T(8,128)(2,1)S(1)}, bf16[256,512]{1,0:T(8,128)(2,1)S(1)}, u32[]{:S(2)}, u32[]{:S(2)}) collective-permute-start(bf16[256,512]{1,0:T(8,128)(2,1)S(1)} %broadcast_select_fusion.2.refs_11_), channel_id=1, source_target_pairs={{0,2},{2,0},{1,3},{3,1},{4,6},{6,4},{5,7},{7,5},{8,10},{10,8},{9,1... | collective-permute-start | bytes 786440 | tf_op jit(solution)/shard_map/ppermute | solution.py:288
  124.0 7.3 %collective-permute-start.31 = (bf16[256,512]{1,0:T(8,128)(2,1)S(1)}, bf16[256,512]{1,0:T(8,128)(2,1)S(1)}, u32[]{:S(2)}, u32[]{:S(2)}) collective-permute-start(bf16[256,512]{1,0:T(8,128)(2,1)S(1)} %broadcast_select_fusion.3.refs_3_), channel_id=1, source_target_pairs={{0,2},{2,0},{1,3},{3,1},{4,6},{6,4},{5,7},{7,5},{8,10},{10,8},{9,1... | collective-permute-start | bytes 786440 | tf_op jit(solution)/shard_map/ppermute | solution.py:288
  (19 other events, 231.3 us)

commit v5 on v3

--- a/solution.py
+++ b/solution.py
@@ -13,7 +13,7 @@
 EPSILON = 1e-06
 ROPE_BASE = 1000000.0
 SCALE = HEAD ** (-0.5)
-VMEM_BYTES = 48 * 1024 * 1024
+VMEM_BYTES = 24 * 1024 * 1024
 IN_VMEM = pl.BlockSpec(memory_space=pltpu.VMEM)
 
 
@@ -334,20 +334,21 @@
             piece, activations, scale, gain, bias, cosine, sine, queries, cotangent
         )
 
+    up = turned(piece, "blk", 1)
     normed, *slabs = norm(activations, scale, gain[None, :], half)
+    up, piece, normed, slabs = lax.optimization_barrier((up, piece, normed, slabs))
+    up_x, up_y, down = swapped(up, "dp"), swapped(up, "groups"), turned(piece, "blk", -1)
     normed_other = swapped(normed, "sub")
-
-    up, down = turned(piece, "blk", 1), turned(piece, "blk", -1)
-    up, down, normed_other = lax.optimization_barrier((up, down, normed_other))
+    up, up_x, up_y, down = lax.optimization_barrier((up, up_x, up_y, down))
+    down_x, down_y = swapped(down, "dp"), swapped(down, "groups")
     twice = turned(up, "blk", 1)
-    up_x, up_y = swapped(up, "dp"), swapped(up, "groups")
-    down_x, down_y = swapped(down, "dp"), swapped(down, "groups")
-    twice, up_x, up_y, down_x, down_y = lax.optimization_barrier(
-        (twice, up_x, up_y, down_x, down_y)
+    up_both = swapped(up_x, "groups")
+    twice, down_x, down_y, normed_other = lax.optimization_barrier(
+        (twice, down_x, down_y, normed_other)
     )
     twice_x, twice_y = swapped(twice, "dp"), swapped(twice, "groups")
-    up_both, down_both = swapped(up_x, "groups"), swapped(down_y, "dp")
-    slabs = [sent_slab(after(slab, twice), turn) for turn, slab in enumerate(slabs)]
+    down_both = swapped(down_y, "dp")
+    slabs[:2] = [sent_slab(after(slabs[turn], twice), turn) for turn in (0, 1)]
     twice_x, twice_y, up_both, down_both, slabs[0] = lax.optimization_barrier(
         (twice_x, twice_y, up_both, down_both, slabs[0])
     )
@@ -355,27 +356,28 @@
 
     gathered = [(1, (up, up_x, up_y, up_both)), (-1, (down, down_x, down_y, down_both))]
     sums = project(normed, normed_other, kv_weight, gathered)
-    sums = after(sums, slabs[1])
+    sums, *slabs = lax.optimization_barrier((sums, *slabs))
+    slabs[2:] = [sent_slab(slabs[turn], turn) for turn in (2, 3)]
     grad_query, grad_pair = attention(
         2, normed, normed_other, (twice, twice_x, twice_y, twice_both), sums, bias, cosine, sine,
         queries, cotangent,
     )
-
-    grad_pair, *slabs = lax.optimization_barrier((grad_pair, *slabs))
-    slabs_own = jnp.stack(slabs)
-    slabs_held = jnp.concatenate([slabs_own, swapped(slabs_own, "sub")])
 
     def slab_of(distance, same):
         source = replica if same else 1 - replica
         turn = (slab_here - (block - distance)) % half
         return (source != core) * half + turn
 
-    pair_up, pair_down = turned(grad_pair, "blk", 1), turned(grad_pair, "blk", -1)
-    pair_x = swapped(grad_pair, "dp")
-    pair_up, pair_down, pair_x = lax.optimization_barrier((pair_up, pair_down, pair_x))
-    pair_twice = turned(pair_up, "blk", 1)
-    pair_up_x, pair_down_x = swapped(pair_up, "dp"), swapped(pair_down, "dp")
-    pair_twice, pair_up_x = lax.optimization_barrier((pair_twice, pair_up_x))
+    pair_up, pair_x = turned(grad_pair, "blk", 1), swapped(grad_pair, "dp")
+    pair_up, pair_x, grad_pair = lax.optimization_barrier((pair_up, pair_x, grad_pair))
+    pair_down, pair_up_x = turned(grad_pair, "blk", -1), swapped(pair_up, "dp")
+    pair_down, pair_up_x, pair_up, *slabs = lax.optimization_barrier(
+        (pair_down, pair_up_x, pair_up, *slabs)
+    )
+    slabs_own = jnp.stack(slabs)
+    slabs_held = jnp.concatenate([slabs_own, swapped(slabs_own, "sub")])
+    pair_twice, pair_down_x = turned(pair_up, "blk", 1), swapped(pair_down, "dp")
+    pair_twice, pair_down_x = lax.optimization_barrier((pair_twice, pair_down_x))
     pair_twice_x = swapped(pair_twice, "dp")
     first = {
         (0, True): grad_pair,

time: 124 us -> 122 us (0.984)
  waiting for transfers between devices: 60.5 us -> 64.5 us
  Pallas kernels: 14.7 us -> 12 us
  local copies, waits for them, and re-layouts: 4.87 us -> 2.88 us
    ppermute x16, starting transfers between devices: 20 us -> 15.3 us  [swapped(): return lax.ppermute(block, axis, [(0, 1), (1, 0)])]
    ppermute x16, waiting for transfers between devices: 23.9 us -> 27.6 us  [swapped(): return lax.ppermute(block, axis, [(0, 1), (1, 0)])]
    ppermute x6, starting transfers between devices: 11.3 us -> 14.9 us  [turned(): lax.ppermute(block, axis, [(i, (i + distance) % size) for i in range(size)])]
    unnamed x32 -> x16, local copies, waits for them, and re-layouts: 3.54 us -> 0.12 us
    pallas_call x1, Pallas kernels: 2.85 us -> 1.46 us  [project(): pl.pallas_call(functools.partial(project_kernel, distances), in_specs=[IN...]
    concatenate x1, local copies, waits for them, and re-layouts: 0.09 us -> 1.4 us  [local(): slabs_held = jnp.concatenate([slabs_own, swapped(slabs_own, 'sub')])]
    pallas_call x1, Pallas kernels: 6.39 us -> 5.08 us  [attention(): pl.pallas_call(functools.partial(attention_kernel, distance), in_specs=[I...]
  transfers between devices with their start and end apart: 26 -> 26, of which waited for: 19 -> 18; matrix products, arithmetic and copies ran while one was open for 3% -> 3% of each run, Pallas kernels for 9% -> 4%
where the time goes in v5:
time: 122 us
  waiting for transfers between devices  64.5 us (53%)
  starting transfers between devices  37.7 us (31%)
  Pallas kernels  12 us (10%)
  other arithmetic  3.69 us (3%)
  local copies, waits for them, and re-layouts  2.88 us (2%)
    ppermute x6, waiting for transfers between devices, turned(): lax.ppermute(block, axis, [(i, (i + distance) % size) for i in range(size)])  32 us
    ppermute x16, waiting for transfers between devices, swapped(): return lax.ppermute(block, axis, [(0, 1), (1, 0)])  27.6 us
    ppermute x16, starting transfers between devices, swapped(): return lax.ppermute(block, axis, [(0, 1), (1, 0)])  15.3 us
    ppermute x6, starting transfers between devices, turned(): lax.ppermute(block, axis, [(i, (i + distance) % size) for i in range(size)])  14.9 us
    ppermute x4, starting transfers between devices, sent_slab(): return lax.ppermute(slab, ('blk', 'dp', 'sub'), slab_route(turn))  7.42 us
    pallas_call x1, Pallas kernels, attention(): pl.pallas_call(functools.partial(attention_kernel, distance), in_specs=[I...  5.08 us
    ppermute x4, waiting for transfers between devices, sent_slab(): return lax.ppermute(slab, ('blk', 'dp', 'sub'), slab_route(turn))  4.87 us
    pallas_call x2, Pallas kernels, gradient(): pl.pallas_call(functools.partial(gradient_kernel, count, sums is None), g...  4.5 us
  transfers between devices with their start and end apart: 26, of which 18 were waited for; matrix products, arithmetic and copies ran while one was open for 3% of the time, Pallas kernels for 4%

profile of v5, /device:TPU:0, one launch (start us, length us, event | category | flops | bytes accessed | tf_op | source)
XLA Modules:
  0.0 121.6 jit_solution(7447075143668274111)
XLA Ops:
  1.8 3.1 %collective-permute-start = (bf16[640,256]{1,0:T(8,128)(2,1)S(1)}, bf16[640,256]{1,0:T(8,128)(2,1)S(1)}, u32[]{:S(2)}, u32[]{:S(2)}) collective-permute-start(bf16[640,256]{1,0:T(8,128)(2,1)S(1)} %dynamic-slice_bitcast_fusion), channel_id=1, source_target_pairs={{0,4},{4,8},{8,12},{12,0},{1,5},{5,9},{9,13},{13,1},{2,6},{6,10},{... | collective-permute-start | bytes 983048 | tf_op jit(solution)/shard_map/ppermute | solution.py:284
  4.8 1.7 %multiply_reduce_fusion = f32[256]{0:T(256)S(1)} fusion(bf16[256,2560]{1,0:T(8,128)(2,1)} %values_ref.1), kind=kLoop, calls=%fused_computation | loop fusion | flops 1965824 | bytes 1311744 | tf_op jit(solution)/shard_map/reduce_sum | solution.py:310
  8.8 5.7 %collective-permute-done.refs_0_ = bf16[640,256]{1,0:T(8,128)(2,1)S(1)} collective-permute-done((bf16[640,256]{1,0:T(8,128)(2,1)S(1)}, bf16[640,256]{1,0:T(8,128)(2,1)S(1)}, u32[]{:S(2)}, u32[]{:S(2)}) %collective-permute-start) | collective-permute-done | bytes 327712 | tf_op jit(solution)/shard_map/ppermute | solution.py:284
  14.6 1.5 %collective-permute-start.2 = (bf16[640,256]{1,0:T(8,128)(2,1)S(1)}, bf16[640,256]{1,0:T(8,128)(2,1)S(1)}, u32[]{:S(2)}, u32[]{:S(2)}) collective-permute-start(bf16[640,256]{1,0:T(8,128)(2,1)S(1)} %collective-permute-done.refs_0_), channel_id=1, source_target_pairs={{0,2},{2,0},{1,3},{3,1},{4,6},{6,4},{5,7},{7,5},{8,10},{10,8},{9,1... | collective-permute-start | bytes 983048 | tf_op jit(solution)/shard_map/ppermute | solution.py:279
  16.1 1.5 %collective-permute-start.3 = (bf16[640,256]{1,0:T(8,128)(2,1)S(1)}, bf16[640,256]{1,0:T(8,128)(2,1)S(1)}, u32[]{:S(2)}, u32[]{:S(2)}) collective-permute-start(bf16[640,256]{1,0:T(8,128)(2,1)S(1)} %collective-permute-done.refs_0_), channel_id=1, source_target_pairs={{0,16},{16,0},{1,17},{17,1},{2,18},{18,2},{3,19},{19,3},{4,20},{20... | collective-permute-start | bytes 983048 | tf_op jit(solution)/shard_map/ppermute | solution.py:279
  17.6 1.7 %collective-permute-start.4 = (bf16[640,256]{1,0:T(8,128)(2,1)S(1)}, bf16[640,256]{1,0:T(8,128)(2,1)S(1)}, u32[]{:S(2)}, u32[]{:S(2)}) collective-permute-start(bf16[640,256]{1,0:T(8,128)(2,1)S(1)} %dynamic-slice_bitcast_fusion), channel_id=1, source_target_pairs={{0,12},{4,0},{8,4},{12,8},{1,13},{5,1},{9,5},{13,9},{2,14},{6,2},{... | collective-permute-start | bytes 983048 | tf_op jit(solution)/shard_map/ppermute | solution.py:284
  19.3 5.4 %collective-permute-done.2.refs_1_ = bf16[640,256]{1,0:T(8,128)(2,1)S(1)} collective-permute-done((bf16[640,256]{1,0:T(8,128)(2,1)S(1)}, bf16[640,256]{1,0:T(8,128)(2,1)S(1)}, u32[]{:S(2)}, u32[]{:S(2)}) %collective-permute-start.2) | collective-permute-done | bytes 327712 | tf_op jit(solution)/shard_map/ppermute | solution.py:279
  28.2 1.5 %collective-permute-start.11 = (bf16[640,256]{1,0:T(8,128)(2,1)S(1)}, bf16[640,256]{1,0:T(8,128)(2,1)S(1)}, u32[]{:S(2)}, u32[]{:S(2)}) collective-permute-start(bf16[640,256]{1,0:T(8,128)(2,1)S(1)} %collective-permute-done.2.refs_1_), channel_id=1, source_target_pairs={{0,16},{16,0},{1,17},{17,1},{2,18},{18,2},{3,19},{19,3},{4,20},{20... | collective-permute-start | bytes 983048 | tf_op jit(solution)/shard_map/ppermute | solution.py:279
  29.7 7.9 %collective-permute-done.5.p0 = bf16[640,256]{1,0:T(8,128)(2,1)S(1)} collective-permute-done((bf16[640,256]{1,0:T(8,128)(2,1)S(1)}, bf16[640,256]{1,0:T(8,128)(2,1)S(1)}, u32[]{:S(2)}, u32[]{:S(2)}) %collective-permute-start.5) | collective-permute-done | bytes 327712 | tf_op jit(solution)/shard_map/ppermute | solution.py:284
  38.3 1.5 %collective-permute-start.9 = (bf16[640,256]{1,0:T(8,128)(2,1)S(1)}, bf16[640,256]{1,0:T(8,128)(2,1)S(1)}, u32[]{:S(2)}, u32[]{:S(2)}) collective-permute-start(bf16[640,256]{1,0:T(8,128)(2,1)S(1)} %collective-permute-done.5.p0), channel_id=1, source_target_pairs={{0,2},{2,0},{1,3},{3,1},{4,6},{6,4},{5,7},{7,5},{8,10},{10,8},{9,1... | collective-permute-start | bytes 983048 | tf_op jit(solution)/shard_map/ppermute | solution.py:279
  41.6 3.8 %collective-permute-done.11.refs_3_ = bf16[640,256]{1,0:T(8,128)(2,1)S(1)} collective-permute-done((bf16[640,256]{1,0:T(8,128)(2,1)S(1)}, bf16[640,256]{1,0:T(8,128)(2,1)S(1)}, u32[]{:S(2)}, u32[]{:S(2)}) %collective-permute-start.11) | collective-permute-done | bytes 327712 | tf_op jit(solution)/shard_map/ppermute | solution.py:279
  45.4 3.4 %collective-permute-start.15 = (bf16[640,256]{1,0:T(8,128)(2,1)S(1)}, bf16[640,256]{1,0:T(8,128)(2,1)S(1)}, u32[]{:S(2)}, u32[]{:S(2)}) collective-permute-start(bf16[640,256]{1,0:T(8,128)(2,1)S(1)} %get-tuple-element.77), channel_id=1, source_target_pairs={{0,2},{1,10},{2,3},{3,11},{4,4},{5,12},{6,5},{7,13},{8,6},{9,14},{... | collective-permute-start | bytes 983048 | tf_op jit(solution)/shard_map/ppermute | solution.py:303
  48.8 1.8 %collective-permute-done.9.p1 = bf16[640,256]{1,0:T(8,128)(2,1)S(1)} collective-permute-done((bf16[640,256]{1,0:T(8,128)(2,1)S(1)}, bf16[640,256]{1,0:T(8,128)(2,1)S(1)}, u32[]{:S(2)}, u32[]{:S(2)}) %collective-permute-start.9) | collective-permute-done | bytes 327712 | tf_op jit(solution)/shard_map/ppermute | solution.py:279
  50.6 3.5 %collective-permute-done.12.refs_7_ = bf16[640,256]{1,0:T(8,128)(2,1)S(1)} collective-permute-done((bf16[640,256]{1,0:T(8,128)(2,1)S(1)}, bf16[640,256]{1,0:T(8,128)(2,1)S(1)}, u32[]{:S(2)}, u32[]{:S(2)}) %collective-permute-start.12) | collective-permute-done | bytes 327712 | tf_op jit(solution)/shard_map/ppermute | solution.py:279
  55.6 1.5 %project.1.sums_ref = f32[2,256,256]{2,1,0:T(8,128)S(1)} custom-call(bf16[256,2560]{1,0:T(8,128)(2,1)S(1)} %get-tuple-element.58.own_ref, bf16[256,2560]{1,0:T(8,128)(2,1)S(1)} %collective-permute-done.8.other_ref, bf16[2,1280,256]{2,1,0:T(8,128)(2,1)S(1)} %copy-done.1, bf16[640,256]{1,0:T(8,128)(2,1)S(1)} %collective-permute-done.refs_0_, ...), custom_call_target="tpu_custom_call" | custom-call | flops 1006632960 | bytes 7000000 | tf_op jit(solution)/shard_map/project/pallas_call | solution.py:91
  57.1 1.3 %collective-permute-done.15 = bf16[640,256]{1,0:T(8,128)(2,1)S(1)} collective-permute-done((bf16[640,256]{1,0:T(8,128)(2,1)S(1)}, bf16[640,256]{1,0:T(8,128)(2,1)S(1)}, u32[]{:S(2)}, u32[]{:S(2)}) %collective-permute-start.15) | collective-permute-done | bytes 327712 | tf_op jit(solution)/shard_map/ppermute | solution.py:303
  58.4 3.9 %collective-permute-done.14.p3 = bf16[640,256]{1,0:T(8,128)(2,1)S(1)} collective-permute-done((bf16[640,256]{1,0:T(8,128)(2,1)S(1)}, bf16[640,256]{1,0:T(8,128)(2,1)S(1)}, u32[]{:S(2)}, u32[]{:S(2)}) %collective-permute-start.14) | collective-permute-done | bytes 327712 | tf_op jit(solution)/shard_map/ppermute | solution.py:279
  62.4 5.1 %attention.1 = (bf16[256,1280]{1,0:T(8,128)(2,1)}, bf16[256,512]{1,0:T(8,128)(2,1)S(1)}) custom-call(bf16[256,2560]{1,0:T(8,128)(2,1)S(1)} %get-tuple-element.58.own_ref, bf16[256,2560]{1,0:T(8,128)(2,1)S(1)} %collective-permute-done.8.other_ref, bf16[640,256]{1,0:T(8,128)(2,1)S(1)} %collective-permute-done.5.p0, ...), custom_call_target="tpu_custom_call" | custom-call | flops 838860800 | bytes 5000000 | tf_op jit(solution)/shard_map/attention/pallas_call | solution.py:165
  67.4 6.7 %collective-permute-start.16 = (bf16[256,512]{1,0:T(8,128)(2,1)S(1)}, bf16[256,512]{1,0:T(8,128)(2,1)S(1)}, u32[]{:S(2)}, u32[]{:S(2)}) collective-permute-start(bf16[256,512]{1,0:T(8,128)(2,1)S(1)} %get-tuple-element.83.refs_7_), channel_id=1, source_target_pairs={{0,4},{4,8},{8,12},{12,0},{1,5},{5,9},{9,13},{13,1},{2,6},{6,10},{... | collective-permute-start | bytes 786440 | tf_op jit(solution)/shard_map/ppermute | solution.py:284
  74.2 1.3 %collective-permute-start.20 = (bf16[640,256]{1,0:T(8,128)(2,1)S(1)}, bf16[640,256]{1,0:T(8,128)(2,1)S(1)}, u32[]{:S(2)}, u32[]{:S(2)}) collective-permute-start(bf16[640,256]{1,0:T(8,128)(2,1)S(1)} %get-tuple-element.87), channel_id=1, source_target_pairs={{0,4},{1,12},{2,5},{3,13},{4,6},{5,14},{6,7},{7,15},{8,0},{9,8},{1... | collective-permute-start | bytes 983048 | tf_op jit(solution)/shard_map/ppermute | solution.py:303
  75.5 2.1 %collective-permute-start.21 = (bf16[640,256]{1,0:T(8,128)(2,1)S(1)}, bf16[640,256]{1,0:T(8,128)(2,1)S(1)}, u32[]{:S(2)}, u32[]{:S(2)}) collective-permute-start(bf16[640,256]{1,0:T(8,128)(2,1)S(1)} %get-tuple-element.88), channel_id=1, source_target_pairs={{0,6},{1,14},{2,7},{3,15},{4,0},{5,8},{6,1},{7,9},{8,2},{9,10},{10... | collective-permute-start | bytes 983048 | tf_op jit(solution)/shard_map/ppermute | solution.py:303
  77.6 3.4 %collective-permute-done.16.refs_9_ = bf16[256,512]{1,0:T(8,128)(2,1)S(1)} collective-permute-done((bf16[256,512]{1,0:T(8,128)(2,1)S(1)}, bf16[256,512]{1,0:T(8,128)(2,1)S(1)}, u32[]{:S(2)}, u32[]{:S(2)}) %collective-permute-start.16) | collective-permute-done | bytes 262176 | tf_op jit(solution)/shard_map/ppermute | solution.py:284
  80.9 3.0 %collective-permute-done.17.refs_8_ = bf16[256,512]{1,0:T(8,128)(2,1)S(1)} collective-permute-done((bf16[256,512]{1,0:T(8,128)(2,1)S(1)}, bf16[256,512]{1,0:T(8,128)(2,1)S(1)}, u32[]{:S(2)}, u32[]{:S(2)}) %collective-permute-start.17) | collective-permute-done | bytes 262176 | tf_op jit(solution)/shard_map/ppermute | solution.py:279
  83.9 2.8 %collective-permute-start.18 = (bf16[256,512]{1,0:T(8,128)(2,1)S(1)}, bf16[256,512]{1,0:T(8,128)(2,1)S(1)}, u32[]{:S(2)}, u32[]{:S(2)}) collective-permute-start(bf16[256,512]{1,0:T(8,128)(2,1)S(1)} %get-tuple-element.83.refs_7_), channel_id=1, source_target_pairs={{0,12},{4,0},{8,4},{12,8},{1,13},{5,1},{9,5},{13,9},{2,14},{6,2},{... | collective-permute-start | bytes 786440 | tf_op jit(solution)/shard_map/ppermute | solution.py:284
  86.7 4.8 %collective-permute-start.19 = (bf16[256,512]{1,0:T(8,128)(2,1)S(1)}, bf16[256,512]{1,0:T(8,128)(2,1)S(1)}, u32[]{:S(2)}, u32[]{:S(2)}) collective-permute-start(bf16[256,512]{1,0:T(8,128)(2,1)S(1)} %collective-permute-done.16.refs_9_), channel_id=1, source_target_pairs={{0,2},{2,0},{1,3},{3,1},{4,6},{6,4},{5,7},{7,5},{8,10},{10,8},{9,1... | collective-permute-start | bytes 786440 | tf_op jit(solution)/shard_map/ppermute | solution.py:279
  91.4 3.5 %collective-permute-done.21 = bf16[640,256]{1,0:T(8,128)(2,1)S(1)} collective-permute-done((bf16[640,256]{1,0:T(8,128)(2,1)S(1)}, bf16[640,256]{1,0:T(8,128)(2,1)S(1)}, u32[]{:S(2)}, u32[]{:S(2)}) %collective-permute-start.21) | collective-permute-done | bytes 327712 | tf_op jit(solution)/shard_map/ppermute | solution.py:303
  95.0 4.3 %collective-permute-done.18.refs_10_ = bf16[256,512]{1,0:T(8,128)(2,1)S(1)} collective-permute-done((bf16[256,512]{1,0:T(8,128)(2,1)S(1)}, bf16[256,512]{1,0:T(8,128)(2,1)S(1)}, u32[]{:S(2)}, u32[]{:S(2)}) %collective-permute-start.18) | collective-permute-done | bytes 262176 | tf_op jit(solution)/shard_map/ppermute | solution.py:284
  102.0 9.3 %collective-permute-done.23.refs_3_ = bf16[256,512]{1,0:T(8,128)(2,1)S(1)} collective-permute-done((bf16[256,512]{1,0:T(8,128)(2,1)S(1)}, bf16[256,512]{1,0:T(8,128)(2,1)S(1)}, u32[]{:S(2)}, u32[]{:S(2)}) %collective-permute-start.23) | collective-permute-done | bytes 262176 | tf_op jit(solution)/shard_map/ppermute | solution.py:284
  112.4 1.4 %constant_dynamic-update-slice_fusion.refs_1_.refs_2_.refs_3_.refs_4_.refs_5_.refs_6_ = bf16[8,640,256]{2,1,0:T(8,128)(2,1)S(1)} fusion(bf16[8,640,256]{2,1,0:T(8,128)(2,1)S(1)} %constant_dynamic-update-slice_fusion.1, bf16[4,640,256]{2,1,0:T(8,128)(2,1)} %collective-permute-done.22), kind=kLoop, calls=%fused_computation.9 | loop fusion | bytes 2621440 | tf_op jit(solution)/shard_map/concatenate | solution.py:378
  113.8 2.2 %gradient.2 = (f32[2,640,256]{2,1,0:T(8,128)S(1)}, f32[2,256]{1,0:T(2,128)S(1)}) custom-call(s32[6]{0:T(128)S(1)} %stack.59.refs_0_, bf16[8,640,256]{2,1,0:T(8,128)(2,1)S(1)} %constant_dynamic-update-slice_fusion.refs_1_.refs_2_.refs_3_.refs_4_.refs_5_.refs_6_, ...), custom_call_target="tpu_custom_call" | custom-call | flops 1006632960 | bytes 5000000 | tf_op jit(solution)/shard_map/gradient/pallas_call | solution.py:223
  116.0 3.3 %collective-permute-done.25.refs_4_ = bf16[256,512]{1,0:T(8,128)(2,1)S(1)} collective-permute-done((bf16[256,512]{1,0:T(8,128)(2,1)S(1)}, bf16[256,512]{1,0:T(8,128)(2,1)S(1)}, u32[]{:S(2)}, u32[]{:S(2)}) %collective-permute-start.25) | collective-permute-done | bytes 262176 | tf_op jit(solution)/shard_map/ppermute | solution.py:279
  119.4 2.3 %gradient.3 = (f32[2,640,256]{2,1,0:T(8,128)}, f32[2,256]{1,0:T(2,128)}) custom-call(s32[2]{0:T(128)S(1)} %pad_add_fusion.refs_0_, bf16[8,640,256]{2,1,0:T(8,128)(2,1)S(1)} %constant_dynamic-update-slice_fusion.refs_1_.refs_2_.refs_3_.refs_4_.refs_5_.refs_6_, ...), custom_call_target="tpu_custom_call" | custom-call | flops 335544320 | bytes 5000000 | tf_op jit(solution)/shard_map/gradient/pallas_call | solution.py:223
  (56 shorter events, 14.5 us)
Async XLA Ops:
  0.6 7.3 %copy-start = (bf16[256,2560]{1,0:T(8,128)(2,1)S(1)}, bf16[256,2560]{1,0:T(8,128)(2,1)}, u32[]{:S(2)}) copy-start(bf16[256,2560]{1,0:T(8,128)(2,1)} %values_ref.1) | copy-start | bytes 3932164
  0.6 5.9 %copy-start.4 = (bf16[5120]{0:T(1024)(128)(2,1)S(1)}, bf16[5120]{0:T(1024)(128)(2,1)}, u32[]{:S(2)}) copy-start(bf16[5120]{0:T(1024)(128)(2,1)} %param.7) | copy-start | bytes 30724
  1.8 12.8 %collective-permute-start = (bf16[640,256]{1,0:T(8,128)(2,1)S(1)}, bf16[640,256]{1,0:T(8,128)(2,1)S(1)}, u32[]{:S(2)}, u32[]{:S(2)}) collective-permute-start(bf16[640,256]{1,0:T(8,128)(2,1)S(1)} %dynamic-slice_bitcast_fusion), channel_id=1, source_target_pairs={{0,4},{4,8},{8,12},{12,0},{1,5},{5,9},{9,13},{13,1},{2,6},{6,10},{... | collective-permute-start | bytes 983048 | tf_op jit(solution)/shard_map/ppermute | solution.py:284
  6.5 49.0 %copy-start.5 = (bf16[2,256]{1,0:T(2,128)(2,1)S(1)}, bf16[2,256]{1,0:T(2,128)(2,1)}, u32[]{:S(2)}) copy-start(bf16[2,256]{1,0:T(2,128)(2,1)} %param.11) | copy-start | bytes 3076
  6.5 1.2 collective-permute-start.1
  7.9 47.7 %copy-start.1 = (bf16[2,1280,256]{2,1,0:T(8,128)(2,1)S(1)}, bf16[2,1280,256]{2,1,0:T(8,128)(2,1)}, u32[]{:S(2)}) copy-start(bf16[2,1280,256]{2,1,0:T(8,128)(2,1)} %weight_ref.1) | copy-start | bytes 3932164
  14.6 23.8 %collective-permute-start.8 = (bf16[256,2560]{1,0:T(8,128)(2,1)S(1)}, bf16[256,2560]{1,0:T(8,128)(2,1)S(1)}, u32[]{:S(2)}, u32[]{:S(2)}) collective-permute-start(bf16[256,2560]{1,0:T(8,128)(2,1)S(1)} %get-tuple-element.58.own_ref), channel_id=1, source_target_pairs={{0,1},{1,0},{2,3},{3,2},{4,5},{5,4},{6,7},{7,6},{8,9},{9,8},{10,11... | collective-permute-start | bytes 3932168 | tf_op jit(solution)/shard_map/ppermute | solution.py:279
  14.6 10.1 %collective-permute-start.2 = (bf16[640,256]{1,0:T(8,128)(2,1)S(1)}, bf16[640,256]{1,0:T(8,128)(2,1)S(1)}, u32[]{:S(2)}, u32[]{:S(2)}) collective-permute-start(bf16[640,256]{1,0:T(8,128)(2,1)S(1)} %collective-permute-done.refs_0_), channel_id=1, source_target_pairs={{0,2},{2,0},{1,3},{3,1},{4,6},{6,4},{5,7},{7,5},{8,10},{10,8},{9,1... | collective-permute-start | bytes 983048 | tf_op jit(solution)/shard_map/ppermute | solution.py:279
  16.1 9.8 %collective-permute-start.3 = (bf16[640,256]{1,0:T(8,128)(2,1)S(1)}, bf16[640,256]{1,0:T(8,128)(2,1)S(1)}, u32[]{:S(2)}, u32[]{:S(2)}) collective-permute-start(bf16[640,256]{1,0:T(8,128)(2,1)S(1)} %collective-permute-done.refs_0_), channel_id=1, source_target_pairs={{0,16},{16,0},{1,17},{17,1},{2,18},{18,2},{3,19},{19,3},{4,20},{20... | collective-permute-start | bytes 983048 | tf_op jit(solution)/shard_map/ppermute | solution.py:279
  17.6 9.6 %collective-permute-start.4 = (bf16[640,256]{1,0:T(8,128)(2,1)S(1)}, bf16[640,256]{1,0:T(8,128)(2,1)S(1)}, u32[]{:S(2)}, u32[]{:S(2)}) collective-permute-start(bf16[640,256]{1,0:T(8,128)(2,1)S(1)} %dynamic-slice_bitcast_fusion), channel_id=1, source_target_pairs={{0,12},{4,0},{8,4},{12,8},{1,13},{5,1},{9,5},{13,9},{2,14},{6,2},{... | collective-permute-start | bytes 983048 | tf_op jit(solution)/shard_map/ppermute | solution.py:284
  27.2 10.5 %collective-permute-start.5 = (bf16[640,256]{1,0:T(8,128)(2,1)S(1)}, bf16[640,256]{1,0:T(8,128)(2,1)S(1)}, u32[]{:S(2)}, u32[]{:S(2)}) collective-permute-start(bf16[640,256]{1,0:T(8,128)(2,1)S(1)} %collective-permute-done.refs_0_), channel_id=1, source_target_pairs={{0,4},{4,8},{8,12},{12,0},{1,5},{5,9},{9,13},{13,1},{2,6},{6,10},{... | collective-permute-start | bytes 983048 | tf_op jit(solution)/shard_map/ppermute | solution.py:284
  27.2 10.5 %collective-permute-start.6 = (bf16[640,256]{1,0:T(8,128)(2,1)S(1)}, bf16[640,256]{1,0:T(8,128)(2,1)S(1)}, u32[]{:S(2)}, u32[]{:S(2)}) collective-permute-start(bf16[640,256]{1,0:T(8,128)(2,1)S(1)} %collective-permute-done.4.refs_4_), channel_id=1, source_target_pairs={{0,2},{2,0},{1,3},{3,1},{4,6},{6,4},{5,7},{7,5},{8,10},{10,8},{9,1... | collective-permute-start | bytes 983048 | tf_op jit(solution)/shard_map/ppermute | solution.py:279
  27.7 10.6 %collective-permute-start.7 = (bf16[640,256]{1,0:T(8,128)(2,1)S(1)}, bf16[640,256]{1,0:T(8,128)(2,1)S(1)}, u32[]{:S(2)}, u32[]{:S(2)}) collective-permute-start(bf16[640,256]{1,0:T(8,128)(2,1)S(1)} %collective-permute-done.4.refs_4_), channel_id=1, source_target_pairs={{0,16},{16,0},{1,17},{17,1},{2,18},{18,2},{3,19},{19,3},{4,20},{20... | collective-permute-start | bytes 983048 | tf_op jit(solution)/shard_map/ppermute | solution.py:279
  28.2 17.2 %collective-permute-start.11 = (bf16[640,256]{1,0:T(8,128)(2,1)S(1)}, bf16[640,256]{1,0:T(8,128)(2,1)S(1)}, u32[]{:S(2)}, u32[]{:S(2)}) collective-permute-start(bf16[640,256]{1,0:T(8,128)(2,1)S(1)} %collective-permute-done.2.refs_1_), channel_id=1, source_target_pairs={{0,16},{16,0},{1,17},{17,1},{2,18},{18,2},{3,19},{19,3},{4,20},{20... | collective-permute-start | bytes 983048 | tf_op jit(solution)/shard_map/ppermute | solution.py:279
  38.3 12.3 %collective-permute-start.9 = (bf16[640,256]{1,0:T(8,128)(2,1)S(1)}, bf16[640,256]{1,0:T(8,128)(2,1)S(1)}, u32[]{:S(2)}, u32[]{:S(2)}) collective-permute-start(bf16[640,256]{1,0:T(8,128)(2,1)S(1)} %collective-permute-done.5.p0), channel_id=1, source_target_pairs={{0,2},{2,0},{1,3},{3,1},{4,6},{6,4},{5,7},{7,5},{8,10},{10,8},{9,1... | collective-permute-start | bytes 983048 | tf_op jit(solution)/shard_map/ppermute | solution.py:279
  39.8 10.8 %collective-permute-start.10 = (bf16[640,256]{1,0:T(8,128)(2,1)S(1)}, bf16[640,256]{1,0:T(8,128)(2,1)S(1)}, u32[]{:S(2)}, u32[]{:S(2)}) collective-permute-start(bf16[640,256]{1,0:T(8,128)(2,1)S(1)} %collective-permute-done.5.p0), channel_id=1, source_target_pairs={{0,16},{16,0},{1,17},{17,1},{2,18},{18,2},{3,19},{19,3},{4,20},{20... | collective-permute-start | bytes 983048 | tf_op jit(solution)/shard_map/ppermute | solution.py:279
  40.3 13.8 %collective-permute-start.12 = (bf16[640,256]{1,0:T(8,128)(2,1)S(1)}, bf16[640,256]{1,0:T(8,128)(2,1)S(1)}, u32[]{:S(2)}, u32[]{:S(2)}) collective-permute-start(bf16[640,256]{1,0:T(8,128)(2,1)S(1)} %collective-permute-done.7.refs_6_), channel_id=1, source_target_pairs={{0,2},{2,0},{1,3},{3,1},{4,6},{6,4},{5,7},{7,5},{8,10},{10,8},{9,1... | collective-permute-start | bytes 983048 | tf_op jit(solution)/shard_map/ppermute | solution.py:279
  40.9 13.2 %collective-permute-start.13 = (bf16[640,256]{1,0:T(8,128)(2,1)S(1)}, bf16[640,256]{1,0:T(8,128)(2,1)S(1)}, u32[]{:S(2)}, u32[]{:S(2)}) collective-permute-start(bf16[640,256]{1,0:T(8,128)(2,1)S(1)} %get-tuple-element.68), channel_id=1, source_target_pairs={{0,0},{1,8},{2,1},{3,9},{4,2},{5,10},{6,3},{7,11},{8,4},{9,12},{10... | collective-permute-start | bytes 983048 | tf_op jit(solution)/shard_map/ppermute | solution.py:303
  45.4 13.1 %collective-permute-start.15 = (bf16[640,256]{1,0:T(8,128)(2,1)S(1)}, bf16[640,256]{1,0:T(8,128)(2,1)S(1)}, u32[]{:S(2)}, u32[]{:S(2)}) collective-permute-start(bf16[640,256]{1,0:T(8,128)(2,1)S(1)} %get-tuple-element.77), channel_id=1, source_target_pairs={{0,2},{1,10},{2,3},{3,11},{4,4},{5,12},{6,5},{7,13},{8,6},{9,14},{... | collective-permute-start | bytes 983048 | tf_op jit(solution)/shard_map/ppermute | solution.py:303
  54.1 8.2 %collective-permute-start.14 = (bf16[640,256]{1,0:T(8,128)(2,1)S(1)}, bf16[640,256]{1,0:T(8,128)(2,1)S(1)}, u32[]{:S(2)}, u32[]{:S(2)}) collective-permute-start(bf16[640,256]{1,0:T(8,128)(2,1)S(1)} %collective-permute-done.9.p1), channel_id=1, source_target_pairs={{0,16},{16,0},{1,17},{17,1},{2,18},{18,2},{3,19},{19,3},{4,20},{20... | collective-permute-start | bytes 983048 | tf_op jit(solution)/shard_map/ppermute | solution.py:279
  55.6 6.7 %copy-start.2 = (bf16[256,1280]{1,0:T(8,128)(2,1)S(1)}, bf16[256,1280]{1,0:T(8,128)(2,1)}, u32[]{:S(2)}) copy-start(bf16[256,1280]{1,0:T(8,128)(2,1)} %queries_ref.1) | copy-start | bytes 1966084
  55.6 6.7 %copy-start.3 = (bf16[256,1280]{1,0:T(8,128)(2,1)S(1)}, bf16[256,1280]{1,0:T(8,128)(2,1)}, u32[]{:S(2)}) copy-start(bf16[256,1280]{1,0:T(8,128)(2,1)} %cotangent_ref.1) | copy-start | bytes 1966084
  67.4 13.5 %collective-permute-start.16 = (bf16[256,512]{1,0:T(8,128)(2,1)S(1)}, bf16[256,512]{1,0:T(8,128)(2,1)S(1)}, u32[]{:S(2)}, u32[]{:S(2)}) collective-permute-start(bf16[256,512]{1,0:T(8,128)(2,1)S(1)} %get-tuple-element.83.refs_7_), channel_id=1, source_target_pairs={{0,4},{4,8},{8,12},{12,0},{1,5},{5,9},{9,13},{13,1},{2,6},{6,10},{... | collective-permute-start | bytes 786440 | tf_op jit(solution)/shard_map/ppermute | solution.py:284
  74.2 9.7 %collective-permute-start.17 = (bf16[256,512]{1,0:T(8,128)(2,1)S(1)}, bf16[256,512]{1,0:T(8,128)(2,1)S(1)}, u32[]{:S(2)}, u32[]{:S(2)}) collective-permute-start(bf16[256,512]{1,0:T(8,128)(2,1)S(1)} %get-tuple-element.83.refs_7_), channel_id=1, source_target_pairs={{0,2},{2,0},{1,3},{3,1},{4,6},{6,4},{5,7},{7,5},{8,10},{10,8},{9,1... | collective-permute-start | bytes 786440 | tf_op jit(solution)/shard_map/ppermute | solution.py:279
  74.2 17.3 %collective-permute-start.20 = (bf16[640,256]{1,0:T(8,128)(2,1)S(1)}, bf16[640,256]{1,0:T(8,128)(2,1)S(1)}, u32[]{:S(2)}, u32[]{:S(2)}) collective-permute-start(bf16[640,256]{1,0:T(8,128)(2,1)S(1)} %get-tuple-element.87), channel_id=1, source_target_pairs={{0,4},{1,12},{2,5},{3,13},{4,6},{5,14},{6,7},{7,15},{8,0},{9,8},{1... | collective-permute-start | bytes 983048 | tf_op jit(solution)/shard_map/ppermute | solution.py:303
  75.5 19.5 %collective-permute-start.21 = (bf16[640,256]{1,0:T(8,128)(2,1)S(1)}, bf16[640,256]{1,0:T(8,128)(2,1)S(1)}, u32[]{:S(2)}, u32[]{:S(2)}) collective-permute-start(bf16[640,256]{1,0:T(8,128)(2,1)S(1)} %get-tuple-element.88), channel_id=1, source_target_pairs={{0,6},{1,14},{2,7},{3,15},{4,0},{5,8},{6,1},{7,9},{8,2},{9,10},{10... | collective-permute-start | bytes 983048 | tf_op jit(solution)/shard_map/ppermute | solution.py:303
  83.9 15.4 %collective-permute-start.18 = (bf16[256,512]{1,0:T(8,128)(2,1)S(1)}, bf16[256,512]{1,0:T(8,128)(2,1)S(1)}, u32[]{:S(2)}, u32[]{:S(2)}) collective-permute-start(bf16[256,512]{1,0:T(8,128)(2,1)S(1)} %get-tuple-element.83.refs_7_), channel_id=1, source_target_pairs={{0,12},{4,0},{8,4},{12,8},{1,13},{5,1},{9,5},{13,9},{2,14},{6,2},{... | collective-permute-start | bytes 786440 | tf_op jit(solution)/shard_map/ppermute | solution.py:284
  86.7 12.7 %collective-permute-start.19 = (bf16[256,512]{1,0:T(8,128)(2,1)S(1)}, bf16[256,512]{1,0:T(8,128)(2,1)S(1)}, u32[]{:S(2)}, u32[]{:S(2)}) collective-permute-start(bf16[256,512]{1,0:T(8,128)(2,1)S(1)} %collective-permute-done.16.refs_9_), channel_id=1, source_target_pairs={{0,2},{2,0},{1,3},{3,1},{4,6},{6,4},{5,7},{7,5},{8,10},{10,8},{9,1... | collective-permute-start | bytes 786440 | tf_op jit(solution)/shard_map/ppermute | solution.py:279
  100.6 11.8 %collective-permute-start.22 = (bf16[4,640,256]{2,1,0:T(8,128)(2,1)}, bf16[4,640,256]{2,1,0:T(8,128)(2,1)}, u32[]{:S(2)}, u32[]{:S(2)}) collective-permute-start(bf16[4,640,256]{2,1,0:T(8,128)(2,1)} %pad_maximum_fusion), channel_id=1, source_target_pairs={{0,1},{1,0},{2,3},{3,2},{4,5},{5,4},{6,7},{7,6},{8,9},{9,8},{10,11... | collective-permute-start | bytes 3932168 | tf_op jit(solution)/shard_map/ppermute | solution.py:279
  100.7 10.6 %collective-permute-start.23 = (bf16[256,512]{1,0:T(8,128)(2,1)S(1)}, bf16[256,512]{1,0:T(8,128)(2,1)S(1)}, u32[]{:S(2)}, u32[]{:S(2)}) collective-permute-start(bf16[256,512]{1,0:T(8,128)(2,1)S(1)} %collective-permute-done.16.refs_9_), channel_id=1, source_target_pairs={{0,4},{4,8},{8,12},{12,0},{1,5},{5,9},{9,13},{13,1},{2,6},{6,10},{... | collective-permute-start | bytes 786440 | tf_op jit(solution)/shard_map/ppermute | solution.py:284
  101.3 10.0 %collective-permute-start.24 = (bf16[256,512]{1,0:T(8,128)(2,1)S(1)}, bf16[256,512]{1,0:T(8,128)(2,1)S(1)}, u32[]{:S(2)}, u32[]{:S(2)}) collective-permute-start(bf16[256,512]{1,0:T(8,128)(2,1)S(1)} %collective-permute-done.18.refs_10_), channel_id=1, source_target_pairs={{0,2},{2,0},{1,3},{3,1},{4,6},{6,4},{5,7},{7,5},{8,10},{10,8},{9,1... | collective-permute-start | bytes 786440 | tf_op jit(solution)/shard_map/ppermute | solution.py:279
  111.3 8.0 %collective-permute-start.25 = (bf16[256,512]{1,0:T(8,128)(2,1)S(1)}, bf16[256,512]{1,0:T(8,128)(2,1)S(1)}, u32[]{:S(2)}, u32[]{:S(2)}) collective-permute-start(bf16[256,512]{1,0:T(8,128)(2,1)S(1)} %collective-permute-done.23.refs_3_), channel_id=1, source_target_pairs={{0,2},{2,0},{1,3},{3,1},{4,6},{6,4},{5,7},{7,5},{8,10},{10,8},{9,1... | collective-permute-start | bytes 786440 | tf_op jit(solution)/shard_map/ppermute | solution.py:279

commit v6 on v5

--- a/solution.py
+++ b/solution.py
@@ -182,13 +182,16 @@
 
 
 def gradient_kernel(count, first, *refs):
-    slabs, pairs = refs[1 : 1 + count], refs[1 + count : 1 + 2 * count]
-    refs = refs[1 + 2 * count :]
+    own, other, pairs = (refs[1 + i * count : 1 + (i + 1) * count] for i in range(3))
+    refs = refs[1 + 3 * count :]
+    core = lax.axis_index("sub")
     weight_ref, bias_ref = refs[-2:]
     columns = weight_ref.shape[2]
     total = None
-    for slab, pair in zip(slabs, pairs):
-        term = product(slab[0], pair[...])
+    for mine, others, pair in zip(own, other, pairs):
+        early = jnp.where(core == 0, mine[0], others[0])
+        late = jnp.where(core == 0, others[0], mine[0])
+        term = product(jnp.concatenate([early, late], 1), pair[...])
         total = term if total is None else total + term
     for j in range(2):
         part = total[:, j * columns : (j + 1) * columns]
@@ -205,18 +208,19 @@
             bias_ref[j : j + 1, :] = part if first else refs[1][j : j + 1, :] + part
 
 
-def gradient(at, slabs, pairs, sums):
-    _, share, length = slabs.shape
+def gradient(at, own, other, pairs, sums):
+    _, share, tokens = own.shape
+    length = pairs[0].shape[0]
     columns = pairs[0].shape[1] // 2
     count = len(pairs)
     tile = share // 2 if share % 32 == 0 else share
 
     def slab_spec(turn):
-        return pl.BlockSpec((1, tile, length), lambda i, at: (at[turn], i, 0))
+        return pl.BlockSpec((1, tile, tokens), lambda i, at: (at[turn], i, 0))
 
     weight_spec = pl.BlockSpec((2, tile, columns), lambda i, at: (0, i, 0))
     bias_spec = pl.BlockSpec((2, columns), lambda i, at: (0, 0))
-    in_specs = [slab_spec(turn) for turn in range(count)]
+    in_specs = [slab_spec(turn) for turn in range(count)] * 2
     in_specs += [pl.BlockSpec((length, 2 * columns), lambda i, at: (0, 0))] * count
     if sums:
         in_specs += [weight_spec, bias_spec]
@@ -237,42 +241,56 @@
             flops=4 * count * length * share * columns, bytes_accessed=5000000, transcendentals=0
         ),
         name="gradient",
-    )(at, *([slabs] * count), *pairs, *(sums or ()))
-
-
-def norm_kernel(values_ref, scale_ref, gain_ref, normed_ref, *slab_refs):
-    blocks, replicas = lax.axis_size("blk"), lax.axis_size("dp")
-    number = lax.axis_index("blk") * replicas + lax.axis_index("dp")
-    half = blocks * replicas // 2
-    share = values_ref.shape[1] // half
-
-    def scaled(place):
-        wide_values = values_ref[:, place].astype(jnp.float32)
-        return wide_values * scale_ref[...] * gain_ref[:, place]
-
-    for slab in range(half):
-        place = pl.ds(slab * share, share)
-        normed_ref[:, place] = scaled(place).astype(jnp.bfloat16)
-    for turn, slab_ref in enumerate(slab_refs):
-        slab = lax.rem(turn + number // 2, half)
-        place = pl.ds(pl.multiple_of(slab * share, 128), share)
-        slab_ref[...] = scaled(place).T.astype(jnp.bfloat16)
-
-
-def norm(activations, scale, gain, slabs):
+    )(at, *([own] * count), *([other] * count), *pairs, *(sums or ()))
+
+
+def norm_kernel(values_ref, scale_ref, gain_ref, normed_ref):
+    wide_values = values_ref[...].astype(jnp.float32)
+    normed_ref[...] = (wide_values * scale_ref[...] * gain_ref[...]).astype(jnp.bfloat16)
+
+
+def norm(activations, scale, gain):
     length, features = activations.shape
     return pl.pallas_call(
         norm_kernel,
         in_specs=[IN_VMEM] * 3,
-        out_specs=[IN_VMEM] * (1 + slabs),
-        out_shape=[jax.ShapeDtypeStruct(activations.shape, jnp.bfloat16)]
-        + [jax.ShapeDtypeStruct((features // slabs, length), jnp.bfloat16)] * slabs,
+        out_specs=IN_VMEM,
+        out_shape=jax.ShapeDtypeStruct(activations.shape, jnp.bfloat16),
+        compiler_params=pltpu.CompilerParams(vmem_limit_bytes=VMEM_BYTES),
+        cost_estimate=pl.CostEstimate(
+            flops=4 * length * features, bytes_accessed=4 * length * features, transcendentals=0
+        ),
+        name="norm",
+    )(activations, scale, gain)
+
+
+def slabs_kernel(own_ref, other_ref, slabs_ref):
+    sequences, share, tokens = slabs_ref.shape
+    core = lax.axis_index("sub")
+    mine = pl.ds(pl.multiple_of(core * tokens, 16), tokens)
+    for half in range(2):
+        for at in range(sequences // 2):
+            place = slice(at * share, (at + 1) * share)
+            values = jnp.where(core == half, own_ref[mine, place], other_ref[mine, place])
+            slabs_ref[half * (sequences // 2) + at] = values.astype(jnp.float32).T.astype(
+                jnp.bfloat16
+            )
+
+
+def make_slabs(normed, normed_other, sequences):
+    length, features = normed.shape
+    share = 2 * features // sequences
+    return pl.pallas_call(
+        slabs_kernel,
+        in_specs=[IN_VMEM] * 2,
+        out_specs=IN_VMEM,
+        out_shape=jax.ShapeDtypeStruct((sequences, share, length // 2), jnp.bfloat16),
         compiler_params=pltpu.CompilerParams(vmem_limit_bytes=VMEM_BYTES),
         cost_estimate=pl.CostEstimate(
             flops=4 * length * features, bytes_accessed=6 * length * features, transcendentals=0
         ),
-        name="norm",
-    )(activations, scale, gain)
+        name="make_slabs",
+    )(normed, normed_other)
 
 
 def swapped(block, axis):
@@ -320,9 +338,6 @@
     _, block_rows, columns = kv_weight.shape
     length = activations.shape[0]
     share = block_rows // replicas
-    half = blocks * replicas // 2
-    number = block * replicas + replica
-    slab_here = number % half
 
     piece = lax.dynamic_slice(kv_weight, (group, replica * share, 0), (1, share, columns))[0]
     scale, gain = scale_and_gain(activations, norm_gain)
@@ -335,47 +350,39 @@
         )
 
     up = turned(piece, "blk", 1)
-    normed, *slabs = norm(activations, scale, gain[None, :], half)
-    up, piece, normed, slabs = lax.optimization_barrier((up, piece, normed, slabs))
+    normed = norm(activations, scale, gain[None, :])
+    up, piece, normed = lax.optimization_barrier((up, piece, normed))
     up_x, up_y, down = swapped(up, "dp"), swapped(up, "groups"), turned(piece, "blk", -1)
     normed_other = swapped(normed, "sub")
-    up, up_x, up_y, down = lax.optimization_barrier((up, up_x, up_y, down))
+    up, up_x, up_y, down, normed_other = lax.optimization_barrier(
+        (up, up_x, up_y, down, normed_other)
+    )
     down_x, down_y = swapped(down, "dp"), swapped(down, "groups")
     twice = turned(up, "blk", 1)
     up_both = swapped(up_x, "groups")
-    twice, down_x, down_y, normed_other = lax.optimization_barrier(
-        (twice, down_x, down_y, normed_other)
-    )
+    slabs = make_slabs(normed, normed_other, blocks * replicas)
+    twice, down_x, down_y, slabs = lax.optimization_barrier((twice, down_x, down_y, slabs))
     twice_x, twice_y = swapped(twice, "dp"), swapped(twice, "groups")
     down_both = swapped(down_y, "dp")
-    slabs[:2] = [sent_slab(after(slabs[turn], twice), turn) for turn in (0, 1)]
-    twice_x, twice_y, up_both, down_both, slabs[0] = lax.optimization_barrier(
-        (twice_x, twice_y, up_both, down_both, slabs[0])
+    slabs = lax.all_to_all(slabs, ("blk", "dp"), 0, 0)
+    twice_x, twice_y, up_both, down_both = lax.optimization_barrier(
+        (twice_x, twice_y, up_both, down_both)
     )
     twice_both = swapped(twice_x, "groups")
 
     gathered = [(1, (up, up_x, up_y, up_both)), (-1, (down, down_x, down_y, down_both))]
     sums = project(normed, normed_other, kv_weight, gathered)
-    sums, *slabs = lax.optimization_barrier((sums, *slabs))
-    slabs[2:] = [sent_slab(slabs[turn], turn) for turn in (2, 3)]
     grad_query, grad_pair = attention(
         2, normed, normed_other, (twice, twice_x, twice_y, twice_both), sums, bias, cosine, sine,
         queries, cotangent,
     )
 
-    def slab_of(distance, same):
-        source = replica if same else 1 - replica
-        turn = (slab_here - (block - distance)) % half
-        return (source != core) * half + turn
-
+    grad_pair, slabs = lax.optimization_barrier((grad_pair, slabs))
     pair_up, pair_x = turned(grad_pair, "blk", 1), swapped(grad_pair, "dp")
     pair_up, pair_x, grad_pair = lax.optimization_barrier((pair_up, pair_x, grad_pair))
     pair_down, pair_up_x = turned(grad_pair, "blk", -1), swapped(pair_up, "dp")
-    pair_down, pair_up_x, pair_up, *slabs = lax.optimization_barrier(
-        (pair_down, pair_up_x, pair_up, *slabs)
-    )
-    slabs_own = jnp.stack(slabs)
-    slabs_held = jnp.concatenate([slabs_own, swapped(slabs_own, "sub")])
+    slabs_other = swapped(slabs, "sub")
+    pair_down, pair_up_x, pair_up = lax.optimization_barrier((pair_down, pair_up_x, pair_up))
     pair_twice, pair_down_x = turned(pair_up, "blk", 1), swapped(pair_down, "dp")
     pair_twice, pair_down_x = lax.optimization_barrier((pair_twice, pair_down_x))
     pair_twice_x = swapped(pair_twice, "dp")
@@ -390,8 +397,12 @@
     last = {(2, True): pair_twice, (2, False): pair_twice_x}
     sums = None
     for some in (first, last):
-        at = jnp.stack([slab_of(*which) for which in some]).astype(jnp.int32)
-        sums = gradient(at, slabs_held, list(some.values()), sums)
+        at = [
+            (block - distance) % blocks * replicas + (replica if same else 1 - replica)
+            for distance, same in some
+        ]
+        at = jnp.stack(at).astype(jnp.int32)
+        sums = gradient(at, slabs, slabs_other, list(some.values()), sums)
     grad_weight, grad_bias = sums
     return (grad_query, grad_weight, grad_bias)
 

time: 122 us -> 128 us (1.049)
  starting transfers between devices: 37.7 us -> 24.2 us
  local copies, waits for them, and re-layouts: 2.88 us -> 14.5 us
  waiting for transfers between devices: 64.5 us -> 70.2 us
  Pallas kernels: 12 us -> 14.8 us
    unnamed x16 -> x44, local copies, waits for them, and re-layouts: 0.12 us -> 13.1 us
    ppermute x4 -> x0, starting transfers between devices: 7.42 us -> none  [sent_slab(): return lax.ppermute(slab, ('blk', 'dp', 'sub'), slab_route(turn))]
    ppermute x16, waiting for transfers between devices: 27.6 us -> 34.2 us  [swapped(): return lax.ppermute(block, axis, [(0, 1), (1, 0)])]
    ppermute x6, starting transfers between devices: 14.9 us -> 8.61 us  [turned(): lax.ppermute(block, axis, [(i, (i + distance) % size) for i in range(size)])]
    ppermute x4 -> x0, waiting for transfers between devices: 4.87 us -> none  [sent_slab(): return lax.ppermute(slab, ('blk', 'dp', 'sub'), slab_route(turn))]
    ppermute x6, waiting for transfers between devices: 32 us -> 36 us  [turned(): lax.ppermute(block, axis, [(i, (i + distance) % size) for i in range(size)])]
    all_to_all x0 -> x1, starting transfers between devices: none -> 3.72 us  [local(): slabs = lax.all_to_all(slabs, ('blk', 'dp'), 0, 0)]
    ppermute x16, starting transfers between devices: 15.3 us -> 11.9 us  [swapped(): return lax.ppermute(block, axis, [(0, 1), (1, 0)])]
  transfers between devices with their start and end apart: 26 -> 23, of which waited for: 18 -> 15; matrix products, arithmetic and copies ran while one was open for 3% -> 2% of each run, Pallas kernels for 4% -> 9%
where the time goes in v6:
time: 128 us; the launch traced here: 127 us
  waiting for transfers between devices  70.2 us (55%)
  starting transfers between devices  24.2 us (19%)
  Pallas kernels  14.8 us (12%)
  local copies, waits for them, and re-layouts  14.5 us (11%)
  other arithmetic  2.47 us (2%)
    ppermute x6, waiting for transfers between devices, turned(): lax.ppermute(block, axis, [(i, (i + distance) % size) for i in range(size)])  36 us
    ppermute x16, waiting for transfers between devices, swapped(): return lax.ppermute(block, axis, [(0, 1), (1, 0)])  34.2 us
    unnamed x44, local copies, waits for them, and re-layouts  13.1 us
    ppermute x16, starting transfers between devices, swapped(): return lax.ppermute(block, axis, [(0, 1), (1, 0)])  11.9 us
    ppermute x6, starting transfers between devices, turned(): lax.ppermute(block, axis, [(i, (i + distance) % size) for i in range(size)])  8.61 us
    pallas_call x1, Pallas kernels, attention(): pl.pallas_call(functools.partial(attention_kernel, distance), in_specs=[I...  6.04 us
    pallas_call x2, Pallas kernels, gradient(): pl.pallas_call(functools.partial(gradient_kernel, count, sums is None), g...  5.52 us
    all_to_all x1, starting transfers between devices, local(): slabs = lax.all_to_all(slabs, ('blk', 'dp'), 0, 0)  3.72 us
  transfers between devices with their start and end apart: 23, of which 15 were waited for; matrix products, arithmetic and copies ran while one was open for 2% of the time, Pallas kernels for 9%

profile of v6, /device:TPU:0, one launch (start us, length us, event | category | flops | bytes accessed | tf_op | source)
XLA Modules:
  0.0 127.1 jit_solution(5763173923761216209)
XLA Ops:
  0.7 1.1 dynamic-slice_bitcast_fusion
  1.8 3.1 %collective-permute-start = (bf16[640,256]{1,0:T(8,128)(2,1)S(1)}, bf16[640,256]{1,0:T(8,128)(2,1)S(1)}, u32[]{:S(2)}, u32[]{:S(2)}) collective-permute-start(bf16[640,256]{1,0:T(8,128)(2,1)S(1)} %dynamic-slice_bitcast_fusion), channel_id=1, source_target_pairs={{0,4},{4,8},{8,12},{12,0},{1,5},{5,9},{9,13},{13,1},{2,6},{6,10},{... | collective-permute-start | bytes 983048 | tf_op jit(solution)/shard_map/ppermute | solution.py:302
  4.8 1.7 %multiply_reduce_fusion = f32[256]{0:T(256)S(1)} fusion(bf16[256,2560]{1,0:T(8,128)(2,1)} %values_ref.1), kind=kLoop, calls=%fused_computation | loop fusion | flops 1965824 | bytes 1311744 | tf_op jit(solution)/shard_map/reduce_sum | solution.py:328
  6.7 1.0 collective-permute-done.1
  8.3 6.3 %collective-permute-done.refs_0_ = bf16[640,256]{1,0:T(8,128)(2,1)S(1)} collective-permute-done((bf16[640,256]{1,0:T(8,128)(2,1)S(1)}, bf16[640,256]{1,0:T(8,128)(2,1)S(1)}, u32[]{:S(2)}, u32[]{:S(2)}) %collective-permute-start) | collective-permute-done | bytes 327712 | tf_op jit(solution)/shard_map/ppermute | solution.py:302
  14.6 1.5 %collective-permute-start.2 = (bf16[640,256]{1,0:T(8,128)(2,1)S(1)}, bf16[640,256]{1,0:T(8,128)(2,1)S(1)}, u32[]{:S(2)}, u32[]{:S(2)}) collective-permute-start(bf16[640,256]{1,0:T(8,128)(2,1)S(1)} %collective-permute-done.refs_0_), channel_id=1, source_target_pairs={{0,2},{2,0},{1,3},{3,1},{4,6},{6,4},{5,7},{7,5},{8,10},{10,8},{9,1... | collective-permute-start | bytes 983048 | tf_op jit(solution)/shard_map/ppermute | solution.py:297
  16.1 1.5 %collective-permute-start.3 = (bf16[640,256]{1,0:T(8,128)(2,1)S(1)}, bf16[640,256]{1,0:T(8,128)(2,1)S(1)}, u32[]{:S(2)}, u32[]{:S(2)}) collective-permute-start(bf16[640,256]{1,0:T(8,128)(2,1)S(1)} %collective-permute-done.refs_0_), channel_id=1, source_target_pairs={{0,16},{16,0},{1,17},{17,1},{2,18},{18,2},{3,19},{19,3},{4,20},{20... | collective-permute-start | bytes 983048 | tf_op jit(solution)/shard_map/ppermute | solution.py:297
  17.6 1.7 %collective-permute-start.4 = (bf16[640,256]{1,0:T(8,128)(2,1)}, bf16[640,256]{1,0:T(8,128)(2,1)S(1)}, u32[]{:S(2)}, u32[]{:S(2)}) collective-permute-start(bf16[640,256]{1,0:T(8,128)(2,1)} %copy-done.19), channel_id=1, source_target_pairs={{0,12},{4,0},{8,4},{12,8},{1,13},{5,1},{9,5},{13,9},{2,14},{6,2},{... | collective-permute-start | bytes 983048 | tf_op jit(solution)/shard_map/ppermute | solution.py:302
  19.3 5.4 %collective-permute-done.2.refs_1_ = bf16[640,256]{1,0:T(8,128)(2,1)S(1)} collective-permute-done((bf16[640,256]{1,0:T(8,128)(2,1)S(1)}, bf16[640,256]{1,0:T(8,128)(2,1)S(1)}, u32[]{:S(2)}, u32[]{:S(2)}) %collective-permute-start.2) | collective-permute-done | bytes 327712 | tf_op jit(solution)/shard_map/ppermute | solution.py:297
  24.7 1.2 collective-permute-done.3.refs_2_
  29.3 1.1 copy-done.3
  30.4 7.6 %collective-permute-done.6.p0 = bf16[640,256]{1,0:T(8,128)(2,1)} collective-permute-done((bf16[640,256]{1,0:T(8,128)(2,1)S(1)}, bf16[640,256]{1,0:T(8,128)(2,1)}, u32[]{:S(2)}, u32[]{:S(2)}) %collective-permute-start.6) | collective-permute-done | bytes 327712 | tf_op jit(solution)/shard_map/ppermute | solution.py:302
  38.8 3.7 %all-to-all-start = ((bf16[8,640,128]{2,1,0:T(8,128)(2,1)}), bf16[8,640,128]{2,1,0:T(8,128)(2,1)S(1)}, u32[]{:S(2)}, u32[]{:S(2)}) async-start(bf16[8,640,128]{2,1,0:T(8,128)(2,1)} %copy-done.3), calls=%async_computation | async-start | bytes 2621440 | tf_op jit(solution)/shard_map/all_to_all | solution.py:367
  42.5 1.1 collective-permute-start.11
  44.6 2.0 %collective-permute-start.12 = (bf16[640,256]{1,0:T(8,128)(2,1)}, bf16[640,256]{1,0:T(8,128)(2,1)S(1)}, u32[]{:S(2)}, u32[]{:S(2)}) collective-permute-start(bf16[640,256]{1,0:T(8,128)(2,1)} %collective-permute-done.8.refs_6_), channel_id=1, source_target_pairs={{0,2},{2,0},{1,3},{3,1},{4,6},{6,4},{5,7},{7,5},{8,10},{10,8},{9,1... | collective-permute-start | bytes 983048 | tf_op jit(solution)/shard_map/ppermute | solution.py:297
  46.6 6.6 %collective-permute-done.11.refs_3_ = bf16[640,256]{1,0:T(8,128)(2,1)S(1)} collective-permute-done((bf16[640,256]{1,0:T(8,128)(2,1)S(1)}, bf16[640,256]{1,0:T(8,128)(2,1)S(1)}, u32[]{:S(2)}, u32[]{:S(2)}) %collective-permute-start.11) | collective-permute-done | bytes 327712 | tf_op jit(solution)/shard_map/ppermute | solution.py:297
  53.2 4.1 %collective-permute-done.10.p2 = bf16[640,256]{1,0:T(8,128)(2,1)S(1)} collective-permute-done((bf16[640,256]{1,0:T(8,128)(2,1)}, bf16[640,256]{1,0:T(8,128)(2,1)S(1)}, u32[]{:S(2)}, u32[]{:S(2)}) %collective-permute-start.10) | collective-permute-done | bytes 327712 | tf_op jit(solution)/shard_map/ppermute | solution.py:297
  57.3 9.2 %collective-permute-done.12.refs_7_ = bf16[640,256]{1,0:T(8,128)(2,1)S(1)} collective-permute-done((bf16[640,256]{1,0:T(8,128)(2,1)}, bf16[640,256]{1,0:T(8,128)(2,1)S(1)}, u32[]{:S(2)}, u32[]{:S(2)}) %collective-permute-start.12) | collective-permute-done | bytes 327712 | tf_op jit(solution)/shard_map/ppermute | solution.py:297
  66.4 4.9 %collective-permute-done.9.p1 = bf16[640,256]{1,0:T(8,128)(2,1)S(1)} collective-permute-done((bf16[640,256]{1,0:T(8,128)(2,1)}, bf16[640,256]{1,0:T(8,128)(2,1)S(1)}, u32[]{:S(2)}, u32[]{:S(2)}) %collective-permute-start.9) | collective-permute-done | bytes 327712 | tf_op jit(solution)/shard_map/ppermute | solution.py:297
  71.3 1.4 %collective-permute-start.13 = (bf16[640,256]{1,0:T(8,128)(2,1)S(1)}, bf16[640,256]{1,0:T(8,128)(2,1)S(1)}, u32[]{:S(2)}, u32[]{:S(2)}) collective-permute-start(bf16[640,256]{1,0:T(8,128)(2,1)S(1)} %collective-permute-done.9.p1), channel_id=1, source_target_pairs={{0,16},{16,0},{1,17},{17,1},{2,18},{18,2},{3,19},{19,3},{4,20},{20... | collective-permute-start | bytes 983048 | tf_op jit(solution)/shard_map/ppermute | solution.py:297
  73.5 1.3 %copy-done.1 = bf16[256,2560]{1,0:T(8,128)(2,1)S(1)} copy-done((bf16[256,2560]{1,0:T(8,128)(2,1)S(1)}, bf16[256,2560]{1,0:T(8,128)(2,1)}, u32[]{:S(2)}) %copy-start.1) | copy-done | bytes 1310744
  74.8 1.3 %copy-done.4 = bf16[2,1280,256]{2,1,0:T(8,128)(2,1)S(1)} copy-done((bf16[2,1280,256]{2,1,0:T(8,128)(2,1)S(1)}, bf16[2,1280,256]{2,1,0:T(8,128)(2,1)}, u32[]{:S(2)}) %copy-start.4) | copy-done | bytes 1310744
  79.0 2.5 %project.1.sums_ref = f32[2,256,256]{2,1,0:T(8,128)S(1)} custom-call(bf16[256,2560]{1,0:T(8,128)(2,1)S(1)} %norm.1.own_ref, bf16[256,2560]{1,0:T(8,128)(2,1)S(1)} %copy-done.1, bf16[2,1280,256]{2,1,0:T(8,128)(2,1)S(1)} %copy-done.4, bf16[640,256]{1,0:T(8,128)(2,1)S(1)} %collective-permute-done.refs_0_, bf16[640,256]{1,0:T(8,128)(2,1)S(1)} %collective-permute-done.2.refs_1_, ...), custom_call_target="tpu_custom_call" | custom-call | flops 1006632960 | bytes 7000000 | tf_op jit(solution)/shard_map/project/pallas_call | solution.py:91
  81.5 6.0 %attention.1 = (bf16[256,1280]{1,0:T(8,128)(2,1)}, bf16[256,512]{1,0:T(8,128)(2,1)S(1)}) custom-call(bf16[256,2560]{1,0:T(8,128)(2,1)S(1)} %norm.1.own_ref, bf16[256,2560]{1,0:T(8,128)(2,1)S(1)} %copy-done.1, bf16[640,256]{1,0:T(8,128)(2,1)} %collective-permute-done.6.p0, bf16[640,256]{1,0:T(8,128)(2,1)S(1)} %collective-permute-done.9.p1, ...), custom_call_target="tpu_custom_call" | custom-call | flops 838860800 | bytes 5000000 | tf_op jit(solution)/shard_map/attention/pallas_call | solution.py:165
  87.6 1.5 %collective-permute-start.15 = (bf16[256,512]{1,0:T(8,128)(2,1)S(1)}, bf16[256,512]{1,0:T(8,128)(2,1)S(1)}, u32[]{:S(2)}, u32[]{:S(2)}) collective-permute-start(bf16[256,512]{1,0:T(8,128)(2,1)S(1)} %get-tuple-element.55.refs_13_), channel_id=1, source_target_pairs={{0,4},{4,8},{8,12},{12,0},{1,5},{5,9},{9,13},{13,1},{2,6},{6,10},{... | collective-permute-start | bytes 786440 | tf_op jit(solution)/shard_map/ppermute | solution.py:302
  89.6 8.5 %collective-permute-done.15.refs_15_ = bf16[256,512]{1,0:T(8,128)(2,1)S(1)} collective-permute-done((bf16[256,512]{1,0:T(8,128)(2,1)S(1)}, bf16[256,512]{1,0:T(8,128)(2,1)S(1)}, u32[]{:S(2)}, u32[]{:S(2)}) %collective-permute-start.15) | collective-permute-done | bytes 262176 | tf_op jit(solution)/shard_map/ppermute | solution.py:302
  98.1 1.7 %collective-permute-start.17 = (bf16[256,512]{1,0:T(8,128)(2,1)S(1)}, bf16[256,512]{1,0:T(8,128)(2,1)S(1)}, u32[]{:S(2)}, u32[]{:S(2)}) collective-permute-start(bf16[256,512]{1,0:T(8,128)(2,1)S(1)} %get-tuple-element.55.refs_13_), channel_id=1, source_target_pairs={{0,12},{4,0},{8,4},{12,8},{1,13},{5,1},{9,5},{13,9},{2,14},{6,2},{... | collective-permute-start | bytes 786440 | tf_op jit(solution)/shard_map/ppermute | solution.py:302
  100.1 5.9 %collective-permute-done.17.refs_16_ = bf16[256,512]{1,0:T(8,128)(2,1)S(1)} collective-permute-done((bf16[256,512]{1,0:T(8,128)(2,1)S(1)}, bf16[256,512]{1,0:T(8,128)(2,1)S(1)}, u32[]{:S(2)}, u32[]{:S(2)}) %collective-permute-start.17) | collective-permute-done | bytes 262176 | tf_op jit(solution)/shard_map/ppermute | solution.py:302
  106.1 1.2 collective-permute-done.18.refs_17_
  109.5 6.9 %collective-permute-done.19.refs_5_ = bf16[256,512]{1,0:T(8,128)(2,1)} collective-permute-done((bf16[256,512]{1,0:T(8,128)(2,1)S(1)}, bf16[256,512]{1,0:T(8,128)(2,1)}, u32[]{:S(2)}, u32[]{:S(2)}) %collective-permute-start.19) | collective-permute-done | bytes 262176 | tf_op jit(solution)/shard_map/ppermute | solution.py:302
  120.9 2.3 %gradient.2 = (f32[2,640,256]{2,1,0:T(8,128)S(1)}, f32[2,256]{1,0:T(2,128)S(1)}) custom-call(s32[6]{0:T(128)S(1)} %stack.39.refs_0_, bf16[8,640,128]{2,1,0:T(8,128)(2,1)S(1)} %all-to-all-done.refs_1_.refs_2_.refs_3_.refs_4_.refs_5_.refs_6_, bf16[8,640,128]{2,1,0:T(8,128)(2,1)S(1)} %all-to-all-done.refs_1_.refs_2_.refs_3_.refs_4_.refs_5_.refs_6_, ...), custom_call_target="tpu_custom_call" | custom-call | flops 1006632960 | bytes 5000000 | tf_op jit(solution)/shard_map/gradient/pallas_call | solution.py:227
  123.8 3.3 %gradient.3 = (f32[2,640,256]{2,1,0:T(8,128)}, f32[2,256]{1,0:T(2,128)}) custom-call(s32[2]{0:T(128)S(1)} %pad_add_fusion.refs_0_, bf16[8,640,128]{2,1,0:T(8,128)(2,1)S(1)} %all-to-all-done.refs_1_.refs_2_.refs_3_.refs_4_.refs_5_.refs_6_, bf16[8,640,128]{2,1,0:T(8,128)(2,1)S(1)} %all-to-all-done.refs_1_.refs_2_.refs_3_.refs_4_.refs_5_.refs_6_, ...), custom_call_target="tpu_custom_call" | custom-call | flops 335544320 | bytes 5000000 | tf_op jit(solution)/shard_map/gradient/pallas_call | solution.py:227
  (77 shorter events, 17.6 us)
Async XLA Ops:
  0.6 7.3 %copy-start.2 = (bf16[256,2560]{1,0:T(8,128)(2,1)S(1)}, bf16[256,2560]{1,0:T(8,128)(2,1)}, u32[]{:S(2)}) copy-start(bf16[256,2560]{1,0:T(8,128)(2,1)} %values_ref.1) | copy-start | bytes 3932164
  0.6 5.9 %copy-start.20 = (bf16[5120]{0:T(1024)(128)(2,1)S(1)}, bf16[5120]{0:T(1024)(128)(2,1)}, u32[]{:S(2)}) copy-start(bf16[5120]{0:T(1024)(128)(2,1)} %param.7) | copy-start | bytes 30724
  1.8 12.8 %copy-start.19 = (bf16[640,256]{1,0:T(8,128)(2,1)}, bf16[640,256]{1,0:T(8,128)(2,1)S(1)}, u32[]{:S(2)}) copy-start(bf16[640,256]{1,0:T(8,128)(2,1)S(1)} %dynamic-slice_bitcast_fusion) | copy-start | bytes 983044
  1.8 12.8 %collective-permute-start = (bf16[640,256]{1,0:T(8,128)(2,1)S(1)}, bf16[640,256]{1,0:T(8,128)(2,1)S(1)}, u32[]{:S(2)}, u32[]{:S(2)}) collective-permute-start(bf16[640,256]{1,0:T(8,128)(2,1)S(1)} %dynamic-slice_bitcast_fusion), channel_id=1, source_target_pairs={{0,4},{4,8},{8,12},{12,0},{1,5},{5,9},{9,13},{13,1},{2,6},{6,10},{... | collective-permute-start | bytes 983048 | tf_op jit(solution)/shard_map/ppermute | solution.py:302
  6.5 1.2 collective-permute-start.1
  14.6 12.8 %collective-permute-start.5 = (bf16[256,2560]{1,0:T(8,128)(2,1)S(1)}, bf16[256,2560]{1,0:T(8,128)(2,1)S(1)}, u32[]{:S(2)}, u32[]{:S(2)}) collective-permute-start(bf16[256,2560]{1,0:T(8,128)(2,1)S(1)} %norm.1.own_ref), channel_id=1, source_target_pairs={{0,1},{1,0},{2,3},{3,2},{4,5},{5,4},{6,7},{7,6},{8,9},{9,8},{10,11... | collective-permute-start | bytes 3932168 | tf_op jit(solution)/shard_map/ppermute | solution.py:297
  14.6 10.1 %collective-permute-start.2 = (bf16[640,256]{1,0:T(8,128)(2,1)S(1)}, bf16[640,256]{1,0:T(8,128)(2,1)S(1)}, u32[]{:S(2)}, u32[]{:S(2)}) collective-permute-start(bf16[640,256]{1,0:T(8,128)(2,1)S(1)} %collective-permute-done.refs_0_), channel_id=1, source_target_pairs={{0,2},{2,0},{1,3},{3,1},{4,6},{6,4},{5,7},{7,5},{8,10},{10,8},{9,1... | collective-permute-start | bytes 983048 | tf_op jit(solution)/shard_map/ppermute | solution.py:297
  16.1 9.8 %collective-permute-start.3 = (bf16[640,256]{1,0:T(8,128)(2,1)S(1)}, bf16[640,256]{1,0:T(8,128)(2,1)S(1)}, u32[]{:S(2)}, u32[]{:S(2)}) collective-permute-start(bf16[640,256]{1,0:T(8,128)(2,1)S(1)} %collective-permute-done.refs_0_), channel_id=1, source_target_pairs={{0,16},{16,0},{1,17},{17,1},{2,18},{18,2},{3,19},{19,3},{4,20},{20... | collective-permute-start | bytes 983048 | tf_op jit(solution)/shard_map/ppermute | solution.py:297
  17.6 9.8 %collective-permute-start.4 = (bf16[640,256]{1,0:T(8,128)(2,1)}, bf16[640,256]{1,0:T(8,128)(2,1)S(1)}, u32[]{:S(2)}, u32[]{:S(2)}) collective-permute-start(bf16[640,256]{1,0:T(8,128)(2,1)} %copy-done.19), channel_id=1, source_target_pairs={{0,12},{4,0},{8,4},{12,8},{1,13},{5,1},{9,5},{13,9},{2,14},{6,2},{... | collective-permute-start | bytes 983048 | tf_op jit(solution)/shard_map/ppermute | solution.py:302
  27.4 1.9 %copy-start.9 = (bf16[640,256]{1,0:T(8,128)(2,1)}, bf16[640,256]{1,0:T(8,128)(2,1)S(1)}, u32[]{:S(2)}) copy-start(bf16[640,256]{1,0:T(8,128)(2,1)S(1)} %collective-permute-done.4.refs_4_) | copy-start | bytes 983044
  27.4 1.9 %copy-start = (bf16[256,2560]{1,0:T(8,128)(2,1)}, bf16[256,2560]{1,0:T(8,128)(2,1)S(1)}, u32[]{:S(2)}) copy-start(bf16[256,2560]{1,0:T(8,128)(2,1)S(1)} %collective-permute-done.5.other_ref) | copy-start | bytes 3932164
  27.4 10.7 %collective-permute-start.6 = (bf16[640,256]{1,0:T(8,128)(2,1)S(1)}, bf16[640,256]{1,0:T(8,128)(2,1)}, u32[]{:S(2)}, u32[]{:S(2)}) collective-permute-start(bf16[640,256]{1,0:T(8,128)(2,1)S(1)} %collective-permute-done.refs_0_), channel_id=1, source_target_pairs={{0,4},{4,8},{8,12},{12,0},{1,5},{5,9},{9,13},{13,1},{2,6},{6,10},{... | collective-permute-start | bytes 983048 | tf_op jit(solution)/shard_map/ppermute | solution.py:302
  27.4 10.6 %collective-permute-start.7 = (bf16[640,256]{1,0:T(8,128)(2,1)S(1)}, bf16[640,256]{1,0:T(8,128)(2,1)S(1)}, u32[]{:S(2)}, u32[]{:S(2)}) collective-permute-start(bf16[640,256]{1,0:T(8,128)(2,1)S(1)} %collective-permute-done.4.refs_4_), channel_id=1, source_target_pairs={{0,2},{2,0},{1,3},{3,1},{4,6},{6,4},{5,7},{7,5},{8,10},{10,8},{9,1... | collective-permute-start | bytes 983048 | tf_op jit(solution)/shard_map/ppermute | solution.py:297
  28.0 10.8 %collective-permute-start.8 = (bf16[640,256]{1,0:T(8,128)(2,1)S(1)}, bf16[640,256]{1,0:T(8,128)(2,1)}, u32[]{:S(2)}, u32[]{:S(2)}) collective-permute-start(bf16[640,256]{1,0:T(8,128)(2,1)S(1)} %collective-permute-done.4.refs_4_), channel_id=1, source_target_pairs={{0,16},{16,0},{1,17},{17,1},{2,18},{18,2},{3,19},{19,3},{4,20},{20... | collective-permute-start | bytes 983048 | tf_op jit(solution)/shard_map/ppermute | solution.py:297
  30.4 42.9 %copy-start.21 = (bf16[2,256]{1,0:T(2,128)(2,1)S(1)}, bf16[2,256]{1,0:T(2,128)(2,1)}, u32[]{:S(2)}) copy-start(bf16[2,256]{1,0:T(2,128)(2,1)} %param.11) | copy-start | bytes 3076
  38.8 48.8 %all-to-all-start = ((bf16[8,640,128]{2,1,0:T(8,128)(2,1)}), bf16[8,640,128]{2,1,0:T(8,128)(2,1)S(1)}, u32[]{:S(2)}, u32[]{:S(2)}) async-start(bf16[8,640,128]{2,1,0:T(8,128)(2,1)} %copy-done.3), calls=%async_computation | async-start | bytes 2621440 | tf_op jit(solution)/shard_map/all_to_all | solution.py:367
  42.5 10.7 %collective-permute-start.11 = (bf16[640,256]{1,0:T(8,128)(2,1)S(1)}, bf16[640,256]{1,0:T(8,128)(2,1)S(1)}, u32[]{:S(2)}, u32[]{:S(2)}) collective-permute-start(bf16[640,256]{1,0:T(8,128)(2,1)S(1)} %collective-permute-done.2.refs_1_), channel_id=1, source_target_pairs={{0,16},{16,0},{1,17},{17,1},{2,18},{18,2},{3,19},{19,3},{4,20},{20... | collective-permute-start | bytes 983048 | tf_op jit(solution)/shard_map/ppermute | solution.py:297
  43.6 13.7 %collective-permute-start.10 = (bf16[640,256]{1,0:T(8,128)(2,1)}, bf16[640,256]{1,0:T(8,128)(2,1)S(1)}, u32[]{:S(2)}, u32[]{:S(2)}) collective-permute-start(bf16[640,256]{1,0:T(8,128)(2,1)} %collective-permute-done.6.p0), channel_id=1, source_target_pairs={{0,16},{16,0},{1,17},{17,1},{2,18},{18,2},{3,19},{19,3},{4,20},{20... | collective-permute-start | bytes 983048 | tf_op jit(solution)/shard_map/ppermute | solution.py:297
  44.6 21.9 %collective-permute-start.12 = (bf16[640,256]{1,0:T(8,128)(2,1)}, bf16[640,256]{1,0:T(8,128)(2,1)S(1)}, u32[]{:S(2)}, u32[]{:S(2)}) collective-permute-start(bf16[640,256]{1,0:T(8,128)(2,1)} %collective-permute-done.8.refs_6_), channel_id=1, source_target_pairs={{0,2},{2,0},{1,3},{3,1},{4,6},{6,4},{5,7},{7,5},{8,10},{10,8},{9,1... | collective-permute-start | bytes 983048 | tf_op jit(solution)/shard_map/ppermute | solution.py:297
  46.6 24.8 %collective-permute-start.9 = (bf16[640,256]{1,0:T(8,128)(2,1)}, bf16[640,256]{1,0:T(8,128)(2,1)S(1)}, u32[]{:S(2)}, u32[]{:S(2)}) collective-permute-start(bf16[640,256]{1,0:T(8,128)(2,1)} %collective-permute-done.6.p0), channel_id=1, source_target_pairs={{0,2},{2,0},{1,3},{3,1},{4,6},{6,4},{5,7},{7,5},{8,10},{10,8},{9,1... | collective-permute-start | bytes 983048 | tf_op jit(solution)/shard_map/ppermute | solution.py:297
  71.3 10.2 %collective-permute-start.13 = (bf16[640,256]{1,0:T(8,128)(2,1)S(1)}, bf16[640,256]{1,0:T(8,128)(2,1)S(1)}, u32[]{:S(2)}, u32[]{:S(2)}) collective-permute-start(bf16[640,256]{1,0:T(8,128)(2,1)S(1)} %collective-permute-done.9.p1), channel_id=1, source_target_pairs={{0,16},{16,0},{1,17},{17,1},{2,18},{18,2},{3,19},{19,3},{4,20},{20... | collective-permute-start | bytes 983048 | tf_op jit(solution)/shard_map/ppermute | solution.py:297
  73.5 1.3 %copy-start.1 = (bf16[256,2560]{1,0:T(8,128)(2,1)S(1)}, bf16[256,2560]{1,0:T(8,128)(2,1)}, u32[]{:S(2)}) copy-start(bf16[256,2560]{1,0:T(8,128)(2,1)} %copy-done) | copy-start | bytes 3932164
  79.0 2.5 %copy-start.5 = (bf16[256,1280]{1,0:T(8,128)(2,1)S(1)}, bf16[256,1280]{1,0:T(8,128)(2,1)}, u32[]{:S(2)}) copy-start(bf16[256,1280]{1,0:T(8,128)(2,1)} %queries_ref.1) | copy-start | bytes 1966084
  79.0 2.5 %copy-start.6 = (bf16[256,1280]{1,0:T(8,128)(2,1)S(1)}, bf16[256,1280]{1,0:T(8,128)(2,1)}, u32[]{:S(2)}) copy-start(bf16[256,1280]{1,0:T(8,128)(2,1)} %cotangent_ref.1) | copy-start | bytes 1966084
  87.6 30.4 %collective-permute-start.14 = (bf16[8,640,128]{2,1,0:T(8,128)(2,1)S(1)}, bf16[8,640,128]{2,1,0:T(8,128)(2,1)S(1)}, u32[]{:S(2)}, u32[]{:S(2)}) collective-permute-start(bf16[8,640,128]{2,1,0:T(8,128)(2,1)S(1)} %all-to-all-done.refs_1_.refs_2_.refs_3_.refs_4_.refs_5_.refs_6_), channel_id=1, source_target_pairs={{0,1},{1,0},{2,3},{3,2},{4,5},{5,4},{6,7},{7,6},{8,9},{9,8},{10,11... | collective-permute-start | bytes 3932168 | tf_op jit(solution)/shard_map/ppermute | solution.py:297
  87.6 10.5 %collective-permute-start.15 = (bf16[256,512]{1,0:T(8,128)(2,1)S(1)}, bf16[256,512]{1,0:T(8,128)(2,1)S(1)}, u32[]{:S(2)}, u32[]{:S(2)}) collective-permute-start(bf16[256,512]{1,0:T(8,128)(2,1)S(1)} %get-tuple-element.55.refs_13_), channel_id=1, source_target_pairs={{0,4},{4,8},{8,12},{12,0},{1,5},{5,9},{9,13},{13,1},{2,6},{6,10},{... | collective-permute-start | bytes 786440 | tf_op jit(solution)/shard_map/ppermute | solution.py:302
  89.1 9.0 %collective-permute-start.16 = (bf16[256,512]{1,0:T(8,128)(2,1)S(1)}, bf16[256,512]{1,0:T(8,128)(2,1)S(1)}, u32[]{:S(2)}, u32[]{:S(2)}) collective-permute-start(bf16[256,512]{1,0:T(8,128)(2,1)S(1)} %get-tuple-element.55.refs_13_), channel_id=1, source_target_pairs={{0,2},{2,0},{1,3},{3,1},{4,6},{6,4},{5,7},{7,5},{8,10},{10,8},{9,1... | collective-permute-start | bytes 786440 | tf_op jit(solution)/shard_map/ppermute | solution.py:297
  98.1 7.9 %collective-permute-start.17 = (bf16[256,512]{1,0:T(8,128)(2,1)S(1)}, bf16[256,512]{1,0:T(8,128)(2,1)S(1)}, u32[]{:S(2)}, u32[]{:S(2)}) collective-permute-start(bf16[256,512]{1,0:T(8,128)(2,1)S(1)} %get-tuple-element.55.refs_13_), channel_id=1, source_target_pairs={{0,12},{4,0},{8,4},{12,8},{1,13},{5,1},{9,5},{13,9},{2,14},{6,2},{... | collective-permute-start | bytes 786440 | tf_op jit(solution)/shard_map/ppermute | solution.py:302
  99.9 7.4 %collective-permute-start.18 = (bf16[256,512]{1,0:T(8,128)(2,1)S(1)}, bf16[256,512]{1,0:T(8,128)(2,1)S(1)}, u32[]{:S(2)}, u32[]{:S(2)}) collective-permute-start(bf16[256,512]{1,0:T(8,128)(2,1)S(1)} %collective-permute-done.15.refs_15_), channel_id=1, source_target_pairs={{0,2},{2,0},{1,3},{3,1},{4,6},{6,4},{5,7},{7,5},{8,10},{10,8},{9,1... | collective-permute-start | bytes 786440 | tf_op jit(solution)/shard_map/ppermute | solution.py:297
  108.0 8.4 %collective-permute-start.19 = (bf16[256,512]{1,0:T(8,128)(2,1)S(1)}, bf16[256,512]{1,0:T(8,128)(2,1)}, u32[]{:S(2)}, u32[]{:S(2)}) collective-permute-start(bf16[256,512]{1,0:T(8,128)(2,1)S(1)} %collective-permute-done.15.refs_15_), channel_id=1, source_target_pairs={{0,4},{4,8},{8,12},{12,0},{1,5},{5,9},{9,13},{13,1},{2,6},{6,10},{... | collective-permute-start | bytes 786440 | tf_op jit(solution)/shard_map/ppermute | solution.py:302
  108.5 7.9 %collective-permute-start.20 = (bf16[256,512]{1,0:T(8,128)(2,1)S(1)}, bf16[256,512]{1,0:T(8,128)(2,1)S(1)}, u32[]{:S(2)}, u32[]{:S(2)}) collective-permute-start(bf16[256,512]{1,0:T(8,128)(2,1)S(1)} %collective-permute-done.17.refs_16_), channel_id=1, source_target_pairs={{0,2},{2,0},{1,3},{3,1},{4,6},{6,4},{5,7},{7,5},{8,10},{10,8},{9,1... | collective-permute-start | bytes 786440 | tf_op jit(solution)/shard_map/ppermute | solution.py:297
  117.1 6.7 %collective-permute-start.21 = (bf16[256,512]{1,0:T(8,128)(2,1)}, bf16[256,512]{1,0:T(8,128)(2,1)}, u32[]{:S(2)}, u32[]{:S(2)}) collective-permute-start(bf16[256,512]{1,0:T(8,128)(2,1)} %collective-permute-done.19.refs_5_), channel_id=1, source_target_pairs={{0,2},{2,0},{1,3},{3,1},{4,6},{6,4},{5,7},{7,5},{8,10},{10,8},{9,1... | collective-permute-start | bytes 786440 | tf_op jit(solution)/shard_map/ppermute | solution.py:297
  (13 other events, 11.8 us)

commit v7 on v6

--- a/solution.py
+++ b/solution.py
@@ -13,7 +13,7 @@
 EPSILON = 1e-06
 ROPE_BASE = 1000000.0
 SCALE = HEAD ** (-0.5)
-VMEM_BYTES = 24 * 1024 * 1024
+VMEM_BYTES = 16 * 1024 * 1024
 IN_VMEM = pl.BlockSpec(memory_space=pltpu.VMEM)
 
 
@@ -64,43 +64,48 @@
     return lax.rem(lax.axis_index("blk") + (blocks - distance), blocks)
 
 
-def project_kernel(distances, own_ref, other_ref, weight_ref, *refs):
+def project_kernel(distances, first, own_ref, other_ref, *refs):
     sums_ref = refs[-1]
-    group, replica = lax.axis_index("groups"), lax.axis_index("dp")
-    half_rows = weight_ref.shape[1] // 2
-    here = lax.axis_index("blk")
-    first = features_of(own_ref, other_ref, here, 0, half_rows)
-    second = features_of(own_ref, other_ref, here, half_rows, half_rows)
-    totals = [
-        product(first, weight_ref[j, :half_rows]) + product(second, weight_ref[j, half_rows:])
-        for j in (group, 1 - group)
-    ]
+    group = lax.axis_index("groups")
+    if first:
+        weight_ref = refs[0]
+        half_rows = weight_ref.shape[1] // 2
+        here = lax.axis_index("blk")
+        early = features_of(own_ref, other_ref, here, 0, half_rows)
+        late = features_of(own_ref, other_ref, here, half_rows, half_rows)
+        totals = [
+            product(early, weight_ref[j, :half_rows]) + product(late, weight_ref[j, half_rows:])
+            for j in (group, 1 - group)
+        ]
+    else:
+        totals = [refs[0][group], refs[0][1 - group]]
     for at, distance in enumerate(distances):
-        pieces = refs[4 * at : 4 * at + 4]
+        pieces = refs[1 + 4 * at : 5 + 4 * at]
         terms = block_terms(own_ref, other_ref, block_from(distance), pieces)
         totals = [total + term for total, term in zip(totals, terms)]
     sums_ref[group] = totals[0]
     sums_ref[1 - group] = totals[1]
 
 
-def project(normed, normed_other, kv_weight, gathered):
+def project(normed, normed_other, start, gathered, first):
     length = normed.shape[0]
-    _, rows, columns = kv_weight.shape
+    columns = start.shape[2]
     distances = tuple(distance for distance, _ in gathered)
     pieces = [piece for _, four in gathered for piece in four]
+    rows = 2 * pieces[0].shape[0]
     return pl.pallas_call(
-        functools.partial(project_kernel, distances),
+        functools.partial(project_kernel, distances, first),
         in_specs=[IN_VMEM] * (3 + len(pieces)),
         out_specs=IN_VMEM,
         out_shape=jax.ShapeDtypeStruct((2, length, columns), jnp.float32),
         compiler_params=pltpu.CompilerParams(vmem_limit_bytes=VMEM_BYTES),
         cost_estimate=pl.CostEstimate(
-            flops=4 * length * rows * columns * (1 + len(distances)),
-            bytes_accessed=7000000,
+            flops=4 * length * rows * columns * (first + len(distances)),
+            bytes_accessed=5000000,
             transcendentals=0,
         ),
         name="project",
-    )(normed, normed_other, kv_weight, *pieces)
+    )(normed, normed_other, start, *pieces)
 
 
 def attention_body(raw_of, cosine, sine, queries_ref, cotangent_ref, grad_query_ref, pair_ref):
@@ -244,53 +249,46 @@
     )(at, *([own] * count), *([other] * count), *pairs, *(sums or ()))
 
 
-def norm_kernel(values_ref, scale_ref, gain_ref, normed_ref):
-    wide_values = values_ref[...].astype(jnp.float32)
-    normed_ref[...] = (wide_values * scale_ref[...] * gain_ref[...]).astype(jnp.bfloat16)
-
-
-def norm(activations, scale, gain):
+def norm_kernel(own_ref, other_ref, gain_ref, normed_ref, normed_other_ref, slabs_ref):
+    core = lax.axis_index("sub")
+    features = own_ref.shape[1]
+    sequences, share, tokens = slabs_ref.shape
+    half = sequences // 2
+    square_sum = jnp.zeros((own_ref.shape[0], 1), jnp.float32)
+    for ref in (own_ref, other_ref):
+        wide_values = ref[...].astype(jnp.float32)
+        square_sum += jnp.sum(wide_values * wide_values, -1, keepdims=True)
+    scale = lax.rsqrt(square_sum / (2 * features) + EPSILON)
+    mine = pl.ds(pl.multiple_of(core * tokens, 16), tokens)
+    for ref, out_ref, which in (
+        (own_ref, normed_ref, core),
+        (other_ref, normed_other_ref, 1 - core),
+    ):
+        for at in range(half):
+            place = slice(at * share, (at + 1) * share)
+            start = pl.multiple_of(which * features + at * share, 128)
+            gain = gain_ref[:, pl.ds(start, share)].astype(jnp.float32)
+            wide_values = ref[:, place].astype(jnp.float32) * scale * gain
+            out_ref[:, place] = wide_values.astype(jnp.bfloat16)
+            taken = out_ref[mine, place].astype(jnp.float32)
+            slabs_ref[which * half + at] = taken.T.astype(jnp.bfloat16)
+
+
+def norm(activations, activations_other, norm_gain, sequences):
     length, features = activations.shape
+    share = 2 * features // sequences
     return pl.pallas_call(
         norm_kernel,
         in_specs=[IN_VMEM] * 3,
-        out_specs=IN_VMEM,
-        out_shape=jax.ShapeDtypeStruct(activations.shape, jnp.bfloat16),
+        out_specs=[IN_VMEM] * 3,
+        out_shape=[jax.ShapeDtypeStruct(activations.shape, jnp.bfloat16)] * 2
+        + [jax.ShapeDtypeStruct((sequences, share, length // 2), jnp.bfloat16)],
         compiler_params=pltpu.CompilerParams(vmem_limit_bytes=VMEM_BYTES),
         cost_estimate=pl.CostEstimate(
-            flops=4 * length * features, bytes_accessed=4 * length * features, transcendentals=0
+            flops=16 * length * features, bytes_accessed=10 * length * features, transcendentals=0
         ),
         name="norm",
-    )(activations, scale, gain)
-
-
-def slabs_kernel(own_ref, other_ref, slabs_ref):
-    sequences, share, tokens = slabs_ref.shape
-    core = lax.axis_index("sub")
-    mine = pl.ds(pl.multiple_of(core * tokens, 16), tokens)
-    for half in range(2):
-        for at in range(sequences // 2):
-            place = slice(at * share, (at + 1) * share)
-            values = jnp.where(core == half, own_ref[mine, place], other_ref[mine, place])
-            slabs_ref[half * (sequences // 2) + at] = values.astype(jnp.float32).T.astype(
-                jnp.bfloat16
-            )
-
-
-def make_slabs(normed, normed_other, sequences):
-    length, features = normed.shape
-    share = 2 * features // sequences
-    return pl.pallas_call(
-        slabs_kernel,
-        in_specs=[IN_VMEM] * 2,
-        out_specs=IN_VMEM,
-        out_shape=jax.ShapeDtypeStruct((sequences, share, length // 2), jnp.bfloat16),
-        compiler_params=pltpu.CompilerParams(vmem_limit_bytes=VMEM_BYTES),
-        cost_estimate=pl.CostEstimate(
-            flops=4 * length * features, bytes_accessed=6 * length * features, transcendentals=0
-        ),
-        name="make_slabs",
-    )(normed, normed_other)
+    )(activations, activations_other, norm_gain[None, :])
 
 
 def swapped(block, axis):
@@ -321,16 +319,6 @@
     return lax.ppermute(slab, ("blk", "dp", "sub"), slab_route(turn))
 
 
-def scale_and_gain(activations, norm_gain):
-    core = lax.axis_index("sub")
-    features = activations.shape[1]
-    wide_values = activations.astype(jnp.float32)
-    square_sum = jnp.sum(wide_values * wide_values, -1, keepdims=True)
-    square_sum = square_sum + swapped(square_sum, "sub")
-    gain = lax.dynamic_slice_in_dim(norm_gain, core * features, features, 0).astype(jnp.float32)
-    return lax.rsqrt(square_sum / (2 * features) + EPSILON), gain
-
-
 def local(activations, norm_gain, queries, cotangent, kv_weight, kv_bias):
     blocks, replicas = lax.axis_size("blk"), lax.axis_size("dp")
     group, block, replica = lax.axis_index("groups"), lax.axis_index("blk"), lax.axis_index("dp")
@@ -340,38 +328,41 @@
     share = block_rows // replicas
 
     piece = lax.dynamic_slice(kv_weight, (group, replica * share, 0), (1, share, columns))[0]
-    scale, gain = scale_and_gain(activations, norm_gain)
     cosine, sine = rope_tables(length)
     bias = kv_bias.astype(jnp.float32)
 
     if not (blocks == 4 and replicas == 2):
         return general(
-            piece, activations, scale, gain, bias, cosine, sine, queries, cotangent
+            piece, activations, norm_gain, bias, cosine, sine, queries, cotangent
         )
 
     up = turned(piece, "blk", 1)
-    normed = norm(activations, scale, gain[None, :])
-    up, piece, normed = lax.optimization_barrier((up, piece, normed))
+    activations_other = swapped(activations, "sub")
+    up, piece = lax.optimization_barrier((up, piece))
     up_x, up_y, down = swapped(up, "dp"), swapped(up, "groups"), turned(piece, "blk", -1)
-    normed_other = swapped(normed, "sub")
-    up, up_x, up_y, down, normed_other = lax.optimization_barrier(
-        (up, up_x, up_y, down, normed_other)
+    normed, normed_other, slabs = norm(
+        activations, activations_other, norm_gain, blocks * replicas
+    )
+    up, up_x, up_y, down, normed, normed_other, slabs = lax.optimization_barrier(
+        (up, up_x, up_y, down, normed, normed_other, slabs)
     )
     down_x, down_y = swapped(down, "dp"), swapped(down, "groups")
     twice = turned(up, "blk", 1)
-    up_both = swapped(up_x, "groups")
-    slabs = make_slabs(normed, normed_other, blocks * replicas)
-    twice, down_x, down_y, slabs = lax.optimization_barrier((twice, down_x, down_y, slabs))
+    up_both = swapped(up_y, "dp")
+    twice, down_x, down_y = lax.optimization_barrier((twice, down_x, down_y))
     twice_x, twice_y = swapped(twice, "dp"), swapped(twice, "groups")
-    down_both = swapped(down_y, "dp")
-    slabs = lax.all_to_all(slabs, ("blk", "dp"), 0, 0)
-    twice_x, twice_y, up_both, down_both = lax.optimization_barrier(
-        (twice_x, twice_y, up_both, down_both)
+    down_both = swapped(down_x, "groups")
+    slabs = lax.all_to_all(after(slabs, twice, up_both), ("blk", "dp"), 0, 0)
+    sums = project(
+        normed, normed_other, kv_weight, [(1, (up, up_x, up_y, up_both))], True
+    )
+    twice_x, twice_y, down_both, sums = lax.optimization_barrier(
+        (twice_x, twice_y, down_both, sums)
     )
     twice_both = swapped(twice_x, "groups")
-
-    gathered = [(1, (up, up_x, up_y, up_both)), (-1, (down, down_x, down_y, down_both))]
-    sums = project(normed, normed_other, kv_weight, gathered)
+    sums = project(
+        normed, normed_other, sums, [(-1, (down, down_x, down_y, down_both))], False
+    )
     grad_query, grad_pair = attention(
         2, normed, normed_other, (twice, twice_x, twice_y, twice_both), sums, bias, cosine, sine,
         queries, cotangent,
@@ -418,14 +409,19 @@
     )
 
 
-def general(piece, activations, scale, gain, bias, cosine, sine, queries, cotangent):
+def general(piece, activations, norm_gain, bias, cosine, sine, queries, cotangent):
     core = lax.axis_index("sub")
     blocks, replicas = lax.axis_size("blk"), lax.axis_size("dp")
     length, features = activations.shape
     share, columns = piece.shape
     half = blocks * replicas // 2
     number = lax.axis_index("blk") * replicas + lax.axis_index("dp")
-    normed = (activations.astype(jnp.float32) * scale * gain).astype(jnp.bfloat16)
+    wide_values = activations.astype(jnp.float32)
+    square_sum = jnp.sum(wide_values * wide_values, -1, keepdims=True)
+    square_sum = square_sum + swapped(square_sum, "sub")
+    scale = lax.rsqrt(square_sum / (2 * features) + EPSILON)
+    gain = lax.dynamic_slice_in_dim(norm_gain, core * features, features, 0).astype(jnp.float32)
+    normed = (wide_values * scale * gain).astype(jnp.bfloat16)
     normed_other = swapped(normed, "sub")
     weight = lax.all_gather(piece, ("groups", "blk", "dp"), axis=0, tiled=True)
     weight = weight.reshape(2, -1, columns)

time: 128 us -> 123 us (0.961)
  waiting for transfers between devices: 70.2 us -> 55.4 us
  starting transfers between devices: 24.2 us -> 30.6 us
  local copies, waits for them, and re-layouts: 14.5 us -> 19.7 us
  other arithmetic: 2.47 us -> 0.73 us
    ppermute x16 -> x15, waiting for transfers between devices: 34.2 us -> 24.7 us  [swapped(): return lax.ppermute(block, axis, [(0, 1), (1, 0)])]
    ppermute x6, waiting for transfers between devices: 36 us -> 30.8 us  [turned(): lax.ppermute(block, axis, [(i, (i + distance) % size) for i in range(size)])]
    unnamed x44 -> x48, local copies, waits for them, and re-layouts: 13.1 us -> 17.9 us
    ppermute x16 -> x15, starting transfers between devices: 11.9 us -> 14.6 us  [swapped(): return lax.ppermute(block, axis, [(0, 1), (1, 0)])]
    ppermute x6, starting transfers between devices: 8.61 us -> 10.6 us  [turned(): lax.ppermute(block, axis, [(i, (i + distance) % size) for i in range(size)])]
    all_to_all x1, starting transfers between devices: 3.72 us -> 5.38 us  [local(): slabs = lax.all_to_all(after(slabs, twice, up_both), ('blk', 'dp'), 0, 0)]
    reduce_sum x1 -> x0, other arithmetic: 1.65 us -> none  [scale_and_gain(): square_sum = jnp.sum(wide_values * wide_values, -1, keepdims=True)]
    pallas_call x3, Pallas kernels: 3.28 us -> 4.68 us  [the longest x2 2.66 us: project(): pl.pallas_call(functools.partial(project_kernel, distances, first), in_sp...]
  transfers between devices with their start and end apart: 23 -> 22, of which waited for: 15 -> 14; matrix products, arithmetic and copies ran while one was open for 2% -> 2% of each run, Pallas kernels for 9% -> 10%
where the time goes in v7:
time: 123 us; the launch traced here: 122 us
  waiting for transfers between devices  55.4 us (45%)
  starting transfers between devices  30.6 us (25%)
  local copies, waits for them, and re-layouts  19.7 us (16%)
  Pallas kernels  15.3 us (12%)
    ppermute x6, waiting for transfers between devices, turned(): lax.ppermute(block, axis, [(i, (i + distance) % size) for i in range(size)])  30.8 us
    ppermute x15, waiting for transfers between devices, swapped(): return lax.ppermute(block, axis, [(0, 1), (1, 0)])  24.7 us
    unnamed x48, local copies, waits for them, and re-layouts  17.9 us
    ppermute x15, starting transfers between devices, swapped(): return lax.ppermute(block, axis, [(0, 1), (1, 0)])  14.6 us
    ppermute x6, starting transfers between devices, turned(): lax.ppermute(block, axis, [(i, (i + distance) % size) for i in range(size)])  10.6 us
    pallas_call x2, Pallas kernels, gradient(): pl.pallas_call(functools.partial(gradient_kernel, count, sums is None), g...  5.53 us
    all_to_all x1, starting transfers between devices, local(): slabs = lax.all_to_all(after(slabs, twice, up_both), ('blk', 'dp'), 0, 0)  5.38 us
    pallas_call x1, Pallas kernels, attention(): pl.pallas_call(functools.partial(attention_kernel, distance), in_specs=[I...  5.07 us
  transfers between devices with their start and end apart: 22, of which 14 were waited for; matrix products, arithmetic and copies ran while one was open for 2% of the time, Pallas kernels for 10%

profile of v7, /device:TPU:0, one launch (start us, length us, event | category | flops | bytes accessed | tf_op | source)
XLA Modules:
  0.0 122.5 jit_solution(5825976660873128501)
XLA Ops:
  2.1 2.7 %collective-permute-start = (bf16[640,256]{1,0:T(8,128)(2,1)S(1)}, bf16[640,256]{1,0:T(8,128)(2,1)S(1)}, u32[]{:S(2)}, u32[]{:S(2)}) collective-permute-start(bf16[640,256]{1,0:T(8,128)(2,1)S(1)} %dynamic-slice_bitcast_fusion), channel_id=1, source_target_pairs={{0,4},{4,8},{8,12},{12,0},{1,5},{5,9},{9,13},{13,1},{2,6},{6,10},{... | collective-permute-start | bytes 983048 | tf_op jit(solution)/shard_map/ppermute | solution.py:300
  4.8 10.4 %collective-permute-done.refs_1_ = bf16[640,256]{1,0:T(8,128)(2,1)S(1)} collective-permute-done((bf16[640,256]{1,0:T(8,128)(2,1)S(1)}, bf16[640,256]{1,0:T(8,128)(2,1)S(1)}, u32[]{:S(2)}, u32[]{:S(2)}) %collective-permute-start) | collective-permute-done | bytes 327712 | tf_op jit(solution)/shard_map/ppermute | solution.py:300
  15.2 1.7 %collective-permute-start.3 = (bf16[640,256]{1,0:T(8,128)(2,1)S(1)}, bf16[640,256]{1,0:T(8,128)(2,1)S(1)}, u32[]{:S(2)}, u32[]{:S(2)}) collective-permute-start(bf16[640,256]{1,0:T(8,128)(2,1)S(1)} %dynamic-slice_bitcast_fusion), channel_id=1, source_target_pairs={{0,12},{4,0},{8,4},{12,8},{1,13},{5,1},{9,5},{13,9},{2,14},{6,2},{... | collective-permute-start | bytes 983048 | tf_op jit(solution)/shard_map/ppermute | solution.py:300
  16.9 1.5 %collective-permute-start.2 = (bf16[640,256]{1,0:T(8,128)(2,1)S(1)}, bf16[640,256]{1,0:T(8,128)(2,1)S(1)}, u32[]{:S(2)}, u32[]{:S(2)}) collective-permute-start(bf16[640,256]{1,0:T(8,128)(2,1)S(1)} %collective-permute-done.refs_1_), channel_id=1, source_target_pairs={{0,16},{16,0},{1,17},{17,1},{2,18},{18,2},{3,19},{19,3},{4,20},{20... | collective-permute-start | bytes 983048 | tf_op jit(solution)/shard_map/ppermute | solution.py:295
  18.4 1.5 %collective-permute-start.1 = (bf16[640,256]{1,0:T(8,128)(2,1)S(1)}, bf16[640,256]{1,0:T(8,128)(2,1)S(1)}, u32[]{:S(2)}, u32[]{:S(2)}) collective-permute-start(bf16[640,256]{1,0:T(8,128)(2,1)S(1)} %collective-permute-done.refs_1_), channel_id=1, source_target_pairs={{0,2},{2,0},{1,3},{3,1},{4,6},{6,4},{5,7},{7,5},{8,10},{10,8},{9,1... | collective-permute-start | bytes 983048 | tf_op jit(solution)/shard_map/ppermute | solution.py:295
  20.7 1.3 %copy-done.3 = bf16[256,2560]{1,0:T(8,128)(2,1)S(1)} copy-done((bf16[256,2560]{1,0:T(8,128)(2,1)S(1)}, bf16[256,2560]{1,0:T(8,128)(2,1)}, u32[]{:S(2)}) %copy-start.3) | copy-done | bytes 1310744
  22.0 2.0 %norm.1 = (bf16[256,2560]{1,0:T(8,128)(2,1)S(1)}, bf16[256,2560]{1,0:T(8,128)(2,1)S(1)}, bf16[8,640,128]{2,1,0:T(8,128)(2,1)S(1)}) custom-call(bf16[256,2560]{1,0:T(8,128)(2,1)S(1)} %copy-done.3, bf16[256,2560]{1,0:T(8,128)(2,1)S(1)} %collective-permute-done.4.other_ref, bf16[1,5120]{1,0:T(2,128)(2,1)S(1)} %broadcast_in_dim.2.gain_ref), custom_call_target="tpu_custom_call" | custom-call | flops 10485760 | bytes 6553600 | tf_op jit(solution)/shard_map/norm/pallas_call | solution.py:280
  28.9 1.4 %collective-permute-start.6 = (bf16[640,256]{1,0:T(8,128)(2,1)S(1)}, bf16[640,256]{1,0:T(8,128)(2,1)}, u32[]{:S(2)}, u32[]{:S(2)}) collective-permute-start(bf16[640,256]{1,0:T(8,128)(2,1)S(1)} %collective-permute-done.3.refs_1_), channel_id=1, source_target_pairs={{0,2},{2,0},{1,3},{3,1},{4,6},{6,4},{5,7},{7,5},{8,10},{10,8},{9,1... | collective-permute-start | bytes 983048 | tf_op jit(solution)/shard_map/ppermute | solution.py:295
  31.7 5.9 %collective-permute-done.5.p0 = bf16[640,256]{1,0:T(8,128)(2,1)S(1)} collective-permute-done((bf16[640,256]{1,0:T(8,128)(2,1)S(1)}, bf16[640,256]{1,0:T(8,128)(2,1)S(1)}, u32[]{:S(2)}, u32[]{:S(2)}) %collective-permute-start.5) | collective-permute-done | bytes 327712 | tf_op jit(solution)/shard_map/ppermute | solution.py:300
  38.3 1.4 %collective-permute-done.6.refs_2_ = bf16[640,256]{1,0:T(8,128)(2,1)} collective-permute-done((bf16[640,256]{1,0:T(8,128)(2,1)S(1)}, bf16[640,256]{1,0:T(8,128)(2,1)}, u32[]{:S(2)}, u32[]{:S(2)}) %collective-permute-start.6) | collective-permute-done | bytes 327712 | tf_op jit(solution)/shard_map/ppermute | solution.py:295
  39.7 3.7 %collective-permute-done.11.refs_4_ = bf16[640,256]{1,0:T(8,128)(2,1)S(1)} collective-permute-done((bf16[640,256]{1,0:T(8,128)(2,1)S(1)}, bf16[640,256]{1,0:T(8,128)(2,1)S(1)}, u32[]{:S(2)}, u32[]{:S(2)}) %collective-permute-start.11) | collective-permute-done | bytes 327712 | tf_op jit(solution)/shard_map/ppermute | solution.py:295
  44.2 5.4 %all-to-all-start = ((bf16[8,640,128]{2,1,0:T(8,128)(2,1)}), bf16[8,640,128]{2,1,0:T(8,128)(2,1)S(1)}, u32[]{:S(2)}, u32[]{:S(2)}) async-start(bf16[8,640,128]{2,1,0:T(8,128)(2,1)} %copy-done.4), calls=%async_computation | async-start | bytes 2621440 | tf_op jit(solution)/shard_map/all_to_all | solution.py:355
  49.5 1.5 %collective-permute-start.10 = (bf16[640,256]{1,0:T(8,128)(2,1)}, bf16[640,256]{1,0:T(8,128)(2,1)S(1)}, u32[]{:S(2)}, u32[]{:S(2)}) collective-permute-start(bf16[640,256]{1,0:T(8,128)(2,1)} %collective-permute-done.6.refs_2_), channel_id=1, source_target_pairs={{0,16},{16,0},{1,17},{17,1},{2,18},{18,2},{3,19},{19,3},{4,20},{20... | collective-permute-start | bytes 983048 | tf_op jit(solution)/shard_map/ppermute | solution.py:295
  51.6 2.0 %collective-permute-start.8 = (bf16[640,256]{1,0:T(8,128)(2,1)S(1)}, bf16[640,256]{1,0:T(8,128)(2,1)S(1)}, u32[]{:S(2)}, u32[]{:S(2)}) collective-permute-start(bf16[640,256]{1,0:T(8,128)(2,1)S(1)} %collective-permute-done.5.p0), channel_id=1, source_target_pairs={{0,2},{2,0},{1,3},{3,1},{4,6},{6,4},{5,7},{7,5},{8,10},{10,8},{9,1... | collective-permute-start | bytes 983048 | tf_op jit(solution)/shard_map/ppermute | solution.py:295
  53.6 1.3 %copy-done.1 = bf16[256,2560]{1,0:T(8,128)(2,1)S(1)} copy-done((bf16[256,2560]{1,0:T(8,128)(2,1)S(1)}, bf16[256,2560]{1,0:T(8,128)(2,1)}, u32[]{:S(2)}) %copy-start.1) | copy-done | bytes 1310744
  54.9 1.3 %copy-done.2 = bf16[2,1280,256]{2,1,0:T(8,128)(2,1)S(1)} copy-done((bf16[2,1280,256]{2,1,0:T(8,128)(2,1)S(1)}, bf16[2,1280,256]{2,1,0:T(8,128)(2,1)}, u32[]{:S(2)}) %copy-start.2) | copy-done | bytes 1310744
  61.2 1.7 %collective-permute-done.9.p2 = bf16[640,256]{1,0:T(8,128)(2,1)S(1)} collective-permute-done((bf16[640,256]{1,0:T(8,128)(2,1)S(1)}, bf16[640,256]{1,0:T(8,128)(2,1)S(1)}, u32[]{:S(2)}, u32[]{:S(2)}) %collective-permute-start.9) | collective-permute-done | bytes 327712 | tf_op jit(solution)/shard_map/ppermute | solution.py:295
  62.9 5.3 %collective-permute-done.8.p1 = bf16[640,256]{1,0:T(8,128)(2,1)S(1)} collective-permute-done((bf16[640,256]{1,0:T(8,128)(2,1)S(1)}, bf16[640,256]{1,0:T(8,128)(2,1)S(1)}, u32[]{:S(2)}, u32[]{:S(2)}) %collective-permute-start.8) | collective-permute-done | bytes 327712 | tf_op jit(solution)/shard_map/ppermute | solution.py:295
  68.2 1.4 %collective-permute-start.12 = (bf16[640,256]{1,0:T(8,128)(2,1)S(1)}, bf16[640,256]{1,0:T(8,128)(2,1)S(1)}, u32[]{:S(2)}, u32[]{:S(2)}) collective-permute-start(bf16[640,256]{1,0:T(8,128)(2,1)S(1)} %collective-permute-done.8.p1), channel_id=1, source_target_pairs={{0,16},{16,0},{1,17},{17,1},{2,18},{18,2},{3,19},{19,3},{4,20},{20... | collective-permute-start | bytes 983048 | tf_op jit(solution)/shard_map/ppermute | solution.py:295
  70.2 1.7 %project.3.sums_ref = f32[2,256,256]{2,1,0:T(8,128)S(1)} custom-call(bf16[256,2560]{1,0:T(8,128)(2,1)S(1)} %get-tuple-element.44.own_ref, bf16[256,2560]{1,0:T(8,128)(2,1)S(1)} %copy-done.1, f32[2,256,256]{2,1,0:T(8,128)S(1)} %project.2.refs_0_, bf16[640,256]{1,0:T(8,128)(2,1)S(1)} %collective-permute-done.3.refs_1_, ...), custom_call_target="tpu_custom_call" | custom-call | flops 335544320 | bytes 5000000 | tf_op jit(solution)/shard_map/project/pallas_call | solution.py:96
  71.9 3.3 %collective-permute-done.12.p3 = bf16[640,256]{1,0:T(8,128)(2,1)S(1)} collective-permute-done((bf16[640,256]{1,0:T(8,128)(2,1)S(1)}, bf16[640,256]{1,0:T(8,128)(2,1)S(1)}, u32[]{:S(2)}, u32[]{:S(2)}) %collective-permute-start.12) | collective-permute-done | bytes 327712 | tf_op jit(solution)/shard_map/ppermute | solution.py:295
  75.2 5.1 %attention.1 = (bf16[256,1280]{1,0:T(8,128)(2,1)}, bf16[256,512]{1,0:T(8,128)(2,1)S(1)}) custom-call(bf16[256,2560]{1,0:T(8,128)(2,1)S(1)} %get-tuple-element.44.own_ref, bf16[256,2560]{1,0:T(8,128)(2,1)S(1)} %copy-done.1, bf16[640,256]{1,0:T(8,128)(2,1)S(1)} %collective-permute-done.5.p0, bf16[640,256]{1,0:T(8,128)(2,1)S(1)} %collective-permute-done.8.p1, ...), custom_call_target="tpu_custom_call" | custom-call | flops 838860800 | bytes 5000000 | tf_op jit(solution)/shard_map/attention/pallas_call | solution.py:170
  80.6 3.3 %collective-permute-start.14 = (bf16[256,512]{1,0:T(8,128)(2,1)S(1)}, bf16[256,512]{1,0:T(8,128)(2,1)S(1)}, u32[]{:S(2)}, u32[]{:S(2)}) collective-permute-start(bf16[256,512]{1,0:T(8,128)(2,1)S(1)} %get-tuple-element.63.refs_13_), channel_id=1, source_target_pairs={{0,4},{4,8},{8,12},{12,0},{1,5},{5,9},{9,13},{13,1},{2,6},{6,10},{... | collective-permute-start | bytes 786440 | tf_op jit(solution)/shard_map/ppermute | solution.py:300
  83.9 5.1 %collective-permute-done.15.refs_14_ = bf16[256,512]{1,0:T(8,128)(2,1)S(1)} collective-permute-done((bf16[256,512]{1,0:T(8,128)(2,1)S(1)}, bf16[256,512]{1,0:T(8,128)(2,1)S(1)}, u32[]{:S(2)}, u32[]{:S(2)}) %collective-permute-start.15) | collective-permute-done | bytes 262176 | tf_op jit(solution)/shard_map/ppermute | solution.py:295
  89.0 3.3 %collective-permute-done.14.refs_15_ = bf16[256,512]{1,0:T(8,128)(2,1)S(1)} collective-permute-done((bf16[256,512]{1,0:T(8,128)(2,1)S(1)}, bf16[256,512]{1,0:T(8,128)(2,1)S(1)}, u32[]{:S(2)}, u32[]{:S(2)}) %collective-permute-start.14) | collective-permute-done | bytes 262176 | tf_op jit(solution)/shard_map/ppermute | solution.py:300
  92.3 2.5 %collective-permute-start.16 = (bf16[256,512]{1,0:T(8,128)(2,1)S(1)}, bf16[256,512]{1,0:T(8,128)(2,1)S(1)}, u32[]{:S(2)}, u32[]{:S(2)}) collective-permute-start(bf16[256,512]{1,0:T(8,128)(2,1)S(1)} %get-tuple-element.63.refs_13_), channel_id=1, source_target_pairs={{0,12},{4,0},{8,4},{12,8},{1,13},{5,1},{9,5},{13,9},{2,14},{6,2},{... | collective-permute-start | bytes 786440 | tf_op jit(solution)/shard_map/ppermute | solution.py:300
  95.8 4.6 %collective-permute-done.16.refs_16_ = bf16[256,512]{1,0:T(8,128)(2,1)S(1)} collective-permute-done((bf16[256,512]{1,0:T(8,128)(2,1)S(1)}, bf16[256,512]{1,0:T(8,128)(2,1)S(1)}, u32[]{:S(2)}, u32[]{:S(2)}) %collective-permute-start.16) | collective-permute-done | bytes 262176 | tf_op jit(solution)/shard_map/ppermute | solution.py:300
  100.4 2.1 %collective-permute-done.17.refs_17_ = bf16[256,512]{1,0:T(8,128)(2,1)S(1)} collective-permute-done((bf16[256,512]{1,0:T(8,128)(2,1)S(1)}, bf16[256,512]{1,0:T(8,128)(2,1)S(1)}, u32[]{:S(2)}, u32[]{:S(2)}) %collective-permute-start.17) | collective-permute-done | bytes 262176 | tf_op jit(solution)/shard_map/ppermute | solution.py:295
  103.2 1.3 %collective-permute-start.19 = (bf16[256,512]{1,0:T(8,128)(2,1)S(1)}, bf16[256,512]{1,0:T(8,128)(2,1)S(1)}, u32[]{:S(2)}, u32[]{:S(2)}) collective-permute-start(bf16[256,512]{1,0:T(8,128)(2,1)S(1)} %collective-permute-done.16.refs_16_), channel_id=1, source_target_pairs={{0,2},{2,0},{1,3},{3,1},{4,6},{6,4},{5,7},{7,5},{8,10},{10,8},{9,1... | collective-permute-start | bytes 786440 | tf_op jit(solution)/shard_map/ppermute | solution.py:295
  105.2 6.6 %collective-permute-done.18.refs_5_ = bf16[256,512]{1,0:T(8,128)(2,1)} collective-permute-done((bf16[256,512]{1,0:T(8,128)(2,1)S(1)}, bf16[256,512]{1,0:T(8,128)(2,1)}, u32[]{:S(2)}, u32[]{:S(2)}) %collective-permute-start.18) | collective-permute-done | bytes 262176 | tf_op jit(solution)/shard_map/ppermute | solution.py:300
  115.9 2.3 %gradient.2 = (f32[2,640,256]{2,1,0:T(8,128)S(1)}, f32[2,256]{1,0:T(2,128)S(1)}) custom-call(s32[6]{0:T(128)S(1)} %stack.39.refs_0_, bf16[8,640,128]{2,1,0:T(8,128)(2,1)S(1)} %all-to-all-done.refs_1_.refs_2_.refs_3_.refs_4_.refs_5_.refs_6_, bf16[8,640,128]{2,1,0:T(8,128)(2,1)S(1)} %all-to-all-done.refs_1_.refs_2_.refs_3_.refs_4_.refs_5_.refs_6_, ...), custom_call_target="tpu_custom_call" | custom-call | flops 1006632960 | bytes 5000000 | tf_op jit(solution)/shard_map/gradient/pallas_call | solution.py:232
  119.2 3.3 %gradient.3 = (f32[2,640,256]{2,1,0:T(8,128)}, f32[2,256]{1,0:T(2,128)}) custom-call(s32[2]{0:T(128)S(1)} %pad_add_fusion.refs_0_, bf16[8,640,128]{2,1,0:T(8,128)(2,1)S(1)} %all-to-all-done.refs_1_.refs_2_.refs_3_.refs_4_.refs_5_.refs_6_, bf16[8,640,128]{2,1,0:T(8,128)(2,1)S(1)} %all-to-all-done.refs_1_.refs_2_.refs_3_.refs_4_.refs_5_.refs_6_, ...), custom_call_target="tpu_custom_call" | custom-call | flops 335544320 | bytes 5000000 | tf_op jit(solution)/shard_map/gradient/pallas_call | solution.py:232
  (74 shorter events, 24.0 us)
Async XLA Ops:
  0.6 20.0 %collective-permute-start.4 = (bf16[256,2560]{1,0:T(8,128)(2,1)}, bf16[256,2560]{1,0:T(8,128)(2,1)S(1)}, u32[]{:S(2)}, u32[]{:S(2)}) collective-permute-start(bf16[256,2560]{1,0:T(8,128)(2,1)} %own_ref.1), channel_id=1, source_target_pairs={{0,1},{1,0},{2,3},{3,2},{4,5},{5,4},{6,7},{7,6},{8,9},{9,8},{10,11... | collective-permute-start | bytes 3932168 | tf_op jit(solution)/shard_map/ppermute | solution.py:295
  2.1 13.0 %collective-permute-start = (bf16[640,256]{1,0:T(8,128)(2,1)S(1)}, bf16[640,256]{1,0:T(8,128)(2,1)S(1)}, u32[]{:S(2)}, u32[]{:S(2)}) collective-permute-start(bf16[640,256]{1,0:T(8,128)(2,1)S(1)} %dynamic-slice_bitcast_fusion), channel_id=1, source_target_pairs={{0,4},{4,8},{8,12},{12,0},{1,5},{5,9},{9,13},{13,1},{2,6},{6,10},{... | collective-permute-start | bytes 983048 | tf_op jit(solution)/shard_map/ppermute | solution.py:300
  15.2 12.7 %copy-start.7 = (bf16[640,256]{1,0:T(8,128)(2,1)}, bf16[640,256]{1,0:T(8,128)(2,1)S(1)}, u32[]{:S(2)}) copy-start(bf16[640,256]{1,0:T(8,128)(2,1)S(1)} %collective-permute-done.refs_1_) | copy-start | bytes 983044
  15.2 11.0 %collective-permute-start.3 = (bf16[640,256]{1,0:T(8,128)(2,1)S(1)}, bf16[640,256]{1,0:T(8,128)(2,1)S(1)}, u32[]{:S(2)}, u32[]{:S(2)}) collective-permute-start(bf16[640,256]{1,0:T(8,128)(2,1)S(1)} %dynamic-slice_bitcast_fusion), channel_id=1, source_target_pairs={{0,12},{4,0},{8,4},{12,8},{1,13},{5,1},{9,5},{13,9},{2,14},{6,2},{... | collective-permute-start | bytes 983048 | tf_op jit(solution)/shard_map/ppermute | solution.py:300
  16.9 9.2 %collective-permute-start.2 = (bf16[640,256]{1,0:T(8,128)(2,1)S(1)}, bf16[640,256]{1,0:T(8,128)(2,1)S(1)}, u32[]{:S(2)}, u32[]{:S(2)}) collective-permute-start(bf16[640,256]{1,0:T(8,128)(2,1)S(1)} %collective-permute-done.refs_1_), channel_id=1, source_target_pairs={{0,16},{16,0},{1,17},{17,1},{2,18},{18,2},{3,19},{19,3},{4,20},{20... | collective-permute-start | bytes 983048 | tf_op jit(solution)/shard_map/ppermute | solution.py:295
  18.4 8.7 %collective-permute-start.1 = (bf16[640,256]{1,0:T(8,128)(2,1)S(1)}, bf16[640,256]{1,0:T(8,128)(2,1)S(1)}, u32[]{:S(2)}, u32[]{:S(2)}) collective-permute-start(bf16[640,256]{1,0:T(8,128)(2,1)S(1)} %collective-permute-done.refs_1_), channel_id=1, source_target_pairs={{0,2},{2,0},{1,3},{3,1},{4,6},{6,4},{5,7},{7,5},{8,10},{10,8},{9,1... | collective-permute-start | bytes 983048 | tf_op jit(solution)/shard_map/ppermute | solution.py:295
  20.7 1.3 %copy-start.3 = (bf16[256,2560]{1,0:T(8,128)(2,1)S(1)}, bf16[256,2560]{1,0:T(8,128)(2,1)}, u32[]{:S(2)}) copy-start(bf16[256,2560]{1,0:T(8,128)(2,1)} %own_ref.1) | copy-start | bytes 3932164
  24.0 1.1 copy-start
  25.1 1.1 copy-start.4
  27.9 25.7 %copy-start.23 = (bf16[2,256]{1,0:T(2,128)(2,1)S(1)}, bf16[2,256]{1,0:T(2,128)(2,1)}, u32[]{:S(2)}) copy-start(bf16[2,256]{1,0:T(2,128)(2,1)} %param.11) | copy-start | bytes 3076
  27.9 9.6 %collective-permute-start.5 = (bf16[640,256]{1,0:T(8,128)(2,1)S(1)}, bf16[640,256]{1,0:T(8,128)(2,1)S(1)}, u32[]{:S(2)}, u32[]{:S(2)}) collective-permute-start(bf16[640,256]{1,0:T(8,128)(2,1)S(1)} %collective-permute-done.refs_1_), channel_id=1, source_target_pairs={{0,4},{4,8},{8,12},{12,0},{1,5},{5,9},{9,13},{13,1},{2,6},{6,10},{... | collective-permute-start | bytes 983048 | tf_op jit(solution)/shard_map/ppermute | solution.py:300
  28.3 9.3 %collective-permute-start.7 = (bf16[640,256]{1,0:T(8,128)(2,1)S(1)}, bf16[640,256]{1,0:T(8,128)(2,1)S(1)}, u32[]{:S(2)}, u32[]{:S(2)}) collective-permute-start(bf16[640,256]{1,0:T(8,128)(2,1)S(1)} %collective-permute-done.3.refs_1_), channel_id=1, source_target_pairs={{0,16},{16,0},{1,17},{17,1},{2,18},{18,2},{3,19},{19,3},{4,20},{20... | collective-permute-start | bytes 983048 | tf_op jit(solution)/shard_map/ppermute | solution.py:295
  28.9 10.8 %collective-permute-start.6 = (bf16[640,256]{1,0:T(8,128)(2,1)S(1)}, bf16[640,256]{1,0:T(8,128)(2,1)}, u32[]{:S(2)}, u32[]{:S(2)}) collective-permute-start(bf16[640,256]{1,0:T(8,128)(2,1)S(1)} %collective-permute-done.3.refs_1_), channel_id=1, source_target_pairs={{0,2},{2,0},{1,3},{3,1},{4,6},{6,4},{5,7},{7,5},{8,10},{10,8},{9,1... | collective-permute-start | bytes 983048 | tf_op jit(solution)/shard_map/ppermute | solution.py:295
  30.3 13.1 %collective-permute-start.11 = (bf16[640,256]{1,0:T(8,128)(2,1)S(1)}, bf16[640,256]{1,0:T(8,128)(2,1)S(1)}, u32[]{:S(2)}, u32[]{:S(2)}) collective-permute-start(bf16[640,256]{1,0:T(8,128)(2,1)S(1)} %collective-permute-done.2.refs_3_), channel_id=1, source_target_pairs={{0,2},{2,0},{1,3},{3,1},{4,6},{6,4},{5,7},{7,5},{8,10},{10,8},{9,1... | collective-permute-start | bytes 983048 | tf_op jit(solution)/shard_map/ppermute | solution.py:295
  44.2 36.1 %all-to-all-start = ((bf16[8,640,128]{2,1,0:T(8,128)(2,1)}), bf16[8,640,128]{2,1,0:T(8,128)(2,1)S(1)}, u32[]{:S(2)}, u32[]{:S(2)}) async-start(bf16[8,640,128]{2,1,0:T(8,128)(2,1)} %copy-done.4), calls=%async_computation | async-start | bytes 2621440 | tf_op jit(solution)/shard_map/all_to_all | solution.py:355
  49.5 11.6 %collective-permute-start.10 = (bf16[640,256]{1,0:T(8,128)(2,1)}, bf16[640,256]{1,0:T(8,128)(2,1)S(1)}, u32[]{:S(2)}, u32[]{:S(2)}) collective-permute-start(bf16[640,256]{1,0:T(8,128)(2,1)} %collective-permute-done.6.refs_2_), channel_id=1, source_target_pairs={{0,16},{16,0},{1,17},{17,1},{2,18},{18,2},{3,19},{19,3},{4,20},{20... | collective-permute-start | bytes 983048 | tf_op jit(solution)/shard_map/ppermute | solution.py:295
  51.0 11.9 %collective-permute-start.9 = (bf16[640,256]{1,0:T(8,128)(2,1)S(1)}, bf16[640,256]{1,0:T(8,128)(2,1)S(1)}, u32[]{:S(2)}, u32[]{:S(2)}) collective-permute-start(bf16[640,256]{1,0:T(8,128)(2,1)S(1)} %collective-permute-done.5.p0), channel_id=1, source_target_pairs={{0,16},{16,0},{1,17},{17,1},{2,18},{18,2},{3,19},{19,3},{4,20},{20... | collective-permute-start | bytes 983048 | tf_op jit(solution)/shard_map/ppermute | solution.py:295
  51.6 16.6 %collective-permute-start.8 = (bf16[640,256]{1,0:T(8,128)(2,1)S(1)}, bf16[640,256]{1,0:T(8,128)(2,1)S(1)}, u32[]{:S(2)}, u32[]{:S(2)}) collective-permute-start(bf16[640,256]{1,0:T(8,128)(2,1)S(1)} %collective-permute-done.5.p0), channel_id=1, source_target_pairs={{0,2},{2,0},{1,3},{3,1},{4,6},{6,4},{5,7},{7,5},{8,10},{10,8},{9,1... | collective-permute-start | bytes 983048 | tf_op jit(solution)/shard_map/ppermute | solution.py:295
  53.6 1.3 %copy-start.1 = (bf16[256,2560]{1,0:T(8,128)(2,1)S(1)}, bf16[256,2560]{1,0:T(8,128)(2,1)}, u32[]{:S(2)}) copy-start(bf16[256,2560]{1,0:T(8,128)(2,1)} %copy-done) | copy-start | bytes 3932164
  54.9 1.3 %copy-start.2 = (bf16[2,1280,256]{2,1,0:T(8,128)(2,1)S(1)}, bf16[2,1280,256]{2,1,0:T(8,128)(2,1)}, u32[]{:S(2)}) copy-start(bf16[2,1280,256]{2,1,0:T(8,128)(2,1)} %refs_0_.1) | copy-start | bytes 3932164
  60.1 10.1 %copy-start.14 = (bf16[640,256]{1,0:T(8,128)(2,1)S(1)}, bf16[640,256]{1,0:T(8,128)(2,1)}, u32[]{:S(2)}) copy-start(bf16[640,256]{1,0:T(8,128)(2,1)} %copy-done.13) | copy-start | bytes 983044
  68.2 7.1 %collective-permute-start.12 = (bf16[640,256]{1,0:T(8,128)(2,1)S(1)}, bf16[640,256]{1,0:T(8,128)(2,1)S(1)}, u32[]{:S(2)}, u32[]{:S(2)}) collective-permute-start(bf16[640,256]{1,0:T(8,128)(2,1)S(1)} %collective-permute-done.8.p1), channel_id=1, source_target_pairs={{0,16},{16,0},{1,17},{17,1},{2,18},{18,2},{3,19},{19,3},{4,20},{20... | collective-permute-start | bytes 983048 | tf_op jit(solution)/shard_map/ppermute | solution.py:295
  70.2 5.0 %copy-start.5 = (bf16[256,1280]{1,0:T(8,128)(2,1)S(1)}, bf16[256,1280]{1,0:T(8,128)(2,1)}, u32[]{:S(2)}) copy-start(bf16[256,1280]{1,0:T(8,128)(2,1)} %queries_ref.1) | copy-start | bytes 1966084
  70.2 5.0 %copy-start.6 = (bf16[256,1280]{1,0:T(8,128)(2,1)S(1)}, bf16[256,1280]{1,0:T(8,128)(2,1)}, u32[]{:S(2)}) copy-start(bf16[256,1280]{1,0:T(8,128)(2,1)} %cotangent_ref.1) | copy-start | bytes 1966084
  80.3 32.7 %collective-permute-start.13 = (bf16[8,640,128]{2,1,0:T(8,128)(2,1)S(1)}, bf16[8,640,128]{2,1,0:T(8,128)(2,1)S(1)}, u32[]{:S(2)}, u32[]{:S(2)}) collective-permute-start(bf16[8,640,128]{2,1,0:T(8,128)(2,1)S(1)} %all-to-all-done.refs_1_.refs_2_.refs_3_.refs_4_.refs_5_.refs_6_), channel_id=1, source_target_pairs={{0,1},{1,0},{2,3},{3,2},{4,5},{5,4},{6,7},{7,6},{8,9},{9,8},{10,11... | collective-permute-start | bytes 3932168 | tf_op jit(solution)/shard_map/ppermute | solution.py:295
  80.3 8.7 %collective-permute-start.15 = (bf16[256,512]{1,0:T(8,128)(2,1)S(1)}, bf16[256,512]{1,0:T(8,128)(2,1)S(1)}, u32[]{:S(2)}, u32[]{:S(2)}) collective-permute-start(bf16[256,512]{1,0:T(8,128)(2,1)S(1)} %get-tuple-element.63.refs_13_), channel_id=1, source_target_pairs={{0,2},{2,0},{1,3},{3,1},{4,6},{6,4},{5,7},{7,5},{8,10},{10,8},{9,1... | collective-permute-start | bytes 786440 | tf_op jit(solution)/shard_map/ppermute | solution.py:295
  80.6 11.7 %collective-permute-start.14 = (bf16[256,512]{1,0:T(8,128)(2,1)S(1)}, bf16[256,512]{1,0:T(8,128)(2,1)S(1)}, u32[]{:S(2)}, u32[]{:S(2)}) collective-permute-start(bf16[256,512]{1,0:T(8,128)(2,1)S(1)} %get-tuple-element.63.refs_13_), channel_id=1, source_target_pairs={{0,4},{4,8},{8,12},{12,0},{1,5},{5,9},{9,13},{13,1},{2,6},{6,10},{... | collective-permute-start | bytes 786440 | tf_op jit(solution)/shard_map/ppermute | solution.py:300
  92.3 8.1 %collective-permute-start.16 = (bf16[256,512]{1,0:T(8,128)(2,1)S(1)}, bf16[256,512]{1,0:T(8,128)(2,1)S(1)}, u32[]{:S(2)}, u32[]{:S(2)}) collective-permute-start(bf16[256,512]{1,0:T(8,128)(2,1)S(1)} %get-tuple-element.63.refs_13_), channel_id=1, source_target_pairs={{0,12},{4,0},{8,4},{12,8},{1,13},{5,1},{9,5},{13,9},{2,14},{6,2},{... | collective-permute-start | bytes 786440 | tf_op jit(solution)/shard_map/ppermute | solution.py:300
  94.8 7.7 %collective-permute-start.17 = (bf16[256,512]{1,0:T(8,128)(2,1)S(1)}, bf16[256,512]{1,0:T(8,128)(2,1)S(1)}, u32[]{:S(2)}, u32[]{:S(2)}) collective-permute-start(bf16[256,512]{1,0:T(8,128)(2,1)S(1)} %collective-permute-done.14.refs_15_), channel_id=1, source_target_pairs={{0,2},{2,0},{1,3},{3,1},{4,6},{6,4},{5,7},{7,5},{8,10},{10,8},{9,1... | collective-permute-start | bytes 786440 | tf_op jit(solution)/shard_map/ppermute | solution.py:295
  103.2 8.6 %collective-permute-start.18 = (bf16[256,512]{1,0:T(8,128)(2,1)S(1)}, bf16[256,512]{1,0:T(8,128)(2,1)}, u32[]{:S(2)}, u32[]{:S(2)}) collective-permute-start(bf16[256,512]{1,0:T(8,128)(2,1)S(1)} %collective-permute-done.14.refs_15_), channel_id=1, source_target_pairs={{0,4},{4,8},{8,12},{12,0},{1,5},{5,9},{9,13},{13,1},{2,6},{6,10},{... | collective-permute-start | bytes 786440 | tf_op jit(solution)/shard_map/ppermute | solution.py:300
  103.2 8.6 %collective-permute-start.19 = (bf16[256,512]{1,0:T(8,128)(2,1)S(1)}, bf16[256,512]{1,0:T(8,128)(2,1)S(1)}, u32[]{:S(2)}, u32[]{:S(2)}) collective-permute-start(bf16[256,512]{1,0:T(8,128)(2,1)S(1)} %collective-permute-done.16.refs_16_), channel_id=1, source_target_pairs={{0,2},{2,0},{1,3},{3,1},{4,6},{6,4},{5,7},{7,5},{8,10},{10,8},{9,1... | collective-permute-start | bytes 786440 | tf_op jit(solution)/shard_map/ppermute | solution.py:295
  112.5 6.7 %collective-permute-start.20 = (bf16[256,512]{1,0:T(8,128)(2,1)}, bf16[256,512]{1,0:T(8,128)(2,1)}, u32[]{:S(2)}, u32[]{:S(2)}) collective-permute-start(bf16[256,512]{1,0:T(8,128)(2,1)} %collective-permute-done.18.refs_5_), channel_id=1, source_target_pairs={{0,2},{2,0},{1,3},{3,1},{4,6},{6,4},{5,7},{7,5},{8,10},{10,8},{9,1... | collective-permute-start | bytes 786440 | tf_op jit(solution)/shard_map/ppermute | solution.py:295
  (14 other events, 11.8 us)

commit v8 on v7

--- a/solution.py
+++ b/solution.py
@@ -15,6 +15,7 @@
 SCALE = HEAD ** (-0.5)
 VMEM_BYTES = 16 * 1024 * 1024
 IN_VMEM = pl.BlockSpec(memory_space=pltpu.VMEM)
+IN_HBM = pl.BlockSpec(memory_space=pltpu.HBM)
 
 
 def rope_tables(length):
@@ -30,6 +31,10 @@
     )
 
 
+def kept(*blocks):
+    return [pltpu.with_memory_space_constraint(block, pltpu.HBM) for block in blocks]
+
+
 def product(left, right):
     return jnp.dot(left, right, preferred_element_type=jnp.float32)
 
@@ -40,19 +45,37 @@
     )
 
 
-def features_of(own_ref, other_ref, block, offset, rows):
-    blocks_held = own_ref.shape[1] // (2 * rows)
-    here = block // blocks_held == lax.axis_index("sub")
-    start = pl.multiple_of((block % blocks_held) * (2 * rows) + offset, 128)
-    place = pl.ds(start, rows)
-    return jnp.where(here, own_ref[:, place], other_ref[:, place])
-
-
-def block_terms(own_ref, other_ref, block, pieces):
+def fetch_features(own_ref, other_ref, block, held_ref, sem):
+    rows = held_ref.shape[1]
+    blocks_held = own_ref.shape[1] // rows
+    place = pl.ds(pl.multiple_of(lax.rem(block, blocks_held) * rows, 128), rows)
+    here = lax.div(block, blocks_held) == lax.axis_index("sub")
+
+    @pl.when(here)
+    def _():
+        pltpu.make_async_copy(own_ref.at[:, place], held_ref, sem).start()
+
+    @pl.when(jnp.logical_not(here))
+    def _():
+        pltpu.make_async_copy(other_ref.at[:, place], held_ref, sem).start()
+
+    return pltpu.make_async_copy(own_ref.at[:, place], held_ref, sem)
+
+
+def fetch_all(sources, held, sems):
+    copies = [
+        pltpu.make_async_copy(source, held.at[at], sems.at[at]) for at, source in enumerate(sources)
+    ]
+    for copy in copies:
+        copy.start()
+    return copies
+
+
+def block_terms(values_ref, pieces):
     replica = lax.axis_index("dp")
     rows = pieces[0].shape[0]
-    near = features_of(own_ref, other_ref, block, replica * rows, rows)
-    far = features_of(own_ref, other_ref, block, (1 - replica) * rows, rows)
+    near = values_ref[:, pl.ds(pl.multiple_of(replica * rows, 128), rows)]
+    far = values_ref[:, pl.ds(pl.multiple_of((1 - replica) * rows, 128), rows)]
     return (
         product(near, pieces[0][...]) + product(far, pieces[1][...]),
         product(near, pieces[2][...]) + product(far, pieces[3][...]),
@@ -64,48 +87,64 @@
     return lax.rem(lax.axis_index("blk") + (blocks - distance), blocks)
 
 
-def project_kernel(distances, first, own_ref, other_ref, *refs):
-    sums_ref = refs[-1]
+def project_kernel(distance, first, own_ref, other_ref, start_ref, *refs):
+    pieces, sums_ref = refs[:4], refs[4]
+    values, held, sem, sems = refs[5:9]
     group = lax.axis_index("groups")
+    copies = [fetch_features(own_ref, other_ref, block_from(distance), values, sem)]
+    copies += fetch_all(pieces, held, sems)
     if first:
-        weight_ref = refs[0]
-        half_rows = weight_ref.shape[1] // 2
-        here = lax.axis_index("blk")
-        early = features_of(own_ref, other_ref, here, 0, half_rows)
-        late = features_of(own_ref, other_ref, here, half_rows, half_rows)
-        totals = [
-            product(early, weight_ref[j, :half_rows]) + product(late, weight_ref[j, half_rows:])
-            for j in (group, 1 - group)
+        own_values, own_weight, own_sems = refs[9:]
+        more = [
+            fetch_features(own_ref, other_ref, block_from(0), own_values, own_sems.at[0]),
+            pltpu.make_async_copy(start_ref, own_weight, own_sems.at[1]),
         ]
+        more[1].start()
+        for copy in more:
+            copy.wait()
+        totals = [product(own_values[...], own_weight[j]) for j in (group, 1 - group)]
     else:
-        totals = [refs[0][group], refs[0][1 - group]]
-    for at, distance in enumerate(distances):
-        pieces = refs[1 + 4 * at : 5 + 4 * at]
-        terms = block_terms(own_ref, other_ref, block_from(distance), pieces)
-        totals = [total + term for total, term in zip(totals, terms)]
-    sums_ref[group] = totals[0]
-    sums_ref[1 - group] = totals[1]
-
-
-def project(normed, normed_other, start, gathered, first):
+        totals = [start_ref[group], start_ref[1 - group]]
+    for copy in copies:
+        copy.wait()
+    terms = block_terms(values, [held.at[at] for at in range(4)])
+    sums_ref[group] = totals[0] + terms[0]
+    sums_ref[1 - group] = totals[1] + terms[1]
+
+
+def piece_scratch(length, rows, columns):
+    return [
+        pltpu.VMEM((length, 2 * rows), jnp.bfloat16),
+        pltpu.VMEM((4, rows, columns), jnp.bfloat16),
+        pltpu.SemaphoreType.DMA,
+        pltpu.SemaphoreType.DMA((4,)),
+    ]
+
+
+def project(normed, normed_other, start, distance, pieces, first):
     length = normed.shape[0]
-    columns = start.shape[2]
-    distances = tuple(distance for distance, _ in gathered)
-    pieces = [piece for _, four in gathered for piece in four]
-    rows = 2 * pieces[0].shape[0]
+    rows, columns = pieces[0].shape
+    scratch = piece_scratch(length, rows, columns)
+    if first:
+        scratch += [
+            pltpu.VMEM((length, 2 * rows), jnp.bfloat16),
+            pltpu.VMEM(start.shape, jnp.bfloat16),
+            pltpu.SemaphoreType.DMA((2,)),
+        ]
     return pl.pallas_call(
-        functools.partial(project_kernel, distances, first),
-        in_specs=[IN_VMEM] * (3 + len(pieces)),
+        functools.partial(project_kernel, distance, first),
+        in_specs=[IN_HBM] * 2 + [IN_HBM if first else IN_VMEM] + [IN_HBM] * 4,
         out_specs=IN_VMEM,
         out_shape=jax.ShapeDtypeStruct((2, length, columns), jnp.float32),
+        scratch_shapes=scratch,
         compiler_params=pltpu.CompilerParams(vmem_limit_bytes=VMEM_BYTES),
         cost_estimate=pl.CostEstimate(
-            flops=4 * length * rows * columns * (first + len(distances)),
-            bytes_accessed=5000000,
+            flops=8 * length * rows * columns * (first + 1),
+            bytes_accessed=4000000,
             transcendentals=0,
         ),
         name="project",
-    )(normed, normed_other, start, *pieces)
+    )(*kept(normed, normed_other), *(kept(start) if first else [start]), *kept(*pieces))
 
 
 def attention_body(raw_of, cosine, sine, queries_ref, cotangent_ref, grad_query_ref, pair_ref):
@@ -148,10 +187,11 @@
 
 def attention_kernel(
     distance, own_ref, other_ref, p0, p1, p2, p3, sums_ref, bias_ref, cosine_ref, sine_ref,
-    queries_ref, cotangent_ref, grad_query_ref, pair_ref, raw_ref,
+    queries_ref, cotangent_ref, grad_query_ref, pair_ref, raw_ref, values, sem,
 ):
     group = lax.axis_index("groups")
-    terms = block_terms(own_ref, other_ref, block_from(distance), (p0, p1, p2, p3))
+    fetch_features(own_ref, other_ref, block_from(distance), values, sem).wait()
+    terms = block_terms(values, (p0, p1, p2, p3))
     raw_ref[group] = sums_ref[group] + terms[0]
     raw_ref[1 - group] = sums_ref[1 - group] + terms[1]
 
@@ -165,13 +205,18 @@
 
 def attention(distance, normed, normed_other, pieces, sums, bias, cosine, sine, queries, cotangent):
     length = normed.shape[0]
-    columns = pieces[0].shape[1]
-    operands = (normed, normed_other, *pieces, sums, bias, cosine, sine, queries, cotangent)
+    rows, columns = pieces[0].shape
+    operands = kept(normed, normed_other)
+    operands += [*pieces, sums, bias, cosine, sine, queries, cotangent]
     return pl.pallas_call(
         functools.partial(attention_kernel, distance),
-        in_specs=[IN_VMEM] * len(operands),
+        in_specs=[IN_HBM] * 2 + [IN_VMEM] * (len(operands) - 2),
         out_specs=[IN_VMEM] * 2,
-        scratch_shapes=[pltpu.VMEM(sums.shape, jnp.float32)],
+        scratch_shapes=[
+            pltpu.VMEM(sums.shape, jnp.float32),
+            pltpu.VMEM((length, 2 * rows), jnp.bfloat16),
+            pltpu.SemaphoreType.DMA,
+        ],
         out_shape=[
             jax.ShapeDtypeStruct(queries.shape, jnp.bfloat16),
             jax.ShapeDtypeStruct((length, 2 * columns), jnp.bfloat16),
@@ -186,70 +231,79 @@
     )(*operands)
 
 
-def gradient_kernel(count, first, *refs):
-    own, other, pairs = (refs[1 + i * count : 1 + (i + 1) * count] for i in range(3))
-    refs = refs[1 + 3 * count :]
-    core = lax.axis_index("sub")
-    weight_ref, bias_ref = refs[-2:]
+def gradient_kernel(sources, first, own_ref, other_ref, *refs):
+    count = len(sources)
+    pairs, refs = refs[:count], refs[count:]
+    sums_refs, refs = ((), refs) if first else (refs[:2], refs[2:])
+    weight_ref, bias_ref, own, other, sems = refs[:5]
+    held = refs[5] if first else None
+    core, replica, replicas = lax.axis_index("sub"), lax.axis_index("dp"), lax.axis_size("dp")
     columns = weight_ref.shape[2]
-    total = None
-    for mine, others, pair in zip(own, other, pairs):
-        early = jnp.where(core == 0, mine[0], others[0])
-        late = jnp.where(core == 0, others[0], mine[0])
-        term = product(jnp.concatenate([early, late], 1), pair[...])
-        total = term if total is None else total + term
-    for j in range(2):
-        part = total[:, j * columns : (j + 1) * columns]
-        weight_ref[j] = part if first else refs[0][j] + part
-
-    @pl.when(pl.program_id(0) == 0)
-    def _():
-        total = None
-        for pair in pairs:
-            term = jnp.sum(pair[...].astype(jnp.float32), axis=0, keepdims=True)
-            total = term if total is None else total + term
+    slots = [
+        block_from(distance) * replicas + (replica if same else 1 - replica)
+        for distance, same in sources
+    ]
+    copies = []
+    for at, slot in enumerate(slots):
+        copies.append(
+            [
+                pltpu.make_async_copy(own_ref.at[slot], own.at[at], sems.at[0, at]),
+                pltpu.make_async_copy(other_ref.at[slot], other.at[at], sems.at[1, at]),
+            ]
+        )
+        if first:
+            copies[at].append(pltpu.make_async_copy(pairs[at], held.at[at], sems.at[2, at]))
+        for copy in copies[at]:
+            copy.start()
+    for at in range(count):
+        for copy in copies[at]:
+            copy.wait()
+        pair = held[at] if first else pairs[at][...]
+        early = jnp.where(core == 0, own[at], other[at])
+        late = jnp.where(core == 0, other[at], own[at])
+        term = product(jnp.concatenate([early, late], 1), pair)
+        bias_term = jnp.sum(pair.astype(jnp.float32), axis=0, keepdims=True)
         for j in range(2):
-            part = total[:, j * columns : (j + 1) * columns]
-            bias_ref[j : j + 1, :] = part if first else refs[1][j : j + 1, :] + part
-
-
-def gradient(at, own, other, pairs, sums):
+            lanes = slice(j * columns, (j + 1) * columns)
+            before, bias_before = (weight_ref[j], bias_ref[j : j + 1]) if at else (None, None)
+            if at == 0 and not first:
+                before, bias_before = sums_refs[0][j], sums_refs[1][j : j + 1]
+            if before is None:
+                weight_ref[j], bias_ref[j : j + 1] = term[:, lanes], bias_term[:, lanes]
+            else:
+                weight_ref[j] = before + term[:, lanes]
+                bias_ref[j : j + 1] = bias_before + bias_term[:, lanes]
+
+
+def gradient(own, other, some, sums):
     _, share, tokens = own.shape
-    length = pairs[0].shape[0]
-    columns = pairs[0].shape[1] // 2
+    pairs = list(some.values())
+    length, columns = pairs[0].shape[0], pairs[0].shape[1] // 2
     count = len(pairs)
-    tile = share // 2 if share % 32 == 0 else share
-
-    def slab_spec(turn):
-        return pl.BlockSpec((1, tile, tokens), lambda i, at: (at[turn], i, 0))
-
-    weight_spec = pl.BlockSpec((2, tile, columns), lambda i, at: (0, i, 0))
-    bias_spec = pl.BlockSpec((2, columns), lambda i, at: (0, 0))
-    in_specs = [slab_spec(turn) for turn in range(count)] * 2
-    in_specs += [pl.BlockSpec((length, 2 * columns), lambda i, at: (0, 0))] * count
-    if sums:
-        in_specs += [weight_spec, bias_spec]
     return pl.pallas_call(
-        functools.partial(gradient_kernel, count, sums is None),
-        grid_spec=pltpu.PrefetchScalarGridSpec(
-            num_scalar_prefetch=1,
-            grid=(share // tile,),
-            in_specs=in_specs,
-            out_specs=[weight_spec, bias_spec],
-        ),
+        functools.partial(gradient_kernel, tuple(some), sums is None),
+        in_specs=[IN_HBM] * 2 + [IN_VMEM if sums else IN_HBM] * count + [IN_VMEM] * len(sums or ()),
+        out_specs=[IN_VMEM] * 2,
         out_shape=[
             jax.ShapeDtypeStruct((2, share, columns), jnp.float32),
             jax.ShapeDtypeStruct((2, columns), jnp.float32),
         ],
+        scratch_shapes=[
+            pltpu.VMEM((count, share, tokens), jnp.bfloat16),
+            pltpu.VMEM((count, share, tokens), jnp.bfloat16),
+            pltpu.SemaphoreType.DMA((3, count)),
+        ]
+        + ([] if sums else [pltpu.VMEM((count, length, 2 * columns), jnp.bfloat16)]),
         compiler_params=pltpu.CompilerParams(vmem_limit_bytes=VMEM_BYTES),
         cost_estimate=pl.CostEstimate(
             flops=4 * count * length * share * columns, bytes_accessed=5000000, transcendentals=0
         ),
         name="gradient",
-    )(at, *([own] * count), *([other] * count), *pairs, *(sums or ()))
-
-
-def norm_kernel(own_ref, other_ref, gain_ref, normed_ref, normed_other_ref, slabs_ref):
+    )(*kept(own, other), *(pairs if sums else kept(*pairs)), *(sums or ()))
+
+
+def norm_kernel(own_ref, other_ref, gain_ref, *refs):
+    results, (normed_ref, normed_other_ref, slabs_ref, sems) = refs[:3], refs[3:]
     core = lax.axis_index("sub")
     features = own_ref.shape[1]
     sequences, share, tokens = slabs_ref.shape
@@ -272,17 +326,29 @@
             out_ref[:, place] = wide_values.astype(jnp.bfloat16)
             taken = out_ref[mine, place].astype(jnp.float32)
             slabs_ref[which * half + at] = taken.T.astype(jnp.bfloat16)
+    copies = [
+        pltpu.make_async_copy(ref, result, sems.at[at])
+        for at, (ref, result) in enumerate(
+            zip((normed_ref, normed_other_ref, slabs_ref), results)
+        )
+    ]
+    for copy in copies:
+        copy.start()
+    for copy in copies:
+        copy.wait()
 
 
 def norm(activations, activations_other, norm_gain, sequences):
     length, features = activations.shape
     share = 2 * features // sequences
+    shapes = [activations.shape] * 2 + [(sequences, share, length // 2)]
     return pl.pallas_call(
         norm_kernel,
         in_specs=[IN_VMEM] * 3,
-        out_specs=[IN_VMEM] * 3,
-        out_shape=[jax.ShapeDtypeStruct(activations.shape, jnp.bfloat16)] * 2
-        + [jax.ShapeDtypeStruct((sequences, share, length // 2), jnp.bfloat16)],
+        out_specs=[IN_HBM] * 3,
+        out_shape=[pltpu.HBM(shape, jnp.bfloat16) for shape in shapes],
+        scratch_shapes=[pltpu.VMEM(shape, jnp.bfloat16) for shape in shapes]
+        + [pltpu.SemaphoreType.DMA((3,))],
         compiler_params=pltpu.CompilerParams(vmem_limit_bytes=VMEM_BYTES),
         cost_estimate=pl.CostEstimate(
             flops=16 * length * features, bytes_accessed=10 * length * features, transcendentals=0
@@ -353,27 +419,24 @@
     twice_x, twice_y = swapped(twice, "dp"), swapped(twice, "groups")
     down_both = swapped(down_x, "groups")
     slabs = lax.all_to_all(after(slabs, twice, up_both), ("blk", "dp"), 0, 0)
-    sums = project(
-        normed, normed_other, kv_weight, [(1, (up, up_x, up_y, up_both))], True
-    )
+    sums = project(normed, normed_other, kv_weight, 1, (up, up_x, up_y, up_both), True)
     twice_x, twice_y, down_both, sums = lax.optimization_barrier(
         (twice_x, twice_y, down_both, sums)
     )
     twice_both = swapped(twice_x, "groups")
-    sums = project(
-        normed, normed_other, sums, [(-1, (down, down_x, down_y, down_both))], False
-    )
+    sums = project(normed, normed_other, sums, -1, (down, down_x, down_y, down_both), False)
     grad_query, grad_pair = attention(
         2, normed, normed_other, (twice, twice_x, twice_y, twice_both), sums, bias, cosine, sine,
         queries, cotangent,
     )
 
-    grad_pair, slabs = lax.optimization_barrier((grad_pair, slabs))
     pair_up, pair_x = turned(grad_pair, "blk", 1), swapped(grad_pair, "dp")
     pair_up, pair_x, grad_pair = lax.optimization_barrier((pair_up, pair_x, grad_pair))
     pair_down, pair_up_x = turned(grad_pair, "blk", -1), swapped(pair_up, "dp")
+    pair_down, pair_up_x, pair_up, slabs = lax.optimization_barrier(
+        (pair_down, pair_up_x, pair_up, slabs)
+    )
     slabs_other = swapped(slabs, "sub")
-    pair_down, pair_up_x, pair_up = lax.optimization_barrier((pair_down, pair_up_x, pair_up))
     pair_twice, pair_down_x = turned(pair_up, "blk", 1), swapped(pair_down, "dp")
     pair_twice, pair_down_x = lax.optimization_barrier((pair_twice, pair_down_x))
     pair_twice_x = swapped(pair_twice, "dp")
@@ -388,12 +451,7 @@
     last = {(2, True): pair_twice, (2, False): pair_twice_x}
     sums = None
     for some in (first, last):
-        at = [
-            (block - distance) % blocks * replicas + (replica if same else 1 - replica)
-            for distance, same in some
-        ]
-        at = jnp.stack(at).astype(jnp.int32)
-        sums = gradient(at, slabs, slabs_other, list(some.values()), sums)
+        sums = gradient(slabs, slabs_other, some, sums)
     grad_weight, grad_bias = sums
     return (grad_query, grad_weight, grad_bias)
 

time: 123 us -> 121 us (0.984)
  local copies, waits for them, and re-layouts: 19.7 us -> 4.86 us
  Pallas kernels: 15.3 us -> 21.1 us
  waiting for transfers between devices: 55.4 us -> 60.8 us
  starting transfers between devices: 30.6 us -> 32.1 us
    unnamed x48 -> x40, local copies, waits for them, and re-layouts: 17.9 us -> 3.16 us
    pallas_call x5, Pallas kernels: 10.2 us -> 14.9 us  [the longest x2 5.54 us: gradient(): pl.pallas_call(functools.partial(gradient_kernel, tuple(some), sums is No...]
    ppermute x15, waiting for transfers between devices: 24.7 us -> 28.8 us  [swapped(): return lax.ppermute(block, axis, [(0, 1), (1, 0)])]
  transfers between devices with their start and end apart: 22 -> 22, of which waited for: 14 -> 15; matrix products, arithmetic and copies ran while one was open for 2% -> 2% of each run, Pallas kernels for 10% -> 15%
where the time goes in v8:
time: 121 us; the launch traced here: 120 us
  waiting for transfers between devices  60.8 us (50%)
  starting transfers between devices  32.1 us (27%)
  Pallas kernels  21.1 us (17%)
  local copies, waits for them, and re-layouts  4.86 us (4%)
    ppermute x6, waiting for transfers between devices, turned(): lax.ppermute(block, axis, [(i, (i + distance) % size) for i in range(size)])  31.9 us
    ppermute x15, waiting for transfers between devices, swapped(): return lax.ppermute(block, axis, [(0, 1), (1, 0)])  28.8 us
    ppermute x15, starting transfers between devices, swapped(): return lax.ppermute(block, axis, [(0, 1), (1, 0)])  15.6 us
    ppermute x6, starting transfers between devices, turned(): lax.ppermute(block, axis, [(i, (i + distance) % size) for i in range(size)])  10.9 us
    pallas_call x1, Pallas kernels, attention(): pl.pallas_call(functools.partial(attention_kernel, distance), in_specs=[I...  6.17 us
    all_to_all x1, starting transfers between devices, local(): slabs = lax.all_to_all(after(slabs, twice, up_both), ('blk', 'dp'), 0, 0)  5.58 us
    pallas_call x2, Pallas kernels, gradient(): pl.pallas_call(functools.partial(gradient_kernel, tuple(some), sums is No...  5.54 us
    pallas_call x2, Pallas kernels, project(): pl.pallas_call(functools.partial(project_kernel, distance, first), in_spe...  5.43 us
  transfers between devices with their start and end apart: 22, of which 15 were waited for; matrix products, arithmetic and copies ran while one was open for 2% of the time, Pallas kernels for 15%

profile of v8, /device:TPU:0, one launch (start us, length us, event | category | flops | bytes accessed | tf_op | source)
XLA Modules:
  0.0 120.3 jit_solution(3870629048470856854)
XLA Ops:
  2.1 2.7 %collective-permute-start = (bf16[640,256]{1,0:T(8,128)(2,1)S(1)}, bf16[640,256]{1,0:T(8,128)(2,1)S(1)}, u32[]{:S(2)}, u32[]{:S(2)}) collective-permute-start(bf16[640,256]{1,0:T(8,128)(2,1)S(1)} %dynamic-slice_bitcast_fusion), channel_id=1, source_target_pairs={{0,4},{4,8},{8,12},{12,0},{1,5},{5,9},{9,13},{13,1},{2,6},{6,10},{... | collective-permute-start | bytes 983048 | tf_op jit(solution)/shard_map/ppermute | solution.py:366
  4.8 10.4 %collective-permute-done.refs_0_ = bf16[640,256]{1,0:T(8,128)(2,1)S(1)} collective-permute-done((bf16[640,256]{1,0:T(8,128)(2,1)S(1)}, bf16[640,256]{1,0:T(8,128)(2,1)S(1)}, u32[]{:S(2)}, u32[]{:S(2)}) %collective-permute-start) | collective-permute-done | bytes 327712 | tf_op jit(solution)/shard_map/ppermute | solution.py:366
  15.2 1.7 %collective-permute-start.3 = (bf16[640,256]{1,0:T(8,128)(2,1)S(1)}, bf16[640,256]{1,0:T(8,128)(2,1)S(1)}, u32[]{:S(2)}, u32[]{:S(2)}) collective-permute-start(bf16[640,256]{1,0:T(8,128)(2,1)S(1)} %dynamic-slice_bitcast_fusion), channel_id=1, source_target_pairs={{0,12},{4,0},{8,4},{12,8},{1,13},{5,1},{9,5},{13,9},{2,14},{6,2},{... | collective-permute-start | bytes 983048 | tf_op jit(solution)/shard_map/ppermute | solution.py:366
  16.9 1.5 %collective-permute-start.2 = (bf16[640,256]{1,0:T(8,128)(2,1)S(1)}, bf16[640,256]{1,0:T(8,128)(2,1)S(1)}, u32[]{:S(2)}, u32[]{:S(2)}) collective-permute-start(bf16[640,256]{1,0:T(8,128)(2,1)S(1)} %collective-permute-done.refs_0_), channel_id=1, source_target_pairs={{0,16},{16,0},{1,17},{17,1},{2,18},{18,2},{3,19},{19,3},{4,20},{20... | collective-permute-start | bytes 983048 | tf_op jit(solution)/shard_map/ppermute | solution.py:361
  18.4 1.5 %collective-permute-start.1 = (bf16[640,256]{1,0:T(8,128)(2,1)S(1)}, bf16[640,256]{1,0:T(8,128)(2,1)S(1)}, u32[]{:S(2)}, u32[]{:S(2)}) collective-permute-start(bf16[640,256]{1,0:T(8,128)(2,1)S(1)} %collective-permute-done.refs_0_), channel_id=1, source_target_pairs={{0,2},{2,0},{1,3},{3,1},{4,6},{6,4},{5,7},{7,5},{8,10},{10,8},{9,1... | collective-permute-start | bytes 983048 | tf_op jit(solution)/shard_map/ppermute | solution.py:361
  20.7 1.3 %copy-done = bf16[256,2560]{1,0:T(8,128)(2,1)S(1)} copy-done((bf16[256,2560]{1,0:T(8,128)(2,1)S(1)}, bf16[256,2560]{1,0:T(8,128)(2,1)}, u32[]{:S(2)}) %copy-start) | copy-done | bytes 1310744
  22.0 3.9 %norm.1 = (bf16[256,2560]{1,0:T(8,128)(2,1)}, bf16[256,2560]{1,0:T(8,128)(2,1)}, bf16[8,640,128]{2,1,0:T(8,128)(2,1)}) custom-call(bf16[256,2560]{1,0:T(8,128)(2,1)S(1)} %copy-done, bf16[256,2560]{1,0:T(8,128)(2,1)S(1)} %collective-permute-done.4.other_ref, bf16[1,5120]{1,0:T(2,128)(2,1)S(1)} %broadcast_in_dim.2.gain_ref), custom_call_target="tpu_custom_call" | custom-call | flops 10485760 | bytes 6553600 | tf_op jit(solution)/shard_map/norm/pallas_call | solution.py:345
  28.2 1.4 %collective-permute-start.6 = (bf16[640,256]{1,0:T(8,128)(2,1)S(1)}, bf16[640,256]{1,0:T(8,128)(2,1)S(1)}, u32[]{:S(2)}, u32[]{:S(2)}) collective-permute-start(bf16[640,256]{1,0:T(8,128)(2,1)S(1)} %collective-permute-done.3.refs_0_), channel_id=1, source_target_pairs={{0,2},{2,0},{1,3},{3,1},{4,6},{6,4},{5,7},{7,5},{8,10},{10,8},{9,1... | collective-permute-start | bytes 983048 | tf_op jit(solution)/shard_map/ppermute | solution.py:361
  30.2 6.6 %collective-permute-done.5.p0 = bf16[640,256]{1,0:T(8,128)(2,1)S(1)} collective-permute-done((bf16[640,256]{1,0:T(8,128)(2,1)S(1)}, bf16[640,256]{1,0:T(8,128)(2,1)S(1)}, u32[]{:S(2)}, u32[]{:S(2)}) %collective-permute-start.5) | collective-permute-done | bytes 327712 | tf_op jit(solution)/shard_map/ppermute | solution.py:366
  36.8 2.0 %collective-permute-done.6.refs_1_ = bf16[640,256]{1,0:T(8,128)(2,1)S(1)} collective-permute-done((bf16[640,256]{1,0:T(8,128)(2,1)S(1)}, bf16[640,256]{1,0:T(8,128)(2,1)S(1)}, u32[]{:S(2)}, u32[]{:S(2)}) %collective-permute-start.6) | collective-permute-done | bytes 327712 | tf_op jit(solution)/shard_map/ppermute | solution.py:361
  39.6 3.2 %collective-permute-done.11.refs_3_ = bf16[640,256]{1,0:T(8,128)(2,1)} collective-permute-done((bf16[640,256]{1,0:T(8,128)(2,1)S(1)}, bf16[640,256]{1,0:T(8,128)(2,1)}, u32[]{:S(2)}, u32[]{:S(2)}) %collective-permute-start.11) | collective-permute-done | bytes 327712 | tf_op jit(solution)/shard_map/ppermute | solution.py:361
  42.8 5.6 %all-to-all-start = ((bf16[8,640,128]{2,1,0:T(8,128)(2,1)}), bf16[8,640,128]{2,1,0:T(8,128)(2,1)S(1)}, u32[]{:S(2)}, u32[]{:S(2)}) async-start(bf16[8,640,128]{2,1,0:T(8,128)(2,1)} %get-tuple-element.61), calls=%async_computation | async-start | bytes 2621440 | tf_op jit(solution)/shard_map/all_to_all | solution.py:421
  48.4 1.5 %collective-permute-start.10 = (bf16[640,256]{1,0:T(8,128)(2,1)S(1)}, bf16[640,256]{1,0:T(8,128)(2,1)S(1)}, u32[]{:S(2)}, u32[]{:S(2)}) collective-permute-start(bf16[640,256]{1,0:T(8,128)(2,1)S(1)} %copy-done.12), channel_id=1, source_target_pairs={{0,16},{16,0},{1,17},{17,1},{2,18},{18,2},{3,19},{19,3},{4,20},{20... | collective-permute-start | bytes 983048 | tf_op jit(solution)/shard_map/ppermute | solution.py:361
  50.5 2.0 %collective-permute-start.8 = (bf16[640,256]{1,0:T(8,128)(2,1)S(1)}, bf16[640,256]{1,0:T(8,128)(2,1)S(1)}, u32[]{:S(2)}, u32[]{:S(2)}) collective-permute-start(bf16[640,256]{1,0:T(8,128)(2,1)S(1)} %collective-permute-done.5.p0), channel_id=1, source_target_pairs={{0,2},{2,0},{1,3},{3,1},{4,6},{6,4},{5,7},{7,5},{8,10},{10,8},{9,1... | collective-permute-start | bytes 983048 | tf_op jit(solution)/shard_map/ppermute | solution.py:361
  52.5 3.2 %project.2.start_ref = f32[2,256,256]{2,1,0:T(8,128)S(1)} custom-call(bf16[256,2560]{1,0:T(8,128)(2,1)} %get-tuple-element.43.own_ref, bf16[256,2560]{1,0:T(8,128)(2,1)} %get-tuple-element.44.other_ref, bf16[2,1280,256]{2,1,0:T(8,128)(2,1)} %start_ref.1, bf16[640,256]{1,0:T(8,128)(2,1)} %copy-done.7, bf16[640,256]{1,0:T(8,128)(2,1)} %copy-done.9, ...), custom_call_target="tpu_custom_call" | custom-call | flops 671088640 | bytes 4000000 | tf_op jit(solution)/shard_map/project/pallas_call | solution.py:134
  55.7 2.5 %collective-permute-done.10.refs_3_ = bf16[640,256]{1,0:T(8,128)(2,1)S(1)} collective-permute-done((bf16[640,256]{1,0:T(8,128)(2,1)S(1)}, bf16[640,256]{1,0:T(8,128)(2,1)S(1)}, u32[]{:S(2)}, u32[]{:S(2)}) %collective-permute-start.10) | collective-permute-done | bytes 327712 | tf_op jit(solution)/shard_map/ppermute | solution.py:361
  58.2 3.5 %collective-permute-done.9.p2 = bf16[640,256]{1,0:T(8,128)(2,1)S(1)} collective-permute-done((bf16[640,256]{1,0:T(8,128)(2,1)S(1)}, bf16[640,256]{1,0:T(8,128)(2,1)S(1)}, u32[]{:S(2)}, u32[]{:S(2)}) %collective-permute-start.9) | collective-permute-done | bytes 327712 | tf_op jit(solution)/shard_map/ppermute | solution.py:361
  61.7 5.4 %collective-permute-done.8.p1 = bf16[640,256]{1,0:T(8,128)(2,1)S(1)} collective-permute-done((bf16[640,256]{1,0:T(8,128)(2,1)S(1)}, bf16[640,256]{1,0:T(8,128)(2,1)S(1)}, u32[]{:S(2)}, u32[]{:S(2)}) %collective-permute-start.8) | collective-permute-done | bytes 327712 | tf_op jit(solution)/shard_map/ppermute | solution.py:361
  69.1 2.2 %project.3.sums_ref = f32[2,256,256]{2,1,0:T(8,128)S(1)} custom-call(bf16[256,2560]{1,0:T(8,128)(2,1)} %get-tuple-element.43.own_ref, bf16[256,2560]{1,0:T(8,128)(2,1)} %get-tuple-element.44.other_ref, f32[2,256,256]{2,1,0:T(8,128)S(1)} %project.2.start_ref, bf16[640,256]{1,0:T(8,128)(2,1)} %copy-done.6, bf16[640,256]{1,0:T(8,128)(2,1)} %copy-done.11, ...), custom_call_target="tpu_custom_call" | custom-call | flops 335544320 | bytes 4000000 | tf_op jit(solution)/shard_map/project/pallas_call | solution.py:134
  71.3 2.9 %collective-permute-done.12.p3 = bf16[640,256]{1,0:T(8,128)(2,1)S(1)} collective-permute-done((bf16[640,256]{1,0:T(8,128)(2,1)S(1)}, bf16[640,256]{1,0:T(8,128)(2,1)S(1)}, u32[]{:S(2)}, u32[]{:S(2)}) %collective-permute-start.12) | collective-permute-done | bytes 327712 | tf_op jit(solution)/shard_map/ppermute | solution.py:361
  74.2 6.2 %attention.1 = (bf16[256,1280]{1,0:T(8,128)(2,1)}, bf16[256,512]{1,0:T(8,128)(2,1)S(1)}) custom-call(bf16[256,2560]{1,0:T(8,128)(2,1)} %get-tuple-element.43.own_ref, bf16[256,2560]{1,0:T(8,128)(2,1)} %get-tuple-element.44.other_ref, bf16[640,256]{1,0:T(8,128)(2,1)S(1)} %collective-permute-done.5.p0, bf16[640,256]{1,0:T(8,128)(2,1)S(1)} %collective-permute-done.8.p1, ...), custom_call_target="tpu_custom_call" | custom-call | flops 838860800 | bytes 5000000 | tf_op jit(solution)/shard_map/attention/pallas_call | solution.py:211
  80.7 3.3 %collective-permute-start.13 = (bf16[256,512]{1,0:T(8,128)(2,1)S(1)}, bf16[256,512]{1,0:T(8,128)(2,1)S(1)}, u32[]{:S(2)}, u32[]{:S(2)}) collective-permute-start(bf16[256,512]{1,0:T(8,128)(2,1)S(1)} %get-tuple-element.58.refs_0_), channel_id=1, source_target_pairs={{0,4},{4,8},{8,12},{12,0},{1,5},{5,9},{9,13},{13,1},{2,6},{6,10},{... | collective-permute-start | bytes 786440 | tf_op jit(solution)/shard_map/ppermute | solution.py:366
  84.0 2.8 %collective-permute-done.14.refs_1_ = bf16[256,512]{1,0:T(8,128)(2,1)S(1)} collective-permute-done((bf16[256,512]{1,0:T(8,128)(2,1)S(1)}, bf16[256,512]{1,0:T(8,128)(2,1)S(1)}, u32[]{:S(2)}, u32[]{:S(2)}) %collective-permute-start.14) | collective-permute-done | bytes 262176 | tf_op jit(solution)/shard_map/ppermute | solution.py:361
  86.8 3.1 %collective-permute-done.13.refs_2_ = bf16[256,512]{1,0:T(8,128)(2,1)S(1)} collective-permute-done((bf16[256,512]{1,0:T(8,128)(2,1)S(1)}, bf16[256,512]{1,0:T(8,128)(2,1)S(1)}, u32[]{:S(2)}, u32[]{:S(2)}) %collective-permute-start.13) | collective-permute-done | bytes 262176 | tf_op jit(solution)/shard_map/ppermute | solution.py:366
  89.9 2.7 %collective-permute-start.15 = (bf16[256,512]{1,0:T(8,128)(2,1)S(1)}, bf16[256,512]{1,0:T(8,128)(2,1)S(1)}, u32[]{:S(2)}, u32[]{:S(2)}) collective-permute-start(bf16[256,512]{1,0:T(8,128)(2,1)S(1)} %get-tuple-element.58.refs_0_), channel_id=1, source_target_pairs={{0,12},{4,0},{8,4},{12,8},{1,13},{5,1},{9,5},{13,9},{2,14},{6,2},{... | collective-permute-start | bytes 786440 | tf_op jit(solution)/shard_map/ppermute | solution.py:366
  93.9 2.7 %collective-permute-done.15.refs_3_ = bf16[256,512]{1,0:T(8,128)(2,1)S(1)} collective-permute-done((bf16[256,512]{1,0:T(8,128)(2,1)S(1)}, bf16[256,512]{1,0:T(8,128)(2,1)S(1)}, u32[]{:S(2)}, u32[]{:S(2)}) %collective-permute-start.15) | collective-permute-done | bytes 262176 | tf_op jit(solution)/shard_map/ppermute | solution.py:366
  96.6 2.5 %collective-permute-done.16.refs_4_ = bf16[256,512]{1,0:T(8,128)(2,1)S(1)} collective-permute-done((bf16[256,512]{1,0:T(8,128)(2,1)S(1)}, bf16[256,512]{1,0:T(8,128)(2,1)S(1)}, u32[]{:S(2)}, u32[]{:S(2)}) %collective-permute-start.16) | collective-permute-done | bytes 262176 | tf_op jit(solution)/shard_map/ppermute | solution.py:361
  99.2 1.3 %collective-permute-start.19 = (bf16[256,512]{1,0:T(8,128)(2,1)S(1)}, bf16[256,512]{1,0:T(8,128)(2,1)S(1)}, u32[]{:S(2)}, u32[]{:S(2)}) collective-permute-start(bf16[256,512]{1,0:T(8,128)(2,1)S(1)} %collective-permute-done.15.refs_3_), channel_id=1, source_target_pairs={{0,2},{2,0},{1,3},{3,1},{4,6},{6,4},{5,7},{7,5},{8,10},{10,8},{9,1... | collective-permute-start | bytes 786440 | tf_op jit(solution)/shard_map/ppermute | solution.py:361
  100.5 9.1 %collective-permute-done.18.refs_0_ = bf16[256,512]{1,0:T(8,128)(2,1)S(1)} collective-permute-done((bf16[256,512]{1,0:T(8,128)(2,1)S(1)}, bf16[256,512]{1,0:T(8,128)(2,1)S(1)}, u32[]{:S(2)}, u32[]{:S(2)}) %collective-permute-start.18) | collective-permute-done | bytes 262176 | tf_op jit(solution)/shard_map/ppermute | solution.py:366
  112.0 2.8 %gradient.2 = (f32[2,640,256]{2,1,0:T(8,128)S(1)}, f32[2,256]{1,0:T(2,128)S(1)}) custom-call(bf16[8,640,128]{2,1,0:T(8,128)(2,1)} %copy-done.4, bf16[8,640,128]{2,1,0:T(8,128)(2,1)} %copy-done.5, bf16[256,512]{1,0:T(8,128)(2,1)} %copy-done.3, bf16[256,512]{1,0:T(8,128)(2,1)} %copy-done.14, bf16[256,512]{1,0:T(8,128)(2,1)} %copy-done.15, ...), custom_call_target="tpu_custom_call" | custom-call | flops 1006632960 | bytes 5000000 | tf_op jit(solution)/shard_map/gradient/pallas_call | solution.py:283
  114.7 2.8 %collective-permute-done.20.refs_1_ = bf16[256,512]{1,0:T(8,128)(2,1)S(1)} collective-permute-done((bf16[256,512]{1,0:T(8,128)(2,1)S(1)}, bf16[256,512]{1,0:T(8,128)(2,1)S(1)}, u32[]{:S(2)}, u32[]{:S(2)}) %collective-permute-start.20) | collective-permute-done | bytes 262176 | tf_op jit(solution)/shard_map/ppermute | solution.py:361
  117.5 2.8 %gradient.3 = (f32[2,640,256]{2,1,0:T(8,128)}, f32[2,256]{1,0:T(2,128)}) custom-call(bf16[8,640,128]{2,1,0:T(8,128)(2,1)} %copy-done.4, bf16[8,640,128]{2,1,0:T(8,128)(2,1)} %copy-done.5, bf16[256,512]{1,0:T(8,128)(2,1)S(1)} %collective-permute-done.18.refs_0_, bf16[256,512]{1,0:T(8,128)(2,1)S(1)} %collective-permute-done.20.refs_1_, ...), custom_call_target="tpu_custom_call" | custom-call | flops 335544320 | bytes 5000000 | tf_op jit(solution)/shard_map/gradient/pallas_call | solution.py:283
  (64 shorter events, 12.4 us)
Async XLA Ops:
  0.6 20.0 %collective-permute-start.4 = (bf16[256,2560]{1,0:T(8,128)(2,1)}, bf16[256,2560]{1,0:T(8,128)(2,1)S(1)}, u32[]{:S(2)}, u32[]{:S(2)}) collective-permute-start(bf16[256,2560]{1,0:T(8,128)(2,1)} %own_ref.1), channel_id=1, source_target_pairs={{0,1},{1,0},{2,3},{3,2},{4,5},{5,4},{6,7},{7,6},{8,9},{9,8},{10,11... | collective-permute-start | bytes 3932168 | tf_op jit(solution)/shard_map/ppermute | solution.py:361
  2.1 13.0 %collective-permute-start = (bf16[640,256]{1,0:T(8,128)(2,1)S(1)}, bf16[640,256]{1,0:T(8,128)(2,1)S(1)}, u32[]{:S(2)}, u32[]{:S(2)}) collective-permute-start(bf16[640,256]{1,0:T(8,128)(2,1)S(1)} %dynamic-slice_bitcast_fusion), channel_id=1, source_target_pairs={{0,4},{4,8},{8,12},{12,0},{1,5},{5,9},{9,13},{13,1},{2,6},{6,10},{... | collective-permute-start | bytes 983048 | tf_op jit(solution)/shard_map/ppermute | solution.py:366
  15.2 12.0 %copy-start.7 = (bf16[640,256]{1,0:T(8,128)(2,1)}, bf16[640,256]{1,0:T(8,128)(2,1)S(1)}, u32[]{:S(2)}) copy-start(bf16[640,256]{1,0:T(8,128)(2,1)S(1)} %collective-permute-done.refs_0_) | copy-start | bytes 983044
  15.2 10.7 %collective-permute-start.3 = (bf16[640,256]{1,0:T(8,128)(2,1)S(1)}, bf16[640,256]{1,0:T(8,128)(2,1)S(1)}, u32[]{:S(2)}, u32[]{:S(2)}) collective-permute-start(bf16[640,256]{1,0:T(8,128)(2,1)S(1)} %dynamic-slice_bitcast_fusion), channel_id=1, source_target_pairs={{0,12},{4,0},{8,4},{12,8},{1,13},{5,1},{9,5},{13,9},{2,14},{6,2},{... | collective-permute-start | bytes 983048 | tf_op jit(solution)/shard_map/ppermute | solution.py:366
  16.9 9.0 %collective-permute-start.2 = (bf16[640,256]{1,0:T(8,128)(2,1)S(1)}, bf16[640,256]{1,0:T(8,128)(2,1)S(1)}, u32[]{:S(2)}, u32[]{:S(2)}) collective-permute-start(bf16[640,256]{1,0:T(8,128)(2,1)S(1)} %collective-permute-done.refs_0_), channel_id=1, source_target_pairs={{0,16},{16,0},{1,17},{17,1},{2,18},{18,2},{3,19},{19,3},{4,20},{20... | collective-permute-start | bytes 983048 | tf_op jit(solution)/shard_map/ppermute | solution.py:361
  18.4 8.7 %collective-permute-start.1 = (bf16[640,256]{1,0:T(8,128)(2,1)S(1)}, bf16[640,256]{1,0:T(8,128)(2,1)S(1)}, u32[]{:S(2)}, u32[]{:S(2)}) collective-permute-start(bf16[640,256]{1,0:T(8,128)(2,1)S(1)} %collective-permute-done.refs_0_), channel_id=1, source_target_pairs={{0,2},{2,0},{1,3},{3,1},{4,6},{6,4},{5,7},{7,5},{8,10},{10,8},{9,1... | collective-permute-start | bytes 983048 | tf_op jit(solution)/shard_map/ppermute | solution.py:361
  25.9 16.9 %copy-start.6 = (bf16[640,256]{1,0:T(8,128)(2,1)}, bf16[640,256]{1,0:T(8,128)(2,1)S(1)}, u32[]{:S(2)}) copy-start(bf16[640,256]{1,0:T(8,128)(2,1)S(1)} %collective-permute-done.3.refs_0_) | copy-start | bytes 983044
  26.0 16.9 %copy-start.8 = (bf16[640,256]{1,0:T(8,128)(2,1)}, bf16[640,256]{1,0:T(8,128)(2,1)S(1)}, u32[]{:S(2)}) copy-start(bf16[640,256]{1,0:T(8,128)(2,1)S(1)} %collective-permute-done.2.refs_2_) | copy-start | bytes 983044
  27.2 15.6 %copy-start.9 = (bf16[640,256]{1,0:T(8,128)(2,1)}, bf16[640,256]{1,0:T(8,128)(2,1)S(1)}, u32[]{:S(2)}) copy-start(bf16[640,256]{1,0:T(8,128)(2,1)S(1)} %collective-permute-done.1.refs_1_) | copy-start | bytes 983044
  27.2 25.3 %copy-start.19 = (bf16[2,256]{1,0:T(2,128)(2,1)S(1)}, bf16[2,256]{1,0:T(2,128)(2,1)}, u32[]{:S(2)}) copy-start(bf16[2,256]{1,0:T(2,128)(2,1)} %param.11) | copy-start | bytes 3076
  27.2 9.6 %collective-permute-start.5 = (bf16[640,256]{1,0:T(8,128)(2,1)S(1)}, bf16[640,256]{1,0:T(8,128)(2,1)S(1)}, u32[]{:S(2)}, u32[]{:S(2)}) collective-permute-start(bf16[640,256]{1,0:T(8,128)(2,1)S(1)} %collective-permute-done.refs_0_), channel_id=1, source_target_pairs={{0,4},{4,8},{8,12},{12,0},{1,5},{5,9},{9,13},{13,1},{2,6},{6,10},{... | collective-permute-start | bytes 983048 | tf_op jit(solution)/shard_map/ppermute | solution.py:366
  27.6 9.3 %collective-permute-start.7 = (bf16[640,256]{1,0:T(8,128)(2,1)S(1)}, bf16[640,256]{1,0:T(8,128)(2,1)S(1)}, u32[]{:S(2)}, u32[]{:S(2)}) collective-permute-start(bf16[640,256]{1,0:T(8,128)(2,1)S(1)} %collective-permute-done.3.refs_0_), channel_id=1, source_target_pairs={{0,16},{16,0},{1,17},{17,1},{2,18},{18,2},{3,19},{19,3},{4,20},{20... | collective-permute-start | bytes 983048 | tf_op jit(solution)/shard_map/ppermute | solution.py:361
  28.2 10.6 %collective-permute-start.6 = (bf16[640,256]{1,0:T(8,128)(2,1)S(1)}, bf16[640,256]{1,0:T(8,128)(2,1)S(1)}, u32[]{:S(2)}, u32[]{:S(2)}) collective-permute-start(bf16[640,256]{1,0:T(8,128)(2,1)S(1)} %collective-permute-done.3.refs_0_), channel_id=1, source_target_pairs={{0,2},{2,0},{1,3},{3,1},{4,6},{6,4},{5,7},{7,5},{8,10},{10,8},{9,1... | collective-permute-start | bytes 983048 | tf_op jit(solution)/shard_map/ppermute | solution.py:361
  29.6 13.3 %collective-permute-start.11 = (bf16[640,256]{1,0:T(8,128)(2,1)S(1)}, bf16[640,256]{1,0:T(8,128)(2,1)}, u32[]{:S(2)}, u32[]{:S(2)}) collective-permute-start(bf16[640,256]{1,0:T(8,128)(2,1)S(1)} %collective-permute-done.2.refs_2_), channel_id=1, source_target_pairs={{0,2},{2,0},{1,3},{3,1},{4,6},{6,4},{5,7},{7,5},{8,10},{10,8},{9,1... | collective-permute-start | bytes 983048 | tf_op jit(solution)/shard_map/ppermute | solution.py:361
  42.8 56.2 %all-to-all-start = ((bf16[8,640,128]{2,1,0:T(8,128)(2,1)}), bf16[8,640,128]{2,1,0:T(8,128)(2,1)S(1)}, u32[]{:S(2)}, u32[]{:S(2)}) async-start(bf16[8,640,128]{2,1,0:T(8,128)(2,1)} %get-tuple-element.61), calls=%async_computation | async-start | bytes 2621440 | tf_op jit(solution)/shard_map/all_to_all | solution.py:421
  48.4 9.8 %collective-permute-start.10 = (bf16[640,256]{1,0:T(8,128)(2,1)S(1)}, bf16[640,256]{1,0:T(8,128)(2,1)S(1)}, u32[]{:S(2)}, u32[]{:S(2)}) collective-permute-start(bf16[640,256]{1,0:T(8,128)(2,1)S(1)} %copy-done.12), channel_id=1, source_target_pairs={{0,16},{16,0},{1,17},{17,1},{2,18},{18,2},{3,19},{19,3},{4,20},{20... | collective-permute-start | bytes 983048 | tf_op jit(solution)/shard_map/ppermute | solution.py:361
  49.9 11.8 %collective-permute-start.9 = (bf16[640,256]{1,0:T(8,128)(2,1)S(1)}, bf16[640,256]{1,0:T(8,128)(2,1)S(1)}, u32[]{:S(2)}, u32[]{:S(2)}) collective-permute-start(bf16[640,256]{1,0:T(8,128)(2,1)S(1)} %collective-permute-done.5.p0), channel_id=1, source_target_pairs={{0,16},{16,0},{1,17},{17,1},{2,18},{18,2},{3,19},{19,3},{4,20},{20... | collective-permute-start | bytes 983048 | tf_op jit(solution)/shard_map/ppermute | solution.py:361
  50.5 16.6 %collective-permute-start.8 = (bf16[640,256]{1,0:T(8,128)(2,1)S(1)}, bf16[640,256]{1,0:T(8,128)(2,1)S(1)}, u32[]{:S(2)}, u32[]{:S(2)}) collective-permute-start(bf16[640,256]{1,0:T(8,128)(2,1)S(1)} %collective-permute-done.5.p0), channel_id=1, source_target_pairs={{0,2},{2,0},{1,3},{3,1},{4,6},{6,4},{5,7},{7,5},{8,10},{10,8},{9,1... | collective-permute-start | bytes 983048 | tf_op jit(solution)/shard_map/ppermute | solution.py:361
  67.1 7.1 %collective-permute-start.12 = (bf16[640,256]{1,0:T(8,128)(2,1)S(1)}, bf16[640,256]{1,0:T(8,128)(2,1)S(1)}, u32[]{:S(2)}, u32[]{:S(2)}) collective-permute-start(bf16[640,256]{1,0:T(8,128)(2,1)S(1)} %collective-permute-done.8.p1), channel_id=1, source_target_pairs={{0,16},{16,0},{1,17},{17,1},{2,18},{18,2},{3,19},{19,3},{4,20},{20... | collective-permute-start | bytes 983048 | tf_op jit(solution)/shard_map/ppermute | solution.py:361
  80.4 30.5 %copy-start.3 = (bf16[256,512]{1,0:T(8,128)(2,1)}, bf16[256,512]{1,0:T(8,128)(2,1)S(1)}, u32[]{:S(2)}) copy-start(bf16[256,512]{1,0:T(8,128)(2,1)S(1)} %get-tuple-element.58.refs_0_) | copy-start | bytes 786436
  80.4 6.4 %collective-permute-start.14 = (bf16[256,512]{1,0:T(8,128)(2,1)S(1)}, bf16[256,512]{1,0:T(8,128)(2,1)S(1)}, u32[]{:S(2)}, u32[]{:S(2)}) collective-permute-start(bf16[256,512]{1,0:T(8,128)(2,1)S(1)} %get-tuple-element.58.refs_0_), channel_id=1, source_target_pairs={{0,2},{2,0},{1,3},{3,1},{4,6},{6,4},{5,7},{7,5},{8,10},{10,8},{9,1... | collective-permute-start | bytes 786440 | tf_op jit(solution)/shard_map/ppermute | solution.py:361
  80.7 9.2 %collective-permute-start.13 = (bf16[256,512]{1,0:T(8,128)(2,1)S(1)}, bf16[256,512]{1,0:T(8,128)(2,1)S(1)}, u32[]{:S(2)}, u32[]{:S(2)}) collective-permute-start(bf16[256,512]{1,0:T(8,128)(2,1)S(1)} %get-tuple-element.58.refs_0_), channel_id=1, source_target_pairs={{0,4},{4,8},{8,12},{12,0},{1,5},{5,9},{9,13},{13,1},{2,6},{6,10},{... | collective-permute-start | bytes 786440 | tf_op jit(solution)/shard_map/ppermute | solution.py:366
  86.8 24.0 %copy-start.14 = (bf16[256,512]{1,0:T(8,128)(2,1)}, bf16[256,512]{1,0:T(8,128)(2,1)S(1)}, u32[]{:S(2)}) copy-start(bf16[256,512]{1,0:T(8,128)(2,1)S(1)} %collective-permute-done.14.refs_1_) | copy-start | bytes 786436
  89.9 20.9 %copy-start.15 = (bf16[256,512]{1,0:T(8,128)(2,1)}, bf16[256,512]{1,0:T(8,128)(2,1)S(1)}, u32[]{:S(2)}) copy-start(bf16[256,512]{1,0:T(8,128)(2,1)S(1)} %collective-permute-done.13.refs_2_) | copy-start | bytes 786436
  89.9 6.6 %collective-permute-start.15 = (bf16[256,512]{1,0:T(8,128)(2,1)S(1)}, bf16[256,512]{1,0:T(8,128)(2,1)S(1)}, u32[]{:S(2)}, u32[]{:S(2)}) collective-permute-start(bf16[256,512]{1,0:T(8,128)(2,1)S(1)} %get-tuple-element.58.refs_0_), channel_id=1, source_target_pairs={{0,12},{4,0},{8,4},{12,8},{1,13},{5,1},{9,5},{13,9},{2,14},{6,2},{... | collective-permute-start | bytes 786440 | tf_op jit(solution)/shard_map/ppermute | solution.py:366
  92.7 6.4 %collective-permute-start.16 = (bf16[256,512]{1,0:T(8,128)(2,1)S(1)}, bf16[256,512]{1,0:T(8,128)(2,1)S(1)}, u32[]{:S(2)}, u32[]{:S(2)}) collective-permute-start(bf16[256,512]{1,0:T(8,128)(2,1)S(1)} %collective-permute-done.13.refs_2_), channel_id=1, source_target_pairs={{0,2},{2,0},{1,3},{3,1},{4,6},{6,4},{5,7},{7,5},{8,10},{10,8},{9,1... | collective-permute-start | bytes 786440 | tf_op jit(solution)/shard_map/ppermute | solution.py:361
  96.6 14.3 %copy-start.16 = (bf16[256,512]{1,0:T(8,128)(2,1)}, bf16[256,512]{1,0:T(8,128)(2,1)S(1)}, u32[]{:S(2)}) copy-start(bf16[256,512]{1,0:T(8,128)(2,1)S(1)} %collective-permute-done.15.refs_3_) | copy-start | bytes 786436
  99.0 11.8 %copy-start.4 = (bf16[8,640,128]{2,1,0:T(8,128)(2,1)}, bf16[8,640,128]{2,1,0:T(8,128)(2,1)S(1)}, u32[]{:S(2)}) copy-start(bf16[8,640,128]{2,1,0:T(8,128)(2,1)S(1)} %all-to-all-done.own_ref) | copy-start | bytes 3932164
  99.0 11.8 %collective-permute-start.17 = (bf16[8,640,128]{2,1,0:T(8,128)(2,1)S(1)}, bf16[8,640,128]{2,1,0:T(8,128)(2,1)S(1)}, u32[]{:S(2)}, u32[]{:S(2)}) collective-permute-start(bf16[8,640,128]{2,1,0:T(8,128)(2,1)S(1)} %all-to-all-done.own_ref), channel_id=1, source_target_pairs={{0,1},{1,0},{2,3},{3,2},{4,5},{5,4},{6,7},{7,6},{8,9},{9,8},{10,11... | collective-permute-start | bytes 3932168 | tf_op jit(solution)/shard_map/ppermute | solution.py:361
  99.1 10.5 %collective-permute-start.18 = (bf16[256,512]{1,0:T(8,128)(2,1)S(1)}, bf16[256,512]{1,0:T(8,128)(2,1)S(1)}, u32[]{:S(2)}, u32[]{:S(2)}) collective-permute-start(bf16[256,512]{1,0:T(8,128)(2,1)S(1)} %collective-permute-done.13.refs_2_), channel_id=1, source_target_pairs={{0,4},{4,8},{8,12},{12,0},{1,5},{5,9},{9,13},{13,1},{2,6},{6,10},{... | collective-permute-start | bytes 786440 | tf_op jit(solution)/shard_map/ppermute | solution.py:366
  99.2 10.4 %collective-permute-start.19 = (bf16[256,512]{1,0:T(8,128)(2,1)S(1)}, bf16[256,512]{1,0:T(8,128)(2,1)S(1)}, u32[]{:S(2)}, u32[]{:S(2)}) collective-permute-start(bf16[256,512]{1,0:T(8,128)(2,1)S(1)} %collective-permute-done.15.refs_3_), channel_id=1, source_target_pairs={{0,2},{2,0},{1,3},{3,1},{4,6},{6,4},{5,7},{7,5},{8,10},{10,8},{9,1... | collective-permute-start | bytes 786440 | tf_op jit(solution)/shard_map/ppermute | solution.py:361
  109.6 7.9 %collective-permute-start.20 = (bf16[256,512]{1,0:T(8,128)(2,1)S(1)}, bf16[256,512]{1,0:T(8,128)(2,1)S(1)}, u32[]{:S(2)}, u32[]{:S(2)}) collective-permute-start(bf16[256,512]{1,0:T(8,128)(2,1)S(1)} %collective-permute-done.18.refs_0_), channel_id=1, source_target_pairs={{0,2},{2,0},{1,3},{3,1},{4,6},{6,4},{5,7},{7,5},{8,10},{10,8},{9,1... | collective-permute-start | bytes 786440 | tf_op jit(solution)/shard_map/ppermute | solution.py:361
  (10 other events, 48.9 us)

commit v9 on v5

--- a/solution.py
+++ b/solution.py
@@ -181,14 +181,16 @@
     )(*operands)
 
 
-def gradient_kernel(count, first, *refs):
-    slabs, pairs = refs[1 : 1 + count], refs[1 + count : 1 + 2 * count]
-    refs = refs[1 + 2 * count :]
+def gradient_kernel(count, first, halves, *refs):
+    at_ref = refs[0]
+    own, other, pairs = (refs[1 + i * count : 1 + (i + 1) * count] for i in range(3))
+    refs = refs[1 + 3 * count :]
     weight_ref, bias_ref = refs[-2:]
     columns = weight_ref.shape[2]
     total = None
-    for slab, pair in zip(slabs, pairs):
-        term = product(slab[0], pair[...])
+    for turn, pair in enumerate(pairs):
+        slab = jnp.where(at_ref[turn] < halves, own[turn][0], other[turn][0])
+        term = product(slab, pair[...])
         total = term if total is None else total + term
     for j in range(2):
         part = total[:, j * columns : (j + 1) * columns]
@@ -205,23 +207,23 @@
             bias_ref[j : j + 1, :] = part if first else refs[1][j : j + 1, :] + part
 
 
-def gradient(at, slabs, pairs, sums):
-    _, share, length = slabs.shape
+def gradient(at, own, other, pairs, sums):
+    halves, share, length = own.shape
     columns = pairs[0].shape[1] // 2
     count = len(pairs)
     tile = share // 2 if share % 32 == 0 else share
 
     def slab_spec(turn):
-        return pl.BlockSpec((1, tile, length), lambda i, at: (at[turn], i, 0))
+        return pl.BlockSpec((1, tile, length), lambda i, at: (at[turn] % halves, i, 0))
 
     weight_spec = pl.BlockSpec((2, tile, columns), lambda i, at: (0, i, 0))
     bias_spec = pl.BlockSpec((2, columns), lambda i, at: (0, 0))
-    in_specs = [slab_spec(turn) for turn in range(count)]
+    in_specs = [slab_spec(turn) for turn in range(count)] * 2
     in_specs += [pl.BlockSpec((length, 2 * columns), lambda i, at: (0, 0))] * count
     if sums:
         in_specs += [weight_spec, bias_spec]
     return pl.pallas_call(
-        functools.partial(gradient_kernel, count, sums is None),
+        functools.partial(gradient_kernel, count, sums is None, halves),
         grid_spec=pltpu.PrefetchScalarGridSpec(
             num_scalar_prefetch=1,
             grid=(share // tile,),
@@ -237,7 +239,7 @@
             flops=4 * count * length * share * columns, bytes_accessed=5000000, transcendentals=0
         ),
         name="gradient",
-    )(at, *([slabs] * count), *pairs, *(sums or ()))
+    )(at, *([own] * count), *([other] * count), *pairs, *(sums or ()))
 
 
 def norm_kernel(values_ref, scale_ref, gain_ref, normed_ref, *slab_refs):
@@ -342,12 +344,12 @@
     up, up_x, up_y, down = lax.optimization_barrier((up, up_x, up_y, down))
     down_x, down_y = swapped(down, "dp"), swapped(down, "groups")
     twice = turned(up, "blk", 1)
-    up_both = swapped(up_x, "groups")
+    up_both = swapped(up_y, "dp")
     twice, down_x, down_y, normed_other = lax.optimization_barrier(
         (twice, down_x, down_y, normed_other)
     )
     twice_x, twice_y = swapped(twice, "dp"), swapped(twice, "groups")
-    down_both = swapped(down_y, "dp")
+    down_both = swapped(down_x, "groups")
     slabs[:2] = [sent_slab(after(slabs[turn], twice), turn) for turn in (0, 1)]
     twice_x, twice_y, up_both, down_both, slabs[0] = lax.optimization_barrier(
         (twice_x, twice_y, up_both, down_both, slabs[0])
@@ -356,26 +358,26 @@
 
     gathered = [(1, (up, up_x, up_y, up_both)), (-1, (down, down_x, down_y, down_both))]
     sums = project(normed, normed_other, kv_weight, gathered)
-    sums, *slabs = lax.optimization_barrier((sums, *slabs))
-    slabs[2:] = [sent_slab(slabs[turn], turn) for turn in (2, 3)]
+    slabs[2:] = [sent_slab(after(slabs[turn], twice_x), turn) for turn in (2, 3)]
+    sums, slabs[1], slabs[2] = lax.optimization_barrier((sums, slabs[1], slabs[2]))
     grad_query, grad_pair = attention(
         2, normed, normed_other, (twice, twice_x, twice_y, twice_both), sums, bias, cosine, sine,
         queries, cotangent,
     )
 
     def slab_of(distance, same):
-        source = replica if same else 1 - replica
-        turn = (slab_here - (block - distance)) % half
-        return (source != core) * half + turn
-
+        from_replica = replica if same else 1 - replica
+        return (slab_here - (block - distance)) % half + half * (from_replica != core)
+
+    grad_pair, slabs[3] = lax.optimization_barrier((grad_pair, slabs[3]))
     pair_up, pair_x = turned(grad_pair, "blk", 1), swapped(grad_pair, "dp")
-    pair_up, pair_x, grad_pair = lax.optimization_barrier((pair_up, pair_x, grad_pair))
+    pair_up, pair_x, grad_pair, *slabs = lax.optimization_barrier(
+        (pair_up, pair_x, grad_pair, *slabs)
+    )
+    slabs_own = jnp.stack(slabs)
+    slabs_other = swapped(slabs_own, "sub")
     pair_down, pair_up_x = turned(grad_pair, "blk", -1), swapped(pair_up, "dp")
-    pair_down, pair_up_x, pair_up, *slabs = lax.optimization_barrier(
-        (pair_down, pair_up_x, pair_up, *slabs)
-    )
-    slabs_own = jnp.stack(slabs)
-    slabs_held = jnp.concatenate([slabs_own, swapped(slabs_own, "sub")])
+    pair_down, pair_up_x, pair_up = lax.optimization_barrier((pair_down, pair_up_x, pair_up))
     pair_twice, pair_down_x = turned(pair_up, "blk", 1), swapped(pair_down, "dp")
     pair_twice, pair_down_x = lax.optimization_barrier((pair_twice, pair_down_x))
     pair_twice_x = swapped(pair_twice, "dp")
@@ -391,7 +393,7 @@
     sums = None
     for some in (first, last):
         at = jnp.stack([slab_of(*which) for which in some]).astype(jnp.int32)
-        sums = gradient(at, slabs_held, list(some.values()), sums)
+        sums = gradient(at, slabs_own, slabs_other, list(some.values()), sums)
     grad_weight, grad_bias = sums
     return (grad_query, grad_weight, grad_bias)
 

time: 122 us -> 124 us (1.016)
  starting transfers between devices: 37.7 us -> 29.2 us
  waiting for transfers between devices: 64.5 us -> 71.4 us
  local copies, waits for them, and re-layouts: 2.88 us -> 6.34 us
    ppermute x4, waiting for transfers between devices: 4.87 us -> 15.7 us  [sent_slab(): return lax.ppermute(slab, ('blk', 'dp', 'sub'), slab_route(turn))]
    ppermute x16, waiting for transfers between devices: 27.6 us -> 18.6 us  [swapped(): return lax.ppermute(block, axis, [(0, 1), (1, 0)])]
    ppermute x6, starting transfers between devices: 14.9 us -> 6.85 us  [turned(): lax.ppermute(block, axis, [(i, (i + distance) % size) for i in range(size)])]
    ppermute x6, waiting for transfers between devices: 32 us -> 37.1 us  [turned(): lax.ppermute(block, axis, [(i, (i + distance) % size) for i in range(size)])]
    unnamed x16 -> x24, local copies, waits for them, and re-layouts: 0.12 us -> 4.99 us
    concatenate x1 -> x0, local copies, waits for them, and re-layouts: 1.4 us -> none  [local(): slabs_held = jnp.concatenate([slabs_own, swapped(slabs_own, 'sub')])]
  transfers between devices with their start and end apart: 26 -> 26, of which waited for: 18 -> 17; matrix products, arithmetic and copies ran while one was open for 3% -> 2% of each run, Pallas kernels for 4% -> 8%
where the time goes in v9:
time: 124 us; the launch traced here: 123 us
  waiting for transfers between devices  71.4 us (58%)
  starting transfers between devices  29.2 us (24%)
  Pallas kernels  13 us (10%)
  local copies, waits for them, and re-layouts  6.34 us (5%)
  other arithmetic  2.64 us (2%)
    ppermute x6, waiting for transfers between devices, turned(): lax.ppermute(block, axis, [(i, (i + distance) % size) for i in range(size)])  37.1 us
    ppermute x16, waiting for transfers between devices, swapped(): return lax.ppermute(block, axis, [(0, 1), (1, 0)])  18.6 us
    ppermute x4, waiting for transfers between devices, sent_slab(): return lax.ppermute(slab, ('blk', 'dp', 'sub'), slab_route(turn))  15.7 us
    ppermute x16, starting transfers between devices, swapped(): return lax.ppermute(block, axis, [(0, 1), (1, 0)])  14.5 us
    ppermute x4, starting transfers between devices, sent_slab(): return lax.ppermute(slab, ('blk', 'dp', 'sub'), slab_route(turn))  7.92 us
    ppermute x6, starting transfers between devices, turned(): lax.ppermute(block, axis, [(i, (i + distance) % size) for i in range(size)])  6.85 us
    pallas_call x2, Pallas kernels, gradient(): pl.pallas_call(functools.partial(gradient_kernel, count, sums is None, ha...  5.53 us
    pallas_call x1, Pallas kernels, attention(): pl.pallas_call(functools.partial(attention_kernel, distance), in_specs=[I...  5.08 us
  transfers between devices with their start and end apart: 26, of which 17 were waited for; matrix products, arithmetic and copies ran while one was open for 2% of the time, Pallas kernels for 8%

profile of v9, /device:TPU:0, one launch (start us, length us, event | category | flops | bytes accessed | tf_op | source)
XLA Modules:
  0.0 123.5 jit_solution(9174210435727395265)
XLA Ops:
  0.7 1.1 dynamic-slice_bitcast_fusion
  1.8 3.1 %collective-permute-start = (bf16[640,256]{1,0:T(8,128)(2,1)S(1)}, bf16[640,256]{1,0:T(8,128)(2,1)S(1)}, u32[]{:S(2)}, u32[]{:S(2)}) collective-permute-start(bf16[640,256]{1,0:T(8,128)(2,1)S(1)} %dynamic-slice_bitcast_fusion), channel_id=1, source_target_pairs={{0,4},{4,8},{8,12},{12,0},{1,5},{5,9},{9,13},{13,1},{2,6},{6,10},{... | collective-permute-start | bytes 983048 | tf_op jit(solution)/shard_map/ppermute | solution.py:286
  4.8 1.7 %multiply_reduce_fusion = f32[256]{0:T(256)S(1)} fusion(bf16[256,2560]{1,0:T(8,128)(2,1)} %values_ref.1), kind=kLoop, calls=%fused_computation | loop fusion | flops 1965824 | bytes 1311744 | tf_op jit(solution)/shard_map/reduce_sum | solution.py:312
  6.7 1.0 collective-permute-done.1
  8.8 5.7 %collective-permute-done.refs_0_ = bf16[640,256]{1,0:T(8,128)(2,1)S(1)} collective-permute-done((bf16[640,256]{1,0:T(8,128)(2,1)S(1)}, bf16[640,256]{1,0:T(8,128)(2,1)S(1)}, u32[]{:S(2)}, u32[]{:S(2)}) %collective-permute-start) | collective-permute-done | bytes 327712 | tf_op jit(solution)/shard_map/ppermute | solution.py:286
  14.6 1.5 %collective-permute-start.2 = (bf16[640,256]{1,0:T(8,128)(2,1)S(1)}, bf16[640,256]{1,0:T(8,128)(2,1)S(1)}, u32[]{:S(2)}, u32[]{:S(2)}) collective-permute-start(bf16[640,256]{1,0:T(8,128)(2,1)S(1)} %collective-permute-done.refs_0_), channel_id=1, source_target_pairs={{0,2},{2,0},{1,3},{3,1},{4,6},{6,4},{5,7},{7,5},{8,10},{10,8},{9,1... | collective-permute-start | bytes 983048 | tf_op jit(solution)/shard_map/ppermute | solution.py:281
  16.1 1.5 %collective-permute-start.3 = (bf16[640,256]{1,0:T(8,128)(2,1)S(1)}, bf16[640,256]{1,0:T(8,128)(2,1)S(1)}, u32[]{:S(2)}, u32[]{:S(2)}) collective-permute-start(bf16[640,256]{1,0:T(8,128)(2,1)S(1)} %collective-permute-done.refs_0_), channel_id=1, source_target_pairs={{0,16},{16,0},{1,17},{17,1},{2,18},{18,2},{3,19},{19,3},{4,20},{20... | collective-permute-start | bytes 983048 | tf_op jit(solution)/shard_map/ppermute | solution.py:281
  17.6 1.7 %collective-permute-start.4 = (bf16[640,256]{1,0:T(8,128)(2,1)S(1)}, bf16[640,256]{1,0:T(8,128)(2,1)S(1)}, u32[]{:S(2)}, u32[]{:S(2)}) collective-permute-start(bf16[640,256]{1,0:T(8,128)(2,1)S(1)} %dynamic-slice_bitcast_fusion), channel_id=1, source_target_pairs={{0,12},{4,0},{8,4},{12,8},{1,13},{5,1},{9,5},{13,9},{2,14},{6,2},{... | collective-permute-start | bytes 983048 | tf_op jit(solution)/shard_map/ppermute | solution.py:286
  19.3 5.4 %collective-permute-done.2.refs_1_ = bf16[640,256]{1,0:T(8,128)(2,1)S(1)} collective-permute-done((bf16[640,256]{1,0:T(8,128)(2,1)S(1)}, bf16[640,256]{1,0:T(8,128)(2,1)S(1)}, u32[]{:S(2)}, u32[]{:S(2)}) %collective-permute-start.2) | collective-permute-done | bytes 327712 | tf_op jit(solution)/shard_map/ppermute | solution.py:281
  24.7 1.2 collective-permute-done.3.refs_2_
  25.9 1.2 %collective-permute-done.4.refs_4_ = bf16[640,256]{1,0:T(8,128)(2,1)S(1)} collective-permute-done((bf16[640,256]{1,0:T(8,128)(2,1)S(1)}, bf16[640,256]{1,0:T(8,128)(2,1)S(1)}, u32[]{:S(2)}, u32[]{:S(2)}) %collective-permute-start.4) | collective-permute-done | bytes 327712 | tf_op jit(solution)/shard_map/ppermute | solution.py:286
  28.2 1.5 %collective-permute-start.11 = (bf16[640,256]{1,0:T(8,128)(2,1)S(1)}, bf16[640,256]{1,0:T(8,128)(2,1)S(1)}, u32[]{:S(2)}, u32[]{:S(2)}) collective-permute-start(bf16[640,256]{1,0:T(8,128)(2,1)S(1)} %collective-permute-done.3.refs_2_), channel_id=1, source_target_pairs={{0,2},{2,0},{1,3},{3,1},{4,6},{6,4},{5,7},{7,5},{8,10},{10,8},{9,1... | collective-permute-start | bytes 983048 | tf_op jit(solution)/shard_map/ppermute | solution.py:281
  29.7 8.0 %collective-permute-done.5.p0 = bf16[640,256]{1,0:T(8,128)(2,1)S(1)} collective-permute-done((bf16[640,256]{1,0:T(8,128)(2,1)S(1)}, bf16[640,256]{1,0:T(8,128)(2,1)S(1)}, u32[]{:S(2)}, u32[]{:S(2)}) %collective-permute-start.5) | collective-permute-done | bytes 327712 | tf_op jit(solution)/shard_map/ppermute | solution.py:286
  39.0 1.5 %collective-permute-start.12 = (bf16[640,256]{1,0:T(8,128)(2,1)S(1)}, bf16[640,256]{1,0:T(8,128)(2,1)S(1)}, u32[]{:S(2)}, u32[]{:S(2)}) collective-permute-start(bf16[640,256]{1,0:T(8,128)(2,1)S(1)} %collective-permute-done.6.refs_5_), channel_id=1, source_target_pairs={{0,16},{16,0},{1,17},{17,1},{2,18},{18,2},{3,19},{19,3},{4,20},{20... | collective-permute-start | bytes 983048 | tf_op jit(solution)/shard_map/ppermute | solution.py:281
  40.6 1.8 %collective-permute-start.9 = (bf16[640,256]{1,0:T(8,128)(2,1)S(1)}, bf16[640,256]{1,0:T(8,128)(2,1)S(1)}, u32[]{:S(2)}, u32[]{:S(2)}) collective-permute-start(bf16[640,256]{1,0:T(8,128)(2,1)S(1)} %collective-permute-done.5.p0), channel_id=1, source_target_pairs={{0,2},{2,0},{1,3},{3,1},{4,6},{6,4},{5,7},{7,5},{8,10},{10,8},{9,1... | collective-permute-start | bytes 983048 | tf_op jit(solution)/shard_map/ppermute | solution.py:281
  42.9 2.4 %collective-permute-start.15 = (bf16[640,256]{1,0:T(8,128)(2,1)S(1)}, bf16[640,256]{1,0:T(8,128)(2,1)S(1)}, u32[]{:S(2)}, u32[]{:S(2)}) collective-permute-start(bf16[640,256]{1,0:T(8,128)(2,1)S(1)} %get-tuple-element.78), channel_id=1, source_target_pairs={{0,2},{1,10},{2,3},{3,11},{4,4},{5,12},{6,5},{7,13},{8,6},{9,14},{... | collective-permute-start | bytes 983048 | tf_op jit(solution)/shard_map/ppermute | solution.py:305
  45.5 5.4 %collective-permute-done.12.refs_7_ = bf16[640,256]{1,0:T(8,128)(2,1)S(1)} collective-permute-done((bf16[640,256]{1,0:T(8,128)(2,1)S(1)}, bf16[640,256]{1,0:T(8,128)(2,1)S(1)}, u32[]{:S(2)}, u32[]{:S(2)}) %collective-permute-start.12) | collective-permute-done | bytes 327712 | tf_op jit(solution)/shard_map/ppermute | solution.py:281
  50.9 2.4 %collective-permute-done.9.p1 = bf16[640,256]{1,0:T(8,128)(2,1)S(1)} collective-permute-done((bf16[640,256]{1,0:T(8,128)(2,1)S(1)}, bf16[640,256]{1,0:T(8,128)(2,1)S(1)}, u32[]{:S(2)}, u32[]{:S(2)}) %collective-permute-start.9) | collective-permute-done | bytes 327712 | tf_op jit(solution)/shard_map/ppermute | solution.py:281
  53.2 1.0 collective-permute-start.14
  54.3 4.6 %collective-permute-start.17 = (bf16[640,256]{1,0:T(8,128)(2,1)S(1)}, bf16[640,256]{1,0:T(8,128)(2,1)S(1)}, u32[]{:S(2)}, u32[]{:S(2)}) collective-permute-start(bf16[640,256]{1,0:T(8,128)(2,1)S(1)} %get-tuple-element.85), channel_id=1, source_target_pairs={{0,6},{1,14},{2,7},{3,15},{4,0},{5,8},{6,1},{7,9},{8,2},{9,10},{10... | collective-permute-start | bytes 983048 | tf_op jit(solution)/shard_map/ppermute | solution.py:305
  59.8 1.5 %project.1.sums_ref = f32[2,256,256]{2,1,0:T(8,128)S(1)} custom-call(bf16[256,2560]{1,0:T(8,128)(2,1)S(1)} %get-tuple-element.60.own_ref, bf16[256,2560]{1,0:T(8,128)(2,1)S(1)} %collective-permute-done.8.other_ref, bf16[2,1280,256]{2,1,0:T(8,128)(2,1)S(1)} %copy-done.1, bf16[640,256]{1,0:T(8,128)(2,1)S(1)} %collective-permute-done.refs_0_, ...), custom_call_target="tpu_custom_call" | custom-call | flops 1006632960 | bytes 7000000 | tf_op jit(solution)/shard_map/project/pallas_call | solution.py:91
  61.3 15.7 %collective-permute-done.16 = bf16[640,256]{1,0:T(8,128)(2,1)S(1)} collective-permute-done((bf16[640,256]{1,0:T(8,128)(2,1)S(1)}, bf16[640,256]{1,0:T(8,128)(2,1)S(1)}, u32[]{:S(2)}, u32[]{:S(2)}) %collective-permute-start.16) | collective-permute-done | bytes 327712 | tf_op jit(solution)/shard_map/ppermute | solution.py:305
  76.9 5.1 %attention.1 = (bf16[256,1280]{1,0:T(8,128)(2,1)}, bf16[256,512]{1,0:T(8,128)(2,1)S(1)}) custom-call(bf16[256,2560]{1,0:T(8,128)(2,1)S(1)} %get-tuple-element.60.own_ref, bf16[256,2560]{1,0:T(8,128)(2,1)S(1)} %collective-permute-done.8.other_ref, bf16[640,256]{1,0:T(8,128)(2,1)S(1)} %collective-permute-done.5.p0, ...), custom_call_target="tpu_custom_call" | custom-call | flops 838860800 | bytes 5000000 | tf_op jit(solution)/shard_map/attention/pallas_call | solution.py:165
  82.0 9.0 %collective-permute-done.18.refs_15_ = bf16[256,512]{1,0:T(8,128)(2,1)S(1)} collective-permute-done((bf16[256,512]{1,0:T(8,128)(2,1)S(1)}, bf16[256,512]{1,0:T(8,128)(2,1)S(1)}, u32[]{:S(2)}, u32[]{:S(2)}) %collective-permute-start.18) | collective-permute-done | bytes 262176 | tf_op jit(solution)/shard_map/ppermute | solution.py:286
  91.2 1.9 %collective-permute-start.20 = (bf16[4,640,256]{2,1,0:T(8,128)(2,1)S(1)}, bf16[4,640,256]{2,1,0:T(8,128)(2,1)S(1)}, u32[]{:S(2)}, u32[]{:S(2)}) collective-permute-start(bf16[4,640,256]{2,1,0:T(8,128)(2,1)S(1)} %pad_maximum_fusion.refs_1_.refs_2_.refs_3_.refs_4_.refs_5_.refs_6_), channel_id=1, source_target_pairs={{0,1},{1,0},{2,3},{3,2},{4,5},{5,4},{6,7},{7,6},{8,9},{9,8},{10,11... | collective-permute-start | bytes 3932168 | tf_op jit(solution)/shard_map/ppermute | solution.py:281
  93.1 2.0 %collective-permute-start.21 = (bf16[256,512]{1,0:T(8,128)(2,1)S(1)}, bf16[256,512]{1,0:T(8,128)(2,1)S(1)}, u32[]{:S(2)}, u32[]{:S(2)}) collective-permute-start(bf16[256,512]{1,0:T(8,128)(2,1)S(1)} %get-tuple-element.95.refs_13_), channel_id=1, source_target_pairs={{0,12},{4,0},{8,4},{12,8},{1,13},{5,1},{9,5},{13,9},{2,14},{6,2},{... | collective-permute-start | bytes 786440 | tf_op jit(solution)/shard_map/ppermute | solution.py:286
  95.8 5.6 %collective-permute-done.21.refs_16_ = bf16[256,512]{1,0:T(8,128)(2,1)S(1)} collective-permute-done((bf16[256,512]{1,0:T(8,128)(2,1)S(1)}, bf16[256,512]{1,0:T(8,128)(2,1)S(1)}, u32[]{:S(2)}, u32[]{:S(2)}) %collective-permute-start.21) | collective-permute-done | bytes 262176 | tf_op jit(solution)/shard_map/ppermute | solution.py:286
  101.4 1.7 %collective-permute-done.22.refs_17_ = bf16[256,512]{1,0:T(8,128)(2,1)S(1)} collective-permute-done((bf16[256,512]{1,0:T(8,128)(2,1)S(1)}, bf16[256,512]{1,0:T(8,128)(2,1)S(1)}, u32[]{:S(2)}, u32[]{:S(2)}) %collective-permute-start.22) | collective-permute-done | bytes 262176 | tf_op jit(solution)/shard_map/ppermute | solution.py:281
  105.2 7.6 %collective-permute-done.23.refs_5_ = bf16[256,512]{1,0:T(8,128)(2,1)} collective-permute-done((bf16[256,512]{1,0:T(8,128)(2,1)S(1)}, bf16[256,512]{1,0:T(8,128)(2,1)}, u32[]{:S(2)}, u32[]{:S(2)}) %collective-permute-start.23) | collective-permute-done | bytes 262176 | tf_op jit(solution)/shard_map/ppermute | solution.py:286
  114.4 1.0 copy-done.5
  117.2 2.3 %gradient.2 = (f32[2,640,256]{2,1,0:T(8,128)S(1)}, f32[2,256]{1,0:T(2,128)S(1)}) custom-call(s32[6]{0:T(128)S(1)} %stack.59.refs_0_, bf16[4,640,256]{2,1,0:T(8,128)(2,1)S(1)} %pad_maximum_fusion.refs_1_.refs_2_.refs_3_.refs_4_.refs_5_.refs_6_, bf16[4,640,256]{2,1,0:T(8,128)(2,1)S(1)} %pad_maximum_fusion.refs_1_.refs_2_.refs_3_.refs_4_.refs_5_.refs_6_, ...), custom_call_target="tpu_custom_call" | custom-call | flops 1006632960 | bytes 5000000 | tf_op jit(solution)/shard_map/gradient/pallas_call | solution.py:225
  120.2 3.3 %gradient.3 = (f32[2,640,256]{2,1,0:T(8,128)}, f32[2,256]{1,0:T(2,128)}) custom-call(s32[2]{0:T(128)S(1)} %pad_add_fusion.refs_0_, bf16[4,640,256]{2,1,0:T(8,128)(2,1)S(1)} %pad_maximum_fusion.refs_1_.refs_2_.refs_3_.refs_4_.refs_5_.refs_6_, bf16[4,640,256]{2,1,0:T(8,128)(2,1)S(1)} %pad_maximum_fusion.refs_1_.refs_2_.refs_3_.refs_4_.refs_5_.refs_6_, ...), custom_call_target="tpu_custom_call" | custom-call | flops 335544320 | bytes 5000000 | tf_op jit(solution)/shard_map/gradient/pallas_call | solution.py:225
  (63 shorter events, 12.4 us)
Async XLA Ops:
  0.6 7.3 %copy-start = (bf16[256,2560]{1,0:T(8,128)(2,1)S(1)}, bf16[256,2560]{1,0:T(8,128)(2,1)}, u32[]{:S(2)}) copy-start(bf16[256,2560]{1,0:T(8,128)(2,1)} %values_ref.1) | copy-start | bytes 3932164
  0.6 5.9 %copy-start.10 = (bf16[5120]{0:T(1024)(128)(2,1)S(1)}, bf16[5120]{0:T(1024)(128)(2,1)}, u32[]{:S(2)}) copy-start(bf16[5120]{0:T(1024)(128)(2,1)} %param.7) | copy-start | bytes 30724
  1.8 12.8 %collective-permute-start = (bf16[640,256]{1,0:T(8,128)(2,1)S(1)}, bf16[640,256]{1,0:T(8,128)(2,1)S(1)}, u32[]{:S(2)}, u32[]{:S(2)}) collective-permute-start(bf16[640,256]{1,0:T(8,128)(2,1)S(1)} %dynamic-slice_bitcast_fusion), channel_id=1, source_target_pairs={{0,4},{4,8},{8,12},{12,0},{1,5},{5,9},{9,13},{13,1},{2,6},{6,10},{... | collective-permute-start | bytes 983048 | tf_op jit(solution)/shard_map/ppermute | solution.py:286
  6.5 53.1 %copy-start.11 = (bf16[2,256]{1,0:T(2,128)(2,1)S(1)}, bf16[2,256]{1,0:T(2,128)(2,1)}, u32[]{:S(2)}) copy-start(bf16[2,256]{1,0:T(2,128)(2,1)} %param.11) | copy-start | bytes 3076
  6.5 1.2 collective-permute-start.1
  7.9 51.9 %copy-start.1 = (bf16[2,1280,256]{2,1,0:T(8,128)(2,1)S(1)}, bf16[2,1280,256]{2,1,0:T(8,128)(2,1)}, u32[]{:S(2)}) copy-start(bf16[2,1280,256]{2,1,0:T(8,128)(2,1)} %weight_ref.1) | copy-start | bytes 3932164
  14.6 23.2 %collective-permute-start.8 = (bf16[256,2560]{1,0:T(8,128)(2,1)S(1)}, bf16[256,2560]{1,0:T(8,128)(2,1)S(1)}, u32[]{:S(2)}, u32[]{:S(2)}) collective-permute-start(bf16[256,2560]{1,0:T(8,128)(2,1)S(1)} %get-tuple-element.60.own_ref), channel_id=1, source_target_pairs={{0,1},{1,0},{2,3},{3,2},{4,5},{5,4},{6,7},{7,6},{8,9},{9,8},{10,11... | collective-permute-start | bytes 3932168 | tf_op jit(solution)/shard_map/ppermute | solution.py:281
  14.6 10.1 %collective-permute-start.2 = (bf16[640,256]{1,0:T(8,128)(2,1)S(1)}, bf16[640,256]{1,0:T(8,128)(2,1)S(1)}, u32[]{:S(2)}, u32[]{:S(2)}) collective-permute-start(bf16[640,256]{1,0:T(8,128)(2,1)S(1)} %collective-permute-done.refs_0_), channel_id=1, source_target_pairs={{0,2},{2,0},{1,3},{3,1},{4,6},{6,4},{5,7},{7,5},{8,10},{10,8},{9,1... | collective-permute-start | bytes 983048 | tf_op jit(solution)/shard_map/ppermute | solution.py:281
  16.1 9.8 %collective-permute-start.3 = (bf16[640,256]{1,0:T(8,128)(2,1)S(1)}, bf16[640,256]{1,0:T(8,128)(2,1)S(1)}, u32[]{:S(2)}, u32[]{:S(2)}) collective-permute-start(bf16[640,256]{1,0:T(8,128)(2,1)S(1)} %collective-permute-done.refs_0_), channel_id=1, source_target_pairs={{0,16},{16,0},{1,17},{17,1},{2,18},{18,2},{3,19},{19,3},{4,20},{20... | collective-permute-start | bytes 983048 | tf_op jit(solution)/shard_map/ppermute | solution.py:281
  17.6 9.6 %collective-permute-start.4 = (bf16[640,256]{1,0:T(8,128)(2,1)S(1)}, bf16[640,256]{1,0:T(8,128)(2,1)S(1)}, u32[]{:S(2)}, u32[]{:S(2)}) collective-permute-start(bf16[640,256]{1,0:T(8,128)(2,1)S(1)} %dynamic-slice_bitcast_fusion), channel_id=1, source_target_pairs={{0,12},{4,0},{8,4},{12,8},{1,13},{5,1},{9,5},{13,9},{2,14},{6,2},{... | collective-permute-start | bytes 983048 | tf_op jit(solution)/shard_map/ppermute | solution.py:286
  27.2 10.5 %collective-permute-start.5 = (bf16[640,256]{1,0:T(8,128)(2,1)S(1)}, bf16[640,256]{1,0:T(8,128)(2,1)S(1)}, u32[]{:S(2)}, u32[]{:S(2)}) collective-permute-start(bf16[640,256]{1,0:T(8,128)(2,1)S(1)} %collective-permute-done.refs_0_), channel_id=1, source_target_pairs={{0,4},{4,8},{8,12},{12,0},{1,5},{5,9},{9,13},{13,1},{2,6},{6,10},{... | collective-permute-start | bytes 983048 | tf_op jit(solution)/shard_map/ppermute | solution.py:286
  27.2 10.6 %collective-permute-start.6 = (bf16[640,256]{1,0:T(8,128)(2,1)S(1)}, bf16[640,256]{1,0:T(8,128)(2,1)S(1)}, u32[]{:S(2)}, u32[]{:S(2)}) collective-permute-start(bf16[640,256]{1,0:T(8,128)(2,1)S(1)} %collective-permute-done.4.refs_4_), channel_id=1, source_target_pairs={{0,2},{2,0},{1,3},{3,1},{4,6},{6,4},{5,7},{7,5},{8,10},{10,8},{9,1... | collective-permute-start | bytes 983048 | tf_op jit(solution)/shard_map/ppermute | solution.py:281
  27.7 10.1 %collective-permute-start.7 = (bf16[640,256]{1,0:T(8,128)(2,1)S(1)}, bf16[640,256]{1,0:T(8,128)(2,1)S(1)}, u32[]{:S(2)}, u32[]{:S(2)}) collective-permute-start(bf16[640,256]{1,0:T(8,128)(2,1)S(1)} %collective-permute-done.4.refs_4_), channel_id=1, source_target_pairs={{0,16},{16,0},{1,17},{17,1},{2,18},{18,2},{3,19},{19,3},{4,20},{20... | collective-permute-start | bytes 983048 | tf_op jit(solution)/shard_map/ppermute | solution.py:281
  28.2 14.7 %collective-permute-start.11 = (bf16[640,256]{1,0:T(8,128)(2,1)S(1)}, bf16[640,256]{1,0:T(8,128)(2,1)S(1)}, u32[]{:S(2)}, u32[]{:S(2)}) collective-permute-start(bf16[640,256]{1,0:T(8,128)(2,1)S(1)} %collective-permute-done.3.refs_2_), channel_id=1, source_target_pairs={{0,2},{2,0},{1,3},{3,1},{4,6},{6,4},{5,7},{7,5},{8,10},{10,8},{9,1... | collective-permute-start | bytes 983048 | tf_op jit(solution)/shard_map/ppermute | solution.py:281
  37.8 7.7 %collective-permute-start.10 = (bf16[640,256]{1,0:T(8,128)(2,1)S(1)}, bf16[640,256]{1,0:T(8,128)(2,1)S(1)}, u32[]{:S(2)}, u32[]{:S(2)}) collective-permute-start(bf16[640,256]{1,0:T(8,128)(2,1)S(1)} %collective-permute-done.5.p0), channel_id=1, source_target_pairs={{0,16},{16,0},{1,17},{17,1},{2,18},{18,2},{3,19},{19,3},{4,20},{20... | collective-permute-start | bytes 983048 | tf_op jit(solution)/shard_map/ppermute | solution.py:281
  38.4 7.0 %collective-permute-start.13 = (bf16[640,256]{1,0:T(8,128)(2,1)S(1)}, bf16[640,256]{1,0:T(8,128)(2,1)S(1)}, u32[]{:S(2)}, u32[]{:S(2)}) collective-permute-start(bf16[640,256]{1,0:T(8,128)(2,1)S(1)} %get-tuple-element.70), channel_id=1, source_target_pairs={{0,0},{1,8},{2,1},{3,9},{4,2},{5,10},{6,3},{7,11},{8,4},{9,12},{10... | collective-permute-start | bytes 983048 | tf_op jit(solution)/shard_map/ppermute | solution.py:305
  39.0 11.8 %collective-permute-start.12 = (bf16[640,256]{1,0:T(8,128)(2,1)S(1)}, bf16[640,256]{1,0:T(8,128)(2,1)S(1)}, u32[]{:S(2)}, u32[]{:S(2)}) collective-permute-start(bf16[640,256]{1,0:T(8,128)(2,1)S(1)} %collective-permute-done.6.refs_5_), channel_id=1, source_target_pairs={{0,16},{16,0},{1,17},{17,1},{2,18},{18,2},{3,19},{19,3},{4,20},{20... | collective-permute-start | bytes 983048 | tf_op jit(solution)/shard_map/ppermute | solution.py:281
  40.6 12.7 %collective-permute-start.9 = (bf16[640,256]{1,0:T(8,128)(2,1)S(1)}, bf16[640,256]{1,0:T(8,128)(2,1)S(1)}, u32[]{:S(2)}, u32[]{:S(2)}) collective-permute-start(bf16[640,256]{1,0:T(8,128)(2,1)S(1)} %collective-permute-done.5.p0), channel_id=1, source_target_pairs={{0,2},{2,0},{1,3},{3,1},{4,6},{6,4},{5,7},{7,5},{8,10},{10,8},{9,1... | collective-permute-start | bytes 983048 | tf_op jit(solution)/shard_map/ppermute | solution.py:281
  42.9 18.4 %collective-permute-start.15 = (bf16[640,256]{1,0:T(8,128)(2,1)S(1)}, bf16[640,256]{1,0:T(8,128)(2,1)S(1)}, u32[]{:S(2)}, u32[]{:S(2)}) collective-permute-start(bf16[640,256]{1,0:T(8,128)(2,1)S(1)} %get-tuple-element.78), channel_id=1, source_target_pairs={{0,2},{1,10},{2,3},{3,11},{4,4},{5,12},{6,5},{7,13},{8,6},{9,14},{... | collective-permute-start | bytes 983048 | tf_op jit(solution)/shard_map/ppermute | solution.py:305
  53.2 23.7 %collective-permute-start.14 = (bf16[640,256]{1,0:T(8,128)(2,1)S(1)}, bf16[640,256]{1,0:T(8,128)(2,1)S(1)}, u32[]{:S(2)}, u32[]{:S(2)}) collective-permute-start(bf16[640,256]{1,0:T(8,128)(2,1)S(1)} %collective-permute-done.9.p1), channel_id=1, source_target_pairs={{0,16},{16,0},{1,17},{17,1},{2,18},{18,2},{3,19},{19,3},{4,20},{20... | collective-permute-start | bytes 983048 | tf_op jit(solution)/shard_map/ppermute | solution.py:281
  54.3 27.8 %collective-permute-start.17 = (bf16[640,256]{1,0:T(8,128)(2,1)S(1)}, bf16[640,256]{1,0:T(8,128)(2,1)S(1)}, u32[]{:S(2)}, u32[]{:S(2)}) collective-permute-start(bf16[640,256]{1,0:T(8,128)(2,1)S(1)} %get-tuple-element.85), channel_id=1, source_target_pairs={{0,6},{1,14},{2,7},{3,15},{4,0},{5,8},{6,1},{7,9},{8,2},{9,10},{10... | collective-permute-start | bytes 983048 | tf_op jit(solution)/shard_map/ppermute | solution.py:305
  58.8 18.1 %collective-permute-start.16 = (bf16[640,256]{1,0:T(8,128)(2,1)S(1)}, bf16[640,256]{1,0:T(8,128)(2,1)S(1)}, u32[]{:S(2)}, u32[]{:S(2)}) collective-permute-start(bf16[640,256]{1,0:T(8,128)(2,1)S(1)} %get-tuple-element.80), channel_id=1, source_target_pairs={{0,4},{1,12},{2,5},{3,13},{4,6},{5,14},{6,7},{7,15},{8,0},{9,8},{1... | collective-permute-start | bytes 983048 | tf_op jit(solution)/shard_map/ppermute | solution.py:305
  59.8 17.2 %copy-start.2 = (bf16[256,1280]{1,0:T(8,128)(2,1)S(1)}, bf16[256,1280]{1,0:T(8,128)(2,1)}, u32[]{:S(2)}) copy-start(bf16[256,1280]{1,0:T(8,128)(2,1)} %queries_ref.1) | copy-start | bytes 1966084
  59.8 17.2 %copy-start.3 = (bf16[256,1280]{1,0:T(8,128)(2,1)S(1)}, bf16[256,1280]{1,0:T(8,128)(2,1)}, u32[]{:S(2)}) copy-start(bf16[256,1280]{1,0:T(8,128)(2,1)} %cotangent_ref.1) | copy-start | bytes 1966084
  82.0 9.0 %collective-permute-start.18 = (bf16[256,512]{1,0:T(8,128)(2,1)S(1)}, bf16[256,512]{1,0:T(8,128)(2,1)S(1)}, u32[]{:S(2)}, u32[]{:S(2)}) collective-permute-start(bf16[256,512]{1,0:T(8,128)(2,1)S(1)} %get-tuple-element.95.refs_13_), channel_id=1, source_target_pairs={{0,4},{4,8},{8,12},{12,0},{1,5},{5,9},{9,13},{13,1},{2,6},{6,10},{... | collective-permute-start | bytes 786440 | tf_op jit(solution)/shard_map/ppermute | solution.py:286
  82.0 9.0 %collective-permute-start.19 = (bf16[256,512]{1,0:T(8,128)(2,1)S(1)}, bf16[256,512]{1,0:T(8,128)(2,1)S(1)}, u32[]{:S(2)}, u32[]{:S(2)}) collective-permute-start(bf16[256,512]{1,0:T(8,128)(2,1)S(1)} %get-tuple-element.95.refs_13_), channel_id=1, source_target_pairs={{0,2},{2,0},{1,3},{3,1},{4,6},{6,4},{5,7},{7,5},{8,10},{10,8},{9,1... | collective-permute-start | bytes 786440 | tf_op jit(solution)/shard_map/ppermute | solution.py:281
  91.2 23.2 %collective-permute-start.20 = (bf16[4,640,256]{2,1,0:T(8,128)(2,1)S(1)}, bf16[4,640,256]{2,1,0:T(8,128)(2,1)S(1)}, u32[]{:S(2)}, u32[]{:S(2)}) collective-permute-start(bf16[4,640,256]{2,1,0:T(8,128)(2,1)S(1)} %pad_maximum_fusion.refs_1_.refs_2_.refs_3_.refs_4_.refs_5_.refs_6_), channel_id=1, source_target_pairs={{0,1},{1,0},{2,3},{3,2},{4,5},{5,4},{6,7},{7,6},{8,9},{9,8},{10,11... | collective-permute-start | bytes 3932168 | tf_op jit(solution)/shard_map/ppermute | solution.py:281
  93.1 8.3 %collective-permute-start.21 = (bf16[256,512]{1,0:T(8,128)(2,1)S(1)}, bf16[256,512]{1,0:T(8,128)(2,1)S(1)}, u32[]{:S(2)}, u32[]{:S(2)}) collective-permute-start(bf16[256,512]{1,0:T(8,128)(2,1)S(1)} %get-tuple-element.95.refs_13_), channel_id=1, source_target_pairs={{0,12},{4,0},{8,4},{12,8},{1,13},{5,1},{9,5},{13,9},{2,14},{6,2},{... | collective-permute-start | bytes 786440 | tf_op jit(solution)/shard_map/ppermute | solution.py:286
  95.1 8.0 %collective-permute-start.22 = (bf16[256,512]{1,0:T(8,128)(2,1)S(1)}, bf16[256,512]{1,0:T(8,128)(2,1)S(1)}, u32[]{:S(2)}, u32[]{:S(2)}) collective-permute-start(bf16[256,512]{1,0:T(8,128)(2,1)S(1)} %collective-permute-done.18.refs_15_), channel_id=1, source_target_pairs={{0,2},{2,0},{1,3},{3,1},{4,6},{6,4},{5,7},{7,5},{8,10},{10,8},{9,1... | collective-permute-start | bytes 786440 | tf_op jit(solution)/shard_map/ppermute | solution.py:281
  103.8 9.0 %collective-permute-start.23 = (bf16[256,512]{1,0:T(8,128)(2,1)S(1)}, bf16[256,512]{1,0:T(8,128)(2,1)}, u32[]{:S(2)}, u32[]{:S(2)}) collective-permute-start(bf16[256,512]{1,0:T(8,128)(2,1)S(1)} %collective-permute-done.18.refs_15_), channel_id=1, source_target_pairs={{0,4},{4,8},{8,12},{12,0},{1,5},{5,9},{9,13},{13,1},{2,6},{6,10},{... | collective-permute-start | bytes 786440 | tf_op jit(solution)/shard_map/ppermute | solution.py:286
  103.8 9.0 %collective-permute-start.24 = (bf16[256,512]{1,0:T(8,128)(2,1)S(1)}, bf16[256,512]{1,0:T(8,128)(2,1)S(1)}, u32[]{:S(2)}, u32[]{:S(2)}) collective-permute-start(bf16[256,512]{1,0:T(8,128)(2,1)S(1)} %collective-permute-done.21.refs_16_), channel_id=1, source_target_pairs={{0,2},{2,0},{1,3},{3,1},{4,6},{6,4},{5,7},{7,5},{8,10},{10,8},{9,1... | collective-permute-start | bytes 786440 | tf_op jit(solution)/shard_map/ppermute | solution.py:281
  113.5 6.7 %collective-permute-start.25 = (bf16[256,512]{1,0:T(8,128)(2,1)}, bf16[256,512]{1,0:T(8,128)(2,1)}, u32[]{:S(2)}, u32[]{:S(2)}) collective-permute-start(bf16[256,512]{1,0:T(8,128)(2,1)} %collective-permute-done.23.refs_5_), channel_id=1, source_target_pairs={{0,2},{2,0},{1,3},{3,1},{4,6},{6,4},{5,7},{7,5},{8,10},{10,8},{9,1... | collective-permute-start | bytes 786440 | tf_op jit(solution)/shard_map/ppermute | solution.py:281
  (6 other events, 5.0 us)

commit v10 on v9

--- a/solution.py
+++ b/solution.py
@@ -181,16 +181,18 @@
     )(*operands)
 
 
-def gradient_kernel(count, first, halves, *refs):
-    at_ref = refs[0]
-    own, other, pairs = (refs[1 + i * count : 1 + (i + 1) * count] for i in range(3))
-    refs = refs[1 + 3 * count :]
+def gradient_kernel(sources, first, *refs):
+    count = len(sources)
+    own, other, pairs = (refs[i * count : (i + 1) * count] for i in range(3))
+    refs = refs[3 * count :]
     weight_ref, bias_ref = refs[-2:]
     columns = weight_ref.shape[2]
+    core, cores_blocks = lax.axis_index("sub"), lax.axis_size("blk") // 2
     total = None
-    for turn, pair in enumerate(pairs):
-        slab = jnp.where(at_ref[turn] < halves, own[turn][0], other[turn][0])
-        term = product(slab, pair[...])
+    for at, (distance, _) in enumerate(sources):
+        here = lax.div(block_from(distance), cores_blocks) == core
+        slab = jnp.where(here, own[at][0], other[at][0])
+        term = product(slab, pairs[at][...])
         total = term if total is None else total + term
     for j in range(2):
         part = total[:, j * columns : (j + 1) * columns]
@@ -207,29 +209,29 @@
             bias_ref[j : j + 1, :] = part if first else refs[1][j : j + 1, :] + part
 
 
-def gradient(at, own, other, pairs, sums):
-    halves, share, length = own.shape
+def gradient(slabs, some, sums):
+    pairs = list(some.values())
+    _, share, length = slabs[0][0].shape
     columns = pairs[0].shape[1] // 2
     count = len(pairs)
     tile = share // 2 if share % 32 == 0 else share
 
-    def slab_spec(turn):
-        return pl.BlockSpec((1, tile, length), lambda i, at: (at[turn] % halves, i, 0))
-
-    weight_spec = pl.BlockSpec((2, tile, columns), lambda i, at: (0, i, 0))
-    bias_spec = pl.BlockSpec((2, columns), lambda i, at: (0, 0))
-    in_specs = [slab_spec(turn) for turn in range(count)] * 2
-    in_specs += [pl.BlockSpec((length, 2 * columns), lambda i, at: (0, 0))] * count
+    def slab_spec(same):
+        return pl.BlockSpec((1, tile, length), lambda i: (0 if same else 1, i, 0))
+
+    weight_spec = pl.BlockSpec((2, tile, columns), lambda i: (0, i, 0))
+    bias_spec = pl.BlockSpec((2, columns), lambda i: (0, 0))
+    in_specs = [slab_spec(same) for _, same in some] * 2
+    in_specs += [pl.BlockSpec((length, 2 * columns), lambda i: (0, 0))] * count
     if sums:
         in_specs += [weight_spec, bias_spec]
+    own = [slabs[distance % 2][0] for distance, _ in some]
+    other = [slabs[distance % 2][1] for distance, _ in some]
     return pl.pallas_call(
-        functools.partial(gradient_kernel, count, sums is None, halves),
-        grid_spec=pltpu.PrefetchScalarGridSpec(
-            num_scalar_prefetch=1,
-            grid=(share // tile,),
-            in_specs=in_specs,
-            out_specs=[weight_spec, bias_spec],
-        ),
+        functools.partial(gradient_kernel, tuple(some), sums is None),
+        grid=(share // tile,),
+        in_specs=in_specs,
+        out_specs=[weight_spec, bias_spec],
         out_shape=[
             jax.ShapeDtypeStruct((2, share, columns), jnp.float32),
             jax.ShapeDtypeStruct((2, columns), jnp.float32),
@@ -239,42 +241,60 @@
             flops=4 * count * length * share * columns, bytes_accessed=5000000, transcendentals=0
         ),
         name="gradient",
-    )(at, *([own] * count), *([other] * count), *pairs, *(sums or ()))
-
-
-def norm_kernel(values_ref, scale_ref, gain_ref, normed_ref, *slab_refs):
-    blocks, replicas = lax.axis_size("blk"), lax.axis_size("dp")
-    number = lax.axis_index("blk") * replicas + lax.axis_index("dp")
-    half = blocks * replicas // 2
-    share = values_ref.shape[1] // half
+    )(*own, *other, *pairs, *(sums or ()))
+
+
+def norm_kernel(values_ref, scale_ref, gain_ref, normed_ref, kept_ref, sent_ref):
+    replica, replicas = lax.axis_index("dp"), lax.axis_size("dp")
+    share = kept_ref.shape[1]
 
     def scaled(place):
         wide_values = values_ref[:, place].astype(jnp.float32)
         return wide_values * scale_ref[...] * gain_ref[:, place]
 
-    for slab in range(half):
+    for slab in range(2 * replicas):
         place = pl.ds(slab * share, share)
         normed_ref[:, place] = scaled(place).astype(jnp.bfloat16)
-    for turn, slab_ref in enumerate(slab_refs):
-        slab = lax.rem(turn + number // 2, half)
-        place = pl.ds(pl.multiple_of(slab * share, 128), share)
-        slab_ref[...] = scaled(place).T.astype(jnp.bfloat16)
-
-
-def norm(activations, scale, gain, slabs):
+    for at in range(2):
+        for ref, owner in ((kept_ref, replica), (sent_ref, 1 - replica)):
+            place = pl.ds(pl.multiple_of((at * replicas + owner) * share, 128), share)
+            ref[at] = scaled(place).T.astype(jnp.bfloat16)
+
+
+def norm(activations, scale, gain, share):
     length, features = activations.shape
+    shapes = [activations.shape, (2, share, length), (2, share, length)]
     return pl.pallas_call(
         norm_kernel,
         in_specs=[IN_VMEM] * 3,
-        out_specs=[IN_VMEM] * (1 + slabs),
-        out_shape=[jax.ShapeDtypeStruct(activations.shape, jnp.bfloat16)]
-        + [jax.ShapeDtypeStruct((features // slabs, length), jnp.bfloat16)] * slabs,
+        out_specs=[IN_VMEM] * 3,
+        out_shape=[jax.ShapeDtypeStruct(shape, jnp.bfloat16) for shape in shapes],
         compiler_params=pltpu.CompilerParams(vmem_limit_bytes=VMEM_BYTES),
         cost_estimate=pl.CostEstimate(
             flops=4 * length * features, bytes_accessed=6 * length * features, transcendentals=0
         ),
         name="norm",
     )(activations, scale, gain)
+
+
+def pack_kernel(kept_ref, arrived_ref, even_ref, odd_ref):
+    parity = lax.rem(lax.axis_index("blk"), 2)
+    for turn, ref in enumerate((even_ref, odd_ref)):
+        at = lax.rem(turn + parity, 2)
+        ref[0] = kept_ref[at]
+        ref[1] = arrived_ref[at]
+
+
+def pack(kept, arrived):
+    return pl.pallas_call(
+        pack_kernel,
+        in_specs=[IN_VMEM] * 2,
+        out_specs=[IN_VMEM] * 2,
+        out_shape=[jax.ShapeDtypeStruct(kept.shape, kept.dtype)] * 2,
+        compiler_params=pltpu.CompilerParams(vmem_limit_bytes=VMEM_BYTES),
+        cost_estimate=pl.CostEstimate(flops=0, bytes_accessed=2600000, transcendentals=0),
+        name="pack",
+    )(kept, arrived)
 
 
 def swapped(block, axis):
@@ -303,6 +323,15 @@
 
 def sent_slab(slab, turn):
     return lax.ppermute(slab, ("blk", "dp", "sub"), slab_route(turn))
+
+
+def sent_along(slabs, turn):
+    route = [
+        (block * 2 + core, (2 * core + (turn + block) % 2) * 2 + block // 2)
+        for block in range(4)
+        for core in range(2)
+    ]
+    return lax.ppermute(slabs, ("blk", "sub"), route)
 
 
 def scale_and_gain(activations, norm_gain):
@@ -337,45 +366,38 @@
         )
 
     up = turned(piece, "blk", 1)
-    normed, *slabs = norm(activations, scale, gain[None, :], half)
-    up, piece, normed, slabs = lax.optimization_barrier((up, piece, normed, slabs))
+    normed, kept, sent = norm(activations, scale, gain[None, :], share)
+    up, piece, normed, kept, sent = lax.optimization_barrier((up, piece, normed, kept, sent))
     up_x, up_y, down = swapped(up, "dp"), swapped(up, "groups"), turned(piece, "blk", -1)
+    arrived = swapped(sent, "dp")
     normed_other = swapped(normed, "sub")
-    up, up_x, up_y, down = lax.optimization_barrier((up, up_x, up_y, down))
+    up, up_y, down, normed_other = lax.optimization_barrier((up, up_y, down, normed_other))
     down_x, down_y = swapped(down, "dp"), swapped(down, "groups")
     twice = turned(up, "blk", 1)
-    up_both = swapped(up_y, "dp")
-    twice, down_x, down_y, normed_other = lax.optimization_barrier(
-        (twice, down_x, down_y, normed_other)
-    )
+    twice, down_y, up_x, arrived = lax.optimization_barrier((twice, down_y, up_x, arrived))
     twice_x, twice_y = swapped(twice, "dp"), swapped(twice, "groups")
-    down_both = swapped(down_x, "groups")
-    slabs[:2] = [sent_slab(after(slabs[turn], twice), turn) for turn in (0, 1)]
-    twice_x, twice_y, up_both, down_both, slabs[0] = lax.optimization_barrier(
-        (twice_x, twice_y, up_both, down_both, slabs[0])
-    )
-    twice_both = swapped(twice_x, "groups")
+    up_both = swapped(up_x, "groups")
+    even, odd = pack(kept, arrived)
+    even = sent_along(even, 0)
+    twice_x, twice_y, up_both, down_x, even = lax.optimization_barrier(
+        (twice_x, twice_y, up_both, down_x, even)
+    )
+    down_both, twice_both = swapped(down_x, "groups"), swapped(twice_y, "dp")
+    odd = sent_along(after(odd, even), 1)
 
     gathered = [(1, (up, up_x, up_y, up_both)), (-1, (down, down_x, down_y, down_both))]
     sums = project(normed, normed_other, kv_weight, gathered)
-    slabs[2:] = [sent_slab(after(slabs[turn], twice_x), turn) for turn in (2, 3)]
-    sums, slabs[1], slabs[2] = lax.optimization_barrier((sums, slabs[1], slabs[2]))
     grad_query, grad_pair = attention(
         2, normed, normed_other, (twice, twice_x, twice_y, twice_both), sums, bias, cosine, sine,
         queries, cotangent,
     )
 
-    def slab_of(distance, same):
-        from_replica = replica if same else 1 - replica
-        return (slab_here - (block - distance)) % half + half * (from_replica != core)
-
-    grad_pair, slabs[3] = lax.optimization_barrier((grad_pair, slabs[3]))
+    grad_pair, odd = lax.optimization_barrier((grad_pair, odd))
     pair_up, pair_x = turned(grad_pair, "blk", 1), swapped(grad_pair, "dp")
-    pair_up, pair_x, grad_pair, *slabs = lax.optimization_barrier(
-        (pair_up, pair_x, grad_pair, *slabs)
-    )
-    slabs_own = jnp.stack(slabs)
-    slabs_other = swapped(slabs_own, "sub")
+    pair_up, pair_x, grad_pair, even, odd = lax.optimization_barrier(
+        (pair_up, pair_x, grad_pair, even, odd)
+    )
+    slabs = ((even, swapped(even, "sub")), (odd, swapped(odd, "sub")))
     pair_down, pair_up_x = turned(grad_pair, "blk", -1), swapped(pair_up, "dp")
     pair_down, pair_up_x, pair_up = lax.optimization_barrier((pair_down, pair_up_x, pair_up))
     pair_twice, pair_down_x = turned(pair_up, "blk", 1), swapped(pair_down, "dp")
@@ -392,8 +414,7 @@
     last = {(2, True): pair_twice, (2, False): pair_twice_x}
     sums = None
     for some in (first, last):
-        at = jnp.stack([slab_of(*which) for which in some]).astype(jnp.int32)
-        sums = gradient(at, slabs_own, slabs_other, list(some.values()), sums)
+        sums = gradient(slabs, some, sums)
     grad_weight, grad_bias = sums
     return (grad_query, grad_weight, grad_bias)
 

time: 124 us -> 113 us (0.911)
  starting transfers between devices: 29.2 us -> 20.4 us
  waiting for transfers between devices: 71.4 us -> 76.7 us
  local copies, waits for them, and re-layouts: 6.34 us -> 1.3 us
  Pallas kernels: 13 us -> 11 us
    ppermute x16 -> x18, waiting for transfers between devices: 18.6 us -> 49.3 us  [swapped(): return lax.ppermute(block, axis, [(0, 1), (1, 0)])]
    ppermute x4 -> x2, waiting for transfers between devices: 15.7 us -> 0.45 us  [sent_along(): return lax.ppermute(slabs, ('blk', 'sub'), route)]
    ppermute x6, waiting for transfers between devices: 37.1 us -> 26.9 us  [turned(): lax.ppermute(block, axis, [(i, (i + distance) % size) for i in range(size)])]
    ppermute x4 -> x2, starting transfers between devices: 7.92 us -> 0.71 us  [sent_along(): return lax.ppermute(slabs, ('blk', 'sub'), route)]
    unnamed x24 -> x12, local copies, waits for them, and re-layouts: 4.99 us -> 0.04 us
    pallas_call x2 -> x3, Pallas kernels: 5.53 us -> 3.58 us  [the longest x2 3.47 us: gradient(): pl.pallas_call(functools.partial(gradient_kernel, tuple(some), sums is No...]
    ppermute x16 -> x18, starting transfers between devices: 14.5 us -> 12.5 us  [swapped(): return lax.ppermute(block, axis, [(0, 1), (1, 0)])]
  transfers between devices with their start and end apart: 26 -> 26, of which waited for: 17 -> 15; matrix products, arithmetic and copies ran while one was open for 2% -> 2% of each run, Pallas kernels for 8% -> 8%
where the time goes in v10:
time: 113 us
  waiting for transfers between devices  76.7 us (68%)
  starting transfers between devices  20.4 us (18%)
  Pallas kernels  11 us (10%)
  other arithmetic  2.4 us (2%)
  local copies, waits for them, and re-layouts  1.3 us (1%)
    ppermute x18, waiting for transfers between devices, swapped(): return lax.ppermute(block, axis, [(0, 1), (1, 0)])  49.3 us
    ppermute x6, waiting for transfers between devices, turned(): lax.ppermute(block, axis, [(i, (i + distance) % size) for i in range(size)])  26.9 us
    ppermute x18, starting transfers between devices, swapped(): return lax.ppermute(block, axis, [(0, 1), (1, 0)])  12.5 us
    ppermute x6, starting transfers between devices, turned(): lax.ppermute(block, axis, [(i, (i + distance) % size) for i in range(size)])  7.11 us
    pallas_call x1, Pallas kernels, attention(): pl.pallas_call(functools.partial(attention_kernel, distance), in_specs=[I...  5.07 us
    pallas_call x2, Pallas kernels, gradient(): pl.pallas_call(functools.partial(gradient_kernel, tuple(some), sums is No...  3.47 us
  transfers between devices with their start and end apart: 26, of which 15 were waited for; matrix products, arithmetic and copies ran while one was open for 2% of the time, Pallas kernels for 8%

profile of v10, /device:TPU:0, one launch (start us, length us, event | category | flops | bytes accessed | tf_op | source)
XLA Modules:
  0.0 112.6 jit_solution(17114518013716279939)
XLA Ops:
  0.7 1.1 dynamic-slice_bitcast_fusion
  1.8 3.1 %collective-permute-start = (bf16[640,256]{1,0:T(8,128)(2,1)S(1)}, bf16[640,256]{1,0:T(8,128)(2,1)S(1)}, u32[]{:S(2)}, u32[]{:S(2)}) collective-permute-start(bf16[640,256]{1,0:T(8,128)(2,1)S(1)} %dynamic-slice_bitcast_fusion), channel_id=1, source_target_pairs={{0,4},{4,8},{8,12},{12,0},{1,5},{5,9},{9,13},{13,1},{2,6},{6,10},{... | collective-permute-start | bytes 983048 | tf_op jit(solution)/shard_map/ppermute | solution.py:306
  4.8 1.7 %multiply_reduce_fusion = f32[256]{0:T(256)S(1)} fusion(bf16[256,2560]{1,0:T(8,128)(2,1)} %values_ref.1), kind=kLoop, calls=%fused_computation | loop fusion | flops 1965824 | bytes 1311744 | tf_op jit(solution)/shard_map/reduce_sum | solution.py:341
  6.7 1.0 collective-permute-done.1
  7.9 0.9 norm.1
  8.8 5.7 %collective-permute-done.refs_0_ = bf16[640,256]{1,0:T(8,128)(2,1)S(1)} collective-permute-done((bf16[640,256]{1,0:T(8,128)(2,1)S(1)}, bf16[640,256]{1,0:T(8,128)(2,1)S(1)}, u32[]{:S(2)}, u32[]{:S(2)}) %collective-permute-start) | collective-permute-done | bytes 327712 | tf_op jit(solution)/shard_map/ppermute | solution.py:306
  14.6 1.5 %collective-permute-start.2 = (bf16[640,256]{1,0:T(8,128)(2,1)S(1)}, bf16[640,256]{1,0:T(8,128)(2,1)S(1)}, u32[]{:S(2)}, u32[]{:S(2)}) collective-permute-start(bf16[640,256]{1,0:T(8,128)(2,1)S(1)} %collective-permute-done.refs_0_), channel_id=1, source_target_pairs={{0,16},{16,0},{1,17},{17,1},{2,18},{18,2},{3,19},{19,3},{4,20},{20... | collective-permute-start | bytes 983048 | tf_op jit(solution)/shard_map/ppermute | solution.py:301
  16.1 1.7 %collective-permute-start.3 = (bf16[640,256]{1,0:T(8,128)(2,1)S(1)}, bf16[640,256]{1,0:T(8,128)(2,1)S(1)}, u32[]{:S(2)}, u32[]{:S(2)}) collective-permute-start(bf16[640,256]{1,0:T(8,128)(2,1)S(1)} %dynamic-slice_bitcast_fusion), channel_id=1, source_target_pairs={{0,12},{4,0},{8,4},{12,8},{1,13},{5,1},{9,5},{13,9},{2,14},{6,2},{... | collective-permute-start | bytes 983048 | tf_op jit(solution)/shard_map/ppermute | solution.py:306
  17.8 1.5 %collective-permute-start.8 = (bf16[2,640,256]{2,1,0:T(8,128)(2,1)S(1)}, bf16[2,640,256]{2,1,0:T(8,128)(2,1)S(1)}, u32[]{:S(2)}, u32[]{:S(2)}) collective-permute-start(bf16[2,640,256]{2,1,0:T(8,128)(2,1)S(1)} %get-tuple-element.54), channel_id=1, source_target_pairs={{0,2},{2,0},{1,3},{3,1},{4,6},{6,4},{5,7},{7,5},{8,10},{10,8},{9,1... | collective-permute-start | bytes 1966088 | tf_op jit(solution)/shard_map/ppermute | solution.py:301
  19.9 4.8 %collective-permute-done.2.refs_2_ = bf16[640,256]{1,0:T(8,128)(2,1)S(1)} collective-permute-done((bf16[640,256]{1,0:T(8,128)(2,1)S(1)}, bf16[640,256]{1,0:T(8,128)(2,1)S(1)}, u32[]{:S(2)}, u32[]{:S(2)}) %collective-permute-start.2) | collective-permute-done | bytes 327712 | tf_op jit(solution)/shard_map/ppermute | solution.py:301
  24.7 1.2 %collective-permute-done.3.refs_4_ = bf16[640,256]{1,0:T(8,128)(2,1)S(1)} collective-permute-done((bf16[640,256]{1,0:T(8,128)(2,1)S(1)}, bf16[640,256]{1,0:T(8,128)(2,1)S(1)}, u32[]{:S(2)}, u32[]{:S(2)}) %collective-permute-start.3) | collective-permute-done | bytes 327712 | tf_op jit(solution)/shard_map/ppermute | solution.py:306
  26.5 15.0 %collective-permute-done.7.refs_1_ = bf16[640,256]{1,0:T(8,128)(2,1)S(1)} collective-permute-done((bf16[640,256]{1,0:T(8,128)(2,1)S(1)}, bf16[640,256]{1,0:T(8,128)(2,1)S(1)}, u32[]{:S(2)}, u32[]{:S(2)}) %collective-permute-start.7) | collective-permute-done | bytes 327712 | tf_op jit(solution)/shard_map/ppermute | solution.py:301
  41.6 0.7 collective-permute-start.13
  42.3 1.6 %collective-permute-start.12 = (bf16[640,256]{1,0:T(8,128)(2,1)S(1)}, bf16[640,256]{1,0:T(8,128)(2,1)S(1)}, u32[]{:S(2)}, u32[]{:S(2)}) collective-permute-start(bf16[640,256]{1,0:T(8,128)(2,1)S(1)} %collective-permute-done.3.refs_4_), channel_id=1, source_target_pairs={{0,2},{2,0},{1,3},{3,1},{4,6},{6,4},{5,7},{7,5},{8,10},{10,8},{9,1... | collective-permute-start | bytes 983048 | tf_op jit(solution)/shard_map/ppermute | solution.py:301
  44.3 1.5 %collective-permute-start.11 = (bf16[640,256]{1,0:T(8,128)(2,1)S(1)}, bf16[640,256]{1,0:T(8,128)(2,1)S(1)}, u32[]{:S(2)}, u32[]{:S(2)}) collective-permute-start(bf16[640,256]{1,0:T(8,128)(2,1)S(1)} %collective-permute-done.7.refs_1_), channel_id=1, source_target_pairs={{0,16},{16,0},{1,17},{17,1},{2,18},{18,2},{3,19},{19,3},{4,20},{20... | collective-permute-start | bytes 983048 | tf_op jit(solution)/shard_map/ppermute | solution.py:301
  46.4 6.5 %collective-permute-done.12.refs_5_ = bf16[640,256]{1,0:T(8,128)(2,1)S(1)} collective-permute-done((bf16[640,256]{1,0:T(8,128)(2,1)S(1)}, bf16[640,256]{1,0:T(8,128)(2,1)S(1)}, u32[]{:S(2)}, u32[]{:S(2)}) %collective-permute-start.12) | collective-permute-done | bytes 327712 | tf_op jit(solution)/shard_map/ppermute | solution.py:301
  52.9 1.4 %collective-permute-done.10.p2 = bf16[640,256]{1,0:T(8,128)(2,1)S(1)} collective-permute-done((bf16[640,256]{1,0:T(8,128)(2,1)S(1)}, bf16[640,256]{1,0:T(8,128)(2,1)S(1)}, u32[]{:S(2)}, u32[]{:S(2)}) %collective-permute-start.10) | collective-permute-done | bytes 327712 | tf_op jit(solution)/shard_map/ppermute | solution.py:301
  54.3 6.6 %collective-permute-done.11.refs_3_ = bf16[640,256]{1,0:T(8,128)(2,1)S(1)} collective-permute-done((bf16[640,256]{1,0:T(8,128)(2,1)S(1)}, bf16[640,256]{1,0:T(8,128)(2,1)S(1)}, u32[]{:S(2)}, u32[]{:S(2)}) %collective-permute-start.11) | collective-permute-done | bytes 327712 | tf_op jit(solution)/shard_map/ppermute | solution.py:301
  62.8 8.8 %collective-permute-done.15.refs_7_ = bf16[640,256]{1,0:T(8,128)(2,1)S(1)} collective-permute-done((bf16[640,256]{1,0:T(8,128)(2,1)S(1)}, bf16[640,256]{1,0:T(8,128)(2,1)S(1)}, u32[]{:S(2)}, u32[]{:S(2)}) %collective-permute-start.15) | collective-permute-done | bytes 327712 | tf_op jit(solution)/shard_map/ppermute | solution.py:301
  71.6 1.4 %project.1.sums_ref = f32[2,256,256]{2,1,0:T(8,128)S(1)} custom-call(bf16[256,2560]{1,0:T(8,128)(2,1)S(1)} %get-tuple-element.48.own_ref, bf16[256,2560]{1,0:T(8,128)(2,1)S(1)} %collective-permute-done.4.other_ref, bf16[2,1280,256]{2,1,0:T(8,128)(2,1)S(1)} %copy-done.1, bf16[640,256]{1,0:T(8,128)(2,1)S(1)} %collective-permute-done.refs_0_, ...), custom_call_target="tpu_custom_call" | custom-call | flops 1006632960 | bytes 7000000 | tf_op jit(solution)/shard_map/project/pallas_call | solution.py:91
  73.1 5.1 %attention.1 = (bf16[256,1280]{1,0:T(8,128)(2,1)}, bf16[256,512]{1,0:T(8,128)(2,1)S(1)}) custom-call(bf16[256,2560]{1,0:T(8,128)(2,1)S(1)} %get-tuple-element.48.own_ref, bf16[256,2560]{1,0:T(8,128)(2,1)S(1)} %collective-permute-done.4.other_ref, bf16[640,256]{1,0:T(8,128)(2,1)S(1)} %collective-permute-done.5.p0, ...), custom_call_target="tpu_custom_call" | custom-call | flops 838860800 | bytes 5000000 | tf_op jit(solution)/shard_map/attention/pallas_call | solution.py:165
  79.1 9.1 %collective-permute-done.17.refs_14_ = bf16[256,512]{1,0:T(8,128)(2,1)S(1)} collective-permute-done((bf16[256,512]{1,0:T(8,128)(2,1)S(1)}, bf16[256,512]{1,0:T(8,128)(2,1)S(1)}, u32[]{:S(2)}, u32[]{:S(2)}) %collective-permute-start.17) | collective-permute-done | bytes 262176 | tf_op jit(solution)/shard_map/ppermute | solution.py:306
  88.2 1.7 %collective-permute-start.20 = (bf16[256,512]{1,0:T(8,128)(2,1)S(1)}, bf16[256,512]{1,0:T(8,128)(2,1)S(1)}, u32[]{:S(2)}, u32[]{:S(2)}) collective-permute-start(bf16[256,512]{1,0:T(8,128)(2,1)S(1)} %get-tuple-element.74.refs_12_), channel_id=1, source_target_pairs={{0,12},{4,0},{8,4},{12,8},{1,13},{5,1},{9,5},{13,9},{2,14},{6,2},{... | collective-permute-start | bytes 786440 | tf_op jit(solution)/shard_map/ppermute | solution.py:306
  89.9 0.6 collective-permute-start.21
  91.1 4.0 %collective-permute-done.20.refs_15_ = bf16[256,512]{1,0:T(8,128)(2,1)S(1)} collective-permute-done((bf16[256,512]{1,0:T(8,128)(2,1)S(1)}, bf16[256,512]{1,0:T(8,128)(2,1)S(1)}, u32[]{:S(2)}, u32[]{:S(2)}) %collective-permute-start.20) | collective-permute-done | bytes 262176 | tf_op jit(solution)/shard_map/ppermute | solution.py:306
  95.1 1.2 %collective-permute-done.21.refs_16_ = bf16[256,512]{1,0:T(8,128)(2,1)S(1)} collective-permute-done((bf16[256,512]{1,0:T(8,128)(2,1)S(1)}, bf16[256,512]{1,0:T(8,128)(2,1)S(1)}, u32[]{:S(2)}, u32[]{:S(2)}) %collective-permute-start.21) | collective-permute-done | bytes 262176 | tf_op jit(solution)/shard_map/ppermute | solution.py:301
  96.9 0.8 collective-permute-start.23
  97.6 6.9 %collective-permute-done.22.refs_4_ = bf16[256,512]{1,0:T(8,128)(2,1)S(1)} collective-permute-done((bf16[256,512]{1,0:T(8,128)(2,1)S(1)}, bf16[256,512]{1,0:T(8,128)(2,1)S(1)}, u32[]{:S(2)}, u32[]{:S(2)}) %collective-permute-start.22) | collective-permute-done | bytes 262176 | tf_op jit(solution)/shard_map/ppermute | solution.py:306
  104.5 0.7 collective-permute-start.24
  105.2 1.7 %gradient.2 = (f32[2,640,256]{2,1,0:T(8,128)S(1)}, f32[2,256]{1,0:T(2,128)S(1)}) custom-call(bf16[2,640,256]{2,1,0:T(8,128)(2,1)S(1)} %collective-permute-done.13.refs_0_.refs_1_, bf16[2,640,256]{2,1,0:T(8,128)(2,1)S(1)} %collective-permute-done.13.refs_0_.refs_1_, bf16[2,640,256]{2,1,0:T(8,128)(2,1)S(1)} %collective-permute-done.16.refs_2_.refs_3_.refs_4_.refs_5_, ...), custom_call_target="tpu_custom_call" | custom-call | flops 1006632960 | bytes 5000000 | tf_op jit(solution)/shard_map/gradient/pallas_call | solution.py:230
  107.0 3.9 %collective-permute-done.24.refs_5_ = bf16[256,512]{1,0:T(8,128)(2,1)S(1)} collective-permute-done((bf16[256,512]{1,0:T(8,128)(2,1)S(1)}, bf16[256,512]{1,0:T(8,128)(2,1)S(1)}, u32[]{:S(2)}, u32[]{:S(2)}) %collective-permute-start.24) | collective-permute-done | bytes 262176 | tf_op jit(solution)/shard_map/ppermute | solution.py:301
  110.9 1.7 %gradient.3 = (f32[2,640,256]{2,1,0:T(8,128)}, f32[2,256]{1,0:T(2,128)}) custom-call(bf16[2,640,256]{2,1,0:T(8,128)(2,1)S(1)} %collective-permute-done.13.refs_0_.refs_1_, bf16[2,640,256]{2,1,0:T(8,128)(2,1)S(1)} %collective-permute-done.13.refs_0_.refs_1_, bf16[2,640,256]{2,1,0:T(8,128)(2,1)S(1)} %collective-permute-done.19.refs_6_.refs_7_.refs_2_.refs_3_, ...), custom_call_target="tpu_custom_call" | custom-call | flops 335544320 | bytes 5000000 | tf_op jit(solution)/shard_map/gradient/pallas_call | solution.py:230
  (49 shorter events, 6.4 us)
Async XLA Ops:
  0.6 7.2 %copy-start = (bf16[256,2560]{1,0:T(8,128)(2,1)S(1)}, bf16[256,2560]{1,0:T(8,128)(2,1)}, u32[]{:S(2)}) copy-start(bf16[256,2560]{1,0:T(8,128)(2,1)} %values_ref.1) | copy-start | bytes 3932164
  0.6 5.9 %copy-start.4 = (bf16[5120]{0:T(1024)(128)(2,1)S(1)}, bf16[5120]{0:T(1024)(128)(2,1)}, u32[]{:S(2)}) copy-start(bf16[5120]{0:T(1024)(128)(2,1)} %param.7) | copy-start | bytes 30724
  1.8 12.8 %collective-permute-start = (bf16[640,256]{1,0:T(8,128)(2,1)S(1)}, bf16[640,256]{1,0:T(8,128)(2,1)S(1)}, u32[]{:S(2)}, u32[]{:S(2)}) collective-permute-start(bf16[640,256]{1,0:T(8,128)(2,1)S(1)} %dynamic-slice_bitcast_fusion), channel_id=1, source_target_pairs={{0,4},{4,8},{8,12},{12,0},{1,5},{5,9},{9,13},{13,1},{2,6},{6,10},{... | collective-permute-start | bytes 983048 | tf_op jit(solution)/shard_map/ppermute | solution.py:306
  6.5 1.2 %collective-permute-start.1 = (f32[256,1]{0,1:T(1,128)S(1)}, f32[256,1]{0,1:T(1,128)S(1)}, u32[]{:S(2)}, u32[]{:S(2)}) collective-permute-start(f32[256,1]{0,1:T(1,128)S(1)} %bitcast.3), channel_id=1, source_target_pairs={{0,1},{1,0},{2,3},{3,2},{4,5},{5,4},{6,7},{7,6},{8,9},{9,8},{10,11... | collective-permute-start | bytes 3080 | tf_op jit(solution)/shard_map/ppermute | solution.py:301
  7.9 54.7 %copy-start.5 = (bf16[2,256]{1,0:T(2,128)(2,1)S(1)}, bf16[2,256]{1,0:T(2,128)(2,1)}, u32[]{:S(2)}) copy-start(bf16[2,256]{1,0:T(2,128)(2,1)} %param.11) | copy-start | bytes 3076
  8.8 62.8 %copy-start.1 = (bf16[2,1280,256]{2,1,0:T(8,128)(2,1)S(1)}, bf16[2,1280,256]{2,1,0:T(8,128)(2,1)}, u32[]{:S(2)}) copy-start(bf16[2,1280,256]{2,1,0:T(8,128)(2,1)} %weight_ref.1) | copy-start | bytes 3932164
  14.6 11.4 %collective-permute-start.4 = (bf16[256,2560]{1,0:T(8,128)(2,1)S(1)}, bf16[256,2560]{1,0:T(8,128)(2,1)S(1)}, u32[]{:S(2)}, u32[]{:S(2)}) collective-permute-start(bf16[256,2560]{1,0:T(8,128)(2,1)S(1)} %get-tuple-element.48.own_ref), channel_id=1, source_target_pairs={{0,1},{1,0},{2,3},{3,2},{4,5},{5,4},{6,7},{7,6},{8,9},{9,8},{10,11... | collective-permute-start | bytes 3932168 | tf_op jit(solution)/shard_map/ppermute | solution.py:301
  14.6 10.1 %collective-permute-start.2 = (bf16[640,256]{1,0:T(8,128)(2,1)S(1)}, bf16[640,256]{1,0:T(8,128)(2,1)S(1)}, u32[]{:S(2)}, u32[]{:S(2)}) collective-permute-start(bf16[640,256]{1,0:T(8,128)(2,1)S(1)} %collective-permute-done.refs_0_), channel_id=1, source_target_pairs={{0,16},{16,0},{1,17},{17,1},{2,18},{18,2},{3,19},{19,3},{4,20},{20... | collective-permute-start | bytes 983048 | tf_op jit(solution)/shard_map/ppermute | solution.py:301
  16.1 9.8 %collective-permute-start.3 = (bf16[640,256]{1,0:T(8,128)(2,1)S(1)}, bf16[640,256]{1,0:T(8,128)(2,1)S(1)}, u32[]{:S(2)}, u32[]{:S(2)}) collective-permute-start(bf16[640,256]{1,0:T(8,128)(2,1)S(1)} %dynamic-slice_bitcast_fusion), channel_id=1, source_target_pairs={{0,12},{4,0},{8,4},{12,8},{1,13},{5,1},{9,5},{13,9},{2,14},{6,2},{... | collective-permute-start | bytes 983048 | tf_op jit(solution)/shard_map/ppermute | solution.py:306
  17.8 23.6 %collective-permute-start.8 = (bf16[2,640,256]{2,1,0:T(8,128)(2,1)S(1)}, bf16[2,640,256]{2,1,0:T(8,128)(2,1)S(1)}, u32[]{:S(2)}, u32[]{:S(2)}) collective-permute-start(bf16[2,640,256]{2,1,0:T(8,128)(2,1)S(1)} %get-tuple-element.54), channel_id=1, source_target_pairs={{0,2},{2,0},{1,3},{3,1},{4,6},{6,4},{5,7},{7,5},{8,10},{10,8},{9,1... | collective-permute-start | bytes 1966088 | tf_op jit(solution)/shard_map/ppermute | solution.py:301
  19.3 22.1 %collective-permute-start.7 = (bf16[640,256]{1,0:T(8,128)(2,1)S(1)}, bf16[640,256]{1,0:T(8,128)(2,1)S(1)}, u32[]{:S(2)}, u32[]{:S(2)}) collective-permute-start(bf16[640,256]{1,0:T(8,128)(2,1)S(1)} %collective-permute-done.refs_0_), channel_id=1, source_target_pairs={{0,2},{2,0},{1,3},{3,1},{4,6},{6,4},{5,7},{7,5},{8,10},{10,8},{9,1... | collective-permute-start | bytes 983048 | tf_op jit(solution)/shard_map/ppermute | solution.py:301
  25.9 15.5 %collective-permute-start.5 = (bf16[640,256]{1,0:T(8,128)(2,1)S(1)}, bf16[640,256]{1,0:T(8,128)(2,1)S(1)}, u32[]{:S(2)}, u32[]{:S(2)}) collective-permute-start(bf16[640,256]{1,0:T(8,128)(2,1)S(1)} %collective-permute-done.refs_0_), channel_id=1, source_target_pairs={{0,4},{4,8},{8,12},{12,0},{1,5},{5,9},{9,13},{13,1},{2,6},{6,10},{... | collective-permute-start | bytes 983048 | tf_op jit(solution)/shard_map/ppermute | solution.py:306
  25.9 15.5 %collective-permute-start.6 = (bf16[640,256]{1,0:T(8,128)(2,1)S(1)}, bf16[640,256]{1,0:T(8,128)(2,1)S(1)}, u32[]{:S(2)}, u32[]{:S(2)}) collective-permute-start(bf16[640,256]{1,0:T(8,128)(2,1)S(1)} %collective-permute-done.3.refs_4_), channel_id=1, source_target_pairs={{0,16},{16,0},{1,17},{17,1},{2,18},{18,2},{3,19},{19,3},{4,20},{20... | collective-permute-start | bytes 983048 | tf_op jit(solution)/shard_map/ppermute | solution.py:301
  41.6 19.4 %collective-permute-start.13 = (bf16[2,640,256]{2,1,0:T(8,128)(2,1)S(1)}, bf16[2,640,256]{2,1,0:T(8,128)(2,1)S(1)}, u32[]{:S(2)}, u32[]{:S(2)}) collective-permute-start(bf16[2,640,256]{2,1,0:T(8,128)(2,1)S(1)} %get-tuple-element.59), channel_id=1, source_target_pairs={{0,0},{1,8},{4,4},{5,12},{8,1},{9,9},{12,5},{13,13},{2,2},{3,10},{... | collective-permute-start | bytes 1966088 | tf_op jit(solution)/shard_map/ppermute | solution.py:334
  42.3 10.6 %collective-permute-start.12 = (bf16[640,256]{1,0:T(8,128)(2,1)S(1)}, bf16[640,256]{1,0:T(8,128)(2,1)S(1)}, u32[]{:S(2)}, u32[]{:S(2)}) collective-permute-start(bf16[640,256]{1,0:T(8,128)(2,1)S(1)} %collective-permute-done.3.refs_4_), channel_id=1, source_target_pairs={{0,2},{2,0},{1,3},{3,1},{4,6},{6,4},{5,7},{7,5},{8,10},{10,8},{9,1... | collective-permute-start | bytes 983048 | tf_op jit(solution)/shard_map/ppermute | solution.py:301
  43.8 10.5 %collective-permute-start.10 = (bf16[640,256]{1,0:T(8,128)(2,1)S(1)}, bf16[640,256]{1,0:T(8,128)(2,1)S(1)}, u32[]{:S(2)}, u32[]{:S(2)}) collective-permute-start(bf16[640,256]{1,0:T(8,128)(2,1)S(1)} %collective-permute-done.5.p0), channel_id=1, source_target_pairs={{0,16},{16,0},{1,17},{17,1},{2,18},{18,2},{3,19},{19,3},{4,20},{20... | collective-permute-start | bytes 983048 | tf_op jit(solution)/shard_map/ppermute | solution.py:301
  44.3 16.6 %collective-permute-start.11 = (bf16[640,256]{1,0:T(8,128)(2,1)S(1)}, bf16[640,256]{1,0:T(8,128)(2,1)S(1)}, u32[]{:S(2)}, u32[]{:S(2)}) collective-permute-start(bf16[640,256]{1,0:T(8,128)(2,1)S(1)} %collective-permute-done.7.refs_1_), channel_id=1, source_target_pairs={{0,16},{16,0},{1,17},{17,1},{2,18},{18,2},{3,19},{19,3},{4,20},{20... | collective-permute-start | bytes 983048 | tf_op jit(solution)/shard_map/ppermute | solution.py:301
  45.9 15.1 %collective-permute-start.9 = (bf16[640,256]{1,0:T(8,128)(2,1)S(1)}, bf16[640,256]{1,0:T(8,128)(2,1)S(1)}, u32[]{:S(2)}, u32[]{:S(2)}) collective-permute-start(bf16[640,256]{1,0:T(8,128)(2,1)S(1)} %collective-permute-done.5.p0), channel_id=1, source_target_pairs={{0,2},{2,0},{1,3},{3,1},{4,6},{6,4},{5,7},{7,5},{8,10},{10,8},{9,1... | collective-permute-start | bytes 983048 | tf_op jit(solution)/shard_map/ppermute | solution.py:301
  61.0 17.6 %collective-permute-start.16 = (bf16[2,640,256]{2,1,0:T(8,128)(2,1)S(1)}, bf16[2,640,256]{2,1,0:T(8,128)(2,1)S(1)}, u32[]{:S(2)}, u32[]{:S(2)}) collective-permute-start(bf16[2,640,256]{2,1,0:T(8,128)(2,1)S(1)} %get-tuple-element.70), channel_id=1, source_target_pairs={{0,4},{1,12},{4,0},{5,8},{8,5},{9,13},{12,1},{13,9},{2,6},{3,14},{... | collective-permute-start | bytes 1966088 | tf_op jit(solution)/shard_map/ppermute | solution.py:334
  61.0 10.6 %collective-permute-start.15 = (bf16[640,256]{1,0:T(8,128)(2,1)S(1)}, bf16[640,256]{1,0:T(8,128)(2,1)S(1)}, u32[]{:S(2)}, u32[]{:S(2)}) collective-permute-start(bf16[640,256]{1,0:T(8,128)(2,1)S(1)} %collective-permute-done.12.refs_5_), channel_id=1, source_target_pairs={{0,16},{16,0},{1,17},{17,1},{2,18},{18,2},{3,19},{19,3},{4,20},{20... | collective-permute-start | bytes 983048 | tf_op jit(solution)/shard_map/ppermute | solution.py:301
  61.6 11.5 %collective-permute-start.14 = (bf16[640,256]{1,0:T(8,128)(2,1)S(1)}, bf16[640,256]{1,0:T(8,128)(2,1)S(1)}, u32[]{:S(2)}, u32[]{:S(2)}) collective-permute-start(bf16[640,256]{1,0:T(8,128)(2,1)S(1)} %collective-permute-done.10.p2), channel_id=1, source_target_pairs={{0,2},{2,0},{1,3},{3,1},{4,6},{6,4},{5,7},{7,5},{8,10},{10,8},{9,1... | collective-permute-start | bytes 983048 | tf_op jit(solution)/shard_map/ppermute | solution.py:301
  62.8 10.3 %copy-start.2 = (bf16[256,1280]{1,0:T(8,128)(2,1)S(1)}, bf16[256,1280]{1,0:T(8,128)(2,1)}, u32[]{:S(2)}) copy-start(bf16[256,1280]{1,0:T(8,128)(2,1)} %queries_ref.1) | copy-start | bytes 1966084
  62.8 10.3 %copy-start.3 = (bf16[256,1280]{1,0:T(8,128)(2,1)S(1)}, bf16[256,1280]{1,0:T(8,128)(2,1)}, u32[]{:S(2)}) copy-start(bf16[256,1280]{1,0:T(8,128)(2,1)} %cotangent_ref.1) | copy-start | bytes 1966084
  78.6 9.6 %collective-permute-start.17 = (bf16[256,512]{1,0:T(8,128)(2,1)S(1)}, bf16[256,512]{1,0:T(8,128)(2,1)S(1)}, u32[]{:S(2)}, u32[]{:S(2)}) collective-permute-start(bf16[256,512]{1,0:T(8,128)(2,1)S(1)} %get-tuple-element.74.refs_12_), channel_id=1, source_target_pairs={{0,4},{4,8},{8,12},{12,0},{1,5},{5,9},{9,13},{13,1},{2,6},{6,10},{... | collective-permute-start | bytes 786440 | tf_op jit(solution)/shard_map/ppermute | solution.py:306
  78.6 9.6 %collective-permute-start.18 = (bf16[256,512]{1,0:T(8,128)(2,1)S(1)}, bf16[256,512]{1,0:T(8,128)(2,1)S(1)}, u32[]{:S(2)}, u32[]{:S(2)}) collective-permute-start(bf16[256,512]{1,0:T(8,128)(2,1)S(1)} %get-tuple-element.74.refs_12_), channel_id=1, source_target_pairs={{0,2},{2,0},{1,3},{3,1},{4,6},{6,4},{5,7},{7,5},{8,10},{10,8},{9,1... | collective-permute-start | bytes 786440 | tf_op jit(solution)/shard_map/ppermute | solution.py:301
  88.2 6.9 %collective-permute-start.20 = (bf16[256,512]{1,0:T(8,128)(2,1)S(1)}, bf16[256,512]{1,0:T(8,128)(2,1)S(1)}, u32[]{:S(2)}, u32[]{:S(2)}) collective-permute-start(bf16[256,512]{1,0:T(8,128)(2,1)S(1)} %get-tuple-element.74.refs_12_), channel_id=1, source_target_pairs={{0,12},{4,0},{8,4},{12,8},{1,13},{5,1},{9,5},{13,9},{2,14},{6,2},{... | collective-permute-start | bytes 786440 | tf_op jit(solution)/shard_map/ppermute | solution.py:306
  89.9 6.4 %collective-permute-start.21 = (bf16[256,512]{1,0:T(8,128)(2,1)S(1)}, bf16[256,512]{1,0:T(8,128)(2,1)S(1)}, u32[]{:S(2)}, u32[]{:S(2)}) collective-permute-start(bf16[256,512]{1,0:T(8,128)(2,1)S(1)} %collective-permute-done.17.refs_14_), channel_id=1, source_target_pairs={{0,2},{2,0},{1,3},{3,1},{4,6},{6,4},{5,7},{7,5},{8,10},{10,8},{9,1... | collective-permute-start | bytes 786440 | tf_op jit(solution)/shard_map/ppermute | solution.py:301
  90.6 14.6 %collective-permute-start.19 = (bf16[2,640,256]{2,1,0:T(8,128)(2,1)S(1)}, bf16[2,640,256]{2,1,0:T(8,128)(2,1)S(1)}, u32[]{:S(2)}, u32[]{:S(2)}) collective-permute-start(bf16[2,640,256]{2,1,0:T(8,128)(2,1)S(1)} %collective-permute-done.13.refs_0_.refs_1_), channel_id=1, source_target_pairs={{0,1},{1,0},{2,3},{3,2},{4,5},{5,4},{6,7},{7,6},{8,9},{9,8},{10,11... | collective-permute-start | bytes 1966088 | tf_op jit(solution)/shard_map/ppermute | solution.py:301
  90.6 14.6 %collective-permute-start.25 = (bf16[2,640,256]{2,1,0:T(8,128)(2,1)S(1)}, bf16[2,640,256]{2,1,0:T(8,128)(2,1)S(1)}, u32[]{:S(2)}, u32[]{:S(2)}) collective-permute-start(bf16[2,640,256]{2,1,0:T(8,128)(2,1)S(1)} %collective-permute-done.16.refs_2_.refs_3_.refs_4_.refs_5_), channel_id=1, source_target_pairs={{0,1},{1,0},{2,3},{3,2},{4,5},{5,4},{6,7},{7,6},{8,9},{9,8},{10,11... | collective-permute-start | bytes 1966088 | tf_op jit(solution)/shard_map/ppermute | solution.py:301
  96.3 8.2 %collective-permute-start.22 = (bf16[256,512]{1,0:T(8,128)(2,1)S(1)}, bf16[256,512]{1,0:T(8,128)(2,1)S(1)}, u32[]{:S(2)}, u32[]{:S(2)}) collective-permute-start(bf16[256,512]{1,0:T(8,128)(2,1)S(1)} %collective-permute-done.17.refs_14_), channel_id=1, source_target_pairs={{0,4},{4,8},{8,12},{12,0},{1,5},{5,9},{9,13},{13,1},{2,6},{6,10},{... | collective-permute-start | bytes 786440 | tf_op jit(solution)/shard_map/ppermute | solution.py:306
  96.9 7.6 %collective-permute-start.23 = (bf16[256,512]{1,0:T(8,128)(2,1)S(1)}, bf16[256,512]{1,0:T(8,128)(2,1)S(1)}, u32[]{:S(2)}, u32[]{:S(2)}) collective-permute-start(bf16[256,512]{1,0:T(8,128)(2,1)S(1)} %collective-permute-done.20.refs_15_), channel_id=1, source_target_pairs={{0,2},{2,0},{1,3},{3,1},{4,6},{6,4},{5,7},{7,5},{8,10},{10,8},{9,1... | collective-permute-start | bytes 786440 | tf_op jit(solution)/shard_map/ppermute | solution.py:301
  104.5 6.4 %collective-permute-start.24 = (bf16[256,512]{1,0:T(8,128)(2,1)S(1)}, bf16[256,512]{1,0:T(8,128)(2,1)S(1)}, u32[]{:S(2)}, u32[]{:S(2)}) collective-permute-start(bf16[256,512]{1,0:T(8,128)(2,1)S(1)} %collective-permute-done.22.refs_4_), channel_id=1, source_target_pairs={{0,2},{2,0},{1,3},{3,1},{4,6},{6,4},{5,7},{7,5},{8,10},{10,8},{9,1... | collective-permute-start | bytes 786440 | tf_op jit(solution)/shard_map/ppermute | solution.py:301

commit v11 on v10

--- a/solution.py
+++ b/solution.py
@@ -367,16 +367,18 @@
 
     up = turned(piece, "blk", 1)
     normed, kept, sent = norm(activations, scale, gain[None, :], share)
-    up, piece, normed, kept, sent = lax.optimization_barrier((up, piece, normed, kept, sent))
-    up_x, up_y, down = swapped(up, "dp"), swapped(up, "groups"), turned(piece, "blk", -1)
     arrived = swapped(sent, "dp")
+    up, piece, normed = lax.optimization_barrier((up, piece, normed))
+    up_y, down = swapped(up, "groups"), turned(piece, "blk", -1)
     normed_other = swapped(normed, "sub")
     up, up_y, down, normed_other = lax.optimization_barrier((up, up_y, down, normed_other))
-    down_x, down_y = swapped(down, "dp"), swapped(down, "groups")
+    up_x, down_y = swapped(up, "dp"), swapped(down, "groups")
     twice = turned(up, "blk", 1)
-    twice, down_y, up_x, arrived = lax.optimization_barrier((twice, down_y, up_x, arrived))
-    twice_x, twice_y = swapped(twice, "dp"), swapped(twice, "groups")
-    up_both = swapped(up_x, "groups")
+    twice, down, down_y, up_x, arrived = lax.optimization_barrier(
+        (twice, down, down_y, up_x, arrived)
+    )
+    down_x, twice_x = swapped(down, "dp"), swapped(twice, "dp")
+    twice_y, up_both = swapped(twice, "groups"), swapped(up_x, "groups")
     even, odd = pack(kept, arrived)
     even = sent_along(even, 0)
     twice_x, twice_y, up_both, down_x, even = lax.optimization_barrier(

time: 113 us -> 112 us (level)
  waiting for transfers between devices: 76.7 us -> 70.1 us
  starting transfers between devices: 20.4 us -> 26.2 us
    ppermute x18, starting transfers between devices: 12.5 us -> 17.7 us  [swapped(): return lax.ppermute(block, axis, [(0, 1), (1, 0)])]
    ppermute x18, waiting for transfers between devices: 49.3 us -> 44.7 us  [swapped(): return lax.ppermute(block, axis, [(0, 1), (1, 0)])]
    ppermute x6, waiting for transfers between devices: 26.9 us -> 24.7 us  [turned(): lax.ppermute(block, axis, [(i, (i + distance) % size) for i in range(size)])]
  transfers between devices with their start and end apart: 26 -> 26, of which waited for: 15 -> 17; matrix products, arithmetic and copies ran while one was open for 2% -> 2% of each run, Pallas kernels for 8% -> 8%
where the time goes in v11:
time: 112 us
  waiting for transfers between devices  70.1 us (63%)
  starting transfers between devices  26.2 us (23%)
  Pallas kernels  11 us (10%)
  other arithmetic  2.4 us (2%)
  local copies, waits for them, and re-layouts  1.3 us (1%)
    ppermute x18, waiting for transfers between devices, swapped(): return lax.ppermute(block, axis, [(0, 1), (1, 0)])  44.7 us
    ppermute x6, waiting for transfers between devices, turned(): lax.ppermute(block, axis, [(i, (i + distance) % size) for i in range(size)])  24.7 us
    ppermute x18, starting transfers between devices, swapped(): return lax.ppermute(block, axis, [(0, 1), (1, 0)])  17.7 us
    ppermute x6, starting transfers between devices, turned(): lax.ppermute(block, axis, [(i, (i + distance) % size) for i in range(size)])  7.19 us
    pallas_call x1, Pallas kernels, attention(): pl.pallas_call(functools.partial(attention_kernel, distance), in_specs=[I...  5.07 us
    pallas_call x2, Pallas kernels, gradient(): pl.pallas_call(functools.partial(gradient_kernel, tuple(some), sums is No...  3.46 us
  transfers between devices with their start and end apart: 26, of which 17 were waited for; matrix products, arithmetic and copies ran while one was open for 2% of the time, Pallas kernels for 8%

profile of v11, /device:TPU:0, one launch (start us, length us, event | category | flops | bytes accessed | tf_op | source)
XLA Modules:
  0.0 111.8 jit_solution(1806466962424824195)
XLA Ops:
  1.8 3.1 %collective-permute-start = (bf16[640,256]{1,0:T(8,128)(2,1)S(1)}, bf16[640,256]{1,0:T(8,128)(2,1)S(1)}, u32[]{:S(2)}, u32[]{:S(2)}) collective-permute-start(bf16[640,256]{1,0:T(8,128)(2,1)S(1)} %dynamic-slice_bitcast_fusion), channel_id=1, source_target_pairs={{0,4},{4,8},{8,12},{12,0},{1,5},{5,9},{9,13},{13,1},{2,6},{6,10},{... | collective-permute-start | bytes 983048 | tf_op jit(solution)/shard_map/ppermute | solution.py:306
  4.8 1.7 %multiply_reduce_fusion = f32[256]{0:T(256)S(1)} fusion(bf16[256,2560]{1,0:T(8,128)(2,1)} %values_ref.1), kind=kLoop, calls=%fused_computation | loop fusion | flops 1965824 | bytes 1311744 | tf_op jit(solution)/shard_map/reduce_sum | solution.py:341
  8.8 5.7 %collective-permute-done.refs_0_ = bf16[640,256]{1,0:T(8,128)(2,1)S(1)} collective-permute-done((bf16[640,256]{1,0:T(8,128)(2,1)S(1)}, bf16[640,256]{1,0:T(8,128)(2,1)S(1)}, u32[]{:S(2)}, u32[]{:S(2)}) %collective-permute-start) | collective-permute-done | bytes 327712 | tf_op jit(solution)/shard_map/ppermute | solution.py:306
  14.6 1.5 %collective-permute-start.2 = (bf16[640,256]{1,0:T(8,128)(2,1)S(1)}, bf16[640,256]{1,0:T(8,128)(2,1)S(1)}, u32[]{:S(2)}, u32[]{:S(2)}) collective-permute-start(bf16[640,256]{1,0:T(8,128)(2,1)S(1)} %collective-permute-done.refs_0_), channel_id=1, source_target_pairs={{0,16},{16,0},{1,17},{17,1},{2,18},{18,2},{3,19},{19,3},{4,20},{20... | collective-permute-start | bytes 983048 | tf_op jit(solution)/shard_map/ppermute | solution.py:301
  16.1 1.7 %collective-permute-start.3 = (bf16[640,256]{1,0:T(8,128)(2,1)S(1)}, bf16[640,256]{1,0:T(8,128)(2,1)S(1)}, u32[]{:S(2)}, u32[]{:S(2)}) collective-permute-start(bf16[640,256]{1,0:T(8,128)(2,1)S(1)} %dynamic-slice_bitcast_fusion), channel_id=1, source_target_pairs={{0,12},{4,0},{8,4},{12,8},{1,13},{5,1},{9,5},{13,9},{2,14},{6,2},{... | collective-permute-start | bytes 983048 | tf_op jit(solution)/shard_map/ppermute | solution.py:306
  17.8 1.5 %collective-permute-start.8 = (bf16[2,640,256]{2,1,0:T(8,128)(2,1)S(1)}, bf16[2,640,256]{2,1,0:T(8,128)(2,1)S(1)}, u32[]{:S(2)}, u32[]{:S(2)}) collective-permute-start(bf16[2,640,256]{2,1,0:T(8,128)(2,1)S(1)} %get-tuple-element.51), channel_id=1, source_target_pairs={{0,2},{2,0},{1,3},{3,1},{4,6},{6,4},{5,7},{7,5},{8,10},{10,8},{9,1... | collective-permute-start | bytes 1966088 | tf_op jit(solution)/shard_map/ppermute | solution.py:301
  19.3 5.4 %collective-permute-done.2.refs_2_ = bf16[640,256]{1,0:T(8,128)(2,1)S(1)} collective-permute-done((bf16[640,256]{1,0:T(8,128)(2,1)S(1)}, bf16[640,256]{1,0:T(8,128)(2,1)S(1)}, u32[]{:S(2)}, u32[]{:S(2)}) %collective-permute-start.2) | collective-permute-done | bytes 327712 | tf_op jit(solution)/shard_map/ppermute | solution.py:301
  24.7 1.2 %collective-permute-done.3.refs_4_ = bf16[640,256]{1,0:T(8,128)(2,1)S(1)} collective-permute-done((bf16[640,256]{1,0:T(8,128)(2,1)S(1)}, bf16[640,256]{1,0:T(8,128)(2,1)S(1)}, u32[]{:S(2)}, u32[]{:S(2)}) %collective-permute-start.3) | collective-permute-done | bytes 327712 | tf_op jit(solution)/shard_map/ppermute | solution.py:306
  26.5 1.5 %collective-permute-start.7 = (bf16[640,256]{1,0:T(8,128)(2,1)S(1)}, bf16[640,256]{1,0:T(8,128)(2,1)S(1)}, u32[]{:S(2)}, u32[]{:S(2)}) collective-permute-start(bf16[640,256]{1,0:T(8,128)(2,1)S(1)} %collective-permute-done.refs_0_), channel_id=1, source_target_pairs={{0,2},{2,0},{1,3},{3,1},{4,6},{6,4},{5,7},{7,5},{8,10},{10,8},{9,1... | collective-permute-start | bytes 983048 | tf_op jit(solution)/shard_map/ppermute | solution.py:301
  27.9 7.5 %collective-permute-done.8.arrived_ref = bf16[2,640,256]{2,1,0:T(8,128)(2,1)S(1)} collective-permute-done((bf16[2,640,256]{2,1,0:T(8,128)(2,1)S(1)}, bf16[2,640,256]{2,1,0:T(8,128)(2,1)S(1)}, u32[]{:S(2)}, u32[]{:S(2)}) %collective-permute-start.8) | collective-permute-done | bytes 655392 | tf_op jit(solution)/shard_map/ppermute | solution.py:301
  35.4 1.3 %collective-permute-done.5.p0 = bf16[640,256]{1,0:T(8,128)(2,1)S(1)} collective-permute-done((bf16[640,256]{1,0:T(8,128)(2,1)S(1)}, bf16[640,256]{1,0:T(8,128)(2,1)S(1)}, u32[]{:S(2)}, u32[]{:S(2)}) %collective-permute-start.5) | collective-permute-done | bytes 327712 | tf_op jit(solution)/shard_map/ppermute | solution.py:306
  36.8 4.7 %collective-permute-done.7.refs_1_ = bf16[640,256]{1,0:T(8,128)(2,1)S(1)} collective-permute-done((bf16[640,256]{1,0:T(8,128)(2,1)S(1)}, bf16[640,256]{1,0:T(8,128)(2,1)S(1)}, u32[]{:S(2)}, u32[]{:S(2)}) %collective-permute-start.7) | collective-permute-done | bytes 327712 | tf_op jit(solution)/shard_map/ppermute | solution.py:301
  42.8 1.5 %collective-permute-start.11 = (bf16[640,256]{1,0:T(8,128)(2,1)S(1)}, bf16[640,256]{1,0:T(8,128)(2,1)S(1)}, u32[]{:S(2)}, u32[]{:S(2)}) collective-permute-start(bf16[640,256]{1,0:T(8,128)(2,1)S(1)} %collective-permute-done.7.refs_1_), channel_id=1, source_target_pairs={{0,16},{16,0},{1,17},{17,1},{2,18},{18,2},{3,19},{19,3},{4,20},{20... | collective-permute-start | bytes 983048 | tf_op jit(solution)/shard_map/ppermute | solution.py:301
  44.3 1.5 %collective-permute-start.12 = (bf16[640,256]{1,0:T(8,128)(2,1)S(1)}, bf16[640,256]{1,0:T(8,128)(2,1)S(1)}, u32[]{:S(2)}, u32[]{:S(2)}) collective-permute-start(bf16[640,256]{1,0:T(8,128)(2,1)S(1)} %collective-permute-done.3.refs_4_), channel_id=1, source_target_pairs={{0,2},{2,0},{1,3},{3,1},{4,6},{6,4},{5,7},{7,5},{8,10},{10,8},{9,1... | collective-permute-start | bytes 983048 | tf_op jit(solution)/shard_map/ppermute | solution.py:301
  46.4 6.5 %collective-permute-done.10.p2 = bf16[640,256]{1,0:T(8,128)(2,1)S(1)} collective-permute-done((bf16[640,256]{1,0:T(8,128)(2,1)S(1)}, bf16[640,256]{1,0:T(8,128)(2,1)S(1)}, u32[]{:S(2)}, u32[]{:S(2)}) %collective-permute-start.10) | collective-permute-done | bytes 327712 | tf_op jit(solution)/shard_map/ppermute | solution.py:301
  52.9 6.8 %collective-permute-done.11.refs_3_ = bf16[640,256]{1,0:T(8,128)(2,1)S(1)} collective-permute-done((bf16[640,256]{1,0:T(8,128)(2,1)S(1)}, bf16[640,256]{1,0:T(8,128)(2,1)S(1)}, u32[]{:S(2)}, u32[]{:S(2)}) %collective-permute-start.11) | collective-permute-done | bytes 327712 | tf_op jit(solution)/shard_map/ppermute | solution.py:301
  59.7 1.5 %collective-permute-done.9.p1 = bf16[640,256]{1,0:T(8,128)(2,1)S(1)} collective-permute-done((bf16[640,256]{1,0:T(8,128)(2,1)S(1)}, bf16[640,256]{1,0:T(8,128)(2,1)S(1)}, u32[]{:S(2)}, u32[]{:S(2)}) %collective-permute-start.9) | collective-permute-done | bytes 327712 | tf_op jit(solution)/shard_map/ppermute | solution.py:301
  62.3 1.5 %collective-permute-start.14 = (bf16[640,256]{1,0:T(8,128)(2,1)S(1)}, bf16[640,256]{1,0:T(8,128)(2,1)S(1)}, u32[]{:S(2)}, u32[]{:S(2)}) collective-permute-start(bf16[640,256]{1,0:T(8,128)(2,1)S(1)} %collective-permute-done.10.p2), channel_id=1, source_target_pairs={{0,2},{2,0},{1,3},{3,1},{4,6},{6,4},{5,7},{7,5},{8,10},{10,8},{9,1... | collective-permute-start | bytes 983048 | tf_op jit(solution)/shard_map/ppermute | solution.py:301
  64.5 7.1 %collective-permute-done.15.refs_7_ = bf16[640,256]{1,0:T(8,128)(2,1)S(1)} collective-permute-done((bf16[640,256]{1,0:T(8,128)(2,1)S(1)}, bf16[640,256]{1,0:T(8,128)(2,1)S(1)}, u32[]{:S(2)}, u32[]{:S(2)}) %collective-permute-start.15) | collective-permute-done | bytes 327712 | tf_op jit(solution)/shard_map/ppermute | solution.py:301
  71.5 1.4 %project.1.sums_ref = f32[2,256,256]{2,1,0:T(8,128)S(1)} custom-call(bf16[256,2560]{1,0:T(8,128)(2,1)S(1)} %get-tuple-element.45.own_ref, bf16[256,2560]{1,0:T(8,128)(2,1)S(1)} %collective-permute-done.4.other_ref, bf16[2,1280,256]{2,1,0:T(8,128)(2,1)S(1)} %copy-done.1, bf16[640,256]{1,0:T(8,128)(2,1)S(1)} %collective-permute-done.refs_0_, ...), custom_call_target="tpu_custom_call" | custom-call | flops 1006632960 | bytes 7000000 | tf_op jit(solution)/shard_map/project/pallas_call | solution.py:91
  73.0 5.1 %attention.1 = (bf16[256,1280]{1,0:T(8,128)(2,1)}, bf16[256,512]{1,0:T(8,128)(2,1)S(1)}) custom-call(bf16[256,2560]{1,0:T(8,128)(2,1)S(1)} %get-tuple-element.45.own_ref, bf16[256,2560]{1,0:T(8,128)(2,1)S(1)} %collective-permute-done.4.other_ref, bf16[640,256]{1,0:T(8,128)(2,1)S(1)} %collective-permute-done.5.p0, ...), custom_call_target="tpu_custom_call" | custom-call | flops 838860800 | bytes 5000000 | tf_op jit(solution)/shard_map/attention/pallas_call | solution.py:165
  78.8 1.5 %collective-permute-start.18 = (bf16[256,512]{1,0:T(8,128)(2,1)S(1)}, bf16[256,512]{1,0:T(8,128)(2,1)S(1)}, u32[]{:S(2)}, u32[]{:S(2)}) collective-permute-start(bf16[256,512]{1,0:T(8,128)(2,1)S(1)} %get-tuple-element.72.refs_12_), channel_id=1, source_target_pairs={{0,2},{2,0},{1,3},{3,1},{4,6},{6,4},{5,7},{7,5},{8,10},{10,8},{9,1... | collective-permute-start | bytes 786440 | tf_op jit(solution)/shard_map/ppermute | solution.py:301
  80.3 7.1 %collective-permute-done.17.refs_14_ = bf16[256,512]{1,0:T(8,128)(2,1)S(1)} collective-permute-done((bf16[256,512]{1,0:T(8,128)(2,1)S(1)}, bf16[256,512]{1,0:T(8,128)(2,1)S(1)}, u32[]{:S(2)}, u32[]{:S(2)}) %collective-permute-start.17) | collective-permute-done | bytes 262176 | tf_op jit(solution)/shard_map/ppermute | solution.py:306
  87.4 1.7 %collective-permute-start.20 = (bf16[256,512]{1,0:T(8,128)(2,1)S(1)}, bf16[256,512]{1,0:T(8,128)(2,1)S(1)}, u32[]{:S(2)}, u32[]{:S(2)}) collective-permute-start(bf16[256,512]{1,0:T(8,128)(2,1)S(1)} %get-tuple-element.72.refs_12_), channel_id=1, source_target_pairs={{0,12},{4,0},{8,4},{12,8},{1,13},{5,1},{9,5},{13,9},{2,14},{6,2},{... | collective-permute-start | bytes 786440 | tf_op jit(solution)/shard_map/ppermute | solution.py:306
  89.1 1.5 %collective-permute-start.21 = (bf16[256,512]{1,0:T(8,128)(2,1)S(1)}, bf16[256,512]{1,0:T(8,128)(2,1)S(1)}, u32[]{:S(2)}, u32[]{:S(2)}) collective-permute-start(bf16[256,512]{1,0:T(8,128)(2,1)S(1)} %collective-permute-done.17.refs_14_), channel_id=1, source_target_pairs={{0,2},{2,0},{1,3},{3,1},{4,6},{6,4},{5,7},{7,5},{8,10},{10,8},{9,1... | collective-permute-start | bytes 786440 | tf_op jit(solution)/shard_map/ppermute | solution.py:301
  91.1 3.2 %collective-permute-done.20.refs_15_ = bf16[256,512]{1,0:T(8,128)(2,1)S(1)} collective-permute-done((bf16[256,512]{1,0:T(8,128)(2,1)S(1)}, bf16[256,512]{1,0:T(8,128)(2,1)S(1)}, u32[]{:S(2)}, u32[]{:S(2)}) %collective-permute-start.20) | collective-permute-done | bytes 262176 | tf_op jit(solution)/shard_map/ppermute | solution.py:306
  96.1 1.5 %collective-permute-start.23 = (bf16[256,512]{1,0:T(8,128)(2,1)S(1)}, bf16[256,512]{1,0:T(8,128)(2,1)S(1)}, u32[]{:S(2)}, u32[]{:S(2)}) collective-permute-start(bf16[256,512]{1,0:T(8,128)(2,1)S(1)} %collective-permute-done.20.refs_15_), channel_id=1, source_target_pairs={{0,2},{2,0},{1,3},{3,1},{4,6},{6,4},{5,7},{7,5},{8,10},{10,8},{9,1... | collective-permute-start | bytes 786440 | tf_op jit(solution)/shard_map/ppermute | solution.py:301
  97.6 6.1 %collective-permute-done.22.refs_4_ = bf16[256,512]{1,0:T(8,128)(2,1)S(1)} collective-permute-done((bf16[256,512]{1,0:T(8,128)(2,1)S(1)}, bf16[256,512]{1,0:T(8,128)(2,1)S(1)}, u32[]{:S(2)}, u32[]{:S(2)}) %collective-permute-start.22) | collective-permute-done | bytes 262176 | tf_op jit(solution)/shard_map/ppermute | solution.py:306
  103.7 1.5 %collective-permute-start.24 = (bf16[256,512]{1,0:T(8,128)(2,1)S(1)}, bf16[256,512]{1,0:T(8,128)(2,1)S(1)}, u32[]{:S(2)}, u32[]{:S(2)}) collective-permute-start(bf16[256,512]{1,0:T(8,128)(2,1)S(1)} %collective-permute-done.22.refs_4_), channel_id=1, source_target_pairs={{0,2},{2,0},{1,3},{3,1},{4,6},{6,4},{5,7},{7,5},{8,10},{10,8},{9,1... | collective-permute-start | bytes 786440 | tf_op jit(solution)/shard_map/ppermute | solution.py:301
  105.2 1.7 %gradient.2 = (f32[2,640,256]{2,1,0:T(8,128)S(1)}, f32[2,256]{1,0:T(2,128)S(1)}) custom-call(bf16[2,640,256]{2,1,0:T(8,128)(2,1)S(1)} %collective-permute-done.13.refs_0_.refs_1_, bf16[2,640,256]{2,1,0:T(8,128)(2,1)S(1)} %collective-permute-done.13.refs_0_.refs_1_, bf16[2,640,256]{2,1,0:T(8,128)(2,1)S(1)} %collective-permute-done.16.refs_2_.refs_3_.refs_4_.refs_5_, ...), custom_call_target="tpu_custom_call" | custom-call | flops 1006632960 | bytes 5000000 | tf_op jit(solution)/shard_map/gradient/pallas_call | solution.py:230
  106.9 3.1 %collective-permute-done.24.refs_5_ = bf16[256,512]{1,0:T(8,128)(2,1)S(1)} collective-permute-done((bf16[256,512]{1,0:T(8,128)(2,1)S(1)}, bf16[256,512]{1,0:T(8,128)(2,1)S(1)}, u32[]{:S(2)}, u32[]{:S(2)}) %collective-permute-start.24) | collective-permute-done | bytes 262176 | tf_op jit(solution)/shard_map/ppermute | solution.py:301
  110.1 1.7 %gradient.3 = (f32[2,640,256]{2,1,0:T(8,128)}, f32[2,256]{1,0:T(2,128)}) custom-call(bf16[2,640,256]{2,1,0:T(8,128)(2,1)S(1)} %collective-permute-done.13.refs_0_.refs_1_, bf16[2,640,256]{2,1,0:T(8,128)(2,1)S(1)} %collective-permute-done.13.refs_0_.refs_1_, bf16[2,640,256]{2,1,0:T(8,128)(2,1)S(1)} %collective-permute-done.19.refs_6_.refs_7_.refs_2_.refs_3_, ...), custom_call_target="tpu_custom_call" | custom-call | flops 335544320 | bytes 5000000 | tf_op jit(solution)/shard_map/gradient/pallas_call | solution.py:230
  (49 shorter events, 10.6 us)
Async XLA Ops:
  0.6 7.2 %copy-start = (bf16[256,2560]{1,0:T(8,128)(2,1)S(1)}, bf16[256,2560]{1,0:T(8,128)(2,1)}, u32[]{:S(2)}) copy-start(bf16[256,2560]{1,0:T(8,128)(2,1)} %values_ref.1) | copy-start | bytes 3932164
  0.6 5.9 %copy-start.4 = (bf16[5120]{0:T(1024)(128)(2,1)S(1)}, bf16[5120]{0:T(1024)(128)(2,1)}, u32[]{:S(2)}) copy-start(bf16[5120]{0:T(1024)(128)(2,1)} %param.7) | copy-start | bytes 30724
  1.8 12.8 %collective-permute-start = (bf16[640,256]{1,0:T(8,128)(2,1)S(1)}, bf16[640,256]{1,0:T(8,128)(2,1)S(1)}, u32[]{:S(2)}, u32[]{:S(2)}) collective-permute-start(bf16[640,256]{1,0:T(8,128)(2,1)S(1)} %dynamic-slice_bitcast_fusion), channel_id=1, source_target_pairs={{0,4},{4,8},{8,12},{12,0},{1,5},{5,9},{9,13},{13,1},{2,6},{6,10},{... | collective-permute-start | bytes 983048 | tf_op jit(solution)/shard_map/ppermute | solution.py:306
  6.5 1.2 %collective-permute-start.1 = (f32[256,1]{0,1:T(1,128)S(1)}, f32[256,1]{0,1:T(1,128)S(1)}, u32[]{:S(2)}, u32[]{:S(2)}) collective-permute-start(f32[256,1]{0,1:T(1,128)S(1)} %bitcast.3), channel_id=1, source_target_pairs={{0,1},{1,0},{2,3},{3,2},{4,5},{5,4},{6,7},{7,6},{8,9},{9,8},{10,11... | collective-permute-start | bytes 3080 | tf_op jit(solution)/shard_map/ppermute | solution.py:301
  7.9 56.4 %copy-start.5 = (bf16[2,256]{1,0:T(2,128)(2,1)S(1)}, bf16[2,256]{1,0:T(2,128)(2,1)}, u32[]{:S(2)}) copy-start(bf16[2,256]{1,0:T(2,128)(2,1)} %param.11) | copy-start | bytes 3076
  8.8 62.7 %copy-start.1 = (bf16[2,1280,256]{2,1,0:T(8,128)(2,1)S(1)}, bf16[2,1280,256]{2,1,0:T(8,128)(2,1)}, u32[]{:S(2)}) copy-start(bf16[2,1280,256]{2,1,0:T(8,128)(2,1)} %weight_ref.1) | copy-start | bytes 3932164
  14.6 11.4 %collective-permute-start.4 = (bf16[256,2560]{1,0:T(8,128)(2,1)S(1)}, bf16[256,2560]{1,0:T(8,128)(2,1)S(1)}, u32[]{:S(2)}, u32[]{:S(2)}) collective-permute-start(bf16[256,2560]{1,0:T(8,128)(2,1)S(1)} %get-tuple-element.45.own_ref), channel_id=1, source_target_pairs={{0,1},{1,0},{2,3},{3,2},{4,5},{5,4},{6,7},{7,6},{8,9},{9,8},{10,11... | collective-permute-start | bytes 3932168 | tf_op jit(solution)/shard_map/ppermute | solution.py:301
  14.6 10.1 %collective-permute-start.2 = (bf16[640,256]{1,0:T(8,128)(2,1)S(1)}, bf16[640,256]{1,0:T(8,128)(2,1)S(1)}, u32[]{:S(2)}, u32[]{:S(2)}) collective-permute-start(bf16[640,256]{1,0:T(8,128)(2,1)S(1)} %collective-permute-done.refs_0_), channel_id=1, source_target_pairs={{0,16},{16,0},{1,17},{17,1},{2,18},{18,2},{3,19},{19,3},{4,20},{20... | collective-permute-start | bytes 983048 | tf_op jit(solution)/shard_map/ppermute | solution.py:301
  16.1 9.8 %collective-permute-start.3 = (bf16[640,256]{1,0:T(8,128)(2,1)S(1)}, bf16[640,256]{1,0:T(8,128)(2,1)S(1)}, u32[]{:S(2)}, u32[]{:S(2)}) collective-permute-start(bf16[640,256]{1,0:T(8,128)(2,1)S(1)} %dynamic-slice_bitcast_fusion), channel_id=1, source_target_pairs={{0,12},{4,0},{8,4},{12,8},{1,13},{5,1},{9,5},{13,9},{2,14},{6,2},{... | collective-permute-start | bytes 983048 | tf_op jit(solution)/shard_map/ppermute | solution.py:306
  17.8 17.6 %collective-permute-start.8 = (bf16[2,640,256]{2,1,0:T(8,128)(2,1)S(1)}, bf16[2,640,256]{2,1,0:T(8,128)(2,1)S(1)}, u32[]{:S(2)}, u32[]{:S(2)}) collective-permute-start(bf16[2,640,256]{2,1,0:T(8,128)(2,1)S(1)} %get-tuple-element.51), channel_id=1, source_target_pairs={{0,2},{2,0},{1,3},{3,1},{4,6},{6,4},{5,7},{7,5},{8,10},{10,8},{9,1... | collective-permute-start | bytes 1966088 | tf_op jit(solution)/shard_map/ppermute | solution.py:301
  25.9 10.8 %collective-permute-start.5 = (bf16[640,256]{1,0:T(8,128)(2,1)S(1)}, bf16[640,256]{1,0:T(8,128)(2,1)S(1)}, u32[]{:S(2)}, u32[]{:S(2)}) collective-permute-start(bf16[640,256]{1,0:T(8,128)(2,1)S(1)} %collective-permute-done.refs_0_), channel_id=1, source_target_pairs={{0,4},{4,8},{8,12},{12,0},{1,5},{5,9},{9,13},{13,1},{2,6},{6,10},{... | collective-permute-start | bytes 983048 | tf_op jit(solution)/shard_map/ppermute | solution.py:306
  25.9 10.8 %collective-permute-start.6 = (bf16[640,256]{1,0:T(8,128)(2,1)S(1)}, bf16[640,256]{1,0:T(8,128)(2,1)S(1)}, u32[]{:S(2)}, u32[]{:S(2)}) collective-permute-start(bf16[640,256]{1,0:T(8,128)(2,1)S(1)} %collective-permute-done.3.refs_4_), channel_id=1, source_target_pairs={{0,16},{16,0},{1,17},{17,1},{2,18},{18,2},{3,19},{19,3},{4,20},{20... | collective-permute-start | bytes 983048 | tf_op jit(solution)/shard_map/ppermute | solution.py:301
  26.5 15.0 %collective-permute-start.7 = (bf16[640,256]{1,0:T(8,128)(2,1)S(1)}, bf16[640,256]{1,0:T(8,128)(2,1)S(1)}, u32[]{:S(2)}, u32[]{:S(2)}) collective-permute-start(bf16[640,256]{1,0:T(8,128)(2,1)S(1)} %collective-permute-done.refs_0_), channel_id=1, source_target_pairs={{0,2},{2,0},{1,3},{3,1},{4,6},{6,4},{5,7},{7,5},{8,10},{10,8},{9,1... | collective-permute-start | bytes 983048 | tf_op jit(solution)/shard_map/ppermute | solution.py:301
  41.5 19.6 %collective-permute-start.13 = (bf16[2,640,256]{2,1,0:T(8,128)(2,1)S(1)}, bf16[2,640,256]{2,1,0:T(8,128)(2,1)S(1)}, u32[]{:S(2)}, u32[]{:S(2)}) collective-permute-start(bf16[2,640,256]{2,1,0:T(8,128)(2,1)S(1)} %get-tuple-element.57), channel_id=1, source_target_pairs={{0,0},{1,8},{4,4},{5,12},{8,1},{9,9},{12,5},{13,13},{2,2},{3,10},{... | collective-permute-start | bytes 1966088 | tf_op jit(solution)/shard_map/ppermute | solution.py:334
  42.2 10.6 %collective-permute-start.10 = (bf16[640,256]{1,0:T(8,128)(2,1)S(1)}, bf16[640,256]{1,0:T(8,128)(2,1)S(1)}, u32[]{:S(2)}, u32[]{:S(2)}) collective-permute-start(bf16[640,256]{1,0:T(8,128)(2,1)S(1)} %collective-permute-done.5.p0), channel_id=1, source_target_pairs={{0,16},{16,0},{1,17},{17,1},{2,18},{18,2},{3,19},{19,3},{4,20},{20... | collective-permute-start | bytes 983048 | tf_op jit(solution)/shard_map/ppermute | solution.py:301
  42.8 16.9 %collective-permute-start.11 = (bf16[640,256]{1,0:T(8,128)(2,1)S(1)}, bf16[640,256]{1,0:T(8,128)(2,1)S(1)}, u32[]{:S(2)}, u32[]{:S(2)}) collective-permute-start(bf16[640,256]{1,0:T(8,128)(2,1)S(1)} %collective-permute-done.7.refs_1_), channel_id=1, source_target_pairs={{0,16},{16,0},{1,17},{17,1},{2,18},{18,2},{3,19},{19,3},{4,20},{20... | collective-permute-start | bytes 983048 | tf_op jit(solution)/shard_map/ppermute | solution.py:301
  44.3 15.4 %collective-permute-start.12 = (bf16[640,256]{1,0:T(8,128)(2,1)S(1)}, bf16[640,256]{1,0:T(8,128)(2,1)S(1)}, u32[]{:S(2)}, u32[]{:S(2)}) collective-permute-start(bf16[640,256]{1,0:T(8,128)(2,1)S(1)} %collective-permute-done.3.refs_4_), channel_id=1, source_target_pairs={{0,2},{2,0},{1,3},{3,1},{4,6},{6,4},{5,7},{7,5},{8,10},{10,8},{9,1... | collective-permute-start | bytes 983048 | tf_op jit(solution)/shard_map/ppermute | solution.py:301
  45.8 15.3 %collective-permute-start.9 = (bf16[640,256]{1,0:T(8,128)(2,1)S(1)}, bf16[640,256]{1,0:T(8,128)(2,1)S(1)}, u32[]{:S(2)}, u32[]{:S(2)}) collective-permute-start(bf16[640,256]{1,0:T(8,128)(2,1)S(1)} %collective-permute-done.5.p0), channel_id=1, source_target_pairs={{0,2},{2,0},{1,3},{3,1},{4,6},{6,4},{5,7},{7,5},{8,10},{10,8},{9,1... | collective-permute-start | bytes 983048 | tf_op jit(solution)/shard_map/ppermute | solution.py:301
  61.2 17.6 %collective-permute-start.16 = (bf16[2,640,256]{2,1,0:T(8,128)(2,1)S(1)}, bf16[2,640,256]{2,1,0:T(8,128)(2,1)S(1)}, u32[]{:S(2)}, u32[]{:S(2)}) collective-permute-start(bf16[2,640,256]{2,1,0:T(8,128)(2,1)S(1)} %get-tuple-element.68), channel_id=1, source_target_pairs={{0,4},{1,12},{4,0},{5,8},{8,5},{9,13},{12,1},{13,9},{2,6},{3,14},{... | collective-permute-start | bytes 1966088 | tf_op jit(solution)/shard_map/ppermute | solution.py:334
  61.8 9.8 %collective-permute-start.15 = (bf16[640,256]{1,0:T(8,128)(2,1)S(1)}, bf16[640,256]{1,0:T(8,128)(2,1)S(1)}, u32[]{:S(2)}, u32[]{:S(2)}) collective-permute-start(bf16[640,256]{1,0:T(8,128)(2,1)S(1)} %collective-permute-done.12.refs_5_), channel_id=1, source_target_pairs={{0,16},{16,0},{1,17},{17,1},{2,18},{18,2},{3,19},{19,3},{4,20},{20... | collective-permute-start | bytes 983048 | tf_op jit(solution)/shard_map/ppermute | solution.py:301
  62.3 10.7 %collective-permute-start.14 = (bf16[640,256]{1,0:T(8,128)(2,1)S(1)}, bf16[640,256]{1,0:T(8,128)(2,1)S(1)}, u32[]{:S(2)}, u32[]{:S(2)}) collective-permute-start(bf16[640,256]{1,0:T(8,128)(2,1)S(1)} %collective-permute-done.10.p2), channel_id=1, source_target_pairs={{0,2},{2,0},{1,3},{3,1},{4,6},{6,4},{5,7},{7,5},{8,10},{10,8},{9,1... | collective-permute-start | bytes 983048 | tf_op jit(solution)/shard_map/ppermute | solution.py:301
  64.5 8.5 %copy-start.2 = (bf16[256,1280]{1,0:T(8,128)(2,1)S(1)}, bf16[256,1280]{1,0:T(8,128)(2,1)}, u32[]{:S(2)}) copy-start(bf16[256,1280]{1,0:T(8,128)(2,1)} %queries_ref.1) | copy-start | bytes 1966084
  64.5 8.5 %copy-start.3 = (bf16[256,1280]{1,0:T(8,128)(2,1)S(1)}, bf16[256,1280]{1,0:T(8,128)(2,1)}, u32[]{:S(2)}) copy-start(bf16[256,1280]{1,0:T(8,128)(2,1)} %cotangent_ref.1) | copy-start | bytes 1966084
  78.8 8.6 %collective-permute-start.17 = (bf16[256,512]{1,0:T(8,128)(2,1)S(1)}, bf16[256,512]{1,0:T(8,128)(2,1)S(1)}, u32[]{:S(2)}, u32[]{:S(2)}) collective-permute-start(bf16[256,512]{1,0:T(8,128)(2,1)S(1)} %get-tuple-element.72.refs_12_), channel_id=1, source_target_pairs={{0,4},{4,8},{8,12},{12,0},{1,5},{5,9},{9,13},{13,1},{2,6},{6,10},{... | collective-permute-start | bytes 786440 | tf_op jit(solution)/shard_map/ppermute | solution.py:306
  78.8 8.6 %collective-permute-start.18 = (bf16[256,512]{1,0:T(8,128)(2,1)S(1)}, bf16[256,512]{1,0:T(8,128)(2,1)S(1)}, u32[]{:S(2)}, u32[]{:S(2)}) collective-permute-start(bf16[256,512]{1,0:T(8,128)(2,1)S(1)} %get-tuple-element.72.refs_12_), channel_id=1, source_target_pairs={{0,2},{2,0},{1,3},{3,1},{4,6},{6,4},{5,7},{7,5},{8,10},{10,8},{9,1... | collective-permute-start | bytes 786440 | tf_op jit(solution)/shard_map/ppermute | solution.py:301
  87.4 7.0 %collective-permute-start.20 = (bf16[256,512]{1,0:T(8,128)(2,1)S(1)}, bf16[256,512]{1,0:T(8,128)(2,1)S(1)}, u32[]{:S(2)}, u32[]{:S(2)}) collective-permute-start(bf16[256,512]{1,0:T(8,128)(2,1)S(1)} %get-tuple-element.72.refs_12_), channel_id=1, source_target_pairs={{0,12},{4,0},{8,4},{12,8},{1,13},{5,1},{9,5},{13,9},{2,14},{6,2},{... | collective-permute-start | bytes 786440 | tf_op jit(solution)/shard_map/ppermute | solution.py:306
  89.1 6.4 %collective-permute-start.21 = (bf16[256,512]{1,0:T(8,128)(2,1)S(1)}, bf16[256,512]{1,0:T(8,128)(2,1)S(1)}, u32[]{:S(2)}, u32[]{:S(2)}) collective-permute-start(bf16[256,512]{1,0:T(8,128)(2,1)S(1)} %collective-permute-done.17.refs_14_), channel_id=1, source_target_pairs={{0,2},{2,0},{1,3},{3,1},{4,6},{6,4},{5,7},{7,5},{8,10},{10,8},{9,1... | collective-permute-start | bytes 786440 | tf_op jit(solution)/shard_map/ppermute | solution.py:301
  90.6 14.6 %collective-permute-start.19 = (bf16[2,640,256]{2,1,0:T(8,128)(2,1)S(1)}, bf16[2,640,256]{2,1,0:T(8,128)(2,1)S(1)}, u32[]{:S(2)}, u32[]{:S(2)}) collective-permute-start(bf16[2,640,256]{2,1,0:T(8,128)(2,1)S(1)} %collective-permute-done.13.refs_0_.refs_1_), channel_id=1, source_target_pairs={{0,1},{1,0},{2,3},{3,2},{4,5},{5,4},{6,7},{7,6},{8,9},{9,8},{10,11... | collective-permute-start | bytes 1966088 | tf_op jit(solution)/shard_map/ppermute | solution.py:301
  90.6 14.6 %collective-permute-start.25 = (bf16[2,640,256]{2,1,0:T(8,128)(2,1)S(1)}, bf16[2,640,256]{2,1,0:T(8,128)(2,1)S(1)}, u32[]{:S(2)}, u32[]{:S(2)}) collective-permute-start(bf16[2,640,256]{2,1,0:T(8,128)(2,1)S(1)} %collective-permute-done.16.refs_2_.refs_3_.refs_4_.refs_5_), channel_id=1, source_target_pairs={{0,1},{1,0},{2,3},{3,2},{4,5},{5,4},{6,7},{7,6},{8,9},{9,8},{10,11... | collective-permute-start | bytes 1966088 | tf_op jit(solution)/shard_map/ppermute | solution.py:301
  95.5 8.2 %collective-permute-start.22 = (bf16[256,512]{1,0:T(8,128)(2,1)S(1)}, bf16[256,512]{1,0:T(8,128)(2,1)S(1)}, u32[]{:S(2)}, u32[]{:S(2)}) collective-permute-start(bf16[256,512]{1,0:T(8,128)(2,1)S(1)} %collective-permute-done.17.refs_14_), channel_id=1, source_target_pairs={{0,4},{4,8},{8,12},{12,0},{1,5},{5,9},{9,13},{13,1},{2,6},{6,10},{... | collective-permute-start | bytes 786440 | tf_op jit(solution)/shard_map/ppermute | solution.py:306
  96.1 7.6 %collective-permute-start.23 = (bf16[256,512]{1,0:T(8,128)(2,1)S(1)}, bf16[256,512]{1,0:T(8,128)(2,1)S(1)}, u32[]{:S(2)}, u32[]{:S(2)}) collective-permute-start(bf16[256,512]{1,0:T(8,128)(2,1)S(1)} %collective-permute-done.20.refs_15_), channel_id=1, source_target_pairs={{0,2},{2,0},{1,3},{3,1},{4,6},{6,4},{5,7},{7,5},{8,10},{10,8},{9,1... | collective-permute-start | bytes 786440 | tf_op jit(solution)/shard_map/ppermute | solution.py:301
  103.7 6.4 %collective-permute-start.24 = (bf16[256,512]{1,0:T(8,128)(2,1)S(1)}, bf16[256,512]{1,0:T(8,128)(2,1)S(1)}, u32[]{:S(2)}, u32[]{:S(2)}) collective-permute-start(bf16[256,512]{1,0:T(8,128)(2,1)S(1)} %collective-permute-done.22.refs_4_), channel_id=1, source_target_pairs={{0,2},{2,0},{1,3},{3,1},{4,6},{6,4},{5,7},{7,5},{8,10},{10,8},{9,1... | collective-permute-start | bytes 786440 | tf_op jit(solution)/shard_map/ppermute | solution.py:301

commit v12 on v10

--- a/solution.py
+++ b/solution.py
@@ -107,9 +107,13 @@
     length, columns = cosine.shape[0], pair_ref.shape[1] // 2
     key_heads = columns // HEAD
     group_size = queries_ref.shape[1] // columns
-    key_at = lax.broadcasted_iota(jnp.int32, (length, length), 0)
-    query_at = lax.broadcasted_iota(jnp.int32, (length, length), 1)
-    causal = key_at <= query_at
+    part = length // 2
+    masks = []
+    for half in range(2):
+        seen = part * (half + 1)
+        key_at = lax.broadcasted_iota(jnp.int32, (seen, part), 0)
+        query_at = lax.broadcasted_iota(jnp.int32, (seen, part), 1) + half * part
+        masks.append(key_at <= query_at)
     for head in range(key_heads):
         lanes = slice(head * HEAD, (head + 1) * HEAD)
         raw = raw_of(0, lanes)
@@ -117,38 +121,52 @@
         keys = wide_keys.astype(jnp.bfloat16)
         keys_across = wide_keys.T.astype(jnp.bfloat16)
         values = raw_of(1, lanes).astype(jnp.bfloat16)
-        grad_rotated = jnp.zeros((length, HEAD), jnp.float32)
-        grad_value = jnp.zeros((length, HEAD), jnp.float32)
+        grad_rotated = [jnp.zeros((part * (half + 1), HEAD), jnp.float32) for half in range(2)]
+        grad_value = [jnp.zeros((part * (half + 1), HEAD), jnp.float32) for half in range(2)]
         for member in range(group_size):
             start = (head * group_size + member) * HEAD
-            query = queries_ref[:, start : start + HEAD]
-            upstream = cotangent_ref[:, start : start + HEAD]
-            scores = jnp.where(causal, product_rows(keys, query), -jnp.inf)
-            peak = jnp.max(scores, 0, keepdims=True)
-            exponentials = jnp.exp((scores - peak) * SCALE)
-            probability = exponentials * (1.0 / jnp.sum(exponentials, 0, keepdims=True))
-            grad_probability = product_rows(values, upstream)
-            total = jnp.sum(probability * grad_probability, 0, keepdims=True)
-            grad_scores = (probability * (grad_probability - total) * SCALE).astype(jnp.bfloat16)
-            grad_rotated += product(grad_scores, query)
-            grad_value += product(probability.astype(jnp.bfloat16), upstream)
-            grad_query = product(keys_across, grad_scores)
-            grad_query_ref[:, start : start + HEAD] = grad_query.T.astype(jnp.bfloat16)
-        grad_key = grad_rotated * cosine - pltpu.roll(grad_rotated, HEAD // 2, 1) * sine
-        pair_ref[:, lanes] = grad_key.astype(jnp.bfloat16)
-        pair_ref[:, columns + head * HEAD : columns + (head + 1) * HEAD] = grad_value.astype(
-            jnp.bfloat16
-        )
-
-
-def attention_kernel(
-    distance, own_ref, other_ref, p0, p1, p2, p3, sums_ref, bias_ref, cosine_ref, sine_ref,
-    queries_ref, cotangent_ref, grad_query_ref, pair_ref, raw_ref,
-):
+            for half in range(2):
+                seen = part * (half + 1)
+                rows = slice(half * part, (half + 1) * part)
+                query = queries_ref[rows, start : start + HEAD]
+                upstream = cotangent_ref[rows, start : start + HEAD]
+                scores = jnp.where(masks[half], product_rows(keys[:seen], query), -jnp.inf)
+                peak = jnp.max(scores, 0, keepdims=True)
+                exponentials = jnp.exp((scores - peak) * SCALE)
+                probability = exponentials * (1.0 / jnp.sum(exponentials, 0, keepdims=True))
+                grad_probability = product_rows(values[:seen], upstream)
+                total = jnp.sum(probability * grad_probability, 0, keepdims=True)
+                grad_scores = (probability * (grad_probability - total) * SCALE).astype(
+                    jnp.bfloat16
+                )
+                grad_rotated[half] += product(grad_scores, query)
+                grad_value[half] += product(probability.astype(jnp.bfloat16), upstream)
+                grad_query = product(keys_across[:, :seen], grad_scores)
+                grad_query_ref[rows, start : start + HEAD] = grad_query.T.astype(jnp.bfloat16)
+        for half in range(2):
+            rows = slice(half * part, (half + 1) * part)
+            rotated, value = grad_rotated[1][rows], grad_value[1][rows]
+            if half == 0:
+                rotated, value = rotated + grad_rotated[0], value + grad_value[0]
+            grad_key = rotated * cosine[rows] - pltpu.roll(rotated, HEAD // 2, 1) * sine[rows]
+            pair_ref[rows, lanes] = grad_key.astype(jnp.bfloat16)
+            pair_ref[rows, columns + head * HEAD : columns + (head + 1) * HEAD] = value.astype(
+                jnp.bfloat16
+            )
+
+
+def attention_kernel(distances, own_ref, other_ref, *refs):
+    pieces, refs = refs[: 4 * len(distances)], refs[4 * len(distances) :]
+    sums_ref, bias_ref, cosine_ref, sine_ref, queries_ref, cotangent_ref = refs[:6]
+    grad_query_ref, pair_ref, raw_ref = refs[6:]
     group = lax.axis_index("groups")
-    terms = block_terms(own_ref, other_ref, block_from(distance), (p0, p1, p2, p3))
-    raw_ref[group] = sums_ref[group] + terms[0]
-    raw_ref[1 - group] = sums_ref[1 - group] + terms[1]
+    totals = [sums_ref[group], sums_ref[1 - group]]
+    for at, distance in enumerate(distances):
+        four = pieces[4 * at : 4 * at + 4]
+        terms = block_terms(own_ref, other_ref, block_from(distance), four)
+        totals = [total + term for total, term in zip(totals, terms)]
+    raw_ref[group] = totals[0]
+    raw_ref[1 - group] = totals[1]
 
     def raw_of(j, lanes):
         return raw_ref[j, :, lanes] + bias_ref[j : j + 1, lanes]
@@ -158,12 +176,14 @@
     )
 
 
-def attention(distance, normed, normed_other, pieces, sums, bias, cosine, sine, queries, cotangent):
+def attention(gathered, normed, normed_other, sums, bias, cosine, sine, queries, cotangent):
     length = normed.shape[0]
+    distances = tuple(distance for distance, _ in gathered)
+    pieces = [piece for _, four in gathered for piece in four]
     columns = pieces[0].shape[1]
     operands = (normed, normed_other, *pieces, sums, bias, cosine, sine, queries, cotangent)
     return pl.pallas_call(
-        functools.partial(attention_kernel, distance),
+        functools.partial(attention_kernel, distances),
         in_specs=[IN_VMEM] * len(operands),
         out_specs=[IN_VMEM] * 2,
         scratch_shapes=[pltpu.VMEM(sums.shape, jnp.float32)],
@@ -244,9 +264,10 @@
     )(*own, *other, *pairs, *(sums or ()))
 
 
-def norm_kernel(values_ref, scale_ref, gain_ref, normed_ref, kept_ref, sent_ref):
+def norm_kernel(values_ref, scale_ref, gain_ref, normed_ref, *slab_refs):
     replica, replicas = lax.axis_index("dp"), lax.axis_size("dp")
-    share = kept_ref.shape[1]
+    parity = lax.rem(lax.axis_index("blk"), 2)
+    share = slab_refs[0].shape[0]
 
     def scaled(place):
         wide_values = values_ref[:, place].astype(jnp.float32)
@@ -255,19 +276,20 @@
     for slab in range(2 * replicas):
         place = pl.ds(slab * share, share)
         normed_ref[:, place] = scaled(place).astype(jnp.bfloat16)
-    for at in range(2):
-        for ref, owner in ((kept_ref, replica), (sent_ref, 1 - replica)):
+    for turn in range(2):
+        at = lax.rem(turn + parity, 2)
+        for ref, owner in zip(slab_refs[2 * turn :], (replica, 1 - replica)):
             place = pl.ds(pl.multiple_of((at * replicas + owner) * share, 128), share)
-            ref[at] = scaled(place).T.astype(jnp.bfloat16)
+            ref[...] = scaled(place).T.astype(jnp.bfloat16)
 
 
 def norm(activations, scale, gain, share):
     length, features = activations.shape
-    shapes = [activations.shape, (2, share, length), (2, share, length)]
+    shapes = [activations.shape] + [(share, length)] * 4
     return pl.pallas_call(
         norm_kernel,
         in_specs=[IN_VMEM] * 3,
-        out_specs=[IN_VMEM] * 3,
+        out_specs=[IN_VMEM] * 5,
         out_shape=[jax.ShapeDtypeStruct(shape, jnp.bfloat16) for shape in shapes],
         compiler_params=pltpu.CompilerParams(vmem_limit_bytes=VMEM_BYTES),
         cost_estimate=pl.CostEstimate(
@@ -277,22 +299,19 @@
     )(activations, scale, gain)
 
 
-def pack_kernel(kept_ref, arrived_ref, even_ref, odd_ref):
-    parity = lax.rem(lax.axis_index("blk"), 2)
-    for turn, ref in enumerate((even_ref, odd_ref)):
-        at = lax.rem(turn + parity, 2)
-        ref[0] = kept_ref[at]
-        ref[1] = arrived_ref[at]
+def pack_kernel(kept_ref, arrived_ref, packed_ref):
+    packed_ref[0] = kept_ref[...]
+    packed_ref[1] = arrived_ref[...]
 
 
 def pack(kept, arrived):
     return pl.pallas_call(
         pack_kernel,
         in_specs=[IN_VMEM] * 2,
-        out_specs=[IN_VMEM] * 2,
-        out_shape=[jax.ShapeDtypeStruct(kept.shape, kept.dtype)] * 2,
+        out_specs=IN_VMEM,
+        out_shape=jax.ShapeDtypeStruct((2, *kept.shape), kept.dtype),
         compiler_params=pltpu.CompilerParams(vmem_limit_bytes=VMEM_BYTES),
-        cost_estimate=pl.CostEstimate(flops=0, bytes_accessed=2600000, transcendentals=0),
+        cost_estimate=pl.CostEstimate(flops=0, bytes_accessed=1300000, transcendentals=0),
         name="pack",
     )(kept, arrived)
 
@@ -366,30 +385,39 @@
         )
 
     up = turned(piece, "blk", 1)
-    normed, kept, sent = norm(activations, scale, gain[None, :], share)
-    up, piece, normed, kept, sent = lax.optimization_barrier((up, piece, normed, kept, sent))
+    normed, kept_even, sent_even, kept_odd, sent_odd = norm(
+        activations, scale, gain[None, :], share
+    )
+    arrived_even = swapped(sent_even, "dp")
+    up, piece, normed, sent_odd, arrived_even = lax.optimization_barrier(
+        (up, piece, normed, sent_odd, arrived_even)
+    )
     up_x, up_y, down = swapped(up, "dp"), swapped(up, "groups"), turned(piece, "blk", -1)
-    arrived = swapped(sent, "dp")
     normed_other = swapped(normed, "sub")
-    up, up_y, down, normed_other = lax.optimization_barrier((up, up_y, down, normed_other))
+    up, up_x, up_y, down, normed_other, sent_odd = lax.optimization_barrier(
+        (up, up_x, up_y, down, normed_other, sent_odd)
+    )
     down_x, down_y = swapped(down, "dp"), swapped(down, "groups")
     twice = turned(up, "blk", 1)
-    twice, down_y, up_x, arrived = lax.optimization_barrier((twice, down_y, up_x, arrived))
+    twice, down_x, down_y, up_x, sent_odd, arrived_even = lax.optimization_barrier(
+        (twice, down_x, down_y, up_x, sent_odd, arrived_even)
+    )
     twice_x, twice_y = swapped(twice, "dp"), swapped(twice, "groups")
     up_both = swapped(up_x, "groups")
-    even, odd = pack(kept, arrived)
-    even = sent_along(even, 0)
-    twice_x, twice_y, up_both, down_x, even = lax.optimization_barrier(
-        (twice_x, twice_y, up_both, down_x, even)
+    even = sent_along(pack(kept_even, arrived_even), 0)
+    arrived_odd = swapped(sent_odd, "dp")
+    twice_x, twice_y, up_both, arrived_odd, even = lax.optimization_barrier(
+        (twice_x, twice_y, up_both, arrived_odd, even)
     )
     down_both, twice_both = swapped(down_x, "groups"), swapped(twice_y, "dp")
-    odd = sent_along(after(odd, even), 1)
-
-    gathered = [(1, (up, up_x, up_y, up_both)), (-1, (down, down_x, down_y, down_both))]
-    sums = project(normed, normed_other, kv_weight, gathered)
+    odd = sent_along(pack(kept_odd, arrived_odd), 1)
+    sums = project(normed, normed_other, kv_weight, [(1, (up, up_x, up_y, up_both))])
+    gathered = [
+        (-1, (down, down_x, down_y, down_both)),
+        (2, (twice, twice_x, twice_y, twice_both)),
+    ]
     grad_query, grad_pair = attention(
-        2, normed, normed_other, (twice, twice_x, twice_y, twice_both), sums, bias, cosine, sine,
-        queries, cotangent,
+        gathered, normed, normed_other, sums, bias, cosine, sine, queries, cotangent
     )
 
     grad_pair, odd = lax.optimization_barrier((grad_pair, odd))

time: 113 us -> 117 us (1.035)
  starting transfers between devices: 20.4 us -> 28.7 us
  waiting for transfers between devices: 76.7 us -> 70.6 us
  Pallas kernels: 11 us -> 13.2 us
    ppermute x18 -> x19, waiting for transfers between devices: 49.3 us -> 34.4 us  [swapped(): return lax.ppermute(block, axis, [(0, 1), (1, 0)])]
    ppermute x6, waiting for transfers between devices: 26.9 us -> 36.1 us  [turned(): lax.ppermute(block, axis, [(i, (i + distance) % size) for i in range(size)])]
    ppermute x6, starting transfers between devices: 7.11 us -> 10.7 us  [turned(): lax.ppermute(block, axis, [(i, (i + distance) % size) for i in range(size)])]
    ppermute x2, starting transfers between devices: 0.71 us -> 3.76 us  [sent_along(): return lax.ppermute(slabs, ('blk', 'sub'), route)]
    pallas_call x2 -> x3, Pallas kernels: 5.17 us -> 7.79 us  [the longest x1 7.7 us: attention(): pl.pallas_call(functools.partial(attention_kernel, distances), in_specs=[...]
    ppermute x18 -> x19, starting transfers between devices: 12.5 us -> 14.2 us  [swapped(): return lax.ppermute(block, axis, [(0, 1), (1, 0)])]
  transfers between devices with their start and end apart: 26 -> 27, of which waited for: 15 -> 17; matrix products, arithmetic and copies ran while one was open for 2% -> 2% of each run, Pallas kernels for 8% -> 10%
where the time goes in v12:
time: 117 us
  waiting for transfers between devices  70.6 us (60%)
  starting transfers between devices  28.7 us (25%)
  Pallas kernels  13.2 us (11%)
  other arithmetic  2.4 us (2%)
  local copies, waits for them, and re-layouts  1.3 us (1%)
    ppermute x6, waiting for transfers between devices, turned(): lax.ppermute(block, axis, [(i, (i + distance) % size) for i in range(size)])  36.1 us
    ppermute x19, waiting for transfers between devices, swapped(): return lax.ppermute(block, axis, [(0, 1), (1, 0)])  34.4 us
    ppermute x19, starting transfers between devices, swapped(): return lax.ppermute(block, axis, [(0, 1), (1, 0)])  14.2 us
    ppermute x6, starting transfers between devices, turned(): lax.ppermute(block, axis, [(i, (i + distance) % size) for i in range(size)])  10.7 us
    pallas_call x1, Pallas kernels, attention(): pl.pallas_call(functools.partial(attention_kernel, distances), in_specs=[...  7.7 us
    ppermute x2, starting transfers between devices, sent_along(): return lax.ppermute(slabs, ('blk', 'sub'), route)  3.76 us
    pallas_call x2, Pallas kernels, gradient(): pl.pallas_call(functools.partial(gradient_kernel, tuple(some), sums is No...  3.48 us
  transfers between devices with their start and end apart: 27, of which 17 were waited for; matrix products, arithmetic and copies ran while one was open for 2% of the time, Pallas kernels for 10%

profile of v12, /device:TPU:0, one launch (start us, length us, event | category | flops | bytes accessed | tf_op | source)
XLA Modules:
  0.0 117.0 jit_solution(2388475969411404372)
XLA Ops:
  0.7 1.1 dynamic-slice_bitcast_fusion
  1.8 3.1 %collective-permute-start = (bf16[640,256]{1,0:T(8,128)(2,1)S(1)}, bf16[640,256]{1,0:T(8,128)(2,1)S(1)}, u32[]{:S(2)}, u32[]{:S(2)}) collective-permute-start(bf16[640,256]{1,0:T(8,128)(2,1)S(1)} %dynamic-slice_bitcast_fusion), channel_id=1, source_target_pairs={{0,4},{4,8},{8,12},{12,0},{1,5},{5,9},{9,13},{13,1},{2,6},{6,10},{... | collective-permute-start | bytes 983048 | tf_op jit(solution)/shard_map/ppermute | solution.py:325
  4.8 1.7 %multiply_reduce_fusion = f32[256]{0:T(256)S(1)} fusion(bf16[256,2560]{1,0:T(8,128)(2,1)} %values_ref.1), kind=kLoop, calls=%fused_computation | loop fusion | flops 1965824 | bytes 1311744 | tf_op jit(solution)/shard_map/reduce_sum | solution.py:360
  8.8 1.6 %collective-permute-start.2 = (bf16[640,256]{1,0:T(8,128)(2,1)S(1)}, bf16[640,256]{1,0:T(8,128)(2,1)S(1)}, u32[]{:S(2)}, u32[]{:S(2)}) collective-permute-start(bf16[640,256]{1,0:T(8,128)(2,1)S(1)} %get-tuple-element.50), channel_id=1, source_target_pairs={{0,2},{2,0},{1,3},{3,1},{4,6},{6,4},{5,7},{7,5},{8,10},{10,8},{9,1... | collective-permute-start | bytes 983048 | tf_op jit(solution)/shard_map/ppermute | solution.py:320
  10.4 4.2 %collective-permute-done.refs_0_ = bf16[640,256]{1,0:T(8,128)(2,1)S(1)} collective-permute-done((bf16[640,256]{1,0:T(8,128)(2,1)S(1)}, bf16[640,256]{1,0:T(8,128)(2,1)S(1)}, u32[]{:S(2)}, u32[]{:S(2)}) %collective-permute-start) | collective-permute-done | bytes 327712 | tf_op jit(solution)/shard_map/ppermute | solution.py:325
  14.6 4.1 %collective-permute-done.2.arrived_ref = bf16[640,256]{1,0:T(8,128)(2,1)S(1)} collective-permute-done((bf16[640,256]{1,0:T(8,128)(2,1)S(1)}, bf16[640,256]{1,0:T(8,128)(2,1)S(1)}, u32[]{:S(2)}, u32[]{:S(2)}) %collective-permute-start.2) | collective-permute-done | bytes 327712 | tf_op jit(solution)/shard_map/ppermute | solution.py:320
  18.7 1.5 %collective-permute-start.3 = (bf16[640,256]{1,0:T(8,128)(2,1)S(1)}, bf16[640,256]{1,0:T(8,128)(2,1)S(1)}, u32[]{:S(2)}, u32[]{:S(2)}) collective-permute-start(bf16[640,256]{1,0:T(8,128)(2,1)S(1)} %collective-permute-done.refs_0_), channel_id=1, source_target_pairs={{0,2},{2,0},{1,3},{3,1},{4,6},{6,4},{5,7},{7,5},{8,10},{10,8},{9,1... | collective-permute-start | bytes 983048 | tf_op jit(solution)/shard_map/ppermute | solution.py:320
  20.2 1.5 %collective-permute-start.4 = (bf16[640,256]{1,0:T(8,128)(2,1)S(1)}, bf16[640,256]{1,0:T(8,128)(2,1)S(1)}, u32[]{:S(2)}, u32[]{:S(2)}) collective-permute-start(bf16[640,256]{1,0:T(8,128)(2,1)S(1)} %collective-permute-done.refs_0_), channel_id=1, source_target_pairs={{0,16},{16,0},{1,17},{17,1},{2,18},{18,2},{3,19},{19,3},{4,20},{20... | collective-permute-start | bytes 983048 | tf_op jit(solution)/shard_map/ppermute | solution.py:320
  21.7 2.2 %collective-permute-start.5 = (bf16[640,256]{1,0:T(8,128)(2,1)S(1)}, bf16[640,256]{1,0:T(8,128)(2,1)S(1)}, u32[]{:S(2)}, u32[]{:S(2)}) collective-permute-start(bf16[640,256]{1,0:T(8,128)(2,1)S(1)} %dynamic-slice_bitcast_fusion), channel_id=1, source_target_pairs={{0,12},{4,0},{8,4},{12,8},{1,13},{5,1},{9,5},{13,9},{2,14},{6,2},{... | collective-permute-start | bytes 983048 | tf_op jit(solution)/shard_map/ppermute | solution.py:325
  24.0 4.9 %collective-permute-done.3.refs_1_ = bf16[640,256]{1,0:T(8,128)(2,1)S(1)} collective-permute-done((bf16[640,256]{1,0:T(8,128)(2,1)S(1)}, bf16[640,256]{1,0:T(8,128)(2,1)S(1)}, u32[]{:S(2)}, u32[]{:S(2)}) %collective-permute-start.3) | collective-permute-done | bytes 327712 | tf_op jit(solution)/shard_map/ppermute | solution.py:320
  28.8 1.2 %collective-permute-done.4.refs_2_ = bf16[640,256]{1,0:T(8,128)(2,1)S(1)} collective-permute-done((bf16[640,256]{1,0:T(8,128)(2,1)S(1)}, bf16[640,256]{1,0:T(8,128)(2,1)S(1)}, u32[]{:S(2)}, u32[]{:S(2)}) %collective-permute-start.4) | collective-permute-done | bytes 327712 | tf_op jit(solution)/shard_map/ppermute | solution.py:320
  30.0 1.2 %collective-permute-done.5.refs_0_ = bf16[640,256]{1,0:T(8,128)(2,1)S(1)} collective-permute-done((bf16[640,256]{1,0:T(8,128)(2,1)S(1)}, bf16[640,256]{1,0:T(8,128)(2,1)S(1)}, u32[]{:S(2)}, u32[]{:S(2)}) %collective-permute-start.5) | collective-permute-done | bytes 327712 | tf_op jit(solution)/shard_map/ppermute | solution.py:325
  31.3 1.6 %collective-permute-start.7 = (bf16[640,256]{1,0:T(8,128)(2,1)S(1)}, bf16[640,256]{1,0:T(8,128)(2,1)S(1)}, u32[]{:S(2)}, u32[]{:S(2)}) collective-permute-start(bf16[640,256]{1,0:T(8,128)(2,1)S(1)} %collective-permute-done.refs_0_), channel_id=1, source_target_pairs={{0,4},{4,8},{8,12},{12,0},{1,5},{5,9},{9,13},{13,1},{2,6},{6,10},{... | collective-permute-start | bytes 983048 | tf_op jit(solution)/shard_map/ppermute | solution.py:325
  33.9 8.4 %collective-permute-done.7.refs_4_ = bf16[640,256]{1,0:T(8,128)(2,1)S(1)} collective-permute-done((bf16[640,256]{1,0:T(8,128)(2,1)S(1)}, bf16[640,256]{1,0:T(8,128)(2,1)S(1)}, u32[]{:S(2)}, u32[]{:S(2)}) %collective-permute-start.7) | collective-permute-done | bytes 327712 | tf_op jit(solution)/shard_map/ppermute | solution.py:325
  44.6 1.4 %collective-permute-start.13 = (bf16[640,256]{1,0:T(8,128)(2,1)S(1)}, bf16[640,256]{1,0:T(8,128)(2,1)S(1)}, u32[]{:S(2)}, u32[]{:S(2)}) collective-permute-start(bf16[640,256]{1,0:T(8,128)(2,1)S(1)} %collective-permute-done.3.refs_1_), channel_id=1, source_target_pairs={{0,16},{16,0},{1,17},{17,1},{2,18},{18,2},{3,19},{19,3},{4,20},{20... | collective-permute-start | bytes 983048 | tf_op jit(solution)/shard_map/ppermute | solution.py:320
  46.0 1.3 %collective-permute-start.14 = (bf16[640,256]{1,0:T(8,128)(2,1)S(1)}, bf16[640,256]{1,0:T(8,128)(2,1)S(1)}, u32[]{:S(2)}, u32[]{:S(2)}) collective-permute-start(bf16[640,256]{1,0:T(8,128)(2,1)S(1)} %get-tuple-element.65), channel_id=1, source_target_pairs={{0,2},{2,0},{1,3},{3,1},{4,6},{6,4},{5,7},{7,5},{8,10},{10,8},{9,1... | collective-permute-start | bytes 983048 | tf_op jit(solution)/shard_map/ppermute | solution.py:320
  47.3 3.8 %collective-permute-done.11.refs_5_ = bf16[640,256]{1,0:T(8,128)(2,1)S(1)} collective-permute-done((bf16[640,256]{1,0:T(8,128)(2,1)S(1)}, bf16[640,256]{1,0:T(8,128)(2,1)S(1)}, u32[]{:S(2)}, u32[]{:S(2)}) %collective-permute-start.11) | collective-permute-done | bytes 327712 | tf_op jit(solution)/shard_map/ppermute | solution.py:320
  51.4 7.0 %collective-permute-done.13.refs_3_ = bf16[640,256]{1,0:T(8,128)(2,1)S(1)} collective-permute-done((bf16[640,256]{1,0:T(8,128)(2,1)S(1)}, bf16[640,256]{1,0:T(8,128)(2,1)S(1)}, u32[]{:S(2)}, u32[]{:S(2)}) %collective-permute-start.13) | collective-permute-done | bytes 327712 | tf_op jit(solution)/shard_map/ppermute | solution.py:320
  58.5 2.9 %collective-permute-start.17 = (bf16[2,640,256]{2,1,0:T(8,128)(2,1)S(1)}, bf16[2,640,256]{2,1,0:T(8,128)(2,1)S(1)}, u32[]{:S(2)}, u32[]{:S(2)}) collective-permute-start(bf16[2,640,256]{2,1,0:T(8,128)(2,1)S(1)} %pack.3), channel_id=1, source_target_pairs={{0,4},{1,12},{4,0},{5,8},{8,5},{9,13},{12,1},{13,9},{2,6},{3,14},{... | collective-permute-start | bytes 1966088 | tf_op jit(solution)/shard_map/ppermute | solution.py:353
  64.9 4.9 %collective-permute-done.10.refs_3_ = bf16[640,256]{1,0:T(8,128)(2,1)S(1)} collective-permute-done((bf16[640,256]{1,0:T(8,128)(2,1)S(1)}, bf16[640,256]{1,0:T(8,128)(2,1)S(1)}, u32[]{:S(2)}, u32[]{:S(2)}) %collective-permute-start.10) | collective-permute-done | bytes 327712 | tf_op jit(solution)/shard_map/ppermute | solution.py:320
  69.8 1.3 %collective-permute-done.16.refs_7_ = bf16[640,256]{1,0:T(8,128)(2,1)S(1)} collective-permute-done((bf16[640,256]{1,0:T(8,128)(2,1)S(1)}, bf16[640,256]{1,0:T(8,128)(2,1)S(1)}, u32[]{:S(2)}, u32[]{:S(2)}) %collective-permute-start.16) | collective-permute-done | bytes 327712 | tf_op jit(solution)/shard_map/ppermute | solution.py:320
  71.1 7.7 %attention.1 = (bf16[256,1280]{1,0:T(8,128)(2,1)}, bf16[256,512]{1,0:T(8,128)(2,1)S(1)}) custom-call(bf16[256,2560]{1,0:T(8,128)(2,1)S(1)} %get-tuple-element.51.own_ref, bf16[256,2560]{1,0:T(8,128)(2,1)S(1)} %collective-permute-done.6.other_ref, bf16[640,256]{1,0:T(8,128)(2,1)S(1)} %collective-permute-done.5.refs_0_, ...), custom_call_target="tpu_custom_call" | custom-call | flops 838860800 | bytes 5000000 | tf_op jit(solution)/shard_map/attention/pallas_call | solution.py:185
  78.8 1.5 %collective-permute-start.18 = (bf16[256,512]{1,0:T(8,128)(2,1)S(1)}, bf16[256,512]{1,0:T(8,128)(2,1)S(1)}, u32[]{:S(2)}, u32[]{:S(2)}) collective-permute-start(bf16[256,512]{1,0:T(8,128)(2,1)S(1)} %get-tuple-element.80.refs_12_), channel_id=1, source_target_pairs={{0,4},{4,8},{8,12},{12,0},{1,5},{5,9},{9,13},{13,1},{2,6},{6,10},{... | collective-permute-start | bytes 786440 | tf_op jit(solution)/shard_map/ppermute | solution.py:325
  80.3 1.3 %collective-permute-start.19 = (bf16[256,512]{1,0:T(8,128)(2,1)S(1)}, bf16[256,512]{1,0:T(8,128)(2,1)S(1)}, u32[]{:S(2)}, u32[]{:S(2)}) collective-permute-start(bf16[256,512]{1,0:T(8,128)(2,1)S(1)} %get-tuple-element.80.refs_12_), channel_id=1, source_target_pairs={{0,2},{2,0},{1,3},{3,1},{4,6},{6,4},{5,7},{7,5},{8,10},{10,8},{9,1... | collective-permute-start | bytes 786440 | tf_op jit(solution)/shard_map/ppermute | solution.py:320
  81.5 7.4 %collective-permute-done.18.refs_14_ = bf16[256,512]{1,0:T(8,128)(2,1)S(1)} collective-permute-done((bf16[256,512]{1,0:T(8,128)(2,1)S(1)}, bf16[256,512]{1,0:T(8,128)(2,1)S(1)}, u32[]{:S(2)}, u32[]{:S(2)}) %collective-permute-start.18) | collective-permute-done | bytes 262176 | tf_op jit(solution)/shard_map/ppermute | solution.py:325
  88.9 2.3 %collective-permute-start.21 = (bf16[256,512]{1,0:T(8,128)(2,1)S(1)}, bf16[256,512]{1,0:T(8,128)(2,1)S(1)}, u32[]{:S(2)}, u32[]{:S(2)}) collective-permute-start(bf16[256,512]{1,0:T(8,128)(2,1)S(1)} %get-tuple-element.80.refs_12_), channel_id=1, source_target_pairs={{0,12},{4,0},{8,4},{12,8},{1,13},{5,1},{9,5},{13,9},{2,14},{6,2},{... | collective-permute-start | bytes 786440 | tf_op jit(solution)/shard_map/ppermute | solution.py:325
  91.8 6.0 %collective-permute-done.21.refs_15_ = bf16[256,512]{1,0:T(8,128)(2,1)S(1)} collective-permute-done((bf16[256,512]{1,0:T(8,128)(2,1)S(1)}, bf16[256,512]{1,0:T(8,128)(2,1)S(1)}, u32[]{:S(2)}, u32[]{:S(2)}) %collective-permute-start.21) | collective-permute-done | bytes 262176 | tf_op jit(solution)/shard_map/ppermute | solution.py:325
  97.8 1.7 %collective-permute-done.22.refs_16_ = bf16[256,512]{1,0:T(8,128)(2,1)S(1)} collective-permute-done((bf16[256,512]{1,0:T(8,128)(2,1)S(1)}, bf16[256,512]{1,0:T(8,128)(2,1)S(1)}, u32[]{:S(2)}, u32[]{:S(2)}) %collective-permute-start.22) | collective-permute-done | bytes 262176 | tf_op jit(solution)/shard_map/ppermute | solution.py:320
  99.8 8.9 %collective-permute-done.23.refs_4_ = bf16[256,512]{1,0:T(8,128)(2,1)S(1)} collective-permute-done((bf16[256,512]{1,0:T(8,128)(2,1)S(1)}, bf16[256,512]{1,0:T(8,128)(2,1)S(1)}, u32[]{:S(2)}, u32[]{:S(2)}) %collective-permute-start.23) | collective-permute-done | bytes 262176 | tf_op jit(solution)/shard_map/ppermute | solution.py:325
  109.4 1.7 %gradient.2 = (f32[2,640,256]{2,1,0:T(8,128)S(1)}, f32[2,256]{1,0:T(2,128)S(1)}) custom-call(bf16[2,640,256]{2,1,0:T(8,128)(2,1)S(1)} %collective-permute-done.15.refs_0_.refs_1_, bf16[2,640,256]{2,1,0:T(8,128)(2,1)S(1)} %collective-permute-done.15.refs_0_.refs_1_, bf16[2,640,256]{2,1,0:T(8,128)(2,1)S(1)} %collective-permute-done.17.refs_2_.refs_3_.refs_4_.refs_5_, ...), custom_call_target="tpu_custom_call" | custom-call | flops 1006632960 | bytes 5000000 | tf_op jit(solution)/shard_map/gradient/pallas_call | solution.py:250
  111.1 4.1 %collective-permute-done.25.refs_5_ = bf16[256,512]{1,0:T(8,128)(2,1)S(1)} collective-permute-done((bf16[256,512]{1,0:T(8,128)(2,1)S(1)}, bf16[256,512]{1,0:T(8,128)(2,1)S(1)}, u32[]{:S(2)}, u32[]{:S(2)}) %collective-permute-start.25) | collective-permute-done | bytes 262176 | tf_op jit(solution)/shard_map/ppermute | solution.py:320
  115.2 1.7 %gradient.3 = (f32[2,640,256]{2,1,0:T(8,128)}, f32[2,256]{1,0:T(2,128)}) custom-call(bf16[2,640,256]{2,1,0:T(8,128)(2,1)S(1)} %collective-permute-done.15.refs_0_.refs_1_, bf16[2,640,256]{2,1,0:T(8,128)(2,1)S(1)} %collective-permute-done.15.refs_0_.refs_1_, bf16[2,640,256]{2,1,0:T(8,128)(2,1)S(1)} %collective-permute-done.20.refs_6_.refs_7_.refs_2_.refs_3_, ...), custom_call_target="tpu_custom_call" | custom-call | flops 335544320 | bytes 5000000 | tf_op jit(solution)/shard_map/gradient/pallas_call | solution.py:250
  (52 shorter events, 10.7 us)
Async XLA Ops:
  0.6 7.2 %copy-start = (bf16[256,2560]{1,0:T(8,128)(2,1)S(1)}, bf16[256,2560]{1,0:T(8,128)(2,1)}, u32[]{:S(2)}) copy-start(bf16[256,2560]{1,0:T(8,128)(2,1)} %values_ref.1) | copy-start | bytes 3932164
  1.8 12.8 %collective-permute-start = (bf16[640,256]{1,0:T(8,128)(2,1)S(1)}, bf16[640,256]{1,0:T(8,128)(2,1)S(1)}, u32[]{:S(2)}, u32[]{:S(2)}) collective-permute-start(bf16[640,256]{1,0:T(8,128)(2,1)S(1)} %dynamic-slice_bitcast_fusion), channel_id=1, source_target_pairs={{0,4},{4,8},{8,12},{12,0},{1,5},{5,9},{9,13},{13,1},{2,6},{6,10},{... | collective-permute-start | bytes 983048 | tf_op jit(solution)/shard_map/ppermute | solution.py:325
  6.5 1.2 %collective-permute-start.1 = (f32[256,1]{0,1:T(1,128)S(1)}, f32[256,1]{0,1:T(1,128)S(1)}, u32[]{:S(2)}, u32[]{:S(2)}) collective-permute-start(f32[256,1]{0,1:T(1,128)S(1)} %bitcast.3), channel_id=1, source_target_pairs={{0,1},{1,0},{2,3},{3,2},{4,5},{5,4},{6,7},{7,6},{8,9},{9,8},{10,11... | collective-permute-start | bytes 3080 | tf_op jit(solution)/shard_map/ppermute | solution.py:320
  8.8 9.9 %collective-permute-start.2 = (bf16[640,256]{1,0:T(8,128)(2,1)S(1)}, bf16[640,256]{1,0:T(8,128)(2,1)S(1)}, u32[]{:S(2)}, u32[]{:S(2)}) collective-permute-start(bf16[640,256]{1,0:T(8,128)(2,1)S(1)} %get-tuple-element.50), channel_id=1, source_target_pairs={{0,2},{2,0},{1,3},{3,1},{4,6},{6,4},{5,7},{7,5},{8,10},{10,8},{9,1... | collective-permute-start | bytes 983048 | tf_op jit(solution)/shard_map/ppermute | solution.py:320
  18.7 12.6 %collective-permute-start.6 = (bf16[256,2560]{1,0:T(8,128)(2,1)S(1)}, bf16[256,2560]{1,0:T(8,128)(2,1)S(1)}, u32[]{:S(2)}, u32[]{:S(2)}) collective-permute-start(bf16[256,2560]{1,0:T(8,128)(2,1)S(1)} %get-tuple-element.51.own_ref), channel_id=1, source_target_pairs={{0,1},{1,0},{2,3},{3,2},{4,5},{5,4},{6,7},{7,6},{8,9},{9,8},{10,11... | collective-permute-start | bytes 3932168 | tf_op jit(solution)/shard_map/ppermute | solution.py:320
  18.7 10.1 %collective-permute-start.3 = (bf16[640,256]{1,0:T(8,128)(2,1)S(1)}, bf16[640,256]{1,0:T(8,128)(2,1)S(1)}, u32[]{:S(2)}, u32[]{:S(2)}) collective-permute-start(bf16[640,256]{1,0:T(8,128)(2,1)S(1)} %collective-permute-done.refs_0_), channel_id=1, source_target_pairs={{0,2},{2,0},{1,3},{3,1},{4,6},{6,4},{5,7},{7,5},{8,10},{10,8},{9,1... | collective-permute-start | bytes 983048 | tf_op jit(solution)/shard_map/ppermute | solution.py:320
  20.2 9.8 %collective-permute-start.4 = (bf16[640,256]{1,0:T(8,128)(2,1)S(1)}, bf16[640,256]{1,0:T(8,128)(2,1)S(1)}, u32[]{:S(2)}, u32[]{:S(2)}) collective-permute-start(bf16[640,256]{1,0:T(8,128)(2,1)S(1)} %collective-permute-done.refs_0_), channel_id=1, source_target_pairs={{0,16},{16,0},{1,17},{17,1},{2,18},{18,2},{3,19},{19,3},{4,20},{20... | collective-permute-start | bytes 983048 | tf_op jit(solution)/shard_map/ppermute | solution.py:320
  21.7 9.6 %collective-permute-start.5 = (bf16[640,256]{1,0:T(8,128)(2,1)S(1)}, bf16[640,256]{1,0:T(8,128)(2,1)S(1)}, u32[]{:S(2)}, u32[]{:S(2)}) collective-permute-start(bf16[640,256]{1,0:T(8,128)(2,1)S(1)} %dynamic-slice_bitcast_fusion), channel_id=1, source_target_pairs={{0,12},{4,0},{8,4},{12,8},{1,13},{5,1},{9,5},{13,9},{2,14},{6,2},{... | collective-permute-start | bytes 983048 | tf_op jit(solution)/shard_map/ppermute | solution.py:325
  31.3 11.0 %collective-permute-start.7 = (bf16[640,256]{1,0:T(8,128)(2,1)S(1)}, bf16[640,256]{1,0:T(8,128)(2,1)S(1)}, u32[]{:S(2)}, u32[]{:S(2)}) collective-permute-start(bf16[640,256]{1,0:T(8,128)(2,1)S(1)} %collective-permute-done.refs_0_), channel_id=1, source_target_pairs={{0,4},{4,8},{8,12},{12,0},{1,5},{5,9},{9,13},{13,1},{2,6},{6,10},{... | collective-permute-start | bytes 983048 | tf_op jit(solution)/shard_map/ppermute | solution.py:325
  32.8 9.4 %collective-permute-start.8 = (bf16[640,256]{1,0:T(8,128)(2,1)S(1)}, bf16[640,256]{1,0:T(8,128)(2,1)S(1)}, u32[]{:S(2)}, u32[]{:S(2)}) collective-permute-start(bf16[640,256]{1,0:T(8,128)(2,1)S(1)} %collective-permute-done.5.refs_0_), channel_id=1, source_target_pairs={{0,2},{2,0},{1,3},{3,1},{4,6},{6,4},{5,7},{7,5},{8,10},{10,8},{9,1... | collective-permute-start | bytes 983048 | tf_op jit(solution)/shard_map/ppermute | solution.py:320
  33.4 8.9 %collective-permute-start.9 = (bf16[640,256]{1,0:T(8,128)(2,1)S(1)}, bf16[640,256]{1,0:T(8,128)(2,1)S(1)}, u32[]{:S(2)}, u32[]{:S(2)}) collective-permute-start(bf16[640,256]{1,0:T(8,128)(2,1)S(1)} %collective-permute-done.5.refs_0_), channel_id=1, source_target_pairs={{0,16},{16,0},{1,17},{17,1},{2,18},{18,2},{3,19},{19,3},{4,20},{20... | collective-permute-start | bytes 983048 | tf_op jit(solution)/shard_map/ppermute | solution.py:320
  42.3 19.1 %copy-start.5 = (bf16[2,256]{1,0:T(2,128)(2,1)S(1)}, bf16[2,256]{1,0:T(2,128)(2,1)}, u32[]{:S(2)}) copy-start(bf16[2,256]{1,0:T(2,128)(2,1)} %param.11) | copy-start | bytes 3076
  42.3 21.5 %copy-start.1 = (bf16[2,1280,256]{2,1,0:T(8,128)(2,1)S(1)}, bf16[2,1280,256]{2,1,0:T(8,128)(2,1)}, u32[]{:S(2)}) copy-start(bf16[2,1280,256]{2,1,0:T(8,128)(2,1)} %weight_ref.1) | copy-start | bytes 3932164
  42.4 16.1 %collective-permute-start.15 = (bf16[2,640,256]{2,1,0:T(8,128)(2,1)S(1)}, bf16[2,640,256]{2,1,0:T(8,128)(2,1)S(1)}, u32[]{:S(2)}, u32[]{:S(2)}) collective-permute-start(bf16[2,640,256]{2,1,0:T(8,128)(2,1)S(1)} %pack.2), channel_id=1, source_target_pairs={{0,0},{1,8},{4,4},{5,12},{8,1},{9,9},{12,5},{13,13},{2,2},{3,10},{... | collective-permute-start | bytes 1966088 | tf_op jit(solution)/shard_map/ppermute | solution.py:353
  43.2 8.0 %collective-permute-start.11 = (bf16[640,256]{1,0:T(8,128)(2,1)S(1)}, bf16[640,256]{1,0:T(8,128)(2,1)S(1)}, u32[]{:S(2)}, u32[]{:S(2)}) collective-permute-start(bf16[640,256]{1,0:T(8,128)(2,1)S(1)} %collective-permute-done.7.refs_4_), channel_id=1, source_target_pairs={{0,2},{2,0},{1,3},{3,1},{4,6},{6,4},{5,7},{7,5},{8,10},{10,8},{9,1... | collective-permute-start | bytes 983048 | tf_op jit(solution)/shard_map/ppermute | solution.py:320
  44.0 7.4 %collective-permute-start.12 = (bf16[640,256]{1,0:T(8,128)(2,1)S(1)}, bf16[640,256]{1,0:T(8,128)(2,1)S(1)}, u32[]{:S(2)}, u32[]{:S(2)}) collective-permute-start(bf16[640,256]{1,0:T(8,128)(2,1)S(1)} %collective-permute-done.7.refs_4_), channel_id=1, source_target_pairs={{0,16},{16,0},{1,17},{17,1},{2,18},{18,2},{3,19},{19,3},{4,20},{20... | collective-permute-start | bytes 983048 | tf_op jit(solution)/shard_map/ppermute | solution.py:320
  44.6 13.8 %collective-permute-start.13 = (bf16[640,256]{1,0:T(8,128)(2,1)S(1)}, bf16[640,256]{1,0:T(8,128)(2,1)S(1)}, u32[]{:S(2)}, u32[]{:S(2)}) collective-permute-start(bf16[640,256]{1,0:T(8,128)(2,1)S(1)} %collective-permute-done.3.refs_1_), channel_id=1, source_target_pairs={{0,16},{16,0},{1,17},{17,1},{2,18},{18,2},{3,19},{19,3},{4,20},{20... | collective-permute-start | bytes 983048 | tf_op jit(solution)/shard_map/ppermute | solution.py:320
  46.0 12.4 %collective-permute-start.14 = (bf16[640,256]{1,0:T(8,128)(2,1)S(1)}, bf16[640,256]{1,0:T(8,128)(2,1)S(1)}, u32[]{:S(2)}, u32[]{:S(2)}) collective-permute-start(bf16[640,256]{1,0:T(8,128)(2,1)S(1)} %get-tuple-element.65), channel_id=1, source_target_pairs={{0,2},{2,0},{1,3},{3,1},{4,6},{6,4},{5,7},{7,5},{8,10},{10,8},{9,1... | collective-permute-start | bytes 983048 | tf_op jit(solution)/shard_map/ppermute | solution.py:320
  58.5 20.3 %collective-permute-start.17 = (bf16[2,640,256]{2,1,0:T(8,128)(2,1)S(1)}, bf16[2,640,256]{2,1,0:T(8,128)(2,1)S(1)}, u32[]{:S(2)}, u32[]{:S(2)}) collective-permute-start(bf16[2,640,256]{2,1,0:T(8,128)(2,1)S(1)} %pack.3), channel_id=1, source_target_pairs={{0,4},{1,12},{4,0},{5,8},{8,5},{9,13},{12,1},{13,9},{2,6},{3,14},{... | collective-permute-start | bytes 1966088 | tf_op jit(solution)/shard_map/ppermute | solution.py:353
  61.4 8.3 %collective-permute-start.10 = (bf16[640,256]{1,0:T(8,128)(2,1)S(1)}, bf16[640,256]{1,0:T(8,128)(2,1)S(1)}, u32[]{:S(2)}, u32[]{:S(2)}) collective-permute-start(bf16[640,256]{1,0:T(8,128)(2,1)S(1)} %collective-permute-done.8.refs_1_), channel_id=1, source_target_pairs={{0,16},{16,0},{1,17},{17,1},{2,18},{18,2},{3,19},{19,3},{4,20},{20... | collective-permute-start | bytes 983048 | tf_op jit(solution)/shard_map/ppermute | solution.py:320
  62.2 8.9 %collective-permute-start.16 = (bf16[640,256]{1,0:T(8,128)(2,1)S(1)}, bf16[640,256]{1,0:T(8,128)(2,1)S(1)}, u32[]{:S(2)}, u32[]{:S(2)}) collective-permute-start(bf16[640,256]{1,0:T(8,128)(2,1)S(1)} %collective-permute-done.12.refs_6_), channel_id=1, source_target_pairs={{0,2},{2,0},{1,3},{3,1},{4,6},{6,4},{5,7},{7,5},{8,10},{10,8},{9,1... | collective-permute-start | bytes 983048 | tf_op jit(solution)/shard_map/ppermute | solution.py:320
  63.8 7.3 %copy-start.2 = (bf16[256,1280]{1,0:T(8,128)(2,1)S(1)}, bf16[256,1280]{1,0:T(8,128)(2,1)}, u32[]{:S(2)}) copy-start(bf16[256,1280]{1,0:T(8,128)(2,1)} %refs_12_.1) | copy-start | bytes 1966084
  63.8 7.3 %copy-start.3 = (bf16[256,1280]{1,0:T(8,128)(2,1)S(1)}, bf16[256,1280]{1,0:T(8,128)(2,1)}, u32[]{:S(2)}) copy-start(bf16[256,1280]{1,0:T(8,128)(2,1)} %refs_13_.1) | copy-start | bytes 1966084
  78.8 10.2 %collective-permute-start.18 = (bf16[256,512]{1,0:T(8,128)(2,1)S(1)}, bf16[256,512]{1,0:T(8,128)(2,1)S(1)}, u32[]{:S(2)}, u32[]{:S(2)}) collective-permute-start(bf16[256,512]{1,0:T(8,128)(2,1)S(1)} %get-tuple-element.80.refs_12_), channel_id=1, source_target_pairs={{0,4},{4,8},{8,12},{12,0},{1,5},{5,9},{9,13},{13,1},{2,6},{6,10},{... | collective-permute-start | bytes 786440 | tf_op jit(solution)/shard_map/ppermute | solution.py:325
  80.3 8.7 %collective-permute-start.19 = (bf16[256,512]{1,0:T(8,128)(2,1)S(1)}, bf16[256,512]{1,0:T(8,128)(2,1)S(1)}, u32[]{:S(2)}, u32[]{:S(2)}) collective-permute-start(bf16[256,512]{1,0:T(8,128)(2,1)S(1)} %get-tuple-element.80.refs_12_), channel_id=1, source_target_pairs={{0,2},{2,0},{1,3},{3,1},{4,6},{6,4},{5,7},{7,5},{8,10},{10,8},{9,1... | collective-permute-start | bytes 786440 | tf_op jit(solution)/shard_map/ppermute | solution.py:320
  88.9 8.9 %collective-permute-start.21 = (bf16[256,512]{1,0:T(8,128)(2,1)S(1)}, bf16[256,512]{1,0:T(8,128)(2,1)S(1)}, u32[]{:S(2)}, u32[]{:S(2)}) collective-permute-start(bf16[256,512]{1,0:T(8,128)(2,1)S(1)} %get-tuple-element.80.refs_12_), channel_id=1, source_target_pairs={{0,12},{4,0},{8,4},{12,8},{1,13},{5,1},{9,5},{13,9},{2,14},{6,2},{... | collective-permute-start | bytes 786440 | tf_op jit(solution)/shard_map/ppermute | solution.py:325
  91.3 8.3 %collective-permute-start.22 = (bf16[256,512]{1,0:T(8,128)(2,1)S(1)}, bf16[256,512]{1,0:T(8,128)(2,1)S(1)}, u32[]{:S(2)}, u32[]{:S(2)}) collective-permute-start(bf16[256,512]{1,0:T(8,128)(2,1)S(1)} %collective-permute-done.18.refs_14_), channel_id=1, source_target_pairs={{0,2},{2,0},{1,3},{3,1},{4,6},{6,4},{5,7},{7,5},{8,10},{10,8},{9,1... | collective-permute-start | bytes 786440 | tf_op jit(solution)/shard_map/ppermute | solution.py:320
  91.3 18.1 %collective-permute-start.20 = (bf16[2,640,256]{2,1,0:T(8,128)(2,1)S(1)}, bf16[2,640,256]{2,1,0:T(8,128)(2,1)S(1)}, u32[]{:S(2)}, u32[]{:S(2)}) collective-permute-start(bf16[2,640,256]{2,1,0:T(8,128)(2,1)S(1)} %collective-permute-done.15.refs_0_.refs_1_), channel_id=1, source_target_pairs={{0,1},{1,0},{2,3},{3,2},{4,5},{5,4},{6,7},{7,6},{8,9},{9,8},{10,11... | collective-permute-start | bytes 1966088 | tf_op jit(solution)/shard_map/ppermute | solution.py:320
  91.3 18.0 %collective-permute-start.26 = (bf16[2,640,256]{2,1,0:T(8,128)(2,1)S(1)}, bf16[2,640,256]{2,1,0:T(8,128)(2,1)S(1)}, u32[]{:S(2)}, u32[]{:S(2)}) collective-permute-start(bf16[2,640,256]{2,1,0:T(8,128)(2,1)S(1)} %collective-permute-done.17.refs_2_.refs_3_.refs_4_.refs_5_), channel_id=1, source_target_pairs={{0,1},{1,0},{2,3},{3,2},{4,5},{5,4},{6,7},{7,6},{8,9},{9,8},{10,11... | collective-permute-start | bytes 1966088 | tf_op jit(solution)/shard_map/ppermute | solution.py:320
  99.5 9.2 %collective-permute-start.23 = (bf16[256,512]{1,0:T(8,128)(2,1)S(1)}, bf16[256,512]{1,0:T(8,128)(2,1)S(1)}, u32[]{:S(2)}, u32[]{:S(2)}) collective-permute-start(bf16[256,512]{1,0:T(8,128)(2,1)S(1)} %collective-permute-done.18.refs_14_), channel_id=1, source_target_pairs={{0,4},{4,8},{8,12},{12,0},{1,5},{5,9},{9,13},{13,1},{2,6},{6,10},{... | collective-permute-start | bytes 786440 | tf_op jit(solution)/shard_map/ppermute | solution.py:325
  99.6 9.2 %collective-permute-start.24 = (bf16[256,512]{1,0:T(8,128)(2,1)S(1)}, bf16[256,512]{1,0:T(8,128)(2,1)S(1)}, u32[]{:S(2)}, u32[]{:S(2)}) collective-permute-start(bf16[256,512]{1,0:T(8,128)(2,1)S(1)} %collective-permute-done.21.refs_15_), channel_id=1, source_target_pairs={{0,2},{2,0},{1,3},{3,1},{4,6},{6,4},{5,7},{7,5},{8,10},{10,8},{9,1... | collective-permute-start | bytes 786440 | tf_op jit(solution)/shard_map/ppermute | solution.py:320
  108.8 6.5 %collective-permute-start.25 = (bf16[256,512]{1,0:T(8,128)(2,1)S(1)}, bf16[256,512]{1,0:T(8,128)(2,1)S(1)}, u32[]{:S(2)}, u32[]{:S(2)}) collective-permute-start(bf16[256,512]{1,0:T(8,128)(2,1)S(1)} %collective-permute-done.23.refs_4_), channel_id=1, source_target_pairs={{0,2},{2,0},{1,3},{3,1},{4,6},{6,4},{5,7},{7,5},{8,10},{10,8},{9,1... | collective-permute-start | bytes 786440 | tf_op jit(solution)/shard_map/ppermute | solution.py:320
  (1 other events, 5.9 us)

commit v13 on v10

--- a/solution.py
+++ b/solution.py
@@ -141,14 +141,20 @@
         )
 
 
-def attention_kernel(
-    distance, own_ref, other_ref, p0, p1, p2, p3, sums_ref, bias_ref, cosine_ref, sine_ref,
-    queries_ref, cotangent_ref, grad_query_ref, pair_ref, raw_ref,
-):
+def attention_kernel(distances, own_ref, other_ref, *refs):
+    pairs, refs = refs[4:6], refs[:4] + refs[6:]
+    pieces = [*refs[:4], *(pair.at[at] for pair in pairs for at in range(2))]
+    refs = refs[4:]
+    sums_ref, bias_ref, cosine_ref, sine_ref, queries_ref, cotangent_ref = refs[:6]
+    grad_query_ref, pair_ref, raw_ref = refs[6:]
     group = lax.axis_index("groups")
-    terms = block_terms(own_ref, other_ref, block_from(distance), (p0, p1, p2, p3))
-    raw_ref[group] = sums_ref[group] + terms[0]
-    raw_ref[1 - group] = sums_ref[1 - group] + terms[1]
+    totals = [sums_ref[group], sums_ref[1 - group]]
+    for at, distance in enumerate(distances):
+        four = pieces[4 * at : 4 * at + 4]
+        terms = block_terms(own_ref, other_ref, block_from(distance), four)
+        totals = [total + term for total, term in zip(totals, terms)]
+    raw_ref[group] = totals[0]
+    raw_ref[1 - group] = totals[1]
 
     def raw_of(j, lanes):
         return raw_ref[j, :, lanes] + bias_ref[j : j + 1, lanes]
@@ -158,18 +164,19 @@
     )
 
 
-def attention(distance, normed, normed_other, pieces, sums, bias, cosine, sine, queries, cotangent):
+def attention(gathered, normed, normed_other, sums, bias, cosine, sine, queries, cotangent):
     length = normed.shape[0]
-    columns = pieces[0].shape[1]
+    distances = tuple(distance for distance, _ in gathered)
+    pieces = [piece for _, parts in gathered for piece in parts]
     operands = (normed, normed_other, *pieces, sums, bias, cosine, sine, queries, cotangent)
     return pl.pallas_call(
-        functools.partial(attention_kernel, distance),
+        functools.partial(attention_kernel, distances),
         in_specs=[IN_VMEM] * len(operands),
         out_specs=[IN_VMEM] * 2,
         scratch_shapes=[pltpu.VMEM(sums.shape, jnp.float32)],
         out_shape=[
             jax.ShapeDtypeStruct(queries.shape, jnp.bfloat16),
-            jax.ShapeDtypeStruct((length, 2 * columns), jnp.bfloat16),
+            jax.ShapeDtypeStruct((length, 2 * bias.shape[1]), jnp.bfloat16),
         ],
         compiler_params=pltpu.CompilerParams(vmem_limit_bytes=VMEM_BYTES),
         cost_estimate=pl.CostEstimate(
@@ -244,9 +251,10 @@
     )(*own, *other, *pairs, *(sums or ()))
 
 
-def norm_kernel(values_ref, scale_ref, gain_ref, normed_ref, kept_ref, sent_ref):
+def norm_kernel(values_ref, scale_ref, gain_ref, normed_ref, *slab_refs):
     replica, replicas = lax.axis_index("dp"), lax.axis_size("dp")
-    share = kept_ref.shape[1]
+    parity = lax.rem(lax.axis_index("blk"), 2)
+    share = slab_refs[0].shape[0]
 
     def scaled(place):
         wide_values = values_ref[:, place].astype(jnp.float32)
@@ -255,19 +263,20 @@
     for slab in range(2 * replicas):
         place = pl.ds(slab * share, share)
         normed_ref[:, place] = scaled(place).astype(jnp.bfloat16)
-    for at in range(2):
-        for ref, owner in ((kept_ref, replica), (sent_ref, 1 - replica)):
+    for turn in range(2):
+        at = lax.rem(turn + parity, 2)
+        for ref, owner in zip(slab_refs[2 * turn :], (replica, 1 - replica)):
             place = pl.ds(pl.multiple_of((at * replicas + owner) * share, 128), share)
-            ref[at] = scaled(place).T.astype(jnp.bfloat16)
+            ref[...] = scaled(place).T.astype(jnp.bfloat16)
 
 
 def norm(activations, scale, gain, share):
     length, features = activations.shape
-    shapes = [activations.shape, (2, share, length), (2, share, length)]
+    shapes = [activations.shape] + [(share, length)] * 4
     return pl.pallas_call(
         norm_kernel,
         in_specs=[IN_VMEM] * 3,
-        out_specs=[IN_VMEM] * 3,
+        out_specs=[IN_VMEM] * 5,
         out_shape=[jax.ShapeDtypeStruct(shape, jnp.bfloat16) for shape in shapes],
         compiler_params=pltpu.CompilerParams(vmem_limit_bytes=VMEM_BYTES),
         cost_estimate=pl.CostEstimate(
@@ -277,22 +286,19 @@
     )(activations, scale, gain)
 
 
-def pack_kernel(kept_ref, arrived_ref, even_ref, odd_ref):
-    parity = lax.rem(lax.axis_index("blk"), 2)
-    for turn, ref in enumerate((even_ref, odd_ref)):
-        at = lax.rem(turn + parity, 2)
-        ref[0] = kept_ref[at]
-        ref[1] = arrived_ref[at]
+def pack_kernel(kept_ref, arrived_ref, packed_ref):
+    packed_ref[0] = kept_ref[...]
+    packed_ref[1] = arrived_ref[...]
 
 
 def pack(kept, arrived):
     return pl.pallas_call(
         pack_kernel,
         in_specs=[IN_VMEM] * 2,
-        out_specs=[IN_VMEM] * 2,
-        out_shape=[jax.ShapeDtypeStruct(kept.shape, kept.dtype)] * 2,
+        out_specs=IN_VMEM,
+        out_shape=jax.ShapeDtypeStruct((2, *kept.shape), kept.dtype),
         compiler_params=pltpu.CompilerParams(vmem_limit_bytes=VMEM_BYTES),
-        cost_estimate=pl.CostEstimate(flops=0, bytes_accessed=2600000, transcendentals=0),
+        cost_estimate=pl.CostEstimate(flops=0, bytes_accessed=1300000, transcendentals=0),
         name="pack",
     )(kept, arrived)
 
@@ -366,38 +372,43 @@
         )
 
     up = turned(piece, "blk", 1)
-    normed, kept, sent = norm(activations, scale, gain[None, :], share)
-    up, piece, normed, kept, sent = lax.optimization_barrier((up, piece, normed, kept, sent))
+    normed, kept_even, sent_even, kept_odd, sent_odd = norm(
+        activations, scale, gain[None, :], share
+    )
+    up, piece, normed, sent_even, sent_odd = lax.optimization_barrier(
+        (up, piece, normed, sent_even, sent_odd)
+    )
     up_x, up_y, down = swapped(up, "dp"), swapped(up, "groups"), turned(piece, "blk", -1)
-    arrived = swapped(sent, "dp")
     normed_other = swapped(normed, "sub")
-    up, up_y, down, normed_other = lax.optimization_barrier((up, up_y, down, normed_other))
-    down_x, down_y = swapped(down, "dp"), swapped(down, "groups")
-    twice = turned(up, "blk", 1)
-    twice, down_y, up_x, arrived = lax.optimization_barrier((twice, down_y, up_x, arrived))
-    twice_x, twice_y = swapped(twice, "dp"), swapped(twice, "groups")
-    up_both = swapped(up_x, "groups")
-    even, odd = pack(kept, arrived)
-    even = sent_along(even, 0)
-    twice_x, twice_y, up_both, down_x, even = lax.optimization_barrier(
-        (twice_x, twice_y, up_both, down_x, even)
-    )
-    down_both, twice_both = swapped(down_x, "groups"), swapped(twice_y, "dp")
-    odd = sent_along(after(odd, even), 1)
-
-    gathered = [(1, (up, up_x, up_y, up_both)), (-1, (down, down_x, down_y, down_both))]
-    sums = project(normed, normed_other, kv_weight, gathered)
+    up, up_x, up_y, down, normed_other, sent_even, sent_odd = lax.optimization_barrier(
+        (up, up_x, up_y, down, normed_other, sent_even, sent_odd)
+    )
+    twice = turned(pack(up, up_x), "blk", 1)
+    down_x, down_y, up_both = swapped(down, "dp"), swapped(down, "groups"), swapped(up_x, "groups")
+    arrived_even = swapped(sent_even, "dp")
+    twice, down_x, down_y, up_both, arrived_even, sent_odd = lax.optimization_barrier(
+        (twice, down_x, down_y, up_both, arrived_even, sent_odd)
+    )
+    twice_y, down_both = swapped(twice, "groups"), swapped(down_y, "dp")
+    arrived_odd = swapped(sent_odd, "dp")
+    even = sent_along(pack(kept_even, arrived_even), 0)
+    sums = project(normed, normed_other, kv_weight, [(1, (up, up_x, up_y, up_both))])
+    twice_y, down_both, arrived_odd, even, sums, cosine, sine = lax.optimization_barrier(
+        (twice_y, down_both, arrived_odd, even, sums, cosine, sine)
+    )
+    odd = sent_along(pack(kept_odd, arrived_odd), 1)
+    even_other = swapped(even, "sub")
+    gathered = [(-1, (down, down_x, down_y, down_both)), (2, (twice, twice_y))]
     grad_query, grad_pair = attention(
-        2, normed, normed_other, (twice, twice_x, twice_y, twice_both), sums, bias, cosine, sine,
-        queries, cotangent,
-    )
-
-    grad_pair, odd = lax.optimization_barrier((grad_pair, odd))
+        gathered, normed, normed_other, sums, bias, cosine, sine, queries, cotangent
+    )
+
+    grad_pair, odd, even_other = lax.optimization_barrier((grad_pair, odd, even_other))
     pair_up, pair_x = turned(grad_pair, "blk", 1), swapped(grad_pair, "dp")
     pair_up, pair_x, grad_pair, even, odd = lax.optimization_barrier(
         (pair_up, pair_x, grad_pair, even, odd)
     )
-    slabs = ((even, swapped(even, "sub")), (odd, swapped(odd, "sub")))
+    slabs = ((even, even_other), (odd, swapped(odd, "sub")))
     pair_down, pair_up_x = turned(grad_pair, "blk", -1), swapped(pair_up, "dp")
     pair_down, pair_up_x, pair_up = lax.optimization_barrier((pair_down, pair_up_x, pair_up))
     pair_twice, pair_down_x = turned(pair_up, "blk", 1), swapped(pair_down, "dp")

time: 113 us -> 118 us (1.044); the launches traced: 113 us -> 116 us
  starting transfers between devices: 20.4 us -> 28.2 us
  waiting for transfers between devices: 76.7 us -> 71.9 us
    ppermute x18 -> x17, waiting for transfers between devices: 49.3 us -> 34.6 us  [swapped(): return lax.ppermute(block, axis, [(0, 1), (1, 0)])]
    ppermute x18 -> x17, starting transfers between devices: 12.5 us -> 20.6 us  [swapped(): return lax.ppermute(block, axis, [(0, 1), (1, 0)])]
    ppermute x2, waiting for transfers between devices: 0.45 us -> 6.72 us  [sent_along(): return lax.ppermute(slabs, ('blk', 'sub'), route)]
    ppermute x6, waiting for transfers between devices: 26.9 us -> 30.6 us  [turned(): lax.ppermute(block, axis, [(i, (i + distance) % size) for i in range(size)])]
    pallas_call x2 -> x4, Pallas kernels: 5.17 us -> 5.64 us  [the longest x1 5.51 us: attention(): pl.pallas_call(functools.partial(attention_kernel, distances), in_specs=[...]
  transfers between devices with their start and end apart: 26 -> 25, of which waited for: 15 -> 19; matrix products, arithmetic and copies ran while one was open for 2% -> 2% of each run, Pallas kernels for 8% -> 8%
where the time goes in v13:
time: 118 us; the launch traced here: 116 us
  waiting for transfers between devices  71.9 us (61%)
  starting transfers between devices  28.2 us (24%)
  Pallas kernels  11.1 us (9%)
  other arithmetic  2.5 us (2%)
  local copies, waits for them, and re-layouts  1.19 us (1%)
    ppermute x17, waiting for transfers between devices, swapped(): return lax.ppermute(block, axis, [(0, 1), (1, 0)])  34.6 us
    ppermute x6, waiting for transfers between devices, turned(): lax.ppermute(block, axis, [(i, (i + distance) % size) for i in range(size)])  30.6 us
    ppermute x17, starting transfers between devices, swapped(): return lax.ppermute(block, axis, [(0, 1), (1, 0)])  20.6 us
    ppermute x6, starting transfers between devices, turned(): lax.ppermute(block, axis, [(i, (i + distance) % size) for i in range(size)])  6.76 us
    ppermute x2, waiting for transfers between devices, sent_along(): return lax.ppermute(slabs, ('blk', 'sub'), route)  6.72 us
    pallas_call x1, Pallas kernels, attention(): pl.pallas_call(functools.partial(attention_kernel, distances), in_specs=[...  5.51 us
    pallas_call x2, Pallas kernels, gradient(): pl.pallas_call(functools.partial(gradient_kernel, tuple(some), sums is No...  3.48 us
  transfers between devices with their start and end apart: 25, of which 19 were waited for; matrix products, arithmetic and copies ran while one was open for 2% of the time, Pallas kernels for 8%

profile of v13, /device:TPU:0, one launch (start us, length us, event | category | flops | bytes accessed | tf_op | source)
XLA Modules:
  0.0 115.6 jit_solution(16214784304485860898)
XLA Ops:
  0.6 1.8 %multiply_reduce_fusion = f32[256]{0:T(256)S(1)} fusion(bf16[256,2560]{1,0:T(8,128)(2,1)} %values_ref.1), kind=kLoop, calls=%fused_computation | loop fusion | flops 1965824 | bytes 1311744 | tf_op jit(solution)/shard_map/reduce_sum | solution.py:347
  3.9 2.7 %collective-permute-start = (bf16[640,256]{1,0:T(8,128)(2,1)S(1)}, bf16[640,256]{1,0:T(8,128)(2,1)S(1)}, u32[]{:S(2)}, u32[]{:S(2)}) collective-permute-start(bf16[640,256]{1,0:T(8,128)(2,1)S(1)} %dynamic-slice_bitcast_fusion), channel_id=1, source_target_pairs={{0,4},{4,8},{8,12},{12,0},{1,5},{5,9},{9,13},{13,1},{2,6},{6,10},{... | collective-permute-start | bytes 983048 | tf_op jit(solution)/shard_map/ppermute | solution.py:312
  7.8 9.1 %collective-permute-done.kept_ref.refs_0_ = bf16[640,256]{1,0:T(8,128)(2,1)S(1)} collective-permute-done((bf16[640,256]{1,0:T(8,128)(2,1)S(1)}, bf16[640,256]{1,0:T(8,128)(2,1)S(1)}, u32[]{:S(2)}, u32[]{:S(2)}) %collective-permute-start) | collective-permute-done | bytes 327712 | tf_op jit(solution)/shard_map/ppermute | solution.py:312
  17.0 1.7 %collective-permute-start.4 = (bf16[640,256]{1,0:T(8,128)(2,1)S(1)}, bf16[640,256]{1,0:T(8,128)(2,1)S(1)}, u32[]{:S(2)}, u32[]{:S(2)}) collective-permute-start(bf16[640,256]{1,0:T(8,128)(2,1)S(1)} %dynamic-slice_bitcast_fusion), channel_id=1, source_target_pairs={{0,12},{4,0},{8,4},{12,8},{1,13},{5,1},{9,5},{13,9},{2,14},{6,2},{... | collective-permute-start | bytes 983048 | tf_op jit(solution)/shard_map/ppermute | solution.py:312
  18.7 1.5 %collective-permute-start.3 = (bf16[640,256]{1,0:T(8,128)(2,1)S(1)}, bf16[640,256]{1,0:T(8,128)(2,1)S(1)}, u32[]{:S(2)}, u32[]{:S(2)}) collective-permute-start(bf16[640,256]{1,0:T(8,128)(2,1)S(1)} %collective-permute-done.kept_ref.refs_0_), channel_id=1, source_target_pairs={{0,16},{16,0},{1,17},{17,1},{2,18},{18,2},{3,19},{19,3},{4,20},{20... | collective-permute-start | bytes 983048 | tf_op jit(solution)/shard_map/ppermute | solution.py:307
  20.2 1.5 %collective-permute-start.2 = (bf16[640,256]{1,0:T(8,128)(2,1)S(1)}, bf16[640,256]{1,0:T(8,128)(2,1)S(1)}, u32[]{:S(2)}, u32[]{:S(2)}) collective-permute-start(bf16[640,256]{1,0:T(8,128)(2,1)S(1)} %collective-permute-done.kept_ref.refs_0_), channel_id=1, source_target_pairs={{0,2},{2,0},{1,3},{3,1},{4,6},{6,4},{5,7},{7,5},{8,10},{10,8},{9,1... | collective-permute-start | bytes 983048 | tf_op jit(solution)/shard_map/ppermute | solution.py:307
  21.7 5.4 %collective-permute-done.4.refs_0_ = bf16[640,256]{1,0:T(8,128)(2,1)S(1)} collective-permute-done((bf16[640,256]{1,0:T(8,128)(2,1)S(1)}, bf16[640,256]{1,0:T(8,128)(2,1)S(1)}, u32[]{:S(2)}, u32[]{:S(2)}) %collective-permute-start.4) | collective-permute-done | bytes 327712 | tf_op jit(solution)/shard_map/ppermute | solution.py:312
  27.1 1.5 %collective-permute-done.3.refs_2_ = bf16[640,256]{1,0:T(8,128)(2,1)S(1)} collective-permute-done((bf16[640,256]{1,0:T(8,128)(2,1)S(1)}, bf16[640,256]{1,0:T(8,128)(2,1)S(1)}, u32[]{:S(2)}, u32[]{:S(2)}) %collective-permute-start.3) | collective-permute-done | bytes 327712 | tf_op jit(solution)/shard_map/ppermute | solution.py:307
  28.5 1.2 %collective-permute-done.2.arrived_ref.refs_1_ = bf16[640,256]{1,0:T(8,128)(2,1)S(1)} collective-permute-done((bf16[640,256]{1,0:T(8,128)(2,1)S(1)}, bf16[640,256]{1,0:T(8,128)(2,1)S(1)}, u32[]{:S(2)}, u32[]{:S(2)}) %collective-permute-start.2) | collective-permute-done | bytes 327712 | tf_op jit(solution)/shard_map/ppermute | solution.py:307
  30.2 1.5 %collective-permute-start.10 = (bf16[640,256]{1,0:T(8,128)(2,1)S(1)}, bf16[640,256]{1,0:T(8,128)(2,1)S(1)}, u32[]{:S(2)}, u32[]{:S(2)}) collective-permute-start(bf16[640,256]{1,0:T(8,128)(2,1)S(1)} %get-tuple-element.64), channel_id=1, source_target_pairs={{0,2},{2,0},{1,3},{3,1},{4,6},{6,4},{5,7},{7,5},{8,10},{10,8},{9,1... | collective-permute-start | bytes 983048 | tf_op jit(solution)/shard_map/ppermute | solution.py:307
  32.7 1.5 %collective-permute-start.9 = (bf16[640,256]{1,0:T(8,128)(2,1)S(1)}, bf16[640,256]{1,0:T(8,128)(2,1)S(1)}, u32[]{:S(2)}, u32[]{:S(2)}) collective-permute-start(bf16[640,256]{1,0:T(8,128)(2,1)S(1)} %collective-permute-done.2.arrived_ref.refs_1_), channel_id=1, source_target_pairs={{0,16},{16,0},{1,17},{17,1},{2,18},{18,2},{3,19},{19,3},{4,20},{20... | collective-permute-start | bytes 983048 | tf_op jit(solution)/shard_map/ppermute | solution.py:307
  34.2 6.6 %collective-permute-done.10.arrived_ref = bf16[640,256]{1,0:T(8,128)(2,1)S(1)} collective-permute-done((bf16[640,256]{1,0:T(8,128)(2,1)S(1)}, bf16[640,256]{1,0:T(8,128)(2,1)S(1)}, u32[]{:S(2)}, u32[]{:S(2)}) %collective-permute-start.10) | collective-permute-done | bytes 327712 | tf_op jit(solution)/shard_map/ppermute | solution.py:307
  40.8 1.5 %collective-permute-done.8.refs_2_ = bf16[640,256]{1,0:T(8,128)(2,1)S(1)} collective-permute-done((bf16[640,256]{1,0:T(8,128)(2,1)S(1)}, bf16[640,256]{1,0:T(8,128)(2,1)S(1)}, u32[]{:S(2)}, u32[]{:S(2)}) %collective-permute-start.8) | collective-permute-done | bytes 327712 | tf_op jit(solution)/shard_map/ppermute | solution.py:307
  42.3 3.4 %collective-permute-done.7.refs_1_ = bf16[640,256]{1,0:T(8,128)(2,1)S(1)} collective-permute-done((bf16[640,256]{1,0:T(8,128)(2,1)S(1)}, bf16[640,256]{1,0:T(8,128)(2,1)S(1)}, u32[]{:S(2)}, u32[]{:S(2)}) %collective-permute-start.7) | collective-permute-done | bytes 327712 | tf_op jit(solution)/shard_map/ppermute | solution.py:307
  45.7 1.2 %collective-permute-done.9.refs_3_ = bf16[640,256]{1,0:T(8,128)(2,1)S(1)} collective-permute-done((bf16[640,256]{1,0:T(8,128)(2,1)S(1)}, bf16[640,256]{1,0:T(8,128)(2,1)S(1)}, u32[]{:S(2)}, u32[]{:S(2)}) %collective-permute-start.9) | collective-permute-done | bytes 327712 | tf_op jit(solution)/shard_map/ppermute | solution.py:307
  48.9 1.5 %collective-permute-start.13 = (bf16[640,256]{1,0:T(8,128)(2,1)S(1)}, bf16[640,256]{1,0:T(8,128)(2,1)S(1)}, u32[]{:S(2)}, u32[]{:S(2)}) collective-permute-start(bf16[640,256]{1,0:T(8,128)(2,1)S(1)} %get-tuple-element.69), channel_id=1, source_target_pairs={{0,2},{2,0},{1,3},{3,1},{4,6},{6,4},{5,7},{7,5},{8,10},{10,8},{9,1... | collective-permute-start | bytes 983048 | tf_op jit(solution)/shard_map/ppermute | solution.py:307
  51.6 1.0 project.1.refs_6_
  52.6 4.6 %collective-permute-done.13.arrived_ref = bf16[640,256]{1,0:T(8,128)(2,1)S(1)} collective-permute-done((bf16[640,256]{1,0:T(8,128)(2,1)S(1)}, bf16[640,256]{1,0:T(8,128)(2,1)S(1)}, u32[]{:S(2)}, u32[]{:S(2)}) %collective-permute-start.13) | collective-permute-done | bytes 327712 | tf_op jit(solution)/shard_map/ppermute | solution.py:307
  57.2 7.0 %collective-permute-done.12.refs_3_ = bf16[640,256]{1,0:T(8,128)(2,1)S(1)} collective-permute-done((bf16[640,256]{1,0:T(8,128)(2,1)S(1)}, bf16[640,256]{1,0:T(8,128)(2,1)S(1)}, u32[]{:S(2)}, u32[]{:S(2)}) %collective-permute-start.12) | collective-permute-done | bytes 327712 | tf_op jit(solution)/shard_map/ppermute | solution.py:307
  64.4 5.3 %collective-permute-start.16 = (bf16[2,640,256]{2,1,0:T(8,128)(2,1)S(1)}, bf16[2,640,256]{2,1,0:T(8,128)(2,1)S(1)}, u32[]{:S(2)}, u32[]{:S(2)}) collective-permute-start(bf16[2,640,256]{2,1,0:T(8,128)(2,1)S(1)} %collective-permute-done.14.refs_0_.refs_1_), channel_id=1, source_target_pairs={{0,1},{1,0},{2,3},{3,2},{4,5},{5,4},{6,7},{7,6},{8,9},{9,8},{10,11... | collective-permute-start | bytes 1966088 | tf_op jit(solution)/shard_map/ppermute | solution.py:307
  69.7 5.5 %attention.1 = (bf16[256,1280]{1,0:T(8,128)(2,1)}, bf16[256,512]{1,0:T(8,128)(2,1)S(1)}) custom-call(bf16[256,2560]{1,0:T(8,128)(2,1)S(1)} %get-tuple-element.55.own_ref, bf16[256,2560]{1,0:T(8,128)(2,1)S(1)} %collective-permute-done.5.other_ref, bf16[640,256]{1,0:T(8,128)(2,1)S(1)} %collective-permute-done.4.refs_0_, ...), custom_call_target="tpu_custom_call" | custom-call | flops 838860800 | bytes 5000000 | tf_op jit(solution)/shard_map/attention/pallas_call | solution.py:172
  75.2 6.7 %collective-permute-done.15.refs_2_.refs_3_.refs_4_.refs_5_ = bf16[2,640,256]{2,1,0:T(8,128)(2,1)S(1)} collective-permute-done((bf16[2,640,256]{2,1,0:T(8,128)(2,1)S(1)}, bf16[2,640,256]{2,1,0:T(8,128)(2,1)S(1)}, u32[]{:S(2)}, u32[]{:S(2)}) %collective-permute-start.15) | collective-permute-done | bytes 655392 | tf_op jit(solution)/shard_map/ppermute | solution.py:340
  82.0 2.6 %collective-permute-start.18 = (bf16[256,512]{1,0:T(8,128)(2,1)S(1)}, bf16[256,512]{1,0:T(8,128)(2,1)S(1)}, u32[]{:S(2)}, u32[]{:S(2)}) collective-permute-start(bf16[256,512]{1,0:T(8,128)(2,1)S(1)} %get-tuple-element.88.refs_12_), channel_id=1, source_target_pairs={{0,2},{2,0},{1,3},{3,1},{4,6},{6,4},{5,7},{7,5},{8,10},{10,8},{9,1... | collective-permute-start | bytes 786440 | tf_op jit(solution)/shard_map/ppermute | solution.py:307
  84.5 4.3 %collective-permute-done.18.refs_13_ = bf16[256,512]{1,0:T(8,128)(2,1)S(1)} collective-permute-done((bf16[256,512]{1,0:T(8,128)(2,1)S(1)}, bf16[256,512]{1,0:T(8,128)(2,1)S(1)}, u32[]{:S(2)}, u32[]{:S(2)}) %collective-permute-start.18) | collective-permute-done | bytes 262176 | tf_op jit(solution)/shard_map/ppermute | solution.py:307
  88.9 3.9 %collective-permute-done.17.refs_14_ = bf16[256,512]{1,0:T(8,128)(2,1)S(1)} collective-permute-done((bf16[256,512]{1,0:T(8,128)(2,1)S(1)}, bf16[256,512]{1,0:T(8,128)(2,1)S(1)}, u32[]{:S(2)}, u32[]{:S(2)}) %collective-permute-start.17) | collective-permute-done | bytes 262176 | tf_op jit(solution)/shard_map/ppermute | solution.py:312
  92.8 6.3 %collective-permute-done.19.refs_15_ = bf16[256,512]{1,0:T(8,128)(2,1)S(1)} collective-permute-done((bf16[256,512]{1,0:T(8,128)(2,1)S(1)}, bf16[256,512]{1,0:T(8,128)(2,1)S(1)}, u32[]{:S(2)}, u32[]{:S(2)}) %collective-permute-start.19) | collective-permute-done | bytes 262176 | tf_op jit(solution)/shard_map/ppermute | solution.py:312
  99.2 2.0 %collective-permute-start.21 = (bf16[256,512]{1,0:T(8,128)(2,1)S(1)}, bf16[256,512]{1,0:T(8,128)(2,1)S(1)}, u32[]{:S(2)}, u32[]{:S(2)}) collective-permute-start(bf16[256,512]{1,0:T(8,128)(2,1)S(1)} %collective-permute-done.17.refs_14_), channel_id=1, source_target_pairs={{0,4},{4,8},{8,12},{12,0},{1,5},{5,9},{9,13},{13,1},{2,6},{6,10},{... | collective-permute-start | bytes 786440 | tf_op jit(solution)/shard_map/ppermute | solution.py:312
  102.0 5.4 %collective-permute-done.21.refs_4_ = bf16[256,512]{1,0:T(8,128)(2,1)S(1)} collective-permute-done((bf16[256,512]{1,0:T(8,128)(2,1)S(1)}, bf16[256,512]{1,0:T(8,128)(2,1)S(1)}, u32[]{:S(2)}, u32[]{:S(2)}) %collective-permute-start.21) | collective-permute-done | bytes 262176 | tf_op jit(solution)/shard_map/ppermute | solution.py:312
  107.5 1.6 %collective-permute-start.23 = (bf16[256,512]{1,0:T(8,128)(2,1)S(1)}, bf16[256,512]{1,0:T(8,128)(2,1)S(1)}, u32[]{:S(2)}, u32[]{:S(2)}) collective-permute-start(bf16[256,512]{1,0:T(8,128)(2,1)S(1)} %collective-permute-done.21.refs_4_), channel_id=1, source_target_pairs={{0,2},{2,0},{1,3},{3,1},{4,6},{6,4},{5,7},{7,5},{8,10},{10,8},{9,1... | collective-permute-start | bytes 786440 | tf_op jit(solution)/shard_map/ppermute | solution.py:307
  109.2 1.7 %gradient.2 = (f32[2,640,256]{2,1,0:T(8,128)S(1)}, f32[2,256]{1,0:T(2,128)S(1)}) custom-call(bf16[2,640,256]{2,1,0:T(8,128)(2,1)S(1)} %collective-permute-done.14.refs_0_.refs_1_, bf16[2,640,256]{2,1,0:T(8,128)(2,1)S(1)} %collective-permute-done.14.refs_0_.refs_1_, bf16[2,640,256]{2,1,0:T(8,128)(2,1)S(1)} %collective-permute-done.15.refs_2_.refs_3_.refs_4_.refs_5_, ...), custom_call_target="tpu_custom_call" | custom-call | flops 1006632960 | bytes 5000000 | tf_op jit(solution)/shard_map/gradient/pallas_call | solution.py:237
  110.9 3.0 %collective-permute-done.23.refs_5_ = bf16[256,512]{1,0:T(8,128)(2,1)S(1)} collective-permute-done((bf16[256,512]{1,0:T(8,128)(2,1)S(1)}, bf16[256,512]{1,0:T(8,128)(2,1)S(1)}, u32[]{:S(2)}, u32[]{:S(2)}) %collective-permute-start.23) | collective-permute-done | bytes 262176 | tf_op jit(solution)/shard_map/ppermute | solution.py:307
  113.9 1.7 %gradient.3 = (f32[2,640,256]{2,1,0:T(8,128)}, f32[2,256]{1,0:T(2,128)}) custom-call(bf16[2,640,256]{2,1,0:T(8,128)(2,1)S(1)} %collective-permute-done.14.refs_0_.refs_1_, bf16[2,640,256]{2,1,0:T(8,128)(2,1)S(1)} %collective-permute-done.14.refs_0_.refs_1_, bf16[2,640,256]{2,1,0:T(8,128)(2,1)S(1)} %collective-permute-done.16.refs_6_.refs_7_.refs_2_.refs_3_, ...), custom_call_target="tpu_custom_call" | custom-call | flops 335544320 | bytes 5000000 | tf_op jit(solution)/shard_map/gradient/pallas_call | solution.py:237
  (49 shorter events, 8.5 us)
Async XLA Ops:
  0.6 6.2 %copy-start = (bf16[256,2560]{1,0:T(8,128)(2,1)S(1)}, bf16[256,2560]{1,0:T(8,128)(2,1)}, u32[]{:S(2)}) copy-start(bf16[256,2560]{1,0:T(8,128)(2,1)} %values_ref.1) | copy-start | bytes 3932164
  0.6 5.9 %copy-start.4 = (bf16[5120]{0:T(1024)(128)(2,1)S(1)}, bf16[5120]{0:T(1024)(128)(2,1)}, u32[]{:S(2)}) copy-start(bf16[5120]{0:T(1024)(128)(2,1)} %param.7) | copy-start | bytes 30724
  2.4 4.3 %collective-permute-start.1 = (f32[256,1]{0,1:T(1,128)S(1)}, f32[256,1]{0,1:T(1,128)S(1)}, u32[]{:S(2)}, u32[]{:S(2)}) collective-permute-start(f32[256,1]{0,1:T(1,128)S(1)} %bitcast.3), channel_id=1, source_target_pairs={{0,1},{1,0},{2,3},{3,2},{4,5},{5,4},{6,7},{7,6},{8,9},{9,8},{10,11... | collective-permute-start | bytes 3080 | tf_op jit(solution)/shard_map/ppermute | solution.py:307
  3.9 13.0 %collective-permute-start = (bf16[640,256]{1,0:T(8,128)(2,1)S(1)}, bf16[640,256]{1,0:T(8,128)(2,1)S(1)}, u32[]{:S(2)}, u32[]{:S(2)}) collective-permute-start(bf16[640,256]{1,0:T(8,128)(2,1)S(1)} %dynamic-slice_bitcast_fusion), channel_id=1, source_target_pairs={{0,4},{4,8},{8,12},{12,0},{1,5},{5,9},{9,13},{13,1},{2,6},{6,10},{... | collective-permute-start | bytes 983048 | tf_op jit(solution)/shard_map/ppermute | solution.py:312
  17.0 12.8 %collective-permute-start.5 = (bf16[256,2560]{1,0:T(8,128)(2,1)S(1)}, bf16[256,2560]{1,0:T(8,128)(2,1)S(1)}, u32[]{:S(2)}, u32[]{:S(2)}) collective-permute-start(bf16[256,2560]{1,0:T(8,128)(2,1)S(1)} %get-tuple-element.55.own_ref), channel_id=1, source_target_pairs={{0,1},{1,0},{2,3},{3,2},{4,5},{5,4},{6,7},{7,6},{8,9},{9,8},{10,11... | collective-permute-start | bytes 3932168 | tf_op jit(solution)/shard_map/ppermute | solution.py:307
  17.0 10.1 %collective-permute-start.4 = (bf16[640,256]{1,0:T(8,128)(2,1)S(1)}, bf16[640,256]{1,0:T(8,128)(2,1)S(1)}, u32[]{:S(2)}, u32[]{:S(2)}) collective-permute-start(bf16[640,256]{1,0:T(8,128)(2,1)S(1)} %dynamic-slice_bitcast_fusion), channel_id=1, source_target_pairs={{0,12},{4,0},{8,4},{12,8},{1,13},{5,1},{9,5},{13,9},{2,14},{6,2},{... | collective-permute-start | bytes 983048 | tf_op jit(solution)/shard_map/ppermute | solution.py:312
  18.7 9.8 %collective-permute-start.3 = (bf16[640,256]{1,0:T(8,128)(2,1)S(1)}, bf16[640,256]{1,0:T(8,128)(2,1)S(1)}, u32[]{:S(2)}, u32[]{:S(2)}) collective-permute-start(bf16[640,256]{1,0:T(8,128)(2,1)S(1)} %collective-permute-done.kept_ref.refs_0_), channel_id=1, source_target_pairs={{0,16},{16,0},{1,17},{17,1},{2,18},{18,2},{3,19},{19,3},{4,20},{20... | collective-permute-start | bytes 983048 | tf_op jit(solution)/shard_map/ppermute | solution.py:307
  20.2 9.6 %collective-permute-start.2 = (bf16[640,256]{1,0:T(8,128)(2,1)S(1)}, bf16[640,256]{1,0:T(8,128)(2,1)S(1)}, u32[]{:S(2)}, u32[]{:S(2)}) collective-permute-start(bf16[640,256]{1,0:T(8,128)(2,1)S(1)} %collective-permute-done.kept_ref.refs_0_), channel_id=1, source_target_pairs={{0,2},{2,0},{1,3},{3,1},{4,6},{6,4},{5,7},{7,5},{8,10},{10,8},{9,1... | collective-permute-start | bytes 983048 | tf_op jit(solution)/shard_map/ppermute | solution.py:307
  29.8 21.7 %copy-start.1 = (bf16[2,1280,256]{2,1,0:T(8,128)(2,1)S(1)}, bf16[2,1280,256]{2,1,0:T(8,128)(2,1)}, u32[]{:S(2)}) copy-start(bf16[2,1280,256]{2,1,0:T(8,128)(2,1)} %weight_ref.1) | copy-start | bytes 3932164
  29.8 17.6 %collective-permute-start.6 = (bf16[2,640,256]{2,1,0:T(8,128)(2,1)S(1)}, bf16[2,640,256]{2,1,0:T(8,128)(2,1)S(1)}, u32[]{:S(2)}, u32[]{:S(2)}) collective-permute-start(bf16[2,640,256]{2,1,0:T(8,128)(2,1)S(1)} %pack.3), channel_id=1, source_target_pairs={{0,4},{4,8},{8,12},{12,0},{1,5},{5,9},{9,13},{13,1},{2,6},{6,10},{... | collective-permute-start | bytes 1966088 | tf_op jit(solution)/shard_map/ppermute | solution.py:312
  30.2 10.6 %collective-permute-start.10 = (bf16[640,256]{1,0:T(8,128)(2,1)S(1)}, bf16[640,256]{1,0:T(8,128)(2,1)S(1)}, u32[]{:S(2)}, u32[]{:S(2)}) collective-permute-start(bf16[640,256]{1,0:T(8,128)(2,1)S(1)} %get-tuple-element.64), channel_id=1, source_target_pairs={{0,2},{2,0},{1,3},{3,1},{4,6},{6,4},{5,7},{7,5},{8,10},{10,8},{9,1... | collective-permute-start | bytes 983048 | tf_op jit(solution)/shard_map/ppermute | solution.py:307
  31.7 10.6 %collective-permute-start.8 = (bf16[640,256]{1,0:T(8,128)(2,1)S(1)}, bf16[640,256]{1,0:T(8,128)(2,1)S(1)}, u32[]{:S(2)}, u32[]{:S(2)}) collective-permute-start(bf16[640,256]{1,0:T(8,128)(2,1)S(1)} %collective-permute-done.4.refs_0_), channel_id=1, source_target_pairs={{0,16},{16,0},{1,17},{17,1},{2,18},{18,2},{3,19},{19,3},{4,20},{20... | collective-permute-start | bytes 983048 | tf_op jit(solution)/shard_map/ppermute | solution.py:307
  32.2 13.5 %collective-permute-start.7 = (bf16[640,256]{1,0:T(8,128)(2,1)S(1)}, bf16[640,256]{1,0:T(8,128)(2,1)S(1)}, u32[]{:S(2)}, u32[]{:S(2)}) collective-permute-start(bf16[640,256]{1,0:T(8,128)(2,1)S(1)} %collective-permute-done.4.refs_0_), channel_id=1, source_target_pairs={{0,2},{2,0},{1,3},{3,1},{4,6},{6,4},{5,7},{7,5},{8,10},{10,8},{9,1... | collective-permute-start | bytes 983048 | tf_op jit(solution)/shard_map/ppermute | solution.py:307
  32.7 14.2 %collective-permute-start.9 = (bf16[640,256]{1,0:T(8,128)(2,1)S(1)}, bf16[640,256]{1,0:T(8,128)(2,1)S(1)}, u32[]{:S(2)}, u32[]{:S(2)}) collective-permute-start(bf16[640,256]{1,0:T(8,128)(2,1)S(1)} %collective-permute-done.2.arrived_ref.refs_1_), channel_id=1, source_target_pairs={{0,16},{16,0},{1,17},{17,1},{2,18},{18,2},{3,19},{19,3},{4,20},{20... | collective-permute-start | bytes 983048 | tf_op jit(solution)/shard_map/ppermute | solution.py:307
  47.5 16.8 %collective-permute-start.14 = (bf16[2,640,256]{2,1,0:T(8,128)(2,1)S(1)}, bf16[2,640,256]{2,1,0:T(8,128)(2,1)S(1)}, u32[]{:S(2)}, u32[]{:S(2)}) collective-permute-start(bf16[2,640,256]{2,1,0:T(8,128)(2,1)S(1)} %pack.4), channel_id=1, source_target_pairs={{0,0},{1,8},{4,4},{5,12},{8,1},{9,9},{12,5},{13,13},{2,2},{3,10},{... | collective-permute-start | bytes 1966088 | tf_op jit(solution)/shard_map/ppermute | solution.py:340
  48.2 16.1 %collective-permute-start.11 = (bf16[2,640,256]{2,1,0:T(8,128)(2,1)S(1)}, bf16[2,640,256]{2,1,0:T(8,128)(2,1)S(1)}, u32[]{:S(2)}, u32[]{:S(2)}) collective-permute-start(bf16[2,640,256]{2,1,0:T(8,128)(2,1)S(1)} %collective-permute-done.6.refs_4_), channel_id=1, source_target_pairs={{0,16},{16,0},{1,17},{17,1},{2,18},{18,2},{3,19},{19,3},{4,20},{20... | collective-permute-start | bytes 1966088 | tf_op jit(solution)/shard_map/ppermute | solution.py:307
  48.9 8.3 %collective-permute-start.13 = (bf16[640,256]{1,0:T(8,128)(2,1)S(1)}, bf16[640,256]{1,0:T(8,128)(2,1)S(1)}, u32[]{:S(2)}, u32[]{:S(2)}) collective-permute-start(bf16[640,256]{1,0:T(8,128)(2,1)S(1)} %get-tuple-element.69), channel_id=1, source_target_pairs={{0,2},{2,0},{1,3},{3,1},{4,6},{6,4},{5,7},{7,5},{8,10},{10,8},{9,1... | collective-permute-start | bytes 983048 | tf_op jit(solution)/shard_map/ppermute | solution.py:307
  50.4 13.9 %collective-permute-start.12 = (bf16[640,256]{1,0:T(8,128)(2,1)S(1)}, bf16[640,256]{1,0:T(8,128)(2,1)S(1)}, u32[]{:S(2)}, u32[]{:S(2)}) collective-permute-start(bf16[640,256]{1,0:T(8,128)(2,1)S(1)} %collective-permute-done.8.refs_2_), channel_id=1, source_target_pairs={{0,2},{2,0},{1,3},{3,1},{4,6},{6,4},{5,7},{7,5},{8,10},{10,8},{9,1... | collective-permute-start | bytes 983048 | tf_op jit(solution)/shard_map/ppermute | solution.py:307
  52.6 17.1 %copy-start.5 = (bf16[2,256]{1,0:T(2,128)(2,1)S(1)}, bf16[2,256]{1,0:T(2,128)(2,1)}, u32[]{:S(2)}) copy-start(bf16[2,256]{1,0:T(2,128)(2,1)} %param.11) | copy-start | bytes 3076
  52.6 17.1 %copy-start.2 = (bf16[256,1280]{1,0:T(8,128)(2,1)S(1)}, bf16[256,1280]{1,0:T(8,128)(2,1)}, u32[]{:S(2)}) copy-start(bf16[256,1280]{1,0:T(8,128)(2,1)} %refs_10_.1) | copy-start | bytes 1966084
  52.6 17.1 %copy-start.3 = (bf16[256,1280]{1,0:T(8,128)(2,1)S(1)}, bf16[256,1280]{1,0:T(8,128)(2,1)}, u32[]{:S(2)}) copy-start(bf16[256,1280]{1,0:T(8,128)(2,1)} %refs_11_.1) | copy-start | bytes 1966084
  64.3 17.7 %collective-permute-start.15 = (bf16[2,640,256]{2,1,0:T(8,128)(2,1)S(1)}, bf16[2,640,256]{2,1,0:T(8,128)(2,1)S(1)}, u32[]{:S(2)}, u32[]{:S(2)}) collective-permute-start(bf16[2,640,256]{2,1,0:T(8,128)(2,1)S(1)} %pack.5), channel_id=1, source_target_pairs={{0,4},{1,12},{4,0},{5,8},{8,5},{9,13},{12,1},{13,9},{2,6},{3,14},{... | collective-permute-start | bytes 1966088 | tf_op jit(solution)/shard_map/ppermute | solution.py:340
  64.4 17.6 %collective-permute-start.16 = (bf16[2,640,256]{2,1,0:T(8,128)(2,1)S(1)}, bf16[2,640,256]{2,1,0:T(8,128)(2,1)S(1)}, u32[]{:S(2)}, u32[]{:S(2)}) collective-permute-start(bf16[2,640,256]{2,1,0:T(8,128)(2,1)S(1)} %collective-permute-done.14.refs_0_.refs_1_), channel_id=1, source_target_pairs={{0,1},{1,0},{2,3},{3,2},{4,5},{5,4},{6,7},{7,6},{8,9},{9,8},{10,11... | collective-permute-start | bytes 1966088 | tf_op jit(solution)/shard_map/ppermute | solution.py:307
  82.0 6.9 %collective-permute-start.18 = (bf16[256,512]{1,0:T(8,128)(2,1)S(1)}, bf16[256,512]{1,0:T(8,128)(2,1)S(1)}, u32[]{:S(2)}, u32[]{:S(2)}) collective-permute-start(bf16[256,512]{1,0:T(8,128)(2,1)S(1)} %get-tuple-element.88.refs_12_), channel_id=1, source_target_pairs={{0,2},{2,0},{1,3},{3,1},{4,6},{6,4},{5,7},{7,5},{8,10},{10,8},{9,1... | collective-permute-start | bytes 786440 | tf_op jit(solution)/shard_map/ppermute | solution.py:307
  84.5 8.2 %collective-permute-start.17 = (bf16[256,512]{1,0:T(8,128)(2,1)S(1)}, bf16[256,512]{1,0:T(8,128)(2,1)S(1)}, u32[]{:S(2)}, u32[]{:S(2)}) collective-permute-start(bf16[256,512]{1,0:T(8,128)(2,1)S(1)} %get-tuple-element.88.refs_12_), channel_id=1, source_target_pairs={{0,4},{4,8},{8,12},{12,0},{1,5},{5,9},{9,13},{13,1},{2,6},{6,10},{... | collective-permute-start | bytes 786440 | tf_op jit(solution)/shard_map/ppermute | solution.py:312
  92.8 6.4 %collective-permute-start.19 = (bf16[256,512]{1,0:T(8,128)(2,1)S(1)}, bf16[256,512]{1,0:T(8,128)(2,1)S(1)}, u32[]{:S(2)}, u32[]{:S(2)}) collective-permute-start(bf16[256,512]{1,0:T(8,128)(2,1)S(1)} %get-tuple-element.88.refs_12_), channel_id=1, source_target_pairs={{0,12},{4,0},{8,4},{12,8},{1,13},{5,1},{9,5},{13,9},{2,14},{6,2},{... | collective-permute-start | bytes 786440 | tf_op jit(solution)/shard_map/ppermute | solution.py:312
  92.8 6.4 %collective-permute-start.20 = (bf16[256,512]{1,0:T(8,128)(2,1)S(1)}, bf16[256,512]{1,0:T(8,128)(2,1)S(1)}, u32[]{:S(2)}, u32[]{:S(2)}) collective-permute-start(bf16[256,512]{1,0:T(8,128)(2,1)S(1)} %collective-permute-done.17.refs_14_), channel_id=1, source_target_pairs={{0,2},{2,0},{1,3},{3,1},{4,6},{6,4},{5,7},{7,5},{8,10},{10,8},{9,1... | collective-permute-start | bytes 786440 | tf_op jit(solution)/shard_map/ppermute | solution.py:307
  92.8 16.3 %collective-permute-start.24 = (bf16[2,640,256]{2,1,0:T(8,128)(2,1)S(1)}, bf16[2,640,256]{2,1,0:T(8,128)(2,1)S(1)}, u32[]{:S(2)}, u32[]{:S(2)}) collective-permute-start(bf16[2,640,256]{2,1,0:T(8,128)(2,1)S(1)} %collective-permute-done.15.refs_2_.refs_3_.refs_4_.refs_5_), channel_id=1, source_target_pairs={{0,1},{1,0},{2,3},{3,2},{4,5},{5,4},{6,7},{7,6},{8,9},{9,8},{10,11... | collective-permute-start | bytes 1966088 | tf_op jit(solution)/shard_map/ppermute | solution.py:307
  99.2 8.2 %collective-permute-start.21 = (bf16[256,512]{1,0:T(8,128)(2,1)S(1)}, bf16[256,512]{1,0:T(8,128)(2,1)S(1)}, u32[]{:S(2)}, u32[]{:S(2)}) collective-permute-start(bf16[256,512]{1,0:T(8,128)(2,1)S(1)} %collective-permute-done.17.refs_14_), channel_id=1, source_target_pairs={{0,4},{4,8},{8,12},{12,0},{1,5},{5,9},{9,13},{13,1},{2,6},{6,10},{... | collective-permute-start | bytes 786440 | tf_op jit(solution)/shard_map/ppermute | solution.py:312
  101.2 6.4 %collective-permute-start.22 = (bf16[256,512]{1,0:T(8,128)(2,1)S(1)}, bf16[256,512]{1,0:T(8,128)(2,1)S(1)}, u32[]{:S(2)}, u32[]{:S(2)}) collective-permute-start(bf16[256,512]{1,0:T(8,128)(2,1)S(1)} %collective-permute-done.19.refs_15_), channel_id=1, source_target_pairs={{0,2},{2,0},{1,3},{3,1},{4,6},{6,4},{5,7},{7,5},{8,10},{10,8},{9,1... | collective-permute-start | bytes 786440 | tf_op jit(solution)/shard_map/ppermute | solution.py:307
  107.5 6.4 %collective-permute-start.23 = (bf16[256,512]{1,0:T(8,128)(2,1)S(1)}, bf16[256,512]{1,0:T(8,128)(2,1)S(1)}, u32[]{:S(2)}, u32[]{:S(2)}) collective-permute-start(bf16[256,512]{1,0:T(8,128)(2,1)S(1)} %collective-permute-done.21.refs_4_), channel_id=1, source_target_pairs={{0,2},{2,0},{1,3},{3,1},{4,6},{6,4},{5,7},{7,5},{8,10},{10,8},{9,1... | collective-permute-start | bytes 786440 | tf_op jit(solution)/shard_map/ppermute | solution.py:307

commit v14 on v13

--- a/solution.py
+++ b/solution.py
@@ -103,152 +103,157 @@
     )(normed, normed_other, kv_weight, *pieces)
 
 
-def attention_body(raw_of, cosine, sine, queries_ref, cotangent_ref, grad_query_ref, pair_ref):
-    length, columns = cosine.shape[0], pair_ref.shape[1] // 2
-    key_heads = columns // HEAD
-    group_size = queries_ref.shape[1] // columns
+def attention_body(raw_keys, raw_values, cosine, sine, queries_ref, cotangent_ref, first, store):
+    length = cosine.shape[0]
     key_at = lax.broadcasted_iota(jnp.int32, (length, length), 0)
     query_at = lax.broadcasted_iota(jnp.int32, (length, length), 1)
     causal = key_at <= query_at
-    for head in range(key_heads):
-        lanes = slice(head * HEAD, (head + 1) * HEAD)
-        raw = raw_of(0, lanes)
-        wide_keys = raw * cosine + pltpu.roll(raw, HEAD // 2, 1) * sine
-        keys = wide_keys.astype(jnp.bfloat16)
-        keys_across = wide_keys.T.astype(jnp.bfloat16)
-        values = raw_of(1, lanes).astype(jnp.bfloat16)
-        grad_rotated = jnp.zeros((length, HEAD), jnp.float32)
-        grad_value = jnp.zeros((length, HEAD), jnp.float32)
-        for member in range(group_size):
-            start = (head * group_size + member) * HEAD
-            query = queries_ref[:, start : start + HEAD]
-            upstream = cotangent_ref[:, start : start + HEAD]
-            scores = jnp.where(causal, product_rows(keys, query), -jnp.inf)
-            peak = jnp.max(scores, 0, keepdims=True)
-            exponentials = jnp.exp((scores - peak) * SCALE)
-            probability = exponentials * (1.0 / jnp.sum(exponentials, 0, keepdims=True))
-            grad_probability = product_rows(values, upstream)
-            total = jnp.sum(probability * grad_probability, 0, keepdims=True)
-            grad_scores = (probability * (grad_probability - total) * SCALE).astype(jnp.bfloat16)
-            grad_rotated += product(grad_scores, query)
-            grad_value += product(probability.astype(jnp.bfloat16), upstream)
-            grad_query = product(keys_across, grad_scores)
-            grad_query_ref[:, start : start + HEAD] = grad_query.T.astype(jnp.bfloat16)
-        grad_key = grad_rotated * cosine - pltpu.roll(grad_rotated, HEAD // 2, 1) * sine
-        pair_ref[:, lanes] = grad_key.astype(jnp.bfloat16)
-        pair_ref[:, columns + head * HEAD : columns + (head + 1) * HEAD] = grad_value.astype(
-            jnp.bfloat16
-        )
-
-
-def attention_kernel(distances, own_ref, other_ref, *refs):
-    pairs, refs = refs[4:6], refs[:4] + refs[6:]
+    wide_keys = raw_keys * cosine + pltpu.roll(raw_keys, HEAD // 2, 1) * sine
+    keys = wide_keys.astype(jnp.bfloat16)
+    keys_across = wide_keys.T.astype(jnp.bfloat16)
+    values = raw_values.astype(jnp.bfloat16)
+    grad_rotated = jnp.zeros((length, HEAD), jnp.float32)
+    grad_value = jnp.zeros((length, HEAD), jnp.float32)
+    for member, start in enumerate(first):
+        query = queries_ref[:, start : start + HEAD]
+        upstream = cotangent_ref[:, start : start + HEAD]
+        scores = jnp.where(causal, product_rows(keys, query), -jnp.inf)
+        peak = jnp.max(scores, 0, keepdims=True)
+        exponentials = jnp.exp((scores - peak) * SCALE)
+        probability = exponentials * (1.0 / jnp.sum(exponentials, 0, keepdims=True))
+        grad_probability = product_rows(values, upstream)
+        total = jnp.sum(probability * grad_probability, 0, keepdims=True)
+        grad_scores = (probability * (grad_probability - total) * SCALE).astype(jnp.bfloat16)
+        grad_rotated += product(grad_scores, query)
+        grad_value += product(probability.astype(jnp.bfloat16), upstream)
+        store(member, product(keys_across, grad_scores).T.astype(jnp.bfloat16))
+    grad_key = grad_rotated * cosine - pltpu.roll(grad_rotated, HEAD // 2, 1) * sine
+    return grad_key.astype(jnp.bfloat16), grad_value.astype(jnp.bfloat16)
+
+
+def query_starts(head, queries, columns):
+    group_size = queries.shape[1] // columns
+    return [(head * group_size + member) * HEAD for member in range(group_size)]
+
+
+def attention_kernel(head, distances, own_ref, other_ref, *refs):
+    pairs = refs[4:6]
     pieces = [*refs[:4], *(pair.at[at] for pair in pairs for at in range(2))]
-    refs = refs[4:]
-    sums_ref, bias_ref, cosine_ref, sine_ref, queries_ref, cotangent_ref = refs[:6]
-    grad_query_ref, pair_ref, raw_ref = refs[6:]
+    sums_ref, bias_ref, cosine_ref, sine_ref, queries_ref, cotangent_ref = refs[6:12]
+    before_ref = refs[12] if head else None
+    grad_query_ref, pair_ref, raw_ref = refs[-3:]
     group = lax.axis_index("groups")
-    totals = [sums_ref[group], sums_ref[1 - group]]
+    lanes = slice(head * HEAD, (head + 1) * HEAD)
+    totals = [sums_ref[group, :, lanes], sums_ref[1 - group, :, lanes]]
     for at, distance in enumerate(distances):
-        four = pieces[4 * at : 4 * at + 4]
+        four = [piece.at[:, lanes] for piece in pieces[4 * at : 4 * at + 4]]
         terms = block_terms(own_ref, other_ref, block_from(distance), four)
         totals = [total + term for total, term in zip(totals, terms)]
     raw_ref[group] = totals[0]
     raw_ref[1 - group] = totals[1]
-
-    def raw_of(j, lanes):
-        return raw_ref[j, :, lanes] + bias_ref[j : j + 1, lanes]
-
-    attention_body(
-        raw_of, cosine_ref[...], sine_ref[...], queries_ref, cotangent_ref, grad_query_ref, pair_ref
-    )
-
-
-def attention(gathered, normed, normed_other, sums, bias, cosine, sine, queries, cotangent):
+    starts = query_starts(head, queries_ref, sums_ref.shape[2])
+    offset = 0
+    if head:
+        offset = before_ref.shape[1]
+        grad_query_ref[:, :offset] = before_ref[...]
+
+    def store(member, value):
+        at = offset + member * HEAD
+        grad_query_ref[:, at : at + HEAD] = value
+
+    pair_ref[:, :HEAD], pair_ref[:, HEAD:] = attention_body(
+        raw_ref[0] + bias_ref[0:1, lanes],
+        raw_ref[1] + bias_ref[1:2, lanes],
+        cosine_ref[...],
+        sine_ref[...],
+        queries_ref,
+        cotangent_ref,
+        starts,
+        store,
+    )
+
+
+def attention(head, gathered, normed, normed_other, sums, bias, tables, queries, cotangent, before):
     length = normed.shape[0]
     distances = tuple(distance for distance, _ in gathered)
     pieces = [piece for _, parts in gathered for piece in parts]
-    operands = (normed, normed_other, *pieces, sums, bias, cosine, sine, queries, cotangent)
+    operands = (normed, normed_other, *pieces, sums, bias, *tables, queries, cotangent, *before)
+    width = queries.shape[1] // 2 * (head + 1)
     return pl.pallas_call(
-        functools.partial(attention_kernel, distances),
+        functools.partial(attention_kernel, head, distances),
         in_specs=[IN_VMEM] * len(operands),
         out_specs=[IN_VMEM] * 2,
-        scratch_shapes=[pltpu.VMEM(sums.shape, jnp.float32)],
+        scratch_shapes=[pltpu.VMEM((2, length, HEAD), jnp.float32)],
         out_shape=[
-            jax.ShapeDtypeStruct(queries.shape, jnp.bfloat16),
-            jax.ShapeDtypeStruct((length, 2 * bias.shape[1]), jnp.bfloat16),
+            jax.ShapeDtypeStruct((length, width), jnp.bfloat16),
+            jax.ShapeDtypeStruct((length, 2 * HEAD), jnp.bfloat16),
         ],
         compiler_params=pltpu.CompilerParams(vmem_limit_bytes=VMEM_BYTES),
         cost_estimate=pl.CostEstimate(
-            flops=10 * length * length * queries.shape[1],
-            bytes_accessed=5000000,
-            transcendentals=length * length * queries.shape[1] // HEAD,
+            flops=5 * length * length * queries.shape[1],
+            bytes_accessed=4000000,
+            transcendentals=length * length * queries.shape[1] // HEAD // 2,
         ),
         name="attention",
     )(*operands)
 
 
-def gradient_kernel(sources, first, *refs):
+def gradient_terms(sources, pairs, slabs):
+    core, core_blocks = lax.axis_index("sub"), lax.axis_size("blk") // 2
+    total = bias_total = None
+    for (distance, same), pair in zip(sources, pairs):
+        here = lax.div(block_from(distance), core_blocks) == core
+        own, other = slabs[distance % 2, same]
+        term = product(jnp.where(here, own[...], other[...]), pair[...])
+        bias_term = jnp.sum(pair[...].astype(jnp.float32), axis=0, keepdims=True)
+        total = term if total is None else total + term
+        bias_total = bias_term if bias_total is None else bias_total + bias_term
+    return total, bias_total
+
+
+def slabs_in(even, odd):
+    slabs = {(0, same): tuple(ref.at[0 if same else 1] for ref in even) for same in (True, False)}
+    if odd:
+        slabs[1, True], slabs[1, False] = (odd[0], odd[1]), (odd[2], odd[3])
+    return slabs
+
+
+def first_kernel(sources, *refs):
     count = len(sources)
-    own, other, pairs = (refs[i * count : (i + 1) * count] for i in range(3))
-    refs = refs[3 * count :]
-    weight_ref, bias_ref = refs[-2:]
-    columns = weight_ref.shape[2]
-    core, cores_blocks = lax.axis_index("sub"), lax.axis_size("blk") // 2
-    total = None
-    for at, (distance, _) in enumerate(sources):
-        here = lax.div(block_from(distance), cores_blocks) == core
-        slab = jnp.where(here, own[at][0], other[at][0])
-        term = product(slab, pairs[at][...])
-        total = term if total is None else total + term
+    pairs, slabs = refs[:count], slabs_in(refs[count : count + 2], refs[count + 2 : count + 6])
+    refs[-2][...], refs[-1][...] = gradient_terms(sources, pairs, slabs)
+
+
+def last_kernel(sources, final, *refs):
+    count = len(sources)
+    pairs, slabs = refs[:count], slabs_in(refs[count : count + 2], ())
+    total, bias_total = gradient_terms(sources, pairs, slabs)
+    sums_ref, bias_sums_ref = refs[count + 2 : count + 4]
+    total, bias_total = sums_ref[...] + total, bias_sums_ref[...] + bias_total
+    if not final:
+        refs[-2][...], refs[-1][...] = total, bias_total
+        return
+    before_ref, bias_before_ref, weight_ref, bias_ref = refs[count + 4 :]
     for j in range(2):
-        part = total[:, j * columns : (j + 1) * columns]
-        weight_ref[j] = part if first else refs[0][j] + part
-
-    @pl.when(pl.program_id(0) == 0)
-    def _():
-        total = None
-        for pair in pairs:
-            term = jnp.sum(pair[...].astype(jnp.float32), axis=0, keepdims=True)
-            total = term if total is None else total + term
-        for j in range(2):
-            part = total[:, j * columns : (j + 1) * columns]
-            bias_ref[j : j + 1, :] = part if first else refs[1][j : j + 1, :] + part
-
-
-def gradient(slabs, some, sums):
-    pairs = list(some.values())
-    _, share, length = slabs[0][0].shape
-    columns = pairs[0].shape[1] // 2
-    count = len(pairs)
-    tile = share // 2 if share % 32 == 0 else share
-
-    def slab_spec(same):
-        return pl.BlockSpec((1, tile, length), lambda i: (0 if same else 1, i, 0))
-
-    weight_spec = pl.BlockSpec((2, tile, columns), lambda i: (0, i, 0))
-    bias_spec = pl.BlockSpec((2, columns), lambda i: (0, 0))
-    in_specs = [slab_spec(same) for _, same in some] * 2
-    in_specs += [pl.BlockSpec((length, 2 * columns), lambda i: (0, 0))] * count
-    if sums:
-        in_specs += [weight_spec, bias_spec]
-    own = [slabs[distance % 2][0] for distance, _ in some]
-    other = [slabs[distance % 2][1] for distance, _ in some]
+        lanes = slice(j * HEAD, (j + 1) * HEAD)
+        weight_ref[j, :, :HEAD], weight_ref[j, :, HEAD:] = before_ref[:, lanes], total[:, lanes]
+        bias_ref[j : j + 1, :HEAD] = bias_before_ref[:, lanes]
+        bias_ref[j : j + 1, HEAD:] = bias_total[:, lanes]
+
+
+def gradient(kernel, operands, share, count, final=False):
+    shapes = ((2, share, 2 * HEAD), (2, 2 * HEAD)) if final else ((share, 2 * HEAD), (1, 2 * HEAD))
     return pl.pallas_call(
-        functools.partial(gradient_kernel, tuple(some), sums is None),
-        grid=(share // tile,),
-        in_specs=in_specs,
-        out_specs=[weight_spec, bias_spec],
-        out_shape=[
-            jax.ShapeDtypeStruct((2, share, columns), jnp.float32),
-            jax.ShapeDtypeStruct((2, columns), jnp.float32),
-        ],
+        kernel,
+        in_specs=[IN_VMEM] * len(operands),
+        out_specs=[IN_VMEM] * 2,
+        out_shape=[jax.ShapeDtypeStruct(shape, jnp.float32) for shape in shapes],
         compiler_params=pltpu.CompilerParams(vmem_limit_bytes=VMEM_BYTES),
         cost_estimate=pl.CostEstimate(
-            flops=4 * count * length * share * columns, bytes_accessed=5000000, transcendentals=0
+            flops=2 * count * HEAD * 2 * share * 2 * HEAD, bytes_accessed=2000000, transcendentals=0
         ),
         name="gradient",
-    )(*own, *other, *pairs, *(sums or ()))
+    )(*operands)
 
 
 def norm_kernel(values_ref, scale_ref, gain_ref, normed_ref, *slab_refs):
@@ -279,9 +284,7 @@
         out_specs=[IN_VMEM] * 5,
         out_shape=[jax.ShapeDtypeStruct(shape, jnp.bfloat16) for shape in shapes],
         compiler_params=pltpu.CompilerParams(vmem_limit_bytes=VMEM_BYTES),
-        cost_estimate=pl.CostEstimate(
-            flops=4 * length * features, bytes_accessed=6 * length * features, transcendentals=0
-        ),
+        cost_estimate=pl.CostEstimate(flops=length, bytes_accessed=length, transcendentals=0),
         name="norm",
     )(activations, scale, gain)
 
@@ -396,49 +399,82 @@
     twice_y, down_both, arrived_odd, even, sums, cosine, sine = lax.optimization_barrier(
         (twice_y, down_both, arrived_odd, even, sums, cosine, sine)
     )
-    odd = sent_along(pack(kept_odd, arrived_odd), 1)
-    even_other = swapped(even, "sub")
+    odd_same, odd_mate = sent_along(kept_odd, 1), sent_along(arrived_odd, 1)
     gathered = [(-1, (down, down_x, down_y, down_both)), (2, (twice, twice_y))]
-    grad_query, grad_pair = attention(
-        gathered, normed, normed_other, sums, bias, cosine, sine, queries, cotangent
-    )
-
-    grad_pair, odd, even_other = lax.optimization_barrier((grad_pair, odd, even_other))
-    pair_up, pair_x = turned(grad_pair, "blk", 1), swapped(grad_pair, "dp")
-    pair_up, pair_x, grad_pair, even, odd = lax.optimization_barrier(
-        (pair_up, pair_x, grad_pair, even, odd)
-    )
-    slabs = ((even, even_other), (odd, swapped(odd, "sub")))
-    pair_down, pair_up_x = turned(grad_pair, "blk", -1), swapped(pair_up, "dp")
-    pair_down, pair_up_x, pair_up = lax.optimization_barrier((pair_down, pair_up_x, pair_up))
-    pair_twice, pair_down_x = turned(pair_up, "blk", 1), swapped(pair_down, "dp")
-    pair_twice, pair_down_x = lax.optimization_barrier((pair_twice, pair_down_x))
-    pair_twice_x = swapped(pair_twice, "dp")
-    first = {
-        (0, True): grad_pair,
-        (0, False): pair_x,
-        (1, True): pair_up,
-        (-1, True): pair_down,
-        (1, False): pair_up_x,
-        (-1, False): pair_down_x,
-    }
-    last = {(2, True): pair_twice, (2, False): pair_twice_x}
-    sums = None
-    for some in (first, last):
-        sums = gradient(slabs, some, sums)
-    grad_weight, grad_bias = sums
+    heads = []
+    before = ()
+    for head in range(2):
+        grad_query, pair = attention(
+            head, gathered, normed, normed_other, sums, bias, (cosine, sine), queries, cotangent,
+            before,
+        )
+        heads.append({(0, True): pair})
+        before = (grad_query,)
+
+    heads[0][0, True], odd_same = lax.optimization_barrier((heads[0][0, True], odd_same))
+    for head in heads:
+        head[1, True], head[0, False] = (
+            turned(head[0, True], "blk", 1),
+            swapped(head[0, True], "dp"),
+        )
+        head.update(zip(head, lax.optimization_barrier(tuple(head.values()))))
+    even_other, odd_same_other = swapped(even, "sub"), swapped(odd_same, "sub")
+    for head in heads:
+        head[-1, True], head[1, False] = (
+            turned(head[0, True], "blk", -1),
+            swapped(head[1, True], "dp"),
+        )
+        head.update(zip(head, lax.optimization_barrier(tuple(head.values()))))
+    odd_mate_other = swapped(odd_mate, "sub")
+    for head in heads:
+        head[2, True], head[-1, False] = (
+            turned(head[1, True], "blk", 1),
+            swapped(head[-1, True], "dp"),
+        )
+        head.update(zip(head, lax.optimization_barrier(tuple(head.values()))))
+    for head in heads:
+        head[2, False] = swapped(head[2, True], "dp")
+
+    slabs = (even, even_other, odd_same, odd_same_other, odd_mate, odd_mate_other)
+    early = ((0, True), (0, False), (1, True), (1, False), (-1, True), (-1, False))
+    late = ((2, True), (2, False))
+    sums = []
+    for head in heads:
+        operands = (*(head[which] for which in early), *slabs)
+        sums.append(gradient(functools.partial(first_kernel, early), operands, share, 6))
+    for at, head in enumerate(heads):
+        operands = (*(head[which] for which in late), *slabs[:2], *sums[at])
+        if at:
+            operands += tuple(sums[0])
+        kernel = functools.partial(last_kernel, late, at == 1)
+        sums[at] = gradient(kernel, operands, share, 2, at == 1)
+    grad_weight, grad_bias = sums[1]
     return (grad_query, grad_weight, grad_bias)
 
 
 def plain_attention_kernel(
     raw_ref, bias_ref, cosine_ref, sine_ref, queries_ref, cotangent_ref, grad_query_ref, pair_ref
 ):
-    def raw_of(j, lanes):
-        return raw_ref[j, :, lanes] + bias_ref[j : j + 1, lanes]
-
-    attention_body(
-        raw_of, cosine_ref[...], sine_ref[...], queries_ref, cotangent_ref, grad_query_ref, pair_ref
-    )
+    columns = raw_ref.shape[2]
+    for head in range(columns // HEAD):
+        lanes = slice(head * HEAD, (head + 1) * HEAD)
+        starts = query_starts(head, queries_ref, columns)
+
+        def store(member, value):
+            grad_query_ref[:, starts[member] : starts[member] + HEAD] = value
+
+        pair_ref[:, lanes], pair_ref[:, columns + head * HEAD : columns + (head + 1) * HEAD] = (
+            attention_body(
+                raw_ref[0, :, lanes] + bias_ref[0:1, lanes],
+                raw_ref[1, :, lanes] + bias_ref[1:2, lanes],
+                cosine_ref[...],
+                sine_ref[...],
+                queries_ref,
+                cotangent_ref,
+                starts,
+                store,
+            )
+        )
 
 
 def general(piece, activations, scale, gain, bias, cosine, sine, queries, cotangent):

time: 118 us -> 116 us (0.983); the launches traced: 116 us -> 116 us
  waiting for transfers between devices: 71.9 us -> 59.8 us
  starting transfers between devices: 28.2 us -> 39.7 us
    ppermute x6 -> x9, waiting for transfers between devices: 30.6 us -> 23.1 us  [turned(): lax.ppermute(block, axis, [(i, (i + distance) % size) for i in range(size)])]
    ppermute x2 -> x3, waiting for transfers between devices: 6.72 us -> 0.01 us  [sent_along(): return lax.ppermute(slabs, ('blk', 'sub'), route)]
    ppermute x6 -> x9, starting transfers between devices: 6.76 us -> 12.6 us  [turned(): lax.ppermute(block, axis, [(i, (i + distance) % size) for i in range(size)])]
    ppermute x17 -> x22, starting transfers between devices: 20.6 us -> 24.2 us  [swapped(): return lax.ppermute(block, axis, [(0, 1), (1, 0)])]
    ppermute x2 -> x3, starting transfers between devices: 0.77 us -> 2.87 us  [sent_along(): return lax.ppermute(slabs, ('blk', 'sub'), route)]
    ppermute x17 -> x22, waiting for transfers between devices: 34.6 us -> 36.6 us  [swapped(): return lax.ppermute(block, axis, [(0, 1), (1, 0)])]
    pallas_call x3 -> x6, Pallas kernels: 8.99 us -> 9.89 us  [the longest x2 6.69 us: attention(): pl.pallas_call(functools.partial(attention_kernel, head, distances), in_s...]
  transfers between devices with their start and end apart: 25 -> 34, of which waited for: 19 -> 20; matrix products, arithmetic and copies ran while one was open for 2% -> 2% of each run, Pallas kernels for 8% -> 9%
where the time goes in v14:
time: 116 us
  waiting for transfers between devices  59.8 us (52%)
  starting transfers between devices  39.7 us (34%)
  Pallas kernels  11.9 us (10%)
  other arithmetic  2.4 us (2%)
  local copies, waits for them, and re-layouts  1.3 us (1%)
    ppermute x22, waiting for transfers between devices, swapped(): return lax.ppermute(block, axis, [(0, 1), (1, 0)])  36.6 us
    ppermute x22, starting transfers between devices, swapped(): return lax.ppermute(block, axis, [(0, 1), (1, 0)])  24.2 us
    ppermute x9, waiting for transfers between devices, turned(): lax.ppermute(block, axis, [(i, (i + distance) % size) for i in range(size)])  23.1 us
    ppermute x9, starting transfers between devices, turned(): lax.ppermute(block, axis, [(i, (i + distance) % size) for i in range(size)])  12.6 us
    pallas_call x2, Pallas kernels, attention(): pl.pallas_call(functools.partial(attention_kernel, head, distances), in_s...  6.69 us
    pallas_call x4, Pallas kernels, gradient(): pl.pallas_call(kernel, in_specs=[IN_VMEM] * len(operands), out_specs=[IN_...  3.2 us
    ppermute x3, starting transfers between devices, sent_along(): return lax.ppermute(slabs, ('blk', 'sub'), route)  2.87 us
  transfers between devices with their start and end apart: 34, of which 20 were waited for; matrix products, arithmetic and copies ran while one was open for 2% of the time, Pallas kernels for 9%

profile of v14, /device:TPU:0, one launch (start us, length us, event | category | flops | bytes accessed | tf_op | source)
XLA Modules:
  0.0 115.9 jit_solution(10172609372254857125)
XLA Ops:
  1.8 3.1 %collective-permute-start = (bf16[640,256]{1,0:T(8,128)(2,1)S(1)}, bf16[640,256]{1,0:T(8,128)(2,1)S(1)}, u32[]{:S(2)}, u32[]{:S(2)}) collective-permute-start(bf16[640,256]{1,0:T(8,128)(2,1)S(1)} %dynamic-slice_bitcast_fusion), channel_id=1, source_target_pairs={{0,4},{4,8},{8,12},{12,0},{1,5},{5,9},{9,13},{13,1},{2,6},{6,10},{... | collective-permute-start | bytes 983048 | tf_op jit(solution)/shard_map/ppermute | solution.py:315
  4.8 1.7 %multiply_reduce_fusion = f32[256]{0:T(256)S(1)} fusion(bf16[256,2560]{1,0:T(8,128)(2,1)} %values_ref.1), kind=kLoop, calls=%fused_computation | loop fusion | flops 1965824 | bytes 1311744 | tf_op jit(solution)/shard_map/reduce_sum | solution.py:350
  8.8 5.8 %collective-permute-done.kept_ref.refs_0_ = bf16[640,256]{1,0:T(8,128)(2,1)S(1)} collective-permute-done((bf16[640,256]{1,0:T(8,128)(2,1)S(1)}, bf16[640,256]{1,0:T(8,128)(2,1)S(1)}, u32[]{:S(2)}, u32[]{:S(2)}) %collective-permute-start) | collective-permute-done | bytes 327712 | tf_op jit(solution)/shard_map/ppermute | solution.py:315
  14.6 1.5 %collective-permute-start.2 = (bf16[640,256]{1,0:T(8,128)(2,1)S(1)}, bf16[640,256]{1,0:T(8,128)(2,1)S(1)}, u32[]{:S(2)}, u32[]{:S(2)}) collective-permute-start(bf16[640,256]{1,0:T(8,128)(2,1)S(1)} %collective-permute-done.kept_ref.refs_0_), channel_id=1, source_target_pairs={{0,2},{2,0},{1,3},{3,1},{4,6},{6,4},{5,7},{7,5},{8,10},{10,8},{9,1... | collective-permute-start | bytes 983048 | tf_op jit(solution)/shard_map/ppermute | solution.py:310
  16.1 1.5 %collective-permute-start.3 = (bf16[640,256]{1,0:T(8,128)(2,1)S(1)}, bf16[640,256]{1,0:T(8,128)(2,1)S(1)}, u32[]{:S(2)}, u32[]{:S(2)}) collective-permute-start(bf16[640,256]{1,0:T(8,128)(2,1)S(1)} %collective-permute-done.kept_ref.refs_0_), channel_id=1, source_target_pairs={{0,16},{16,0},{1,17},{17,1},{2,18},{18,2},{3,19},{19,3},{4,20},{20... | collective-permute-start | bytes 983048 | tf_op jit(solution)/shard_map/ppermute | solution.py:310
  17.6 1.7 %collective-permute-start.4 = (bf16[640,256]{1,0:T(8,128)(2,1)S(1)}, bf16[640,256]{1,0:T(8,128)(2,1)S(1)}, u32[]{:S(2)}, u32[]{:S(2)}) collective-permute-start(bf16[640,256]{1,0:T(8,128)(2,1)S(1)} %dynamic-slice_bitcast_fusion), channel_id=1, source_target_pairs={{0,12},{4,0},{8,4},{12,8},{1,13},{5,1},{9,5},{13,9},{2,14},{6,2},{... | collective-permute-start | bytes 983048 | tf_op jit(solution)/shard_map/ppermute | solution.py:315
  19.3 5.4 %collective-permute-done.2.arrived_ref.refs_1_ = bf16[640,256]{1,0:T(8,128)(2,1)S(1)} collective-permute-done((bf16[640,256]{1,0:T(8,128)(2,1)S(1)}, bf16[640,256]{1,0:T(8,128)(2,1)S(1)}, u32[]{:S(2)}, u32[]{:S(2)}) %collective-permute-start.2) | collective-permute-done | bytes 327712 | tf_op jit(solution)/shard_map/ppermute | solution.py:310
  24.7 1.2 %collective-permute-done.3.refs_2_ = bf16[640,256]{1,0:T(8,128)(2,1)S(1)} collective-permute-done((bf16[640,256]{1,0:T(8,128)(2,1)S(1)}, bf16[640,256]{1,0:T(8,128)(2,1)S(1)}, u32[]{:S(2)}, u32[]{:S(2)}) %collective-permute-start.3) | collective-permute-done | bytes 327712 | tf_op jit(solution)/shard_map/ppermute | solution.py:310
  25.9 1.2 %collective-permute-done.4.refs_0_ = bf16[640,256]{1,0:T(8,128)(2,1)S(1)} collective-permute-done((bf16[640,256]{1,0:T(8,128)(2,1)S(1)}, bf16[640,256]{1,0:T(8,128)(2,1)S(1)}, u32[]{:S(2)}, u32[]{:S(2)}) %collective-permute-start.4) | collective-permute-done | bytes 327712 | tf_op jit(solution)/shard_map/ppermute | solution.py:315
  28.4 1.5 %collective-permute-start.9 = (bf16[640,256]{1,0:T(8,128)(2,1)S(1)}, bf16[640,256]{1,0:T(8,128)(2,1)S(1)}, u32[]{:S(2)}, u32[]{:S(2)}) collective-permute-start(bf16[640,256]{1,0:T(8,128)(2,1)S(1)} %collective-permute-done.2.arrived_ref.refs_1_), channel_id=1, source_target_pairs={{0,16},{16,0},{1,17},{17,1},{2,18},{18,2},{3,19},{19,3},{4,20},{20... | collective-permute-start | bytes 983048 | tf_op jit(solution)/shard_map/ppermute | solution.py:310
  29.9 1.5 %collective-permute-start.10 = (bf16[640,256]{1,0:T(8,128)(2,1)S(1)}, bf16[640,256]{1,0:T(8,128)(2,1)S(1)}, u32[]{:S(2)}, u32[]{:S(2)}) collective-permute-start(bf16[640,256]{1,0:T(8,128)(2,1)S(1)} %get-tuple-element.89), channel_id=1, source_target_pairs={{0,2},{2,0},{1,3},{3,1},{4,6},{6,4},{5,7},{7,5},{8,10},{10,8},{9,1... | collective-permute-start | bytes 983048 | tf_op jit(solution)/shard_map/ppermute | solution.py:310
  31.4 6.6 %collective-permute-done.7.refs_1_ = bf16[640,256]{1,0:T(8,128)(2,1)S(1)} collective-permute-done((bf16[640,256]{1,0:T(8,128)(2,1)S(1)}, bf16[640,256]{1,0:T(8,128)(2,1)S(1)}, u32[]{:S(2)}, u32[]{:S(2)}) %collective-permute-start.7) | collective-permute-done | bytes 327712 | tf_op jit(solution)/shard_map/ppermute | solution.py:310
  38.5 4.8 %collective-permute-done.9.refs_3_ = bf16[640,256]{1,0:T(8,128)(2,1)S(1)} collective-permute-done((bf16[640,256]{1,0:T(8,128)(2,1)S(1)}, bf16[640,256]{1,0:T(8,128)(2,1)S(1)}, u32[]{:S(2)}, u32[]{:S(2)}) %collective-permute-start.9) | collective-permute-done | bytes 327712 | tf_op jit(solution)/shard_map/ppermute | solution.py:310
  43.3 1.5 %collective-permute-done.6.refs_4_ = bf16[2,640,256]{2,1,0:T(8,128)(2,1)S(1)} collective-permute-done((bf16[2,640,256]{2,1,0:T(8,128)(2,1)S(1)}, bf16[2,640,256]{2,1,0:T(8,128)(2,1)S(1)}, u32[]{:S(2)}, u32[]{:S(2)}) %collective-permute-start.6) | collective-permute-done | bytes 655392 | tf_op jit(solution)/shard_map/ppermute | solution.py:315
  50.1 4.2 %collective-permute-done.12.refs_3_ = bf16[640,256]{1,0:T(8,128)(2,1)S(1)} collective-permute-done((bf16[640,256]{1,0:T(8,128)(2,1)S(1)}, bf16[640,256]{1,0:T(8,128)(2,1)S(1)}, u32[]{:S(2)}, u32[]{:S(2)}) %collective-permute-start.12) | collective-permute-done | bytes 327712 | tf_op jit(solution)/shard_map/ppermute | solution.py:310
  54.3 7.0 %collective-permute-done.13 = bf16[640,256]{1,0:T(8,128)(2,1)S(1)} collective-permute-done((bf16[640,256]{1,0:T(8,128)(2,1)S(1)}, bf16[640,256]{1,0:T(8,128)(2,1)S(1)}, u32[]{:S(2)}, u32[]{:S(2)}) %collective-permute-start.13) | collective-permute-done | bytes 327712 | tf_op jit(solution)/shard_map/ppermute | solution.py:310
  61.3 2.9 %attention.2 = (bf16[256,640]{1,0:T(8,128)(2,1)S(1)}, bf16[256,256]{1,0:T(8,128)(2,1)S(1)}) custom-call(bf16[256,2560]{1,0:T(8,128)(2,1)S(1)} %get-tuple-element.80.own_ref, bf16[256,2560]{1,0:T(8,128)(2,1)S(1)} %collective-permute-done.5.other_ref, bf16[640,256]{1,0:T(8,128)(2,1)S(1)} %collective-permute-done.4.refs_0_, ...), custom_call_target="tpu_custom_call" | custom-call | flops 419430400 | bytes 4000000 | tf_op jit(solution)/shard_map/attention/pallas_call | solution.py:182
  64.3 3.5 %collective-permute-start.27 = (bf16[256,256]{1,0:T(8,128)(2,1)S(1)}, bf16[256,256]{1,0:T(8,128)(2,1)S(1)}, u32[]{:S(2)}, u32[]{:S(2)}) collective-permute-start(bf16[256,256]{1,0:T(8,128)(2,1)S(1)} %get-tuple-element.139.refs_0_), channel_id=1, source_target_pairs={{0,4},{4,8},{8,12},{12,0},{1,5},{5,9},{9,13},{13,1},{2,6},{6,10},{... | collective-permute-start | bytes 393224 | tf_op jit(solution)/shard_map/ppermute | solution.py:315
  67.8 5.6 %collective-permute-start.22 = (bf16[2,640,256]{2,1,0:T(8,128)(2,1)S(1)}, bf16[2,640,256]{2,1,0:T(8,128)(2,1)S(1)}, u32[]{:S(2)}, u32[]{:S(2)}) collective-permute-start(bf16[2,640,256]{2,1,0:T(8,128)(2,1)S(1)} %collective-permute-done.14.refs_6_.refs_2_), channel_id=1, source_target_pairs={{0,1},{1,0},{2,3},{3,2},{4,5},{5,4},{6,7},{7,6},{8,9},{9,8},{10,11... | collective-permute-start | bytes 1966088 | tf_op jit(solution)/shard_map/ppermute | solution.py:310
  73.4 2.1 %collective-permute-start.25 = (bf16[640,256]{1,0:T(8,128)(2,1)S(1)}, bf16[640,256]{1,0:T(8,128)(2,1)S(1)}, u32[]{:S(2)}, u32[]{:S(2)}) collective-permute-start(bf16[640,256]{1,0:T(8,128)(2,1)S(1)} %collective-permute-done.13), channel_id=1, source_target_pairs={{0,4},{1,12},{4,0},{5,8},{8,5},{9,13},{12,1},{13,9},{2,6},{3,14},{... | collective-permute-start | bytes 983048 | tf_op jit(solution)/shard_map/ppermute | solution.py:343
  75.5 3.7 %attention.3 = (bf16[256,1280]{1,0:T(8,128)(2,1)}, bf16[256,256]{1,0:T(8,128)(2,1)S(1)}) custom-call(bf16[256,2560]{1,0:T(8,128)(2,1)S(1)} %get-tuple-element.80.own_ref, bf16[256,2560]{1,0:T(8,128)(2,1)S(1)} %collective-permute-done.5.other_ref, bf16[640,256]{1,0:T(8,128)(2,1)S(1)} %collective-permute-done.4.refs_0_, ...), custom_call_target="tpu_custom_call" | custom-call | flops 419430400 | bytes 4000000 | tf_op jit(solution)/shard_map/attention/pallas_call | solution.py:182
  80.1 3.6 %collective-permute-start.29 = (bf16[256,256]{1,0:T(8,128)(2,1)S(1)}, bf16[256,256]{1,0:T(8,128)(2,1)S(1)}, u32[]{:S(2)}, u32[]{:S(2)}) collective-permute-start(bf16[256,256]{1,0:T(8,128)(2,1)S(1)} %get-tuple-element.139.refs_0_), channel_id=1, source_target_pairs={{0,12},{4,0},{8,4},{12,8},{1,13},{5,1},{9,5},{13,9},{2,14},{6,2},{... | collective-permute-start | bytes 393224 | tf_op jit(solution)/shard_map/ppermute | solution.py:315
  83.7 4.5 %collective-permute-done.15.refs_2_ = bf16[256,256]{1,0:T(8,128)(2,1)S(1)} collective-permute-done((bf16[256,256]{1,0:T(8,128)(2,1)S(1)}, bf16[256,256]{1,0:T(8,128)(2,1)S(1)}, u32[]{:S(2)}, u32[]{:S(2)}) %collective-permute-start.15) | collective-permute-done | bytes 131104 | tf_op jit(solution)/shard_map/ppermute | solution.py:315
  89.7 1.3 %collective-permute-done.29.refs_4_ = bf16[256,256]{1,0:T(8,128)(2,1)S(1)} collective-permute-done((bf16[256,256]{1,0:T(8,128)(2,1)S(1)}, bf16[256,256]{1,0:T(8,128)(2,1)S(1)}, u32[]{:S(2)}, u32[]{:S(2)}) %collective-permute-start.29) | collective-permute-done | bytes 131104 | tf_op jit(solution)/shard_map/ppermute | solution.py:315
  90.9 1.4 %collective-permute-start.18 = (bf16[256,256]{1,0:T(8,128)(2,1)S(1)}, bf16[256,256]{1,0:T(8,128)(2,1)S(1)}, u32[]{:S(2)}, u32[]{:S(2)}) collective-permute-start(bf16[256,256]{1,0:T(8,128)(2,1)S(1)} %collective-permute-done.15.refs_2_), channel_id=1, source_target_pairs={{0,2},{2,0},{1,3},{3,1},{4,6},{6,4},{5,7},{7,5},{8,10},{10,8},{9,1... | collective-permute-start | bytes 393224 | tf_op jit(solution)/shard_map/ppermute | solution.py:310
  92.4 2.2 %collective-permute-done.30.refs_3_ = bf16[256,256]{1,0:T(8,128)(2,1)S(1)} collective-permute-done((bf16[256,256]{1,0:T(8,128)(2,1)S(1)}, bf16[256,256]{1,0:T(8,128)(2,1)S(1)}, u32[]{:S(2)}, u32[]{:S(2)}) %collective-permute-start.30) | collective-permute-done | bytes 131104 | tf_op jit(solution)/shard_map/ppermute | solution.py:310
  96.5 1.4 %collective-permute-start.32 = (bf16[256,256]{1,0:T(8,128)(2,1)S(1)}, bf16[256,256]{1,0:T(8,128)(2,1)S(1)}, u32[]{:S(2)}, u32[]{:S(2)}) collective-permute-start(bf16[256,256]{1,0:T(8,128)(2,1)S(1)} %collective-permute-done.29.refs_4_), channel_id=1, source_target_pairs={{0,2},{2,0},{1,3},{3,1},{4,6},{6,4},{5,7},{7,5},{8,10},{10,8},{9,1... | collective-permute-start | bytes 393224 | tf_op jit(solution)/shard_map/ppermute | solution.py:310
  97.9 3.5 %collective-permute-done.31.refs_0_ = bf16[256,256]{1,0:T(8,128)(2,1)S(1)} collective-permute-done((bf16[256,256]{1,0:T(8,128)(2,1)S(1)}, bf16[256,256]{1,0:T(8,128)(2,1)S(1)}, u32[]{:S(2)}, u32[]{:S(2)}) %collective-permute-start.31) | collective-permute-done | bytes 131104 | tf_op jit(solution)/shard_map/ppermute | solution.py:315
  101.4 1.4 %collective-permute-start.20 = (bf16[256,256]{1,0:T(8,128)(2,1)S(1)}, bf16[256,256]{1,0:T(8,128)(2,1)S(1)}, u32[]{:S(2)}, u32[]{:S(2)}) collective-permute-start(bf16[256,256]{1,0:T(8,128)(2,1)S(1)} %collective-permute-done.17.refs_4_), channel_id=1, source_target_pairs={{0,2},{2,0},{1,3},{3,1},{4,6},{6,4},{5,7},{7,5},{8,10},{10,8},{9,1... | collective-permute-start | bytes 393224 | tf_op jit(solution)/shard_map/ppermute | solution.py:310
  102.8 5.3 %collective-permute-done.19.refs_0_ = bf16[256,256]{1,0:T(8,128)(2,1)S(1)} collective-permute-done((bf16[256,256]{1,0:T(8,128)(2,1)S(1)}, bf16[256,256]{1,0:T(8,128)(2,1)S(1)}, u32[]{:S(2)}, u32[]{:S(2)}) %collective-permute-start.19) | collective-permute-done | bytes 131104 | tf_op jit(solution)/shard_map/ppermute | solution.py:315
  110.9 2.2 %collective-permute-done.33.refs_1_ = bf16[256,256]{1,0:T(8,128)(2,1)S(1)} collective-permute-done((bf16[256,256]{1,0:T(8,128)(2,1)S(1)}, bf16[256,256]{1,0:T(8,128)(2,1)S(1)}, u32[]{:S(2)}, u32[]{:S(2)}) %collective-permute-start.33) | collective-permute-done | bytes 131104 | tf_op jit(solution)/shard_map/ppermute | solution.py:310
  114.5 1.4 %gradient.7 = (f32[2,640,256]{2,1,0:T(8,128)}, f32[2,256]{1,0:T(2,128)}) custom-call(bf16[256,256]{1,0:T(8,128)(2,1)S(1)} %collective-permute-done.19.refs_0_, bf16[256,256]{1,0:T(8,128)(2,1)S(1)} %collective-permute-done.21.refs_1_, bf16[2,640,256]{2,1,0:T(8,128)(2,1)S(1)} %collective-permute-done.14.refs_6_.refs_2_, ...), custom_call_target="tpu_custom_call" | custom-call | flops 167772160 | bytes 2000000 | tf_op jit(solution)/shard_map/gradient/pallas_call | solution.py:246
  (69 shorter events, 18.6 us)
Async XLA Ops:
  1.8 12.8 %collective-permute-start = (bf16[640,256]{1,0:T(8,128)(2,1)S(1)}, bf16[640,256]{1,0:T(8,128)(2,1)S(1)}, u32[]{:S(2)}, u32[]{:S(2)}) collective-permute-start(bf16[640,256]{1,0:T(8,128)(2,1)S(1)} %dynamic-slice_bitcast_fusion), channel_id=1, source_target_pairs={{0,4},{4,8},{8,12},{12,0},{1,5},{5,9},{9,13},{13,1},{2,6},{6,10},{... | collective-permute-start | bytes 983048 | tf_op jit(solution)/shard_map/ppermute | solution.py:315
  14.6 12.6 %collective-permute-start.5 = (bf16[256,2560]{1,0:T(8,128)(2,1)S(1)}, bf16[256,2560]{1,0:T(8,128)(2,1)S(1)}, u32[]{:S(2)}, u32[]{:S(2)}) collective-permute-start(bf16[256,2560]{1,0:T(8,128)(2,1)S(1)} %get-tuple-element.80.own_ref), channel_id=1, source_target_pairs={{0,1},{1,0},{2,3},{3,2},{4,5},{5,4},{6,7},{7,6},{8,9},{9,8},{10,11... | collective-permute-start | bytes 3932168 | tf_op jit(solution)/shard_map/ppermute | solution.py:310
  14.6 10.1 %collective-permute-start.2 = (bf16[640,256]{1,0:T(8,128)(2,1)S(1)}, bf16[640,256]{1,0:T(8,128)(2,1)S(1)}, u32[]{:S(2)}, u32[]{:S(2)}) collective-permute-start(bf16[640,256]{1,0:T(8,128)(2,1)S(1)} %collective-permute-done.kept_ref.refs_0_), channel_id=1, source_target_pairs={{0,2},{2,0},{1,3},{3,1},{4,6},{6,4},{5,7},{7,5},{8,10},{10,8},{9,1... | collective-permute-start | bytes 983048 | tf_op jit(solution)/shard_map/ppermute | solution.py:310
  16.1 9.8 %collective-permute-start.3 = (bf16[640,256]{1,0:T(8,128)(2,1)S(1)}, bf16[640,256]{1,0:T(8,128)(2,1)S(1)}, u32[]{:S(2)}, u32[]{:S(2)}) collective-permute-start(bf16[640,256]{1,0:T(8,128)(2,1)S(1)} %collective-permute-done.kept_ref.refs_0_), channel_id=1, source_target_pairs={{0,16},{16,0},{1,17},{17,1},{2,18},{18,2},{3,19},{19,3},{4,20},{20... | collective-permute-start | bytes 983048 | tf_op jit(solution)/shard_map/ppermute | solution.py:310
  17.6 9.6 %collective-permute-start.4 = (bf16[640,256]{1,0:T(8,128)(2,1)S(1)}, bf16[640,256]{1,0:T(8,128)(2,1)S(1)}, u32[]{:S(2)}, u32[]{:S(2)}) collective-permute-start(bf16[640,256]{1,0:T(8,128)(2,1)S(1)} %dynamic-slice_bitcast_fusion), channel_id=1, source_target_pairs={{0,12},{4,0},{8,4},{12,8},{1,13},{5,1},{9,5},{13,9},{2,14},{6,2},{... | collective-permute-start | bytes 983048 | tf_op jit(solution)/shard_map/ppermute | solution.py:315
  27.2 17.6 %collective-permute-start.6 = (bf16[2,640,256]{2,1,0:T(8,128)(2,1)S(1)}, bf16[2,640,256]{2,1,0:T(8,128)(2,1)S(1)}, u32[]{:S(2)}, u32[]{:S(2)}) collective-permute-start(bf16[2,640,256]{2,1,0:T(8,128)(2,1)S(1)} %pack.2), channel_id=1, source_target_pairs={{0,4},{4,8},{8,12},{12,0},{1,5},{5,9},{9,13},{13,1},{2,6},{6,10},{... | collective-permute-start | bytes 1966088 | tf_op jit(solution)/shard_map/ppermute | solution.py:315
  27.3 10.7 %collective-permute-start.7 = (bf16[640,256]{1,0:T(8,128)(2,1)S(1)}, bf16[640,256]{1,0:T(8,128)(2,1)S(1)}, u32[]{:S(2)}, u32[]{:S(2)}) collective-permute-start(bf16[640,256]{1,0:T(8,128)(2,1)S(1)} %collective-permute-done.4.refs_0_), channel_id=1, source_target_pairs={{0,2},{2,0},{1,3},{3,1},{4,6},{6,4},{5,7},{7,5},{8,10},{10,8},{9,1... | collective-permute-start | bytes 983048 | tf_op jit(solution)/shard_map/ppermute | solution.py:310
  27.9 10.6 %collective-permute-start.8 = (bf16[640,256]{1,0:T(8,128)(2,1)S(1)}, bf16[640,256]{1,0:T(8,128)(2,1)S(1)}, u32[]{:S(2)}, u32[]{:S(2)}) collective-permute-start(bf16[640,256]{1,0:T(8,128)(2,1)S(1)} %collective-permute-done.4.refs_0_), channel_id=1, source_target_pairs={{0,16},{16,0},{1,17},{17,1},{2,18},{18,2},{3,19},{19,3},{4,20},{20... | collective-permute-start | bytes 983048 | tf_op jit(solution)/shard_map/ppermute | solution.py:310
  28.4 14.9 %collective-permute-start.9 = (bf16[640,256]{1,0:T(8,128)(2,1)S(1)}, bf16[640,256]{1,0:T(8,128)(2,1)S(1)}, u32[]{:S(2)}, u32[]{:S(2)}) collective-permute-start(bf16[640,256]{1,0:T(8,128)(2,1)S(1)} %collective-permute-done.2.arrived_ref.refs_1_), channel_id=1, source_target_pairs={{0,16},{16,0},{1,17},{17,1},{2,18},{18,2},{3,19},{19,3},{4,20},{20... | collective-permute-start | bytes 983048 | tf_op jit(solution)/shard_map/ppermute | solution.py:310
  29.9 13.4 %collective-permute-start.10 = (bf16[640,256]{1,0:T(8,128)(2,1)S(1)}, bf16[640,256]{1,0:T(8,128)(2,1)S(1)}, u32[]{:S(2)}, u32[]{:S(2)}) collective-permute-start(bf16[640,256]{1,0:T(8,128)(2,1)S(1)} %get-tuple-element.89), channel_id=1, source_target_pairs={{0,2},{2,0},{1,3},{3,1},{4,6},{6,4},{5,7},{7,5},{8,10},{10,8},{9,1... | collective-permute-start | bytes 983048 | tf_op jit(solution)/shard_map/ppermute | solution.py:310
  44.8 16.5 %collective-permute-start.11 = (bf16[2,640,256]{2,1,0:T(8,128)(2,1)S(1)}, bf16[2,640,256]{2,1,0:T(8,128)(2,1)S(1)}, u32[]{:S(2)}, u32[]{:S(2)}) collective-permute-start(bf16[2,640,256]{2,1,0:T(8,128)(2,1)S(1)} %collective-permute-done.6.refs_4_), channel_id=1, source_target_pairs={{0,16},{16,0},{1,17},{17,1},{2,18},{18,2},{3,19},{19,3},{4,20},{20... | collective-permute-start | bytes 1966088 | tf_op jit(solution)/shard_map/ppermute | solution.py:310
  45.4 15.9 %collective-permute-start.14 = (bf16[2,640,256]{2,1,0:T(8,128)(2,1)S(1)}, bf16[2,640,256]{2,1,0:T(8,128)(2,1)S(1)}, u32[]{:S(2)}, u32[]{:S(2)}) collective-permute-start(bf16[2,640,256]{2,1,0:T(8,128)(2,1)S(1)} %pack.3), channel_id=1, source_target_pairs={{0,0},{1,8},{4,4},{5,12},{8,1},{9,9},{12,5},{13,13},{2,2},{3,10},{... | collective-permute-start | bytes 1966088 | tf_op jit(solution)/shard_map/ppermute | solution.py:343
  46.2 18.1 %collective-permute-start.23 = (bf16[640,256]{1,0:T(8,128)(2,1)S(1)}, bf16[640,256]{1,0:T(8,128)(2,1)S(1)}, u32[]{:S(2)}, u32[]{:S(2)}) collective-permute-start(bf16[640,256]{1,0:T(8,128)(2,1)S(1)} %get-tuple-element.124), channel_id=1, source_target_pairs={{0,4},{1,12},{4,0},{5,8},{8,5},{9,13},{12,1},{13,9},{2,6},{3,14},{... | collective-permute-start | bytes 983048 | tf_op jit(solution)/shard_map/ppermute | solution.py:343
  46.2 8.0 %collective-permute-start.12 = (bf16[640,256]{1,0:T(8,128)(2,1)S(1)}, bf16[640,256]{1,0:T(8,128)(2,1)S(1)}, u32[]{:S(2)}, u32[]{:S(2)}) collective-permute-start(bf16[640,256]{1,0:T(8,128)(2,1)S(1)} %collective-permute-done.8.refs_2_), channel_id=1, source_target_pairs={{0,2},{2,0},{1,3},{3,1},{4,6},{6,4},{5,7},{7,5},{8,10},{10,8},{9,1... | collective-permute-start | bytes 983048 | tf_op jit(solution)/shard_map/ppermute | solution.py:310
  47.2 14.1 %collective-permute-start.13 = (bf16[640,256]{1,0:T(8,128)(2,1)S(1)}, bf16[640,256]{1,0:T(8,128)(2,1)S(1)}, u32[]{:S(2)}, u32[]{:S(2)}) collective-permute-start(bf16[640,256]{1,0:T(8,128)(2,1)S(1)} %get-tuple-element.94), channel_id=1, source_target_pairs={{0,2},{2,0},{1,3},{3,1},{4,6},{6,4},{5,7},{7,5},{8,10},{10,8},{9,1... | collective-permute-start | bytes 983048 | tf_op jit(solution)/shard_map/ppermute | solution.py:310
  64.3 15.0 %collective-permute-start.27 = (bf16[256,256]{1,0:T(8,128)(2,1)S(1)}, bf16[256,256]{1,0:T(8,128)(2,1)S(1)}, u32[]{:S(2)}, u32[]{:S(2)}) collective-permute-start(bf16[256,256]{1,0:T(8,128)(2,1)S(1)} %get-tuple-element.139.refs_0_), channel_id=1, source_target_pairs={{0,4},{4,8},{8,12},{12,0},{1,5},{5,9},{9,13},{13,1},{2,6},{6,10},{... | collective-permute-start | bytes 393224 | tf_op jit(solution)/shard_map/ppermute | solution.py:315
  67.8 12.3 %collective-permute-start.28 = (bf16[256,256]{1,0:T(8,128)(2,1)S(1)}, bf16[256,256]{1,0:T(8,128)(2,1)S(1)}, u32[]{:S(2)}, u32[]{:S(2)}) collective-permute-start(bf16[256,256]{1,0:T(8,128)(2,1)S(1)} %get-tuple-element.139.refs_0_), channel_id=1, source_target_pairs={{0,2},{2,0},{1,3},{3,1},{4,6},{6,4},{5,7},{7,5},{8,10},{10,8},{9,1... | collective-permute-start | bytes 393224 | tf_op jit(solution)/shard_map/ppermute | solution.py:310
  67.8 42.4 %collective-permute-start.22 = (bf16[2,640,256]{2,1,0:T(8,128)(2,1)S(1)}, bf16[2,640,256]{2,1,0:T(8,128)(2,1)S(1)}, u32[]{:S(2)}, u32[]{:S(2)}) collective-permute-start(bf16[2,640,256]{2,1,0:T(8,128)(2,1)S(1)} %collective-permute-done.14.refs_6_.refs_2_), channel_id=1, source_target_pairs={{0,1},{1,0},{2,3},{3,2},{4,5},{5,4},{6,7},{7,6},{8,9},{9,8},{10,11... | collective-permute-start | bytes 1966088 | tf_op jit(solution)/shard_map/ppermute | solution.py:310
  73.4 21.5 %collective-permute-start.25 = (bf16[640,256]{1,0:T(8,128)(2,1)S(1)}, bf16[640,256]{1,0:T(8,128)(2,1)S(1)}, u32[]{:S(2)}, u32[]{:S(2)}) collective-permute-start(bf16[640,256]{1,0:T(8,128)(2,1)S(1)} %collective-permute-done.13), channel_id=1, source_target_pairs={{0,4},{1,12},{4,0},{5,8},{8,5},{9,13},{12,1},{13,9},{2,6},{3,14},{... | collective-permute-start | bytes 983048 | tf_op jit(solution)/shard_map/ppermute | solution.py:343
  79.2 9.0 %collective-permute-start.15 = (bf16[256,256]{1,0:T(8,128)(2,1)S(1)}, bf16[256,256]{1,0:T(8,128)(2,1)S(1)}, u32[]{:S(2)}, u32[]{:S(2)}) collective-permute-start(bf16[256,256]{1,0:T(8,128)(2,1)S(1)} %get-tuple-element.117.refs_0_), channel_id=1, source_target_pairs={{0,4},{4,8},{8,12},{12,0},{1,5},{5,9},{9,13},{13,1},{2,6},{6,10},{... | collective-permute-start | bytes 393224 | tf_op jit(solution)/shard_map/ppermute | solution.py:315
  79.3 10.1 %collective-permute-start.16 = (bf16[256,256]{1,0:T(8,128)(2,1)S(1)}, bf16[256,256]{1,0:T(8,128)(2,1)S(1)}, u32[]{:S(2)}, u32[]{:S(2)}) collective-permute-start(bf16[256,256]{1,0:T(8,128)(2,1)S(1)} %get-tuple-element.117.refs_0_), channel_id=1, source_target_pairs={{0,2},{2,0},{1,3},{3,1},{4,6},{6,4},{5,7},{7,5},{8,10},{10,8},{9,1... | collective-permute-start | bytes 393224 | tf_op jit(solution)/shard_map/ppermute | solution.py:310
  80.1 10.9 %collective-permute-start.29 = (bf16[256,256]{1,0:T(8,128)(2,1)S(1)}, bf16[256,256]{1,0:T(8,128)(2,1)S(1)}, u32[]{:S(2)}, u32[]{:S(2)}) collective-permute-start(bf16[256,256]{1,0:T(8,128)(2,1)S(1)} %get-tuple-element.139.refs_0_), channel_id=1, source_target_pairs={{0,12},{4,0},{8,4},{12,8},{1,13},{5,1},{9,5},{13,9},{2,14},{6,2},{... | collective-permute-start | bytes 393224 | tf_op jit(solution)/shard_map/ppermute | solution.py:315
  88.2 6.4 %collective-permute-start.30 = (bf16[256,256]{1,0:T(8,128)(2,1)S(1)}, bf16[256,256]{1,0:T(8,128)(2,1)S(1)}, u32[]{:S(2)}, u32[]{:S(2)}) collective-permute-start(bf16[256,256]{1,0:T(8,128)(2,1)S(1)} %collective-permute-done.27.refs_2_), channel_id=1, source_target_pairs={{0,2},{2,0},{1,3},{3,1},{4,6},{6,4},{5,7},{7,5},{8,10},{10,8},{9,1... | collective-permute-start | bytes 393224 | tf_op jit(solution)/shard_map/ppermute | solution.py:310
  89.4 5.5 %collective-permute-start.17 = (bf16[256,256]{1,0:T(8,128)(2,1)S(1)}, bf16[256,256]{1,0:T(8,128)(2,1)S(1)}, u32[]{:S(2)}, u32[]{:S(2)}) collective-permute-start(bf16[256,256]{1,0:T(8,128)(2,1)S(1)} %get-tuple-element.117.refs_0_), channel_id=1, source_target_pairs={{0,12},{4,0},{8,4},{12,8},{1,13},{5,1},{9,5},{13,9},{2,14},{6,2},{... | collective-permute-start | bytes 393224 | tf_op jit(solution)/shard_map/ppermute | solution.py:315
  90.9 5.5 %collective-permute-start.18 = (bf16[256,256]{1,0:T(8,128)(2,1)S(1)}, bf16[256,256]{1,0:T(8,128)(2,1)S(1)}, u32[]{:S(2)}, u32[]{:S(2)}) collective-permute-start(bf16[256,256]{1,0:T(8,128)(2,1)S(1)} %collective-permute-done.15.refs_2_), channel_id=1, source_target_pairs={{0,2},{2,0},{1,3},{3,1},{4,6},{6,4},{5,7},{7,5},{8,10},{10,8},{9,1... | collective-permute-start | bytes 393224 | tf_op jit(solution)/shard_map/ppermute | solution.py:310
  94.6 6.8 %collective-permute-start.31 = (bf16[256,256]{1,0:T(8,128)(2,1)S(1)}, bf16[256,256]{1,0:T(8,128)(2,1)S(1)}, u32[]{:S(2)}, u32[]{:S(2)}) collective-permute-start(bf16[256,256]{1,0:T(8,128)(2,1)S(1)} %collective-permute-done.27.refs_2_), channel_id=1, source_target_pairs={{0,4},{4,8},{8,12},{12,0},{1,5},{5,9},{9,13},{13,1},{2,6},{6,10},{... | collective-permute-start | bytes 393224 | tf_op jit(solution)/shard_map/ppermute | solution.py:315
  94.9 15.3 %collective-permute-start.24 = (bf16[640,256]{1,0:T(8,128)(2,1)S(1)}, bf16[640,256]{1,0:T(8,128)(2,1)S(1)}, u32[]{:S(2)}, u32[]{:S(2)}) collective-permute-start(bf16[640,256]{1,0:T(8,128)(2,1)S(1)} %collective-permute-done.23.refs_8_), channel_id=1, source_target_pairs={{0,1},{1,0},{2,3},{3,2},{4,5},{5,4},{6,7},{7,6},{8,9},{9,8},{10,11... | collective-permute-start | bytes 983048 | tf_op jit(solution)/shard_map/ppermute | solution.py:310
  94.9 15.2 %collective-permute-start.26 = (bf16[640,256]{1,0:T(8,128)(2,1)S(1)}, bf16[640,256]{1,0:T(8,128)(2,1)S(1)}, u32[]{:S(2)}, u32[]{:S(2)}) collective-permute-start(bf16[640,256]{1,0:T(8,128)(2,1)S(1)} %collective-permute-done.25.refs_10_), channel_id=1, source_target_pairs={{0,1},{1,0},{2,3},{3,2},{4,5},{5,4},{6,7},{7,6},{8,9},{9,8},{10,11... | collective-permute-start | bytes 983048 | tf_op jit(solution)/shard_map/ppermute | solution.py:310
  101.4 6.8 %collective-permute-start.19 = (bf16[256,256]{1,0:T(8,128)(2,1)S(1)}, bf16[256,256]{1,0:T(8,128)(2,1)S(1)}, u32[]{:S(2)}, u32[]{:S(2)}) collective-permute-start(bf16[256,256]{1,0:T(8,128)(2,1)S(1)} %collective-permute-done.15.refs_2_), channel_id=1, source_target_pairs={{0,4},{4,8},{8,12},{12,0},{1,5},{5,9},{9,13},{13,1},{2,6},{6,10},{... | collective-permute-start | bytes 393224 | tf_op jit(solution)/shard_map/ppermute | solution.py:315
  101.4 7.8 %collective-permute-start.20 = (bf16[256,256]{1,0:T(8,128)(2,1)S(1)}, bf16[256,256]{1,0:T(8,128)(2,1)S(1)}, u32[]{:S(2)}, u32[]{:S(2)}) collective-permute-start(bf16[256,256]{1,0:T(8,128)(2,1)S(1)} %collective-permute-done.17.refs_4_), channel_id=1, source_target_pairs={{0,2},{2,0},{1,3},{3,1},{4,6},{6,4},{5,7},{7,5},{8,10},{10,8},{9,1... | collective-permute-start | bytes 393224 | tf_op jit(solution)/shard_map/ppermute | solution.py:310
  108.1 5.0 %collective-permute-start.33 = (bf16[256,256]{1,0:T(8,128)(2,1)S(1)}, bf16[256,256]{1,0:T(8,128)(2,1)S(1)}, u32[]{:S(2)}, u32[]{:S(2)}) collective-permute-start(bf16[256,256]{1,0:T(8,128)(2,1)S(1)} %collective-permute-done.31.refs_0_), channel_id=1, source_target_pairs={{0,2},{2,0},{1,3},{3,1},{4,6},{6,4},{5,7},{7,5},{8,10},{10,8},{9,1... | collective-permute-start | bytes 393224 | tf_op jit(solution)/shard_map/ppermute | solution.py:310
  109.3 5.2 %collective-permute-start.21 = (bf16[256,256]{1,0:T(8,128)(2,1)S(1)}, bf16[256,256]{1,0:T(8,128)(2,1)S(1)}, u32[]{:S(2)}, u32[]{:S(2)}) collective-permute-start(bf16[256,256]{1,0:T(8,128)(2,1)S(1)} %collective-permute-done.19.refs_0_), channel_id=1, source_target_pairs={{0,2},{2,0},{1,3},{3,1},{4,6},{6,4},{5,7},{7,5},{8,10},{10,8},{9,1... | collective-permute-start | bytes 393224 | tf_op jit(solution)/shard_map/ppermute | solution.py:310
  (8 other events, 100.0 us)

commit v15 on v14

--- a/solution.py
+++ b/solution.py
@@ -411,20 +411,25 @@
         heads.append({(0, True): pair})
         before = (grad_query,)
 
-    heads[0][0, True], odd_same = lax.optimization_barrier((heads[0][0, True], odd_same))
+    heads[0][0, True], heads[1][0, True], odd_same, odd_mate = lax.optimization_barrier(
+        (heads[0][0, True], heads[1][0, True], odd_same, odd_mate)
+    )
     for head in heads:
         head[1, True], head[0, False] = (
             turned(head[0, True], "blk", 1),
             swapped(head[0, True], "dp"),
         )
         head.update(zip(head, lax.optimization_barrier(tuple(head.values()))))
-    even_other, odd_same_other = swapped(even, "sub"), swapped(odd_same, "sub")
     for head in heads:
         head[-1, True], head[1, False] = (
             turned(head[0, True], "blk", -1),
             swapped(head[1, True], "dp"),
         )
         head.update(zip(head, lax.optimization_barrier(tuple(head.values()))))
+    even, odd_same, odd_mate = (
+        after(slab, *(head[-1, True] for head in heads)) for slab in (even, odd_same, odd_mate)
+    )
+    even_other, odd_same_other = swapped(even, "sub"), swapped(odd_same, "sub")
     odd_mate_other = swapped(odd_mate, "sub")
     for head in heads:
         head[2, True], head[-1, False] = (

time: 116 us -> 121 us (1.043)
  waiting for transfers between devices: 59.8 us -> 68.8 us
  starting transfers between devices: 39.7 us -> 35.5 us
    ppermute x9, waiting for transfers between devices: 23.1 us -> 34.5 us  [turned(): lax.ppermute(block, axis, [(i, (i + distance) % size) for i in range(size)])]
    ppermute x22, starting transfers between devices: 24.2 us -> 17.5 us  [swapped(): return lax.ppermute(block, axis, [(0, 1), (1, 0)])]
    ppermute x9, starting transfers between devices: 12.6 us -> 17.2 us  [turned(): lax.ppermute(block, axis, [(i, (i + distance) % size) for i in range(size)])]
    ppermute x22, waiting for transfers between devices: 36.6 us -> 33.1 us  [swapped(): return lax.ppermute(block, axis, [(0, 1), (1, 0)])]
    ppermute x3, starting transfers between devices: 2.87 us -> 0.78 us  [sent_along(): return lax.ppermute(slabs, ('blk', 'sub'), route)]
  transfers between devices with their start and end apart: 34 -> 34, of which waited for: 20 -> 21; matrix products, arithmetic and copies ran while one was open for 2% -> 2% of each run, Pallas kernels for 9% -> 9%
where the time goes in v15:
time: 121 us
  waiting for transfers between devices  68.8 us (57%)
  starting transfers between devices  35.5 us (29%)
  Pallas kernels  11.9 us (10%)
  other arithmetic  2.5 us (2%)
    ppermute x9, waiting for transfers between devices, turned(): lax.ppermute(block, axis, [(i, (i + distance) % size) for i in range(size)])  34.5 us
    ppermute x22, waiting for transfers between devices, swapped(): return lax.ppermute(block, axis, [(0, 1), (1, 0)])  33.1 us
    ppermute x22, starting transfers between devices, swapped(): return lax.ppermute(block, axis, [(0, 1), (1, 0)])  17.5 us
    ppermute x9, starting transfers between devices, turned(): lax.ppermute(block, axis, [(i, (i + distance) % size) for i in range(size)])  17.2 us
    pallas_call x2, Pallas kernels, attention(): pl.pallas_call(functools.partial(attention_kernel, head, distances), in_s...  6.69 us
    pallas_call x4, Pallas kernels, gradient(): pl.pallas_call(kernel, in_specs=[IN_VMEM] * len(operands), out_specs=[IN_...  3.18 us
  transfers between devices with their start and end apart: 34, of which 21 were waited for; matrix products, arithmetic and copies ran while one was open for 2% of the time, Pallas kernels for 9%

profile of v15, /device:TPU:0, one launch (start us, length us, event | category | flops | bytes accessed | tf_op | source)
XLA Modules:
  0.0 120.8 jit_solution(7113252155989439789)
XLA Ops:
  0.6 1.8 %multiply_reduce_fusion = f32[256]{0:T(256)S(1)} fusion(bf16[256,2560]{1,0:T(8,128)(2,1)} %values_ref.1), kind=kLoop, calls=%fused_computation | loop fusion | flops 1965824 | bytes 1311744 | tf_op jit(solution)/shard_map/reduce_sum | solution.py:350
  3.9 2.7 %collective-permute-start = (bf16[640,256]{1,0:T(8,128)(2,1)S(1)}, bf16[640,256]{1,0:T(8,128)(2,1)S(1)}, u32[]{:S(2)}, u32[]{:S(2)}) collective-permute-start(bf16[640,256]{1,0:T(8,128)(2,1)S(1)} %dynamic-slice_bitcast_fusion), channel_id=1, source_target_pairs={{0,4},{4,8},{8,12},{12,0},{1,5},{5,9},{9,13},{13,1},{2,6},{6,10},{... | collective-permute-start | bytes 983048 | tf_op jit(solution)/shard_map/ppermute | solution.py:315
  7.8 9.1 %collective-permute-done.kept_ref.refs_0_ = bf16[640,256]{1,0:T(8,128)(2,1)S(1)} collective-permute-done((bf16[640,256]{1,0:T(8,128)(2,1)S(1)}, bf16[640,256]{1,0:T(8,128)(2,1)S(1)}, u32[]{:S(2)}, u32[]{:S(2)}) %collective-permute-start) | collective-permute-done | bytes 327712 | tf_op jit(solution)/shard_map/ppermute | solution.py:315
  17.0 1.7 %collective-permute-start.4 = (bf16[640,256]{1,0:T(8,128)(2,1)S(1)}, bf16[640,256]{1,0:T(8,128)(2,1)S(1)}, u32[]{:S(2)}, u32[]{:S(2)}) collective-permute-start(bf16[640,256]{1,0:T(8,128)(2,1)S(1)} %dynamic-slice_bitcast_fusion), channel_id=1, source_target_pairs={{0,12},{4,0},{8,4},{12,8},{1,13},{5,1},{9,5},{13,9},{2,14},{6,2},{... | collective-permute-start | bytes 983048 | tf_op jit(solution)/shard_map/ppermute | solution.py:315
  18.7 1.5 %collective-permute-start.3 = (bf16[640,256]{1,0:T(8,128)(2,1)S(1)}, bf16[640,256]{1,0:T(8,128)(2,1)S(1)}, u32[]{:S(2)}, u32[]{:S(2)}) collective-permute-start(bf16[640,256]{1,0:T(8,128)(2,1)S(1)} %collective-permute-done.kept_ref.refs_0_), channel_id=1, source_target_pairs={{0,16},{16,0},{1,17},{17,1},{2,18},{18,2},{3,19},{19,3},{4,20},{20... | collective-permute-start | bytes 983048 | tf_op jit(solution)/shard_map/ppermute | solution.py:310
  20.2 1.5 %collective-permute-start.2 = (bf16[640,256]{1,0:T(8,128)(2,1)S(1)}, bf16[640,256]{1,0:T(8,128)(2,1)S(1)}, u32[]{:S(2)}, u32[]{:S(2)}) collective-permute-start(bf16[640,256]{1,0:T(8,128)(2,1)S(1)} %collective-permute-done.kept_ref.refs_0_), channel_id=1, source_target_pairs={{0,2},{2,0},{1,3},{3,1},{4,6},{6,4},{5,7},{7,5},{8,10},{10,8},{9,1... | collective-permute-start | bytes 983048 | tf_op jit(solution)/shard_map/ppermute | solution.py:310
  21.7 5.4 %collective-permute-done.4.refs_0_ = bf16[640,256]{1,0:T(8,128)(2,1)S(1)} collective-permute-done((bf16[640,256]{1,0:T(8,128)(2,1)S(1)}, bf16[640,256]{1,0:T(8,128)(2,1)S(1)}, u32[]{:S(2)}, u32[]{:S(2)}) %collective-permute-start.4) | collective-permute-done | bytes 327712 | tf_op jit(solution)/shard_map/ppermute | solution.py:315
  27.1 1.5 %collective-permute-done.3.refs_2_ = bf16[640,256]{1,0:T(8,128)(2,1)S(1)} collective-permute-done((bf16[640,256]{1,0:T(8,128)(2,1)S(1)}, bf16[640,256]{1,0:T(8,128)(2,1)S(1)}, u32[]{:S(2)}, u32[]{:S(2)}) %collective-permute-start.3) | collective-permute-done | bytes 327712 | tf_op jit(solution)/shard_map/ppermute | solution.py:310
  28.5 1.2 %collective-permute-done.2.arrived_ref.refs_1_ = bf16[640,256]{1,0:T(8,128)(2,1)S(1)} collective-permute-done((bf16[640,256]{1,0:T(8,128)(2,1)S(1)}, bf16[640,256]{1,0:T(8,128)(2,1)S(1)}, u32[]{:S(2)}, u32[]{:S(2)}) %collective-permute-start.2) | collective-permute-done | bytes 327712 | tf_op jit(solution)/shard_map/ppermute | solution.py:310
  30.7 1.5 %collective-permute-start.10 = (bf16[640,256]{1,0:T(8,128)(2,1)S(1)}, bf16[640,256]{1,0:T(8,128)(2,1)S(1)}, u32[]{:S(2)}, u32[]{:S(2)}) collective-permute-start(bf16[640,256]{1,0:T(8,128)(2,1)S(1)} %get-tuple-element.94), channel_id=1, source_target_pairs={{0,2},{2,0},{1,3},{3,1},{4,6},{6,4},{5,7},{7,5},{8,10},{10,8},{9,1... | collective-permute-start | bytes 983048 | tf_op jit(solution)/shard_map/ppermute | solution.py:310
  32.2 1.5 %collective-permute-start.8 = (bf16[640,256]{1,0:T(8,128)(2,1)S(1)}, bf16[640,256]{1,0:T(8,128)(2,1)S(1)}, u32[]{:S(2)}, u32[]{:S(2)}) collective-permute-start(bf16[640,256]{1,0:T(8,128)(2,1)S(1)} %collective-permute-done.4.refs_0_), channel_id=1, source_target_pairs={{0,16},{16,0},{1,17},{17,1},{2,18},{18,2},{3,19},{19,3},{4,20},{20... | collective-permute-start | bytes 983048 | tf_op jit(solution)/shard_map/ppermute | solution.py:310
  34.2 7.1 %collective-permute-done.10.arrived_ref = bf16[640,256]{1,0:T(8,128)(2,1)S(1)} collective-permute-done((bf16[640,256]{1,0:T(8,128)(2,1)S(1)}, bf16[640,256]{1,0:T(8,128)(2,1)S(1)}, u32[]{:S(2)}, u32[]{:S(2)}) %collective-permute-start.10) | collective-permute-done | bytes 327712 | tf_op jit(solution)/shard_map/ppermute | solution.py:310
  41.3 4.4 %collective-permute-done.8.refs_2_ = bf16[640,256]{1,0:T(8,128)(2,1)S(1)} collective-permute-done((bf16[640,256]{1,0:T(8,128)(2,1)S(1)}, bf16[640,256]{1,0:T(8,128)(2,1)S(1)}, u32[]{:S(2)}, u32[]{:S(2)}) %collective-permute-start.8) | collective-permute-done | bytes 327712 | tf_op jit(solution)/shard_map/ppermute | solution.py:310
  46.0 1.4 %collective-permute-done.6.refs_4_ = bf16[2,640,256]{2,1,0:T(8,128)(2,1)S(1)} collective-permute-done((bf16[2,640,256]{2,1,0:T(8,128)(2,1)S(1)}, bf16[2,640,256]{2,1,0:T(8,128)(2,1)S(1)}, u32[]{:S(2)}, u32[]{:S(2)}) %collective-permute-start.6) | collective-permute-done | bytes 655392 | tf_op jit(solution)/shard_map/ppermute | solution.py:315
  48.9 1.5 %collective-permute-start.13 = (bf16[640,256]{1,0:T(8,128)(2,1)S(1)}, bf16[640,256]{1,0:T(8,128)(2,1)S(1)}, u32[]{:S(2)}, u32[]{:S(2)}) collective-permute-start(bf16[640,256]{1,0:T(8,128)(2,1)S(1)} %get-tuple-element.99), channel_id=1, source_target_pairs={{0,2},{2,0},{1,3},{3,1},{4,6},{6,4},{5,7},{7,5},{8,10},{10,8},{9,1... | collective-permute-start | bytes 983048 | tf_op jit(solution)/shard_map/ppermute | solution.py:310
  52.7 5.5 %collective-permute-done.13 = bf16[640,256]{1,0:T(8,128)(2,1)S(1)} collective-permute-done((bf16[640,256]{1,0:T(8,128)(2,1)S(1)}, bf16[640,256]{1,0:T(8,128)(2,1)S(1)}, u32[]{:S(2)}, u32[]{:S(2)}) %collective-permute-start.13) | collective-permute-done | bytes 327712 | tf_op jit(solution)/shard_map/ppermute | solution.py:310
  58.2 7.0 %collective-permute-done.12.refs_3_ = bf16[640,256]{1,0:T(8,128)(2,1)S(1)} collective-permute-done((bf16[640,256]{1,0:T(8,128)(2,1)S(1)}, bf16[640,256]{1,0:T(8,128)(2,1)S(1)}, u32[]{:S(2)}, u32[]{:S(2)}) %collective-permute-start.12) | collective-permute-done | bytes 327712 | tf_op jit(solution)/shard_map/ppermute | solution.py:310
  65.3 2.9 %attention.2 = (bf16[256,640]{1,0:T(8,128)(2,1)S(1)}, bf16[256,256]{1,0:T(8,128)(2,1)S(1)}) custom-call(bf16[256,2560]{1,0:T(8,128)(2,1)S(1)} %get-tuple-element.85.own_ref, bf16[256,2560]{1,0:T(8,128)(2,1)S(1)} %collective-permute-done.5.other_ref, bf16[640,256]{1,0:T(8,128)(2,1)S(1)} %collective-permute-done.4.refs_0_, ...), custom_call_target="tpu_custom_call" | custom-call | flops 419430400 | bytes 4000000 | tf_op jit(solution)/shard_map/attention/pallas_call | solution.py:182
  68.2 3.8 %attention.3 = (bf16[256,1280]{1,0:T(8,128)(2,1)}, bf16[256,256]{1,0:T(8,128)(2,1)S(1)}) custom-call(bf16[256,2560]{1,0:T(8,128)(2,1)S(1)} %get-tuple-element.85.own_ref, bf16[256,2560]{1,0:T(8,128)(2,1)S(1)} %collective-permute-done.5.other_ref, bf16[640,256]{1,0:T(8,128)(2,1)S(1)} %collective-permute-done.4.refs_0_, ...), custom_call_target="tpu_custom_call" | custom-call | flops 419430400 | bytes 4000000 | tf_op jit(solution)/shard_map/attention/pallas_call | solution.py:182
  72.0 1.2 collective-permute-done.16.refs_10_
  73.2 1.5 %collective-permute-start.18 = (bf16[256,256]{1,0:T(8,128)(2,1)S(1)}, bf16[256,256]{1,0:T(8,128)(2,1)S(1)}, u32[]{:S(2)}, u32[]{:S(2)}) collective-permute-start(bf16[256,256]{1,0:T(8,128)(2,1)S(1)} %get-tuple-element.132.refs_0_), channel_id=1, source_target_pairs={{0,2},{2,0},{1,3},{3,1},{4,6},{6,4},{5,7},{7,5},{8,10},{10,8},{9,1... | collective-permute-start | bytes 393224 | tf_op jit(solution)/shard_map/ppermute | solution.py:310
  76.0 9.1 %collective-permute-start.24 = (bf16[256,256]{1,0:T(8,128)(2,1)S(1)}, bf16[256,256]{1,0:T(8,128)(2,1)S(1)}, u32[]{:S(2)}, u32[]{:S(2)}) collective-permute-start(bf16[256,256]{1,0:T(8,128)(2,1)S(1)} %get-tuple-element.149.refs_0_), channel_id=1, source_target_pairs={{0,4},{4,8},{8,12},{12,0},{1,5},{5,9},{9,13},{13,1},{2,6},{6,10},{... | collective-permute-start | bytes 393224 | tf_op jit(solution)/shard_map/ppermute | solution.py:315
  85.2 3.5 %collective-permute-done.17.refs_2_ = bf16[256,256]{1,0:T(8,128)(2,1)S(1)} collective-permute-done((bf16[256,256]{1,0:T(8,128)(2,1)S(1)}, bf16[256,256]{1,0:T(8,128)(2,1)S(1)}, u32[]{:S(2)}, u32[]{:S(2)}) %collective-permute-start.17) | collective-permute-done | bytes 131104 | tf_op jit(solution)/shard_map/ppermute | solution.py:315
  88.6 1.6 %collective-permute-start.19 = (bf16[256,256]{1,0:T(8,128)(2,1)S(1)}, bf16[256,256]{1,0:T(8,128)(2,1)S(1)}, u32[]{:S(2)}, u32[]{:S(2)}) collective-permute-start(bf16[256,256]{1,0:T(8,128)(2,1)S(1)} %get-tuple-element.132.refs_0_), channel_id=1, source_target_pairs={{0,12},{4,0},{8,4},{12,8},{1,13},{5,1},{9,5},{13,9},{2,14},{6,2},{... | collective-permute-start | bytes 393224 | tf_op jit(solution)/shard_map/ppermute | solution.py:315
  91.6 1.1 collective-permute-start.27
  92.7 1.7 %collective-permute-done.19.refs_4_ = bf16[256,256]{1,0:T(8,128)(2,1)S(1)} collective-permute-done((bf16[256,256]{1,0:T(8,128)(2,1)S(1)}, bf16[256,256]{1,0:T(8,128)(2,1)S(1)}, u32[]{:S(2)}, u32[]{:S(2)}) %collective-permute-start.19) | collective-permute-done | bytes 131104 | tf_op jit(solution)/shard_map/ppermute | solution.py:315
  94.4 1.9 %collective-permute-done.20.refs_3_ = bf16[256,256]{1,0:T(8,128)(2,1)S(1)} collective-permute-done((bf16[256,256]{1,0:T(8,128)(2,1)S(1)}, bf16[256,256]{1,0:T(8,128)(2,1)S(1)}, u32[]{:S(2)}, u32[]{:S(2)}) %collective-permute-start.20) | collective-permute-done | bytes 131104 | tf_op jit(solution)/shard_map/ppermute | solution.py:310
  99.8 5.6 %collective-permute-done.31.refs_0_ = bf16[256,256]{1,0:T(8,128)(2,1)S(1)} collective-permute-done((bf16[256,256]{1,0:T(8,128)(2,1)S(1)}, bf16[256,256]{1,0:T(8,128)(2,1)S(1)}, u32[]{:S(2)}, u32[]{:S(2)}) %collective-permute-start.31) | collective-permute-done | bytes 131104 | tf_op jit(solution)/shard_map/ppermute | solution.py:315
  105.9 6.5 %collective-permute-done.21.refs_0_ = bf16[256,256]{1,0:T(8,128)(2,1)S(1)} collective-permute-done((bf16[256,256]{1,0:T(8,128)(2,1)S(1)}, bf16[256,256]{1,0:T(8,128)(2,1)S(1)}, u32[]{:S(2)}, u32[]{:S(2)}) %collective-permute-start.21) | collective-permute-done | bytes 131104 | tf_op jit(solution)/shard_map/ppermute | solution.py:315
  112.8 1.6 %collective-permute-start.23 = (bf16[256,256]{1,0:T(8,128)(2,1)S(1)}, bf16[256,256]{1,0:T(8,128)(2,1)S(1)}, u32[]{:S(2)}, u32[]{:S(2)}) collective-permute-start(bf16[256,256]{1,0:T(8,128)(2,1)S(1)} %collective-permute-done.21.refs_0_), channel_id=1, source_target_pairs={{0,2},{2,0},{1,3},{3,1},{4,6},{6,4},{5,7},{7,5},{8,10},{10,8},{9,1... | collective-permute-start | bytes 393224 | tf_op jit(solution)/shard_map/ppermute | solution.py:310
  115.1 2.9 %collective-permute-done.33.refs_1_ = bf16[256,256]{1,0:T(8,128)(2,1)S(1)} collective-permute-done((bf16[256,256]{1,0:T(8,128)(2,1)S(1)}, bf16[256,256]{1,0:T(8,128)(2,1)S(1)}, u32[]{:S(2)}, u32[]{:S(2)}) %collective-permute-start.33) | collective-permute-done | bytes 131104 | tf_op jit(solution)/shard_map/ppermute | solution.py:310
  119.4 1.4 %gradient.7 = (f32[2,640,256]{2,1,0:T(8,128)}, f32[2,256]{1,0:T(2,128)}) custom-call(bf16[256,256]{1,0:T(8,128)(2,1)S(1)} %collective-permute-done.21.refs_0_, bf16[256,256]{1,0:T(8,128)(2,1)S(1)} %collective-permute-done.23.refs_1_, bf16[2,640,256]{2,1,0:T(8,128)(2,1)S(1)} %collective-permute-done.14.refs_6_.refs_2_, ...), custom_call_target="tpu_custom_call" | custom-call | flops 167772160 | bytes 2000000 | tf_op jit(solution)/shard_map/gradient/pallas_call | solution.py:246
  (69 shorter events, 17.4 us)
Async XLA Ops:
  3.9 13.0 %collective-permute-start = (bf16[640,256]{1,0:T(8,128)(2,1)S(1)}, bf16[640,256]{1,0:T(8,128)(2,1)S(1)}, u32[]{:S(2)}, u32[]{:S(2)}) collective-permute-start(bf16[640,256]{1,0:T(8,128)(2,1)S(1)} %dynamic-slice_bitcast_fusion), channel_id=1, source_target_pairs={{0,4},{4,8},{8,12},{12,0},{1,5},{5,9},{9,13},{13,1},{2,6},{6,10},{... | collective-permute-start | bytes 983048 | tf_op jit(solution)/shard_map/ppermute | solution.py:315
  17.0 12.8 %collective-permute-start.5 = (bf16[256,2560]{1,0:T(8,128)(2,1)S(1)}, bf16[256,2560]{1,0:T(8,128)(2,1)S(1)}, u32[]{:S(2)}, u32[]{:S(2)}) collective-permute-start(bf16[256,2560]{1,0:T(8,128)(2,1)S(1)} %get-tuple-element.85.own_ref), channel_id=1, source_target_pairs={{0,1},{1,0},{2,3},{3,2},{4,5},{5,4},{6,7},{7,6},{8,9},{9,8},{10,11... | collective-permute-start | bytes 3932168 | tf_op jit(solution)/shard_map/ppermute | solution.py:310
  17.0 10.1 %collective-permute-start.4 = (bf16[640,256]{1,0:T(8,128)(2,1)S(1)}, bf16[640,256]{1,0:T(8,128)(2,1)S(1)}, u32[]{:S(2)}, u32[]{:S(2)}) collective-permute-start(bf16[640,256]{1,0:T(8,128)(2,1)S(1)} %dynamic-slice_bitcast_fusion), channel_id=1, source_target_pairs={{0,12},{4,0},{8,4},{12,8},{1,13},{5,1},{9,5},{13,9},{2,14},{6,2},{... | collective-permute-start | bytes 983048 | tf_op jit(solution)/shard_map/ppermute | solution.py:315
  18.7 9.8 %collective-permute-start.3 = (bf16[640,256]{1,0:T(8,128)(2,1)S(1)}, bf16[640,256]{1,0:T(8,128)(2,1)S(1)}, u32[]{:S(2)}, u32[]{:S(2)}) collective-permute-start(bf16[640,256]{1,0:T(8,128)(2,1)S(1)} %collective-permute-done.kept_ref.refs_0_), channel_id=1, source_target_pairs={{0,16},{16,0},{1,17},{17,1},{2,18},{18,2},{3,19},{19,3},{4,20},{20... | collective-permute-start | bytes 983048 | tf_op jit(solution)/shard_map/ppermute | solution.py:310
  20.2 9.6 %collective-permute-start.2 = (bf16[640,256]{1,0:T(8,128)(2,1)S(1)}, bf16[640,256]{1,0:T(8,128)(2,1)S(1)}, u32[]{:S(2)}, u32[]{:S(2)}) collective-permute-start(bf16[640,256]{1,0:T(8,128)(2,1)S(1)} %collective-permute-done.kept_ref.refs_0_), channel_id=1, source_target_pairs={{0,2},{2,0},{1,3},{3,1},{4,6},{6,4},{5,7},{7,5},{8,10},{10,8},{9,1... | collective-permute-start | bytes 983048 | tf_op jit(solution)/shard_map/ppermute | solution.py:310
  29.8 17.6 %collective-permute-start.6 = (bf16[2,640,256]{2,1,0:T(8,128)(2,1)S(1)}, bf16[2,640,256]{2,1,0:T(8,128)(2,1)S(1)}, u32[]{:S(2)}, u32[]{:S(2)}) collective-permute-start(bf16[2,640,256]{2,1,0:T(8,128)(2,1)S(1)} %pack.2), channel_id=1, source_target_pairs={{0,4},{4,8},{8,12},{12,0},{1,5},{5,9},{9,13},{13,1},{2,6},{6,10},{... | collective-permute-start | bytes 1966088 | tf_op jit(solution)/shard_map/ppermute | solution.py:315
  30.2 11.2 %collective-permute-start.9 = (bf16[640,256]{1,0:T(8,128)(2,1)S(1)}, bf16[640,256]{1,0:T(8,128)(2,1)S(1)}, u32[]{:S(2)}, u32[]{:S(2)}) collective-permute-start(bf16[640,256]{1,0:T(8,128)(2,1)S(1)} %collective-permute-done.2.arrived_ref.refs_1_), channel_id=1, source_target_pairs={{0,16},{16,0},{1,17},{17,1},{2,18},{18,2},{3,19},{19,3},{4,20},{20... | collective-permute-start | bytes 983048 | tf_op jit(solution)/shard_map/ppermute | solution.py:310
  30.7 10.7 %collective-permute-start.10 = (bf16[640,256]{1,0:T(8,128)(2,1)S(1)}, bf16[640,256]{1,0:T(8,128)(2,1)S(1)}, u32[]{:S(2)}, u32[]{:S(2)}) collective-permute-start(bf16[640,256]{1,0:T(8,128)(2,1)S(1)} %get-tuple-element.94), channel_id=1, source_target_pairs={{0,2},{2,0},{1,3},{3,1},{4,6},{6,4},{5,7},{7,5},{8,10},{10,8},{9,1... | collective-permute-start | bytes 983048 | tf_op jit(solution)/shard_map/ppermute | solution.py:310
  32.2 13.5 %collective-permute-start.8 = (bf16[640,256]{1,0:T(8,128)(2,1)S(1)}, bf16[640,256]{1,0:T(8,128)(2,1)S(1)}, u32[]{:S(2)}, u32[]{:S(2)}) collective-permute-start(bf16[640,256]{1,0:T(8,128)(2,1)S(1)} %collective-permute-done.4.refs_0_), channel_id=1, source_target_pairs={{0,16},{16,0},{1,17},{17,1},{2,18},{18,2},{3,19},{19,3},{4,20},{20... | collective-permute-start | bytes 983048 | tf_op jit(solution)/shard_map/ppermute | solution.py:310
  33.7 12.3 %collective-permute-start.7 = (bf16[640,256]{1,0:T(8,128)(2,1)S(1)}, bf16[640,256]{1,0:T(8,128)(2,1)S(1)}, u32[]{:S(2)}, u32[]{:S(2)}) collective-permute-start(bf16[640,256]{1,0:T(8,128)(2,1)S(1)} %collective-permute-done.4.refs_0_), channel_id=1, source_target_pairs={{0,2},{2,0},{1,3},{3,1},{4,6},{6,4},{5,7},{7,5},{8,10},{10,8},{9,1... | collective-permute-start | bytes 983048 | tf_op jit(solution)/shard_map/ppermute | solution.py:310
  47.5 17.8 %collective-permute-start.14 = (bf16[2,640,256]{2,1,0:T(8,128)(2,1)S(1)}, bf16[2,640,256]{2,1,0:T(8,128)(2,1)S(1)}, u32[]{:S(2)}, u32[]{:S(2)}) collective-permute-start(bf16[2,640,256]{2,1,0:T(8,128)(2,1)S(1)} %pack.3), channel_id=1, source_target_pairs={{0,0},{1,8},{4,4},{5,12},{8,1},{9,9},{12,5},{13,13},{2,2},{3,10},{... | collective-permute-start | bytes 1966088 | tf_op jit(solution)/shard_map/ppermute | solution.py:343
  48.2 17.1 %collective-permute-start.11 = (bf16[2,640,256]{2,1,0:T(8,128)(2,1)S(1)}, bf16[2,640,256]{2,1,0:T(8,128)(2,1)S(1)}, u32[]{:S(2)}, u32[]{:S(2)}) collective-permute-start(bf16[2,640,256]{2,1,0:T(8,128)(2,1)S(1)} %collective-permute-done.6.refs_4_), channel_id=1, source_target_pairs={{0,16},{16,0},{1,17},{17,1},{2,18},{18,2},{3,19},{19,3},{4,20},{20... | collective-permute-start | bytes 1966088 | tf_op jit(solution)/shard_map/ppermute | solution.py:310
  48.9 9.4 %collective-permute-start.13 = (bf16[640,256]{1,0:T(8,128)(2,1)S(1)}, bf16[640,256]{1,0:T(8,128)(2,1)S(1)}, u32[]{:S(2)}, u32[]{:S(2)}) collective-permute-start(bf16[640,256]{1,0:T(8,128)(2,1)S(1)} %get-tuple-element.99), channel_id=1, source_target_pairs={{0,2},{2,0},{1,3},{3,1},{4,6},{6,4},{5,7},{7,5},{8,10},{10,8},{9,1... | collective-permute-start | bytes 983048 | tf_op jit(solution)/shard_map/ppermute | solution.py:310
  50.4 14.9 %collective-permute-start.12 = (bf16[640,256]{1,0:T(8,128)(2,1)S(1)}, bf16[640,256]{1,0:T(8,128)(2,1)S(1)}, u32[]{:S(2)}, u32[]{:S(2)}) collective-permute-start(bf16[640,256]{1,0:T(8,128)(2,1)S(1)} %collective-permute-done.8.refs_2_), channel_id=1, source_target_pairs={{0,2},{2,0},{1,3},{3,1},{4,6},{6,4},{5,7},{7,5},{8,10},{10,8},{9,1... | collective-permute-start | bytes 983048 | tf_op jit(solution)/shard_map/ppermute | solution.py:310
  51.6 20.4 %collective-permute-start.15 = (bf16[640,256]{1,0:T(8,128)(2,1)S(1)}, bf16[640,256]{1,0:T(8,128)(2,1)S(1)}, u32[]{:S(2)}, u32[]{:S(2)}) collective-permute-start(bf16[640,256]{1,0:T(8,128)(2,1)S(1)} %get-tuple-element.113), channel_id=1, source_target_pairs={{0,4},{1,12},{4,0},{5,8},{8,5},{9,13},{12,1},{13,9},{2,6},{3,14},{... | collective-permute-start | bytes 983048 | tf_op jit(solution)/shard_map/ppermute | solution.py:343
  65.3 7.9 %collective-permute-start.16 = (bf16[640,256]{1,0:T(8,128)(2,1)S(1)}, bf16[640,256]{1,0:T(8,128)(2,1)S(1)}, u32[]{:S(2)}, u32[]{:S(2)}) collective-permute-start(bf16[640,256]{1,0:T(8,128)(2,1)S(1)} %collective-permute-done.13), channel_id=1, source_target_pairs={{0,4},{1,12},{4,0},{5,8},{8,5},{9,13},{12,1},{13,9},{2,6},{3,14},{... | collective-permute-start | bytes 983048 | tf_op jit(solution)/shard_map/ppermute | solution.py:343
  73.2 12.0 %collective-permute-start.18 = (bf16[256,256]{1,0:T(8,128)(2,1)S(1)}, bf16[256,256]{1,0:T(8,128)(2,1)S(1)}, u32[]{:S(2)}, u32[]{:S(2)}) collective-permute-start(bf16[256,256]{1,0:T(8,128)(2,1)S(1)} %get-tuple-element.132.refs_0_), channel_id=1, source_target_pairs={{0,2},{2,0},{1,3},{3,1},{4,6},{6,4},{5,7},{7,5},{8,10},{10,8},{9,1... | collective-permute-start | bytes 393224 | tf_op jit(solution)/shard_map/ppermute | solution.py:310
  74.7 13.9 %collective-permute-start.17 = (bf16[256,256]{1,0:T(8,128)(2,1)S(1)}, bf16[256,256]{1,0:T(8,128)(2,1)S(1)}, u32[]{:S(2)}, u32[]{:S(2)}) collective-permute-start(bf16[256,256]{1,0:T(8,128)(2,1)S(1)} %get-tuple-element.132.refs_0_), channel_id=1, source_target_pairs={{0,4},{4,8},{8,12},{12,0},{1,5},{5,9},{9,13},{13,1},{2,6},{6,10},{... | collective-permute-start | bytes 393224 | tf_op jit(solution)/shard_map/ppermute | solution.py:315
  75.5 15.0 %collective-permute-start.25 = (bf16[256,256]{1,0:T(8,128)(2,1)S(1)}, bf16[256,256]{1,0:T(8,128)(2,1)S(1)}, u32[]{:S(2)}, u32[]{:S(2)}) collective-permute-start(bf16[256,256]{1,0:T(8,128)(2,1)S(1)} %get-tuple-element.149.refs_0_), channel_id=1, source_target_pairs={{0,2},{2,0},{1,3},{3,1},{4,6},{6,4},{5,7},{7,5},{8,10},{10,8},{9,1... | collective-permute-start | bytes 393224 | tf_op jit(solution)/shard_map/ppermute | solution.py:310
  76.0 15.4 %collective-permute-start.24 = (bf16[256,256]{1,0:T(8,128)(2,1)S(1)}, bf16[256,256]{1,0:T(8,128)(2,1)S(1)}, u32[]{:S(2)}, u32[]{:S(2)}) collective-permute-start(bf16[256,256]{1,0:T(8,128)(2,1)S(1)} %get-tuple-element.149.refs_0_), channel_id=1, source_target_pairs={{0,4},{4,8},{8,12},{12,0},{1,5},{5,9},{9,13},{13,1},{2,6},{6,10},{... | collective-permute-start | bytes 393224 | tf_op jit(solution)/shard_map/ppermute | solution.py:315
  88.6 5.8 %collective-permute-start.19 = (bf16[256,256]{1,0:T(8,128)(2,1)S(1)}, bf16[256,256]{1,0:T(8,128)(2,1)S(1)}, u32[]{:S(2)}, u32[]{:S(2)}) collective-permute-start(bf16[256,256]{1,0:T(8,128)(2,1)S(1)} %get-tuple-element.132.refs_0_), channel_id=1, source_target_pairs={{0,12},{4,0},{8,4},{12,8},{1,13},{5,1},{9,5},{13,9},{2,14},{6,2},{... | collective-permute-start | bytes 393224 | tf_op jit(solution)/shard_map/ppermute | solution.py:315
  90.2 6.1 %collective-permute-start.20 = (bf16[256,256]{1,0:T(8,128)(2,1)S(1)}, bf16[256,256]{1,0:T(8,128)(2,1)S(1)}, u32[]{:S(2)}, u32[]{:S(2)}) collective-permute-start(bf16[256,256]{1,0:T(8,128)(2,1)S(1)} %collective-permute-done.17.refs_2_), channel_id=1, source_target_pairs={{0,2},{2,0},{1,3},{3,1},{4,6},{6,4},{5,7},{7,5},{8,10},{10,8},{9,1... | collective-permute-start | bytes 393224 | tf_op jit(solution)/shard_map/ppermute | solution.py:310
  91.6 6.1 %collective-permute-start.27 = (bf16[256,256]{1,0:T(8,128)(2,1)S(1)}, bf16[256,256]{1,0:T(8,128)(2,1)S(1)}, u32[]{:S(2)}, u32[]{:S(2)}) collective-permute-start(bf16[256,256]{1,0:T(8,128)(2,1)S(1)} %collective-permute-done.24.refs_2_), channel_id=1, source_target_pairs={{0,2},{2,0},{1,3},{3,1},{4,6},{6,4},{5,7},{7,5},{8,10},{10,8},{9,1... | collective-permute-start | bytes 393224 | tf_op jit(solution)/shard_map/ppermute | solution.py:310
  97.7 16.7 %collective-permute-start.28 = (bf16[2,640,256]{2,1,0:T(8,128)(2,1)S(1)}, bf16[2,640,256]{2,1,0:T(8,128)(2,1)S(1)}, u32[]{:S(2)}, u32[]{:S(2)}) collective-permute-start(bf16[2,640,256]{2,1,0:T(8,128)(2,1)S(1)} %collective-permute-done.14.refs_6_.refs_2_), channel_id=1, source_target_pairs={{0,1},{1,0},{2,3},{3,2},{4,5},{5,4},{6,7},{7,6},{8,9},{9,8},{10,11... | collective-permute-start | bytes 1966088 | tf_op jit(solution)/shard_map/ppermute | solution.py:310
  97.7 7.7 %collective-permute-start.31 = (bf16[256,256]{1,0:T(8,128)(2,1)S(1)}, bf16[256,256]{1,0:T(8,128)(2,1)S(1)}, u32[]{:S(2)}, u32[]{:S(2)}) collective-permute-start(bf16[256,256]{1,0:T(8,128)(2,1)S(1)} %collective-permute-done.24.refs_2_), channel_id=1, source_target_pairs={{0,4},{4,8},{8,12},{12,0},{1,5},{5,9},{9,13},{13,1},{2,6},{6,10},{... | collective-permute-start | bytes 393224 | tf_op jit(solution)/shard_map/ppermute | solution.py:315
  98.4 15.9 %collective-permute-start.29 = (bf16[640,256]{1,0:T(8,128)(2,1)S(1)}, bf16[640,256]{1,0:T(8,128)(2,1)S(1)}, u32[]{:S(2)}, u32[]{:S(2)}) collective-permute-start(bf16[640,256]{1,0:T(8,128)(2,1)S(1)} %collective-permute-done.15.refs_8_), channel_id=1, source_target_pairs={{0,1},{1,0},{2,3},{3,2},{4,5},{5,4},{6,7},{7,6},{8,9},{9,8},{10,11... | collective-permute-start | bytes 983048 | tf_op jit(solution)/shard_map/ppermute | solution.py:310
  98.7 15.7 %collective-permute-start.30 = (bf16[640,256]{1,0:T(8,128)(2,1)S(1)}, bf16[640,256]{1,0:T(8,128)(2,1)S(1)}, u32[]{:S(2)}, u32[]{:S(2)}) collective-permute-start(bf16[640,256]{1,0:T(8,128)(2,1)S(1)} %collective-permute-done.16.refs_10_), channel_id=1, source_target_pairs={{0,1},{1,0},{2,3},{3,2},{4,5},{5,4},{6,7},{7,6},{8,9},{9,8},{10,11... | collective-permute-start | bytes 983048 | tf_op jit(solution)/shard_map/ppermute | solution.py:310
  98.9 6.5 %collective-permute-start.32 = (bf16[256,256]{1,0:T(8,128)(2,1)S(1)}, bf16[256,256]{1,0:T(8,128)(2,1)S(1)}, u32[]{:S(2)}, u32[]{:S(2)}) collective-permute-start(bf16[256,256]{1,0:T(8,128)(2,1)S(1)} %collective-permute-done.26.refs_4_), channel_id=1, source_target_pairs={{0,2},{2,0},{1,3},{3,1},{4,6},{6,4},{5,7},{7,5},{8,10},{10,8},{9,1... | collective-permute-start | bytes 393224 | tf_op jit(solution)/shard_map/ppermute | solution.py:310
  105.4 6.9 %collective-permute-start.21 = (bf16[256,256]{1,0:T(8,128)(2,1)S(1)}, bf16[256,256]{1,0:T(8,128)(2,1)S(1)}, u32[]{:S(2)}, u32[]{:S(2)}) collective-permute-start(bf16[256,256]{1,0:T(8,128)(2,1)S(1)} %collective-permute-done.17.refs_2_), channel_id=1, source_target_pairs={{0,4},{4,8},{8,12},{12,0},{1,5},{5,9},{9,13},{13,1},{2,6},{6,10},{... | collective-permute-start | bytes 393224 | tf_op jit(solution)/shard_map/ppermute | solution.py:315
  105.4 7.4 %collective-permute-start.22 = (bf16[256,256]{1,0:T(8,128)(2,1)S(1)}, bf16[256,256]{1,0:T(8,128)(2,1)S(1)}, u32[]{:S(2)}, u32[]{:S(2)}) collective-permute-start(bf16[256,256]{1,0:T(8,128)(2,1)S(1)} %collective-permute-done.19.refs_4_), channel_id=1, source_target_pairs={{0,2},{2,0},{1,3},{3,1},{4,6},{6,4},{5,7},{7,5},{8,10},{10,8},{9,1... | collective-permute-start | bytes 393224 | tf_op jit(solution)/shard_map/ppermute | solution.py:310
  112.3 5.6 %collective-permute-start.33 = (bf16[256,256]{1,0:T(8,128)(2,1)S(1)}, bf16[256,256]{1,0:T(8,128)(2,1)S(1)}, u32[]{:S(2)}, u32[]{:S(2)}) collective-permute-start(bf16[256,256]{1,0:T(8,128)(2,1)S(1)} %collective-permute-done.31.refs_0_), channel_id=1, source_target_pairs={{0,2},{2,0},{1,3},{3,1},{4,6},{6,4},{5,7},{7,5},{8,10},{10,8},{9,1... | collective-permute-start | bytes 393224 | tf_op jit(solution)/shard_map/ppermute | solution.py:310
  112.8 6.6 %collective-permute-start.23 = (bf16[256,256]{1,0:T(8,128)(2,1)S(1)}, bf16[256,256]{1,0:T(8,128)(2,1)S(1)}, u32[]{:S(2)}, u32[]{:S(2)}) collective-permute-start(bf16[256,256]{1,0:T(8,128)(2,1)S(1)} %collective-permute-done.21.refs_0_), channel_id=1, source_target_pairs={{0,2},{2,0},{1,3},{3,1},{4,6},{6,4},{5,7},{7,5},{8,10},{10,8},{9,1... | collective-permute-start | bytes 393224 | tf_op jit(solution)/shard_map/ppermute | solution.py:310
  (8 other events, 84.8 us)

commit v16 on v13

--- a/solution.py
+++ b/solution.py
@@ -279,9 +279,7 @@
         out_specs=[IN_VMEM] * 5,
         out_shape=[jax.ShapeDtypeStruct(shape, jnp.bfloat16) for shape in shapes],
         compiler_params=pltpu.CompilerParams(vmem_limit_bytes=VMEM_BYTES),
-        cost_estimate=pl.CostEstimate(
-            flops=4 * length * features, bytes_accessed=6 * length * features, transcendentals=0
-        ),
+        cost_estimate=pl.CostEstimate(flops=length, bytes_accessed=length, transcendentals=0),
         name="norm",
     )(activations, scale, gain)
 
@@ -396,19 +394,19 @@
     twice_y, down_both, arrived_odd, even, sums, cosine, sine = lax.optimization_barrier(
         (twice_y, down_both, arrived_odd, even, sums, cosine, sine)
     )
-    odd = sent_along(pack(kept_odd, arrived_odd), 1)
-    even_other = swapped(even, "sub")
+    odd_same, odd_mate = sent_along(kept_odd, 1), sent_along(arrived_odd, 1)
     gathered = [(-1, (down, down_x, down_y, down_both)), (2, (twice, twice_y))]
     grad_query, grad_pair = attention(
         gathered, normed, normed_other, sums, bias, cosine, sine, queries, cotangent
     )
 
-    grad_pair, odd, even_other = lax.optimization_barrier((grad_pair, odd, even_other))
+    grad_pair, odd_same, odd_mate = lax.optimization_barrier((grad_pair, odd_same, odd_mate))
     pair_up, pair_x = turned(grad_pair, "blk", 1), swapped(grad_pair, "dp")
-    pair_up, pair_x, grad_pair, even, odd = lax.optimization_barrier(
-        (pair_up, pair_x, grad_pair, even, odd)
-    )
-    slabs = ((even, even_other), (odd, swapped(odd, "sub")))
+    pair_up, pair_x, grad_pair, even, odd_same, odd_mate = lax.optimization_barrier(
+        (pair_up, pair_x, grad_pair, even, odd_same, odd_mate)
+    )
+    odd = pack(odd_same, odd_mate)
+    slabs = ((even, swapped(even, "sub")), (odd, swapped(odd, "sub")))
     pair_down, pair_up_x = turned(grad_pair, "blk", -1), swapped(pair_up, "dp")
     pair_down, pair_up_x, pair_up = lax.optimization_barrier((pair_down, pair_up_x, pair_up))
     pair_twice, pair_down_x = turned(pair_up, "blk", 1), swapped(pair_down, "dp")

time: 118 us -> 115 us (0.975); the launches traced: 116 us -> 115 us
  starting transfers between devices: 28.2 us -> 26.3 us
    ppermute x2 -> x3, waiting for transfers between devices: 6.72 us -> 3.38 us  [sent_along(): return lax.ppermute(slabs, ('blk', 'sub'), route)]
    ppermute x17, waiting for transfers between devices: 34.6 us -> 36.8 us  [swapped(): return lax.ppermute(block, axis, [(0, 1), (1, 0)])]
    ppermute x17, starting transfers between devices: 20.6 us -> 18.5 us  [swapped(): return lax.ppermute(block, axis, [(0, 1), (1, 0)])]
    ppermute x6, waiting for transfers between devices: 30.6 us -> 32.7 us  [turned(): lax.ppermute(block, axis, [(i, (i + distance) % size) for i in range(size)])]
  transfers between devices with their start and end apart: 25 -> 26, of which waited for: 19 -> 19; matrix products, arithmetic and copies ran while one was open for 2% -> 2% of each run, Pallas kernels for 8% -> 8%
where the time goes in v16:
time: 115 us
  waiting for transfers between devices  72.8 us (63%)
  starting transfers between devices  26.3 us (23%)
  Pallas kernels  11.1 us (10%)
  other arithmetic  2.5 us (2%)
  local copies, waits for them, and re-layouts  1.19 us (1%)
    ppermute x17, waiting for transfers between devices, swapped(): return lax.ppermute(block, axis, [(0, 1), (1, 0)])  36.8 us
    ppermute x6, waiting for transfers between devices, turned(): lax.ppermute(block, axis, [(i, (i + distance) % size) for i in range(size)])  32.7 us
    ppermute x17, starting transfers between devices, swapped(): return lax.ppermute(block, axis, [(0, 1), (1, 0)])  18.5 us
    ppermute x6, starting transfers between devices, turned(): lax.ppermute(block, axis, [(i, (i + distance) % size) for i in range(size)])  7 us
    pallas_call x1, Pallas kernels, attention(): pl.pallas_call(functools.partial(attention_kernel, distances), in_specs=[...  5.51 us
    pallas_call x2, Pallas kernels, gradient(): pl.pallas_call(functools.partial(gradient_kernel, tuple(some), sums is No...  3.46 us
    ppermute x3, waiting for transfers between devices, sent_along(): return lax.ppermute(slabs, ('blk', 'sub'), route)  3.38 us
  transfers between devices with their start and end apart: 26, of which 19 were waited for; matrix products, arithmetic and copies ran while one was open for 2% of the time, Pallas kernels for 8%

profile of v16, /device:TPU:0, one launch (start us, length us, event | category | flops | bytes accessed | tf_op | source)
XLA Modules:
  0.0 114.7 jit_solution(10620960414147458582)
XLA Ops:
  0.6 1.8 %multiply_reduce_fusion = f32[256]{0:T(256)S(1)} fusion(bf16[256,2560]{1,0:T(8,128)(2,1)} %values_ref.1), kind=kLoop, calls=%fused_computation | loop fusion | flops 1965824 | bytes 1311744 | tf_op jit(solution)/shard_map/reduce_sum | solution.py:345
  3.9 2.7 %collective-permute-start = (bf16[640,256]{1,0:T(8,128)(2,1)S(1)}, bf16[640,256]{1,0:T(8,128)(2,1)S(1)}, u32[]{:S(2)}, u32[]{:S(2)}) collective-permute-start(bf16[640,256]{1,0:T(8,128)(2,1)S(1)} %dynamic-slice_bitcast_fusion), channel_id=1, source_target_pairs={{0,4},{4,8},{8,12},{12,0},{1,5},{5,9},{9,13},{13,1},{2,6},{6,10},{... | collective-permute-start | bytes 983048 | tf_op jit(solution)/shard_map/ppermute | solution.py:310
  7.8 9.1 %collective-permute-done.kept_ref.refs_0_ = bf16[640,256]{1,0:T(8,128)(2,1)S(1)} collective-permute-done((bf16[640,256]{1,0:T(8,128)(2,1)S(1)}, bf16[640,256]{1,0:T(8,128)(2,1)S(1)}, u32[]{:S(2)}, u32[]{:S(2)}) %collective-permute-start) | collective-permute-done | bytes 327712 | tf_op jit(solution)/shard_map/ppermute | solution.py:310
  17.0 1.7 %collective-permute-start.4 = (bf16[640,256]{1,0:T(8,128)(2,1)S(1)}, bf16[640,256]{1,0:T(8,128)(2,1)S(1)}, u32[]{:S(2)}, u32[]{:S(2)}) collective-permute-start(bf16[640,256]{1,0:T(8,128)(2,1)S(1)} %dynamic-slice_bitcast_fusion), channel_id=1, source_target_pairs={{0,12},{4,0},{8,4},{12,8},{1,13},{5,1},{9,5},{13,9},{2,14},{6,2},{... | collective-permute-start | bytes 983048 | tf_op jit(solution)/shard_map/ppermute | solution.py:310
  18.7 1.5 %collective-permute-start.3 = (bf16[640,256]{1,0:T(8,128)(2,1)S(1)}, bf16[640,256]{1,0:T(8,128)(2,1)S(1)}, u32[]{:S(2)}, u32[]{:S(2)}) collective-permute-start(bf16[640,256]{1,0:T(8,128)(2,1)S(1)} %collective-permute-done.kept_ref.refs_0_), channel_id=1, source_target_pairs={{0,16},{16,0},{1,17},{17,1},{2,18},{18,2},{3,19},{19,3},{4,20},{20... | collective-permute-start | bytes 983048 | tf_op jit(solution)/shard_map/ppermute | solution.py:305
  20.2 1.5 %collective-permute-start.2 = (bf16[640,256]{1,0:T(8,128)(2,1)S(1)}, bf16[640,256]{1,0:T(8,128)(2,1)S(1)}, u32[]{:S(2)}, u32[]{:S(2)}) collective-permute-start(bf16[640,256]{1,0:T(8,128)(2,1)S(1)} %collective-permute-done.kept_ref.refs_0_), channel_id=1, source_target_pairs={{0,2},{2,0},{1,3},{3,1},{4,6},{6,4},{5,7},{7,5},{8,10},{10,8},{9,1... | collective-permute-start | bytes 983048 | tf_op jit(solution)/shard_map/ppermute | solution.py:305
  21.7 5.4 %collective-permute-done.4.refs_0_ = bf16[640,256]{1,0:T(8,128)(2,1)S(1)} collective-permute-done((bf16[640,256]{1,0:T(8,128)(2,1)S(1)}, bf16[640,256]{1,0:T(8,128)(2,1)S(1)}, u32[]{:S(2)}, u32[]{:S(2)}) %collective-permute-start.4) | collective-permute-done | bytes 327712 | tf_op jit(solution)/shard_map/ppermute | solution.py:310
  27.1 1.5 %collective-permute-done.3.refs_2_ = bf16[640,256]{1,0:T(8,128)(2,1)S(1)} collective-permute-done((bf16[640,256]{1,0:T(8,128)(2,1)S(1)}, bf16[640,256]{1,0:T(8,128)(2,1)S(1)}, u32[]{:S(2)}, u32[]{:S(2)}) %collective-permute-start.3) | collective-permute-done | bytes 327712 | tf_op jit(solution)/shard_map/ppermute | solution.py:305
  28.5 1.2 %collective-permute-done.2.arrived_ref.refs_1_ = bf16[640,256]{1,0:T(8,128)(2,1)S(1)} collective-permute-done((bf16[640,256]{1,0:T(8,128)(2,1)S(1)}, bf16[640,256]{1,0:T(8,128)(2,1)S(1)}, u32[]{:S(2)}, u32[]{:S(2)}) %collective-permute-start.2) | collective-permute-done | bytes 327712 | tf_op jit(solution)/shard_map/ppermute | solution.py:305
  30.2 1.5 %collective-permute-start.10 = (bf16[640,256]{1,0:T(8,128)(2,1)S(1)}, bf16[640,256]{1,0:T(8,128)(2,1)S(1)}, u32[]{:S(2)}, u32[]{:S(2)}) collective-permute-start(bf16[640,256]{1,0:T(8,128)(2,1)S(1)} %get-tuple-element.65), channel_id=1, source_target_pairs={{0,2},{2,0},{1,3},{3,1},{4,6},{6,4},{5,7},{7,5},{8,10},{10,8},{9,1... | collective-permute-start | bytes 983048 | tf_op jit(solution)/shard_map/ppermute | solution.py:305
  32.7 1.5 %collective-permute-start.9 = (bf16[640,256]{1,0:T(8,128)(2,1)S(1)}, bf16[640,256]{1,0:T(8,128)(2,1)S(1)}, u32[]{:S(2)}, u32[]{:S(2)}) collective-permute-start(bf16[640,256]{1,0:T(8,128)(2,1)S(1)} %collective-permute-done.2.arrived_ref.refs_1_), channel_id=1, source_target_pairs={{0,16},{16,0},{1,17},{17,1},{2,18},{18,2},{3,19},{19,3},{4,20},{20... | collective-permute-start | bytes 983048 | tf_op jit(solution)/shard_map/ppermute | solution.py:305
  34.2 6.6 %collective-permute-done.10.arrived_ref = bf16[640,256]{1,0:T(8,128)(2,1)S(1)} collective-permute-done((bf16[640,256]{1,0:T(8,128)(2,1)S(1)}, bf16[640,256]{1,0:T(8,128)(2,1)S(1)}, u32[]{:S(2)}, u32[]{:S(2)}) %collective-permute-start.10) | collective-permute-done | bytes 327712 | tf_op jit(solution)/shard_map/ppermute | solution.py:305
  40.8 1.5 %collective-permute-done.8.refs_2_ = bf16[640,256]{1,0:T(8,128)(2,1)S(1)} collective-permute-done((bf16[640,256]{1,0:T(8,128)(2,1)S(1)}, bf16[640,256]{1,0:T(8,128)(2,1)S(1)}, u32[]{:S(2)}, u32[]{:S(2)}) %collective-permute-start.8) | collective-permute-done | bytes 327712 | tf_op jit(solution)/shard_map/ppermute | solution.py:305
  42.3 3.4 %collective-permute-done.7.refs_1_ = bf16[640,256]{1,0:T(8,128)(2,1)S(1)} collective-permute-done((bf16[640,256]{1,0:T(8,128)(2,1)S(1)}, bf16[640,256]{1,0:T(8,128)(2,1)S(1)}, u32[]{:S(2)}, u32[]{:S(2)}) %collective-permute-start.7) | collective-permute-done | bytes 327712 | tf_op jit(solution)/shard_map/ppermute | solution.py:305
  48.9 1.5 %collective-permute-start.13 = (bf16[640,256]{1,0:T(8,128)(2,1)S(1)}, bf16[640,256]{1,0:T(8,128)(2,1)S(1)}, u32[]{:S(2)}, u32[]{:S(2)}) collective-permute-start(bf16[640,256]{1,0:T(8,128)(2,1)S(1)} %get-tuple-element.70), channel_id=1, source_target_pairs={{0,2},{2,0},{1,3},{3,1},{4,6},{6,4},{5,7},{7,5},{8,10},{10,8},{9,1... | collective-permute-start | bytes 983048 | tf_op jit(solution)/shard_map/ppermute | solution.py:305
  52.7 4.5 %collective-permute-done.13 = bf16[640,256]{1,0:T(8,128)(2,1)S(1)} collective-permute-done((bf16[640,256]{1,0:T(8,128)(2,1)S(1)}, bf16[640,256]{1,0:T(8,128)(2,1)S(1)}, u32[]{:S(2)}, u32[]{:S(2)}) %collective-permute-start.13) | collective-permute-done | bytes 327712 | tf_op jit(solution)/shard_map/ppermute | solution.py:305
  57.2 7.0 %collective-permute-done.12.refs_3_ = bf16[640,256]{1,0:T(8,128)(2,1)S(1)} collective-permute-done((bf16[640,256]{1,0:T(8,128)(2,1)S(1)}, bf16[640,256]{1,0:T(8,128)(2,1)S(1)}, u32[]{:S(2)}, u32[]{:S(2)}) %collective-permute-start.12) | collective-permute-done | bytes 327712 | tf_op jit(solution)/shard_map/ppermute | solution.py:305
  64.3 5.5 %attention.1 = (bf16[256,1280]{1,0:T(8,128)(2,1)}, bf16[256,512]{1,0:T(8,128)(2,1)S(1)}) custom-call(bf16[256,2560]{1,0:T(8,128)(2,1)S(1)} %get-tuple-element.56.own_ref, bf16[256,2560]{1,0:T(8,128)(2,1)S(1)} %collective-permute-done.5.other_ref, bf16[640,256]{1,0:T(8,128)(2,1)S(1)} %collective-permute-done.4.refs_0_, ...), custom_call_target="tpu_custom_call" | custom-call | flops 838860800 | bytes 5000000 | tf_op jit(solution)/shard_map/attention/pallas_call | solution.py:172
  69.8 3.4 %collective-permute-done.16.arrived_ref = bf16[640,256]{1,0:T(8,128)(2,1)S(1)} collective-permute-done((bf16[640,256]{1,0:T(8,128)(2,1)S(1)}, bf16[640,256]{1,0:T(8,128)(2,1)S(1)}, u32[]{:S(2)}, u32[]{:S(2)}) %collective-permute-start.16) | collective-permute-done | bytes 327712 | tf_op jit(solution)/shard_map/ppermute | solution.py:338
  73.2 1.3 %collective-permute-start.18 = (bf16[256,512]{1,0:T(8,128)(2,1)S(1)}, bf16[256,512]{1,0:T(8,128)(2,1)S(1)}, u32[]{:S(2)}, u32[]{:S(2)}) collective-permute-start(bf16[256,512]{1,0:T(8,128)(2,1)S(1)} %get-tuple-element.89.refs_12_), channel_id=1, source_target_pairs={{0,2},{2,0},{1,3},{3,1},{4,6},{6,4},{5,7},{7,5},{8,10},{10,8},{9,1... | collective-permute-start | bytes 786440 | tf_op jit(solution)/shard_map/ppermute | solution.py:305
  74.5 5.1 %collective-permute-done.18.refs_13_ = bf16[256,512]{1,0:T(8,128)(2,1)S(1)} collective-permute-done((bf16[256,512]{1,0:T(8,128)(2,1)S(1)}, bf16[256,512]{1,0:T(8,128)(2,1)S(1)}, u32[]{:S(2)}, u32[]{:S(2)}) %collective-permute-start.18) | collective-permute-done | bytes 262176 | tf_op jit(solution)/shard_map/ppermute | solution.py:305
  79.5 9.4 %collective-permute-done.17.refs_14_ = bf16[256,512]{1,0:T(8,128)(2,1)S(1)} collective-permute-done((bf16[256,512]{1,0:T(8,128)(2,1)S(1)}, bf16[256,512]{1,0:T(8,128)(2,1)S(1)}, u32[]{:S(2)}, u32[]{:S(2)}) %collective-permute-start.17) | collective-permute-done | bytes 262176 | tf_op jit(solution)/shard_map/ppermute | solution.py:310
  89.5 1.7 %collective-permute-start.21 = (bf16[256,512]{1,0:T(8,128)(2,1)S(1)}, bf16[256,512]{1,0:T(8,128)(2,1)S(1)}, u32[]{:S(2)}, u32[]{:S(2)}) collective-permute-start(bf16[256,512]{1,0:T(8,128)(2,1)S(1)} %collective-permute-done.17.refs_14_), channel_id=1, source_target_pairs={{0,2},{2,0},{1,3},{3,1},{4,6},{6,4},{5,7},{7,5},{8,10},{10,8},{9,1... | collective-permute-start | bytes 786440 | tf_op jit(solution)/shard_map/ppermute | solution.py:305
  91.8 4.0 %collective-permute-done.20.refs_15_ = bf16[256,512]{1,0:T(8,128)(2,1)S(1)} collective-permute-done((bf16[256,512]{1,0:T(8,128)(2,1)S(1)}, bf16[256,512]{1,0:T(8,128)(2,1)S(1)}, u32[]{:S(2)}, u32[]{:S(2)}) %collective-permute-start.20) | collective-permute-done | bytes 262176 | tf_op jit(solution)/shard_map/ppermute | solution.py:310
  95.9 1.7 %collective-permute-start.22 = (bf16[256,512]{1,0:T(8,128)(2,1)S(1)}, bf16[256,512]{1,0:T(8,128)(2,1)S(1)}, u32[]{:S(2)}, u32[]{:S(2)}) collective-permute-start(bf16[256,512]{1,0:T(8,128)(2,1)S(1)} %collective-permute-done.17.refs_14_), channel_id=1, source_target_pairs={{0,4},{4,8},{8,12},{12,0},{1,5},{5,9},{9,13},{13,1},{2,6},{6,10},{... | collective-permute-start | bytes 786440 | tf_op jit(solution)/shard_map/ppermute | solution.py:310
  97.6 2.2 %collective-permute-start.23 = (bf16[256,512]{1,0:T(8,128)(2,1)S(1)}, bf16[256,512]{1,0:T(8,128)(2,1)S(1)}, u32[]{:S(2)}, u32[]{:S(2)}) collective-permute-start(bf16[256,512]{1,0:T(8,128)(2,1)S(1)} %collective-permute-done.20.refs_15_), channel_id=1, source_target_pairs={{0,2},{2,0},{1,3},{3,1},{4,6},{6,4},{5,7},{7,5},{8,10},{10,8},{9,1... | collective-permute-start | bytes 786440 | tf_op jit(solution)/shard_map/ppermute | solution.py:305
  99.8 4.3 %collective-permute-done.22.refs_4_ = bf16[256,512]{1,0:T(8,128)(2,1)S(1)} collective-permute-done((bf16[256,512]{1,0:T(8,128)(2,1)S(1)}, bf16[256,512]{1,0:T(8,128)(2,1)S(1)}, u32[]{:S(2)}, u32[]{:S(2)}) %collective-permute-start.22) | collective-permute-done | bytes 262176 | tf_op jit(solution)/shard_map/ppermute | solution.py:310
  104.1 2.1 %collective-permute-done.23.refs_17_ = bf16[256,512]{1,0:T(8,128)(2,1)S(1)} collective-permute-done((bf16[256,512]{1,0:T(8,128)(2,1)S(1)}, bf16[256,512]{1,0:T(8,128)(2,1)S(1)}, u32[]{:S(2)}, u32[]{:S(2)}) %collective-permute-start.23) | collective-permute-done | bytes 262176 | tf_op jit(solution)/shard_map/ppermute | solution.py:305
  106.1 2.5 %collective-permute-start.24 = (bf16[256,512]{1,0:T(8,128)(2,1)S(1)}, bf16[256,512]{1,0:T(8,128)(2,1)S(1)}, u32[]{:S(2)}, u32[]{:S(2)}) collective-permute-start(bf16[256,512]{1,0:T(8,128)(2,1)S(1)} %collective-permute-done.22.refs_4_), channel_id=1, source_target_pairs={{0,2},{2,0},{1,3},{3,1},{4,6},{6,4},{5,7},{7,5},{8,10},{10,8},{9,1... | collective-permute-start | bytes 786440 | tf_op jit(solution)/shard_map/ppermute | solution.py:305
  108.6 1.7 %gradient.2 = (f32[2,640,256]{2,1,0:T(8,128)S(1)}, f32[2,256]{1,0:T(2,128)S(1)}) custom-call(bf16[2,640,256]{2,1,0:T(8,128)(2,1)S(1)} %collective-permute-done.14.refs_0_.refs_1_, bf16[2,640,256]{2,1,0:T(8,128)(2,1)S(1)} %collective-permute-done.14.refs_0_.refs_1_, bf16[2,640,256]{2,1,0:T(8,128)(2,1)S(1)} %pack.5.refs_2_.refs_3_.refs_4_.refs_5_, ...), custom_call_target="tpu_custom_call" | custom-call | flops 1006632960 | bytes 5000000 | tf_op jit(solution)/shard_map/gradient/pallas_call | solution.py:237
  110.4 2.6 %collective-permute-done.24.refs_5_ = bf16[256,512]{1,0:T(8,128)(2,1)S(1)} collective-permute-done((bf16[256,512]{1,0:T(8,128)(2,1)S(1)}, bf16[256,512]{1,0:T(8,128)(2,1)S(1)}, u32[]{:S(2)}, u32[]{:S(2)}) %collective-permute-start.24) | collective-permute-done | bytes 262176 | tf_op jit(solution)/shard_map/ppermute | solution.py:305
  113.0 1.7 %gradient.3 = (f32[2,640,256]{2,1,0:T(8,128)}, f32[2,256]{1,0:T(2,128)}) custom-call(bf16[2,640,256]{2,1,0:T(8,128)(2,1)S(1)} %collective-permute-done.14.refs_0_.refs_1_, bf16[2,640,256]{2,1,0:T(8,128)(2,1)S(1)} %collective-permute-done.14.refs_0_.refs_1_, bf16[2,640,256]{2,1,0:T(8,128)(2,1)S(1)} %collective-permute-done.19.refs_6_.refs_7_.refs_2_.refs_3_, ...), custom_call_target="tpu_custom_call" | custom-call | flops 335544320 | bytes 5000000 | tf_op jit(solution)/shard_map/gradient/pallas_call | solution.py:237
  (51 shorter events, 10.9 us)
Async XLA Ops:
  0.6 6.2 %copy-start = (bf16[256,2560]{1,0:T(8,128)(2,1)S(1)}, bf16[256,2560]{1,0:T(8,128)(2,1)}, u32[]{:S(2)}) copy-start(bf16[256,2560]{1,0:T(8,128)(2,1)} %values_ref.1) | copy-start | bytes 3932164
  0.6 5.9 %copy-start.4 = (bf16[5120]{0:T(1024)(128)(2,1)S(1)}, bf16[5120]{0:T(1024)(128)(2,1)}, u32[]{:S(2)}) copy-start(bf16[5120]{0:T(1024)(128)(2,1)} %param.7) | copy-start | bytes 30724
  2.4 4.3 %collective-permute-start.1 = (f32[256,1]{0,1:T(1,128)S(1)}, f32[256,1]{0,1:T(1,128)S(1)}, u32[]{:S(2)}, u32[]{:S(2)}) collective-permute-start(f32[256,1]{0,1:T(1,128)S(1)} %bitcast.3), channel_id=1, source_target_pairs={{0,1},{1,0},{2,3},{3,2},{4,5},{5,4},{6,7},{7,6},{8,9},{9,8},{10,11... | collective-permute-start | bytes 3080 | tf_op jit(solution)/shard_map/ppermute | solution.py:305
  3.9 13.0 %collective-permute-start = (bf16[640,256]{1,0:T(8,128)(2,1)S(1)}, bf16[640,256]{1,0:T(8,128)(2,1)S(1)}, u32[]{:S(2)}, u32[]{:S(2)}) collective-permute-start(bf16[640,256]{1,0:T(8,128)(2,1)S(1)} %dynamic-slice_bitcast_fusion), channel_id=1, source_target_pairs={{0,4},{4,8},{8,12},{12,0},{1,5},{5,9},{9,13},{13,1},{2,6},{6,10},{... | collective-permute-start | bytes 983048 | tf_op jit(solution)/shard_map/ppermute | solution.py:310
  17.0 12.8 %collective-permute-start.5 = (bf16[256,2560]{1,0:T(8,128)(2,1)S(1)}, bf16[256,2560]{1,0:T(8,128)(2,1)S(1)}, u32[]{:S(2)}, u32[]{:S(2)}) collective-permute-start(bf16[256,2560]{1,0:T(8,128)(2,1)S(1)} %get-tuple-element.56.own_ref), channel_id=1, source_target_pairs={{0,1},{1,0},{2,3},{3,2},{4,5},{5,4},{6,7},{7,6},{8,9},{9,8},{10,11... | collective-permute-start | bytes 3932168 | tf_op jit(solution)/shard_map/ppermute | solution.py:305
  17.0 10.1 %collective-permute-start.4 = (bf16[640,256]{1,0:T(8,128)(2,1)S(1)}, bf16[640,256]{1,0:T(8,128)(2,1)S(1)}, u32[]{:S(2)}, u32[]{:S(2)}) collective-permute-start(bf16[640,256]{1,0:T(8,128)(2,1)S(1)} %dynamic-slice_bitcast_fusion), channel_id=1, source_target_pairs={{0,12},{4,0},{8,4},{12,8},{1,13},{5,1},{9,5},{13,9},{2,14},{6,2},{... | collective-permute-start | bytes 983048 | tf_op jit(solution)/shard_map/ppermute | solution.py:310
  18.7 9.8 %collective-permute-start.3 = (bf16[640,256]{1,0:T(8,128)(2,1)S(1)}, bf16[640,256]{1,0:T(8,128)(2,1)S(1)}, u32[]{:S(2)}, u32[]{:S(2)}) collective-permute-start(bf16[640,256]{1,0:T(8,128)(2,1)S(1)} %collective-permute-done.kept_ref.refs_0_), channel_id=1, source_target_pairs={{0,16},{16,0},{1,17},{17,1},{2,18},{18,2},{3,19},{19,3},{4,20},{20... | collective-permute-start | bytes 983048 | tf_op jit(solution)/shard_map/ppermute | solution.py:305
  20.2 9.6 %collective-permute-start.2 = (bf16[640,256]{1,0:T(8,128)(2,1)S(1)}, bf16[640,256]{1,0:T(8,128)(2,1)S(1)}, u32[]{:S(2)}, u32[]{:S(2)}) collective-permute-start(bf16[640,256]{1,0:T(8,128)(2,1)S(1)} %collective-permute-done.kept_ref.refs_0_), channel_id=1, source_target_pairs={{0,2},{2,0},{1,3},{3,1},{4,6},{6,4},{5,7},{7,5},{8,10},{10,8},{9,1... | collective-permute-start | bytes 983048 | tf_op jit(solution)/shard_map/ppermute | solution.py:305
  29.8 21.8 %copy-start.1 = (bf16[2,1280,256]{2,1,0:T(8,128)(2,1)S(1)}, bf16[2,1280,256]{2,1,0:T(8,128)(2,1)}, u32[]{:S(2)}) copy-start(bf16[2,1280,256]{2,1,0:T(8,128)(2,1)} %weight_ref.1) | copy-start | bytes 3932164
  29.8 17.6 %collective-permute-start.6 = (bf16[2,640,256]{2,1,0:T(8,128)(2,1)S(1)}, bf16[2,640,256]{2,1,0:T(8,128)(2,1)S(1)}, u32[]{:S(2)}, u32[]{:S(2)}) collective-permute-start(bf16[2,640,256]{2,1,0:T(8,128)(2,1)S(1)} %pack.3), channel_id=1, source_target_pairs={{0,4},{4,8},{8,12},{12,0},{1,5},{5,9},{9,13},{13,1},{2,6},{6,10},{... | collective-permute-start | bytes 1966088 | tf_op jit(solution)/shard_map/ppermute | solution.py:310
  30.2 10.6 %collective-permute-start.10 = (bf16[640,256]{1,0:T(8,128)(2,1)S(1)}, bf16[640,256]{1,0:T(8,128)(2,1)S(1)}, u32[]{:S(2)}, u32[]{:S(2)}) collective-permute-start(bf16[640,256]{1,0:T(8,128)(2,1)S(1)} %get-tuple-element.65), channel_id=1, source_target_pairs={{0,2},{2,0},{1,3},{3,1},{4,6},{6,4},{5,7},{7,5},{8,10},{10,8},{9,1... | collective-permute-start | bytes 983048 | tf_op jit(solution)/shard_map/ppermute | solution.py:305
  31.7 10.6 %collective-permute-start.8 = (bf16[640,256]{1,0:T(8,128)(2,1)S(1)}, bf16[640,256]{1,0:T(8,128)(2,1)S(1)}, u32[]{:S(2)}, u32[]{:S(2)}) collective-permute-start(bf16[640,256]{1,0:T(8,128)(2,1)S(1)} %collective-permute-done.4.refs_0_), channel_id=1, source_target_pairs={{0,16},{16,0},{1,17},{17,1},{2,18},{18,2},{3,19},{19,3},{4,20},{20... | collective-permute-start | bytes 983048 | tf_op jit(solution)/shard_map/ppermute | solution.py:305
  32.2 13.5 %collective-permute-start.7 = (bf16[640,256]{1,0:T(8,128)(2,1)S(1)}, bf16[640,256]{1,0:T(8,128)(2,1)S(1)}, u32[]{:S(2)}, u32[]{:S(2)}) collective-permute-start(bf16[640,256]{1,0:T(8,128)(2,1)S(1)} %collective-permute-done.4.refs_0_), channel_id=1, source_target_pairs={{0,2},{2,0},{1,3},{3,1},{4,6},{6,4},{5,7},{7,5},{8,10},{10,8},{9,1... | collective-permute-start | bytes 983048 | tf_op jit(solution)/shard_map/ppermute | solution.py:305
  32.7 14.2 %collective-permute-start.9 = (bf16[640,256]{1,0:T(8,128)(2,1)S(1)}, bf16[640,256]{1,0:T(8,128)(2,1)S(1)}, u32[]{:S(2)}, u32[]{:S(2)}) collective-permute-start(bf16[640,256]{1,0:T(8,128)(2,1)S(1)} %collective-permute-done.2.arrived_ref.refs_1_), channel_id=1, source_target_pairs={{0,16},{16,0},{1,17},{17,1},{2,18},{18,2},{3,19},{19,3},{4,20},{20... | collective-permute-start | bytes 983048 | tf_op jit(solution)/shard_map/ppermute | solution.py:305
  47.5 16.8 %collective-permute-start.14 = (bf16[2,640,256]{2,1,0:T(8,128)(2,1)S(1)}, bf16[2,640,256]{2,1,0:T(8,128)(2,1)S(1)}, u32[]{:S(2)}, u32[]{:S(2)}) collective-permute-start(bf16[2,640,256]{2,1,0:T(8,128)(2,1)S(1)} %pack.4), channel_id=1, source_target_pairs={{0,0},{1,8},{4,4},{5,12},{8,1},{9,9},{12,5},{13,13},{2,2},{3,10},{... | collective-permute-start | bytes 1966088 | tf_op jit(solution)/shard_map/ppermute | solution.py:338
  48.2 16.1 %collective-permute-start.11 = (bf16[2,640,256]{2,1,0:T(8,128)(2,1)S(1)}, bf16[2,640,256]{2,1,0:T(8,128)(2,1)S(1)}, u32[]{:S(2)}, u32[]{:S(2)}) collective-permute-start(bf16[2,640,256]{2,1,0:T(8,128)(2,1)S(1)} %collective-permute-done.6.refs_4_), channel_id=1, source_target_pairs={{0,16},{16,0},{1,17},{17,1},{2,18},{18,2},{3,19},{19,3},{4,20},{20... | collective-permute-start | bytes 1966088 | tf_op jit(solution)/shard_map/ppermute | solution.py:305
  48.9 8.3 %collective-permute-start.13 = (bf16[640,256]{1,0:T(8,128)(2,1)S(1)}, bf16[640,256]{1,0:T(8,128)(2,1)S(1)}, u32[]{:S(2)}, u32[]{:S(2)}) collective-permute-start(bf16[640,256]{1,0:T(8,128)(2,1)S(1)} %get-tuple-element.70), channel_id=1, source_target_pairs={{0,2},{2,0},{1,3},{3,1},{4,6},{6,4},{5,7},{7,5},{8,10},{10,8},{9,1... | collective-permute-start | bytes 983048 | tf_op jit(solution)/shard_map/ppermute | solution.py:305
  50.4 13.9 %collective-permute-start.12 = (bf16[640,256]{1,0:T(8,128)(2,1)S(1)}, bf16[640,256]{1,0:T(8,128)(2,1)S(1)}, u32[]{:S(2)}, u32[]{:S(2)}) collective-permute-start(bf16[640,256]{1,0:T(8,128)(2,1)S(1)} %collective-permute-done.8.refs_2_), channel_id=1, source_target_pairs={{0,2},{2,0},{1,3},{3,1},{4,6},{6,4},{5,7},{7,5},{8,10},{10,8},{9,1... | collective-permute-start | bytes 983048 | tf_op jit(solution)/shard_map/ppermute | solution.py:305
  51.5 12.7 %copy-start.5 = (bf16[2,256]{1,0:T(2,128)(2,1)S(1)}, bf16[2,256]{1,0:T(2,128)(2,1)}, u32[]{:S(2)}) copy-start(bf16[2,256]{1,0:T(2,128)(2,1)} %param.11) | copy-start | bytes 3076
  51.6 12.7 %copy-start.2 = (bf16[256,1280]{1,0:T(8,128)(2,1)S(1)}, bf16[256,1280]{1,0:T(8,128)(2,1)}, u32[]{:S(2)}) copy-start(bf16[256,1280]{1,0:T(8,128)(2,1)} %refs_10_.1) | copy-start | bytes 1966084
  51.6 12.7 %copy-start.3 = (bf16[256,1280]{1,0:T(8,128)(2,1)S(1)}, bf16[256,1280]{1,0:T(8,128)(2,1)}, u32[]{:S(2)}) copy-start(bf16[256,1280]{1,0:T(8,128)(2,1)} %refs_11_.1) | copy-start | bytes 1966084
  51.6 18.2 %collective-permute-start.15 = (bf16[640,256]{1,0:T(8,128)(2,1)S(1)}, bf16[640,256]{1,0:T(8,128)(2,1)S(1)}, u32[]{:S(2)}, u32[]{:S(2)}) collective-permute-start(bf16[640,256]{1,0:T(8,128)(2,1)S(1)} %get-tuple-element.82), channel_id=1, source_target_pairs={{0,4},{1,12},{4,0},{5,8},{8,5},{9,13},{12,1},{13,9},{2,6},{3,14},{... | collective-permute-start | bytes 983048 | tf_op jit(solution)/shard_map/ppermute | solution.py:338
  64.2 8.9 %collective-permute-start.16 = (bf16[640,256]{1,0:T(8,128)(2,1)S(1)}, bf16[640,256]{1,0:T(8,128)(2,1)S(1)}, u32[]{:S(2)}, u32[]{:S(2)}) collective-permute-start(bf16[640,256]{1,0:T(8,128)(2,1)S(1)} %collective-permute-done.13), channel_id=1, source_target_pairs={{0,4},{1,12},{4,0},{5,8},{8,5},{9,13},{12,1},{13,9},{2,6},{3,14},{... | collective-permute-start | bytes 983048 | tf_op jit(solution)/shard_map/ppermute | solution.py:338
  73.2 6.4 %collective-permute-start.18 = (bf16[256,512]{1,0:T(8,128)(2,1)S(1)}, bf16[256,512]{1,0:T(8,128)(2,1)S(1)}, u32[]{:S(2)}, u32[]{:S(2)}) collective-permute-start(bf16[256,512]{1,0:T(8,128)(2,1)S(1)} %get-tuple-element.89.refs_12_), channel_id=1, source_target_pairs={{0,2},{2,0},{1,3},{3,1},{4,6},{6,4},{5,7},{7,5},{8,10},{10,8},{9,1... | collective-permute-start | bytes 786440 | tf_op jit(solution)/shard_map/ppermute | solution.py:305
  74.5 14.5 %collective-permute-start.17 = (bf16[256,512]{1,0:T(8,128)(2,1)S(1)}, bf16[256,512]{1,0:T(8,128)(2,1)S(1)}, u32[]{:S(2)}, u32[]{:S(2)}) collective-permute-start(bf16[256,512]{1,0:T(8,128)(2,1)S(1)} %get-tuple-element.89.refs_12_), channel_id=1, source_target_pairs={{0,4},{4,8},{8,12},{12,0},{1,5},{5,9},{9,13},{13,1},{2,6},{6,10},{... | collective-permute-start | bytes 786440 | tf_op jit(solution)/shard_map/ppermute | solution.py:310
  88.9 6.9 %collective-permute-start.20 = (bf16[256,512]{1,0:T(8,128)(2,1)S(1)}, bf16[256,512]{1,0:T(8,128)(2,1)S(1)}, u32[]{:S(2)}, u32[]{:S(2)}) collective-permute-start(bf16[256,512]{1,0:T(8,128)(2,1)S(1)} %get-tuple-element.89.refs_12_), channel_id=1, source_target_pairs={{0,12},{4,0},{8,4},{12,8},{1,13},{5,1},{9,5},{13,9},{2,14},{6,2},{... | collective-permute-start | bytes 786440 | tf_op jit(solution)/shard_map/ppermute | solution.py:310
  89.5 6.4 %collective-permute-start.21 = (bf16[256,512]{1,0:T(8,128)(2,1)S(1)}, bf16[256,512]{1,0:T(8,128)(2,1)S(1)}, u32[]{:S(2)}, u32[]{:S(2)}) collective-permute-start(bf16[256,512]{1,0:T(8,128)(2,1)S(1)} %collective-permute-done.17.refs_14_), channel_id=1, source_target_pairs={{0,2},{2,0},{1,3},{3,1},{4,6},{6,4},{5,7},{7,5},{8,10},{10,8},{9,1... | collective-permute-start | bytes 786440 | tf_op jit(solution)/shard_map/ppermute | solution.py:305
  91.3 17.4 %collective-permute-start.25 = (bf16[2,640,256]{2,1,0:T(8,128)(2,1)S(1)}, bf16[2,640,256]{2,1,0:T(8,128)(2,1)S(1)}, u32[]{:S(2)}, u32[]{:S(2)}) collective-permute-start(bf16[2,640,256]{2,1,0:T(8,128)(2,1)S(1)} %pack.5.refs_2_.refs_3_.refs_4_.refs_5_), channel_id=1, source_target_pairs={{0,1},{1,0},{2,3},{3,2},{4,5},{5,4},{6,7},{7,6},{8,9},{9,8},{10,11... | collective-permute-start | bytes 1966088 | tf_op jit(solution)/shard_map/ppermute | solution.py:305
  91.4 17.3 %collective-permute-start.19 = (bf16[2,640,256]{2,1,0:T(8,128)(2,1)S(1)}, bf16[2,640,256]{2,1,0:T(8,128)(2,1)S(1)}, u32[]{:S(2)}, u32[]{:S(2)}) collective-permute-start(bf16[2,640,256]{2,1,0:T(8,128)(2,1)S(1)} %collective-permute-done.14.refs_0_.refs_1_), channel_id=1, source_target_pairs={{0,1},{1,0},{2,3},{3,2},{4,5},{5,4},{6,7},{7,6},{8,9},{9,8},{10,11... | collective-permute-start | bytes 1966088 | tf_op jit(solution)/shard_map/ppermute | solution.py:305
  95.9 8.2 %collective-permute-start.22 = (bf16[256,512]{1,0:T(8,128)(2,1)S(1)}, bf16[256,512]{1,0:T(8,128)(2,1)S(1)}, u32[]{:S(2)}, u32[]{:S(2)}) collective-permute-start(bf16[256,512]{1,0:T(8,128)(2,1)S(1)} %collective-permute-done.17.refs_14_), channel_id=1, source_target_pairs={{0,4},{4,8},{8,12},{12,0},{1,5},{5,9},{9,13},{13,1},{2,6},{6,10},{... | collective-permute-start | bytes 786440 | tf_op jit(solution)/shard_map/ppermute | solution.py:310
  97.6 8.6 %collective-permute-start.23 = (bf16[256,512]{1,0:T(8,128)(2,1)S(1)}, bf16[256,512]{1,0:T(8,128)(2,1)S(1)}, u32[]{:S(2)}, u32[]{:S(2)}) collective-permute-start(bf16[256,512]{1,0:T(8,128)(2,1)S(1)} %collective-permute-done.20.refs_15_), channel_id=1, source_target_pairs={{0,2},{2,0},{1,3},{3,1},{4,6},{6,4},{5,7},{7,5},{8,10},{10,8},{9,1... | collective-permute-start | bytes 786440 | tf_op jit(solution)/shard_map/ppermute | solution.py:305
  106.1 6.8 %collective-permute-start.24 = (bf16[256,512]{1,0:T(8,128)(2,1)S(1)}, bf16[256,512]{1,0:T(8,128)(2,1)S(1)}, u32[]{:S(2)}, u32[]{:S(2)}) collective-permute-start(bf16[256,512]{1,0:T(8,128)(2,1)S(1)} %collective-permute-done.22.refs_4_), channel_id=1, source_target_pairs={{0,2},{2,0},{1,3},{3,1},{4,6},{6,4},{5,7},{7,5},{8,10},{10,8},{9,1... | collective-permute-start | bytes 786440 | tf_op jit(solution)/shard_map/ppermute | solution.py:305

commit v17 on v11

--- a/solution.py
+++ b/solution.py
@@ -141,14 +141,18 @@
         )
 
 
-def attention_kernel(
-    distance, own_ref, other_ref, p0, p1, p2, p3, sums_ref, bias_ref, cosine_ref, sine_ref,
-    queries_ref, cotangent_ref, grad_query_ref, pair_ref, raw_ref,
-):
+def attention_kernel(distances, own_ref, other_ref, *refs):
+    pieces, refs = refs[: 4 * len(distances)], refs[4 * len(distances) :]
+    sums_ref, bias_ref, cosine_ref, sine_ref, queries_ref, cotangent_ref = refs[:6]
+    grad_query_ref, pair_ref, raw_ref = refs[6:]
     group = lax.axis_index("groups")
-    terms = block_terms(own_ref, other_ref, block_from(distance), (p0, p1, p2, p3))
-    raw_ref[group] = sums_ref[group] + terms[0]
-    raw_ref[1 - group] = sums_ref[1 - group] + terms[1]
+    totals = [sums_ref[group], sums_ref[1 - group]]
+    for at, distance in enumerate(distances):
+        four = pieces[4 * at : 4 * at + 4]
+        terms = block_terms(own_ref, other_ref, block_from(distance), four)
+        totals = [total + term for total, term in zip(totals, terms)]
+    raw_ref[group] = totals[0]
+    raw_ref[1 - group] = totals[1]
 
     def raw_of(j, lanes):
         return raw_ref[j, :, lanes] + bias_ref[j : j + 1, lanes]
@@ -158,12 +162,14 @@
     )
 
 
-def attention(distance, normed, normed_other, pieces, sums, bias, cosine, sine, queries, cotangent):
+def attention(gathered, normed, normed_other, sums, bias, cosine, sine, queries, cotangent):
     length = normed.shape[0]
+    distances = tuple(distance for distance, _ in gathered)
+    pieces = [piece for _, four in gathered for piece in four]
     columns = pieces[0].shape[1]
     operands = (normed, normed_other, *pieces, sums, bias, cosine, sine, queries, cotangent)
     return pl.pallas_call(
-        functools.partial(attention_kernel, distance),
+        functools.partial(attention_kernel, distances),
         in_specs=[IN_VMEM] * len(operands),
         out_specs=[IN_VMEM] * 2,
         scratch_shapes=[pltpu.VMEM(sums.shape, jnp.float32)],
@@ -374,24 +380,24 @@
     up, up_y, down, normed_other = lax.optimization_barrier((up, up_y, down, normed_other))
     up_x, down_y = swapped(up, "dp"), swapped(down, "groups")
     twice = turned(up, "blk", 1)
-    twice, down, down_y, up_x, arrived = lax.optimization_barrier(
-        (twice, down, down_y, up_x, arrived)
-    )
-    down_x, twice_x = swapped(down, "dp"), swapped(twice, "dp")
-    twice_y, up_both = swapped(twice, "groups"), swapped(up_x, "groups")
+    twice, down, down_y, arrived = lax.optimization_barrier((twice, down, down_y, arrived))
+    twice_x, twice_y = swapped(twice, "dp"), swapped(twice, "groups")
+    up_x, down = lax.optimization_barrier((up_x, down))
+    down_x, up_both = swapped(down, "dp"), swapped(up_x, "groups")
     even, odd = pack(kept, arrived)
     even = sent_along(even, 0)
-    twice_x, twice_y, up_both, down_x, even = lax.optimization_barrier(
-        (twice_x, twice_y, up_both, down_x, even)
+    twice_x, twice_y, up_both, down_x = lax.optimization_barrier(
+        (twice_x, twice_y, up_both, down_x)
     )
     down_both, twice_both = swapped(down_x, "groups"), swapped(twice_y, "dp")
     odd = sent_along(after(odd, even), 1)
-
-    gathered = [(1, (up, up_x, up_y, up_both)), (-1, (down, down_x, down_y, down_both))]
-    sums = project(normed, normed_other, kv_weight, gathered)
+    sums = project(normed, normed_other, kv_weight, [(1, (up, up_x, up_y, up_both))])
+    gathered = [
+        (-1, (down, down_x, down_y, down_both)),
+        (2, (twice, twice_x, twice_y, twice_both)),
+    ]
     grad_query, grad_pair = attention(
-        2, normed, normed_other, (twice, twice_x, twice_y, twice_both), sums, bias, cosine, sine,
-        queries, cotangent,
+        gathered, normed, normed_other, sums, bias, cosine, sine, queries, cotangent
     )
 
     grad_pair, odd = lax.optimization_barrier((grad_pair, odd))

time: 112 us -> 117 us (1.045)
  starting transfers between devices: 26.2 us -> 28.9 us
  waiting for transfers between devices: 70.1 us -> 72.1 us
    ppermute x6, waiting for transfers between devices: 24.7 us -> 28.1 us  [turned(): lax.ppermute(block, axis, [(i, (i + distance) % size) for i in range(size)])]
    ppermute x18, starting transfers between devices: 17.7 us -> 19.7 us  [swapped(): return lax.ppermute(block, axis, [(0, 1), (1, 0)])]
    ppermute x6, starting transfers between devices: 7.19 us -> 8.51 us  [turned(): lax.ppermute(block, axis, [(i, (i + distance) % size) for i in range(size)])]
  transfers between devices with their start and end apart: 26 -> 26, of which waited for: 17 -> 18; matrix products, arithmetic and copies ran while one was open for 2% -> 2% of each run, Pallas kernels for 8% -> 8%
where the time goes in v17:
time: 117 us
  waiting for transfers between devices  72.1 us (62%)
  starting transfers between devices  28.9 us (25%)
  Pallas kernels  11.1 us (9%)
  other arithmetic  2.5 us (2%)
  local copies, waits for them, and re-layouts  1.19 us (1%)
    ppermute x18, waiting for transfers between devices, swapped(): return lax.ppermute(block, axis, [(0, 1), (1, 0)])  44 us
    ppermute x6, waiting for transfers between devices, turned(): lax.ppermute(block, axis, [(i, (i + distance) % size) for i in range(size)])  28.1 us
    ppermute x18, starting transfers between devices, swapped(): return lax.ppermute(block, axis, [(0, 1), (1, 0)])  19.7 us
    ppermute x6, starting transfers between devices, turned(): lax.ppermute(block, axis, [(i, (i + distance) % size) for i in range(size)])  8.51 us
    pallas_call x1, Pallas kernels, attention(): pl.pallas_call(functools.partial(attention_kernel, distances), in_specs=[...  5.52 us
    pallas_call x2, Pallas kernels, gradient(): pl.pallas_call(functools.partial(gradient_kernel, tuple(some), sums is No...  3.49 us
  transfers between devices with their start and end apart: 26, of which 18 were waited for; matrix products, arithmetic and copies ran while one was open for 2% of the time, Pallas kernels for 8%

profile of v17, /device:TPU:0, one launch (start us, length us, event | category | flops | bytes accessed | tf_op | source)
XLA Modules:
  0.0 116.5 jit_solution(15222165885532150948)
XLA Ops:
  0.6 1.8 %multiply_reduce_fusion = f32[256]{0:T(256)S(1)} fusion(bf16[256,2560]{1,0:T(8,128)(2,1)} %values_ref.1), kind=kLoop, calls=%fused_computation | loop fusion | flops 1965824 | bytes 1311744 | tf_op jit(solution)/shard_map/reduce_sum | solution.py:347
  3.9 2.7 %collective-permute-start = (bf16[640,256]{1,0:T(8,128)(2,1)S(1)}, bf16[640,256]{1,0:T(8,128)(2,1)S(1)}, u32[]{:S(2)}, u32[]{:S(2)}) collective-permute-start(bf16[640,256]{1,0:T(8,128)(2,1)S(1)} %dynamic-slice_bitcast_fusion), channel_id=1, source_target_pairs={{0,4},{4,8},{8,12},{12,0},{1,5},{5,9},{9,13},{13,1},{2,6},{6,10},{... | collective-permute-start | bytes 983048 | tf_op jit(solution)/shard_map/ppermute | solution.py:312
  7.8 9.1 %collective-permute-done.refs_0_ = bf16[640,256]{1,0:T(8,128)(2,1)S(1)} collective-permute-done((bf16[640,256]{1,0:T(8,128)(2,1)S(1)}, bf16[640,256]{1,0:T(8,128)(2,1)S(1)}, u32[]{:S(2)}, u32[]{:S(2)}) %collective-permute-start) | collective-permute-done | bytes 327712 | tf_op jit(solution)/shard_map/ppermute | solution.py:312
  17.0 1.7 %collective-permute-start.3 = (bf16[640,256]{1,0:T(8,128)(2,1)S(1)}, bf16[640,256]{1,0:T(8,128)(2,1)S(1)}, u32[]{:S(2)}, u32[]{:S(2)}) collective-permute-start(bf16[640,256]{1,0:T(8,128)(2,1)S(1)} %dynamic-slice_bitcast_fusion), channel_id=1, source_target_pairs={{0,12},{4,0},{8,4},{12,8},{1,13},{5,1},{9,5},{13,9},{2,14},{6,2},{... | collective-permute-start | bytes 983048 | tf_op jit(solution)/shard_map/ppermute | solution.py:312
  18.7 1.5 %collective-permute-start.2 = (bf16[640,256]{1,0:T(8,128)(2,1)S(1)}, bf16[640,256]{1,0:T(8,128)(2,1)S(1)}, u32[]{:S(2)}, u32[]{:S(2)}) collective-permute-start(bf16[640,256]{1,0:T(8,128)(2,1)S(1)} %collective-permute-done.refs_0_), channel_id=1, source_target_pairs={{0,16},{16,0},{1,17},{17,1},{2,18},{18,2},{3,19},{19,3},{4,20},{20... | collective-permute-start | bytes 983048 | tf_op jit(solution)/shard_map/ppermute | solution.py:307
  20.2 1.5 %collective-permute-start.8 = (bf16[2,640,256]{2,1,0:T(8,128)(2,1)S(1)}, bf16[2,640,256]{2,1,0:T(8,128)(2,1)S(1)}, u32[]{:S(2)}, u32[]{:S(2)}) collective-permute-start(bf16[2,640,256]{2,1,0:T(8,128)(2,1)S(1)} %get-tuple-element.51), channel_id=1, source_target_pairs={{0,2},{2,0},{1,3},{3,1},{4,6},{6,4},{5,7},{7,5},{8,10},{10,8},{9,1... | collective-permute-start | bytes 1966088 | tf_op jit(solution)/shard_map/ppermute | solution.py:307
  21.7 5.4 %collective-permute-done.3.refs_0_ = bf16[640,256]{1,0:T(8,128)(2,1)S(1)} collective-permute-done((bf16[640,256]{1,0:T(8,128)(2,1)S(1)}, bf16[640,256]{1,0:T(8,128)(2,1)S(1)}, u32[]{:S(2)}, u32[]{:S(2)}) %collective-permute-start.3) | collective-permute-done | bytes 327712 | tf_op jit(solution)/shard_map/ppermute | solution.py:312
  27.1 1.5 %collective-permute-done.2.refs_2_ = bf16[640,256]{1,0:T(8,128)(2,1)S(1)} collective-permute-done((bf16[640,256]{1,0:T(8,128)(2,1)S(1)}, bf16[640,256]{1,0:T(8,128)(2,1)S(1)}, u32[]{:S(2)}, u32[]{:S(2)}) %collective-permute-start.2) | collective-permute-done | bytes 327712 | tf_op jit(solution)/shard_map/ppermute | solution.py:307
  28.5 1.5 %collective-permute-start.7 = (bf16[640,256]{1,0:T(8,128)(2,1)S(1)}, bf16[640,256]{1,0:T(8,128)(2,1)S(1)}, u32[]{:S(2)}, u32[]{:S(2)}) collective-permute-start(bf16[640,256]{1,0:T(8,128)(2,1)S(1)} %collective-permute-done.3.refs_0_), channel_id=1, source_target_pairs={{0,16},{16,0},{1,17},{17,1},{2,18},{18,2},{3,19},{19,3},{4,20},{20... | collective-permute-start | bytes 983048 | tf_op jit(solution)/shard_map/ppermute | solution.py:307
  30.4 6.5 %collective-permute-done.8.arrived_ref = bf16[2,640,256]{2,1,0:T(8,128)(2,1)S(1)} collective-permute-done((bf16[2,640,256]{2,1,0:T(8,128)(2,1)S(1)}, bf16[2,640,256]{2,1,0:T(8,128)(2,1)S(1)}, u32[]{:S(2)}, u32[]{:S(2)}) %collective-permute-start.8) | collective-permute-done | bytes 655392 | tf_op jit(solution)/shard_map/ppermute | solution.py:307
  37.6 3.0 %collective-permute-done.6.refs_4_ = bf16[640,256]{1,0:T(8,128)(2,1)S(1)} collective-permute-done((bf16[640,256]{1,0:T(8,128)(2,1)S(1)}, bf16[640,256]{1,0:T(8,128)(2,1)S(1)}, u32[]{:S(2)}, u32[]{:S(2)}) %collective-permute-start.6) | collective-permute-done | bytes 327712 | tf_op jit(solution)/shard_map/ppermute | solution.py:312
  41.4 1.6 %collective-permute-start.5 = (bf16[640,256]{1,0:T(8,128)(2,1)S(1)}, bf16[640,256]{1,0:T(8,128)(2,1)S(1)}, u32[]{:S(2)}, u32[]{:S(2)}) collective-permute-start(bf16[640,256]{1,0:T(8,128)(2,1)S(1)} %collective-permute-done.refs_0_), channel_id=1, source_target_pairs={{0,2},{2,0},{1,3},{3,1},{4,6},{6,4},{5,7},{7,5},{8,10},{10,8},{9,1... | collective-permute-start | bytes 983048 | tf_op jit(solution)/shard_map/ppermute | solution.py:307
  44.0 8.0 %collective-permute-done.5.refs_1_ = bf16[640,256]{1,0:T(8,128)(2,1)S(1)} collective-permute-done((bf16[640,256]{1,0:T(8,128)(2,1)S(1)}, bf16[640,256]{1,0:T(8,128)(2,1)S(1)}, u32[]{:S(2)}, u32[]{:S(2)}) %collective-permute-start.5) | collective-permute-done | bytes 327712 | tf_op jit(solution)/shard_map/ppermute | solution.py:307
  52.1 1.5 %collective-permute-start.12 = (bf16[640,256]{1,0:T(8,128)(2,1)S(1)}, bf16[640,256]{1,0:T(8,128)(2,1)S(1)}, u32[]{:S(2)}, u32[]{:S(2)}) collective-permute-start(bf16[640,256]{1,0:T(8,128)(2,1)S(1)} %collective-permute-done.3.refs_0_), channel_id=1, source_target_pairs={{0,2},{2,0},{1,3},{3,1},{4,6},{6,4},{5,7},{7,5},{8,10},{10,8},{9,1... | collective-permute-start | bytes 983048 | tf_op jit(solution)/shard_map/ppermute | solution.py:307
  54.1 5.0 %collective-permute-done.9.refs_5_ = bf16[640,256]{1,0:T(8,128)(2,1)S(1)} collective-permute-done((bf16[640,256]{1,0:T(8,128)(2,1)S(1)}, bf16[640,256]{1,0:T(8,128)(2,1)S(1)}, u32[]{:S(2)}, u32[]{:S(2)}) %collective-permute-start.9) | collective-permute-done | bytes 327712 | tf_op jit(solution)/shard_map/ppermute | solution.py:307
  59.1 6.1 %collective-permute-done.12.refs_1_ = bf16[640,256]{1,0:T(8,128)(2,1)S(1)} collective-permute-done((bf16[640,256]{1,0:T(8,128)(2,1)S(1)}, bf16[640,256]{1,0:T(8,128)(2,1)S(1)}, u32[]{:S(2)}, u32[]{:S(2)}) %collective-permute-start.12) | collective-permute-done | bytes 327712 | tf_op jit(solution)/shard_map/ppermute | solution.py:307
  65.7 1.5 %collective-permute-start.14 = (bf16[640,256]{1,0:T(8,128)(2,1)S(1)}, bf16[640,256]{1,0:T(8,128)(2,1)S(1)}, u32[]{:S(2)}, u32[]{:S(2)}) collective-permute-start(bf16[640,256]{1,0:T(8,128)(2,1)S(1)} %collective-permute-done.10.refs_6_), channel_id=1, source_target_pairs={{0,2},{2,0},{1,3},{3,1},{4,6},{6,4},{5,7},{7,5},{8,10},{10,8},{9,1... | collective-permute-start | bytes 983048 | tf_op jit(solution)/shard_map/ppermute | solution.py:307
  68.9 5.0 %collective-permute-done.13.refs_3_ = bf16[640,256]{1,0:T(8,128)(2,1)S(1)} collective-permute-done((bf16[640,256]{1,0:T(8,128)(2,1)S(1)}, bf16[640,256]{1,0:T(8,128)(2,1)S(1)}, u32[]{:S(2)}, u32[]{:S(2)}) %collective-permute-start.13) | collective-permute-done | bytes 327712 | tf_op jit(solution)/shard_map/ppermute | solution.py:307
  74.1 5.5 %attention.1 = (bf16[256,1280]{1,0:T(8,128)(2,1)}, bf16[256,512]{1,0:T(8,128)(2,1)S(1)}) custom-call(bf16[256,2560]{1,0:T(8,128)(2,1)S(1)} %get-tuple-element.45.own_ref, bf16[256,2560]{1,0:T(8,128)(2,1)S(1)} %collective-permute-done.4.other_ref, bf16[640,256]{1,0:T(8,128)(2,1)S(1)} %collective-permute-done.3.refs_0_, ...), custom_call_target="tpu_custom_call" | custom-call | flops 838860800 | bytes 5000000 | tf_op jit(solution)/shard_map/attention/pallas_call | solution.py:171
  79.7 1.5 %collective-permute-start.18 = (bf16[256,512]{1,0:T(8,128)(2,1)S(1)}, bf16[256,512]{1,0:T(8,128)(2,1)S(1)}, u32[]{:S(2)}, u32[]{:S(2)}) collective-permute-start(bf16[256,512]{1,0:T(8,128)(2,1)S(1)} %get-tuple-element.72.refs_12_), channel_id=1, source_target_pairs={{0,2},{2,0},{1,3},{3,1},{4,6},{6,4},{5,7},{7,5},{8,10},{10,8},{9,1... | collective-permute-start | bytes 786440 | tf_op jit(solution)/shard_map/ppermute | solution.py:307
  81.2 4.9 %collective-permute-done.18.refs_13_ = bf16[256,512]{1,0:T(8,128)(2,1)S(1)} collective-permute-done((bf16[256,512]{1,0:T(8,128)(2,1)S(1)}, bf16[256,512]{1,0:T(8,128)(2,1)S(1)}, u32[]{:S(2)}, u32[]{:S(2)}) %collective-permute-start.18) | collective-permute-done | bytes 262176 | tf_op jit(solution)/shard_map/ppermute | solution.py:307
  86.0 4.7 %collective-permute-done.17.refs_14_ = bf16[256,512]{1,0:T(8,128)(2,1)S(1)} collective-permute-done((bf16[256,512]{1,0:T(8,128)(2,1)S(1)}, bf16[256,512]{1,0:T(8,128)(2,1)S(1)}, u32[]{:S(2)}, u32[]{:S(2)}) %collective-permute-start.17) | collective-permute-done | bytes 262176 | tf_op jit(solution)/shard_map/ppermute | solution.py:312
  90.8 1.9 %collective-permute-start.21 = (bf16[256,512]{1,0:T(8,128)(2,1)S(1)}, bf16[256,512]{1,0:T(8,128)(2,1)S(1)}, u32[]{:S(2)}, u32[]{:S(2)}) collective-permute-start(bf16[256,512]{1,0:T(8,128)(2,1)S(1)} %collective-permute-done.17.refs_14_), channel_id=1, source_target_pairs={{0,2},{2,0},{1,3},{3,1},{4,6},{6,4},{5,7},{7,5},{8,10},{10,8},{9,1... | collective-permute-start | bytes 786440 | tf_op jit(solution)/shard_map/ppermute | solution.py:307
  93.1 4.0 %collective-permute-done.20.refs_15_ = bf16[256,512]{1,0:T(8,128)(2,1)S(1)} collective-permute-done((bf16[256,512]{1,0:T(8,128)(2,1)S(1)}, bf16[256,512]{1,0:T(8,128)(2,1)S(1)}, u32[]{:S(2)}, u32[]{:S(2)}) %collective-permute-start.20) | collective-permute-done | bytes 262176 | tf_op jit(solution)/shard_map/ppermute | solution.py:312
  97.2 3.8 %collective-permute-start.22 = (bf16[256,512]{1,0:T(8,128)(2,1)S(1)}, bf16[256,512]{1,0:T(8,128)(2,1)S(1)}, u32[]{:S(2)}, u32[]{:S(2)}) collective-permute-start(bf16[256,512]{1,0:T(8,128)(2,1)S(1)} %collective-permute-done.17.refs_14_), channel_id=1, source_target_pairs={{0,4},{4,8},{8,12},{12,0},{1,5},{5,9},{9,13},{13,1},{2,6},{6,10},{... | collective-permute-start | bytes 786440 | tf_op jit(solution)/shard_map/ppermute | solution.py:312
  101.0 2.5 %collective-permute-start.23 = (bf16[256,512]{1,0:T(8,128)(2,1)S(1)}, bf16[256,512]{1,0:T(8,128)(2,1)S(1)}, u32[]{:S(2)}, u32[]{:S(2)}) collective-permute-start(bf16[256,512]{1,0:T(8,128)(2,1)S(1)} %collective-permute-done.20.refs_15_), channel_id=1, source_target_pairs={{0,2},{2,0},{1,3},{3,1},{4,6},{6,4},{5,7},{7,5},{8,10},{10,8},{9,1... | collective-permute-start | bytes 786440 | tf_op jit(solution)/shard_map/ppermute | solution.py:307
  103.5 1.9 %collective-permute-done.22.refs_4_ = bf16[256,512]{1,0:T(8,128)(2,1)S(1)} collective-permute-done((bf16[256,512]{1,0:T(8,128)(2,1)S(1)}, bf16[256,512]{1,0:T(8,128)(2,1)S(1)}, u32[]{:S(2)}, u32[]{:S(2)}) %collective-permute-start.22) | collective-permute-done | bytes 262176 | tf_op jit(solution)/shard_map/ppermute | solution.py:312
  105.4 3.0 %collective-permute-done.23.refs_17_ = bf16[256,512]{1,0:T(8,128)(2,1)S(1)} collective-permute-done((bf16[256,512]{1,0:T(8,128)(2,1)S(1)}, bf16[256,512]{1,0:T(8,128)(2,1)S(1)}, u32[]{:S(2)}, u32[]{:S(2)}) %collective-permute-start.23) | collective-permute-done | bytes 262176 | tf_op jit(solution)/shard_map/ppermute | solution.py:307
  108.4 1.7 %collective-permute-start.24 = (bf16[256,512]{1,0:T(8,128)(2,1)S(1)}, bf16[256,512]{1,0:T(8,128)(2,1)S(1)}, u32[]{:S(2)}, u32[]{:S(2)}) collective-permute-start(bf16[256,512]{1,0:T(8,128)(2,1)S(1)} %collective-permute-done.22.refs_4_), channel_id=1, source_target_pairs={{0,2},{2,0},{1,3},{3,1},{4,6},{6,4},{5,7},{7,5},{8,10},{10,8},{9,1... | collective-permute-start | bytes 786440 | tf_op jit(solution)/shard_map/ppermute | solution.py:307
  110.1 1.7 %gradient.2 = (f32[2,640,256]{2,1,0:T(8,128)S(1)}, f32[2,256]{1,0:T(2,128)S(1)}) custom-call(bf16[2,640,256]{2,1,0:T(8,128)(2,1)S(1)} %collective-permute-done.15.refs_0_.refs_1_, bf16[2,640,256]{2,1,0:T(8,128)(2,1)S(1)} %collective-permute-done.15.refs_0_.refs_1_, bf16[2,640,256]{2,1,0:T(8,128)(2,1)S(1)} %collective-permute-done.16.refs_2_.refs_3_.refs_4_.refs_5_, ...), custom_call_target="tpu_custom_call" | custom-call | flops 1006632960 | bytes 5000000 | tf_op jit(solution)/shard_map/gradient/pallas_call | solution.py:236
  111.9 2.9 %collective-permute-done.24.refs_5_ = bf16[256,512]{1,0:T(8,128)(2,1)S(1)} collective-permute-done((bf16[256,512]{1,0:T(8,128)(2,1)S(1)}, bf16[256,512]{1,0:T(8,128)(2,1)S(1)}, u32[]{:S(2)}, u32[]{:S(2)}) %collective-permute-start.24) | collective-permute-done | bytes 262176 | tf_op jit(solution)/shard_map/ppermute | solution.py:307
  114.8 1.8 %gradient.3 = (f32[2,640,256]{2,1,0:T(8,128)}, f32[2,256]{1,0:T(2,128)}) custom-call(bf16[2,640,256]{2,1,0:T(8,128)(2,1)S(1)} %collective-permute-done.15.refs_0_.refs_1_, bf16[2,640,256]{2,1,0:T(8,128)(2,1)S(1)} %collective-permute-done.15.refs_0_.refs_1_, bf16[2,640,256]{2,1,0:T(8,128)(2,1)S(1)} %collective-permute-done.19.refs_6_.refs_7_.refs_2_.refs_3_, ...), custom_call_target="tpu_custom_call" | custom-call | flops 335544320 | bytes 5000000 | tf_op jit(solution)/shard_map/gradient/pallas_call | solution.py:236
  (49 shorter events, 9.1 us)
Async XLA Ops:
  0.6 6.2 %copy-start = (bf16[256,2560]{1,0:T(8,128)(2,1)S(1)}, bf16[256,2560]{1,0:T(8,128)(2,1)}, u32[]{:S(2)}) copy-start(bf16[256,2560]{1,0:T(8,128)(2,1)} %values_ref.1) | copy-start | bytes 3932164
  0.6 5.9 %copy-start.4 = (bf16[5120]{0:T(1024)(128)(2,1)S(1)}, bf16[5120]{0:T(1024)(128)(2,1)}, u32[]{:S(2)}) copy-start(bf16[5120]{0:T(1024)(128)(2,1)} %param.7) | copy-start | bytes 30724
  2.4 4.3 %collective-permute-start.1 = (f32[256,1]{0,1:T(1,128)S(1)}, f32[256,1]{0,1:T(1,128)S(1)}, u32[]{:S(2)}, u32[]{:S(2)}) collective-permute-start(f32[256,1]{0,1:T(1,128)S(1)} %bitcast.3), channel_id=1, source_target_pairs={{0,1},{1,0},{2,3},{3,2},{4,5},{5,4},{6,7},{7,6},{8,9},{9,8},{10,11... | collective-permute-start | bytes 3080 | tf_op jit(solution)/shard_map/ppermute | solution.py:307
  3.9 13.0 %collective-permute-start = (bf16[640,256]{1,0:T(8,128)(2,1)S(1)}, bf16[640,256]{1,0:T(8,128)(2,1)S(1)}, u32[]{:S(2)}, u32[]{:S(2)}) collective-permute-start(bf16[640,256]{1,0:T(8,128)(2,1)S(1)} %dynamic-slice_bitcast_fusion), channel_id=1, source_target_pairs={{0,4},{4,8},{8,12},{12,0},{1,5},{5,9},{9,13},{13,1},{2,6},{6,10},{... | collective-permute-start | bytes 983048 | tf_op jit(solution)/shard_map/ppermute | solution.py:312
  6.9 47.2 %copy-start.5 = (bf16[2,256]{1,0:T(2,128)(2,1)S(1)}, bf16[2,256]{1,0:T(2,128)(2,1)}, u32[]{:S(2)}) copy-start(bf16[2,256]{1,0:T(2,128)(2,1)} %param.11) | copy-start | bytes 3076
  7.8 60.0 %copy-start.1 = (bf16[2,1280,256]{2,1,0:T(8,128)(2,1)S(1)}, bf16[2,1280,256]{2,1,0:T(8,128)(2,1)}, u32[]{:S(2)}) copy-start(bf16[2,1280,256]{2,1,0:T(8,128)(2,1)} %weight_ref.1) | copy-start | bytes 3932164
  17.0 11.6 %collective-permute-start.4 = (bf16[256,2560]{1,0:T(8,128)(2,1)S(1)}, bf16[256,2560]{1,0:T(8,128)(2,1)S(1)}, u32[]{:S(2)}, u32[]{:S(2)}) collective-permute-start(bf16[256,2560]{1,0:T(8,128)(2,1)S(1)} %get-tuple-element.45.own_ref), channel_id=1, source_target_pairs={{0,1},{1,0},{2,3},{3,2},{4,5},{5,4},{6,7},{7,6},{8,9},{9,8},{10,11... | collective-permute-start | bytes 3932168 | tf_op jit(solution)/shard_map/ppermute | solution.py:307
  17.0 10.1 %collective-permute-start.3 = (bf16[640,256]{1,0:T(8,128)(2,1)S(1)}, bf16[640,256]{1,0:T(8,128)(2,1)S(1)}, u32[]{:S(2)}, u32[]{:S(2)}) collective-permute-start(bf16[640,256]{1,0:T(8,128)(2,1)S(1)} %dynamic-slice_bitcast_fusion), channel_id=1, source_target_pairs={{0,12},{4,0},{8,4},{12,8},{1,13},{5,1},{9,5},{13,9},{2,14},{6,2},{... | collective-permute-start | bytes 983048 | tf_op jit(solution)/shard_map/ppermute | solution.py:312
  18.7 9.8 %collective-permute-start.2 = (bf16[640,256]{1,0:T(8,128)(2,1)S(1)}, bf16[640,256]{1,0:T(8,128)(2,1)S(1)}, u32[]{:S(2)}, u32[]{:S(2)}) collective-permute-start(bf16[640,256]{1,0:T(8,128)(2,1)S(1)} %collective-permute-done.refs_0_), channel_id=1, source_target_pairs={{0,16},{16,0},{1,17},{17,1},{2,18},{18,2},{3,19},{19,3},{4,20},{20... | collective-permute-start | bytes 983048 | tf_op jit(solution)/shard_map/ppermute | solution.py:307
  20.2 16.6 %collective-permute-start.8 = (bf16[2,640,256]{2,1,0:T(8,128)(2,1)S(1)}, bf16[2,640,256]{2,1,0:T(8,128)(2,1)S(1)}, u32[]{:S(2)}, u32[]{:S(2)}) collective-permute-start(bf16[2,640,256]{2,1,0:T(8,128)(2,1)S(1)} %get-tuple-element.51), channel_id=1, source_target_pairs={{0,2},{2,0},{1,3},{3,1},{4,6},{6,4},{5,7},{7,5},{8,10},{10,8},{9,1... | collective-permute-start | bytes 1966088 | tf_op jit(solution)/shard_map/ppermute | solution.py:307
  28.5 9.0 %collective-permute-start.7 = (bf16[640,256]{1,0:T(8,128)(2,1)S(1)}, bf16[640,256]{1,0:T(8,128)(2,1)S(1)}, u32[]{:S(2)}, u32[]{:S(2)}) collective-permute-start(bf16[640,256]{1,0:T(8,128)(2,1)S(1)} %collective-permute-done.3.refs_0_), channel_id=1, source_target_pairs={{0,16},{16,0},{1,17},{17,1},{2,18},{18,2},{3,19},{19,3},{4,20},{20... | collective-permute-start | bytes 983048 | tf_op jit(solution)/shard_map/ppermute | solution.py:307
  30.1 10.5 %collective-permute-start.6 = (bf16[640,256]{1,0:T(8,128)(2,1)S(1)}, bf16[640,256]{1,0:T(8,128)(2,1)S(1)}, u32[]{:S(2)}, u32[]{:S(2)}) collective-permute-start(bf16[640,256]{1,0:T(8,128)(2,1)S(1)} %collective-permute-done.refs_0_), channel_id=1, source_target_pairs={{0,4},{4,8},{8,12},{12,0},{1,5},{5,9},{9,13},{13,1},{2,6},{6,10},{... | collective-permute-start | bytes 983048 | tf_op jit(solution)/shard_map/ppermute | solution.py:312
  40.7 13.4 %collective-permute-start.15 = (bf16[2,640,256]{2,1,0:T(8,128)(2,1)S(1)}, bf16[2,640,256]{2,1,0:T(8,128)(2,1)S(1)}, u32[]{:S(2)}, u32[]{:S(2)}) collective-permute-start(bf16[2,640,256]{2,1,0:T(8,128)(2,1)S(1)} %get-tuple-element.67), channel_id=1, source_target_pairs={{0,0},{1,8},{4,4},{5,12},{8,1},{9,9},{12,5},{13,13},{2,2},{3,10},{... | collective-permute-start | bytes 1966088 | tf_op jit(solution)/shard_map/ppermute | solution.py:340
  41.4 10.6 %collective-permute-start.5 = (bf16[640,256]{1,0:T(8,128)(2,1)S(1)}, bf16[640,256]{1,0:T(8,128)(2,1)S(1)}, u32[]{:S(2)}, u32[]{:S(2)}) collective-permute-start(bf16[640,256]{1,0:T(8,128)(2,1)S(1)} %collective-permute-done.refs_0_), channel_id=1, source_target_pairs={{0,2},{2,0},{1,3},{3,1},{4,6},{6,4},{5,7},{7,5},{8,10},{10,8},{9,1... | collective-permute-start | bytes 983048 | tf_op jit(solution)/shard_map/ppermute | solution.py:307
  43.0 11.1 %collective-permute-start.10 = (bf16[640,256]{1,0:T(8,128)(2,1)S(1)}, bf16[640,256]{1,0:T(8,128)(2,1)S(1)}, u32[]{:S(2)}, u32[]{:S(2)}) collective-permute-start(bf16[640,256]{1,0:T(8,128)(2,1)S(1)} %collective-permute-done.6.refs_4_), channel_id=1, source_target_pairs={{0,16},{16,0},{1,17},{17,1},{2,18},{18,2},{3,19},{19,3},{4,20},{20... | collective-permute-start | bytes 983048 | tf_op jit(solution)/shard_map/ppermute | solution.py:307
  43.5 15.6 %collective-permute-start.9 = (bf16[640,256]{1,0:T(8,128)(2,1)S(1)}, bf16[640,256]{1,0:T(8,128)(2,1)S(1)}, u32[]{:S(2)}, u32[]{:S(2)}) collective-permute-start(bf16[640,256]{1,0:T(8,128)(2,1)S(1)} %collective-permute-done.6.refs_4_), channel_id=1, source_target_pairs={{0,2},{2,0},{1,3},{3,1},{4,6},{6,4},{5,7},{7,5},{8,10},{10,8},{9,1... | collective-permute-start | bytes 983048 | tf_op jit(solution)/shard_map/ppermute | solution.py:307
  52.1 13.1 %collective-permute-start.12 = (bf16[640,256]{1,0:T(8,128)(2,1)S(1)}, bf16[640,256]{1,0:T(8,128)(2,1)S(1)}, u32[]{:S(2)}, u32[]{:S(2)}) collective-permute-start(bf16[640,256]{1,0:T(8,128)(2,1)S(1)} %collective-permute-done.3.refs_0_), channel_id=1, source_target_pairs={{0,2},{2,0},{1,3},{3,1},{4,6},{6,4},{5,7},{7,5},{8,10},{10,8},{9,1... | collective-permute-start | bytes 983048 | tf_op jit(solution)/shard_map/ppermute | solution.py:307
  53.5 11.6 %collective-permute-start.11 = (bf16[640,256]{1,0:T(8,128)(2,1)S(1)}, bf16[640,256]{1,0:T(8,128)(2,1)S(1)}, u32[]{:S(2)}, u32[]{:S(2)}) collective-permute-start(bf16[640,256]{1,0:T(8,128)(2,1)S(1)} %collective-permute-done.5.refs_1_), channel_id=1, source_target_pairs={{0,16},{16,0},{1,17},{17,1},{2,18},{18,2},{3,19},{19,3},{4,20},{20... | collective-permute-start | bytes 983048 | tf_op jit(solution)/shard_map/ppermute | solution.py:307
  54.1 25.6 %collective-permute-start.16 = (bf16[2,640,256]{2,1,0:T(8,128)(2,1)S(1)}, bf16[2,640,256]{2,1,0:T(8,128)(2,1)S(1)}, u32[]{:S(2)}, u32[]{:S(2)}) collective-permute-start(bf16[2,640,256]{2,1,0:T(8,128)(2,1)S(1)} %get-tuple-element.68), channel_id=1, source_target_pairs={{0,4},{1,12},{4,0},{5,8},{8,5},{9,13},{12,1},{13,9},{2,6},{3,14},{... | collective-permute-start | bytes 1966088 | tf_op jit(solution)/shard_map/ppermute | solution.py:340
  65.1 8.8 %collective-permute-start.13 = (bf16[640,256]{1,0:T(8,128)(2,1)S(1)}, bf16[640,256]{1,0:T(8,128)(2,1)S(1)}, u32[]{:S(2)}, u32[]{:S(2)}) collective-permute-start(bf16[640,256]{1,0:T(8,128)(2,1)S(1)} %collective-permute-done.12.refs_1_), channel_id=1, source_target_pairs={{0,16},{16,0},{1,17},{17,1},{2,18},{18,2},{3,19},{19,3},{4,20},{20... | collective-permute-start | bytes 983048 | tf_op jit(solution)/shard_map/ppermute | solution.py:307
  65.7 8.5 %collective-permute-start.14 = (bf16[640,256]{1,0:T(8,128)(2,1)S(1)}, bf16[640,256]{1,0:T(8,128)(2,1)S(1)}, u32[]{:S(2)}, u32[]{:S(2)}) collective-permute-start(bf16[640,256]{1,0:T(8,128)(2,1)S(1)} %collective-permute-done.10.refs_6_), channel_id=1, source_target_pairs={{0,2},{2,0},{1,3},{3,1},{4,6},{6,4},{5,7},{7,5},{8,10},{10,8},{9,1... | collective-permute-start | bytes 983048 | tf_op jit(solution)/shard_map/ppermute | solution.py:307
  67.8 6.3 %copy-start.2 = (bf16[256,1280]{1,0:T(8,128)(2,1)S(1)}, bf16[256,1280]{1,0:T(8,128)(2,1)}, u32[]{:S(2)}) copy-start(bf16[256,1280]{1,0:T(8,128)(2,1)} %refs_12_.1) | copy-start | bytes 1966084
  67.8 6.3 %copy-start.3 = (bf16[256,1280]{1,0:T(8,128)(2,1)S(1)}, bf16[256,1280]{1,0:T(8,128)(2,1)}, u32[]{:S(2)}) copy-start(bf16[256,1280]{1,0:T(8,128)(2,1)} %refs_13_.1) | copy-start | bytes 1966084
  79.7 6.4 %collective-permute-start.18 = (bf16[256,512]{1,0:T(8,128)(2,1)S(1)}, bf16[256,512]{1,0:T(8,128)(2,1)S(1)}, u32[]{:S(2)}, u32[]{:S(2)}) collective-permute-start(bf16[256,512]{1,0:T(8,128)(2,1)S(1)} %get-tuple-element.72.refs_12_), channel_id=1, source_target_pairs={{0,2},{2,0},{1,3},{3,1},{4,6},{6,4},{5,7},{7,5},{8,10},{10,8},{9,1... | collective-permute-start | bytes 786440 | tf_op jit(solution)/shard_map/ppermute | solution.py:307
  81.2 9.6 %collective-permute-start.17 = (bf16[256,512]{1,0:T(8,128)(2,1)S(1)}, bf16[256,512]{1,0:T(8,128)(2,1)S(1)}, u32[]{:S(2)}, u32[]{:S(2)}) collective-permute-start(bf16[256,512]{1,0:T(8,128)(2,1)S(1)} %get-tuple-element.72.refs_12_), channel_id=1, source_target_pairs={{0,4},{4,8},{8,12},{12,0},{1,5},{5,9},{9,13},{13,1},{2,6},{6,10},{... | collective-permute-start | bytes 786440 | tf_op jit(solution)/shard_map/ppermute | solution.py:312
  90.8 6.4 %collective-permute-start.20 = (bf16[256,512]{1,0:T(8,128)(2,1)S(1)}, bf16[256,512]{1,0:T(8,128)(2,1)S(1)}, u32[]{:S(2)}, u32[]{:S(2)}) collective-permute-start(bf16[256,512]{1,0:T(8,128)(2,1)S(1)} %get-tuple-element.72.refs_12_), channel_id=1, source_target_pairs={{0,12},{4,0},{8,4},{12,8},{1,13},{5,1},{9,5},{13,9},{2,14},{6,2},{... | collective-permute-start | bytes 786440 | tf_op jit(solution)/shard_map/ppermute | solution.py:312
  90.8 6.4 %collective-permute-start.21 = (bf16[256,512]{1,0:T(8,128)(2,1)S(1)}, bf16[256,512]{1,0:T(8,128)(2,1)S(1)}, u32[]{:S(2)}, u32[]{:S(2)}) collective-permute-start(bf16[256,512]{1,0:T(8,128)(2,1)S(1)} %collective-permute-done.17.refs_14_), channel_id=1, source_target_pairs={{0,2},{2,0},{1,3},{3,1},{4,6},{6,4},{5,7},{7,5},{8,10},{10,8},{9,1... | collective-permute-start | bytes 786440 | tf_op jit(solution)/shard_map/ppermute | solution.py:307
  92.6 17.5 %collective-permute-start.25 = (bf16[2,640,256]{2,1,0:T(8,128)(2,1)S(1)}, bf16[2,640,256]{2,1,0:T(8,128)(2,1)S(1)}, u32[]{:S(2)}, u32[]{:S(2)}) collective-permute-start(bf16[2,640,256]{2,1,0:T(8,128)(2,1)S(1)} %collective-permute-done.16.refs_2_.refs_3_.refs_4_.refs_5_), channel_id=1, source_target_pairs={{0,1},{1,0},{2,3},{3,2},{4,5},{5,4},{6,7},{7,6},{8,9},{9,8},{10,11... | collective-permute-start | bytes 1966088 | tf_op jit(solution)/shard_map/ppermute | solution.py:307
  92.6 17.5 %collective-permute-start.19 = (bf16[2,640,256]{2,1,0:T(8,128)(2,1)S(1)}, bf16[2,640,256]{2,1,0:T(8,128)(2,1)S(1)}, u32[]{:S(2)}, u32[]{:S(2)}) collective-permute-start(bf16[2,640,256]{2,1,0:T(8,128)(2,1)S(1)} %collective-permute-done.15.refs_0_.refs_1_), channel_id=1, source_target_pairs={{0,1},{1,0},{2,3},{3,2},{4,5},{5,4},{6,7},{7,6},{8,9},{9,8},{10,11... | collective-permute-start | bytes 1966088 | tf_op jit(solution)/shard_map/ppermute | solution.py:307
  97.2 8.2 %collective-permute-start.22 = (bf16[256,512]{1,0:T(8,128)(2,1)S(1)}, bf16[256,512]{1,0:T(8,128)(2,1)S(1)}, u32[]{:S(2)}, u32[]{:S(2)}) collective-permute-start(bf16[256,512]{1,0:T(8,128)(2,1)S(1)} %collective-permute-done.17.refs_14_), channel_id=1, source_target_pairs={{0,4},{4,8},{8,12},{12,0},{1,5},{5,9},{9,13},{13,1},{2,6},{6,10},{... | collective-permute-start | bytes 786440 | tf_op jit(solution)/shard_map/ppermute | solution.py:312
  101.0 7.4 %collective-permute-start.23 = (bf16[256,512]{1,0:T(8,128)(2,1)S(1)}, bf16[256,512]{1,0:T(8,128)(2,1)S(1)}, u32[]{:S(2)}, u32[]{:S(2)}) collective-permute-start(bf16[256,512]{1,0:T(8,128)(2,1)S(1)} %collective-permute-done.20.refs_15_), channel_id=1, source_target_pairs={{0,2},{2,0},{1,3},{3,1},{4,6},{6,4},{5,7},{7,5},{8,10},{10,8},{9,1... | collective-permute-start | bytes 786440 | tf_op jit(solution)/shard_map/ppermute | solution.py:307
  108.4 6.4 %collective-permute-start.24 = (bf16[256,512]{1,0:T(8,128)(2,1)S(1)}, bf16[256,512]{1,0:T(8,128)(2,1)S(1)}, u32[]{:S(2)}, u32[]{:S(2)}) collective-permute-start(bf16[256,512]{1,0:T(8,128)(2,1)S(1)} %collective-permute-done.22.refs_4_), channel_id=1, source_target_pairs={{0,2},{2,0},{1,3},{3,1},{4,6},{6,4},{5,7},{7,5},{8,10},{10,8},{9,1... | collective-permute-start | bytes 786440 | tf_op jit(solution)/shard_map/ppermute | solution.py:307

commit v18 on v11

--- a/solution.py
+++ b/solution.py
@@ -107,9 +107,14 @@
     length, columns = cosine.shape[0], pair_ref.shape[1] // 2
     key_heads = columns // HEAD
     group_size = queries_ref.shape[1] // columns
-    key_at = lax.broadcasted_iota(jnp.int32, (length, length), 0)
-    query_at = lax.broadcasted_iota(jnp.int32, (length, length), 1)
-    causal = key_at <= query_at
+    part = length // 2
+    masks = []
+    for half in range(2):
+        seen = part * (half + 1)
+        key_at = lax.broadcasted_iota(jnp.int32, (seen, part), 0)
+        query_at = lax.broadcasted_iota(jnp.int32, (seen, part), 1) + half * part
+        masks.append(key_at <= query_at)
+    unseen = jnp.zeros((length - part, part), jnp.bfloat16)
     for head in range(key_heads):
         lanes = slice(head * HEAD, (head + 1) * HEAD)
         raw = raw_of(0, lanes)
@@ -123,15 +128,25 @@
             start = (head * group_size + member) * HEAD
             query = queries_ref[:, start : start + HEAD]
             upstream = cotangent_ref[:, start : start + HEAD]
-            scores = jnp.where(causal, product_rows(keys, query), -jnp.inf)
-            peak = jnp.max(scores, 0, keepdims=True)
-            exponentials = jnp.exp((scores - peak) * SCALE)
-            probability = exponentials * (1.0 / jnp.sum(exponentials, 0, keepdims=True))
+            scores = product_rows(keys, query)
             grad_probability = product_rows(values, upstream)
-            total = jnp.sum(probability * grad_probability, 0, keepdims=True)
-            grad_scores = (probability * (grad_probability - total) * SCALE).astype(jnp.bfloat16)
+            weights, grad_scores = [], []
+            for half in range(2):
+                rows, columns_at = slice(part * (half + 1)), slice(half * part, (half + 1) * part)
+                seen = jnp.where(masks[half], scores[rows, columns_at], -jnp.inf)
+                peak = jnp.max(seen, 0, keepdims=True)
+                exponentials = jnp.exp((seen - peak) * SCALE)
+                probability = exponentials * (1.0 / jnp.sum(exponentials, 0, keepdims=True))
+                upward = grad_probability[rows, columns_at]
+                total = jnp.sum(probability * upward, 0, keepdims=True)
+                weights.append(probability.astype(jnp.bfloat16))
+                grad_scores.append((probability * (upward - total) * SCALE).astype(jnp.bfloat16))
+            weights, grad_scores = (
+                jnp.concatenate([jnp.concatenate([early, unseen], 0), late], 1)
+                for early, late in (weights, grad_scores)
+            )
             grad_rotated += product(grad_scores, query)
-            grad_value += product(probability.astype(jnp.bfloat16), upstream)
+            grad_value += product(weights, upstream)
             grad_query = product(keys_across, grad_scores)
             grad_query_ref[:, start : start + HEAD] = grad_query.T.astype(jnp.bfloat16)
         grad_key = grad_rotated * cosine - pltpu.roll(grad_rotated, HEAD // 2, 1) * sine
@@ -183,16 +198,23 @@
 
 def gradient_kernel(sources, first, *refs):
     count = len(sources)
-    own, other, pairs = (refs[i * count : (i + 1) * count] for i in range(3))
-    refs = refs[3 * count :]
+    own, other, refs = refs[:count], refs[count : 2 * count], refs[2 * count :]
+    pairs = []
+    for _, _, parts in sources:
+        held, refs = refs[:parts], refs[parts:]
+        pairs.append(held)
+    pairs = [
+        held[0][...] if len(held) == 1 else jnp.concatenate([ref[...] for ref in held], 1)
+        for held in pairs
+    ]
     weight_ref, bias_ref = refs[-2:]
     columns = weight_ref.shape[2]
     core, cores_blocks = lax.axis_index("sub"), lax.axis_size("blk") // 2
     total = None
-    for at, (distance, _) in enumerate(sources):
+    for at, (distance, _, _) in enumerate(sources):
         here = lax.div(block_from(distance), cores_blocks) == core
         slab = jnp.where(here, own[at][0], other[at][0])
-        term = product(slab, pairs[at][...])
+        term = product(slab, pairs[at])
         total = term if total is None else total + term
     for j in range(2):
         part = total[:, j * columns : (j + 1) * columns]
@@ -202,7 +224,7 @@
     def _():
         total = None
         for pair in pairs:
-            term = jnp.sum(pair[...].astype(jnp.float32), axis=0, keepdims=True)
+            term = jnp.sum(pair.astype(jnp.float32), axis=0, keepdims=True)
             total = term if total is None else total + term
         for j in range(2):
             part = total[:, j * columns : (j + 1) * columns]
@@ -210,10 +232,11 @@
 
 
 def gradient(slabs, some, sums):
-    pairs = list(some.values())
+    pairs = [part for parts in some.values() for part in parts]
+    sources = tuple((*which, len(parts)) for which, parts in some.items())
     _, share, length = slabs[0][0].shape
-    columns = pairs[0].shape[1] // 2
-    count = len(pairs)
+    columns = next(iter(some.values()))[0].shape[1] // 2
+    count = len(some)
     tile = share // 2 if share % 32 == 0 else share
 
     def slab_spec(same):
@@ -222,13 +245,13 @@
     weight_spec = pl.BlockSpec((2, tile, columns), lambda i: (0, i, 0))
     bias_spec = pl.BlockSpec((2, columns), lambda i: (0, 0))
     in_specs = [slab_spec(same) for _, same in some] * 2
-    in_specs += [pl.BlockSpec((length, 2 * columns), lambda i: (0, 0))] * count
+    in_specs += [pl.BlockSpec(pair.shape, lambda i: (0, 0)) for pair in pairs]
     if sums:
         in_specs += [weight_spec, bias_spec]
     own = [slabs[distance % 2][0] for distance, _ in some]
     other = [slabs[distance % 2][1] for distance, _ in some]
     return pl.pallas_call(
-        functools.partial(gradient_kernel, tuple(some), sums is None),
+        functools.partial(gradient_kernel, sources, sums is None),
         grid=(share // tile,),
         in_specs=in_specs,
         out_specs=[weight_spec, bias_spec],
@@ -399,21 +422,25 @@
     pair_up, pair_x, grad_pair, even, odd = lax.optimization_barrier(
         (pair_up, pair_x, grad_pair, even, odd)
     )
-    slabs = ((even, swapped(even, "sub")), (odd, swapped(odd, "sub")))
     pair_down, pair_up_x = turned(grad_pair, "blk", -1), swapped(pair_up, "dp")
     pair_down, pair_up_x, pair_up = lax.optimization_barrier((pair_down, pair_up_x, pair_up))
     pair_twice, pair_down_x = turned(pair_up, "blk", 1), swapped(pair_down, "dp")
-    pair_twice, pair_down_x = lax.optimization_barrier((pair_twice, pair_down_x))
-    pair_twice_x = swapped(pair_twice, "dp")
+    even, odd = after(even, pair_down), after(odd, pair_down)
+    slabs = ((even, swapped(even, "sub")), (odd, swapped(odd, "sub")))
+    twice_x_values = turned(pair_up_x[:, columns:], "blk", 1)
+    pair_twice, pair_down_x, twice_x_values = lax.optimization_barrier(
+        (pair_twice, pair_down_x, twice_x_values)
+    )
+    twice_x_keys = swapped(pair_twice[:, :columns], "dp")
     first = {
-        (0, True): grad_pair,
-        (0, False): pair_x,
-        (1, True): pair_up,
-        (-1, True): pair_down,
-        (1, False): pair_up_x,
-        (-1, False): pair_down_x,
+        (0, True): (grad_pair,),
+        (0, False): (pair_x,),
+        (1, True): (pair_up,),
+        (-1, True): (pair_down,),
+        (1, False): (pair_up_x,),
+        (-1, False): (pair_down_x,),
     }
-    last = {(2, True): pair_twice, (2, False): pair_twice_x}
+    last = {(2, True): (pair_twice,), (2, False): (twice_x_keys, twice_x_values)}
     sums = None
     for some in (first, last):
         sums = gradient(slabs, some, sums)

time: 112 us -> 116 us (1.036)
  waiting for transfers between devices: 70.1 us -> 73.1 us
    ppermute x6 -> x7, waiting for transfers between devices: 24.7 us -> 29.1 us  [turned(): lax.ppermute(block, axis, [(i, (i + distance) % size) for i in range(size)])]
    ppermute x18, waiting for transfers between devices: 44.7 us -> 43.3 us  [swapped(): return lax.ppermute(block, axis, [(0, 1), (1, 0)])]
    ppermute x6 -> x7, starting transfers between devices: 7.19 us -> 7.94 us  [turned(): lax.ppermute(block, axis, [(i, (i + distance) % size) for i in range(size)])]
  transfers between devices with their start and end apart: 26 -> 27, of which waited for: 17 -> 17; matrix products, arithmetic and copies ran while one was open for 2% -> 2% of each run, Pallas kernels for 8% -> 8%
where the time goes in v18:
time: 116 us
  waiting for transfers between devices  73.1 us (63%)
  starting transfers between devices  27 us (23%)
  Pallas kernels  10.9 us (9%)
  other arithmetic  2.4 us (2%)
  local copies, waits for them, and re-layouts  1.32 us (1%)
    ppermute x18, waiting for transfers between devices, swapped(): return lax.ppermute(block, axis, [(0, 1), (1, 0)])  43.3 us
    ppermute x7, waiting for transfers between devices, turned(): lax.ppermute(block, axis, [(i, (i + distance) % size) for i in range(size)])  29.1 us
    ppermute x18, starting transfers between devices, swapped(): return lax.ppermute(block, axis, [(0, 1), (1, 0)])  17.7 us
    ppermute x7, starting transfers between devices, turned(): lax.ppermute(block, axis, [(i, (i + distance) % size) for i in range(size)])  7.94 us
    pallas_call x1, Pallas kernels, attention(): pl.pallas_call(functools.partial(attention_kernel, distance), in_specs=[I...  4.98 us
    pallas_call x2, Pallas kernels, gradient(): pl.pallas_call(functools.partial(gradient_kernel, sources, sums is None),...  3.47 us
  transfers between devices with their start and end apart: 27, of which 17 were waited for; matrix products, arithmetic and copies ran while one was open for 2% of the time, Pallas kernels for 8%

profile of v18, /device:TPU:0, one launch (start us, length us, event | category | flops | bytes accessed | tf_op | source)
XLA Modules:
  0.0 115.6 jit_solution(6251034637608449266)
XLA Ops:
  1.8 3.1 %collective-permute-start = (bf16[640,256]{1,0:T(8,128)(2,1)S(1)}, bf16[640,256]{1,0:T(8,128)(2,1)S(1)}, u32[]{:S(2)}, u32[]{:S(2)}) collective-permute-start(bf16[640,256]{1,0:T(8,128)(2,1)S(1)} %dynamic-slice_bitcast_fusion), channel_id=1, source_target_pairs={{0,4},{4,8},{8,12},{12,0},{1,5},{5,9},{9,13},{13,1},{2,6},{6,10},{... | collective-permute-start | bytes 983048 | tf_op jit(solution)/shard_map/ppermute | solution.py:329
  4.8 1.7 %multiply_reduce_fusion = f32[256]{0:T(256)S(1)} fusion(bf16[256,2560]{1,0:T(8,128)(2,1)} %values_ref.1), kind=kLoop, calls=%fused_computation | loop fusion | flops 1965824 | bytes 1311744 | tf_op jit(solution)/shard_map/reduce_sum | solution.py:364
  8.8 5.7 %collective-permute-done.refs_0_ = bf16[640,256]{1,0:T(8,128)(2,1)S(1)} collective-permute-done((bf16[640,256]{1,0:T(8,128)(2,1)S(1)}, bf16[640,256]{1,0:T(8,128)(2,1)S(1)}, u32[]{:S(2)}, u32[]{:S(2)}) %collective-permute-start) | collective-permute-done | bytes 327712 | tf_op jit(solution)/shard_map/ppermute | solution.py:329
  14.6 1.5 %collective-permute-start.2 = (bf16[640,256]{1,0:T(8,128)(2,1)S(1)}, bf16[640,256]{1,0:T(8,128)(2,1)S(1)}, u32[]{:S(2)}, u32[]{:S(2)}) collective-permute-start(bf16[640,256]{1,0:T(8,128)(2,1)S(1)} %collective-permute-done.refs_0_), channel_id=1, source_target_pairs={{0,16},{16,0},{1,17},{17,1},{2,18},{18,2},{3,19},{19,3},{4,20},{20... | collective-permute-start | bytes 983048 | tf_op jit(solution)/shard_map/ppermute | solution.py:324
  16.1 1.7 %collective-permute-start.3 = (bf16[640,256]{1,0:T(8,128)(2,1)S(1)}, bf16[640,256]{1,0:T(8,128)(2,1)S(1)}, u32[]{:S(2)}, u32[]{:S(2)}) collective-permute-start(bf16[640,256]{1,0:T(8,128)(2,1)S(1)} %dynamic-slice_bitcast_fusion), channel_id=1, source_target_pairs={{0,12},{4,0},{8,4},{12,8},{1,13},{5,1},{9,5},{13,9},{2,14},{6,2},{... | collective-permute-start | bytes 983048 | tf_op jit(solution)/shard_map/ppermute | solution.py:329
  17.8 1.5 %collective-permute-start.8 = (bf16[2,640,256]{2,1,0:T(8,128)(2,1)S(1)}, bf16[2,640,256]{2,1,0:T(8,128)(2,1)S(1)}, u32[]{:S(2)}, u32[]{:S(2)}) collective-permute-start(bf16[2,640,256]{2,1,0:T(8,128)(2,1)S(1)} %get-tuple-element.54), channel_id=1, source_target_pairs={{0,2},{2,0},{1,3},{3,1},{4,6},{6,4},{5,7},{7,5},{8,10},{10,8},{9,1... | collective-permute-start | bytes 1966088 | tf_op jit(solution)/shard_map/ppermute | solution.py:324
  19.3 5.4 %collective-permute-done.2.refs_2_ = bf16[640,256]{1,0:T(8,128)(2,1)S(1)} collective-permute-done((bf16[640,256]{1,0:T(8,128)(2,1)S(1)}, bf16[640,256]{1,0:T(8,128)(2,1)S(1)}, u32[]{:S(2)}, u32[]{:S(2)}) %collective-permute-start.2) | collective-permute-done | bytes 327712 | tf_op jit(solution)/shard_map/ppermute | solution.py:324
  24.7 1.2 %collective-permute-done.3.refs_4_ = bf16[640,256]{1,0:T(8,128)(2,1)S(1)} collective-permute-done((bf16[640,256]{1,0:T(8,128)(2,1)S(1)}, bf16[640,256]{1,0:T(8,128)(2,1)S(1)}, u32[]{:S(2)}, u32[]{:S(2)}) %collective-permute-start.3) | collective-permute-done | bytes 327712 | tf_op jit(solution)/shard_map/ppermute | solution.py:329
  26.5 1.5 %collective-permute-start.7 = (bf16[640,256]{1,0:T(8,128)(2,1)S(1)}, bf16[640,256]{1,0:T(8,128)(2,1)S(1)}, u32[]{:S(2)}, u32[]{:S(2)}) collective-permute-start(bf16[640,256]{1,0:T(8,128)(2,1)S(1)} %collective-permute-done.refs_0_), channel_id=1, source_target_pairs={{0,2},{2,0},{1,3},{3,1},{4,6},{6,4},{5,7},{7,5},{8,10},{10,8},{9,1... | collective-permute-start | bytes 983048 | tf_op jit(solution)/shard_map/ppermute | solution.py:324
  27.9 7.5 %collective-permute-done.8.arrived_ref = bf16[2,640,256]{2,1,0:T(8,128)(2,1)S(1)} collective-permute-done((bf16[2,640,256]{2,1,0:T(8,128)(2,1)S(1)}, bf16[2,640,256]{2,1,0:T(8,128)(2,1)S(1)}, u32[]{:S(2)}, u32[]{:S(2)}) %collective-permute-start.8) | collective-permute-done | bytes 655392 | tf_op jit(solution)/shard_map/ppermute | solution.py:324
  35.4 1.3 %collective-permute-done.5.p0 = bf16[640,256]{1,0:T(8,128)(2,1)S(1)} collective-permute-done((bf16[640,256]{1,0:T(8,128)(2,1)S(1)}, bf16[640,256]{1,0:T(8,128)(2,1)S(1)}, u32[]{:S(2)}, u32[]{:S(2)}) %collective-permute-start.5) | collective-permute-done | bytes 327712 | tf_op jit(solution)/shard_map/ppermute | solution.py:329
  36.8 4.7 %collective-permute-done.7.refs_1_ = bf16[640,256]{1,0:T(8,128)(2,1)S(1)} collective-permute-done((bf16[640,256]{1,0:T(8,128)(2,1)S(1)}, bf16[640,256]{1,0:T(8,128)(2,1)S(1)}, u32[]{:S(2)}, u32[]{:S(2)}) %collective-permute-start.7) | collective-permute-done | bytes 327712 | tf_op jit(solution)/shard_map/ppermute | solution.py:324
  42.8 1.5 %collective-permute-start.11 = (bf16[640,256]{1,0:T(8,128)(2,1)S(1)}, bf16[640,256]{1,0:T(8,128)(2,1)S(1)}, u32[]{:S(2)}, u32[]{:S(2)}) collective-permute-start(bf16[640,256]{1,0:T(8,128)(2,1)S(1)} %collective-permute-done.7.refs_1_), channel_id=1, source_target_pairs={{0,16},{16,0},{1,17},{17,1},{2,18},{18,2},{3,19},{19,3},{4,20},{20... | collective-permute-start | bytes 983048 | tf_op jit(solution)/shard_map/ppermute | solution.py:324
  44.3 1.5 %collective-permute-start.12 = (bf16[640,256]{1,0:T(8,128)(2,1)S(1)}, bf16[640,256]{1,0:T(8,128)(2,1)S(1)}, u32[]{:S(2)}, u32[]{:S(2)}) collective-permute-start(bf16[640,256]{1,0:T(8,128)(2,1)S(1)} %collective-permute-done.3.refs_4_), channel_id=1, source_target_pairs={{0,2},{2,0},{1,3},{3,1},{4,6},{6,4},{5,7},{7,5},{8,10},{10,8},{9,1... | collective-permute-start | bytes 983048 | tf_op jit(solution)/shard_map/ppermute | solution.py:324
  46.4 6.5 %collective-permute-done.10.p2 = bf16[640,256]{1,0:T(8,128)(2,1)S(1)} collective-permute-done((bf16[640,256]{1,0:T(8,128)(2,1)S(1)}, bf16[640,256]{1,0:T(8,128)(2,1)S(1)}, u32[]{:S(2)}, u32[]{:S(2)}) %collective-permute-start.10) | collective-permute-done | bytes 327712 | tf_op jit(solution)/shard_map/ppermute | solution.py:324
  52.9 6.8 %collective-permute-done.11.refs_3_ = bf16[640,256]{1,0:T(8,128)(2,1)S(1)} collective-permute-done((bf16[640,256]{1,0:T(8,128)(2,1)S(1)}, bf16[640,256]{1,0:T(8,128)(2,1)S(1)}, u32[]{:S(2)}, u32[]{:S(2)}) %collective-permute-start.11) | collective-permute-done | bytes 327712 | tf_op jit(solution)/shard_map/ppermute | solution.py:324
  59.7 1.5 %collective-permute-done.9.p1 = bf16[640,256]{1,0:T(8,128)(2,1)S(1)} collective-permute-done((bf16[640,256]{1,0:T(8,128)(2,1)S(1)}, bf16[640,256]{1,0:T(8,128)(2,1)S(1)}, u32[]{:S(2)}, u32[]{:S(2)}) %collective-permute-start.9) | collective-permute-done | bytes 327712 | tf_op jit(solution)/shard_map/ppermute | solution.py:324
  62.3 1.5 %collective-permute-start.14 = (bf16[640,256]{1,0:T(8,128)(2,1)S(1)}, bf16[640,256]{1,0:T(8,128)(2,1)S(1)}, u32[]{:S(2)}, u32[]{:S(2)}) collective-permute-start(bf16[640,256]{1,0:T(8,128)(2,1)S(1)} %collective-permute-done.10.p2), channel_id=1, source_target_pairs={{0,2},{2,0},{1,3},{3,1},{4,6},{6,4},{5,7},{7,5},{8,10},{10,8},{9,1... | collective-permute-start | bytes 983048 | tf_op jit(solution)/shard_map/ppermute | solution.py:324
  64.5 7.1 %collective-permute-done.15.refs_7_ = bf16[640,256]{1,0:T(8,128)(2,1)S(1)} collective-permute-done((bf16[640,256]{1,0:T(8,128)(2,1)S(1)}, bf16[640,256]{1,0:T(8,128)(2,1)S(1)}, u32[]{:S(2)}, u32[]{:S(2)}) %collective-permute-start.15) | collective-permute-done | bytes 327712 | tf_op jit(solution)/shard_map/ppermute | solution.py:324
  71.5 1.4 %project.1.sums_ref = f32[2,256,256]{2,1,0:T(8,128)S(1)} custom-call(bf16[256,2560]{1,0:T(8,128)(2,1)S(1)} %get-tuple-element.48.own_ref, bf16[256,2560]{1,0:T(8,128)(2,1)S(1)} %collective-permute-done.4.other_ref, bf16[2,1280,256]{2,1,0:T(8,128)(2,1)S(1)} %copy-done.1, bf16[640,256]{1,0:T(8,128)(2,1)S(1)} %collective-permute-done.refs_0_, ...), custom_call_target="tpu_custom_call" | custom-call | flops 1006632960 | bytes 7000000 | tf_op jit(solution)/shard_map/project/pallas_call | solution.py:91
  73.0 5.0 %attention.1 = (bf16[256,1280]{1,0:T(8,128)(2,1)}, bf16[256,512]{1,0:T(8,128)(2,1)S(1)}) custom-call(bf16[256,2560]{1,0:T(8,128)(2,1)S(1)} %get-tuple-element.48.own_ref, bf16[256,2560]{1,0:T(8,128)(2,1)S(1)} %collective-permute-done.4.other_ref, bf16[640,256]{1,0:T(8,128)(2,1)S(1)} %collective-permute-done.5.p0, ...), custom_call_target="tpu_custom_call" | custom-call | flops 838860800 | bytes 5000000 | tf_op jit(solution)/shard_map/attention/pallas_call | solution.py:180
  78.8 1.5 %collective-permute-start.18 = (bf16[256,512]{1,0:T(8,128)(2,1)S(1)}, bf16[256,512]{1,0:T(8,128)(2,1)S(1)}, u32[]{:S(2)}, u32[]{:S(2)}) collective-permute-start(bf16[256,512]{1,0:T(8,128)(2,1)S(1)} %get-tuple-element.75.refs_12_), channel_id=1, source_target_pairs={{0,2},{2,0},{1,3},{3,1},{4,6},{6,4},{5,7},{7,5},{8,10},{10,8},{9,1... | collective-permute-start | bytes 786440 | tf_op jit(solution)/shard_map/ppermute | solution.py:324
  80.3 7.0 %collective-permute-done.17.refs_14_ = bf16[256,512]{1,0:T(8,128)(2,1)S(1)} collective-permute-done((bf16[256,512]{1,0:T(8,128)(2,1)S(1)}, bf16[256,512]{1,0:T(8,128)(2,1)S(1)}, u32[]{:S(2)}, u32[]{:S(2)}) %collective-permute-start.17) | collective-permute-done | bytes 262176 | tf_op jit(solution)/shard_map/ppermute | solution.py:329
  87.3 1.7 %collective-permute-start.19 = (bf16[256,512]{1,0:T(8,128)(2,1)S(1)}, bf16[256,512]{1,0:T(8,128)(2,1)S(1)}, u32[]{:S(2)}, u32[]{:S(2)}) collective-permute-start(bf16[256,512]{1,0:T(8,128)(2,1)S(1)} %get-tuple-element.75.refs_12_), channel_id=1, source_target_pairs={{0,12},{4,0},{8,4},{12,8},{1,13},{5,1},{9,5},{13,9},{2,14},{6,2},{... | collective-permute-start | bytes 786440 | tf_op jit(solution)/shard_map/ppermute | solution.py:329
  89.0 1.5 %collective-permute-start.20 = (bf16[256,512]{1,0:T(8,128)(2,1)S(1)}, bf16[256,512]{1,0:T(8,128)(2,1)S(1)}, u32[]{:S(2)}, u32[]{:S(2)}) collective-permute-start(bf16[256,512]{1,0:T(8,128)(2,1)S(1)} %collective-permute-done.17.refs_14_), channel_id=1, source_target_pairs={{0,2},{2,0},{1,3},{3,1},{4,6},{6,4},{5,7},{7,5},{8,10},{10,8},{9,1... | collective-permute-start | bytes 786440 | tf_op jit(solution)/shard_map/ppermute | solution.py:324
  90.5 3.8 %collective-permute-done.19.refs_15_ = bf16[256,512]{1,0:T(8,128)(2,1)S(1)} collective-permute-done((bf16[256,512]{1,0:T(8,128)(2,1)S(1)}, bf16[256,512]{1,0:T(8,128)(2,1)S(1)}, u32[]{:S(2)}, u32[]{:S(2)}) %collective-permute-start.19) | collective-permute-done | bytes 262176 | tf_op jit(solution)/shard_map/ppermute | solution.py:329
  96.6 1.5 %collective-permute-start.23 = (bf16[256,512]{1,0:T(8,128)(2,1)S(1)}, bf16[256,512]{1,0:T(8,128)(2,1)S(1)}, u32[]{:S(2)}, u32[]{:S(2)}) collective-permute-start(bf16[256,512]{1,0:T(8,128)(2,1)S(1)} %collective-permute-done.19.refs_15_), channel_id=1, source_target_pairs={{0,2},{2,0},{1,3},{3,1},{4,6},{6,4},{5,7},{7,5},{8,10},{10,8},{9,1... | collective-permute-start | bytes 786440 | tf_op jit(solution)/shard_map/ppermute | solution.py:324
  98.8 10.0 %collective-permute-done.24.refs_6_ = bf16[256,256]{1,0:T(8,128)(2,1)S(1)} collective-permute-done((bf16[256,256]{1,0:T(8,128)(2,1)S(1)}, bf16[256,256]{1,0:T(8,128)(2,1)S(1)}, u32[]{:S(2)}, u32[]{:S(2)}) %collective-permute-start.24) | collective-permute-done | bytes 131104 | tf_op jit(solution)/shard_map/ppermute | solution.py:329
  108.8 1.6 %collective-permute-start.25 = (bf16[256,256]{1,0:T(8,128)(2,1)S(1)}, bf16[256,256]{1,0:T(8,128)(2,1)S(1)}, u32[]{:S(2)}, u32[]{:S(2)}) collective-permute-start(bf16[256,256]{1,0:T(8,128)(2,1)S(1)} %slice.7), channel_id=1, source_target_pairs={{0,2},{2,0},{1,3},{3,1},{4,6},{6,4},{5,7},{7,5},{8,10},{10,8},{9,1... | collective-permute-start | bytes 393224 | tf_op jit(solution)/shard_map/ppermute | solution.py:324
  110.3 1.7 %gradient.2 = (f32[2,640,256]{2,1,0:T(8,128)S(1)}, f32[2,256]{1,0:T(2,128)S(1)}) custom-call(bf16[2,640,256]{2,1,0:T(8,128)(2,1)S(1)} %collective-permute-done.13.refs_0_.refs_1_, bf16[2,640,256]{2,1,0:T(8,128)(2,1)S(1)} %collective-permute-done.13.refs_0_.refs_1_, bf16[2,640,256]{2,1,0:T(8,128)(2,1)S(1)} %collective-permute-done.16.refs_2_.refs_3_.refs_4_.refs_5_, ...), custom_call_target="tpu_custom_call" | custom-call | flops 1006632960 | bytes 5000000 | tf_op jit(solution)/shard_map/gradient/pallas_call | solution.py:253
  112.1 1.7 %collective-permute-done.25.refs_5_ = bf16[256,256]{1,0:T(8,128)(2,1)S(1)} collective-permute-done((bf16[256,256]{1,0:T(8,128)(2,1)S(1)}, bf16[256,256]{1,0:T(8,128)(2,1)S(1)}, u32[]{:S(2)}, u32[]{:S(2)}) %collective-permute-start.25) | collective-permute-done | bytes 131104 | tf_op jit(solution)/shard_map/ppermute | solution.py:324
  113.8 1.8 %gradient.3 = (f32[2,640,256]{2,1,0:T(8,128)}, f32[2,256]{1,0:T(2,128)}) custom-call(bf16[2,640,256]{2,1,0:T(8,128)(2,1)S(1)} %collective-permute-done.13.refs_0_.refs_1_, bf16[2,640,256]{2,1,0:T(8,128)(2,1)S(1)} %collective-permute-done.13.refs_0_.refs_1_, bf16[2,640,256]{2,1,0:T(8,128)(2,1)S(1)} %collective-permute-done.21.refs_6_.refs_7_.refs_2_.refs_3_, ...), custom_call_target="tpu_custom_call" | custom-call | flops 335544320 | bytes 5000000 | tf_op jit(solution)/shard_map/gradient/pallas_call | solution.py:253
  (53 shorter events, 11.4 us)
Async XLA Ops:
  0.6 7.2 %copy-start = (bf16[256,2560]{1,0:T(8,128)(2,1)S(1)}, bf16[256,2560]{1,0:T(8,128)(2,1)}, u32[]{:S(2)}) copy-start(bf16[256,2560]{1,0:T(8,128)(2,1)} %values_ref.1) | copy-start | bytes 3932164
  1.8 12.8 %collective-permute-start = (bf16[640,256]{1,0:T(8,128)(2,1)S(1)}, bf16[640,256]{1,0:T(8,128)(2,1)S(1)}, u32[]{:S(2)}, u32[]{:S(2)}) collective-permute-start(bf16[640,256]{1,0:T(8,128)(2,1)S(1)} %dynamic-slice_bitcast_fusion), channel_id=1, source_target_pairs={{0,4},{4,8},{8,12},{12,0},{1,5},{5,9},{9,13},{13,1},{2,6},{6,10},{... | collective-permute-start | bytes 983048 | tf_op jit(solution)/shard_map/ppermute | solution.py:329
  6.5 1.2 %collective-permute-start.1 = (f32[256,1]{0,1:T(1,128)S(1)}, f32[256,1]{0,1:T(1,128)S(1)}, u32[]{:S(2)}, u32[]{:S(2)}) collective-permute-start(f32[256,1]{0,1:T(1,128)S(1)} %bitcast.3), channel_id=1, source_target_pairs={{0,1},{1,0},{2,3},{3,2},{4,5},{5,4},{6,7},{7,6},{8,9},{9,8},{10,11... | collective-permute-start | bytes 3080 | tf_op jit(solution)/shard_map/ppermute | solution.py:324
  7.9 56.4 %copy-start.5 = (bf16[2,256]{1,0:T(2,128)(2,1)S(1)}, bf16[2,256]{1,0:T(2,128)(2,1)}, u32[]{:S(2)}) copy-start(bf16[2,256]{1,0:T(2,128)(2,1)} %param.11) | copy-start | bytes 3076
  8.8 62.7 %copy-start.1 = (bf16[2,1280,256]{2,1,0:T(8,128)(2,1)S(1)}, bf16[2,1280,256]{2,1,0:T(8,128)(2,1)}, u32[]{:S(2)}) copy-start(bf16[2,1280,256]{2,1,0:T(8,128)(2,1)} %weight_ref.1) | copy-start | bytes 3932164
  14.6 11.4 %collective-permute-start.4 = (bf16[256,2560]{1,0:T(8,128)(2,1)S(1)}, bf16[256,2560]{1,0:T(8,128)(2,1)S(1)}, u32[]{:S(2)}, u32[]{:S(2)}) collective-permute-start(bf16[256,2560]{1,0:T(8,128)(2,1)S(1)} %get-tuple-element.48.own_ref), channel_id=1, source_target_pairs={{0,1},{1,0},{2,3},{3,2},{4,5},{5,4},{6,7},{7,6},{8,9},{9,8},{10,11... | collective-permute-start | bytes 3932168 | tf_op jit(solution)/shard_map/ppermute | solution.py:324
  14.6 10.1 %collective-permute-start.2 = (bf16[640,256]{1,0:T(8,128)(2,1)S(1)}, bf16[640,256]{1,0:T(8,128)(2,1)S(1)}, u32[]{:S(2)}, u32[]{:S(2)}) collective-permute-start(bf16[640,256]{1,0:T(8,128)(2,1)S(1)} %collective-permute-done.refs_0_), channel_id=1, source_target_pairs={{0,16},{16,0},{1,17},{17,1},{2,18},{18,2},{3,19},{19,3},{4,20},{20... | collective-permute-start | bytes 983048 | tf_op jit(solution)/shard_map/ppermute | solution.py:324
  16.1 9.8 %collective-permute-start.3 = (bf16[640,256]{1,0:T(8,128)(2,1)S(1)}, bf16[640,256]{1,0:T(8,128)(2,1)S(1)}, u32[]{:S(2)}, u32[]{:S(2)}) collective-permute-start(bf16[640,256]{1,0:T(8,128)(2,1)S(1)} %dynamic-slice_bitcast_fusion), channel_id=1, source_target_pairs={{0,12},{4,0},{8,4},{12,8},{1,13},{5,1},{9,5},{13,9},{2,14},{6,2},{... | collective-permute-start | bytes 983048 | tf_op jit(solution)/shard_map/ppermute | solution.py:329
  17.8 17.6 %collective-permute-start.8 = (bf16[2,640,256]{2,1,0:T(8,128)(2,1)S(1)}, bf16[2,640,256]{2,1,0:T(8,128)(2,1)S(1)}, u32[]{:S(2)}, u32[]{:S(2)}) collective-permute-start(bf16[2,640,256]{2,1,0:T(8,128)(2,1)S(1)} %get-tuple-element.54), channel_id=1, source_target_pairs={{0,2},{2,0},{1,3},{3,1},{4,6},{6,4},{5,7},{7,5},{8,10},{10,8},{9,1... | collective-permute-start | bytes 1966088 | tf_op jit(solution)/shard_map/ppermute | solution.py:324
  25.9 10.8 %collective-permute-start.5 = (bf16[640,256]{1,0:T(8,128)(2,1)S(1)}, bf16[640,256]{1,0:T(8,128)(2,1)S(1)}, u32[]{:S(2)}, u32[]{:S(2)}) collective-permute-start(bf16[640,256]{1,0:T(8,128)(2,1)S(1)} %collective-permute-done.refs_0_), channel_id=1, source_target_pairs={{0,4},{4,8},{8,12},{12,0},{1,5},{5,9},{9,13},{13,1},{2,6},{6,10},{... | collective-permute-start | bytes 983048 | tf_op jit(solution)/shard_map/ppermute | solution.py:329
  25.9 10.8 %collective-permute-start.6 = (bf16[640,256]{1,0:T(8,128)(2,1)S(1)}, bf16[640,256]{1,0:T(8,128)(2,1)S(1)}, u32[]{:S(2)}, u32[]{:S(2)}) collective-permute-start(bf16[640,256]{1,0:T(8,128)(2,1)S(1)} %collective-permute-done.3.refs_4_), channel_id=1, source_target_pairs={{0,16},{16,0},{1,17},{17,1},{2,18},{18,2},{3,19},{19,3},{4,20},{20... | collective-permute-start | bytes 983048 | tf_op jit(solution)/shard_map/ppermute | solution.py:324
  26.5 15.0 %collective-permute-start.7 = (bf16[640,256]{1,0:T(8,128)(2,1)S(1)}, bf16[640,256]{1,0:T(8,128)(2,1)S(1)}, u32[]{:S(2)}, u32[]{:S(2)}) collective-permute-start(bf16[640,256]{1,0:T(8,128)(2,1)S(1)} %collective-permute-done.refs_0_), channel_id=1, source_target_pairs={{0,2},{2,0},{1,3},{3,1},{4,6},{6,4},{5,7},{7,5},{8,10},{10,8},{9,1... | collective-permute-start | bytes 983048 | tf_op jit(solution)/shard_map/ppermute | solution.py:324
  41.5 19.6 %collective-permute-start.13 = (bf16[2,640,256]{2,1,0:T(8,128)(2,1)S(1)}, bf16[2,640,256]{2,1,0:T(8,128)(2,1)S(1)}, u32[]{:S(2)}, u32[]{:S(2)}) collective-permute-start(bf16[2,640,256]{2,1,0:T(8,128)(2,1)S(1)} %get-tuple-element.60), channel_id=1, source_target_pairs={{0,0},{1,8},{4,4},{5,12},{8,1},{9,9},{12,5},{13,13},{2,2},{3,10},{... | collective-permute-start | bytes 1966088 | tf_op jit(solution)/shard_map/ppermute | solution.py:357
  42.2 10.6 %collective-permute-start.10 = (bf16[640,256]{1,0:T(8,128)(2,1)S(1)}, bf16[640,256]{1,0:T(8,128)(2,1)S(1)}, u32[]{:S(2)}, u32[]{:S(2)}) collective-permute-start(bf16[640,256]{1,0:T(8,128)(2,1)S(1)} %collective-permute-done.5.p0), channel_id=1, source_target_pairs={{0,16},{16,0},{1,17},{17,1},{2,18},{18,2},{3,19},{19,3},{4,20},{20... | collective-permute-start | bytes 983048 | tf_op jit(solution)/shard_map/ppermute | solution.py:324
  42.8 16.9 %collective-permute-start.11 = (bf16[640,256]{1,0:T(8,128)(2,1)S(1)}, bf16[640,256]{1,0:T(8,128)(2,1)S(1)}, u32[]{:S(2)}, u32[]{:S(2)}) collective-permute-start(bf16[640,256]{1,0:T(8,128)(2,1)S(1)} %collective-permute-done.7.refs_1_), channel_id=1, source_target_pairs={{0,16},{16,0},{1,17},{17,1},{2,18},{18,2},{3,19},{19,3},{4,20},{20... | collective-permute-start | bytes 983048 | tf_op jit(solution)/shard_map/ppermute | solution.py:324
  44.3 15.4 %collective-permute-start.12 = (bf16[640,256]{1,0:T(8,128)(2,1)S(1)}, bf16[640,256]{1,0:T(8,128)(2,1)S(1)}, u32[]{:S(2)}, u32[]{:S(2)}) collective-permute-start(bf16[640,256]{1,0:T(8,128)(2,1)S(1)} %collective-permute-done.3.refs_4_), channel_id=1, source_target_pairs={{0,2},{2,0},{1,3},{3,1},{4,6},{6,4},{5,7},{7,5},{8,10},{10,8},{9,1... | collective-permute-start | bytes 983048 | tf_op jit(solution)/shard_map/ppermute | solution.py:324
  45.8 15.3 %collective-permute-start.9 = (bf16[640,256]{1,0:T(8,128)(2,1)S(1)}, bf16[640,256]{1,0:T(8,128)(2,1)S(1)}, u32[]{:S(2)}, u32[]{:S(2)}) collective-permute-start(bf16[640,256]{1,0:T(8,128)(2,1)S(1)} %collective-permute-done.5.p0), channel_id=1, source_target_pairs={{0,2},{2,0},{1,3},{3,1},{4,6},{6,4},{5,7},{7,5},{8,10},{10,8},{9,1... | collective-permute-start | bytes 983048 | tf_op jit(solution)/shard_map/ppermute | solution.py:324
  61.2 17.6 %collective-permute-start.16 = (bf16[2,640,256]{2,1,0:T(8,128)(2,1)S(1)}, bf16[2,640,256]{2,1,0:T(8,128)(2,1)S(1)}, u32[]{:S(2)}, u32[]{:S(2)}) collective-permute-start(bf16[2,640,256]{2,1,0:T(8,128)(2,1)S(1)} %get-tuple-element.71), channel_id=1, source_target_pairs={{0,4},{1,12},{4,0},{5,8},{8,5},{9,13},{12,1},{13,9},{2,6},{3,14},{... | collective-permute-start | bytes 1966088 | tf_op jit(solution)/shard_map/ppermute | solution.py:357
  61.8 9.8 %collective-permute-start.15 = (bf16[640,256]{1,0:T(8,128)(2,1)S(1)}, bf16[640,256]{1,0:T(8,128)(2,1)S(1)}, u32[]{:S(2)}, u32[]{:S(2)}) collective-permute-start(bf16[640,256]{1,0:T(8,128)(2,1)S(1)} %collective-permute-done.12.refs_5_), channel_id=1, source_target_pairs={{0,16},{16,0},{1,17},{17,1},{2,18},{18,2},{3,19},{19,3},{4,20},{20... | collective-permute-start | bytes 983048 | tf_op jit(solution)/shard_map/ppermute | solution.py:324
  62.3 10.7 %collective-permute-start.14 = (bf16[640,256]{1,0:T(8,128)(2,1)S(1)}, bf16[640,256]{1,0:T(8,128)(2,1)S(1)}, u32[]{:S(2)}, u32[]{:S(2)}) collective-permute-start(bf16[640,256]{1,0:T(8,128)(2,1)S(1)} %collective-permute-done.10.p2), channel_id=1, source_target_pairs={{0,2},{2,0},{1,3},{3,1},{4,6},{6,4},{5,7},{7,5},{8,10},{10,8},{9,1... | collective-permute-start | bytes 983048 | tf_op jit(solution)/shard_map/ppermute | solution.py:324
  64.5 8.5 %copy-start.2 = (bf16[256,1280]{1,0:T(8,128)(2,1)S(1)}, bf16[256,1280]{1,0:T(8,128)(2,1)}, u32[]{:S(2)}) copy-start(bf16[256,1280]{1,0:T(8,128)(2,1)} %queries_ref.1) | copy-start | bytes 1966084
  64.5 8.5 %copy-start.3 = (bf16[256,1280]{1,0:T(8,128)(2,1)S(1)}, bf16[256,1280]{1,0:T(8,128)(2,1)}, u32[]{:S(2)}) copy-start(bf16[256,1280]{1,0:T(8,128)(2,1)} %cotangent_ref.1) | copy-start | bytes 1966084
  78.8 8.5 %collective-permute-start.17 = (bf16[256,512]{1,0:T(8,128)(2,1)S(1)}, bf16[256,512]{1,0:T(8,128)(2,1)S(1)}, u32[]{:S(2)}, u32[]{:S(2)}) collective-permute-start(bf16[256,512]{1,0:T(8,128)(2,1)S(1)} %get-tuple-element.75.refs_12_), channel_id=1, source_target_pairs={{0,4},{4,8},{8,12},{12,0},{1,5},{5,9},{9,13},{13,1},{2,6},{6,10},{... | collective-permute-start | bytes 786440 | tf_op jit(solution)/shard_map/ppermute | solution.py:329
  78.8 8.5 %collective-permute-start.18 = (bf16[256,512]{1,0:T(8,128)(2,1)S(1)}, bf16[256,512]{1,0:T(8,128)(2,1)S(1)}, u32[]{:S(2)}, u32[]{:S(2)}) collective-permute-start(bf16[256,512]{1,0:T(8,128)(2,1)S(1)} %get-tuple-element.75.refs_12_), channel_id=1, source_target_pairs={{0,2},{2,0},{1,3},{3,1},{4,6},{6,4},{5,7},{7,5},{8,10},{10,8},{9,1... | collective-permute-start | bytes 786440 | tf_op jit(solution)/shard_map/ppermute | solution.py:324
  87.3 7.0 %collective-permute-start.19 = (bf16[256,512]{1,0:T(8,128)(2,1)S(1)}, bf16[256,512]{1,0:T(8,128)(2,1)S(1)}, u32[]{:S(2)}, u32[]{:S(2)}) collective-permute-start(bf16[256,512]{1,0:T(8,128)(2,1)S(1)} %get-tuple-element.75.refs_12_), channel_id=1, source_target_pairs={{0,12},{4,0},{8,4},{12,8},{1,13},{5,1},{9,5},{13,9},{2,14},{6,2},{... | collective-permute-start | bytes 786440 | tf_op jit(solution)/shard_map/ppermute | solution.py:329
  89.0 6.4 %collective-permute-start.20 = (bf16[256,512]{1,0:T(8,128)(2,1)S(1)}, bf16[256,512]{1,0:T(8,128)(2,1)S(1)}, u32[]{:S(2)}, u32[]{:S(2)}) collective-permute-start(bf16[256,512]{1,0:T(8,128)(2,1)S(1)} %collective-permute-done.17.refs_14_), channel_id=1, source_target_pairs={{0,2},{2,0},{1,3},{3,1},{4,6},{6,4},{5,7},{7,5},{8,10},{10,8},{9,1... | collective-permute-start | bytes 786440 | tf_op jit(solution)/shard_map/ppermute | solution.py:324
  95.4 14.9 %collective-permute-start.26 = (bf16[2,640,256]{2,1,0:T(8,128)(2,1)S(1)}, bf16[2,640,256]{2,1,0:T(8,128)(2,1)S(1)}, u32[]{:S(2)}, u32[]{:S(2)}) collective-permute-start(bf16[2,640,256]{2,1,0:T(8,128)(2,1)S(1)} %collective-permute-done.16.refs_2_.refs_3_.refs_4_.refs_5_), channel_id=1, source_target_pairs={{0,1},{1,0},{2,3},{3,2},{4,5},{5,4},{6,7},{7,6},{8,9},{9,8},{10,11... | collective-permute-start | bytes 1966088 | tf_op jit(solution)/shard_map/ppermute | solution.py:324
  95.4 14.9 %collective-permute-start.21 = (bf16[2,640,256]{2,1,0:T(8,128)(2,1)S(1)}, bf16[2,640,256]{2,1,0:T(8,128)(2,1)S(1)}, u32[]{:S(2)}, u32[]{:S(2)}) collective-permute-start(bf16[2,640,256]{2,1,0:T(8,128)(2,1)S(1)} %collective-permute-done.13.refs_0_.refs_1_), channel_id=1, source_target_pairs={{0,1},{1,0},{2,3},{3,2},{4,5},{5,4},{6,7},{7,6},{8,9},{9,8},{10,11... | collective-permute-start | bytes 1966088 | tf_op jit(solution)/shard_map/ppermute | solution.py:324
  95.9 12.8 %collective-permute-start.22 = (bf16[256,512]{1,0:T(8,128)(2,1)S(1)}, bf16[256,512]{1,0:T(8,128)(2,1)S(1)}, u32[]{:S(2)}, u32[]{:S(2)}) collective-permute-start(bf16[256,512]{1,0:T(8,128)(2,1)S(1)} %collective-permute-done.17.refs_14_), channel_id=1, source_target_pairs={{0,4},{4,8},{8,12},{12,0},{1,5},{5,9},{9,13},{13,1},{2,6},{6,10},{... | collective-permute-start | bytes 786440 | tf_op jit(solution)/shard_map/ppermute | solution.py:329
  96.6 12.1 %collective-permute-start.23 = (bf16[256,512]{1,0:T(8,128)(2,1)S(1)}, bf16[256,512]{1,0:T(8,128)(2,1)S(1)}, u32[]{:S(2)}, u32[]{:S(2)}) collective-permute-start(bf16[256,512]{1,0:T(8,128)(2,1)S(1)} %collective-permute-done.19.refs_15_), channel_id=1, source_target_pairs={{0,2},{2,0},{1,3},{3,1},{4,6},{6,4},{5,7},{7,5},{8,10},{10,8},{9,1... | collective-permute-start | bytes 786440 | tf_op jit(solution)/shard_map/ppermute | solution.py:324
  98.1 10.6 %collective-permute-start.24 = (bf16[256,256]{1,0:T(8,128)(2,1)S(1)}, bf16[256,256]{1,0:T(8,128)(2,1)S(1)}, u32[]{:S(2)}, u32[]{:S(2)}) collective-permute-start(bf16[256,256]{1,0:T(8,128)(2,1)S(1)} %slice.6), channel_id=1, source_target_pairs={{0,4},{4,8},{8,12},{12,0},{1,5},{5,9},{9,13},{13,1},{2,6},{6,10},{... | collective-permute-start | bytes 393224 | tf_op jit(solution)/shard_map/ppermute | solution.py:329
  108.8 5.0 %collective-permute-start.25 = (bf16[256,256]{1,0:T(8,128)(2,1)S(1)}, bf16[256,256]{1,0:T(8,128)(2,1)S(1)}, u32[]{:S(2)}, u32[]{:S(2)}) collective-permute-start(bf16[256,256]{1,0:T(8,128)(2,1)S(1)} %slice.7), channel_id=1, source_target_pairs={{0,2},{2,0},{1,3},{3,1},{4,6},{6,4},{5,7},{7,5},{8,10},{10,8},{9,1... | collective-permute-start | bytes 393224 | tf_op jit(solution)/shard_map/ppermute | solution.py:324
  (1 other events, 5.9 us)

commit v19 on v13

--- a/solution.py
+++ b/solution.py
@@ -142,9 +142,7 @@
 
 
 def attention_kernel(distances, own_ref, other_ref, *refs):
-    pairs, refs = refs[4:6], refs[:4] + refs[6:]
-    pieces = [*refs[:4], *(pair.at[at] for pair in pairs for at in range(2))]
-    refs = refs[4:]
+    pieces, refs = refs[: 4 * len(distances)], refs[4 * len(distances) :]
     sums_ref, bias_ref, cosine_ref, sine_ref, queries_ref, cotangent_ref = refs[:6]
     grad_query_ref, pair_ref, raw_ref = refs[6:]
     group = lax.axis_index("groups")
@@ -167,7 +165,8 @@
 def attention(gathered, normed, normed_other, sums, bias, cosine, sine, queries, cotangent):
     length = normed.shape[0]
     distances = tuple(distance for distance, _ in gathered)
-    pieces = [piece for _, parts in gathered for piece in parts]
+    pieces = [piece for _, four in gathered for piece in four]
+    columns = pieces[0].shape[1]
     operands = (normed, normed_other, *pieces, sums, bias, cosine, sine, queries, cotangent)
     return pl.pallas_call(
         functools.partial(attention_kernel, distances),
@@ -176,7 +175,7 @@
         scratch_shapes=[pltpu.VMEM(sums.shape, jnp.float32)],
         out_shape=[
             jax.ShapeDtypeStruct(queries.shape, jnp.bfloat16),
-            jax.ShapeDtypeStruct((length, 2 * bias.shape[1]), jnp.bfloat16),
+            jax.ShapeDtypeStruct((length, 2 * columns), jnp.bfloat16),
         ],
         compiler_params=pltpu.CompilerParams(vmem_limit_bytes=VMEM_BYTES),
         cost_estimate=pl.CostEstimate(
@@ -375,40 +374,44 @@
     normed, kept_even, sent_even, kept_odd, sent_odd = norm(
         activations, scale, gain[None, :], share
     )
-    up, piece, normed, sent_even, sent_odd = lax.optimization_barrier(
-        (up, piece, normed, sent_even, sent_odd)
+    arrived_even = swapped(sent_even, "dp")
+    up, piece, normed, sent_odd, arrived_even = lax.optimization_barrier(
+        (up, piece, normed, sent_odd, arrived_even)
     )
     up_x, up_y, down = swapped(up, "dp"), swapped(up, "groups"), turned(piece, "blk", -1)
+    up, up_x, up_y, down, normed, sent_odd = lax.optimization_barrier(
+        (up, up_x, up_y, down, normed, sent_odd)
+    )
     normed_other = swapped(normed, "sub")
-    up, up_x, up_y, down, normed_other, sent_even, sent_odd = lax.optimization_barrier(
-        (up, up_x, up_y, down, normed_other, sent_even, sent_odd)
-    )
-    twice = turned(pack(up, up_x), "blk", 1)
-    down_x, down_y, up_both = swapped(down, "dp"), swapped(down, "groups"), swapped(up_x, "groups")
-    arrived_even = swapped(sent_even, "dp")
-    twice, down_x, down_y, up_both, arrived_even, sent_odd = lax.optimization_barrier(
-        (twice, down_x, down_y, up_both, arrived_even, sent_odd)
-    )
-    twice_y, down_both = swapped(twice, "groups"), swapped(down_y, "dp")
+    down_x, down_y = swapped(down, "dp"), swapped(down, "groups")
+    twice = turned(up, "blk", 1)
+    twice, down_x, down_y, up_x, sent_odd, arrived_even, normed_other = lax.optimization_barrier(
+        (twice, down_x, down_y, up_x, sent_odd, arrived_even, normed_other)
+    )
+    twice_x, twice_y = swapped(twice, "dp"), swapped(twice, "groups")
+    up_both = swapped(up_x, "groups")
+    even = sent_along(pack(kept_even, arrived_even), 0)
     arrived_odd = swapped(sent_odd, "dp")
-    even = sent_along(pack(kept_even, arrived_even), 0)
+    twice_x, twice_y, up_both, arrived_odd, even = lax.optimization_barrier(
+        (twice_x, twice_y, up_both, arrived_odd, even)
+    )
+    down_both, twice_both = swapped(down_x, "groups"), swapped(twice_y, "dp")
+    odd = sent_along(pack(kept_odd, arrived_odd), 1)
     sums = project(normed, normed_other, kv_weight, [(1, (up, up_x, up_y, up_both))])
-    twice_y, down_both, arrived_odd, even, sums, cosine, sine = lax.optimization_barrier(
-        (twice_y, down_both, arrived_odd, even, sums, cosine, sine)
-    )
-    odd = sent_along(pack(kept_odd, arrived_odd), 1)
-    even_other = swapped(even, "sub")
-    gathered = [(-1, (down, down_x, down_y, down_both)), (2, (twice, twice_y))]
+    gathered = [
+        (-1, (down, down_x, down_y, down_both)),
+        (2, (twice, twice_x, twice_y, twice_both)),
+    ]
     grad_query, grad_pair = attention(
         gathered, normed, normed_other, sums, bias, cosine, sine, queries, cotangent
     )
 
-    grad_pair, odd, even_other = lax.optimization_barrier((grad_pair, odd, even_other))
+    grad_pair, odd = lax.optimization_barrier((grad_pair, odd))
     pair_up, pair_x = turned(grad_pair, "blk", 1), swapped(grad_pair, "dp")
     pair_up, pair_x, grad_pair, even, odd = lax.optimization_barrier(
         (pair_up, pair_x, grad_pair, even, odd)
     )
-    slabs = ((even, even_other), (odd, swapped(odd, "sub")))
+    slabs = ((even, swapped(even, "sub")), (odd, swapped(odd, "sub")))
     pair_down, pair_up_x = turned(grad_pair, "blk", -1), swapped(pair_up, "dp")
     pair_down, pair_up_x, pair_up = lax.optimization_barrier((pair_down, pair_up_x, pair_up))
     pair_twice, pair_down_x = turned(pair_up, "blk", 1), swapped(pair_down, "dp")

time: 118 us -> 115 us (0.975); the launches traced: 116 us -> 115 us
    ppermute x6, waiting for transfers between devices: 30.6 us -> 36.8 us  [turned(): lax.ppermute(block, axis, [(i, (i + distance) % size) for i in range(size)])]
    ppermute x2, waiting for transfers between devices: 6.72 us -> 0.81 us  [sent_along(): return lax.ppermute(slabs, ('blk', 'sub'), route)]
    ppermute x17 -> x19, starting transfers between devices: 20.6 us -> 14.9 us  [swapped(): return lax.ppermute(block, axis, [(0, 1), (1, 0)])]
    ppermute x2, starting transfers between devices: 0.77 us -> 3.76 us  [sent_along(): return lax.ppermute(slabs, ('blk', 'sub'), route)]
    ppermute x6, starting transfers between devices: 6.76 us -> 9.7 us  [turned(): lax.ppermute(block, axis, [(i, (i + distance) % size) for i in range(size)])]
    ppermute x17 -> x19, waiting for transfers between devices: 34.6 us -> 33.5 us  [swapped(): return lax.ppermute(block, axis, [(0, 1), (1, 0)])]
  transfers between devices with their start and end apart: 25 -> 27, of which waited for: 19 -> 18; matrix products, arithmetic and copies ran while one was open for 2% -> 2% of each run, Pallas kernels for 8% -> 8%
where the time goes in v19:
time: 115 us
  waiting for transfers between devices  71.2 us (62%)
  starting transfers between devices  28.3 us (25%)
  Pallas kernels  11 us (10%)
  other arithmetic  2.4 us (2%)
  local copies, waits for them, and re-layouts  1.3 us (1%)
    ppermute x6, waiting for transfers between devices, turned(): lax.ppermute(block, axis, [(i, (i + distance) % size) for i in range(size)])  36.8 us
    ppermute x19, waiting for transfers between devices, swapped(): return lax.ppermute(block, axis, [(0, 1), (1, 0)])  33.5 us
    ppermute x19, starting transfers between devices, swapped(): return lax.ppermute(block, axis, [(0, 1), (1, 0)])  14.9 us
    ppermute x6, starting transfers between devices, turned(): lax.ppermute(block, axis, [(i, (i + distance) % size) for i in range(size)])  9.7 us
    pallas_call x1, Pallas kernels, attention(): pl.pallas_call(functools.partial(attention_kernel, distances), in_specs=[...  5.5 us
    ppermute x2, starting transfers between devices, sent_along(): return lax.ppermute(slabs, ('blk', 'sub'), route)  3.76 us
    pallas_call x2, Pallas kernels, gradient(): pl.pallas_call(functools.partial(gradient_kernel, tuple(some), sums is No...  3.49 us
  transfers between devices with their start and end apart: 27, of which 18 were waited for; matrix products, arithmetic and copies ran while one was open for 2% of the time, Pallas kernels for 8%

profile of v19, /device:TPU:0, one launch (start us, length us, event | category | flops | bytes accessed | tf_op | source)
XLA Modules:
  0.0 115.1 jit_solution(8879372676401683849)
XLA Ops:
  0.7 1.1 dynamic-slice_bitcast_fusion
  1.8 3.1 %collective-permute-start = (bf16[640,256]{1,0:T(8,128)(2,1)S(1)}, bf16[640,256]{1,0:T(8,128)(2,1)S(1)}, u32[]{:S(2)}, u32[]{:S(2)}) collective-permute-start(bf16[640,256]{1,0:T(8,128)(2,1)S(1)} %dynamic-slice_bitcast_fusion), channel_id=1, source_target_pairs={{0,4},{4,8},{8,12},{12,0},{1,5},{5,9},{9,13},{13,1},{2,6},{6,10},{... | collective-permute-start | bytes 983048 | tf_op jit(solution)/shard_map/ppermute | solution.py:311
  4.8 1.7 %multiply_reduce_fusion = f32[256]{0:T(256)S(1)} fusion(bf16[256,2560]{1,0:T(8,128)(2,1)} %values_ref.1), kind=kLoop, calls=%fused_computation | loop fusion | flops 1965824 | bytes 1311744 | tf_op jit(solution)/shard_map/reduce_sum | solution.py:346
  6.7 1.0 collective-permute-done.1
  8.8 1.6 %collective-permute-start.2 = (bf16[640,256]{1,0:T(8,128)(2,1)S(1)}, bf16[640,256]{1,0:T(8,128)(2,1)S(1)}, u32[]{:S(2)}, u32[]{:S(2)}) collective-permute-start(bf16[640,256]{1,0:T(8,128)(2,1)S(1)} %get-tuple-element.51), channel_id=1, source_target_pairs={{0,2},{2,0},{1,3},{3,1},{4,6},{6,4},{5,7},{7,5},{8,10},{10,8},{9,1... | collective-permute-start | bytes 983048 | tf_op jit(solution)/shard_map/ppermute | solution.py:306
  10.4 4.2 %collective-permute-done.refs_0_ = bf16[640,256]{1,0:T(8,128)(2,1)S(1)} collective-permute-done((bf16[640,256]{1,0:T(8,128)(2,1)S(1)}, bf16[640,256]{1,0:T(8,128)(2,1)S(1)}, u32[]{:S(2)}, u32[]{:S(2)}) %collective-permute-start) | collective-permute-done | bytes 327712 | tf_op jit(solution)/shard_map/ppermute | solution.py:311
  14.6 4.1 %collective-permute-done.2.arrived_ref = bf16[640,256]{1,0:T(8,128)(2,1)S(1)} collective-permute-done((bf16[640,256]{1,0:T(8,128)(2,1)S(1)}, bf16[640,256]{1,0:T(8,128)(2,1)S(1)}, u32[]{:S(2)}, u32[]{:S(2)}) %collective-permute-start.2) | collective-permute-done | bytes 327712 | tf_op jit(solution)/shard_map/ppermute | solution.py:306
  18.7 1.5 %collective-permute-start.3 = (bf16[640,256]{1,0:T(8,128)(2,1)S(1)}, bf16[640,256]{1,0:T(8,128)(2,1)S(1)}, u32[]{:S(2)}, u32[]{:S(2)}) collective-permute-start(bf16[640,256]{1,0:T(8,128)(2,1)S(1)} %collective-permute-done.refs_0_), channel_id=1, source_target_pairs={{0,2},{2,0},{1,3},{3,1},{4,6},{6,4},{5,7},{7,5},{8,10},{10,8},{9,1... | collective-permute-start | bytes 983048 | tf_op jit(solution)/shard_map/ppermute | solution.py:306
  20.2 1.5 %collective-permute-start.4 = (bf16[640,256]{1,0:T(8,128)(2,1)S(1)}, bf16[640,256]{1,0:T(8,128)(2,1)S(1)}, u32[]{:S(2)}, u32[]{:S(2)}) collective-permute-start(bf16[640,256]{1,0:T(8,128)(2,1)S(1)} %collective-permute-done.refs_0_), channel_id=1, source_target_pairs={{0,16},{16,0},{1,17},{17,1},{2,18},{18,2},{3,19},{19,3},{4,20},{20... | collective-permute-start | bytes 983048 | tf_op jit(solution)/shard_map/ppermute | solution.py:306
  21.7 2.2 %collective-permute-start.5 = (bf16[640,256]{1,0:T(8,128)(2,1)S(1)}, bf16[640,256]{1,0:T(8,128)(2,1)S(1)}, u32[]{:S(2)}, u32[]{:S(2)}) collective-permute-start(bf16[640,256]{1,0:T(8,128)(2,1)S(1)} %dynamic-slice_bitcast_fusion), channel_id=1, source_target_pairs={{0,12},{4,0},{8,4},{12,8},{1,13},{5,1},{9,5},{13,9},{2,14},{6,2},{... | collective-permute-start | bytes 983048 | tf_op jit(solution)/shard_map/ppermute | solution.py:311
  23.9 3.7 %collective-permute-done.3.refs_1_ = bf16[640,256]{1,0:T(8,128)(2,1)S(1)} collective-permute-done((bf16[640,256]{1,0:T(8,128)(2,1)S(1)}, bf16[640,256]{1,0:T(8,128)(2,1)S(1)}, u32[]{:S(2)}, u32[]{:S(2)}) %collective-permute-start.3) | collective-permute-done | bytes 327712 | tf_op jit(solution)/shard_map/ppermute | solution.py:306
  27.7 1.2 %collective-permute-done.4.refs_2_ = bf16[640,256]{1,0:T(8,128)(2,1)S(1)} collective-permute-done((bf16[640,256]{1,0:T(8,128)(2,1)S(1)}, bf16[640,256]{1,0:T(8,128)(2,1)S(1)}, u32[]{:S(2)}, u32[]{:S(2)}) %collective-permute-start.4) | collective-permute-done | bytes 327712 | tf_op jit(solution)/shard_map/ppermute | solution.py:306
  28.9 1.2 %collective-permute-done.5.refs_0_ = bf16[640,256]{1,0:T(8,128)(2,1)S(1)} collective-permute-done((bf16[640,256]{1,0:T(8,128)(2,1)S(1)}, bf16[640,256]{1,0:T(8,128)(2,1)S(1)}, u32[]{:S(2)}, u32[]{:S(2)}) %collective-permute-start.5) | collective-permute-done | bytes 327712 | tf_op jit(solution)/shard_map/ppermute | solution.py:311
  30.1 1.6 %collective-permute-start.6 = (bf16[640,256]{1,0:T(8,128)(2,1)S(1)}, bf16[640,256]{1,0:T(8,128)(2,1)S(1)}, u32[]{:S(2)}, u32[]{:S(2)}) collective-permute-start(bf16[640,256]{1,0:T(8,128)(2,1)S(1)} %collective-permute-done.refs_0_), channel_id=1, source_target_pairs={{0,4},{4,8},{8,12},{12,0},{1,5},{5,9},{9,13},{13,1},{2,6},{6,10},{... | collective-permute-start | bytes 983048 | tf_op jit(solution)/shard_map/ppermute | solution.py:311
  32.7 9.8 %collective-permute-done.6.refs_4_ = bf16[640,256]{1,0:T(8,128)(2,1)S(1)} collective-permute-done((bf16[640,256]{1,0:T(8,128)(2,1)S(1)}, bf16[640,256]{1,0:T(8,128)(2,1)S(1)}, u32[]{:S(2)}, u32[]{:S(2)}) %collective-permute-start.6) | collective-permute-done | bytes 327712 | tf_op jit(solution)/shard_map/ppermute | solution.py:311
  44.8 1.5 %collective-permute-start.13 = (bf16[640,256]{1,0:T(8,128)(2,1)S(1)}, bf16[640,256]{1,0:T(8,128)(2,1)S(1)}, u32[]{:S(2)}, u32[]{:S(2)}) collective-permute-start(bf16[640,256]{1,0:T(8,128)(2,1)S(1)} %collective-permute-done.3.refs_1_), channel_id=1, source_target_pairs={{0,16},{16,0},{1,17},{17,1},{2,18},{18,2},{3,19},{19,3},{4,20},{20... | collective-permute-start | bytes 983048 | tf_op jit(solution)/shard_map/ppermute | solution.py:306
  46.3 1.3 %collective-permute-start.14 = (bf16[640,256]{1,0:T(8,128)(2,1)S(1)}, bf16[640,256]{1,0:T(8,128)(2,1)S(1)}, u32[]{:S(2)}, u32[]{:S(2)}) collective-permute-start(bf16[640,256]{1,0:T(8,128)(2,1)S(1)} %get-tuple-element.67), channel_id=1, source_target_pairs={{0,2},{2,0},{1,3},{3,1},{4,6},{6,4},{5,7},{7,5},{8,10},{10,8},{9,1... | collective-permute-start | bytes 983048 | tf_op jit(solution)/shard_map/ppermute | solution.py:306
  47.6 3.8 %collective-permute-done.11.refs_5_ = bf16[640,256]{1,0:T(8,128)(2,1)S(1)} collective-permute-done((bf16[640,256]{1,0:T(8,128)(2,1)S(1)}, bf16[640,256]{1,0:T(8,128)(2,1)S(1)}, u32[]{:S(2)}, u32[]{:S(2)}) %collective-permute-start.11) | collective-permute-done | bytes 327712 | tf_op jit(solution)/shard_map/ppermute | solution.py:306
  51.7 7.0 %collective-permute-done.13.refs_3_ = bf16[640,256]{1,0:T(8,128)(2,1)S(1)} collective-permute-done((bf16[640,256]{1,0:T(8,128)(2,1)S(1)}, bf16[640,256]{1,0:T(8,128)(2,1)S(1)}, u32[]{:S(2)}, u32[]{:S(2)}) %collective-permute-start.13) | collective-permute-done | bytes 327712 | tf_op jit(solution)/shard_map/ppermute | solution.py:306
  58.8 2.9 %collective-permute-start.17 = (bf16[2,640,256]{2,1,0:T(8,128)(2,1)S(1)}, bf16[2,640,256]{2,1,0:T(8,128)(2,1)S(1)}, u32[]{:S(2)}, u32[]{:S(2)}) collective-permute-start(bf16[2,640,256]{2,1,0:T(8,128)(2,1)S(1)} %pack.3), channel_id=1, source_target_pairs={{0,4},{1,12},{4,0},{5,8},{8,5},{9,13},{12,1},{13,9},{2,6},{3,14},{... | collective-permute-start | bytes 1966088 | tf_op jit(solution)/shard_map/ppermute | solution.py:339
  63.7 1.0 project.1.refs_8_
  64.7 5.3 %collective-permute-done.10.refs_3_ = bf16[640,256]{1,0:T(8,128)(2,1)S(1)} collective-permute-done((bf16[640,256]{1,0:T(8,128)(2,1)S(1)}, bf16[640,256]{1,0:T(8,128)(2,1)S(1)}, u32[]{:S(2)}, u32[]{:S(2)}) %collective-permute-start.10) | collective-permute-done | bytes 327712 | tf_op jit(solution)/shard_map/ppermute | solution.py:306
  71.0 5.5 %attention.1 = (bf16[256,1280]{1,0:T(8,128)(2,1)}, bf16[256,512]{1,0:T(8,128)(2,1)S(1)}) custom-call(bf16[256,2560]{1,0:T(8,128)(2,1)S(1)} %get-tuple-element.56.own_ref, bf16[256,2560]{1,0:T(8,128)(2,1)S(1)} %collective-permute-done.9.other_ref, bf16[640,256]{1,0:T(8,128)(2,1)S(1)} %collective-permute-done.5.refs_0_, ...), custom_call_target="tpu_custom_call" | custom-call | flops 838860800 | bytes 5000000 | tf_op jit(solution)/shard_map/attention/pallas_call | solution.py:171
  77.9 1.7 %collective-permute-start.19 = (bf16[256,512]{1,0:T(8,128)(2,1)S(1)}, bf16[256,512]{1,0:T(8,128)(2,1)S(1)}, u32[]{:S(2)}, u32[]{:S(2)}) collective-permute-start(bf16[256,512]{1,0:T(8,128)(2,1)S(1)} %get-tuple-element.82.refs_12_), channel_id=1, source_target_pairs={{0,2},{2,0},{1,3},{3,1},{4,6},{6,4},{5,7},{7,5},{8,10},{10,8},{9,1... | collective-permute-start | bytes 786440 | tf_op jit(solution)/shard_map/ppermute | solution.py:306
  79.6 8.6 %collective-permute-done.18.refs_14_ = bf16[256,512]{1,0:T(8,128)(2,1)S(1)} collective-permute-done((bf16[256,512]{1,0:T(8,128)(2,1)S(1)}, bf16[256,512]{1,0:T(8,128)(2,1)S(1)}, u32[]{:S(2)}, u32[]{:S(2)}) %collective-permute-start.18) | collective-permute-done | bytes 262176 | tf_op jit(solution)/shard_map/ppermute | solution.py:311
  88.2 2.0 %collective-permute-start.21 = (bf16[256,512]{1,0:T(8,128)(2,1)S(1)}, bf16[256,512]{1,0:T(8,128)(2,1)S(1)}, u32[]{:S(2)}, u32[]{:S(2)}) collective-permute-start(bf16[256,512]{1,0:T(8,128)(2,1)S(1)} %get-tuple-element.82.refs_12_), channel_id=1, source_target_pairs={{0,12},{4,0},{8,4},{12,8},{1,13},{5,1},{9,5},{13,9},{2,14},{6,2},{... | collective-permute-start | bytes 786440 | tf_op jit(solution)/shard_map/ppermute | solution.py:311
  91.5 5.1 %collective-permute-done.21.refs_15_ = bf16[256,512]{1,0:T(8,128)(2,1)S(1)} collective-permute-done((bf16[256,512]{1,0:T(8,128)(2,1)S(1)}, bf16[256,512]{1,0:T(8,128)(2,1)S(1)}, u32[]{:S(2)}, u32[]{:S(2)}) %collective-permute-start.21) | collective-permute-done | bytes 262176 | tf_op jit(solution)/shard_map/ppermute | solution.py:311
  96.6 1.6 %collective-permute-done.22.refs_16_ = bf16[256,512]{1,0:T(8,128)(2,1)S(1)} collective-permute-done((bf16[256,512]{1,0:T(8,128)(2,1)S(1)}, bf16[256,512]{1,0:T(8,128)(2,1)S(1)}, u32[]{:S(2)}, u32[]{:S(2)}) %collective-permute-start.22) | collective-permute-done | bytes 262176 | tf_op jit(solution)/shard_map/ppermute | solution.py:306
  99.0 7.9 %collective-permute-done.23.refs_4_ = bf16[256,512]{1,0:T(8,128)(2,1)S(1)} collective-permute-done((bf16[256,512]{1,0:T(8,128)(2,1)S(1)}, bf16[256,512]{1,0:T(8,128)(2,1)S(1)}, u32[]{:S(2)}, u32[]{:S(2)}) %collective-permute-start.23) | collective-permute-done | bytes 262176 | tf_op jit(solution)/shard_map/ppermute | solution.py:311
  107.0 1.7 %gradient.2 = (f32[2,640,256]{2,1,0:T(8,128)S(1)}, f32[2,256]{1,0:T(2,128)S(1)}) custom-call(bf16[2,640,256]{2,1,0:T(8,128)(2,1)S(1)} %collective-permute-done.15.refs_0_.refs_1_, bf16[2,640,256]{2,1,0:T(8,128)(2,1)S(1)} %collective-permute-done.15.refs_0_.refs_1_, bf16[2,640,256]{2,1,0:T(8,128)(2,1)S(1)} %collective-permute-done.17.refs_2_.refs_3_.refs_4_.refs_5_, ...), custom_call_target="tpu_custom_call" | custom-call | flops 1006632960 | bytes 5000000 | tf_op jit(solution)/shard_map/gradient/pallas_call | solution.py:236
  108.8 4.5 %collective-permute-done.25.refs_5_ = bf16[256,512]{1,0:T(8,128)(2,1)S(1)} collective-permute-done((bf16[256,512]{1,0:T(8,128)(2,1)S(1)}, bf16[256,512]{1,0:T(8,128)(2,1)S(1)}, u32[]{:S(2)}, u32[]{:S(2)}) %collective-permute-start.25) | collective-permute-done | bytes 262176 | tf_op jit(solution)/shard_map/ppermute | solution.py:306
  113.3 1.7 %gradient.3 = (f32[2,640,256]{2,1,0:T(8,128)}, f32[2,256]{1,0:T(2,128)}) custom-call(bf16[2,640,256]{2,1,0:T(8,128)(2,1)S(1)} %collective-permute-done.15.refs_0_.refs_1_, bf16[2,640,256]{2,1,0:T(8,128)(2,1)S(1)} %collective-permute-done.15.refs_0_.refs_1_, bf16[2,640,256]{2,1,0:T(8,128)(2,1)S(1)} %collective-permute-done.20.refs_6_.refs_7_.refs_2_.refs_3_, ...), custom_call_target="tpu_custom_call" | custom-call | flops 335544320 | bytes 5000000 | tf_op jit(solution)/shard_map/gradient/pallas_call | solution.py:236
  (52 shorter events, 11.3 us)
Async XLA Ops:
  0.6 7.2 %copy-start = (bf16[256,2560]{1,0:T(8,128)(2,1)S(1)}, bf16[256,2560]{1,0:T(8,128)(2,1)}, u32[]{:S(2)}) copy-start(bf16[256,2560]{1,0:T(8,128)(2,1)} %values_ref.1) | copy-start | bytes 3932164
  1.8 12.8 %collective-permute-start = (bf16[640,256]{1,0:T(8,128)(2,1)S(1)}, bf16[640,256]{1,0:T(8,128)(2,1)S(1)}, u32[]{:S(2)}, u32[]{:S(2)}) collective-permute-start(bf16[640,256]{1,0:T(8,128)(2,1)S(1)} %dynamic-slice_bitcast_fusion), channel_id=1, source_target_pairs={{0,4},{4,8},{8,12},{12,0},{1,5},{5,9},{9,13},{13,1},{2,6},{6,10},{... | collective-permute-start | bytes 983048 | tf_op jit(solution)/shard_map/ppermute | solution.py:311
  6.5 1.2 %collective-permute-start.1 = (f32[256,1]{0,1:T(1,128)S(1)}, f32[256,1]{0,1:T(1,128)S(1)}, u32[]{:S(2)}, u32[]{:S(2)}) collective-permute-start(f32[256,1]{0,1:T(1,128)S(1)} %bitcast.3), channel_id=1, source_target_pairs={{0,1},{1,0},{2,3},{3,2},{4,5},{5,4},{6,7},{7,6},{8,9},{9,8},{10,11... | collective-permute-start | bytes 3080 | tf_op jit(solution)/shard_map/ppermute | solution.py:306
  8.8 9.9 %collective-permute-start.2 = (bf16[640,256]{1,0:T(8,128)(2,1)S(1)}, bf16[640,256]{1,0:T(8,128)(2,1)S(1)}, u32[]{:S(2)}, u32[]{:S(2)}) collective-permute-start(bf16[640,256]{1,0:T(8,128)(2,1)S(1)} %get-tuple-element.51), channel_id=1, source_target_pairs={{0,2},{2,0},{1,3},{3,1},{4,6},{6,4},{5,7},{7,5},{8,10},{10,8},{9,1... | collective-permute-start | bytes 983048 | tf_op jit(solution)/shard_map/ppermute | solution.py:306
  18.7 9.0 %collective-permute-start.3 = (bf16[640,256]{1,0:T(8,128)(2,1)S(1)}, bf16[640,256]{1,0:T(8,128)(2,1)S(1)}, u32[]{:S(2)}, u32[]{:S(2)}) collective-permute-start(bf16[640,256]{1,0:T(8,128)(2,1)S(1)} %collective-permute-done.refs_0_), channel_id=1, source_target_pairs={{0,2},{2,0},{1,3},{3,1},{4,6},{6,4},{5,7},{7,5},{8,10},{10,8},{9,1... | collective-permute-start | bytes 983048 | tf_op jit(solution)/shard_map/ppermute | solution.py:306
  20.2 8.7 %collective-permute-start.4 = (bf16[640,256]{1,0:T(8,128)(2,1)S(1)}, bf16[640,256]{1,0:T(8,128)(2,1)S(1)}, u32[]{:S(2)}, u32[]{:S(2)}) collective-permute-start(bf16[640,256]{1,0:T(8,128)(2,1)S(1)} %collective-permute-done.refs_0_), channel_id=1, source_target_pairs={{0,16},{16,0},{1,17},{17,1},{2,18},{18,2},{3,19},{19,3},{4,20},{20... | collective-permute-start | bytes 983048 | tf_op jit(solution)/shard_map/ppermute | solution.py:306
  21.7 8.4 %collective-permute-start.5 = (bf16[640,256]{1,0:T(8,128)(2,1)S(1)}, bf16[640,256]{1,0:T(8,128)(2,1)S(1)}, u32[]{:S(2)}, u32[]{:S(2)}) collective-permute-start(bf16[640,256]{1,0:T(8,128)(2,1)S(1)} %dynamic-slice_bitcast_fusion), channel_id=1, source_target_pairs={{0,12},{4,0},{8,4},{12,8},{1,13},{5,1},{9,5},{13,9},{2,14},{6,2},{... | collective-permute-start | bytes 983048 | tf_op jit(solution)/shard_map/ppermute | solution.py:311
  30.1 12.4 %collective-permute-start.9 = (bf16[256,2560]{1,0:T(8,128)(2,1)S(1)}, bf16[256,2560]{1,0:T(8,128)(2,1)S(1)}, u32[]{:S(2)}, u32[]{:S(2)}) collective-permute-start(bf16[256,2560]{1,0:T(8,128)(2,1)S(1)} %get-tuple-element.56.own_ref), channel_id=1, source_target_pairs={{0,1},{1,0},{2,3},{3,2},{4,5},{5,4},{6,7},{7,6},{8,9},{9,8},{10,11... | collective-permute-start | bytes 3932168 | tf_op jit(solution)/shard_map/ppermute | solution.py:306
  30.1 12.4 %collective-permute-start.6 = (bf16[640,256]{1,0:T(8,128)(2,1)S(1)}, bf16[640,256]{1,0:T(8,128)(2,1)S(1)}, u32[]{:S(2)}, u32[]{:S(2)}) collective-permute-start(bf16[640,256]{1,0:T(8,128)(2,1)S(1)} %collective-permute-done.refs_0_), channel_id=1, source_target_pairs={{0,4},{4,8},{8,12},{12,0},{1,5},{5,9},{9,13},{13,1},{2,6},{6,10},{... | collective-permute-start | bytes 983048 | tf_op jit(solution)/shard_map/ppermute | solution.py:311
  31.7 10.9 %collective-permute-start.7 = (bf16[640,256]{1,0:T(8,128)(2,1)S(1)}, bf16[640,256]{1,0:T(8,128)(2,1)S(1)}, u32[]{:S(2)}, u32[]{:S(2)}) collective-permute-start(bf16[640,256]{1,0:T(8,128)(2,1)S(1)} %collective-permute-done.5.refs_0_), channel_id=1, source_target_pairs={{0,2},{2,0},{1,3},{3,1},{4,6},{6,4},{5,7},{7,5},{8,10},{10,8},{9,1... | collective-permute-start | bytes 983048 | tf_op jit(solution)/shard_map/ppermute | solution.py:306
  32.2 10.3 %collective-permute-start.8 = (bf16[640,256]{1,0:T(8,128)(2,1)S(1)}, bf16[640,256]{1,0:T(8,128)(2,1)S(1)}, u32[]{:S(2)}, u32[]{:S(2)}) collective-permute-start(bf16[640,256]{1,0:T(8,128)(2,1)S(1)} %collective-permute-done.5.refs_0_), channel_id=1, source_target_pairs={{0,16},{16,0},{1,17},{17,1},{2,18},{18,2},{3,19},{19,3},{4,20},{20... | collective-permute-start | bytes 983048 | tf_op jit(solution)/shard_map/ppermute | solution.py:306
  42.6 19.1 %copy-start.5 = (bf16[2,256]{1,0:T(2,128)(2,1)S(1)}, bf16[2,256]{1,0:T(2,128)(2,1)}, u32[]{:S(2)}) copy-start(bf16[2,256]{1,0:T(2,128)(2,1)} %param.11) | copy-start | bytes 3076
  42.6 21.0 %copy-start.1 = (bf16[2,1280,256]{2,1,0:T(8,128)(2,1)S(1)}, bf16[2,1280,256]{2,1,0:T(8,128)(2,1)}, u32[]{:S(2)}) copy-start(bf16[2,1280,256]{2,1,0:T(8,128)(2,1)} %weight_ref.1) | copy-start | bytes 3932164
  42.6 16.1 %collective-permute-start.15 = (bf16[2,640,256]{2,1,0:T(8,128)(2,1)S(1)}, bf16[2,640,256]{2,1,0:T(8,128)(2,1)S(1)}, u32[]{:S(2)}, u32[]{:S(2)}) collective-permute-start(bf16[2,640,256]{2,1,0:T(8,128)(2,1)S(1)} %pack.2), channel_id=1, source_target_pairs={{0,0},{1,8},{4,4},{5,12},{8,1},{9,9},{12,5},{13,13},{2,2},{3,10},{... | collective-permute-start | bytes 1966088 | tf_op jit(solution)/shard_map/ppermute | solution.py:339
  43.5 8.0 %collective-permute-start.11 = (bf16[640,256]{1,0:T(8,128)(2,1)S(1)}, bf16[640,256]{1,0:T(8,128)(2,1)S(1)}, u32[]{:S(2)}, u32[]{:S(2)}) collective-permute-start(bf16[640,256]{1,0:T(8,128)(2,1)S(1)} %collective-permute-done.6.refs_4_), channel_id=1, source_target_pairs={{0,2},{2,0},{1,3},{3,1},{4,6},{6,4},{5,7},{7,5},{8,10},{10,8},{9,1... | collective-permute-start | bytes 983048 | tf_op jit(solution)/shard_map/ppermute | solution.py:306
  44.3 7.4 %collective-permute-start.12 = (bf16[640,256]{1,0:T(8,128)(2,1)S(1)}, bf16[640,256]{1,0:T(8,128)(2,1)S(1)}, u32[]{:S(2)}, u32[]{:S(2)}) collective-permute-start(bf16[640,256]{1,0:T(8,128)(2,1)S(1)} %collective-permute-done.6.refs_4_), channel_id=1, source_target_pairs={{0,16},{16,0},{1,17},{17,1},{2,18},{18,2},{3,19},{19,3},{4,20},{20... | collective-permute-start | bytes 983048 | tf_op jit(solution)/shard_map/ppermute | solution.py:306
  44.8 13.9 %collective-permute-start.13 = (bf16[640,256]{1,0:T(8,128)(2,1)S(1)}, bf16[640,256]{1,0:T(8,128)(2,1)S(1)}, u32[]{:S(2)}, u32[]{:S(2)}) collective-permute-start(bf16[640,256]{1,0:T(8,128)(2,1)S(1)} %collective-permute-done.3.refs_1_), channel_id=1, source_target_pairs={{0,16},{16,0},{1,17},{17,1},{2,18},{18,2},{3,19},{19,3},{4,20},{20... | collective-permute-start | bytes 983048 | tf_op jit(solution)/shard_map/ppermute | solution.py:306
  46.3 12.4 %collective-permute-start.14 = (bf16[640,256]{1,0:T(8,128)(2,1)S(1)}, bf16[640,256]{1,0:T(8,128)(2,1)S(1)}, u32[]{:S(2)}, u32[]{:S(2)}) collective-permute-start(bf16[640,256]{1,0:T(8,128)(2,1)S(1)} %get-tuple-element.67), channel_id=1, source_target_pairs={{0,2},{2,0},{1,3},{3,1},{4,6},{6,4},{5,7},{7,5},{8,10},{10,8},{9,1... | collective-permute-start | bytes 983048 | tf_op jit(solution)/shard_map/ppermute | solution.py:306
  58.8 18.5 %collective-permute-start.17 = (bf16[2,640,256]{2,1,0:T(8,128)(2,1)S(1)}, bf16[2,640,256]{2,1,0:T(8,128)(2,1)S(1)}, u32[]{:S(2)}, u32[]{:S(2)}) collective-permute-start(bf16[2,640,256]{2,1,0:T(8,128)(2,1)S(1)} %pack.3), channel_id=1, source_target_pairs={{0,4},{1,12},{4,0},{5,8},{8,5},{9,13},{12,1},{13,9},{2,6},{3,14},{... | collective-permute-start | bytes 1966088 | tf_op jit(solution)/shard_map/ppermute | solution.py:339
  61.7 8.3 %collective-permute-start.10 = (bf16[640,256]{1,0:T(8,128)(2,1)S(1)}, bf16[640,256]{1,0:T(8,128)(2,1)S(1)}, u32[]{:S(2)}, u32[]{:S(2)}) collective-permute-start(bf16[640,256]{1,0:T(8,128)(2,1)S(1)} %collective-permute-done.7.refs_1_), channel_id=1, source_target_pairs={{0,16},{16,0},{1,17},{17,1},{2,18},{18,2},{3,19},{19,3},{4,20},{20... | collective-permute-start | bytes 983048 | tf_op jit(solution)/shard_map/ppermute | solution.py:306
  62.3 8.7 %collective-permute-start.16 = (bf16[640,256]{1,0:T(8,128)(2,1)S(1)}, bf16[640,256]{1,0:T(8,128)(2,1)S(1)}, u32[]{:S(2)}, u32[]{:S(2)}) collective-permute-start(bf16[640,256]{1,0:T(8,128)(2,1)S(1)} %collective-permute-done.12.refs_6_), channel_id=1, source_target_pairs={{0,2},{2,0},{1,3},{3,1},{4,6},{6,4},{5,7},{7,5},{8,10},{10,8},{9,1... | collective-permute-start | bytes 983048 | tf_op jit(solution)/shard_map/ppermute | solution.py:306
  63.7 7.3 %copy-start.2 = (bf16[256,1280]{1,0:T(8,128)(2,1)S(1)}, bf16[256,1280]{1,0:T(8,128)(2,1)}, u32[]{:S(2)}) copy-start(bf16[256,1280]{1,0:T(8,128)(2,1)} %refs_12_.1) | copy-start | bytes 1966084
  63.7 7.3 %copy-start.3 = (bf16[256,1280]{1,0:T(8,128)(2,1)S(1)}, bf16[256,1280]{1,0:T(8,128)(2,1)}, u32[]{:S(2)}) copy-start(bf16[256,1280]{1,0:T(8,128)(2,1)} %refs_13_.1) | copy-start | bytes 1966084
  77.3 10.9 %collective-permute-start.18 = (bf16[256,512]{1,0:T(8,128)(2,1)S(1)}, bf16[256,512]{1,0:T(8,128)(2,1)S(1)}, u32[]{:S(2)}, u32[]{:S(2)}) collective-permute-start(bf16[256,512]{1,0:T(8,128)(2,1)S(1)} %get-tuple-element.82.refs_12_), channel_id=1, source_target_pairs={{0,4},{4,8},{8,12},{12,0},{1,5},{5,9},{9,13},{13,1},{2,6},{6,10},{... | collective-permute-start | bytes 786440 | tf_op jit(solution)/shard_map/ppermute | solution.py:311
  77.9 10.3 %collective-permute-start.19 = (bf16[256,512]{1,0:T(8,128)(2,1)S(1)}, bf16[256,512]{1,0:T(8,128)(2,1)S(1)}, u32[]{:S(2)}, u32[]{:S(2)}) collective-permute-start(bf16[256,512]{1,0:T(8,128)(2,1)S(1)} %get-tuple-element.82.refs_12_), channel_id=1, source_target_pairs={{0,2},{2,0},{1,3},{3,1},{4,6},{6,4},{5,7},{7,5},{8,10},{10,8},{9,1... | collective-permute-start | bytes 786440 | tf_op jit(solution)/shard_map/ppermute | solution.py:306
  88.2 8.3 %collective-permute-start.21 = (bf16[256,512]{1,0:T(8,128)(2,1)S(1)}, bf16[256,512]{1,0:T(8,128)(2,1)S(1)}, u32[]{:S(2)}, u32[]{:S(2)}) collective-permute-start(bf16[256,512]{1,0:T(8,128)(2,1)S(1)} %get-tuple-element.82.refs_12_), channel_id=1, source_target_pairs={{0,12},{4,0},{8,4},{12,8},{1,13},{5,1},{9,5},{13,9},{2,14},{6,2},{... | collective-permute-start | bytes 786440 | tf_op jit(solution)/shard_map/ppermute | solution.py:311
  90.2 7.9 %collective-permute-start.22 = (bf16[256,512]{1,0:T(8,128)(2,1)S(1)}, bf16[256,512]{1,0:T(8,128)(2,1)S(1)}, u32[]{:S(2)}, u32[]{:S(2)}) collective-permute-start(bf16[256,512]{1,0:T(8,128)(2,1)S(1)} %collective-permute-done.18.refs_14_), channel_id=1, source_target_pairs={{0,2},{2,0},{1,3},{3,1},{4,6},{6,4},{5,7},{7,5},{8,10},{10,8},{9,1... | collective-permute-start | bytes 786440 | tf_op jit(solution)/shard_map/ppermute | solution.py:306
  91.0 16.0 %collective-permute-start.20 = (bf16[2,640,256]{2,1,0:T(8,128)(2,1)S(1)}, bf16[2,640,256]{2,1,0:T(8,128)(2,1)S(1)}, u32[]{:S(2)}, u32[]{:S(2)}) collective-permute-start(bf16[2,640,256]{2,1,0:T(8,128)(2,1)S(1)} %collective-permute-done.15.refs_0_.refs_1_), channel_id=1, source_target_pairs={{0,1},{1,0},{2,3},{3,2},{4,5},{5,4},{6,7},{7,6},{8,9},{9,8},{10,11... | collective-permute-start | bytes 1966088 | tf_op jit(solution)/shard_map/ppermute | solution.py:306
  91.0 16.0 %collective-permute-start.26 = (bf16[2,640,256]{2,1,0:T(8,128)(2,1)S(1)}, bf16[2,640,256]{2,1,0:T(8,128)(2,1)S(1)}, u32[]{:S(2)}, u32[]{:S(2)}) collective-permute-start(bf16[2,640,256]{2,1,0:T(8,128)(2,1)S(1)} %collective-permute-done.17.refs_2_.refs_3_.refs_4_.refs_5_), channel_id=1, source_target_pairs={{0,1},{1,0},{2,3},{3,2},{4,5},{5,4},{6,7},{7,6},{8,9},{9,8},{10,11... | collective-permute-start | bytes 1966088 | tf_op jit(solution)/shard_map/ppermute | solution.py:306
  98.1 8.8 %collective-permute-start.23 = (bf16[256,512]{1,0:T(8,128)(2,1)S(1)}, bf16[256,512]{1,0:T(8,128)(2,1)S(1)}, u32[]{:S(2)}, u32[]{:S(2)}) collective-permute-start(bf16[256,512]{1,0:T(8,128)(2,1)S(1)} %collective-permute-done.18.refs_14_), channel_id=1, source_target_pairs={{0,4},{4,8},{8,12},{12,0},{1,5},{5,9},{9,13},{13,1},{2,6},{6,10},{... | collective-permute-start | bytes 786440 | tf_op jit(solution)/shard_map/ppermute | solution.py:311
  98.3 8.6 %collective-permute-start.24 = (bf16[256,512]{1,0:T(8,128)(2,1)S(1)}, bf16[256,512]{1,0:T(8,128)(2,1)S(1)}, u32[]{:S(2)}, u32[]{:S(2)}) collective-permute-start(bf16[256,512]{1,0:T(8,128)(2,1)S(1)} %collective-permute-done.21.refs_15_), channel_id=1, source_target_pairs={{0,2},{2,0},{1,3},{3,1},{4,6},{6,4},{5,7},{7,5},{8,10},{10,8},{9,1... | collective-permute-start | bytes 786440 | tf_op jit(solution)/shard_map/ppermute | solution.py:306
  106.9 6.4 %collective-permute-start.25 = (bf16[256,512]{1,0:T(8,128)(2,1)S(1)}, bf16[256,512]{1,0:T(8,128)(2,1)S(1)}, u32[]{:S(2)}, u32[]{:S(2)}) collective-permute-start(bf16[256,512]{1,0:T(8,128)(2,1)S(1)} %collective-permute-done.23.refs_4_), channel_id=1, source_target_pairs={{0,2},{2,0},{1,3},{3,1},{4,6},{6,4},{5,7},{7,5},{8,10},{10,8},{9,1... | collective-permute-start | bytes 786440 | tf_op jit(solution)/shard_map/ppermute | solution.py:306
  (1 other events, 5.9 us)

commit v20 on v11

--- a/solution.py
+++ b/solution.py
@@ -244,30 +244,38 @@
     )(*own, *other, *pairs, *(sums or ()))
 
 
-def norm_kernel(values_ref, scale_ref, gain_ref, normed_ref, kept_ref, sent_ref):
+def norm_kernel(values_ref, scale_ref, gain_ref, normed_ref, kept_ref, early_ref, late_ref):
     replica, replicas = lax.axis_index("dp"), lax.axis_size("dp")
-    share = kept_ref.shape[1]
+    share, early = kept_ref.shape[1], early_ref.shape[0]
 
     def scaled(place):
         wide_values = values_ref[:, place].astype(jnp.float32)
         return wide_values * scale_ref[...] * gain_ref[:, place]
 
-    for slab in range(2 * replicas):
-        place = pl.ds(slab * share, share)
+    def slab(at, owner):
+        place = pl.ds(pl.multiple_of((at * replicas + owner) * share, 128), share)
+        return scaled(place).T.astype(jnp.bfloat16)
+
+    for at in range(2 * replicas):
+        place = pl.ds(at * share, share)
         normed_ref[:, place] = scaled(place).astype(jnp.bfloat16)
     for at in range(2):
-        for ref, owner in ((kept_ref, replica), (sent_ref, 1 - replica)):
-            place = pl.ds(pl.multiple_of((at * replicas + owner) * share, 128), share)
-            ref[at] = scaled(place).T.astype(jnp.bfloat16)
+        kept_ref[at] = slab(at, replica)
+    sent = slab(0, 1 - replica)
+    early_ref[...] = sent[:early]
+    late_ref[: share - early] = sent[early:]
+    late_ref[share - early :] = slab(1, 1 - replica)
 
 
 def norm(activations, scale, gain, share):
     length, features = activations.shape
-    shapes = [activations.shape, (2, share, length), (2, share, length)]
+    early = share // 2
+    shapes = [activations.shape, (2, share, length)]
+    shapes += [(early, length), (2 * share - early, length)]
     return pl.pallas_call(
         norm_kernel,
         in_specs=[IN_VMEM] * 3,
-        out_specs=[IN_VMEM] * 3,
+        out_specs=[IN_VMEM] * 4,
         out_shape=[jax.ShapeDtypeStruct(shape, jnp.bfloat16) for shape in shapes],
         compiler_params=pltpu.CompilerParams(vmem_limit_bytes=VMEM_BYTES),
         cost_estimate=pl.CostEstimate(
@@ -277,24 +285,29 @@
     )(activations, scale, gain)
 
 
-def pack_kernel(kept_ref, arrived_ref, even_ref, odd_ref):
+def pack_kernel(kept_ref, early_ref, late_ref, even_ref, odd_ref, arrived_ref):
     parity = lax.rem(lax.axis_index("blk"), 2)
+    early, rest = early_ref.shape[0], kept_ref.shape[1] - early_ref.shape[0]
+    arrived_ref[0, :early] = early_ref[...]
+    arrived_ref[0, early:] = late_ref[:rest]
+    arrived_ref[1] = late_ref[rest:]
     for turn, ref in enumerate((even_ref, odd_ref)):
         at = lax.rem(turn + parity, 2)
         ref[0] = kept_ref[at]
         ref[1] = arrived_ref[at]
 
 
-def pack(kept, arrived):
+def pack(kept, early, late):
     return pl.pallas_call(
         pack_kernel,
-        in_specs=[IN_VMEM] * 2,
+        in_specs=[IN_VMEM] * 3,
         out_specs=[IN_VMEM] * 2,
         out_shape=[jax.ShapeDtypeStruct(kept.shape, kept.dtype)] * 2,
+        scratch_shapes=[pltpu.VMEM(kept.shape, kept.dtype)],
         compiler_params=pltpu.CompilerParams(vmem_limit_bytes=VMEM_BYTES),
         cost_estimate=pl.CostEstimate(flops=0, bytes_accessed=2600000, transcendentals=0),
         name="pack",
-    )(kept, arrived)
+    )(kept, early, late)
 
 
 def swapped(block, axis):
@@ -366,20 +379,21 @@
         )
 
     up = turned(piece, "blk", 1)
-    normed, kept, sent = norm(activations, scale, gain[None, :], share)
-    arrived = swapped(sent, "dp")
-    up, piece, normed = lax.optimization_barrier((up, piece, normed))
+    normed, kept, sent_early, sent_late = norm(activations, scale, gain[None, :], share)
+    early = swapped(sent_early, "dp")
+    up, piece, normed, early, sent_late = lax.optimization_barrier(
+        (up, piece, normed, early, sent_late)
+    )
+    late = swapped(sent_late, "dp")
     up_y, down = swapped(up, "groups"), turned(piece, "blk", -1)
     normed_other = swapped(normed, "sub")
     up, up_y, down, normed_other = lax.optimization_barrier((up, up_y, down, normed_other))
     up_x, down_y = swapped(up, "dp"), swapped(down, "groups")
     twice = turned(up, "blk", 1)
-    twice, down, down_y, up_x, arrived = lax.optimization_barrier(
-        (twice, down, down_y, up_x, arrived)
-    )
+    twice, down, down_y, up_x, late = lax.optimization_barrier((twice, down, down_y, up_x, late))
     down_x, twice_x = swapped(down, "dp"), swapped(twice, "dp")
     twice_y, up_both = swapped(twice, "groups"), swapped(up_x, "groups")
-    even, odd = pack(kept, arrived)
+    even, odd = pack(kept, early, late)
     even = sent_along(even, 0)
     twice_x, twice_y, up_both, down_x, even = lax.optimization_barrier(
         (twice_x, twice_y, up_both, down_x, even)

time: 112 us -> 110 us (0.982)
    ppermute x18 -> x19, waiting for transfers between devices: 44.7 us -> 40.5 us  [swapped(): return lax.ppermute(block, axis, [(0, 1), (1, 0)])]
    ppermute x18 -> x19, starting transfers between devices: 17.7 us -> 15.2 us  [swapped(): return lax.ppermute(block, axis, [(0, 1), (1, 0)])]
    ppermute x6, starting transfers between devices: 7.19 us -> 9.24 us  [turned(): lax.ppermute(block, axis, [(i, (i + distance) % size) for i in range(size)])]
    ppermute x2, waiting for transfers between devices: 0.7 us -> 2.54 us  [sent_along(): return lax.ppermute(slabs, ('blk', 'sub'), route)]
    ppermute x6, waiting for transfers between devices: 24.7 us -> 26 us  [turned(): lax.ppermute(block, axis, [(i, (i + distance) % size) for i in range(size)])]
  transfers between devices with their start and end apart: 26 -> 27, of which waited for: 17 -> 17; matrix products, arithmetic and copies ran while one was open for 2% -> 2% of each run, Pallas kernels for 8% -> 8%
where the time goes in v20:
time: 110 us
  waiting for transfers between devices  69 us (63%)
  starting transfers between devices  25.1 us (23%)
  Pallas kernels  11 us (10%)
  other arithmetic  2.4 us (2%)
  local copies, waits for them, and re-layouts  1.3 us (1%)
    ppermute x19, waiting for transfers between devices, swapped(): return lax.ppermute(block, axis, [(0, 1), (1, 0)])  40.5 us
    ppermute x6, waiting for transfers between devices, turned(): lax.ppermute(block, axis, [(i, (i + distance) % size) for i in range(size)])  26 us
    ppermute x19, starting transfers between devices, swapped(): return lax.ppermute(block, axis, [(0, 1), (1, 0)])  15.2 us
    ppermute x6, starting transfers between devices, turned(): lax.ppermute(block, axis, [(i, (i + distance) % size) for i in range(size)])  9.24 us
    pallas_call x1, Pallas kernels, attention(): pl.pallas_call(functools.partial(attention_kernel, distance), in_specs=[I...  5.08 us
    pallas_call x2, Pallas kernels, gradient(): pl.pallas_call(functools.partial(gradient_kernel, tuple(some), sums is No...  3.47 us
    ppermute x2, waiting for transfers between devices, sent_along(): return lax.ppermute(slabs, ('blk', 'sub'), route)  2.54 us
  transfers between devices with their start and end apart: 27, of which 17 were waited for; matrix products, arithmetic and copies ran while one was open for 2% of the time, Pallas kernels for 8%

profile of v20, /device:TPU:0, one launch (start us, length us, event | category | flops | bytes accessed | tf_op | source)
XLA Modules:
  0.0 109.7 jit_solution(4773851352771695238)
XLA Ops:
  0.7 1.1 %dynamic-slice_bitcast_fusion = bf16[640,256]{1,0:T(8,128)(2,1)S(1)} fusion(bf16[2,1280,256]{2,1,0:T(8,128)(2,1)} %weight_ref.1, s32[]{:T(128)S(6)} %select_n.9, s32[]{:T(128)S(6)} %select_n.10), kind=kLoop, calls=%fused_computation.1 | loop fusion | bytes 655368 | tf_op jit(solution)/shard_map/squeeze | solution.py:371
  1.8 3.1 %collective-permute-start = (bf16[640,256]{1,0:T(8,128)(2,1)S(1)}, bf16[640,256]{1,0:T(8,128)(2,1)S(1)}, u32[]{:S(2)}, u32[]{:S(2)}) collective-permute-start(bf16[640,256]{1,0:T(8,128)(2,1)S(1)} %dynamic-slice_bitcast_fusion), channel_id=1, source_target_pairs={{0,4},{4,8},{8,12},{12,0},{1,5},{5,9},{9,13},{13,1},{2,6},{6,10},{... | collective-permute-start | bytes 983048 | tf_op jit(solution)/shard_map/ppermute | solution.py:319
  4.8 1.7 %multiply_reduce_fusion = f32[256]{0:T(256)S(1)} fusion(bf16[256,2560]{1,0:T(8,128)(2,1)} %values_ref.1), kind=kLoop, calls=%fused_computation | loop fusion | flops 1965824 | bytes 1311744 | tf_op jit(solution)/shard_map/reduce_sum | solution.py:354
  8.8 1.6 %collective-permute-start.2 = (bf16[320,256]{1,0:T(8,128)(2,1)S(1)}, bf16[320,256]{1,0:T(8,128)(2,1)S(1)}, u32[]{:S(2)}, u32[]{:S(2)}) collective-permute-start(bf16[320,256]{1,0:T(8,128)(2,1)S(1)} %get-tuple-element.48), channel_id=1, source_target_pairs={{0,2},{2,0},{1,3},{3,1},{4,6},{6,4},{5,7},{7,5},{8,10},{10,8},{9,1... | collective-permute-start | bytes 491528 | tf_op jit(solution)/shard_map/ppermute | solution.py:314
  10.4 4.8 %collective-permute-done.2.early_ref = bf16[320,256]{1,0:T(8,128)(2,1)S(1)} collective-permute-done((bf16[320,256]{1,0:T(8,128)(2,1)S(1)}, bf16[320,256]{1,0:T(8,128)(2,1)S(1)}, u32[]{:S(2)}, u32[]{:S(2)}) %collective-permute-start.2) | collective-permute-done | bytes 163872 | tf_op jit(solution)/shard_map/ppermute | solution.py:314
  15.2 1.5 %collective-permute-start.3 = (bf16[640,256]{1,0:T(8,128)(2,1)S(1)}, bf16[640,256]{1,0:T(8,128)(2,1)S(1)}, u32[]{:S(2)}, u32[]{:S(2)}) collective-permute-start(bf16[640,256]{1,0:T(8,128)(2,1)S(1)} %collective-permute-done.refs_0_), channel_id=1, source_target_pairs={{0,16},{16,0},{1,17},{17,1},{2,18},{18,2},{3,19},{19,3},{4,20},{20... | collective-permute-start | bytes 983048 | tf_op jit(solution)/shard_map/ppermute | solution.py:314
  16.7 2.2 %collective-permute-start.4 = (bf16[640,256]{1,0:T(8,128)(2,1)S(1)}, bf16[640,256]{1,0:T(8,128)(2,1)S(1)}, u32[]{:S(2)}, u32[]{:S(2)}) collective-permute-start(bf16[640,256]{1,0:T(8,128)(2,1)S(1)} %dynamic-slice_bitcast_fusion), channel_id=1, source_target_pairs={{0,12},{4,0},{8,4},{12,8},{1,13},{5,1},{9,5},{13,9},{2,14},{6,2},{... | collective-permute-start | bytes 983048 | tf_op jit(solution)/shard_map/ppermute | solution.py:319
  19.0 1.5 %collective-permute-start.9 = (bf16[960,256]{1,0:T(8,128)(2,1)S(1)}, bf16[960,256]{1,0:T(8,128)(2,1)S(1)}, u32[]{:S(2)}, u32[]{:S(2)}) collective-permute-start(bf16[960,256]{1,0:T(8,128)(2,1)S(1)} %get-tuple-element.56), channel_id=1, source_target_pairs={{0,2},{2,0},{1,3},{3,1},{4,6},{6,4},{5,7},{7,5},{8,10},{10,8},{9,1... | collective-permute-start | bytes 1474568 | tf_op jit(solution)/shard_map/ppermute | solution.py:314
  20.5 4.9 %collective-permute-done.3.refs_2_ = bf16[640,256]{1,0:T(8,128)(2,1)S(1)} collective-permute-done((bf16[640,256]{1,0:T(8,128)(2,1)S(1)}, bf16[640,256]{1,0:T(8,128)(2,1)S(1)}, u32[]{:S(2)}, u32[]{:S(2)}) %collective-permute-start.3) | collective-permute-done | bytes 327712 | tf_op jit(solution)/shard_map/ppermute | solution.py:314
  25.3 1.2 %collective-permute-done.4.refs_4_ = bf16[640,256]{1,0:T(8,128)(2,1)S(1)} collective-permute-done((bf16[640,256]{1,0:T(8,128)(2,1)S(1)}, bf16[640,256]{1,0:T(8,128)(2,1)S(1)}, u32[]{:S(2)}, u32[]{:S(2)}) %collective-permute-start.4) | collective-permute-done | bytes 327712 | tf_op jit(solution)/shard_map/ppermute | solution.py:319
  26.6 1.6 %collective-permute-start.6 = (bf16[640,256]{1,0:T(8,128)(2,1)S(1)}, bf16[640,256]{1,0:T(8,128)(2,1)S(1)}, u32[]{:S(2)}, u32[]{:S(2)}) collective-permute-start(bf16[640,256]{1,0:T(8,128)(2,1)S(1)} %collective-permute-done.refs_0_), channel_id=1, source_target_pairs={{0,4},{4,8},{8,12},{12,0},{1,5},{5,9},{9,13},{13,1},{2,6},{6,10},{... | collective-permute-start | bytes 983048 | tf_op jit(solution)/shard_map/ppermute | solution.py:319
  28.7 1.5 %collective-permute-start.8 = (bf16[640,256]{1,0:T(8,128)(2,1)S(1)}, bf16[640,256]{1,0:T(8,128)(2,1)S(1)}, u32[]{:S(2)}, u32[]{:S(2)}) collective-permute-start(bf16[640,256]{1,0:T(8,128)(2,1)S(1)} %collective-permute-done.refs_0_), channel_id=1, source_target_pairs={{0,2},{2,0},{1,3},{3,1},{4,6},{6,4},{5,7},{7,5},{8,10},{10,8},{9,1... | collective-permute-start | bytes 983048 | tf_op jit(solution)/shard_map/ppermute | solution.py:314
  30.1 2.9 %collective-permute-done.9.late_ref = bf16[960,256]{1,0:T(8,128)(2,1)S(1)} collective-permute-done((bf16[960,256]{1,0:T(8,128)(2,1)S(1)}, bf16[960,256]{1,0:T(8,128)(2,1)S(1)}, u32[]{:S(2)}, u32[]{:S(2)}) %collective-permute-start.9) | collective-permute-done | bytes 491552 | tf_op jit(solution)/shard_map/ppermute | solution.py:314
  33.1 4.8 %collective-permute-done.6.p0 = bf16[640,256]{1,0:T(8,128)(2,1)S(1)} collective-permute-done((bf16[640,256]{1,0:T(8,128)(2,1)S(1)}, bf16[640,256]{1,0:T(8,128)(2,1)S(1)}, u32[]{:S(2)}, u32[]{:S(2)}) %collective-permute-start.6) | collective-permute-done | bytes 327712 | tf_op jit(solution)/shard_map/ppermute | solution.py:319
  37.9 1.2 %collective-permute-done.8.refs_1_ = bf16[640,256]{1,0:T(8,128)(2,1)S(1)} collective-permute-done((bf16[640,256]{1,0:T(8,128)(2,1)S(1)}, bf16[640,256]{1,0:T(8,128)(2,1)S(1)}, u32[]{:S(2)}, u32[]{:S(2)}) %collective-permute-start.8) | collective-permute-done | bytes 327712 | tf_op jit(solution)/shard_map/ppermute | solution.py:314
  39.9 1.6 %collective-permute-start.10 = (bf16[640,256]{1,0:T(8,128)(2,1)S(1)}, bf16[640,256]{1,0:T(8,128)(2,1)S(1)}, u32[]{:S(2)}, u32[]{:S(2)}) collective-permute-start(bf16[640,256]{1,0:T(8,128)(2,1)S(1)} %collective-permute-done.6.p0), channel_id=1, source_target_pairs={{0,2},{2,0},{1,3},{3,1},{4,6},{6,4},{5,7},{7,5},{8,10},{10,8},{9,1... | collective-permute-start | bytes 983048 | tf_op jit(solution)/shard_map/ppermute | solution.py:314
  42.0 1.5 %collective-permute-start.12 = (bf16[640,256]{1,0:T(8,128)(2,1)S(1)}, bf16[640,256]{1,0:T(8,128)(2,1)S(1)}, u32[]{:S(2)}, u32[]{:S(2)}) collective-permute-start(bf16[640,256]{1,0:T(8,128)(2,1)S(1)} %collective-permute-done.8.refs_1_), channel_id=1, source_target_pairs={{0,16},{16,0},{1,17},{17,1},{2,18},{18,2},{3,19},{19,3},{4,20},{20... | collective-permute-start | bytes 983048 | tf_op jit(solution)/shard_map/ppermute | solution.py:314
  44.0 5.3 %collective-permute-done.10.p1 = bf16[640,256]{1,0:T(8,128)(2,1)S(1)} collective-permute-done((bf16[640,256]{1,0:T(8,128)(2,1)S(1)}, bf16[640,256]{1,0:T(8,128)(2,1)S(1)}, u32[]{:S(2)}, u32[]{:S(2)}) %collective-permute-start.10) | collective-permute-done | bytes 327712 | tf_op jit(solution)/shard_map/ppermute | solution.py:314
  49.3 1.6 %collective-permute-done.11.p2 = bf16[640,256]{1,0:T(8,128)(2,1)S(1)} collective-permute-done((bf16[640,256]{1,0:T(8,128)(2,1)S(1)}, bf16[640,256]{1,0:T(8,128)(2,1)S(1)}, u32[]{:S(2)}, u32[]{:S(2)}) %collective-permute-start.11) | collective-permute-done | bytes 327712 | tf_op jit(solution)/shard_map/ppermute | solution.py:314
  50.9 7.0 %collective-permute-done.12.refs_3_ = bf16[640,256]{1,0:T(8,128)(2,1)S(1)} collective-permute-done((bf16[640,256]{1,0:T(8,128)(2,1)S(1)}, bf16[640,256]{1,0:T(8,128)(2,1)S(1)}, u32[]{:S(2)}, u32[]{:S(2)}) %collective-permute-start.12) | collective-permute-done | bytes 327712 | tf_op jit(solution)/shard_map/ppermute | solution.py:314
  59.6 6.8 %collective-permute-done.16.refs_7_ = bf16[640,256]{1,0:T(8,128)(2,1)S(1)} collective-permute-done((bf16[640,256]{1,0:T(8,128)(2,1)S(1)}, bf16[640,256]{1,0:T(8,128)(2,1)S(1)}, u32[]{:S(2)}, u32[]{:S(2)}) %collective-permute-start.16) | collective-permute-done | bytes 327712 | tf_op jit(solution)/shard_map/ppermute | solution.py:314
  66.4 1.4 %project.1.sums_ref = f32[2,256,256]{2,1,0:T(8,128)S(1)} custom-call(bf16[256,2560]{1,0:T(8,128)(2,1)S(1)} %get-tuple-element.50.own_ref, bf16[256,2560]{1,0:T(8,128)(2,1)S(1)} %collective-permute-done.5.other_ref, bf16[2,1280,256]{2,1,0:T(8,128)(2,1)S(1)} %copy-done.1, bf16[640,256]{1,0:T(8,128)(2,1)S(1)} %collective-permute-done.refs_0_, ...), custom_call_target="tpu_custom_call" | custom-call | flops 1006632960 | bytes 7000000 | tf_op jit(solution)/shard_map/project/pallas_call | solution.py:91
  67.9 5.1 %attention.1 = (bf16[256,1280]{1,0:T(8,128)(2,1)}, bf16[256,512]{1,0:T(8,128)(2,1)S(1)}) custom-call(bf16[256,2560]{1,0:T(8,128)(2,1)S(1)} %get-tuple-element.50.own_ref, bf16[256,2560]{1,0:T(8,128)(2,1)S(1)} %collective-permute-done.5.other_ref, bf16[640,256]{1,0:T(8,128)(2,1)S(1)} %collective-permute-done.6.p0, ...), custom_call_target="tpu_custom_call" | custom-call | flops 838860800 | bytes 5000000 | tf_op jit(solution)/shard_map/attention/pallas_call | solution.py:165
  73.0 2.5 %collective-permute-done.17.refs_2_.refs_3_.refs_4_.refs_5_ = bf16[2,640,256]{2,1,0:T(8,128)(2,1)S(1)} collective-permute-done((bf16[2,640,256]{2,1,0:T(8,128)(2,1)S(1)}, bf16[2,640,256]{2,1,0:T(8,128)(2,1)S(1)}, u32[]{:S(2)}, u32[]{:S(2)}) %collective-permute-start.17) | collective-permute-done | bytes 655392 | tf_op jit(solution)/shard_map/ppermute | solution.py:347
  76.3 9.0 %collective-permute-done.18.refs_14_ = bf16[256,512]{1,0:T(8,128)(2,1)S(1)} collective-permute-done((bf16[256,512]{1,0:T(8,128)(2,1)S(1)}, bf16[256,512]{1,0:T(8,128)(2,1)S(1)}, u32[]{:S(2)}, u32[]{:S(2)}) %collective-permute-start.18) | collective-permute-done | bytes 262176 | tf_op jit(solution)/shard_map/ppermute | solution.py:319
  85.2 1.7 %collective-permute-start.21 = (bf16[256,512]{1,0:T(8,128)(2,1)S(1)}, bf16[256,512]{1,0:T(8,128)(2,1)S(1)}, u32[]{:S(2)}, u32[]{:S(2)}) collective-permute-start(bf16[256,512]{1,0:T(8,128)(2,1)S(1)} %get-tuple-element.78.refs_12_), channel_id=1, source_target_pairs={{0,12},{4,0},{8,4},{12,8},{1,13},{5,1},{9,5},{13,9},{2,14},{6,2},{... | collective-permute-start | bytes 786440 | tf_op jit(solution)/shard_map/ppermute | solution.py:319
  88.2 4.1 %collective-permute-done.21.refs_15_ = bf16[256,512]{1,0:T(8,128)(2,1)S(1)} collective-permute-done((bf16[256,512]{1,0:T(8,128)(2,1)S(1)}, bf16[256,512]{1,0:T(8,128)(2,1)S(1)}, u32[]{:S(2)}, u32[]{:S(2)}) %collective-permute-start.21) | collective-permute-done | bytes 262176 | tf_op jit(solution)/shard_map/ppermute | solution.py:319
  92.3 1.1 %collective-permute-done.22.refs_16_ = bf16[256,512]{1,0:T(8,128)(2,1)S(1)} collective-permute-done((bf16[256,512]{1,0:T(8,128)(2,1)S(1)}, bf16[256,512]{1,0:T(8,128)(2,1)S(1)}, u32[]{:S(2)}, u32[]{:S(2)}) %collective-permute-start.22) | collective-permute-done | bytes 262176 | tf_op jit(solution)/shard_map/ppermute | solution.py:314
  94.8 6.8 %collective-permute-done.23.refs_4_ = bf16[256,512]{1,0:T(8,128)(2,1)S(1)} collective-permute-done((bf16[256,512]{1,0:T(8,128)(2,1)S(1)}, bf16[256,512]{1,0:T(8,128)(2,1)S(1)}, u32[]{:S(2)}, u32[]{:S(2)}) %collective-permute-start.23) | collective-permute-done | bytes 262176 | tf_op jit(solution)/shard_map/ppermute | solution.py:319
  102.4 1.7 %gradient.2 = (f32[2,640,256]{2,1,0:T(8,128)S(1)}, f32[2,256]{1,0:T(2,128)S(1)}) custom-call(bf16[2,640,256]{2,1,0:T(8,128)(2,1)S(1)} %collective-permute-done.14.refs_0_.refs_1_, bf16[2,640,256]{2,1,0:T(8,128)(2,1)S(1)} %collective-permute-done.14.refs_0_.refs_1_, bf16[2,640,256]{2,1,0:T(8,128)(2,1)S(1)} %collective-permute-done.17.refs_2_.refs_3_.refs_4_.refs_5_, ...), custom_call_target="tpu_custom_call" | custom-call | flops 1006632960 | bytes 5000000 | tf_op jit(solution)/shard_map/gradient/pallas_call | solution.py:230
  104.1 3.9 %collective-permute-done.25.refs_5_ = bf16[256,512]{1,0:T(8,128)(2,1)S(1)} collective-permute-done((bf16[256,512]{1,0:T(8,128)(2,1)S(1)}, bf16[256,512]{1,0:T(8,128)(2,1)S(1)}, u32[]{:S(2)}, u32[]{:S(2)}) %collective-permute-start.25) | collective-permute-done | bytes 262176 | tf_op jit(solution)/shard_map/ppermute | solution.py:314
  108.0 1.7 %gradient.3 = (f32[2,640,256]{2,1,0:T(8,128)}, f32[2,256]{1,0:T(2,128)}) custom-call(bf16[2,640,256]{2,1,0:T(8,128)(2,1)S(1)} %collective-permute-done.14.refs_0_.refs_1_, bf16[2,640,256]{2,1,0:T(8,128)(2,1)S(1)} %collective-permute-done.14.refs_0_.refs_1_, bf16[2,640,256]{2,1,0:T(8,128)(2,1)S(1)} %collective-permute-done.20.refs_6_.refs_7_.refs_2_.refs_3_, ...), custom_call_target="tpu_custom_call" | custom-call | flops 335544320 | bytes 5000000 | tf_op jit(solution)/shard_map/gradient/pallas_call | solution.py:230
  (51 shorter events, 10.4 us)
Async XLA Ops:
  0.6 7.2 %copy-start = (bf16[256,2560]{1,0:T(8,128)(2,1)S(1)}, bf16[256,2560]{1,0:T(8,128)(2,1)}, u32[]{:S(2)}) copy-start(bf16[256,2560]{1,0:T(8,128)(2,1)} %values_ref.1) | copy-start | bytes 3932164
  1.8 13.4 %collective-permute-start = (bf16[640,256]{1,0:T(8,128)(2,1)S(1)}, bf16[640,256]{1,0:T(8,128)(2,1)S(1)}, u32[]{:S(2)}, u32[]{:S(2)}) collective-permute-start(bf16[640,256]{1,0:T(8,128)(2,1)S(1)} %dynamic-slice_bitcast_fusion), channel_id=1, source_target_pairs={{0,4},{4,8},{8,12},{12,0},{1,5},{5,9},{9,13},{13,1},{2,6},{6,10},{... | collective-permute-start | bytes 983048 | tf_op jit(solution)/shard_map/ppermute | solution.py:319
  6.5 1.2 %collective-permute-start.1 = (f32[256,1]{0,1:T(1,128)S(1)}, f32[256,1]{0,1:T(1,128)S(1)}, u32[]{:S(2)}, u32[]{:S(2)}) collective-permute-start(f32[256,1]{0,1:T(1,128)S(1)} %bitcast.3), channel_id=1, source_target_pairs={{0,1},{1,0},{2,3},{3,2},{4,5},{5,4},{6,7},{7,6},{8,9},{9,8},{10,11... | collective-permute-start | bytes 3080 | tf_op jit(solution)/shard_map/ppermute | solution.py:314
  7.9 51.5 %copy-start.5 = (bf16[2,256]{1,0:T(2,128)(2,1)S(1)}, bf16[2,256]{1,0:T(2,128)(2,1)}, u32[]{:S(2)}) copy-start(bf16[2,256]{1,0:T(2,128)(2,1)} %param.11) | copy-start | bytes 3076
  8.8 57.6 %copy-start.1 = (bf16[2,1280,256]{2,1,0:T(8,128)(2,1)S(1)}, bf16[2,1280,256]{2,1,0:T(8,128)(2,1)}, u32[]{:S(2)}) copy-start(bf16[2,1280,256]{2,1,0:T(8,128)(2,1)} %weight_ref.1) | copy-start | bytes 3932164
  8.8 6.4 %collective-permute-start.2 = (bf16[320,256]{1,0:T(8,128)(2,1)S(1)}, bf16[320,256]{1,0:T(8,128)(2,1)S(1)}, u32[]{:S(2)}, u32[]{:S(2)}) collective-permute-start(bf16[320,256]{1,0:T(8,128)(2,1)S(1)} %get-tuple-element.48), channel_id=1, source_target_pairs={{0,2},{2,0},{1,3},{3,1},{4,6},{6,4},{5,7},{7,5},{8,10},{10,8},{9,1... | collective-permute-start | bytes 491528 | tf_op jit(solution)/shard_map/ppermute | solution.py:314
  15.2 11.4 %collective-permute-start.5 = (bf16[256,2560]{1,0:T(8,128)(2,1)S(1)}, bf16[256,2560]{1,0:T(8,128)(2,1)S(1)}, u32[]{:S(2)}, u32[]{:S(2)}) collective-permute-start(bf16[256,2560]{1,0:T(8,128)(2,1)S(1)} %get-tuple-element.50.own_ref), channel_id=1, source_target_pairs={{0,1},{1,0},{2,3},{3,2},{4,5},{5,4},{6,7},{7,6},{8,9},{9,8},{10,11... | collective-permute-start | bytes 3932168 | tf_op jit(solution)/shard_map/ppermute | solution.py:314
  15.2 10.1 %collective-permute-start.3 = (bf16[640,256]{1,0:T(8,128)(2,1)S(1)}, bf16[640,256]{1,0:T(8,128)(2,1)S(1)}, u32[]{:S(2)}, u32[]{:S(2)}) collective-permute-start(bf16[640,256]{1,0:T(8,128)(2,1)S(1)} %collective-permute-done.refs_0_), channel_id=1, source_target_pairs={{0,16},{16,0},{1,17},{17,1},{2,18},{18,2},{3,19},{19,3},{4,20},{20... | collective-permute-start | bytes 983048 | tf_op jit(solution)/shard_map/ppermute | solution.py:314
  16.7 9.8 %collective-permute-start.4 = (bf16[640,256]{1,0:T(8,128)(2,1)S(1)}, bf16[640,256]{1,0:T(8,128)(2,1)S(1)}, u32[]{:S(2)}, u32[]{:S(2)}) collective-permute-start(bf16[640,256]{1,0:T(8,128)(2,1)S(1)} %dynamic-slice_bitcast_fusion), channel_id=1, source_target_pairs={{0,12},{4,0},{8,4},{12,8},{1,13},{5,1},{9,5},{13,9},{2,14},{6,2},{... | collective-permute-start | bytes 983048 | tf_op jit(solution)/shard_map/ppermute | solution.py:319
  19.0 14.1 %collective-permute-start.9 = (bf16[960,256]{1,0:T(8,128)(2,1)S(1)}, bf16[960,256]{1,0:T(8,128)(2,1)S(1)}, u32[]{:S(2)}, u32[]{:S(2)}) collective-permute-start(bf16[960,256]{1,0:T(8,128)(2,1)S(1)} %get-tuple-element.56), channel_id=1, source_target_pairs={{0,2},{2,0},{1,3},{3,1},{4,6},{6,4},{5,7},{7,5},{8,10},{10,8},{9,1... | collective-permute-start | bytes 1474568 | tf_op jit(solution)/shard_map/ppermute | solution.py:314
  26.6 11.3 %collective-permute-start.6 = (bf16[640,256]{1,0:T(8,128)(2,1)S(1)}, bf16[640,256]{1,0:T(8,128)(2,1)S(1)}, u32[]{:S(2)}, u32[]{:S(2)}) collective-permute-start(bf16[640,256]{1,0:T(8,128)(2,1)S(1)} %collective-permute-done.refs_0_), channel_id=1, source_target_pairs={{0,4},{4,8},{8,12},{12,0},{1,5},{5,9},{9,13},{13,1},{2,6},{6,10},{... | collective-permute-start | bytes 983048 | tf_op jit(solution)/shard_map/ppermute | solution.py:319
  28.1 9.8 %collective-permute-start.7 = (bf16[640,256]{1,0:T(8,128)(2,1)S(1)}, bf16[640,256]{1,0:T(8,128)(2,1)S(1)}, u32[]{:S(2)}, u32[]{:S(2)}) collective-permute-start(bf16[640,256]{1,0:T(8,128)(2,1)S(1)} %collective-permute-done.4.refs_4_), channel_id=1, source_target_pairs={{0,16},{16,0},{1,17},{17,1},{2,18},{18,2},{3,19},{19,3},{4,20},{20... | collective-permute-start | bytes 983048 | tf_op jit(solution)/shard_map/ppermute | solution.py:314
  28.7 10.4 %collective-permute-start.8 = (bf16[640,256]{1,0:T(8,128)(2,1)S(1)}, bf16[640,256]{1,0:T(8,128)(2,1)S(1)}, u32[]{:S(2)}, u32[]{:S(2)}) collective-permute-start(bf16[640,256]{1,0:T(8,128)(2,1)S(1)} %collective-permute-done.refs_0_), channel_id=1, source_target_pairs={{0,2},{2,0},{1,3},{3,1},{4,6},{6,4},{5,7},{7,5},{8,10},{10,8},{9,1... | collective-permute-start | bytes 983048 | tf_op jit(solution)/shard_map/ppermute | solution.py:314
  39.2 18.7 %collective-permute-start.14 = (bf16[2,640,256]{2,1,0:T(8,128)(2,1)S(1)}, bf16[2,640,256]{2,1,0:T(8,128)(2,1)S(1)}, u32[]{:S(2)}, u32[]{:S(2)}) collective-permute-start(bf16[2,640,256]{2,1,0:T(8,128)(2,1)S(1)} %get-tuple-element.63), channel_id=1, source_target_pairs={{0,0},{1,8},{4,4},{5,12},{8,1},{9,9},{12,5},{13,13},{2,2},{3,10},{... | collective-permute-start | bytes 1966088 | tf_op jit(solution)/shard_map/ppermute | solution.py:347
  39.9 9.4 %collective-permute-start.10 = (bf16[640,256]{1,0:T(8,128)(2,1)S(1)}, bf16[640,256]{1,0:T(8,128)(2,1)S(1)}, u32[]{:S(2)}, u32[]{:S(2)}) collective-permute-start(bf16[640,256]{1,0:T(8,128)(2,1)S(1)} %collective-permute-done.6.p0), channel_id=1, source_target_pairs={{0,2},{2,0},{1,3},{3,1},{4,6},{6,4},{5,7},{7,5},{8,10},{10,8},{9,1... | collective-permute-start | bytes 983048 | tf_op jit(solution)/shard_map/ppermute | solution.py:314
  41.5 9.4 %collective-permute-start.11 = (bf16[640,256]{1,0:T(8,128)(2,1)S(1)}, bf16[640,256]{1,0:T(8,128)(2,1)S(1)}, u32[]{:S(2)}, u32[]{:S(2)}) collective-permute-start(bf16[640,256]{1,0:T(8,128)(2,1)S(1)} %collective-permute-done.6.p0), channel_id=1, source_target_pairs={{0,16},{16,0},{1,17},{17,1},{2,18},{18,2},{3,19},{19,3},{4,20},{20... | collective-permute-start | bytes 983048 | tf_op jit(solution)/shard_map/ppermute | solution.py:314
  42.0 15.9 %collective-permute-start.12 = (bf16[640,256]{1,0:T(8,128)(2,1)S(1)}, bf16[640,256]{1,0:T(8,128)(2,1)S(1)}, u32[]{:S(2)}, u32[]{:S(2)}) collective-permute-start(bf16[640,256]{1,0:T(8,128)(2,1)S(1)} %collective-permute-done.8.refs_1_), channel_id=1, source_target_pairs={{0,16},{16,0},{1,17},{17,1},{2,18},{18,2},{3,19},{19,3},{4,20},{20... | collective-permute-start | bytes 983048 | tf_op jit(solution)/shard_map/ppermute | solution.py:314
  43.5 14.4 %collective-permute-start.13 = (bf16[640,256]{1,0:T(8,128)(2,1)S(1)}, bf16[640,256]{1,0:T(8,128)(2,1)S(1)}, u32[]{:S(2)}, u32[]{:S(2)}) collective-permute-start(bf16[640,256]{1,0:T(8,128)(2,1)S(1)} %collective-permute-done.4.refs_4_), channel_id=1, source_target_pairs={{0,2},{2,0},{1,3},{3,1},{4,6},{6,4},{5,7},{7,5},{8,10},{10,8},{9,1... | collective-permute-start | bytes 983048 | tf_op jit(solution)/shard_map/ppermute | solution.py:314
  57.9 17.6 %collective-permute-start.17 = (bf16[2,640,256]{2,1,0:T(8,128)(2,1)S(1)}, bf16[2,640,256]{2,1,0:T(8,128)(2,1)S(1)}, u32[]{:S(2)}, u32[]{:S(2)}) collective-permute-start(bf16[2,640,256]{2,1,0:T(8,128)(2,1)S(1)} %get-tuple-element.74), channel_id=1, source_target_pairs={{0,4},{1,12},{4,0},{5,8},{8,5},{9,13},{12,1},{13,9},{2,6},{3,14},{... | collective-permute-start | bytes 1966088 | tf_op jit(solution)/shard_map/ppermute | solution.py:347
  57.9 8.5 %collective-permute-start.16 = (bf16[640,256]{1,0:T(8,128)(2,1)S(1)}, bf16[640,256]{1,0:T(8,128)(2,1)S(1)}, u32[]{:S(2)}, u32[]{:S(2)}) collective-permute-start(bf16[640,256]{1,0:T(8,128)(2,1)S(1)} %collective-permute-done.13.refs_5_), channel_id=1, source_target_pairs={{0,16},{16,0},{1,17},{17,1},{2,18},{18,2},{3,19},{19,3},{4,20},{20... | collective-permute-start | bytes 983048 | tf_op jit(solution)/shard_map/ppermute | solution.py:314
  58.4 9.5 %collective-permute-start.15 = (bf16[640,256]{1,0:T(8,128)(2,1)S(1)}, bf16[640,256]{1,0:T(8,128)(2,1)S(1)}, u32[]{:S(2)}, u32[]{:S(2)}) collective-permute-start(bf16[640,256]{1,0:T(8,128)(2,1)S(1)} %collective-permute-done.11.p2), channel_id=1, source_target_pairs={{0,2},{2,0},{1,3},{3,1},{4,6},{6,4},{5,7},{7,5},{8,10},{10,8},{9,1... | collective-permute-start | bytes 983048 | tf_op jit(solution)/shard_map/ppermute | solution.py:314
  59.6 8.3 %copy-start.2 = (bf16[256,1280]{1,0:T(8,128)(2,1)S(1)}, bf16[256,1280]{1,0:T(8,128)(2,1)}, u32[]{:S(2)}) copy-start(bf16[256,1280]{1,0:T(8,128)(2,1)} %queries_ref.1) | copy-start | bytes 1966084
  59.6 8.3 %copy-start.3 = (bf16[256,1280]{1,0:T(8,128)(2,1)S(1)}, bf16[256,1280]{1,0:T(8,128)(2,1)}, u32[]{:S(2)}) copy-start(bf16[256,1280]{1,0:T(8,128)(2,1)} %cotangent_ref.1) | copy-start | bytes 1966084
  75.5 9.7 %collective-permute-start.18 = (bf16[256,512]{1,0:T(8,128)(2,1)S(1)}, bf16[256,512]{1,0:T(8,128)(2,1)S(1)}, u32[]{:S(2)}, u32[]{:S(2)}) collective-permute-start(bf16[256,512]{1,0:T(8,128)(2,1)S(1)} %get-tuple-element.78.refs_12_), channel_id=1, source_target_pairs={{0,4},{4,8},{8,12},{12,0},{1,5},{5,9},{9,13},{13,1},{2,6},{6,10},{... | collective-permute-start | bytes 786440 | tf_op jit(solution)/shard_map/ppermute | solution.py:319
  75.5 9.7 %collective-permute-start.19 = (bf16[256,512]{1,0:T(8,128)(2,1)S(1)}, bf16[256,512]{1,0:T(8,128)(2,1)S(1)}, u32[]{:S(2)}, u32[]{:S(2)}) collective-permute-start(bf16[256,512]{1,0:T(8,128)(2,1)S(1)} %get-tuple-element.78.refs_12_), channel_id=1, source_target_pairs={{0,2},{2,0},{1,3},{3,1},{4,6},{6,4},{5,7},{7,5},{8,10},{10,8},{9,1... | collective-permute-start | bytes 786440 | tf_op jit(solution)/shard_map/ppermute | solution.py:314
  85.2 7.0 %collective-permute-start.21 = (bf16[256,512]{1,0:T(8,128)(2,1)S(1)}, bf16[256,512]{1,0:T(8,128)(2,1)S(1)}, u32[]{:S(2)}, u32[]{:S(2)}) collective-permute-start(bf16[256,512]{1,0:T(8,128)(2,1)S(1)} %get-tuple-element.78.refs_12_), channel_id=1, source_target_pairs={{0,12},{4,0},{8,4},{12,8},{1,13},{5,1},{9,5},{13,9},{2,14},{6,2},{... | collective-permute-start | bytes 786440 | tf_op jit(solution)/shard_map/ppermute | solution.py:319
  87.0 6.5 %collective-permute-start.22 = (bf16[256,512]{1,0:T(8,128)(2,1)S(1)}, bf16[256,512]{1,0:T(8,128)(2,1)S(1)}, u32[]{:S(2)}, u32[]{:S(2)}) collective-permute-start(bf16[256,512]{1,0:T(8,128)(2,1)S(1)} %collective-permute-done.18.refs_14_), channel_id=1, source_target_pairs={{0,2},{2,0},{1,3},{3,1},{4,6},{6,4},{5,7},{7,5},{8,10},{10,8},{9,1... | collective-permute-start | bytes 786440 | tf_op jit(solution)/shard_map/ppermute | solution.py:314
  87.7 14.6 %collective-permute-start.20 = (bf16[2,640,256]{2,1,0:T(8,128)(2,1)S(1)}, bf16[2,640,256]{2,1,0:T(8,128)(2,1)S(1)}, u32[]{:S(2)}, u32[]{:S(2)}) collective-permute-start(bf16[2,640,256]{2,1,0:T(8,128)(2,1)S(1)} %collective-permute-done.14.refs_0_.refs_1_), channel_id=1, source_target_pairs={{0,1},{1,0},{2,3},{3,2},{4,5},{5,4},{6,7},{7,6},{8,9},{9,8},{10,11... | collective-permute-start | bytes 1966088 | tf_op jit(solution)/shard_map/ppermute | solution.py:314
  87.7 14.6 %collective-permute-start.26 = (bf16[2,640,256]{2,1,0:T(8,128)(2,1)S(1)}, bf16[2,640,256]{2,1,0:T(8,128)(2,1)S(1)}, u32[]{:S(2)}, u32[]{:S(2)}) collective-permute-start(bf16[2,640,256]{2,1,0:T(8,128)(2,1)S(1)} %collective-permute-done.17.refs_2_.refs_3_.refs_4_.refs_5_), channel_id=1, source_target_pairs={{0,1},{1,0},{2,3},{3,2},{4,5},{5,4},{6,7},{7,6},{8,9},{9,8},{10,11... | collective-permute-start | bytes 1966088 | tf_op jit(solution)/shard_map/ppermute | solution.py:314
  93.4 8.2 %collective-permute-start.23 = (bf16[256,512]{1,0:T(8,128)(2,1)S(1)}, bf16[256,512]{1,0:T(8,128)(2,1)S(1)}, u32[]{:S(2)}, u32[]{:S(2)}) collective-permute-start(bf16[256,512]{1,0:T(8,128)(2,1)S(1)} %collective-permute-done.18.refs_14_), channel_id=1, source_target_pairs={{0,4},{4,8},{8,12},{12,0},{1,5},{5,9},{9,13},{13,1},{2,6},{6,10},{... | collective-permute-start | bytes 786440 | tf_op jit(solution)/shard_map/ppermute | solution.py:319
  94.0 7.6 %collective-permute-start.24 = (bf16[256,512]{1,0:T(8,128)(2,1)S(1)}, bf16[256,512]{1,0:T(8,128)(2,1)S(1)}, u32[]{:S(2)}, u32[]{:S(2)}) collective-permute-start(bf16[256,512]{1,0:T(8,128)(2,1)S(1)} %collective-permute-done.21.refs_15_), channel_id=1, source_target_pairs={{0,2},{2,0},{1,3},{3,1},{4,6},{6,4},{5,7},{7,5},{8,10},{10,8},{9,1... | collective-permute-start | bytes 786440 | tf_op jit(solution)/shard_map/ppermute | solution.py:314
  101.6 6.4 %collective-permute-start.25 = (bf16[256,512]{1,0:T(8,128)(2,1)S(1)}, bf16[256,512]{1,0:T(8,128)(2,1)S(1)}, u32[]{:S(2)}, u32[]{:S(2)}) collective-permute-start(bf16[256,512]{1,0:T(8,128)(2,1)S(1)} %collective-permute-done.23.refs_4_), channel_id=1, source_target_pairs={{0,2},{2,0},{1,3},{3,1},{4,6},{6,4},{5,7},{7,5},{8,10},{10,8},{9,1... | collective-permute-start | bytes 786440 | tf_op jit(solution)/shard_map/ppermute | solution.py:314
  (1 other events, 5.9 us)

commit v21 on v20

--- a/solution.py
+++ b/solution.py
@@ -395,14 +395,15 @@
     twice_y, up_both = swapped(twice, "groups"), swapped(up_x, "groups")
     even, odd = pack(kept, early, late)
     even = sent_along(even, 0)
-    twice_x, twice_y, up_both, down_x, even = lax.optimization_barrier(
-        (twice_x, twice_y, up_both, down_x, even)
+    odd = sent_along(after(odd, twice_y), 1)
+    twice_x, twice_y, up_both, down_x = lax.optimization_barrier(
+        (twice_x, twice_y, up_both, down_x)
     )
     down_both, twice_both = swapped(down_x, "groups"), swapped(twice_y, "dp")
-    odd = sent_along(after(odd, even), 1)
 
     gathered = [(1, (up, up_x, up_y, up_both)), (-1, (down, down_x, down_y, down_both))]
     sums = project(normed, normed_other, kv_weight, gathered)
+    sums = after(sums, even)
     grad_query, grad_pair = attention(
         2, normed, normed_other, (twice, twice_x, twice_y, twice_both), sums, bias, cosine, sine,
         queries, cotangent,

time: 110 us -> 113 us (1.027)
  starting transfers between devices: 25.1 us -> 37.7 us
  waiting for transfers between devices: 69 us -> 59.5 us
    ppermute x19, waiting for transfers between devices: 40.5 us -> 32.4 us  [swapped(): return lax.ppermute(block, axis, [(0, 1), (1, 0)])]
    ppermute x6, starting transfers between devices: 9.24 us -> 15.6 us  [turned(): lax.ppermute(block, axis, [(i, (i + distance) % size) for i in range(size)])]
    ppermute x19, starting transfers between devices: 15.2 us -> 21.4 us  [swapped(): return lax.ppermute(block, axis, [(0, 1), (1, 0)])]
  transfers between devices with their start and end apart: 27 -> 27, of which waited for: 17 -> 16; matrix products, arithmetic and copies ran while one was open for 2% -> 2% of each run, Pallas kernels for 8% -> 8%
where the time goes in v21:
time: 113 us
  waiting for transfers between devices  59.5 us (53%)
  starting transfers between devices  37.7 us (33%)
  Pallas kernels  11 us (10%)
  other arithmetic  2.4 us (2%)
  local copies, waits for them, and re-layouts  1.3 us (1%)
    ppermute x19, waiting for transfers between devices, swapped(): return lax.ppermute(block, axis, [(0, 1), (1, 0)])  32.4 us
    ppermute x6, waiting for transfers between devices, turned(): lax.ppermute(block, axis, [(i, (i + distance) % size) for i in range(size)])  25.2 us
    ppermute x19, starting transfers between devices, swapped(): return lax.ppermute(block, axis, [(0, 1), (1, 0)])  21.4 us
    ppermute x6, starting transfers between devices, turned(): lax.ppermute(block, axis, [(i, (i + distance) % size) for i in range(size)])  15.6 us
    pallas_call x1, Pallas kernels, attention(): pl.pallas_call(functools.partial(attention_kernel, distance), in_specs=[I...  5.07 us
    pallas_call x2, Pallas kernels, gradient(): pl.pallas_call(functools.partial(gradient_kernel, tuple(some), sums is No...  3.47 us
  transfers between devices with their start and end apart: 27, of which 16 were waited for; matrix products, arithmetic and copies ran while one was open for 2% of the time, Pallas kernels for 8%

profile of v21, /device:TPU:0, one launch (start us, length us, event | category | flops | bytes accessed | tf_op | source)
XLA Modules:
  0.0 112.8 jit_solution(13026187893436666625)
XLA Ops:
  1.8 3.1 %collective-permute-start = (bf16[640,256]{1,0:T(8,128)(2,1)S(1)}, bf16[640,256]{1,0:T(8,128)(2,1)S(1)}, u32[]{:S(2)}, u32[]{:S(2)}) collective-permute-start(bf16[640,256]{1,0:T(8,128)(2,1)S(1)} %dynamic-slice_bitcast_fusion), channel_id=1, source_target_pairs={{0,4},{4,8},{8,12},{12,0},{1,5},{5,9},{9,13},{13,1},{2,6},{6,10},{... | collective-permute-start | bytes 983048 | tf_op jit(solution)/shard_map/ppermute | solution.py:319
  4.8 1.7 %multiply_reduce_fusion = f32[256]{0:T(256)S(1)} fusion(bf16[256,2560]{1,0:T(8,128)(2,1)} %values_ref.1), kind=kLoop, calls=%fused_computation | loop fusion | flops 1965824 | bytes 1311744 | tf_op jit(solution)/shard_map/reduce_sum | solution.py:354
  8.8 1.6 %collective-permute-start.2 = (bf16[320,256]{1,0:T(8,128)(2,1)S(1)}, bf16[320,256]{1,0:T(8,128)(2,1)S(1)}, u32[]{:S(2)}, u32[]{:S(2)}) collective-permute-start(bf16[320,256]{1,0:T(8,128)(2,1)S(1)} %get-tuple-element.48), channel_id=1, source_target_pairs={{0,2},{2,0},{1,3},{3,1},{4,6},{6,4},{5,7},{7,5},{8,10},{10,8},{9,1... | collective-permute-start | bytes 491528 | tf_op jit(solution)/shard_map/ppermute | solution.py:314
  10.4 4.8 %collective-permute-done.2.early_ref = bf16[320,256]{1,0:T(8,128)(2,1)S(1)} collective-permute-done((bf16[320,256]{1,0:T(8,128)(2,1)S(1)}, bf16[320,256]{1,0:T(8,128)(2,1)S(1)}, u32[]{:S(2)}, u32[]{:S(2)}) %collective-permute-start.2) | collective-permute-done | bytes 163872 | tf_op jit(solution)/shard_map/ppermute | solution.py:314
  15.2 1.5 %collective-permute-start.3 = (bf16[640,256]{1,0:T(8,128)(2,1)S(1)}, bf16[640,256]{1,0:T(8,128)(2,1)S(1)}, u32[]{:S(2)}, u32[]{:S(2)}) collective-permute-start(bf16[640,256]{1,0:T(8,128)(2,1)S(1)} %collective-permute-done.refs_0_), channel_id=1, source_target_pairs={{0,16},{16,0},{1,17},{17,1},{2,18},{18,2},{3,19},{19,3},{4,20},{20... | collective-permute-start | bytes 983048 | tf_op jit(solution)/shard_map/ppermute | solution.py:314
  16.7 2.2 %collective-permute-start.4 = (bf16[640,256]{1,0:T(8,128)(2,1)S(1)}, bf16[640,256]{1,0:T(8,128)(2,1)S(1)}, u32[]{:S(2)}, u32[]{:S(2)}) collective-permute-start(bf16[640,256]{1,0:T(8,128)(2,1)S(1)} %dynamic-slice_bitcast_fusion), channel_id=1, source_target_pairs={{0,12},{4,0},{8,4},{12,8},{1,13},{5,1},{9,5},{13,9},{2,14},{6,2},{... | collective-permute-start | bytes 983048 | tf_op jit(solution)/shard_map/ppermute | solution.py:319
  19.0 1.5 %collective-permute-start.9 = (bf16[960,256]{1,0:T(8,128)(2,1)S(1)}, bf16[960,256]{1,0:T(8,128)(2,1)S(1)}, u32[]{:S(2)}, u32[]{:S(2)}) collective-permute-start(bf16[960,256]{1,0:T(8,128)(2,1)S(1)} %get-tuple-element.56), channel_id=1, source_target_pairs={{0,2},{2,0},{1,3},{3,1},{4,6},{6,4},{5,7},{7,5},{8,10},{10,8},{9,1... | collective-permute-start | bytes 1474568 | tf_op jit(solution)/shard_map/ppermute | solution.py:314
  20.5 4.9 %collective-permute-done.3.refs_2_ = bf16[640,256]{1,0:T(8,128)(2,1)S(1)} collective-permute-done((bf16[640,256]{1,0:T(8,128)(2,1)S(1)}, bf16[640,256]{1,0:T(8,128)(2,1)S(1)}, u32[]{:S(2)}, u32[]{:S(2)}) %collective-permute-start.3) | collective-permute-done | bytes 327712 | tf_op jit(solution)/shard_map/ppermute | solution.py:314
  26.6 1.6 %collective-permute-start.6 = (bf16[640,256]{1,0:T(8,128)(2,1)S(1)}, bf16[640,256]{1,0:T(8,128)(2,1)S(1)}, u32[]{:S(2)}, u32[]{:S(2)}) collective-permute-start(bf16[640,256]{1,0:T(8,128)(2,1)S(1)} %collective-permute-done.refs_0_), channel_id=1, source_target_pairs={{0,4},{4,8},{8,12},{12,0},{1,5},{5,9},{9,13},{13,1},{2,6},{6,10},{... | collective-permute-start | bytes 983048 | tf_op jit(solution)/shard_map/ppermute | solution.py:319
  30.1 2.9 %collective-permute-done.9.late_ref = bf16[960,256]{1,0:T(8,128)(2,1)S(1)} collective-permute-done((bf16[960,256]{1,0:T(8,128)(2,1)S(1)}, bf16[960,256]{1,0:T(8,128)(2,1)S(1)}, u32[]{:S(2)}, u32[]{:S(2)}) %collective-permute-start.9) | collective-permute-done | bytes 491552 | tf_op jit(solution)/shard_map/ppermute | solution.py:314
  33.1 4.8 %collective-permute-done.6.p0 = bf16[640,256]{1,0:T(8,128)(2,1)S(1)} collective-permute-done((bf16[640,256]{1,0:T(8,128)(2,1)S(1)}, bf16[640,256]{1,0:T(8,128)(2,1)S(1)}, u32[]{:S(2)}, u32[]{:S(2)}) %collective-permute-start.6) | collective-permute-done | bytes 327712 | tf_op jit(solution)/shard_map/ppermute | solution.py:319
  39.4 1.7 %collective-permute-start.10 = (bf16[640,256]{1,0:T(8,128)(2,1)S(1)}, bf16[640,256]{1,0:T(8,128)(2,1)S(1)}, u32[]{:S(2)}, u32[]{:S(2)}) collective-permute-start(bf16[640,256]{1,0:T(8,128)(2,1)S(1)} %collective-permute-done.6.p0), channel_id=1, source_target_pairs={{0,2},{2,0},{1,3},{3,1},{4,6},{6,4},{5,7},{7,5},{8,10},{10,8},{9,1... | collective-permute-start | bytes 983048 | tf_op jit(solution)/shard_map/ppermute | solution.py:314
  41.1 1.5 %collective-permute-start.12 = (bf16[640,256]{1,0:T(8,128)(2,1)S(1)}, bf16[640,256]{1,0:T(8,128)(2,1)S(1)}, u32[]{:S(2)}, u32[]{:S(2)}) collective-permute-start(bf16[640,256]{1,0:T(8,128)(2,1)S(1)} %collective-permute-done.8.refs_1_), channel_id=1, source_target_pairs={{0,16},{16,0},{1,17},{17,1},{2,18},{18,2},{3,19},{19,3},{4,20},{20... | collective-permute-start | bytes 983048 | tf_op jit(solution)/shard_map/ppermute | solution.py:314
  44.0 5.8 %collective-permute-done.11.p2 = bf16[640,256]{1,0:T(8,128)(2,1)S(1)} collective-permute-done((bf16[640,256]{1,0:T(8,128)(2,1)S(1)}, bf16[640,256]{1,0:T(8,128)(2,1)S(1)}, u32[]{:S(2)}, u32[]{:S(2)}) %collective-permute-start.11) | collective-permute-done | bytes 327712 | tf_op jit(solution)/shard_map/ppermute | solution.py:314
  50.0 4.8 %collective-permute-done.12.refs_3_ = bf16[640,256]{1,0:T(8,128)(2,1)S(1)} collective-permute-done((bf16[640,256]{1,0:T(8,128)(2,1)S(1)}, bf16[640,256]{1,0:T(8,128)(2,1)S(1)}, u32[]{:S(2)}, u32[]{:S(2)}) %collective-permute-start.12) | collective-permute-done | bytes 327712 | tf_op jit(solution)/shard_map/ppermute | solution.py:314
  54.8 1.7 %collective-permute-start.15 = (bf16[640,256]{1,0:T(8,128)(2,1)S(1)}, bf16[640,256]{1,0:T(8,128)(2,1)S(1)}, u32[]{:S(2)}, u32[]{:S(2)}) collective-permute-start(bf16[640,256]{1,0:T(8,128)(2,1)S(1)} %collective-permute-done.13.refs_5_), channel_id=1, source_target_pairs={{0,16},{16,0},{1,17},{17,1},{2,18},{18,2},{3,19},{19,3},{4,20},{20... | collective-permute-start | bytes 983048 | tf_op jit(solution)/shard_map/ppermute | solution.py:314
  56.5 1.5 %collective-permute-start.14 = (bf16[640,256]{1,0:T(8,128)(2,1)S(1)}, bf16[640,256]{1,0:T(8,128)(2,1)S(1)}, u32[]{:S(2)}, u32[]{:S(2)}) collective-permute-start(bf16[640,256]{1,0:T(8,128)(2,1)S(1)} %collective-permute-done.11.p2), channel_id=1, source_target_pairs={{0,2},{2,0},{1,3},{3,1},{4,6},{6,4},{5,7},{7,5},{8,10},{10,8},{9,1... | collective-permute-start | bytes 983048 | tf_op jit(solution)/shard_map/ppermute | solution.py:314
  58.7 3.9 %collective-permute-done.15.refs_7_ = bf16[640,256]{1,0:T(8,128)(2,1)S(1)} collective-permute-done((bf16[640,256]{1,0:T(8,128)(2,1)S(1)}, bf16[640,256]{1,0:T(8,128)(2,1)S(1)}, u32[]{:S(2)}, u32[]{:S(2)}) %collective-permute-start.15) | collective-permute-done | bytes 327712 | tf_op jit(solution)/shard_map/ppermute | solution.py:314
  64.1 5.1 %attention.1 = (bf16[256,1280]{1,0:T(8,128)(2,1)}, bf16[256,512]{1,0:T(8,128)(2,1)S(1)}) custom-call(bf16[256,2560]{1,0:T(8,128)(2,1)S(1)} %get-tuple-element.50.own_ref, bf16[256,2560]{1,0:T(8,128)(2,1)S(1)} %collective-permute-done.5.other_ref, bf16[640,256]{1,0:T(8,128)(2,1)S(1)} %collective-permute-done.6.p0, ...), custom_call_target="tpu_custom_call" | custom-call | flops 838860800 | bytes 5000000 | tf_op jit(solution)/shard_map/attention/pallas_call | solution.py:165
  69.1 1.9 %collective-permute-done.17.refs_2_.refs_3_.refs_4_.refs_5_ = bf16[2,640,256]{2,1,0:T(8,128)(2,1)S(1)} collective-permute-done((bf16[2,640,256]{2,1,0:T(8,128)(2,1)S(1)}, bf16[2,640,256]{2,1,0:T(8,128)(2,1)S(1)}, u32[]{:S(2)}, u32[]{:S(2)}) %collective-permute-start.17) | collective-permute-done | bytes 655392 | tf_op jit(solution)/shard_map/ppermute | solution.py:347
  71.0 1.8 %collective-permute-start.19 = (bf16[256,512]{1,0:T(8,128)(2,1)S(1)}, bf16[256,512]{1,0:T(8,128)(2,1)S(1)}, u32[]{:S(2)}, u32[]{:S(2)}) collective-permute-start(bf16[256,512]{1,0:T(8,128)(2,1)S(1)} %get-tuple-element.78.refs_12_), channel_id=1, source_target_pairs={{0,2},{2,0},{1,3},{3,1},{4,6},{6,4},{5,7},{7,5},{8,10},{10,8},{9,1... | collective-permute-start | bytes 786440 | tf_op jit(solution)/shard_map/ppermute | solution.py:314
  72.9 6.8 %collective-permute-done.18.refs_14_ = bf16[256,512]{1,0:T(8,128)(2,1)S(1)} collective-permute-done((bf16[256,512]{1,0:T(8,128)(2,1)S(1)}, bf16[256,512]{1,0:T(8,128)(2,1)S(1)}, u32[]{:S(2)}, u32[]{:S(2)}) %collective-permute-start.18) | collective-permute-done | bytes 262176 | tf_op jit(solution)/shard_map/ppermute | solution.py:319
  79.6 7.0 %collective-permute-start.21 = (bf16[256,512]{1,0:T(8,128)(2,1)S(1)}, bf16[256,512]{1,0:T(8,128)(2,1)S(1)}, u32[]{:S(2)}, u32[]{:S(2)}) collective-permute-start(bf16[256,512]{1,0:T(8,128)(2,1)S(1)} %get-tuple-element.78.refs_12_), channel_id=1, source_target_pairs={{0,12},{4,0},{8,4},{12,8},{1,13},{5,1},{9,5},{13,9},{2,14},{6,2},{... | collective-permute-start | bytes 786440 | tf_op jit(solution)/shard_map/ppermute | solution.py:319
  86.6 1.7 %collective-permute-start.22 = (bf16[256,512]{1,0:T(8,128)(2,1)S(1)}, bf16[256,512]{1,0:T(8,128)(2,1)S(1)}, u32[]{:S(2)}, u32[]{:S(2)}) collective-permute-start(bf16[256,512]{1,0:T(8,128)(2,1)S(1)} %collective-permute-done.18.refs_14_), channel_id=1, source_target_pairs={{0,2},{2,0},{1,3},{3,1},{4,6},{6,4},{5,7},{7,5},{8,10},{10,8},{9,1... | collective-permute-start | bytes 786440 | tf_op jit(solution)/shard_map/ppermute | solution.py:314
  88.8 7.0 %collective-permute-done.21.refs_15_ = bf16[256,512]{1,0:T(8,128)(2,1)S(1)} collective-permute-done((bf16[256,512]{1,0:T(8,128)(2,1)S(1)}, bf16[256,512]{1,0:T(8,128)(2,1)S(1)}, u32[]{:S(2)}, u32[]{:S(2)}) %collective-permute-start.21) | collective-permute-done | bytes 262176 | tf_op jit(solution)/shard_map/ppermute | solution.py:319
  95.8 1.7 %collective-permute-start.23 = (bf16[256,512]{1,0:T(8,128)(2,1)S(1)}, bf16[256,512]{1,0:T(8,128)(2,1)S(1)}, u32[]{:S(2)}, u32[]{:S(2)}) collective-permute-start(bf16[256,512]{1,0:T(8,128)(2,1)S(1)} %collective-permute-done.18.refs_14_), channel_id=1, source_target_pairs={{0,4},{4,8},{8,12},{12,0},{1,5},{5,9},{9,13},{13,1},{2,6},{6,10},{... | collective-permute-start | bytes 786440 | tf_op jit(solution)/shard_map/ppermute | solution.py:319
  97.6 1.7 %collective-permute-start.24 = (bf16[256,512]{1,0:T(8,128)(2,1)S(1)}, bf16[256,512]{1,0:T(8,128)(2,1)S(1)}, u32[]{:S(2)}, u32[]{:S(2)}) collective-permute-start(bf16[256,512]{1,0:T(8,128)(2,1)S(1)} %collective-permute-done.21.refs_15_), channel_id=1, source_target_pairs={{0,2},{2,0},{1,3},{3,1},{4,6},{6,4},{5,7},{7,5},{8,10},{10,8},{9,1... | collective-permute-start | bytes 786440 | tf_op jit(solution)/shard_map/ppermute | solution.py:314
  99.3 5.4 %collective-permute-done.23.refs_4_ = bf16[256,512]{1,0:T(8,128)(2,1)S(1)} collective-permute-done((bf16[256,512]{1,0:T(8,128)(2,1)S(1)}, bf16[256,512]{1,0:T(8,128)(2,1)S(1)}, u32[]{:S(2)}, u32[]{:S(2)}) %collective-permute-start.23) | collective-permute-done | bytes 262176 | tf_op jit(solution)/shard_map/ppermute | solution.py:319
  104.7 1.7 %collective-permute-start.25 = (bf16[256,512]{1,0:T(8,128)(2,1)S(1)}, bf16[256,512]{1,0:T(8,128)(2,1)S(1)}, u32[]{:S(2)}, u32[]{:S(2)}) collective-permute-start(bf16[256,512]{1,0:T(8,128)(2,1)S(1)} %collective-permute-done.23.refs_4_), channel_id=1, source_target_pairs={{0,2},{2,0},{1,3},{3,1},{4,6},{6,4},{5,7},{7,5},{8,10},{10,8},{9,1... | collective-permute-start | bytes 786440 | tf_op jit(solution)/shard_map/ppermute | solution.py:314
  106.4 1.7 %gradient.2 = (f32[2,640,256]{2,1,0:T(8,128)S(1)}, f32[2,256]{1,0:T(2,128)S(1)}) custom-call(bf16[2,640,256]{2,1,0:T(8,128)(2,1)S(1)} %collective-permute-done.16.refs_0_.refs_1_, bf16[2,640,256]{2,1,0:T(8,128)(2,1)S(1)} %collective-permute-done.16.refs_0_.refs_1_, bf16[2,640,256]{2,1,0:T(8,128)(2,1)S(1)} %collective-permute-done.17.refs_2_.refs_3_.refs_4_.refs_5_, ...), custom_call_target="tpu_custom_call" | custom-call | flops 1006632960 | bytes 5000000 | tf_op jit(solution)/shard_map/gradient/pallas_call | solution.py:230
  108.1 2.9 %collective-permute-done.25.refs_5_ = bf16[256,512]{1,0:T(8,128)(2,1)S(1)} collective-permute-done((bf16[256,512]{1,0:T(8,128)(2,1)S(1)}, bf16[256,512]{1,0:T(8,128)(2,1)S(1)}, u32[]{:S(2)}, u32[]{:S(2)}) %collective-permute-start.25) | collective-permute-done | bytes 262176 | tf_op jit(solution)/shard_map/ppermute | solution.py:314
  111.1 1.7 %gradient.3 = (f32[2,640,256]{2,1,0:T(8,128)}, f32[2,256]{1,0:T(2,128)}) custom-call(bf16[2,640,256]{2,1,0:T(8,128)(2,1)S(1)} %collective-permute-done.16.refs_0_.refs_1_, bf16[2,640,256]{2,1,0:T(8,128)(2,1)S(1)} %collective-permute-done.16.refs_0_.refs_1_, bf16[2,640,256]{2,1,0:T(8,128)(2,1)S(1)} %collective-permute-done.20.refs_6_.refs_7_.refs_2_.refs_3_, ...), custom_call_target="tpu_custom_call" | custom-call | flops 335544320 | bytes 5000000 | tf_op jit(solution)/shard_map/gradient/pallas_call | solution.py:230
  (51 shorter events, 12.4 us)
Async XLA Ops:
  0.6 7.2 %copy-start = (bf16[256,2560]{1,0:T(8,128)(2,1)S(1)}, bf16[256,2560]{1,0:T(8,128)(2,1)}, u32[]{:S(2)}) copy-start(bf16[256,2560]{1,0:T(8,128)(2,1)} %values_ref.1) | copy-start | bytes 3932164
  0.6 5.9 %copy-start.4 = (bf16[5120]{0:T(1024)(128)(2,1)S(1)}, bf16[5120]{0:T(1024)(128)(2,1)}, u32[]{:S(2)}) copy-start(bf16[5120]{0:T(1024)(128)(2,1)} %param.7) | copy-start | bytes 30724
  1.8 13.4 %collective-permute-start = (bf16[640,256]{1,0:T(8,128)(2,1)S(1)}, bf16[640,256]{1,0:T(8,128)(2,1)S(1)}, u32[]{:S(2)}, u32[]{:S(2)}) collective-permute-start(bf16[640,256]{1,0:T(8,128)(2,1)S(1)} %dynamic-slice_bitcast_fusion), channel_id=1, source_target_pairs={{0,4},{4,8},{8,12},{12,0},{1,5},{5,9},{9,13},{13,1},{2,6},{6,10},{... | collective-permute-start | bytes 983048 | tf_op jit(solution)/shard_map/ppermute | solution.py:319
  6.5 1.2 %collective-permute-start.1 = (f32[256,1]{0,1:T(1,128)S(1)}, f32[256,1]{0,1:T(1,128)S(1)}, u32[]{:S(2)}, u32[]{:S(2)}) collective-permute-start(f32[256,1]{0,1:T(1,128)S(1)} %bitcast.3), channel_id=1, source_target_pairs={{0,1},{1,0},{2,3},{3,2},{4,5},{5,4},{6,7},{7,6},{8,9},{9,8},{10,11... | collective-permute-start | bytes 3080 | tf_op jit(solution)/shard_map/ppermute | solution.py:314
  7.9 50.7 %copy-start.5 = (bf16[2,256]{1,0:T(2,128)(2,1)S(1)}, bf16[2,256]{1,0:T(2,128)(2,1)}, u32[]{:S(2)}) copy-start(bf16[2,256]{1,0:T(2,128)(2,1)} %param.11) | copy-start | bytes 3076
  8.8 53.8 %copy-start.1 = (bf16[2,1280,256]{2,1,0:T(8,128)(2,1)S(1)}, bf16[2,1280,256]{2,1,0:T(8,128)(2,1)}, u32[]{:S(2)}) copy-start(bf16[2,1280,256]{2,1,0:T(8,128)(2,1)} %weight_ref.1) | copy-start | bytes 3932164
  8.8 6.4 %collective-permute-start.2 = (bf16[320,256]{1,0:T(8,128)(2,1)S(1)}, bf16[320,256]{1,0:T(8,128)(2,1)S(1)}, u32[]{:S(2)}, u32[]{:S(2)}) collective-permute-start(bf16[320,256]{1,0:T(8,128)(2,1)S(1)} %get-tuple-element.48), channel_id=1, source_target_pairs={{0,2},{2,0},{1,3},{3,1},{4,6},{6,4},{5,7},{7,5},{8,10},{10,8},{9,1... | collective-permute-start | bytes 491528 | tf_op jit(solution)/shard_map/ppermute | solution.py:314
  15.2 11.4 %collective-permute-start.5 = (bf16[256,2560]{1,0:T(8,128)(2,1)S(1)}, bf16[256,2560]{1,0:T(8,128)(2,1)S(1)}, u32[]{:S(2)}, u32[]{:S(2)}) collective-permute-start(bf16[256,2560]{1,0:T(8,128)(2,1)S(1)} %get-tuple-element.50.own_ref), channel_id=1, source_target_pairs={{0,1},{1,0},{2,3},{3,2},{4,5},{5,4},{6,7},{7,6},{8,9},{9,8},{10,11... | collective-permute-start | bytes 3932168 | tf_op jit(solution)/shard_map/ppermute | solution.py:314
  15.2 10.1 %collective-permute-start.3 = (bf16[640,256]{1,0:T(8,128)(2,1)S(1)}, bf16[640,256]{1,0:T(8,128)(2,1)S(1)}, u32[]{:S(2)}, u32[]{:S(2)}) collective-permute-start(bf16[640,256]{1,0:T(8,128)(2,1)S(1)} %collective-permute-done.refs_0_), channel_id=1, source_target_pairs={{0,16},{16,0},{1,17},{17,1},{2,18},{18,2},{3,19},{19,3},{4,20},{20... | collective-permute-start | bytes 983048 | tf_op jit(solution)/shard_map/ppermute | solution.py:314
  16.7 9.8 %collective-permute-start.4 = (bf16[640,256]{1,0:T(8,128)(2,1)S(1)}, bf16[640,256]{1,0:T(8,128)(2,1)S(1)}, u32[]{:S(2)}, u32[]{:S(2)}) collective-permute-start(bf16[640,256]{1,0:T(8,128)(2,1)S(1)} %dynamic-slice_bitcast_fusion), channel_id=1, source_target_pairs={{0,12},{4,0},{8,4},{12,8},{1,13},{5,1},{9,5},{13,9},{2,14},{6,2},{... | collective-permute-start | bytes 983048 | tf_op jit(solution)/shard_map/ppermute | solution.py:319
  19.0 14.1 %collective-permute-start.9 = (bf16[960,256]{1,0:T(8,128)(2,1)S(1)}, bf16[960,256]{1,0:T(8,128)(2,1)S(1)}, u32[]{:S(2)}, u32[]{:S(2)}) collective-permute-start(bf16[960,256]{1,0:T(8,128)(2,1)S(1)} %get-tuple-element.56), channel_id=1, source_target_pairs={{0,2},{2,0},{1,3},{3,1},{4,6},{6,4},{5,7},{7,5},{8,10},{10,8},{9,1... | collective-permute-start | bytes 1474568 | tf_op jit(solution)/shard_map/ppermute | solution.py:314
  26.6 11.3 %collective-permute-start.6 = (bf16[640,256]{1,0:T(8,128)(2,1)S(1)}, bf16[640,256]{1,0:T(8,128)(2,1)S(1)}, u32[]{:S(2)}, u32[]{:S(2)}) collective-permute-start(bf16[640,256]{1,0:T(8,128)(2,1)S(1)} %collective-permute-done.refs_0_), channel_id=1, source_target_pairs={{0,4},{4,8},{8,12},{12,0},{1,5},{5,9},{9,13},{13,1},{2,6},{6,10},{... | collective-permute-start | bytes 983048 | tf_op jit(solution)/shard_map/ppermute | solution.py:319
  28.1 9.8 %collective-permute-start.7 = (bf16[640,256]{1,0:T(8,128)(2,1)S(1)}, bf16[640,256]{1,0:T(8,128)(2,1)S(1)}, u32[]{:S(2)}, u32[]{:S(2)}) collective-permute-start(bf16[640,256]{1,0:T(8,128)(2,1)S(1)} %collective-permute-done.4.refs_4_), channel_id=1, source_target_pairs={{0,16},{16,0},{1,17},{17,1},{2,18},{18,2},{3,19},{19,3},{4,20},{20... | collective-permute-start | bytes 983048 | tf_op jit(solution)/shard_map/ppermute | solution.py:314
  28.7 10.4 %collective-permute-start.8 = (bf16[640,256]{1,0:T(8,128)(2,1)S(1)}, bf16[640,256]{1,0:T(8,128)(2,1)S(1)}, u32[]{:S(2)}, u32[]{:S(2)}) collective-permute-start(bf16[640,256]{1,0:T(8,128)(2,1)S(1)} %collective-permute-done.refs_0_), channel_id=1, source_target_pairs={{0,2},{2,0},{1,3},{3,1},{4,6},{6,4},{5,7},{7,5},{8,10},{10,8},{9,1... | collective-permute-start | bytes 983048 | tf_op jit(solution)/shard_map/ppermute | solution.py:314
  39.1 10.6 %collective-permute-start.11 = (bf16[640,256]{1,0:T(8,128)(2,1)S(1)}, bf16[640,256]{1,0:T(8,128)(2,1)S(1)}, u32[]{:S(2)}, u32[]{:S(2)}) collective-permute-start(bf16[640,256]{1,0:T(8,128)(2,1)S(1)} %collective-permute-done.6.p0), channel_id=1, source_target_pairs={{0,16},{16,0},{1,17},{17,1},{2,18},{18,2},{3,19},{19,3},{4,20},{20... | collective-permute-start | bytes 983048 | tf_op jit(solution)/shard_map/ppermute | solution.py:314
  39.4 10.6 %collective-permute-start.10 = (bf16[640,256]{1,0:T(8,128)(2,1)S(1)}, bf16[640,256]{1,0:T(8,128)(2,1)S(1)}, u32[]{:S(2)}, u32[]{:S(2)}) collective-permute-start(bf16[640,256]{1,0:T(8,128)(2,1)S(1)} %collective-permute-done.6.p0), channel_id=1, source_target_pairs={{0,2},{2,0},{1,3},{3,1},{4,6},{6,4},{5,7},{7,5},{8,10},{10,8},{9,1... | collective-permute-start | bytes 983048 | tf_op jit(solution)/shard_map/ppermute | solution.py:314
  41.1 13.7 %collective-permute-start.12 = (bf16[640,256]{1,0:T(8,128)(2,1)S(1)}, bf16[640,256]{1,0:T(8,128)(2,1)S(1)}, u32[]{:S(2)}, u32[]{:S(2)}) collective-permute-start(bf16[640,256]{1,0:T(8,128)(2,1)S(1)} %collective-permute-done.8.refs_1_), channel_id=1, source_target_pairs={{0,16},{16,0},{1,17},{17,1},{2,18},{18,2},{3,19},{19,3},{4,20},{20... | collective-permute-start | bytes 983048 | tf_op jit(solution)/shard_map/ppermute | solution.py:314
  42.6 12.2 %collective-permute-start.13 = (bf16[640,256]{1,0:T(8,128)(2,1)S(1)}, bf16[640,256]{1,0:T(8,128)(2,1)S(1)}, u32[]{:S(2)}, u32[]{:S(2)}) collective-permute-start(bf16[640,256]{1,0:T(8,128)(2,1)S(1)} %collective-permute-done.4.refs_4_), channel_id=1, source_target_pairs={{0,2},{2,0},{1,3},{3,1},{4,6},{6,4},{5,7},{7,5},{8,10},{10,8},{9,1... | collective-permute-start | bytes 983048 | tf_op jit(solution)/shard_map/ppermute | solution.py:314
  43.3 20.8 %collective-permute-start.16 = (bf16[2,640,256]{2,1,0:T(8,128)(2,1)S(1)}, bf16[2,640,256]{2,1,0:T(8,128)(2,1)S(1)}, u32[]{:S(2)}, u32[]{:S(2)}) collective-permute-start(bf16[2,640,256]{2,1,0:T(8,128)(2,1)S(1)} %get-tuple-element.69), channel_id=1, source_target_pairs={{0,0},{1,8},{4,4},{5,12},{8,1},{9,9},{12,5},{13,13},{2,2},{3,10},{... | collective-permute-start | bytes 1966088 | tf_op jit(solution)/shard_map/ppermute | solution.py:347
  49.7 21.3 %collective-permute-start.17 = (bf16[2,640,256]{2,1,0:T(8,128)(2,1)S(1)}, bf16[2,640,256]{2,1,0:T(8,128)(2,1)S(1)}, u32[]{:S(2)}, u32[]{:S(2)}) collective-permute-start(bf16[2,640,256]{2,1,0:T(8,128)(2,1)S(1)} %get-tuple-element.74), channel_id=1, source_target_pairs={{0,4},{1,12},{4,0},{5,8},{8,5},{9,13},{12,1},{13,9},{2,6},{3,14},{... | collective-permute-start | bytes 1966088 | tf_op jit(solution)/shard_map/ppermute | solution.py:347
  54.8 7.8 %collective-permute-start.15 = (bf16[640,256]{1,0:T(8,128)(2,1)S(1)}, bf16[640,256]{1,0:T(8,128)(2,1)S(1)}, u32[]{:S(2)}, u32[]{:S(2)}) collective-permute-start(bf16[640,256]{1,0:T(8,128)(2,1)S(1)} %collective-permute-done.13.refs_5_), channel_id=1, source_target_pairs={{0,16},{16,0},{1,17},{17,1},{2,18},{18,2},{3,19},{19,3},{4,20},{20... | collective-permute-start | bytes 983048 | tf_op jit(solution)/shard_map/ppermute | solution.py:314
  56.5 7.5 %collective-permute-start.14 = (bf16[640,256]{1,0:T(8,128)(2,1)S(1)}, bf16[640,256]{1,0:T(8,128)(2,1)S(1)}, u32[]{:S(2)}, u32[]{:S(2)}) collective-permute-start(bf16[640,256]{1,0:T(8,128)(2,1)S(1)} %collective-permute-done.11.p2), channel_id=1, source_target_pairs={{0,2},{2,0},{1,3},{3,1},{4,6},{6,4},{5,7},{7,5},{8,10},{10,8},{9,1... | collective-permute-start | bytes 983048 | tf_op jit(solution)/shard_map/ppermute | solution.py:314
  58.7 5.3 %copy-start.2 = (bf16[256,1280]{1,0:T(8,128)(2,1)S(1)}, bf16[256,1280]{1,0:T(8,128)(2,1)}, u32[]{:S(2)}) copy-start(bf16[256,1280]{1,0:T(8,128)(2,1)} %queries_ref.1) | copy-start | bytes 1966084
  71.0 8.6 %collective-permute-start.18 = (bf16[256,512]{1,0:T(8,128)(2,1)S(1)}, bf16[256,512]{1,0:T(8,128)(2,1)S(1)}, u32[]{:S(2)}, u32[]{:S(2)}) collective-permute-start(bf16[256,512]{1,0:T(8,128)(2,1)S(1)} %get-tuple-element.78.refs_12_), channel_id=1, source_target_pairs={{0,4},{4,8},{8,12},{12,0},{1,5},{5,9},{9,13},{13,1},{2,6},{6,10},{... | collective-permute-start | bytes 786440 | tf_op jit(solution)/shard_map/ppermute | solution.py:319
  71.0 8.6 %collective-permute-start.19 = (bf16[256,512]{1,0:T(8,128)(2,1)S(1)}, bf16[256,512]{1,0:T(8,128)(2,1)S(1)}, u32[]{:S(2)}, u32[]{:S(2)}) collective-permute-start(bf16[256,512]{1,0:T(8,128)(2,1)S(1)} %get-tuple-element.78.refs_12_), channel_id=1, source_target_pairs={{0,2},{2,0},{1,3},{3,1},{4,6},{6,4},{5,7},{7,5},{8,10},{10,8},{9,1... | collective-permute-start | bytes 786440 | tf_op jit(solution)/shard_map/ppermute | solution.py:314
  79.6 16.2 %collective-permute-start.21 = (bf16[256,512]{1,0:T(8,128)(2,1)S(1)}, bf16[256,512]{1,0:T(8,128)(2,1)S(1)}, u32[]{:S(2)}, u32[]{:S(2)}) collective-permute-start(bf16[256,512]{1,0:T(8,128)(2,1)S(1)} %get-tuple-element.78.refs_12_), channel_id=1, source_target_pairs={{0,12},{4,0},{8,4},{12,8},{1,13},{5,1},{9,5},{13,9},{2,14},{6,2},{... | collective-permute-start | bytes 786440 | tf_op jit(solution)/shard_map/ppermute | solution.py:319
  86.6 9.2 %collective-permute-start.22 = (bf16[256,512]{1,0:T(8,128)(2,1)S(1)}, bf16[256,512]{1,0:T(8,128)(2,1)S(1)}, u32[]{:S(2)}, u32[]{:S(2)}) collective-permute-start(bf16[256,512]{1,0:T(8,128)(2,1)S(1)} %collective-permute-done.18.refs_14_), channel_id=1, source_target_pairs={{0,2},{2,0},{1,3},{3,1},{4,6},{6,4},{5,7},{7,5},{8,10},{10,8},{9,1... | collective-permute-start | bytes 786440 | tf_op jit(solution)/shard_map/ppermute | solution.py:314
  88.3 18.1 %collective-permute-start.20 = (bf16[2,640,256]{2,1,0:T(8,128)(2,1)S(1)}, bf16[2,640,256]{2,1,0:T(8,128)(2,1)S(1)}, u32[]{:S(2)}, u32[]{:S(2)}) collective-permute-start(bf16[2,640,256]{2,1,0:T(8,128)(2,1)S(1)} %collective-permute-done.16.refs_0_.refs_1_), channel_id=1, source_target_pairs={{0,1},{1,0},{2,3},{3,2},{4,5},{5,4},{6,7},{7,6},{8,9},{9,8},{10,11... | collective-permute-start | bytes 1966088 | tf_op jit(solution)/shard_map/ppermute | solution.py:314
  88.3 18.1 %collective-permute-start.26 = (bf16[2,640,256]{2,1,0:T(8,128)(2,1)S(1)}, bf16[2,640,256]{2,1,0:T(8,128)(2,1)S(1)}, u32[]{:S(2)}, u32[]{:S(2)}) collective-permute-start(bf16[2,640,256]{2,1,0:T(8,128)(2,1)S(1)} %collective-permute-done.17.refs_2_.refs_3_.refs_4_.refs_5_), channel_id=1, source_target_pairs={{0,1},{1,0},{2,3},{3,2},{4,5},{5,4},{6,7},{7,6},{8,9},{9,8},{10,11... | collective-permute-start | bytes 1966088 | tf_op jit(solution)/shard_map/ppermute | solution.py:314
  95.8 8.9 %collective-permute-start.23 = (bf16[256,512]{1,0:T(8,128)(2,1)S(1)}, bf16[256,512]{1,0:T(8,128)(2,1)S(1)}, u32[]{:S(2)}, u32[]{:S(2)}) collective-permute-start(bf16[256,512]{1,0:T(8,128)(2,1)S(1)} %collective-permute-done.18.refs_14_), channel_id=1, source_target_pairs={{0,4},{4,8},{8,12},{12,0},{1,5},{5,9},{9,13},{13,1},{2,6},{6,10},{... | collective-permute-start | bytes 786440 | tf_op jit(solution)/shard_map/ppermute | solution.py:319
  97.6 7.1 %collective-permute-start.24 = (bf16[256,512]{1,0:T(8,128)(2,1)S(1)}, bf16[256,512]{1,0:T(8,128)(2,1)S(1)}, u32[]{:S(2)}, u32[]{:S(2)}) collective-permute-start(bf16[256,512]{1,0:T(8,128)(2,1)S(1)} %collective-permute-done.21.refs_15_), channel_id=1, source_target_pairs={{0,2},{2,0},{1,3},{3,1},{4,6},{6,4},{5,7},{7,5},{8,10},{10,8},{9,1... | collective-permute-start | bytes 786440 | tf_op jit(solution)/shard_map/ppermute | solution.py:314
  104.7 6.4 %collective-permute-start.25 = (bf16[256,512]{1,0:T(8,128)(2,1)S(1)}, bf16[256,512]{1,0:T(8,128)(2,1)S(1)}, u32[]{:S(2)}, u32[]{:S(2)}) collective-permute-start(bf16[256,512]{1,0:T(8,128)(2,1)S(1)} %collective-permute-done.23.refs_4_), channel_id=1, source_target_pairs={{0,2},{2,0},{1,3},{3,1},{4,6},{6,4},{5,7},{7,5},{8,10},{10,8},{9,1... | collective-permute-start | bytes 786440 | tf_op jit(solution)/shard_map/ppermute | solution.py:314
  (1 other events, 5.3 us)

commit v22 on v20

--- a/solution.py
+++ b/solution.py
@@ -395,11 +395,11 @@
     twice_y, up_both = swapped(twice, "groups"), swapped(up_x, "groups")
     even, odd = pack(kept, early, late)
     even = sent_along(even, 0)
+    odd = sent_along(after(odd, twice_y), 1)
     twice_x, twice_y, up_both, down_x, even = lax.optimization_barrier(
         (twice_x, twice_y, up_both, down_x, even)
     )
     down_both, twice_both = swapped(down_x, "groups"), swapped(twice_y, "dp")
-    odd = sent_along(after(odd, even), 1)
 
     gathered = [(1, (up, up_x, up_y, up_both)), (-1, (down, down_x, down_y, down_both))]
     sums = project(normed, normed_other, kv_weight, gathered)

time: 110 us -> 110 us (level)
  waiting for transfers between devices: 69 us -> 63.6 us
  starting transfers between devices: 25.1 us -> 30.2 us
    ppermute x19, starting transfers between devices: 15.2 us -> 20.2 us  [swapped(): return lax.ppermute(block, axis, [(0, 1), (1, 0)])]
    ppermute x2, waiting for transfers between devices: 2.54 us -> 0.01 us  [sent_along(): return lax.ppermute(slabs, ('blk', 'sub'), route)]
    ppermute x19, waiting for transfers between devices: 40.5 us -> 38.6 us  [swapped(): return lax.ppermute(block, axis, [(0, 1), (1, 0)])]
  transfers between devices with their start and end apart: 27 -> 27, of which waited for: 17 -> 16; matrix products, arithmetic and copies ran while one was open for 2% -> 2% of each run, Pallas kernels for 8% -> 8%
where the time goes in v22:
time: 110 us; the launch traced here: 109 us
  waiting for transfers between devices  63.6 us (58%)
  starting transfers between devices  30.2 us (27%)
  Pallas kernels  11 us (10%)
  other arithmetic  2.4 us (2%)
  local copies, waits for them, and re-layouts  1.3 us (1%)
    ppermute x19, waiting for transfers between devices, swapped(): return lax.ppermute(block, axis, [(0, 1), (1, 0)])  38.6 us
    ppermute x6, waiting for transfers between devices, turned(): lax.ppermute(block, axis, [(i, (i + distance) % size) for i in range(size)])  25.1 us
    ppermute x19, starting transfers between devices, swapped(): return lax.ppermute(block, axis, [(0, 1), (1, 0)])  20.2 us
    ppermute x6, starting transfers between devices, turned(): lax.ppermute(block, axis, [(i, (i + distance) % size) for i in range(size)])  9.25 us
    pallas_call x1, Pallas kernels, attention(): pl.pallas_call(functools.partial(attention_kernel, distance), in_specs=[I...  5.07 us
    pallas_call x2, Pallas kernels, gradient(): pl.pallas_call(functools.partial(gradient_kernel, tuple(some), sums is No...  3.47 us
  transfers between devices with their start and end apart: 27, of which 16 were waited for; matrix products, arithmetic and copies ran while one was open for 2% of the time, Pallas kernels for 8%

profile of v22, /device:TPU:0, one launch (start us, length us, event | category | flops | bytes accessed | tf_op | source)
XLA Modules:
  0.0 109.3 jit_solution(13118349415812795569)
XLA Ops:
  1.8 3.1 %collective-permute-start = (bf16[640,256]{1,0:T(8,128)(2,1)S(1)}, bf16[640,256]{1,0:T(8,128)(2,1)S(1)}, u32[]{:S(2)}, u32[]{:S(2)}) collective-permute-start(bf16[640,256]{1,0:T(8,128)(2,1)S(1)} %dynamic-slice_bitcast_fusion), channel_id=1, source_target_pairs={{0,4},{4,8},{8,12},{12,0},{1,5},{5,9},{9,13},{13,1},{2,6},{6,10},{... | collective-permute-start | bytes 983048 | tf_op jit(solution)/shard_map/ppermute | solution.py:319
  4.8 1.7 %multiply_reduce_fusion = f32[256]{0:T(256)S(1)} fusion(bf16[256,2560]{1,0:T(8,128)(2,1)} %values_ref.1), kind=kLoop, calls=%fused_computation | loop fusion | flops 1965824 | bytes 1311744 | tf_op jit(solution)/shard_map/reduce_sum | solution.py:354
  8.8 1.6 %collective-permute-start.2 = (bf16[320,256]{1,0:T(8,128)(2,1)S(1)}, bf16[320,256]{1,0:T(8,128)(2,1)S(1)}, u32[]{:S(2)}, u32[]{:S(2)}) collective-permute-start(bf16[320,256]{1,0:T(8,128)(2,1)S(1)} %get-tuple-element.48), channel_id=1, source_target_pairs={{0,2},{2,0},{1,3},{3,1},{4,6},{6,4},{5,7},{7,5},{8,10},{10,8},{9,1... | collective-permute-start | bytes 491528 | tf_op jit(solution)/shard_map/ppermute | solution.py:314
  10.4 4.8 %collective-permute-done.2.early_ref = bf16[320,256]{1,0:T(8,128)(2,1)S(1)} collective-permute-done((bf16[320,256]{1,0:T(8,128)(2,1)S(1)}, bf16[320,256]{1,0:T(8,128)(2,1)S(1)}, u32[]{:S(2)}, u32[]{:S(2)}) %collective-permute-start.2) | collective-permute-done | bytes 163872 | tf_op jit(solution)/shard_map/ppermute | solution.py:314
  15.2 1.5 %collective-permute-start.3 = (bf16[640,256]{1,0:T(8,128)(2,1)S(1)}, bf16[640,256]{1,0:T(8,128)(2,1)S(1)}, u32[]{:S(2)}, u32[]{:S(2)}) collective-permute-start(bf16[640,256]{1,0:T(8,128)(2,1)S(1)} %collective-permute-done.refs_0_), channel_id=1, source_target_pairs={{0,16},{16,0},{1,17},{17,1},{2,18},{18,2},{3,19},{19,3},{4,20},{20... | collective-permute-start | bytes 983048 | tf_op jit(solution)/shard_map/ppermute | solution.py:314
  16.7 2.2 %collective-permute-start.4 = (bf16[640,256]{1,0:T(8,128)(2,1)S(1)}, bf16[640,256]{1,0:T(8,128)(2,1)S(1)}, u32[]{:S(2)}, u32[]{:S(2)}) collective-permute-start(bf16[640,256]{1,0:T(8,128)(2,1)S(1)} %dynamic-slice_bitcast_fusion), channel_id=1, source_target_pairs={{0,12},{4,0},{8,4},{12,8},{1,13},{5,1},{9,5},{13,9},{2,14},{6,2},{... | collective-permute-start | bytes 983048 | tf_op jit(solution)/shard_map/ppermute | solution.py:319
  19.0 1.5 %collective-permute-start.9 = (bf16[960,256]{1,0:T(8,128)(2,1)S(1)}, bf16[960,256]{1,0:T(8,128)(2,1)S(1)}, u32[]{:S(2)}, u32[]{:S(2)}) collective-permute-start(bf16[960,256]{1,0:T(8,128)(2,1)S(1)} %get-tuple-element.56), channel_id=1, source_target_pairs={{0,2},{2,0},{1,3},{3,1},{4,6},{6,4},{5,7},{7,5},{8,10},{10,8},{9,1... | collective-permute-start | bytes 1474568 | tf_op jit(solution)/shard_map/ppermute | solution.py:314
  20.5 4.9 %collective-permute-done.3.refs_2_ = bf16[640,256]{1,0:T(8,128)(2,1)S(1)} collective-permute-done((bf16[640,256]{1,0:T(8,128)(2,1)S(1)}, bf16[640,256]{1,0:T(8,128)(2,1)S(1)}, u32[]{:S(2)}, u32[]{:S(2)}) %collective-permute-start.3) | collective-permute-done | bytes 327712 | tf_op jit(solution)/shard_map/ppermute | solution.py:314
  26.6 1.6 %collective-permute-start.6 = (bf16[640,256]{1,0:T(8,128)(2,1)S(1)}, bf16[640,256]{1,0:T(8,128)(2,1)S(1)}, u32[]{:S(2)}, u32[]{:S(2)}) collective-permute-start(bf16[640,256]{1,0:T(8,128)(2,1)S(1)} %collective-permute-done.refs_0_), channel_id=1, source_target_pairs={{0,4},{4,8},{8,12},{12,0},{1,5},{5,9},{9,13},{13,1},{2,6},{6,10},{... | collective-permute-start | bytes 983048 | tf_op jit(solution)/shard_map/ppermute | solution.py:319
  28.7 1.5 %collective-permute-start.8 = (bf16[640,256]{1,0:T(8,128)(2,1)S(1)}, bf16[640,256]{1,0:T(8,128)(2,1)S(1)}, u32[]{:S(2)}, u32[]{:S(2)}) collective-permute-start(bf16[640,256]{1,0:T(8,128)(2,1)S(1)} %collective-permute-done.refs_0_), channel_id=1, source_target_pairs={{0,2},{2,0},{1,3},{3,1},{4,6},{6,4},{5,7},{7,5},{8,10},{10,8},{9,1... | collective-permute-start | bytes 983048 | tf_op jit(solution)/shard_map/ppermute | solution.py:314
  30.1 2.9 %collective-permute-done.9.late_ref = bf16[960,256]{1,0:T(8,128)(2,1)S(1)} collective-permute-done((bf16[960,256]{1,0:T(8,128)(2,1)S(1)}, bf16[960,256]{1,0:T(8,128)(2,1)S(1)}, u32[]{:S(2)}, u32[]{:S(2)}) %collective-permute-start.9) | collective-permute-done | bytes 491552 | tf_op jit(solution)/shard_map/ppermute | solution.py:314
  33.1 4.8 %collective-permute-done.6.p0 = bf16[640,256]{1,0:T(8,128)(2,1)S(1)} collective-permute-done((bf16[640,256]{1,0:T(8,128)(2,1)S(1)}, bf16[640,256]{1,0:T(8,128)(2,1)S(1)}, u32[]{:S(2)}, u32[]{:S(2)}) %collective-permute-start.6) | collective-permute-done | bytes 327712 | tf_op jit(solution)/shard_map/ppermute | solution.py:319
  40.3 1.7 %collective-permute-start.10 = (bf16[640,256]{1,0:T(8,128)(2,1)S(1)}, bf16[640,256]{1,0:T(8,128)(2,1)S(1)}, u32[]{:S(2)}, u32[]{:S(2)}) collective-permute-start(bf16[640,256]{1,0:T(8,128)(2,1)S(1)} %collective-permute-done.6.p0), channel_id=1, source_target_pairs={{0,2},{2,0},{1,3},{3,1},{4,6},{6,4},{5,7},{7,5},{8,10},{10,8},{9,1... | collective-permute-start | bytes 983048 | tf_op jit(solution)/shard_map/ppermute | solution.py:314
  42.0 1.5 %collective-permute-start.12 = (bf16[640,256]{1,0:T(8,128)(2,1)S(1)}, bf16[640,256]{1,0:T(8,128)(2,1)S(1)}, u32[]{:S(2)}, u32[]{:S(2)}) collective-permute-start(bf16[640,256]{1,0:T(8,128)(2,1)S(1)} %collective-permute-done.8.refs_1_), channel_id=1, source_target_pairs={{0,16},{16,0},{1,17},{17,1},{2,18},{18,2},{3,19},{19,3},{4,20},{20... | collective-permute-start | bytes 983048 | tf_op jit(solution)/shard_map/ppermute | solution.py:314
  44.0 5.3 %collective-permute-done.11.p2 = bf16[640,256]{1,0:T(8,128)(2,1)S(1)} collective-permute-done((bf16[640,256]{1,0:T(8,128)(2,1)S(1)}, bf16[640,256]{1,0:T(8,128)(2,1)S(1)}, u32[]{:S(2)}, u32[]{:S(2)}) %collective-permute-start.11) | collective-permute-done | bytes 327712 | tf_op jit(solution)/shard_map/ppermute | solution.py:314
  49.3 7.0 %collective-permute-done.12.refs_3_ = bf16[640,256]{1,0:T(8,128)(2,1)S(1)} collective-permute-done((bf16[640,256]{1,0:T(8,128)(2,1)S(1)}, bf16[640,256]{1,0:T(8,128)(2,1)S(1)}, u32[]{:S(2)}, u32[]{:S(2)}) %collective-permute-start.12) | collective-permute-done | bytes 327712 | tf_op jit(solution)/shard_map/ppermute | solution.py:314
  56.3 2.3 %collective-permute-start.16 = (bf16[640,256]{1,0:T(8,128)(2,1)S(1)}, bf16[640,256]{1,0:T(8,128)(2,1)S(1)}, u32[]{:S(2)}, u32[]{:S(2)}) collective-permute-start(bf16[640,256]{1,0:T(8,128)(2,1)S(1)} %collective-permute-done.13.refs_5_), channel_id=1, source_target_pairs={{0,16},{16,0},{1,17},{17,1},{2,18},{18,2},{3,19},{19,3},{4,20},{20... | collective-permute-start | bytes 983048 | tf_op jit(solution)/shard_map/ppermute | solution.py:314
  58.6 1.3 %collective-permute-start.15 = (bf16[640,256]{1,0:T(8,128)(2,1)S(1)}, bf16[640,256]{1,0:T(8,128)(2,1)S(1)}, u32[]{:S(2)}, u32[]{:S(2)}) collective-permute-start(bf16[640,256]{1,0:T(8,128)(2,1)S(1)} %collective-permute-done.11.p2), channel_id=1, source_target_pairs={{0,2},{2,0},{1,3},{3,1},{4,6},{6,4},{5,7},{7,5},{8,10},{10,8},{9,1... | collective-permute-start | bytes 983048 | tf_op jit(solution)/shard_map/ppermute | solution.py:314
  60.6 5.8 %collective-permute-done.16.refs_7_ = bf16[640,256]{1,0:T(8,128)(2,1)S(1)} collective-permute-done((bf16[640,256]{1,0:T(8,128)(2,1)S(1)}, bf16[640,256]{1,0:T(8,128)(2,1)S(1)}, u32[]{:S(2)}, u32[]{:S(2)}) %collective-permute-start.16) | collective-permute-done | bytes 327712 | tf_op jit(solution)/shard_map/ppermute | solution.py:314
  66.4 1.4 %project.1.sums_ref = f32[2,256,256]{2,1,0:T(8,128)S(1)} custom-call(bf16[256,2560]{1,0:T(8,128)(2,1)S(1)} %get-tuple-element.50.own_ref, bf16[256,2560]{1,0:T(8,128)(2,1)S(1)} %collective-permute-done.5.other_ref, bf16[2,1280,256]{2,1,0:T(8,128)(2,1)S(1)} %copy-done.1, bf16[640,256]{1,0:T(8,128)(2,1)S(1)} %collective-permute-done.refs_0_, ...), custom_call_target="tpu_custom_call" | custom-call | flops 1006632960 | bytes 7000000 | tf_op jit(solution)/shard_map/project/pallas_call | solution.py:91
  67.8 1.3 %collective-permute-done.15.p3 = bf16[640,256]{1,0:T(8,128)(2,1)S(1)} collective-permute-done((bf16[640,256]{1,0:T(8,128)(2,1)S(1)}, bf16[640,256]{1,0:T(8,128)(2,1)S(1)}, u32[]{:S(2)}, u32[]{:S(2)}) %collective-permute-start.15) | collective-permute-done | bytes 327712 | tf_op jit(solution)/shard_map/ppermute | solution.py:314
  69.2 5.1 %attention.1 = (bf16[256,1280]{1,0:T(8,128)(2,1)}, bf16[256,512]{1,0:T(8,128)(2,1)S(1)}) custom-call(bf16[256,2560]{1,0:T(8,128)(2,1)S(1)} %get-tuple-element.50.own_ref, bf16[256,2560]{1,0:T(8,128)(2,1)S(1)} %collective-permute-done.5.other_ref, bf16[640,256]{1,0:T(8,128)(2,1)S(1)} %collective-permute-done.6.p0, ...), custom_call_target="tpu_custom_call" | custom-call | flops 838860800 | bytes 5000000 | tf_op jit(solution)/shard_map/attention/pallas_call | solution.py:165
  75.5 8.8 %collective-permute-done.18.refs_14_ = bf16[256,512]{1,0:T(8,128)(2,1)S(1)} collective-permute-done((bf16[256,512]{1,0:T(8,128)(2,1)S(1)}, bf16[256,512]{1,0:T(8,128)(2,1)S(1)}, u32[]{:S(2)}, u32[]{:S(2)}) %collective-permute-start.18) | collective-permute-done | bytes 262176 | tf_op jit(solution)/shard_map/ppermute | solution.py:319
  84.4 1.7 %collective-permute-start.21 = (bf16[256,512]{1,0:T(8,128)(2,1)S(1)}, bf16[256,512]{1,0:T(8,128)(2,1)S(1)}, u32[]{:S(2)}, u32[]{:S(2)}) collective-permute-start(bf16[256,512]{1,0:T(8,128)(2,1)S(1)} %get-tuple-element.78.refs_12_), channel_id=1, source_target_pairs={{0,12},{4,0},{8,4},{12,8},{1,13},{5,1},{9,5},{13,9},{2,14},{6,2},{... | collective-permute-start | bytes 786440 | tf_op jit(solution)/shard_map/ppermute | solution.py:319
  86.1 1.3 %collective-permute-start.22 = (bf16[256,512]{1,0:T(8,128)(2,1)S(1)}, bf16[256,512]{1,0:T(8,128)(2,1)S(1)}, u32[]{:S(2)}, u32[]{:S(2)}) collective-permute-start(bf16[256,512]{1,0:T(8,128)(2,1)S(1)} %collective-permute-done.18.refs_14_), channel_id=1, source_target_pairs={{0,2},{2,0},{1,3},{3,1},{4,6},{6,4},{5,7},{7,5},{8,10},{10,8},{9,1... | collective-permute-start | bytes 786440 | tf_op jit(solution)/shard_map/ppermute | solution.py:314
  88.0 3.9 %collective-permute-done.21.refs_15_ = bf16[256,512]{1,0:T(8,128)(2,1)S(1)} collective-permute-done((bf16[256,512]{1,0:T(8,128)(2,1)S(1)}, bf16[256,512]{1,0:T(8,128)(2,1)S(1)}, u32[]{:S(2)}, u32[]{:S(2)}) %collective-permute-start.21) | collective-permute-done | bytes 262176 | tf_op jit(solution)/shard_map/ppermute | solution.py:319
  93.7 1.4 %collective-permute-start.24 = (bf16[256,512]{1,0:T(8,128)(2,1)S(1)}, bf16[256,512]{1,0:T(8,128)(2,1)S(1)}, u32[]{:S(2)}, u32[]{:S(2)}) collective-permute-start(bf16[256,512]{1,0:T(8,128)(2,1)S(1)} %collective-permute-done.21.refs_15_), channel_id=1, source_target_pairs={{0,2},{2,0},{1,3},{3,1},{4,6},{6,4},{5,7},{7,5},{8,10},{10,8},{9,1... | collective-permute-start | bytes 786440 | tf_op jit(solution)/shard_map/ppermute | solution.py:314
  95.0 6.2 %collective-permute-done.23.refs_4_ = bf16[256,512]{1,0:T(8,128)(2,1)S(1)} collective-permute-done((bf16[256,512]{1,0:T(8,128)(2,1)S(1)}, bf16[256,512]{1,0:T(8,128)(2,1)S(1)}, u32[]{:S(2)}, u32[]{:S(2)}) %collective-permute-start.23) | collective-permute-done | bytes 262176 | tf_op jit(solution)/shard_map/ppermute | solution.py:319
  101.2 1.4 %collective-permute-start.25 = (bf16[256,512]{1,0:T(8,128)(2,1)S(1)}, bf16[256,512]{1,0:T(8,128)(2,1)S(1)}, u32[]{:S(2)}, u32[]{:S(2)}) collective-permute-start(bf16[256,512]{1,0:T(8,128)(2,1)S(1)} %collective-permute-done.23.refs_4_), channel_id=1, source_target_pairs={{0,2},{2,0},{1,3},{3,1},{4,6},{6,4},{5,7},{7,5},{8,10},{10,8},{9,1... | collective-permute-start | bytes 786440 | tf_op jit(solution)/shard_map/ppermute | solution.py:314
  102.6 1.7 %gradient.2 = (f32[2,640,256]{2,1,0:T(8,128)S(1)}, f32[2,256]{1,0:T(2,128)S(1)}) custom-call(bf16[2,640,256]{2,1,0:T(8,128)(2,1)S(1)} %collective-permute-done.14.refs_0_.refs_1_, bf16[2,640,256]{2,1,0:T(8,128)(2,1)S(1)} %collective-permute-done.14.refs_0_.refs_1_, bf16[2,640,256]{2,1,0:T(8,128)(2,1)S(1)} %collective-permute-done.17.refs_2_.refs_3_.refs_4_.refs_5_, ...), custom_call_target="tpu_custom_call" | custom-call | flops 1006632960 | bytes 5000000 | tf_op jit(solution)/shard_map/gradient/pallas_call | solution.py:230
  104.3 3.3 %collective-permute-done.25.refs_5_ = bf16[256,512]{1,0:T(8,128)(2,1)S(1)} collective-permute-done((bf16[256,512]{1,0:T(8,128)(2,1)S(1)}, bf16[256,512]{1,0:T(8,128)(2,1)S(1)}, u32[]{:S(2)}, u32[]{:S(2)}) %collective-permute-start.25) | collective-permute-done | bytes 262176 | tf_op jit(solution)/shard_map/ppermute | solution.py:314
  107.6 1.7 %gradient.3 = (f32[2,640,256]{2,1,0:T(8,128)}, f32[2,256]{1,0:T(2,128)}) custom-call(bf16[2,640,256]{2,1,0:T(8,128)(2,1)S(1)} %collective-permute-done.14.refs_0_.refs_1_, bf16[2,640,256]{2,1,0:T(8,128)(2,1)S(1)} %collective-permute-done.14.refs_0_.refs_1_, bf16[2,640,256]{2,1,0:T(8,128)(2,1)S(1)} %collective-permute-done.20.refs_6_.refs_7_.refs_2_.refs_3_, ...), custom_call_target="tpu_custom_call" | custom-call | flops 335544320 | bytes 5000000 | tf_op jit(solution)/shard_map/gradient/pallas_call | solution.py:230
  (51 shorter events, 12.3 us)
Async XLA Ops:
  0.6 7.2 %copy-start = (bf16[256,2560]{1,0:T(8,128)(2,1)S(1)}, bf16[256,2560]{1,0:T(8,128)(2,1)}, u32[]{:S(2)}) copy-start(bf16[256,2560]{1,0:T(8,128)(2,1)} %values_ref.1) | copy-start | bytes 3932164
  1.8 13.4 %collective-permute-start = (bf16[640,256]{1,0:T(8,128)(2,1)S(1)}, bf16[640,256]{1,0:T(8,128)(2,1)S(1)}, u32[]{:S(2)}, u32[]{:S(2)}) collective-permute-start(bf16[640,256]{1,0:T(8,128)(2,1)S(1)} %dynamic-slice_bitcast_fusion), channel_id=1, source_target_pairs={{0,4},{4,8},{8,12},{12,0},{1,5},{5,9},{9,13},{13,1},{2,6},{6,10},{... | collective-permute-start | bytes 983048 | tf_op jit(solution)/shard_map/ppermute | solution.py:319
  6.5 1.2 %collective-permute-start.1 = (f32[256,1]{0,1:T(1,128)S(1)}, f32[256,1]{0,1:T(1,128)S(1)}, u32[]{:S(2)}, u32[]{:S(2)}) collective-permute-start(f32[256,1]{0,1:T(1,128)S(1)} %bitcast.3), channel_id=1, source_target_pairs={{0,1},{1,0},{2,3},{3,2},{4,5},{5,4},{6,7},{7,6},{8,9},{9,8},{10,11... | collective-permute-start | bytes 3080 | tf_op jit(solution)/shard_map/ppermute | solution.py:314
  7.9 52.5 %copy-start.5 = (bf16[2,256]{1,0:T(2,128)(2,1)S(1)}, bf16[2,256]{1,0:T(2,128)(2,1)}, u32[]{:S(2)}) copy-start(bf16[2,256]{1,0:T(2,128)(2,1)} %param.11) | copy-start | bytes 3076
  8.8 57.6 %copy-start.1 = (bf16[2,1280,256]{2,1,0:T(8,128)(2,1)S(1)}, bf16[2,1280,256]{2,1,0:T(8,128)(2,1)}, u32[]{:S(2)}) copy-start(bf16[2,1280,256]{2,1,0:T(8,128)(2,1)} %weight_ref.1) | copy-start | bytes 3932164
  8.8 6.4 %collective-permute-start.2 = (bf16[320,256]{1,0:T(8,128)(2,1)S(1)}, bf16[320,256]{1,0:T(8,128)(2,1)S(1)}, u32[]{:S(2)}, u32[]{:S(2)}) collective-permute-start(bf16[320,256]{1,0:T(8,128)(2,1)S(1)} %get-tuple-element.48), channel_id=1, source_target_pairs={{0,2},{2,0},{1,3},{3,1},{4,6},{6,4},{5,7},{7,5},{8,10},{10,8},{9,1... | collective-permute-start | bytes 491528 | tf_op jit(solution)/shard_map/ppermute | solution.py:314
  15.2 11.4 %collective-permute-start.5 = (bf16[256,2560]{1,0:T(8,128)(2,1)S(1)}, bf16[256,2560]{1,0:T(8,128)(2,1)S(1)}, u32[]{:S(2)}, u32[]{:S(2)}) collective-permute-start(bf16[256,2560]{1,0:T(8,128)(2,1)S(1)} %get-tuple-element.50.own_ref), channel_id=1, source_target_pairs={{0,1},{1,0},{2,3},{3,2},{4,5},{5,4},{6,7},{7,6},{8,9},{9,8},{10,11... | collective-permute-start | bytes 3932168 | tf_op jit(solution)/shard_map/ppermute | solution.py:314
  15.2 10.1 %collective-permute-start.3 = (bf16[640,256]{1,0:T(8,128)(2,1)S(1)}, bf16[640,256]{1,0:T(8,128)(2,1)S(1)}, u32[]{:S(2)}, u32[]{:S(2)}) collective-permute-start(bf16[640,256]{1,0:T(8,128)(2,1)S(1)} %collective-permute-done.refs_0_), channel_id=1, source_target_pairs={{0,16},{16,0},{1,17},{17,1},{2,18},{18,2},{3,19},{19,3},{4,20},{20... | collective-permute-start | bytes 983048 | tf_op jit(solution)/shard_map/ppermute | solution.py:314
  16.7 9.8 %collective-permute-start.4 = (bf16[640,256]{1,0:T(8,128)(2,1)S(1)}, bf16[640,256]{1,0:T(8,128)(2,1)S(1)}, u32[]{:S(2)}, u32[]{:S(2)}) collective-permute-start(bf16[640,256]{1,0:T(8,128)(2,1)S(1)} %dynamic-slice_bitcast_fusion), channel_id=1, source_target_pairs={{0,12},{4,0},{8,4},{12,8},{1,13},{5,1},{9,5},{13,9},{2,14},{6,2},{... | collective-permute-start | bytes 983048 | tf_op jit(solution)/shard_map/ppermute | solution.py:319
  19.0 14.1 %collective-permute-start.9 = (bf16[960,256]{1,0:T(8,128)(2,1)S(1)}, bf16[960,256]{1,0:T(8,128)(2,1)S(1)}, u32[]{:S(2)}, u32[]{:S(2)}) collective-permute-start(bf16[960,256]{1,0:T(8,128)(2,1)S(1)} %get-tuple-element.56), channel_id=1, source_target_pairs={{0,2},{2,0},{1,3},{3,1},{4,6},{6,4},{5,7},{7,5},{8,10},{10,8},{9,1... | collective-permute-start | bytes 1474568 | tf_op jit(solution)/shard_map/ppermute | solution.py:314
  26.6 11.3 %collective-permute-start.6 = (bf16[640,256]{1,0:T(8,128)(2,1)S(1)}, bf16[640,256]{1,0:T(8,128)(2,1)S(1)}, u32[]{:S(2)}, u32[]{:S(2)}) collective-permute-start(bf16[640,256]{1,0:T(8,128)(2,1)S(1)} %collective-permute-done.refs_0_), channel_id=1, source_target_pairs={{0,4},{4,8},{8,12},{12,0},{1,5},{5,9},{9,13},{13,1},{2,6},{6,10},{... | collective-permute-start | bytes 983048 | tf_op jit(solution)/shard_map/ppermute | solution.py:319
  28.1 9.8 %collective-permute-start.7 = (bf16[640,256]{1,0:T(8,128)(2,1)S(1)}, bf16[640,256]{1,0:T(8,128)(2,1)S(1)}, u32[]{:S(2)}, u32[]{:S(2)}) collective-permute-start(bf16[640,256]{1,0:T(8,128)(2,1)S(1)} %collective-permute-done.4.refs_4_), channel_id=1, source_target_pairs={{0,16},{16,0},{1,17},{17,1},{2,18},{18,2},{3,19},{19,3},{4,20},{20... | collective-permute-start | bytes 983048 | tf_op jit(solution)/shard_map/ppermute | solution.py:314
  28.7 10.4 %collective-permute-start.8 = (bf16[640,256]{1,0:T(8,128)(2,1)S(1)}, bf16[640,256]{1,0:T(8,128)(2,1)S(1)}, u32[]{:S(2)}, u32[]{:S(2)}) collective-permute-start(bf16[640,256]{1,0:T(8,128)(2,1)S(1)} %collective-permute-done.refs_0_), channel_id=1, source_target_pairs={{0,2},{2,0},{1,3},{3,1},{4,6},{6,4},{5,7},{7,5},{8,10},{10,8},{9,1... | collective-permute-start | bytes 983048 | tf_op jit(solution)/shard_map/ppermute | solution.py:314
  39.2 17.1 %collective-permute-start.14 = (bf16[2,640,256]{2,1,0:T(8,128)(2,1)S(1)}, bf16[2,640,256]{2,1,0:T(8,128)(2,1)S(1)}, u32[]{:S(2)}, u32[]{:S(2)}) collective-permute-start(bf16[2,640,256]{2,1,0:T(8,128)(2,1)S(1)} %get-tuple-element.63), channel_id=1, source_target_pairs={{0,0},{1,8},{4,4},{5,12},{8,1},{9,9},{12,5},{13,13},{2,2},{3,10},{... | collective-permute-start | bytes 1966088 | tf_op jit(solution)/shard_map/ppermute | solution.py:347
  39.9 9.4 %collective-permute-start.11 = (bf16[640,256]{1,0:T(8,128)(2,1)S(1)}, bf16[640,256]{1,0:T(8,128)(2,1)S(1)}, u32[]{:S(2)}, u32[]{:S(2)}) collective-permute-start(bf16[640,256]{1,0:T(8,128)(2,1)S(1)} %collective-permute-done.6.p0), channel_id=1, source_target_pairs={{0,16},{16,0},{1,17},{17,1},{2,18},{18,2},{3,19},{19,3},{4,20},{20... | collective-permute-start | bytes 983048 | tf_op jit(solution)/shard_map/ppermute | solution.py:314
  40.3 9.0 %collective-permute-start.10 = (bf16[640,256]{1,0:T(8,128)(2,1)S(1)}, bf16[640,256]{1,0:T(8,128)(2,1)S(1)}, u32[]{:S(2)}, u32[]{:S(2)}) collective-permute-start(bf16[640,256]{1,0:T(8,128)(2,1)S(1)} %collective-permute-done.6.p0), channel_id=1, source_target_pairs={{0,2},{2,0},{1,3},{3,1},{4,6},{6,4},{5,7},{7,5},{8,10},{10,8},{9,1... | collective-permute-start | bytes 983048 | tf_op jit(solution)/shard_map/ppermute | solution.py:314
  42.0 14.4 %collective-permute-start.12 = (bf16[640,256]{1,0:T(8,128)(2,1)S(1)}, bf16[640,256]{1,0:T(8,128)(2,1)S(1)}, u32[]{:S(2)}, u32[]{:S(2)}) collective-permute-start(bf16[640,256]{1,0:T(8,128)(2,1)S(1)} %collective-permute-done.8.refs_1_), channel_id=1, source_target_pairs={{0,16},{16,0},{1,17},{17,1},{2,18},{18,2},{3,19},{19,3},{4,20},{20... | collective-permute-start | bytes 983048 | tf_op jit(solution)/shard_map/ppermute | solution.py:314
  43.5 12.8 %collective-permute-start.13 = (bf16[640,256]{1,0:T(8,128)(2,1)S(1)}, bf16[640,256]{1,0:T(8,128)(2,1)S(1)}, u32[]{:S(2)}, u32[]{:S(2)}) collective-permute-start(bf16[640,256]{1,0:T(8,128)(2,1)S(1)} %collective-permute-done.4.refs_4_), channel_id=1, source_target_pairs={{0,2},{2,0},{1,3},{3,1},{4,6},{6,4},{5,7},{7,5},{8,10},{10,8},{9,1... | collective-permute-start | bytes 983048 | tf_op jit(solution)/shard_map/ppermute | solution.py:314
  49.3 24.9 %collective-permute-start.17 = (bf16[2,640,256]{2,1,0:T(8,128)(2,1)S(1)}, bf16[2,640,256]{2,1,0:T(8,128)(2,1)S(1)}, u32[]{:S(2)}, u32[]{:S(2)}) collective-permute-start(bf16[2,640,256]{2,1,0:T(8,128)(2,1)S(1)} %get-tuple-element.73), channel_id=1, source_target_pairs={{0,4},{1,12},{4,0},{5,8},{8,5},{9,13},{12,1},{13,9},{2,6},{3,14},{... | collective-permute-start | bytes 1966088 | tf_op jit(solution)/shard_map/ppermute | solution.py:347
  56.3 10.1 %collective-permute-start.16 = (bf16[640,256]{1,0:T(8,128)(2,1)S(1)}, bf16[640,256]{1,0:T(8,128)(2,1)S(1)}, u32[]{:S(2)}, u32[]{:S(2)}) collective-permute-start(bf16[640,256]{1,0:T(8,128)(2,1)S(1)} %collective-permute-done.13.refs_5_), channel_id=1, source_target_pairs={{0,16},{16,0},{1,17},{17,1},{2,18},{18,2},{3,19},{19,3},{4,20},{20... | collective-permute-start | bytes 983048 | tf_op jit(solution)/shard_map/ppermute | solution.py:314
  58.6 10.6 %collective-permute-start.15 = (bf16[640,256]{1,0:T(8,128)(2,1)S(1)}, bf16[640,256]{1,0:T(8,128)(2,1)S(1)}, u32[]{:S(2)}, u32[]{:S(2)}) collective-permute-start(bf16[640,256]{1,0:T(8,128)(2,1)S(1)} %collective-permute-done.11.p2), channel_id=1, source_target_pairs={{0,2},{2,0},{1,3},{3,1},{4,6},{6,4},{5,7},{7,5},{8,10},{10,8},{9,1... | collective-permute-start | bytes 983048 | tf_op jit(solution)/shard_map/ppermute | solution.py:314
  60.6 8.6 %copy-start.2 = (bf16[256,1280]{1,0:T(8,128)(2,1)S(1)}, bf16[256,1280]{1,0:T(8,128)(2,1)}, u32[]{:S(2)}) copy-start(bf16[256,1280]{1,0:T(8,128)(2,1)} %queries_ref.1) | copy-start | bytes 1966084
  60.6 8.6 %copy-start.3 = (bf16[256,1280]{1,0:T(8,128)(2,1)S(1)}, bf16[256,1280]{1,0:T(8,128)(2,1)}, u32[]{:S(2)}) copy-start(bf16[256,1280]{1,0:T(8,128)(2,1)} %cotangent_ref.1) | copy-start | bytes 1966084
  74.2 10.1 %collective-permute-start.18 = (bf16[256,512]{1,0:T(8,128)(2,1)S(1)}, bf16[256,512]{1,0:T(8,128)(2,1)S(1)}, u32[]{:S(2)}, u32[]{:S(2)}) collective-permute-start(bf16[256,512]{1,0:T(8,128)(2,1)S(1)} %get-tuple-element.78.refs_12_), channel_id=1, source_target_pairs={{0,4},{4,8},{8,12},{12,0},{1,5},{5,9},{9,13},{13,1},{2,6},{6,10},{... | collective-permute-start | bytes 786440 | tf_op jit(solution)/shard_map/ppermute | solution.py:319
  74.2 10.1 %collective-permute-start.19 = (bf16[256,512]{1,0:T(8,128)(2,1)S(1)}, bf16[256,512]{1,0:T(8,128)(2,1)S(1)}, u32[]{:S(2)}, u32[]{:S(2)}) collective-permute-start(bf16[256,512]{1,0:T(8,128)(2,1)S(1)} %get-tuple-element.78.refs_12_), channel_id=1, source_target_pairs={{0,2},{2,0},{1,3},{3,1},{4,6},{6,4},{5,7},{7,5},{8,10},{10,8},{9,1... | collective-permute-start | bytes 786440 | tf_op jit(solution)/shard_map/ppermute | solution.py:314
  84.4 7.5 %collective-permute-start.21 = (bf16[256,512]{1,0:T(8,128)(2,1)S(1)}, bf16[256,512]{1,0:T(8,128)(2,1)S(1)}, u32[]{:S(2)}, u32[]{:S(2)}) collective-permute-start(bf16[256,512]{1,0:T(8,128)(2,1)S(1)} %get-tuple-element.78.refs_12_), channel_id=1, source_target_pairs={{0,12},{4,0},{8,4},{12,8},{1,13},{5,1},{9,5},{13,9},{2,14},{6,2},{... | collective-permute-start | bytes 786440 | tf_op jit(solution)/shard_map/ppermute | solution.py:319
  86.1 6.9 %collective-permute-start.22 = (bf16[256,512]{1,0:T(8,128)(2,1)S(1)}, bf16[256,512]{1,0:T(8,128)(2,1)S(1)}, u32[]{:S(2)}, u32[]{:S(2)}) collective-permute-start(bf16[256,512]{1,0:T(8,128)(2,1)S(1)} %collective-permute-done.18.refs_14_), channel_id=1, source_target_pairs={{0,2},{2,0},{1,3},{3,1},{4,6},{6,4},{5,7},{7,5},{8,10},{10,8},{9,1... | collective-permute-start | bytes 786440 | tf_op jit(solution)/shard_map/ppermute | solution.py:314
  87.5 15.1 %collective-permute-start.20 = (bf16[2,640,256]{2,1,0:T(8,128)(2,1)S(1)}, bf16[2,640,256]{2,1,0:T(8,128)(2,1)S(1)}, u32[]{:S(2)}, u32[]{:S(2)}) collective-permute-start(bf16[2,640,256]{2,1,0:T(8,128)(2,1)S(1)} %collective-permute-done.14.refs_0_.refs_1_), channel_id=1, source_target_pairs={{0,1},{1,0},{2,3},{3,2},{4,5},{5,4},{6,7},{7,6},{8,9},{9,8},{10,11... | collective-permute-start | bytes 1966088 | tf_op jit(solution)/shard_map/ppermute | solution.py:314
  87.5 15.1 %collective-permute-start.26 = (bf16[2,640,256]{2,1,0:T(8,128)(2,1)S(1)}, bf16[2,640,256]{2,1,0:T(8,128)(2,1)S(1)}, u32[]{:S(2)}, u32[]{:S(2)}) collective-permute-start(bf16[2,640,256]{2,1,0:T(8,128)(2,1)S(1)} %collective-permute-done.17.refs_2_.refs_3_.refs_4_.refs_5_), channel_id=1, source_target_pairs={{0,1},{1,0},{2,3},{3,2},{4,5},{5,4},{6,7},{7,6},{8,9},{9,8},{10,11... | collective-permute-start | bytes 1966088 | tf_op jit(solution)/shard_map/ppermute | solution.py:314
  93.0 8.2 %collective-permute-start.23 = (bf16[256,512]{1,0:T(8,128)(2,1)S(1)}, bf16[256,512]{1,0:T(8,128)(2,1)S(1)}, u32[]{:S(2)}, u32[]{:S(2)}) collective-permute-start(bf16[256,512]{1,0:T(8,128)(2,1)S(1)} %collective-permute-done.18.refs_14_), channel_id=1, source_target_pairs={{0,4},{4,8},{8,12},{12,0},{1,5},{5,9},{9,13},{13,1},{2,6},{6,10},{... | collective-permute-start | bytes 786440 | tf_op jit(solution)/shard_map/ppermute | solution.py:319
  93.7 7.6 %collective-permute-start.24 = (bf16[256,512]{1,0:T(8,128)(2,1)S(1)}, bf16[256,512]{1,0:T(8,128)(2,1)S(1)}, u32[]{:S(2)}, u32[]{:S(2)}) collective-permute-start(bf16[256,512]{1,0:T(8,128)(2,1)S(1)} %collective-permute-done.21.refs_15_), channel_id=1, source_target_pairs={{0,2},{2,0},{1,3},{3,1},{4,6},{6,4},{5,7},{7,5},{8,10},{10,8},{9,1... | collective-permute-start | bytes 786440 | tf_op jit(solution)/shard_map/ppermute | solution.py:314
  101.2 6.4 %collective-permute-start.25 = (bf16[256,512]{1,0:T(8,128)(2,1)S(1)}, bf16[256,512]{1,0:T(8,128)(2,1)S(1)}, u32[]{:S(2)}, u32[]{:S(2)}) collective-permute-start(bf16[256,512]{1,0:T(8,128)(2,1)S(1)} %collective-permute-done.23.refs_4_), channel_id=1, source_target_pairs={{0,2},{2,0},{1,3},{3,1},{4,6},{6,4},{5,7},{7,5},{8,10},{10,8},{9,1... | collective-permute-start | bytes 786440 | tf_op jit(solution)/shard_map/ppermute | solution.py:314
  (1 other events, 5.9 us)

commit v23 on v22

--- a/solution.py
+++ b/solution.py
@@ -107,9 +107,14 @@
     length, columns = cosine.shape[0], pair_ref.shape[1] // 2
     key_heads = columns // HEAD
     group_size = queries_ref.shape[1] // columns
-    key_at = lax.broadcasted_iota(jnp.int32, (length, length), 0)
-    query_at = lax.broadcasted_iota(jnp.int32, (length, length), 1)
-    causal = key_at <= query_at
+    part = length // 2
+    masks = []
+    for half in range(2):
+        seen = part * (half + 1)
+        key_at = lax.broadcasted_iota(jnp.int32, (seen, part), 0)
+        query_at = lax.broadcasted_iota(jnp.int32, (seen, part), 1) + half * part
+        masks.append(key_at <= query_at)
+    unseen = jnp.zeros((length - part, part), jnp.bfloat16)
     for head in range(key_heads):
         lanes = slice(head * HEAD, (head + 1) * HEAD)
         raw = raw_of(0, lanes)
@@ -123,15 +128,25 @@
             start = (head * group_size + member) * HEAD
             query = queries_ref[:, start : start + HEAD]
             upstream = cotangent_ref[:, start : start + HEAD]
-            scores = jnp.where(causal, product_rows(keys, query), -jnp.inf)
-            peak = jnp.max(scores, 0, keepdims=True)
-            exponentials = jnp.exp((scores - peak) * SCALE)
-            probability = exponentials * (1.0 / jnp.sum(exponentials, 0, keepdims=True))
+            scores = product_rows(keys, query)
             grad_probability = product_rows(values, upstream)
-            total = jnp.sum(probability * grad_probability, 0, keepdims=True)
-            grad_scores = (probability * (grad_probability - total) * SCALE).astype(jnp.bfloat16)
+            weights, grad_scores = [], []
+            for half in range(2):
+                rows, columns_at = slice(part * (half + 1)), slice(half * part, (half + 1) * part)
+                seen = jnp.where(masks[half], scores[rows, columns_at], -jnp.inf)
+                peak = jnp.max(seen, 0, keepdims=True)
+                exponentials = jnp.exp((seen - peak) * SCALE)
+                probability = exponentials * (1.0 / jnp.sum(exponentials, 0, keepdims=True))
+                upward = grad_probability[rows, columns_at]
+                total = jnp.sum(probability * upward, 0, keepdims=True)
+                weights.append(probability.astype(jnp.bfloat16))
+                grad_scores.append((probability * (upward - total) * SCALE).astype(jnp.bfloat16))
+            weights, grad_scores = (
+                jnp.concatenate([jnp.concatenate([early, unseen], 0), late], 1)
+                for early, late in (weights, grad_scores)
+            )
             grad_rotated += product(grad_scores, query)
-            grad_value += product(probability.astype(jnp.bfloat16), upstream)
+            grad_value += product(weights, upstream)
             grad_query = product(keys_across, grad_scores)
             grad_query_ref[:, start : start + HEAD] = grad_query.T.astype(jnp.bfloat16)
         grad_key = grad_rotated * cosine - pltpu.roll(grad_rotated, HEAD // 2, 1) * sine

time: 110 us -> 109 us (level)
  no operation moved by 1% of the time
where the time goes in v23:
time: 109 us
  waiting for transfers between devices  63.7 us (58%)
  starting transfers between devices  30.1 us (28%)
  Pallas kernels  10.9 us (10%)
  other arithmetic  2.4 us (2%)
  local copies, waits for them, and re-layouts  1.3 us (1%)
    ppermute x19, waiting for transfers between devices, swapped(): return lax.ppermute(block, axis, [(0, 1), (1, 0)])  38.6 us
    ppermute x6, waiting for transfers between devices, turned(): lax.ppermute(block, axis, [(i, (i + distance) % size) for i in range(size)])  25.1 us
    ppermute x19, starting transfers between devices, swapped(): return lax.ppermute(block, axis, [(0, 1), (1, 0)])  20.2 us
    ppermute x6, starting transfers between devices, turned(): lax.ppermute(block, axis, [(i, (i + distance) % size) for i in range(size)])  9.25 us
    pallas_call x1, Pallas kernels, attention(): pl.pallas_call(functools.partial(attention_kernel, distance), in_specs=[I...  4.97 us
    pallas_call x2, Pallas kernels, gradient(): pl.pallas_call(functools.partial(gradient_kernel, tuple(some), sums is No...  3.47 us
  transfers between devices with their start and end apart: 27, of which 16 were waited for; matrix products, arithmetic and copies ran while one was open for 2% of the time, Pallas kernels for 8%

profile of v23, /device:TPU:0, one launch (start us, length us, event | category | flops | bytes accessed | tf_op | source)
XLA Modules:
  0.0 109.2 jit_solution(13969584208441108709)
XLA Ops:
  1.8 3.1 %collective-permute-start = (bf16[640,256]{1,0:T(8,128)(2,1)S(1)}, bf16[640,256]{1,0:T(8,128)(2,1)S(1)}, u32[]{:S(2)}, u32[]{:S(2)}) collective-permute-start(bf16[640,256]{1,0:T(8,128)(2,1)S(1)} %dynamic-slice_bitcast_fusion), channel_id=1, source_target_pairs={{0,4},{4,8},{8,12},{12,0},{1,5},{5,9},{9,13},{13,1},{2,6},{6,10},{... | collective-permute-start | bytes 983048 | tf_op jit(solution)/shard_map/ppermute | solution.py:334
  4.8 1.7 %multiply_reduce_fusion = f32[256]{0:T(256)S(1)} fusion(bf16[256,2560]{1,0:T(8,128)(2,1)} %values_ref.1), kind=kLoop, calls=%fused_computation | loop fusion | flops 1965824 | bytes 1311744 | tf_op jit(solution)/shard_map/reduce_sum | solution.py:369
  8.8 1.6 %collective-permute-start.2 = (bf16[320,256]{1,0:T(8,128)(2,1)S(1)}, bf16[320,256]{1,0:T(8,128)(2,1)S(1)}, u32[]{:S(2)}, u32[]{:S(2)}) collective-permute-start(bf16[320,256]{1,0:T(8,128)(2,1)S(1)} %get-tuple-element.48), channel_id=1, source_target_pairs={{0,2},{2,0},{1,3},{3,1},{4,6},{6,4},{5,7},{7,5},{8,10},{10,8},{9,1... | collective-permute-start | bytes 491528 | tf_op jit(solution)/shard_map/ppermute | solution.py:329
  10.4 4.8 %collective-permute-done.2.early_ref = bf16[320,256]{1,0:T(8,128)(2,1)S(1)} collective-permute-done((bf16[320,256]{1,0:T(8,128)(2,1)S(1)}, bf16[320,256]{1,0:T(8,128)(2,1)S(1)}, u32[]{:S(2)}, u32[]{:S(2)}) %collective-permute-start.2) | collective-permute-done | bytes 163872 | tf_op jit(solution)/shard_map/ppermute | solution.py:329
  15.2 1.5 %collective-permute-start.3 = (bf16[640,256]{1,0:T(8,128)(2,1)S(1)}, bf16[640,256]{1,0:T(8,128)(2,1)S(1)}, u32[]{:S(2)}, u32[]{:S(2)}) collective-permute-start(bf16[640,256]{1,0:T(8,128)(2,1)S(1)} %collective-permute-done.refs_0_), channel_id=1, source_target_pairs={{0,16},{16,0},{1,17},{17,1},{2,18},{18,2},{3,19},{19,3},{4,20},{20... | collective-permute-start | bytes 983048 | tf_op jit(solution)/shard_map/ppermute | solution.py:329
  16.7 2.2 %collective-permute-start.4 = (bf16[640,256]{1,0:T(8,128)(2,1)S(1)}, bf16[640,256]{1,0:T(8,128)(2,1)S(1)}, u32[]{:S(2)}, u32[]{:S(2)}) collective-permute-start(bf16[640,256]{1,0:T(8,128)(2,1)S(1)} %dynamic-slice_bitcast_fusion), channel_id=1, source_target_pairs={{0,12},{4,0},{8,4},{12,8},{1,13},{5,1},{9,5},{13,9},{2,14},{6,2},{... | collective-permute-start | bytes 983048 | tf_op jit(solution)/shard_map/ppermute | solution.py:334
  19.0 1.5 %collective-permute-start.9 = (bf16[960,256]{1,0:T(8,128)(2,1)S(1)}, bf16[960,256]{1,0:T(8,128)(2,1)S(1)}, u32[]{:S(2)}, u32[]{:S(2)}) collective-permute-start(bf16[960,256]{1,0:T(8,128)(2,1)S(1)} %get-tuple-element.56), channel_id=1, source_target_pairs={{0,2},{2,0},{1,3},{3,1},{4,6},{6,4},{5,7},{7,5},{8,10},{10,8},{9,1... | collective-permute-start | bytes 1474568 | tf_op jit(solution)/shard_map/ppermute | solution.py:329
  20.5 4.9 %collective-permute-done.3.refs_2_ = bf16[640,256]{1,0:T(8,128)(2,1)S(1)} collective-permute-done((bf16[640,256]{1,0:T(8,128)(2,1)S(1)}, bf16[640,256]{1,0:T(8,128)(2,1)S(1)}, u32[]{:S(2)}, u32[]{:S(2)}) %collective-permute-start.3) | collective-permute-done | bytes 327712 | tf_op jit(solution)/shard_map/ppermute | solution.py:329
  26.6 1.6 %collective-permute-start.6 = (bf16[640,256]{1,0:T(8,128)(2,1)S(1)}, bf16[640,256]{1,0:T(8,128)(2,1)S(1)}, u32[]{:S(2)}, u32[]{:S(2)}) collective-permute-start(bf16[640,256]{1,0:T(8,128)(2,1)S(1)} %collective-permute-done.refs_0_), channel_id=1, source_target_pairs={{0,4},{4,8},{8,12},{12,0},{1,5},{5,9},{9,13},{13,1},{2,6},{6,10},{... | collective-permute-start | bytes 983048 | tf_op jit(solution)/shard_map/ppermute | solution.py:334
  28.7 1.5 %collective-permute-start.8 = (bf16[640,256]{1,0:T(8,128)(2,1)S(1)}, bf16[640,256]{1,0:T(8,128)(2,1)S(1)}, u32[]{:S(2)}, u32[]{:S(2)}) collective-permute-start(bf16[640,256]{1,0:T(8,128)(2,1)S(1)} %collective-permute-done.refs_0_), channel_id=1, source_target_pairs={{0,2},{2,0},{1,3},{3,1},{4,6},{6,4},{5,7},{7,5},{8,10},{10,8},{9,1... | collective-permute-start | bytes 983048 | tf_op jit(solution)/shard_map/ppermute | solution.py:329
  30.1 2.9 %collective-permute-done.9.late_ref = bf16[960,256]{1,0:T(8,128)(2,1)S(1)} collective-permute-done((bf16[960,256]{1,0:T(8,128)(2,1)S(1)}, bf16[960,256]{1,0:T(8,128)(2,1)S(1)}, u32[]{:S(2)}, u32[]{:S(2)}) %collective-permute-start.9) | collective-permute-done | bytes 491552 | tf_op jit(solution)/shard_map/ppermute | solution.py:329
  33.1 4.8 %collective-permute-done.6.p0 = bf16[640,256]{1,0:T(8,128)(2,1)S(1)} collective-permute-done((bf16[640,256]{1,0:T(8,128)(2,1)S(1)}, bf16[640,256]{1,0:T(8,128)(2,1)S(1)}, u32[]{:S(2)}, u32[]{:S(2)}) %collective-permute-start.6) | collective-permute-done | bytes 327712 | tf_op jit(solution)/shard_map/ppermute | solution.py:334
  40.3 1.7 %collective-permute-start.10 = (bf16[640,256]{1,0:T(8,128)(2,1)S(1)}, bf16[640,256]{1,0:T(8,128)(2,1)S(1)}, u32[]{:S(2)}, u32[]{:S(2)}) collective-permute-start(bf16[640,256]{1,0:T(8,128)(2,1)S(1)} %collective-permute-done.6.p0), channel_id=1, source_target_pairs={{0,2},{2,0},{1,3},{3,1},{4,6},{6,4},{5,7},{7,5},{8,10},{10,8},{9,1... | collective-permute-start | bytes 983048 | tf_op jit(solution)/shard_map/ppermute | solution.py:329
  42.0 1.5 %collective-permute-start.12 = (bf16[640,256]{1,0:T(8,128)(2,1)S(1)}, bf16[640,256]{1,0:T(8,128)(2,1)S(1)}, u32[]{:S(2)}, u32[]{:S(2)}) collective-permute-start(bf16[640,256]{1,0:T(8,128)(2,1)S(1)} %collective-permute-done.8.refs_1_), channel_id=1, source_target_pairs={{0,16},{16,0},{1,17},{17,1},{2,18},{18,2},{3,19},{19,3},{4,20},{20... | collective-permute-start | bytes 983048 | tf_op jit(solution)/shard_map/ppermute | solution.py:329
  44.0 5.3 %collective-permute-done.11.p2 = bf16[640,256]{1,0:T(8,128)(2,1)S(1)} collective-permute-done((bf16[640,256]{1,0:T(8,128)(2,1)S(1)}, bf16[640,256]{1,0:T(8,128)(2,1)S(1)}, u32[]{:S(2)}, u32[]{:S(2)}) %collective-permute-start.11) | collective-permute-done | bytes 327712 | tf_op jit(solution)/shard_map/ppermute | solution.py:329
  49.3 7.0 %collective-permute-done.12.refs_3_ = bf16[640,256]{1,0:T(8,128)(2,1)S(1)} collective-permute-done((bf16[640,256]{1,0:T(8,128)(2,1)S(1)}, bf16[640,256]{1,0:T(8,128)(2,1)S(1)}, u32[]{:S(2)}, u32[]{:S(2)}) %collective-permute-start.12) | collective-permute-done | bytes 327712 | tf_op jit(solution)/shard_map/ppermute | solution.py:329
  56.3 2.3 %collective-permute-start.16 = (bf16[640,256]{1,0:T(8,128)(2,1)S(1)}, bf16[640,256]{1,0:T(8,128)(2,1)S(1)}, u32[]{:S(2)}, u32[]{:S(2)}) collective-permute-start(bf16[640,256]{1,0:T(8,128)(2,1)S(1)} %collective-permute-done.13.refs_5_), channel_id=1, source_target_pairs={{0,16},{16,0},{1,17},{17,1},{2,18},{18,2},{3,19},{19,3},{4,20},{20... | collective-permute-start | bytes 983048 | tf_op jit(solution)/shard_map/ppermute | solution.py:329
  58.6 1.3 %collective-permute-start.15 = (bf16[640,256]{1,0:T(8,128)(2,1)S(1)}, bf16[640,256]{1,0:T(8,128)(2,1)S(1)}, u32[]{:S(2)}, u32[]{:S(2)}) collective-permute-start(bf16[640,256]{1,0:T(8,128)(2,1)S(1)} %collective-permute-done.11.p2), channel_id=1, source_target_pairs={{0,2},{2,0},{1,3},{3,1},{4,6},{6,4},{5,7},{7,5},{8,10},{10,8},{9,1... | collective-permute-start | bytes 983048 | tf_op jit(solution)/shard_map/ppermute | solution.py:329
  60.6 5.8 %collective-permute-done.16.refs_7_ = bf16[640,256]{1,0:T(8,128)(2,1)S(1)} collective-permute-done((bf16[640,256]{1,0:T(8,128)(2,1)S(1)}, bf16[640,256]{1,0:T(8,128)(2,1)S(1)}, u32[]{:S(2)}, u32[]{:S(2)}) %collective-permute-start.16) | collective-permute-done | bytes 327712 | tf_op jit(solution)/shard_map/ppermute | solution.py:329
  66.4 1.4 %project.1.sums_ref = f32[2,256,256]{2,1,0:T(8,128)S(1)} custom-call(bf16[256,2560]{1,0:T(8,128)(2,1)S(1)} %get-tuple-element.50.own_ref, bf16[256,2560]{1,0:T(8,128)(2,1)S(1)} %collective-permute-done.5.other_ref, bf16[2,1280,256]{2,1,0:T(8,128)(2,1)S(1)} %copy-done.1, bf16[640,256]{1,0:T(8,128)(2,1)S(1)} %collective-permute-done.refs_0_, ...), custom_call_target="tpu_custom_call" | custom-call | flops 1006632960 | bytes 7000000 | tf_op jit(solution)/shard_map/project/pallas_call | solution.py:91
  67.8 1.3 %collective-permute-done.15.p3 = bf16[640,256]{1,0:T(8,128)(2,1)S(1)} collective-permute-done((bf16[640,256]{1,0:T(8,128)(2,1)S(1)}, bf16[640,256]{1,0:T(8,128)(2,1)S(1)}, u32[]{:S(2)}, u32[]{:S(2)}) %collective-permute-start.15) | collective-permute-done | bytes 327712 | tf_op jit(solution)/shard_map/ppermute | solution.py:329
  69.2 5.0 %attention.1 = (bf16[256,1280]{1,0:T(8,128)(2,1)}, bf16[256,512]{1,0:T(8,128)(2,1)S(1)}) custom-call(bf16[256,2560]{1,0:T(8,128)(2,1)S(1)} %get-tuple-element.50.own_ref, bf16[256,2560]{1,0:T(8,128)(2,1)S(1)} %collective-permute-done.5.other_ref, bf16[640,256]{1,0:T(8,128)(2,1)S(1)} %collective-permute-done.6.p0, ...), custom_call_target="tpu_custom_call" | custom-call | flops 838860800 | bytes 5000000 | tf_op jit(solution)/shard_map/attention/pallas_call | solution.py:180
  75.4 8.8 %collective-permute-done.18.refs_14_ = bf16[256,512]{1,0:T(8,128)(2,1)S(1)} collective-permute-done((bf16[256,512]{1,0:T(8,128)(2,1)S(1)}, bf16[256,512]{1,0:T(8,128)(2,1)S(1)}, u32[]{:S(2)}, u32[]{:S(2)}) %collective-permute-start.18) | collective-permute-done | bytes 262176 | tf_op jit(solution)/shard_map/ppermute | solution.py:334
  84.3 1.7 %collective-permute-start.21 = (bf16[256,512]{1,0:T(8,128)(2,1)S(1)}, bf16[256,512]{1,0:T(8,128)(2,1)S(1)}, u32[]{:S(2)}, u32[]{:S(2)}) collective-permute-start(bf16[256,512]{1,0:T(8,128)(2,1)S(1)} %get-tuple-element.78.refs_12_), channel_id=1, source_target_pairs={{0,12},{4,0},{8,4},{12,8},{1,13},{5,1},{9,5},{13,9},{2,14},{6,2},{... | collective-permute-start | bytes 786440 | tf_op jit(solution)/shard_map/ppermute | solution.py:334
  86.0 1.3 %collective-permute-start.22 = (bf16[256,512]{1,0:T(8,128)(2,1)S(1)}, bf16[256,512]{1,0:T(8,128)(2,1)S(1)}, u32[]{:S(2)}, u32[]{:S(2)}) collective-permute-start(bf16[256,512]{1,0:T(8,128)(2,1)S(1)} %collective-permute-done.18.refs_14_), channel_id=1, source_target_pairs={{0,2},{2,0},{1,3},{3,1},{4,6},{6,4},{5,7},{7,5},{8,10},{10,8},{9,1... | collective-permute-start | bytes 786440 | tf_op jit(solution)/shard_map/ppermute | solution.py:329
  87.9 3.9 %collective-permute-done.21.refs_15_ = bf16[256,512]{1,0:T(8,128)(2,1)S(1)} collective-permute-done((bf16[256,512]{1,0:T(8,128)(2,1)S(1)}, bf16[256,512]{1,0:T(8,128)(2,1)S(1)}, u32[]{:S(2)}, u32[]{:S(2)}) %collective-permute-start.21) | collective-permute-done | bytes 262176 | tf_op jit(solution)/shard_map/ppermute | solution.py:334
  93.6 1.3 %collective-permute-start.24 = (bf16[256,512]{1,0:T(8,128)(2,1)S(1)}, bf16[256,512]{1,0:T(8,128)(2,1)S(1)}, u32[]{:S(2)}, u32[]{:S(2)}) collective-permute-start(bf16[256,512]{1,0:T(8,128)(2,1)S(1)} %collective-permute-done.21.refs_15_), channel_id=1, source_target_pairs={{0,2},{2,0},{1,3},{3,1},{4,6},{6,4},{5,7},{7,5},{8,10},{10,8},{9,1... | collective-permute-start | bytes 786440 | tf_op jit(solution)/shard_map/ppermute | solution.py:329
  94.9 6.2 %collective-permute-done.23.refs_4_ = bf16[256,512]{1,0:T(8,128)(2,1)S(1)} collective-permute-done((bf16[256,512]{1,0:T(8,128)(2,1)S(1)}, bf16[256,512]{1,0:T(8,128)(2,1)S(1)}, u32[]{:S(2)}, u32[]{:S(2)}) %collective-permute-start.23) | collective-permute-done | bytes 262176 | tf_op jit(solution)/shard_map/ppermute | solution.py:334
  101.1 1.4 %collective-permute-start.25 = (bf16[256,512]{1,0:T(8,128)(2,1)S(1)}, bf16[256,512]{1,0:T(8,128)(2,1)S(1)}, u32[]{:S(2)}, u32[]{:S(2)}) collective-permute-start(bf16[256,512]{1,0:T(8,128)(2,1)S(1)} %collective-permute-done.23.refs_4_), channel_id=1, source_target_pairs={{0,2},{2,0},{1,3},{3,1},{4,6},{6,4},{5,7},{7,5},{8,10},{10,8},{9,1... | collective-permute-start | bytes 786440 | tf_op jit(solution)/shard_map/ppermute | solution.py:329
  102.5 1.7 %gradient.2 = (f32[2,640,256]{2,1,0:T(8,128)S(1)}, f32[2,256]{1,0:T(2,128)S(1)}) custom-call(bf16[2,640,256]{2,1,0:T(8,128)(2,1)S(1)} %collective-permute-done.14.refs_0_.refs_1_, bf16[2,640,256]{2,1,0:T(8,128)(2,1)S(1)} %collective-permute-done.14.refs_0_.refs_1_, bf16[2,640,256]{2,1,0:T(8,128)(2,1)S(1)} %collective-permute-done.17.refs_2_.refs_3_.refs_4_.refs_5_, ...), custom_call_target="tpu_custom_call" | custom-call | flops 1006632960 | bytes 5000000 | tf_op jit(solution)/shard_map/gradient/pallas_call | solution.py:245
  104.2 3.3 %collective-permute-done.25.refs_5_ = bf16[256,512]{1,0:T(8,128)(2,1)S(1)} collective-permute-done((bf16[256,512]{1,0:T(8,128)(2,1)S(1)}, bf16[256,512]{1,0:T(8,128)(2,1)S(1)}, u32[]{:S(2)}, u32[]{:S(2)}) %collective-permute-start.25) | collective-permute-done | bytes 262176 | tf_op jit(solution)/shard_map/ppermute | solution.py:329
  107.5 1.7 %gradient.3 = (f32[2,640,256]{2,1,0:T(8,128)}, f32[2,256]{1,0:T(2,128)}) custom-call(bf16[2,640,256]{2,1,0:T(8,128)(2,1)S(1)} %collective-permute-done.14.refs_0_.refs_1_, bf16[2,640,256]{2,1,0:T(8,128)(2,1)S(1)} %collective-permute-done.14.refs_0_.refs_1_, bf16[2,640,256]{2,1,0:T(8,128)(2,1)S(1)} %collective-permute-done.20.refs_6_.refs_7_.refs_2_.refs_3_, ...), custom_call_target="tpu_custom_call" | custom-call | flops 335544320 | bytes 5000000 | tf_op jit(solution)/shard_map/gradient/pallas_call | solution.py:245
  (51 shorter events, 12.3 us)
Async XLA Ops:
  0.6 7.2 %copy-start = (bf16[256,2560]{1,0:T(8,128)(2,1)S(1)}, bf16[256,2560]{1,0:T(8,128)(2,1)}, u32[]{:S(2)}) copy-start(bf16[256,2560]{1,0:T(8,128)(2,1)} %values_ref.1) | copy-start | bytes 3932164
  1.8 13.4 %collective-permute-start = (bf16[640,256]{1,0:T(8,128)(2,1)S(1)}, bf16[640,256]{1,0:T(8,128)(2,1)S(1)}, u32[]{:S(2)}, u32[]{:S(2)}) collective-permute-start(bf16[640,256]{1,0:T(8,128)(2,1)S(1)} %dynamic-slice_bitcast_fusion), channel_id=1, source_target_pairs={{0,4},{4,8},{8,12},{12,0},{1,5},{5,9},{9,13},{13,1},{2,6},{6,10},{... | collective-permute-start | bytes 983048 | tf_op jit(solution)/shard_map/ppermute | solution.py:334
  6.5 1.2 %collective-permute-start.1 = (f32[256,1]{0,1:T(1,128)S(1)}, f32[256,1]{0,1:T(1,128)S(1)}, u32[]{:S(2)}, u32[]{:S(2)}) collective-permute-start(f32[256,1]{0,1:T(1,128)S(1)} %bitcast.3), channel_id=1, source_target_pairs={{0,1},{1,0},{2,3},{3,2},{4,5},{5,4},{6,7},{7,6},{8,9},{9,8},{10,11... | collective-permute-start | bytes 3080 | tf_op jit(solution)/shard_map/ppermute | solution.py:329
  7.9 52.5 %copy-start.5 = (bf16[2,256]{1,0:T(2,128)(2,1)S(1)}, bf16[2,256]{1,0:T(2,128)(2,1)}, u32[]{:S(2)}) copy-start(bf16[2,256]{1,0:T(2,128)(2,1)} %param.11) | copy-start | bytes 3076
  8.8 57.6 %copy-start.1 = (bf16[2,1280,256]{2,1,0:T(8,128)(2,1)S(1)}, bf16[2,1280,256]{2,1,0:T(8,128)(2,1)}, u32[]{:S(2)}) copy-start(bf16[2,1280,256]{2,1,0:T(8,128)(2,1)} %weight_ref.1) | copy-start | bytes 3932164
  8.8 6.4 %collective-permute-start.2 = (bf16[320,256]{1,0:T(8,128)(2,1)S(1)}, bf16[320,256]{1,0:T(8,128)(2,1)S(1)}, u32[]{:S(2)}, u32[]{:S(2)}) collective-permute-start(bf16[320,256]{1,0:T(8,128)(2,1)S(1)} %get-tuple-element.48), channel_id=1, source_target_pairs={{0,2},{2,0},{1,3},{3,1},{4,6},{6,4},{5,7},{7,5},{8,10},{10,8},{9,1... | collective-permute-start | bytes 491528 | tf_op jit(solution)/shard_map/ppermute | solution.py:329
  15.2 11.4 %collective-permute-start.5 = (bf16[256,2560]{1,0:T(8,128)(2,1)S(1)}, bf16[256,2560]{1,0:T(8,128)(2,1)S(1)}, u32[]{:S(2)}, u32[]{:S(2)}) collective-permute-start(bf16[256,2560]{1,0:T(8,128)(2,1)S(1)} %get-tuple-element.50.own_ref), channel_id=1, source_target_pairs={{0,1},{1,0},{2,3},{3,2},{4,5},{5,4},{6,7},{7,6},{8,9},{9,8},{10,11... | collective-permute-start | bytes 3932168 | tf_op jit(solution)/shard_map/ppermute | solution.py:329
  15.2 10.1 %collective-permute-start.3 = (bf16[640,256]{1,0:T(8,128)(2,1)S(1)}, bf16[640,256]{1,0:T(8,128)(2,1)S(1)}, u32[]{:S(2)}, u32[]{:S(2)}) collective-permute-start(bf16[640,256]{1,0:T(8,128)(2,1)S(1)} %collective-permute-done.refs_0_), channel_id=1, source_target_pairs={{0,16},{16,0},{1,17},{17,1},{2,18},{18,2},{3,19},{19,3},{4,20},{20... | collective-permute-start | bytes 983048 | tf_op jit(solution)/shard_map/ppermute | solution.py:329
  16.7 9.8 %collective-permute-start.4 = (bf16[640,256]{1,0:T(8,128)(2,1)S(1)}, bf16[640,256]{1,0:T(8,128)(2,1)S(1)}, u32[]{:S(2)}, u32[]{:S(2)}) collective-permute-start(bf16[640,256]{1,0:T(8,128)(2,1)S(1)} %dynamic-slice_bitcast_fusion), channel_id=1, source_target_pairs={{0,12},{4,0},{8,4},{12,8},{1,13},{5,1},{9,5},{13,9},{2,14},{6,2},{... | collective-permute-start | bytes 983048 | tf_op jit(solution)/shard_map/ppermute | solution.py:334
  19.0 14.1 %collective-permute-start.9 = (bf16[960,256]{1,0:T(8,128)(2,1)S(1)}, bf16[960,256]{1,0:T(8,128)(2,1)S(1)}, u32[]{:S(2)}, u32[]{:S(2)}) collective-permute-start(bf16[960,256]{1,0:T(8,128)(2,1)S(1)} %get-tuple-element.56), channel_id=1, source_target_pairs={{0,2},{2,0},{1,3},{3,1},{4,6},{6,4},{5,7},{7,5},{8,10},{10,8},{9,1... | collective-permute-start | bytes 1474568 | tf_op jit(solution)/shard_map/ppermute | solution.py:329
  26.6 11.3 %collective-permute-start.6 = (bf16[640,256]{1,0:T(8,128)(2,1)S(1)}, bf16[640,256]{1,0:T(8,128)(2,1)S(1)}, u32[]{:S(2)}, u32[]{:S(2)}) collective-permute-start(bf16[640,256]{1,0:T(8,128)(2,1)S(1)} %collective-permute-done.refs_0_), channel_id=1, source_target_pairs={{0,4},{4,8},{8,12},{12,0},{1,5},{5,9},{9,13},{13,1},{2,6},{6,10},{... | collective-permute-start | bytes 983048 | tf_op jit(solution)/shard_map/ppermute | solution.py:334
  28.1 9.8 %collective-permute-start.7 = (bf16[640,256]{1,0:T(8,128)(2,1)S(1)}, bf16[640,256]{1,0:T(8,128)(2,1)S(1)}, u32[]{:S(2)}, u32[]{:S(2)}) collective-permute-start(bf16[640,256]{1,0:T(8,128)(2,1)S(1)} %collective-permute-done.4.refs_4_), channel_id=1, source_target_pairs={{0,16},{16,0},{1,17},{17,1},{2,18},{18,2},{3,19},{19,3},{4,20},{20... | collective-permute-start | bytes 983048 | tf_op jit(solution)/shard_map/ppermute | solution.py:329
  28.7 10.4 %collective-permute-start.8 = (bf16[640,256]{1,0:T(8,128)(2,1)S(1)}, bf16[640,256]{1,0:T(8,128)(2,1)S(1)}, u32[]{:S(2)}, u32[]{:S(2)}) collective-permute-start(bf16[640,256]{1,0:T(8,128)(2,1)S(1)} %collective-permute-done.refs_0_), channel_id=1, source_target_pairs={{0,2},{2,0},{1,3},{3,1},{4,6},{6,4},{5,7},{7,5},{8,10},{10,8},{9,1... | collective-permute-start | bytes 983048 | tf_op jit(solution)/shard_map/ppermute | solution.py:329
  39.2 17.1 %collective-permute-start.14 = (bf16[2,640,256]{2,1,0:T(8,128)(2,1)S(1)}, bf16[2,640,256]{2,1,0:T(8,128)(2,1)S(1)}, u32[]{:S(2)}, u32[]{:S(2)}) collective-permute-start(bf16[2,640,256]{2,1,0:T(8,128)(2,1)S(1)} %get-tuple-element.63), channel_id=1, source_target_pairs={{0,0},{1,8},{4,4},{5,12},{8,1},{9,9},{12,5},{13,13},{2,2},{3,10},{... | collective-permute-start | bytes 1966088 | tf_op jit(solution)/shard_map/ppermute | solution.py:362
  39.9 9.4 %collective-permute-start.11 = (bf16[640,256]{1,0:T(8,128)(2,1)S(1)}, bf16[640,256]{1,0:T(8,128)(2,1)S(1)}, u32[]{:S(2)}, u32[]{:S(2)}) collective-permute-start(bf16[640,256]{1,0:T(8,128)(2,1)S(1)} %collective-permute-done.6.p0), channel_id=1, source_target_pairs={{0,16},{16,0},{1,17},{17,1},{2,18},{18,2},{3,19},{19,3},{4,20},{20... | collective-permute-start | bytes 983048 | tf_op jit(solution)/shard_map/ppermute | solution.py:329
  40.3 9.0 %collective-permute-start.10 = (bf16[640,256]{1,0:T(8,128)(2,1)S(1)}, bf16[640,256]{1,0:T(8,128)(2,1)S(1)}, u32[]{:S(2)}, u32[]{:S(2)}) collective-permute-start(bf16[640,256]{1,0:T(8,128)(2,1)S(1)} %collective-permute-done.6.p0), channel_id=1, source_target_pairs={{0,2},{2,0},{1,3},{3,1},{4,6},{6,4},{5,7},{7,5},{8,10},{10,8},{9,1... | collective-permute-start | bytes 983048 | tf_op jit(solution)/shard_map/ppermute | solution.py:329
  42.0 14.4 %collective-permute-start.12 = (bf16[640,256]{1,0:T(8,128)(2,1)S(1)}, bf16[640,256]{1,0:T(8,128)(2,1)S(1)}, u32[]{:S(2)}, u32[]{:S(2)}) collective-permute-start(bf16[640,256]{1,0:T(8,128)(2,1)S(1)} %collective-permute-done.8.refs_1_), channel_id=1, source_target_pairs={{0,16},{16,0},{1,17},{17,1},{2,18},{18,2},{3,19},{19,3},{4,20},{20... | collective-permute-start | bytes 983048 | tf_op jit(solution)/shard_map/ppermute | solution.py:329
  43.5 12.8 %collective-permute-start.13 = (bf16[640,256]{1,0:T(8,128)(2,1)S(1)}, bf16[640,256]{1,0:T(8,128)(2,1)S(1)}, u32[]{:S(2)}, u32[]{:S(2)}) collective-permute-start(bf16[640,256]{1,0:T(8,128)(2,1)S(1)} %collective-permute-done.4.refs_4_), channel_id=1, source_target_pairs={{0,2},{2,0},{1,3},{3,1},{4,6},{6,4},{5,7},{7,5},{8,10},{10,8},{9,1... | collective-permute-start | bytes 983048 | tf_op jit(solution)/shard_map/ppermute | solution.py:329
  49.3 24.8 %collective-permute-start.17 = (bf16[2,640,256]{2,1,0:T(8,128)(2,1)S(1)}, bf16[2,640,256]{2,1,0:T(8,128)(2,1)S(1)}, u32[]{:S(2)}, u32[]{:S(2)}) collective-permute-start(bf16[2,640,256]{2,1,0:T(8,128)(2,1)S(1)} %get-tuple-element.73), channel_id=1, source_target_pairs={{0,4},{1,12},{4,0},{5,8},{8,5},{9,13},{12,1},{13,9},{2,6},{3,14},{... | collective-permute-start | bytes 1966088 | tf_op jit(solution)/shard_map/ppermute | solution.py:362
  56.3 10.1 %collective-permute-start.16 = (bf16[640,256]{1,0:T(8,128)(2,1)S(1)}, bf16[640,256]{1,0:T(8,128)(2,1)S(1)}, u32[]{:S(2)}, u32[]{:S(2)}) collective-permute-start(bf16[640,256]{1,0:T(8,128)(2,1)S(1)} %collective-permute-done.13.refs_5_), channel_id=1, source_target_pairs={{0,16},{16,0},{1,17},{17,1},{2,18},{18,2},{3,19},{19,3},{4,20},{20... | collective-permute-start | bytes 983048 | tf_op jit(solution)/shard_map/ppermute | solution.py:329
  58.6 10.6 %collective-permute-start.15 = (bf16[640,256]{1,0:T(8,128)(2,1)S(1)}, bf16[640,256]{1,0:T(8,128)(2,1)S(1)}, u32[]{:S(2)}, u32[]{:S(2)}) collective-permute-start(bf16[640,256]{1,0:T(8,128)(2,1)S(1)} %collective-permute-done.11.p2), channel_id=1, source_target_pairs={{0,2},{2,0},{1,3},{3,1},{4,6},{6,4},{5,7},{7,5},{8,10},{10,8},{9,1... | collective-permute-start | bytes 983048 | tf_op jit(solution)/shard_map/ppermute | solution.py:329
  60.6 8.6 %copy-start.2 = (bf16[256,1280]{1,0:T(8,128)(2,1)S(1)}, bf16[256,1280]{1,0:T(8,128)(2,1)}, u32[]{:S(2)}) copy-start(bf16[256,1280]{1,0:T(8,128)(2,1)} %queries_ref.1) | copy-start | bytes 1966084
  60.6 8.6 %copy-start.3 = (bf16[256,1280]{1,0:T(8,128)(2,1)S(1)}, bf16[256,1280]{1,0:T(8,128)(2,1)}, u32[]{:S(2)}) copy-start(bf16[256,1280]{1,0:T(8,128)(2,1)} %cotangent_ref.1) | copy-start | bytes 1966084
  74.1 10.1 %collective-permute-start.18 = (bf16[256,512]{1,0:T(8,128)(2,1)S(1)}, bf16[256,512]{1,0:T(8,128)(2,1)S(1)}, u32[]{:S(2)}, u32[]{:S(2)}) collective-permute-start(bf16[256,512]{1,0:T(8,128)(2,1)S(1)} %get-tuple-element.78.refs_12_), channel_id=1, source_target_pairs={{0,4},{4,8},{8,12},{12,0},{1,5},{5,9},{9,13},{13,1},{2,6},{6,10},{... | collective-permute-start | bytes 786440 | tf_op jit(solution)/shard_map/ppermute | solution.py:334
  74.2 10.1 %collective-permute-start.19 = (bf16[256,512]{1,0:T(8,128)(2,1)S(1)}, bf16[256,512]{1,0:T(8,128)(2,1)S(1)}, u32[]{:S(2)}, u32[]{:S(2)}) collective-permute-start(bf16[256,512]{1,0:T(8,128)(2,1)S(1)} %get-tuple-element.78.refs_12_), channel_id=1, source_target_pairs={{0,2},{2,0},{1,3},{3,1},{4,6},{6,4},{5,7},{7,5},{8,10},{10,8},{9,1... | collective-permute-start | bytes 786440 | tf_op jit(solution)/shard_map/ppermute | solution.py:329
  84.3 7.5 %collective-permute-start.21 = (bf16[256,512]{1,0:T(8,128)(2,1)S(1)}, bf16[256,512]{1,0:T(8,128)(2,1)S(1)}, u32[]{:S(2)}, u32[]{:S(2)}) collective-permute-start(bf16[256,512]{1,0:T(8,128)(2,1)S(1)} %get-tuple-element.78.refs_12_), channel_id=1, source_target_pairs={{0,12},{4,0},{8,4},{12,8},{1,13},{5,1},{9,5},{13,9},{2,14},{6,2},{... | collective-permute-start | bytes 786440 | tf_op jit(solution)/shard_map/ppermute | solution.py:334
  86.0 6.9 %collective-permute-start.22 = (bf16[256,512]{1,0:T(8,128)(2,1)S(1)}, bf16[256,512]{1,0:T(8,128)(2,1)S(1)}, u32[]{:S(2)}, u32[]{:S(2)}) collective-permute-start(bf16[256,512]{1,0:T(8,128)(2,1)S(1)} %collective-permute-done.18.refs_14_), channel_id=1, source_target_pairs={{0,2},{2,0},{1,3},{3,1},{4,6},{6,4},{5,7},{7,5},{8,10},{10,8},{9,1... | collective-permute-start | bytes 786440 | tf_op jit(solution)/shard_map/ppermute | solution.py:329
  87.4 15.1 %collective-permute-start.20 = (bf16[2,640,256]{2,1,0:T(8,128)(2,1)S(1)}, bf16[2,640,256]{2,1,0:T(8,128)(2,1)S(1)}, u32[]{:S(2)}, u32[]{:S(2)}) collective-permute-start(bf16[2,640,256]{2,1,0:T(8,128)(2,1)S(1)} %collective-permute-done.14.refs_0_.refs_1_), channel_id=1, source_target_pairs={{0,1},{1,0},{2,3},{3,2},{4,5},{5,4},{6,7},{7,6},{8,9},{9,8},{10,11... | collective-permute-start | bytes 1966088 | tf_op jit(solution)/shard_map/ppermute | solution.py:329
  87.4 15.1 %collective-permute-start.26 = (bf16[2,640,256]{2,1,0:T(8,128)(2,1)S(1)}, bf16[2,640,256]{2,1,0:T(8,128)(2,1)S(1)}, u32[]{:S(2)}, u32[]{:S(2)}) collective-permute-start(bf16[2,640,256]{2,1,0:T(8,128)(2,1)S(1)} %collective-permute-done.17.refs_2_.refs_3_.refs_4_.refs_5_), channel_id=1, source_target_pairs={{0,1},{1,0},{2,3},{3,2},{4,5},{5,4},{6,7},{7,6},{8,9},{9,8},{10,11... | collective-permute-start | bytes 1966088 | tf_op jit(solution)/shard_map/ppermute | solution.py:329
  93.0 8.2 %collective-permute-start.23 = (bf16[256,512]{1,0:T(8,128)(2,1)S(1)}, bf16[256,512]{1,0:T(8,128)(2,1)S(1)}, u32[]{:S(2)}, u32[]{:S(2)}) collective-permute-start(bf16[256,512]{1,0:T(8,128)(2,1)S(1)} %collective-permute-done.18.refs_14_), channel_id=1, source_target_pairs={{0,4},{4,8},{8,12},{12,0},{1,5},{5,9},{9,13},{13,1},{2,6},{6,10},{... | collective-permute-start | bytes 786440 | tf_op jit(solution)/shard_map/ppermute | solution.py:334
  93.6 7.6 %collective-permute-start.24 = (bf16[256,512]{1,0:T(8,128)(2,1)S(1)}, bf16[256,512]{1,0:T(8,128)(2,1)S(1)}, u32[]{:S(2)}, u32[]{:S(2)}) collective-permute-start(bf16[256,512]{1,0:T(8,128)(2,1)S(1)} %collective-permute-done.21.refs_15_), channel_id=1, source_target_pairs={{0,2},{2,0},{1,3},{3,1},{4,6},{6,4},{5,7},{7,5},{8,10},{10,8},{9,1... | collective-permute-start | bytes 786440 | tf_op jit(solution)/shard_map/ppermute | solution.py:329
  101.1 6.4 %collective-permute-start.25 = (bf16[256,512]{1,0:T(8,128)(2,1)S(1)}, bf16[256,512]{1,0:T(8,128)(2,1)S(1)}, u32[]{:S(2)}, u32[]{:S(2)}) collective-permute-start(bf16[256,512]{1,0:T(8,128)(2,1)S(1)} %collective-permute-done.23.refs_4_), channel_id=1, source_target_pairs={{0,2},{2,0},{1,3},{3,1},{4,6},{6,4},{5,7},{7,5},{8,10},{10,8},{9,1... | collective-permute-start | bytes 786440 | tf_op jit(solution)/shard_map/ppermute | solution.py:329
  (1 other events, 5.9 us)
